TPU v7x, 32 devices: a whole 2x2x4 slice. The times are simulated.
32 devices in a mesh: ctx: 8 (over y, x, core), head: 4 (over z).
Axes of the slice: x: 2, y: 2, z: 4, core: 2. Of those that a mesh axis runs over, the one named last changes fastest.
Arguments:
- query: bfloat16 [3072, 1024], P('ctx', 'head'), may hold values from -140 to 140
- key: bfloat16 [3072, 1024], P('ctx', 'head'), may hold values from -6 to 6
- value: bfloat16 [3072, 1024], P('ctx', 'head'), may hold values from -6 to 6
- block_mask: int32 [24, 3], P('ctx'), may hold values 0 or 1
- out_weight: bfloat16 [1024, 4096], P('head'), may hold values from -0.1875 to 0.1875
- cotangent: bfloat16 [3072, 4096], P(('ctx', 'head')), may hold values from -6 to 6
Outputs:
- mixed: bfloat16 [3072, 4096], P(('ctx', 'head'))
- grad_query: bfloat16 [3072, 1024], P('ctx', 'head')
- grad_key: bfloat16 [3072, 1024], P('ctx', 'head')
- grad_value: bfloat16 [3072, 1024], P('ctx', 'head')
All inputs are finite; a program needn't handle non-finite values. No bound on the sum of `block_mask` on one device may be relied on, other than what follows from the above.
Results may differ from a plain program's by a relative error of at most 0.006.
Values may be sent and summed in bfloat16 or wider, within the bound.
No kernel may reach another device: no remote copies, remote signals or barrier semaphores. Data moves between devices by JAX's collectives and lax.ppermute only.
A program may use at most 64 MiB of HBM per device.

v0:
```python
import math

import jax
import jax.numpy as jnp
from jax import lax
from jax.sharding import PartitionSpec as P

DH = 128


def carried_in(part, axis, combine, identity, reverse):
    count = lax.axis_size(axis)
    place = lax.axis_index(axis)
    ahead = count - 1 - place if reverse else place
    gathered = lax.all_gather(part, axis)
    state = jnp.zeros_like(part) + jnp.asarray(identity, part.dtype)

    def one(lap, state):
        source = count - 1 - lap if reverse else lap
        return combine(state, lax.dynamic_index_in_dim(gathered, source, 0, False))

    return lax.fori_loop(0, ahead, one, state)


def keep_table(mask, rows):
    count = mask.shape[0]
    blk = rows // count
    full = jnp.broadcast_to((mask > 0)[:, None, :, None], (count, blk, count, blk)).reshape(
        rows, rows
    )
    pos = jnp.arange(rows)
    same = pos[:, None] // blk == pos[None, :] // blk
    causal = pos[:, None] >= pos[None, :]
    return (causal & (full | same), causal)


def add_one(earlier, later):
    return earlier + later


def on_device(query, key, value, block_mask, out_weight, cotangent):
    rows = query.shape[0]
    heads = query.shape[1] // DH
    width = heads * DH
    length = rows * lax.axis_size("ctx")
    scale = 1.0 / math.sqrt(DH * length)
    inv_root = 1.0 / math.sqrt(DH)
    single_float_type = jnp.float32
    upper_limit = lax.Precision.HIGHEST
    qh = query.reshape(rows, heads, DH).transpose(1, 0, 2)
    kh = key.reshape(rows, heads, DH).transpose(1, 0, 2)
    vh = value.reshape(rows, heads, DH).transpose(1, 0, 2)
    keep, causal = keep_table(block_mask, rows)
    grad_attn = jnp.einsum(
        "rn,kn->rk",
        lax.all_gather(cotangent, "head", axis=0, tiled=True),
        out_weight,
        preferred_element_type=single_float_type,
    ).astype(jnp.bfloat16)
    gradient_heads = grad_attn.reshape(rows, heads, DH).transpose(1, 0, 2)
    own_state = jnp.einsum("hjd,hje->hde", kh, vh, preferred_element_type=single_float_type)
    own_grad = scale * jnp.einsum(
        "hid,hie->hde", qh, gradient_heads, preferred_element_type=single_float_type
    )
    empty = jnp.zeros_like(own_state)
    linear_state = carried_in(own_state, "ctx", add_one, empty, False)
    grad_state = carried_in(own_grad, "ctx", add_one, empty, True)
    raw = jnp.einsum("hid,hjd->hij", qh, kh, preferred_element_type=single_float_type)
    scores = jnp.where(keep[None], raw * inv_root, -1e30)
    top = jnp.max(scores, -1, keepdims=True)
    expo = jnp.exp(scores - top)
    probs = (expo / jnp.sum(expo, -1, keepdims=True)).astype(jnp.bfloat16)
    soft = jnp.einsum("hij,hjd->hid", probs, vh, preferred_element_type=single_float_type)
    inner = jnp.where(causal[None], raw, 0.0).astype(jnp.bfloat16)
    intra = jnp.einsum("hij,hjd->hid", inner, vh, preferred_element_type=single_float_type)
    inter = jnp.einsum(
        "hid,hde->hie", qh.astype(single_float_type), linear_state, precision=upper_limit
    )
    attn_heads = (soft + scale * (intra + inter)).astype(jnp.bfloat16)
    attn = attn_heads.transpose(1, 0, 2).reshape(rows, width)
    partial_out = jnp.dot(attn, out_weight, preferred_element_type=single_float_type)
    mixed = lax.psum_scatter(partial_out, "head", scatter_dimension=0, tiled=True).astype(
        jnp.bfloat16
    )
    dprod = jnp.einsum("hid,hjd->hij", gradient_heads, vh, preferred_element_type=single_float_type)
    delta = jnp.sum(gradient_heads.astype(single_float_type) * soft, -1)
    dscore = (probs.astype(single_float_type) * (dprod - delta[:, :, None]) * inv_root).astype(
        jnp.bfloat16
    )
    dinner = jnp.where(causal[None], dprod, 0.0).astype(jnp.bfloat16)
    grad_q = jnp.einsum(
        "hij,hjd->hid", dscore, kh, preferred_element_type=single_float_type
    ) + scale * (
        jnp.einsum("hij,hjd->hid", dinner, kh, preferred_element_type=single_float_type)
        + jnp.einsum(
            "ykd,yod->yko",
            gradient_heads.astype(single_float_type),
            linear_state,
            precision=upper_limit,
        )
    )
    grad_k = (
        jnp.einsum("hij,hid->hjd", dscore, qh, preferred_element_type=single_float_type)
        + scale * jnp.einsum("hij,hid->hjd", dinner, qh, preferred_element_type=single_float_type)
        + jnp.einsum(
            "hjb,hab->hja", vh.astype(single_float_type), grad_state, precision=upper_limit
        )
    )
    value_gradient = (
        jnp.einsum("hij,hid->hjd", probs, gradient_heads, preferred_element_type=single_float_type)
        + scale
        * jnp.einsum(
            "hij,hid->hjd", inner, gradient_heads, preferred_element_type=single_float_type
        )
        + jnp.einsum(
            "hja,hab->hjb", kh.astype(single_float_type), grad_state, precision=upper_limit
        )
    )

    def flat(x):
        return x.astype(jnp.bfloat16).transpose(1, 0, 2).reshape(rows, width)

    return (mixed, flat(grad_q), flat(grad_k), flat(value_gradient))


def solution(mesh):
    return jax.shard_map(
        on_device,
        mesh=mesh,
        in_specs=(
            P("ctx", "head"),
            P("ctx", "head"),
            P("ctx", "head"),
            P("ctx", None),
            P("head", None),
            P(("ctx", "head"), None),
        ),
        out_specs=(P(("ctx", "head"), None), P("ctx", "head"), P("ctx", "head"), P("ctx", "head")),
        check_vma=False,
    )
```

profile of v0, /device:TPU:0, one launch (start us, length us, event | category | flops | bytes accessed | tf_op | source)
XLA Modules:
  0.0 247.7 jit_solution(11638238138145634389)
XLA Ops:
  7.2 0.0 all-gather.6.cloned.1.call-start
  7.3 0.7 all-gather.6.cloned.1.call-update
  7.9 0.0 all-gather.8.cloned.1.call-start
  8.0 1.9 fusion.24
  9.9 0.0 all-gather.8.cloned.1.call-update
  10.0 0.0 all-gather.10.cloned.1.call-start
  10.1 0.3 copy.75
  10.4 0.2 broadcast_in_dim.45
  10.6 0.2 fusion.22
  10.8 0.9 copy.69
  11.7 0.3 fusion.29
  12.0 1.1 convolution_bitcast_fusion.3
  13.1 2.5 fusion.55
  15.6 1.4 divide_convert_fusion
  16.9 58.9 %all-gather.6.cloned.1.call-done = bf16[384,4096]{1,0:T(8,128)(2,1)} async-done(((bf16[96,4096]{1,0:T(8,128)(2,1)}), bf16[384,4096]{1,0:T(8,128)(2,1)}) %all-gather.6.cloned.1.call-update) | async-done | bytes 3145744 | tf_op jit(solution)/shard_map/all_gather | solution.py:56
  75.9 3.2 %convolution_convert_fusion = bf16[384,256]{0,1:T(8,128)(2,1)S(1)} fusion(bf16[384,4096]{1,0:T(8,128)(2,1)} %all-gather.6.cloned.1.call-done, bf16[256,4096]{1,0:T(8,128)(2,1)S(1)} %copy-done), kind=kOutput, calls=%fused_computation.32 | convolution fusion | flops 805404672 | bytes 5439488 | tf_op jit(solution)/shard_map/rn,kn->rk/dot_general | solution.py:54
  79.0 0.2 fusion.18
  79.2 0.7 copy.92
  80.0 0.0 reduce-scatter.2.cloned.1.call-start
  80.0 20.4 %all-gather.8.cloned.1.call-done = f32[16,128,128]{2,1,0:T(8,128)} async-done(((f32[2,128,128]{2,1,0:T(8,128)}), f32[16,128,128]{2,1,0:T(8,128)}) %all-gather.8.cloned.1.call-update) | async-done | bytes 1048592 | tf_op jit(solution)/shard_map/all_gather | solution.py:15
  100.5 0.9 multiply_reduce_fusion
  101.5 0.0 copy-done.15
  101.5 0.4 fusion.14
  101.9 3.7 %fusion.56 = f32[384,4096]{1,0:T(8,128)} fusion(bf16[384,256]{0,1:T(8,128)(2,1)S(1)} %bitcast.228, bf16[256,4096]{1,0:T(8,128)(2,1)S(1)} %copy-done), kind=kOutput, calls=%fused_computation.83 | convolution fusion | flops 805306368 | bytes 8585216 | tf_op jit(solution)/shard_map/dot_general | solution.py:81
  105.6 1.4 multiply_convert_fusion
  107.1 1.5 fusion.28
  108.6 0.4 fusion.27
  109.0 1.0 fusion.15
  110.0 1.7 copy.96
  111.7 1.3 fusion.57
  113.1 1.4 fusion.30
  114.5 0.3 fusion.11
  114.8 1.1 fusion.13
  116.0 9.9 %all-gather.10.cloned.1.call-done = f32[16,128,128]{2,1,0:T(8,128)} async-done(((f32[2,128,128]{2,1,0:T(8,128)}), f32[16,128,128]{2,1,0:T(8,128)}) %all-gather.10.cloned.1.call-update) | async-done | bytes 1048592 | tf_op jit(solution)/shard_map/all_gather | solution.py:15
  125.9 6.7 %while.23 = (s32[]{:T(128)}, f32[2,128,128]{2,1,0:T(8,128)S(1)}, s32[]{:T(128)}, f32[8,2,128,128]{3,2,1,0:T(8,128)}, s32[]{:T(128)}, /*index=5*/s32[]{:T(128)}, s32[]{:T(128)}, s32[]{:T(128)}) while((s32[]{:T(128)}, f32[2,128,128]{2,1,0:T(8,128)S(1)}, s32[]{:T(128)}, f32[8,2,128,128]{3,2,1,0:T(8,128)}, s32[]{:T(128)}, /*index=5*/s32[]{:T(128)}, ...), condition=%wide.region_7.8_spmd, body=%wide.region_6.7_spmd.sunk | while | flops 32774 | bytes 393359 | solution.py:22
  125.9 0.9 bitcast_add_fusion.5
  126.9 0.9 bitcast_add_fusion.5
  127.9 0.9 bitcast_add_fusion.5
  128.8 0.9 bitcast_add_fusion.5
  129.8 0.9 bitcast_add_fusion.5
  130.7 0.9 bitcast_add_fusion.5
  131.7 0.9 bitcast_add_fusion.5
  132.7 0.4 fusion.17
  133.1 0.8 copy.98
  133.9 1.5 fusion.16
  135.4 0.8 copy.97
  136.2 102.6 %reduce-scatter.2.cloned.1.call-done = f32[96,4096]{1,0:T(8,128)} async-done(((f32[384,4096]{1,0:T(8,128)}), f32[96,4096]{1,0:T(8,128)}) %reduce-scatter.2.cloned.1.call-update) | async-done | bytes 1572880 | tf_op jit(solution)/shard_map/reduce_scatter | solution.py:82
  238.8 2.4 convert_element_type.50
  (41 shorter events, 0.2 us)
Async XLA Ops:
  7.2 68.7 %copy-start = (bf16[256,4096]{1,0:T(8,128)(2,1)S(1)}, bf16[256,4096]{1,0:T(8,128)(2,1)}, u32[]{:S(2)}) copy-start(bf16[256,4096]{1,0:T(8,128)(2,1)} %param.14) | copy-start | bytes 6291460
  7.2 4.5 %copy-start.8 = (bf16[384,256]{1,0:T(8,128)(2,1)S(1)}, bf16[384,256]{1,0:T(8,128)(2,1)}, u32[]{:S(2)}) copy-start(bf16[384,256]{1,0:T(8,128)(2,1)} %param.11) | copy-start | bytes 589828
  7.2 2.9 %copy-start.16 = (s32[3,3]{1,0:T(4,128)S(1)}, s32[3,3]{1,0:T(4,128)}, u32[]{:S(2)}) copy-start(s32[3,3]{1,0:T(4,128)} %param.13) | copy-start | bytes 112
  7.2 4.5 %copy-start.6 = (bf16[384,256]{1,0:T(8,128)(2,1)S(1)}, bf16[384,256]{1,0:T(8,128)(2,1)}, u32[]{:S(2)}) copy-start(bf16[384,256]{1,0:T(8,128)(2,1)} %param.10) | copy-start | bytes 589828
  7.2 68.6 %all-gather.6.cloned.1.call-start = ((), (), s32[]{:S(2)}) async-start(), calls=%async_computation.2 | async-start | bytes 3932160 | tf_op jit(solution)/shard_map/all_gather | solution.py:56
  7.9 92.5 %all-gather.8.cloned.1.call-start = ((), (), s32[]{:S(2)}) async-start(), calls=%async_computation.3 | async-start | bytes 1179648 | tf_op jit(solution)/shard_map/all_gather | solution.py:15
  9.9 2.0 copy-start.4
  10.0 115.9 %all-gather.10.cloned.1.call-start = ((), (), s32[]{:S(2)}) async-start(), calls=%async_computation.4 | async-start | bytes 1179648 | tf_op jit(solution)/shard_map/all_gather | solution.py:15
  12.0 3.6 %copy-start.13 = (bf16[2,384,384]{1,2,0:T(8,128)(2,1)}, bf16[2,384,384]{1,2,0:T(8,128)(2,1)S(1)}, u32[]{:S(2)}) copy-start(bf16[2,384,384]{1,2,0:T(8,128)(2,1)S(1)} %fusion.29) | copy-start | bytes 1769476
  79.0 21.5 %copy-start.1 = (bf16[384,256]{0,1:T(8,128)(2,1)}, bf16[384,256]{0,1:T(8,128)(2,1)S(1)}, u32[]{:S(2)}) copy-start(bf16[384,256]{0,1:T(8,128)(2,1)S(1)} %convolution_convert_fusion) | copy-start | bytes 589828
  80.0 158.8 %reduce-scatter.2.cloned.1.call-start = ((), (), s32[]{:S(2)}) async-start(), calls=%async_computation.1 | async-start | bytes 7864320 | tf_op jit(solution)/shard_map/reduce_scatter | solution.py:82
  100.5 1.0 copy-start.15
  105.6 3.0 %copy-start.9 = (bf16[384,256]{1,0:T(8,128)(2,1)S(1)}, bf16[384,256]{1,0:T(8,128)(2,1)}, u32[]{:S(2)}) copy-start(bf16[384,256]{1,0:T(8,128)(2,1)} %param.11) | copy-start | bytes 589828
  107.1 1.9 copy-start.11
  107.1 1.9 copy-start.2
  111.7 2.7 %copy-start.3 = (bf16[384,256]{0,1:T(8,128)(2,1)S(1)}, bf16[384,256]{0,1:T(8,128)(2,1)}, u32[]{:S(2)}) copy-start(bf16[384,256]{0,1:T(8,128)(2,1)} %copy-done.1) | copy-start | bytes 589828
  111.7 2.7 %copy-start.14 = (bf16[2,384,384]{1,2,0:T(8,128)(2,1)S(1)}, bf16[2,384,384]{1,2,0:T(8,128)(2,1)}, u32[]{:S(2)}) copy-start(bf16[2,384,384]{1,2,0:T(8,128)(2,1)} %copy-done.13) | copy-start | bytes 1769476
  113.1 1.8 copy-start.7
  113.1 1.8 copy-start.12
  116.0 16.7 %copy-start.10 = (bf16[384,256]{1,0:T(8,128)(2,1)S(1)}, bf16[384,256]{1,0:T(8,128)(2,1)}, u32[]{:S(2)}) copy-start(bf16[384,256]{1,0:T(8,128)(2,1)} %param.11) | copy-start | bytes 589828
  132.6 1.3 copy-start.5
Sparse Core Ops, SparseCore 0:
  9.6 66.1 all-gather.5
  78.3 22.1 all-gather.7
  102.4 23.4 all-gather.9
  128.1 110.7 reduce-scatter.1
where the time goes:
time: 248 us
  waiting for transfers between devices  193 us (78%)
  matrix products  24.5 us (10%)
  between operations  14.1 us (6%)
  other arithmetic  10.5 us (4%)
  local copies, waits for them, and re-layouts  5.66 us (2%)
    reduce_scatter x1, waiting for transfers between devices, on_device(): lax.psum_scatter(partial_out, 'head', scatter_dimension=0, tiled=True)  103 us
    all_gather x1, waiting for transfers between devices, on_device(): lax.all_gather(cotangent, 'head', axis=0, tiled=True)  58.9 us
    all_gather x2, waiting for transfers between devices, carried_in(): gathered = lax.all_gather(part, axis)  30.4 us
    add x7, other arithmetic, add_one(): return earlier + later  6.56 us
  transfers between devices with their start and end apart: 4, of which 4 were waited for; matrix products, arithmetic and copies ran while one was open for 15% of the time, Pallas kernels for 0%

commit v1 on v0

--- a/solution.py
+++ b/solution.py
@@ -8,18 +8,19 @@
 DH = 128
 
 
-def carried_in(part, axis, combine, identity, reverse):
+def carried_in(part, axis, reverse):
     count = lax.axis_size(axis)
     place = lax.axis_index(axis)
-    ahead = count - 1 - place if reverse else place
-    gathered = lax.all_gather(part, axis)
-    state = jnp.zeros_like(part) + jnp.asarray(identity, part.dtype)
-
-    def one(lap, state):
-        source = count - 1 - lap if reverse else lap
-        return combine(state, lax.dynamic_index_in_dim(gathered, source, 0, False))
-
-    return lax.fori_loop(0, ahead, one, state)
+    total = part
+    carried = jnp.zeros_like(part)
+    step = 1
+    while step < count:
+        other = lax.ppermute(total, axis, [(i, i ^ step) for i in range(count)])
+        upper = (place & step) > 0
+        carried = carried + jnp.where(upper ^ reverse, other, 0.0)
+        total = total + other
+        step *= 2
+    return carried
 
 
 def keep_table(mask, rows):
@@ -32,10 +33,6 @@
     same = pos[:, None] // blk == pos[None, :] // blk
     causal = pos[:, None] >= pos[None, :]
     return (causal & (full | same), causal)
-
-
-def add_one(earlier, later):
-    return earlier + later
 
 
 def on_device(query, key, value, block_mask, out_weight, cotangent):
@@ -51,20 +48,21 @@
     kh = key.reshape(rows, heads, DH).transpose(1, 0, 2)
     vh = value.reshape(rows, heads, DH).transpose(1, 0, 2)
     keep, causal = keep_table(block_mask, rows)
-    grad_attn = jnp.einsum(
-        "rn,kn->rk",
-        lax.all_gather(cotangent, "head", axis=0, tiled=True),
-        out_weight,
-        preferred_element_type=single_float_type,
+    shards = lax.axis_size("ctx")
+    piece = width // shards
+    part = lax.dynamic_slice_in_dim(out_weight, lax.axis_index("ctx") * piece, piece, 0)
+    weight = lax.all_gather(part, ("head", "ctx"), axis=0, tiled=True)
+    grad_own = jnp.einsum(
+        "rn,kn->rk", cotangent, weight, preferred_element_type=single_float_type
     ).astype(jnp.bfloat16)
+    grad_attn = lax.all_to_all(grad_own, "head", 1, 0, tiled=True)
     gradient_heads = grad_attn.reshape(rows, heads, DH).transpose(1, 0, 2)
     own_state = jnp.einsum("hjd,hje->hde", kh, vh, preferred_element_type=single_float_type)
     own_grad = scale * jnp.einsum(
         "hid,hie->hde", qh, gradient_heads, preferred_element_type=single_float_type
     )
-    empty = jnp.zeros_like(own_state)
-    linear_state = carried_in(own_state, "ctx", add_one, empty, False)
-    grad_state = carried_in(own_grad, "ctx", add_one, empty, True)
+    linear_state = carried_in(own_state, "ctx", False)
+    grad_state = carried_in(own_grad, "ctx", True)
     raw = jnp.einsum("hid,hjd->hij", qh, kh, preferred_element_type=single_float_type)
     scores = jnp.where(keep[None], raw * inv_root, -1e30)
     top = jnp.max(scores, -1, keepdims=True)
@@ -78,10 +76,8 @@
     )
     attn_heads = (soft + scale * (intra + inter)).astype(jnp.bfloat16)
     attn = attn_heads.transpose(1, 0, 2).reshape(rows, width)
-    partial_out = jnp.dot(attn, out_weight, preferred_element_type=single_float_type)
-    mixed = lax.psum_scatter(partial_out, "head", scatter_dimension=0, tiled=True).astype(
-        jnp.bfloat16
-    )
+    attn_own = lax.all_to_all(attn, "head", 0, 1, tiled=True)
+    mixed = jnp.dot(attn_own, weight, preferred_element_type=single_float_type).astype(jnp.bfloat16)
     dprod = jnp.einsum("hid,hjd->hij", gradient_heads, vh, preferred_element_type=single_float_type)
     delta = jnp.sum(gradient_heads.astype(single_float_type) * soft, -1)
     dscore = (probs.astype(single_float_type) * (dprod - delta[:, :, None]) * inv_root).astype(

time: 248 us -> 151 us (0.61)
  waiting for transfers between devices: 193 us -> 76.8 us
  starting transfers between devices: 0.16 us -> 15.2 us
  local copies, waits for them, and re-layouts: 5.66 us -> 14.4 us
  other arithmetic: 10.5 us -> 3.66 us
    reduce_scatter x1 -> x0, waiting for transfers between devices: 103 us -> none  [on_device(): lax.psum_scatter(partial_out, 'head', scatter_dimension=0, tiled=True)]
    all_gather x3 -> x1, waiting for transfers between devices: 89.3 us -> 65.3 us  [on_device(): weight = lax.all_gather(part, ('head', 'ctx'), axis=0, tiled=True)]
    ppermute x0 -> x6, starting transfers between devices: none -> 7.83 us  [carried_in(): other = lax.ppermute(total, axis, [(i, i ^ step) for i in range(count)])]
    all_to_all x0 -> x2, starting transfers between devices: none -> 7.36 us  [the longest x1 3.99 us: on_device(): attn_own = lax.all_to_all(attn, 'head', 0, 1, tiled=True)]
    ppermute x0 -> x6, waiting for transfers between devices: none -> 6.31 us  [carried_in(): other = lax.ppermute(total, axis, [(i, i ^ step) for i in range(count)])]
    all_to_all x0 -> x2, waiting for transfers between devices: none -> 5.22 us  [the longest x1 5.22 us: on_device(): grad_attn = lax.all_to_all(grad_own, 'head', 1, 0, tiled=True)]
    dot_general x2, matrix products: 6.83 us -> 12 us  [the longest x1 6.23 us: on_device(): jnp.einsum('rn,kn->rk', cotangent, weight, preferred_element_type=single_...]
    add x7 -> x6, other arithmetic: 6.56 us -> 2.07 us  [the longest x4 1.37 us: carried_in(): total = total + other]
  transfers between devices with their start and end apart: 4 -> 9, of which waited for: 4 -> 4; matrix products, arithmetic and copies ran while one was open for 15% -> 20% of each run, Pallas kernels for 0% -> 0%
where the time goes in v1:
time: 151 us
  waiting for transfers between devices  76.8 us (51%)
  matrix products  26.5 us (18%)
  starting transfers between devices  15.2 us (10%)
  local copies, waits for them, and re-layouts  14.4 us (10%)
  between operations  14.3 us (9%)
  other arithmetic  3.66 us (2%)
    all_gather x1, waiting for transfers between devices, on_device(): weight = lax.all_gather(part, ('head', 'ctx'), axis=0, tiled=True)  65.3 us
    ppermute x6, starting transfers between devices, carried_in(): other = lax.ppermute(total, axis, [(i, i ^ step) for i in range(count)])  7.83 us
    ppermute x6, waiting for transfers between devices, carried_in(): other = lax.ppermute(total, axis, [(i, i ^ step) for i in range(count)])  6.31 us
    dot_general x1, matrix products, on_device(): jnp.einsum('rn,kn->rk', cotangent, weight, preferred_element_type=single_...  6.23 us
    dot_general x1, matrix products, on_device(): jnp.dot(attn_own, weight, preferred_element_type=single_float_type)  5.77 us
    unnamed x35, local copies, waits for them, and re-layouts  5.29 us
    all_to_all x1, waiting for transfers between devices, on_device(): grad_attn = lax.all_to_all(grad_own, 'head', 1, 0, tiled=True)  5.22 us
    all_to_all x1, starting transfers between devices, on_device(): attn_own = lax.all_to_all(attn, 'head', 0, 1, tiled=True)  3.99 us
  transfers between devices with their start and end apart: 9, of which 4 were waited for; matrix products, arithmetic and copies ran while one was open for 20% of the time, Pallas kernels for 0%

profile of v1, /device:TPU:0, one launch (start us, length us, event | category | flops | bytes accessed | tf_op | source)
XLA Modules:
  0.0 150.9 jit_solution(17671451723324597982)
XLA Ops:
  7.3 1.5 %copy-done = bf16[256,4096]{1,0:T(8,128)(2,1)S(1)} copy-done((bf16[256,4096]{1,0:T(8,128)(2,1)S(1)}, bf16[256,4096]{1,0:T(8,128)(2,1)}, u32[]{:S(2)}) %copy-start) | copy-done | bytes 2097176
  8.8 0.7 constant_dynamic-slice_fusion
  9.5 1.3 fusion.25
  10.8 0.5 collective-permute-start
  12.0 1.6 %fusion.61 = (f32[2,384]{1,0:T(2,128)S(1)}, f32[2,384,384]{1,2,0:T(8,128)}) fusion(pred[384,384]{0,1:T(8,128)(4,1)S(1)} %copy.40, bf16[384,256]{1,0:T(8,128)(2,1)S(1)} %copy-done.3, bf16[384,256]{1,0:T(8,128)(2,1)S(1)} %copy-done.2), kind=kOutput, calls=%fused_computation.91 | convolution fusion | flops 76677504 | bytes 1723392 | tf_op jit(solution)/shard_map/sub | solution.py:69
  13.6 1.4 divide_convert_fusion
  15.1 0.9 copy.46
  16.0 2.6 %collective-permute-start.1 = (f32[2,128,128]{2,1,0:T(8,128)S(1)}, f32[2,128,128]{2,1,0:T(8,128)S(1)}, u32[]{:S(2)}, u32[]{:S(2)}) collective-permute-start(f32[2,128,128]{2,1,0:T(8,128)S(1)} %add.79), channel_id=1, source_target_pairs={{0,8},{4,12},{8,0},{12,4},{16,24},{20,28},{24,16},{28,20},{1,9},{5... | collective-permute-start | bytes 393224 | tf_op jit(solution)/shard_map/ppermute | solution.py:18
  18.6 1.1 fusion.29
  19.7 3.0 %collective-permute-done.1 = f32[2,128,128]{2,1,0:T(8,128)S(1)} collective-permute-done((f32[2,128,128]{2,1,0:T(8,128)S(1)}, f32[2,128,128]{2,1,0:T(8,128)S(1)}, u32[]{:S(2)}, u32[]{:S(2)}) %collective-permute-start.1) | collective-permute-done | bytes 131104 | tf_op jit(solution)/shard_map/ppermute | solution.py:18
  22.7 0.7 copy-done.8
  23.4 0.7 add.81
  24.1 1.8 %collective-permute-start.2 = (f32[2,128,128]{2,1,0:T(8,128)}, f32[2,128,128]{2,1,0:T(8,128)}, u32[]{:S(2)}, u32[]{:S(2)}) collective-permute-start(f32[2,128,128]{2,1,0:T(8,128)} %add.81), channel_id=1, source_target_pairs={{0,16},{4,20},{8,24},{12,28},{16,0},{20,4},{24,8},{28,12},{1,17},{... | collective-permute-start | bytes 393224 | tf_op jit(solution)/shard_map/ppermute | solution.py:18
  25.8 65.3 %all-gather.2.cloned.1.call-done = bf16[1024,4096]{1,0:T(8,128)(2,1)} async-done(((bf16[32,4096]{1,0:T(8,128)(2,1)}), bf16[1024,4096]{1,0:T(8,128)(2,1)}) %all-gather.2.cloned.1.call-update) | async-done | bytes 8388624 | tf_op jit(solution)/shard_map/all_gather | solution.py:54
  91.1 6.2 %convolution_convert_fusion.1 = bf16[1024,96]{0,1:T(8,128)(2,1)S(1)} fusion(bf16[1024,4096]{1,0:T(8,128)(2,1)} %all-gather.2.cloned.1.call-done, bf16[96,4096]{1,0:T(8,128)(2,1)} %param.11), kind=kOutput, calls=%fused_computation.31 | convolution fusion | flops 805404672 | bytes 9371648 | tf_op jit(solution)/shard_map/rn,kn->rk/dot_general | solution.py:55
  97.3 0.7 copy.195
  98.0 3.4 %all-to-all-start.1 = ((bf16[96,4,256]{2,0,1:T(8,128)(2,1)}), bf16[96,4,256]{2,0,1:T(8,128)(2,1)S(1)}, u32[]{:S(2)}, u32[]{:S(2)}) async-start(bf16[96,4,256]{2,0,1:T(8,128)(2,1)} %bitcast.230), calls=%async_computation.1 | async-start | bytes 393216 | tf_op jit(solution)/shard_map/all_to_all | solution.py:58
  101.4 2.2 %convolution_bitcast_fusion.3 = f32[384,2,128]{0,2,1:T(8,128)} fusion(bf16[2,384,384]{1,2,0:T(8,128)(2,1)} %fusion.29, pred[384,384]{0,1:T(8,128)(4,1)} %copy.46, bf16[384,256]{1,0:T(8,128)(2,1)S(1)} %copy-done.1), kind=kOutput, calls=%fused_computation.11 | convolution fusion | flops 75792384 | bytes 1327104 | tf_op jit(solution)/shard_map/hij,hjd->hid/dot_general | solution.py:73
  103.7 0.7 select_add_fusion.1
  104.3 5.2 %all-to-all-done.1 = bf16[96,4,256]{2,0,1:T(8,128)(2,1)S(1)} async-done(((bf16[96,4,256]{2,0,1:T(8,128)(2,1)}), bf16[96,4,256]{2,0,1:T(8,128)(2,1)S(1)}, u32[]{:S(2)}, u32[]{:S(2)}) %all-to-all-start.1) | async-done | bytes 196640 | tf_op jit(solution)/shard_map/all_to_all | solution.py:58
  109.5 0.7 reshape.177
  110.3 1.1 copy.100
  111.4 0.9 fusion.18
  112.3 0.4 multiply_reduce_fusion
  112.7 1.1 fusion.33
  113.8 1.1 fusion.14
  114.8 1.8 %copy.51 = bf16[384,2,128]{2,1,0:T(2,128)(2,1)} copy(bf16[384,2,128]{0,2,1:T(8,128)(2,1)} %fusion.14) | data formatting | bytes 393216 | tf_op jit(solution)/shard_map/convert_element_type | solution.py:77
  116.6 1.7 %all_to_all.26 = bf16[4,96,256]{2,1,0:T(8,128)(2,1)} reshape(bf16[384,2,128]{2,1,0:T(2,128)(2,1)} %copy.51) | data formatting | bytes 393216 | tf_op jit(solution)/shard_map/all_to_all | solution.py:79
  118.4 4.0 %all-to-all-start = ((bf16[4,96,256]{2,1,0:T(8,128)(2,1)}), bf16[4,96,256]{2,1,0:T(8,128)(2,1)}, u32[]{:S(2)}, u32[]{:S(2)}) async-start(bf16[4,96,256]{2,1,0:T(8,128)(2,1)} %all_to_all.26), calls=%async_computation | async-start | bytes 393216 | tf_op jit(solution)/shard_map/all_to_all | solution.py:79
  122.4 0.4 multiply_convert_fusion
  122.7 0.5 copy-done.14
  123.3 0.4 fusion.27
  123.6 0.4 fusion.30
  124.0 1.2 fusion.13
  125.3 1.1 fusion.11
  126.4 0.3 fusion.28
  126.7 1.5 collective-permute-start.4
  128.2 0.3 fusion.15
  128.6 0.8 copy.71
  129.4 3.3 %collective-permute-done.4 = f32[2,128,128]{2,1,0:T(8,128)S(1)} collective-permute-done((f32[2,128,128]{2,1,0:T(8,128)S(1)}, f32[2,128,128]{2,1,0:T(8,128)S(1)}, u32[]{:S(2)}, u32[]{:S(2)}) %collective-permute-start.4) | collective-permute-done | bytes 131104 | tf_op jit(solution)/shard_map/ppermute | solution.py:18
  132.7 0.7 add.92
  133.3 1.5 collective-permute-start.5
  134.8 0.9 copy.115
  135.8 5.8 %convolution_convert_fusion = bf16[96,4096]{1,0:T(8,128)(2,1)} fusion(bf16[96,1024]{1,0:T(8,128)(2,1)S(1)} %bitcast.224, bf16[1024,4096]{1,0:T(8,128)(2,1)} %all-gather.2.cloned.1.call-done), kind=kOutput, calls=%fused_computation.1 | convolution fusion | flops 805699584 | bytes 9371648 | tf_op jit(solution)/shard_map/dot_general | solution.py:80
  141.6 0.4 fusion.16
  142.0 0.8 copy.72
  142.8 0.4 fusion.17
  143.2 0.8 copy.73
  (46 shorter events, 0.9 us)
Async XLA Ops:
  7.2 1.6 %copy-start = (bf16[256,4096]{1,0:T(8,128)(2,1)S(1)}, bf16[256,4096]{1,0:T(8,128)(2,1)}, u32[]{:S(2)}) copy-start(bf16[256,4096]{1,0:T(8,128)(2,1)} %param.10) | copy-start | bytes 6291460
  7.2 4.8 %copy-start.3 = (bf16[384,256]{1,0:T(8,128)(2,1)S(1)}, bf16[384,256]{1,0:T(8,128)(2,1)}, u32[]{:S(2)}) copy-start(bf16[384,256]{1,0:T(8,128)(2,1)} %param.7) | copy-start | bytes 589828
  7.2 4.2 %copy-start.15 = (s32[3,3]{1,0:T(4,128)S(1)}, s32[3,3]{1,0:T(4,128)}, u32[]{:S(2)}) copy-start(s32[3,3]{1,0:T(4,128)} %param.9) | copy-start | bytes 112
  7.2 4.8 %copy-start.2 = (bf16[384,256]{1,0:T(8,128)(2,1)S(1)}, bf16[384,256]{1,0:T(8,128)(2,1)}, u32[]{:S(2)}) copy-start(bf16[384,256]{1,0:T(8,128)(2,1)} %param.6) | copy-start | bytes 589828
  7.2 83.9 %all-gather.2.cloned.1.call-start = ((), (), s32[]{:S(2)}) async-start(), calls=%async_computation.2 | async-start | bytes 8650752 | tf_op jit(solution)/shard_map/all_gather | solution.py:54
  10.8 5.2 %collective-permute-start = (f32[2,128,128]{2,1,0:T(8,128)S(1)}, f32[2,128,128]{2,1,0:T(8,128)S(1)}, u32[]{:S(2)}, u32[]{:S(2)}) collective-permute-start(f32[2,128,128]{2,1,0:T(8,128)S(1)} %fusion.25), channel_id=1, source_target_pairs={{0,4},{4,0},{8,12},{12,8},{16,20},{20,16},{24,28},{28,24},{1,5},{5... | collective-permute-start | bytes 393224 | tf_op jit(solution)/shard_map/ppermute | solution.py:18
  16.0 81.4 %copy-start.7 = (f32[2,128,128]{2,1,0:T(8,128)}, f32[2,128,128]{2,1,0:T(8,128)S(1)}, u32[]{:S(2)}) copy-start(f32[2,128,128]{2,1,0:T(8,128)S(1)} %collective-permute-done) | copy-start | bytes 393220
  16.0 6.7 %collective-permute-start.1 = (f32[2,128,128]{2,1,0:T(8,128)S(1)}, f32[2,128,128]{2,1,0:T(8,128)S(1)}, u32[]{:S(2)}, u32[]{:S(2)}) collective-permute-start(f32[2,128,128]{2,1,0:T(8,128)S(1)} %add.79), channel_id=1, source_target_pairs={{0,8},{4,12},{8,0},{12,4},{16,24},{20,28},{24,16},{28,20},{1,9},{5... | collective-permute-start | bytes 393224 | tf_op jit(solution)/shard_map/ppermute | solution.py:18
  22.7 0.7 copy-start.8
  24.1 77.4 %copy-start.1 = (bf16[384,256]{1,0:T(8,128)(2,1)S(1)}, bf16[384,256]{1,0:T(8,128)(2,1)}, u32[]{:S(2)}) copy-start(bf16[384,256]{1,0:T(8,128)(2,1)} %param.8) | copy-start | bytes 589828
  24.1 79.6 %collective-permute-start.2 = (f32[2,128,128]{2,1,0:T(8,128)}, f32[2,128,128]{2,1,0:T(8,128)}, u32[]{:S(2)}, u32[]{:S(2)}) collective-permute-start(f32[2,128,128]{2,1,0:T(8,128)} %add.81), channel_id=1, source_target_pairs={{0,16},{4,20},{8,24},{12,28},{16,0},{20,4},{24,8},{28,12},{1,17},{... | collective-permute-start | bytes 393224 | tf_op jit(solution)/shard_map/ppermute | solution.py:18
  98.0 11.5 %all-to-all-start.1 = ((bf16[96,4,256]{2,0,1:T(8,128)(2,1)}), bf16[96,4,256]{2,0,1:T(8,128)(2,1)S(1)}, u32[]{:S(2)}, u32[]{:S(2)}) async-start(bf16[96,4,256]{2,0,1:T(8,128)(2,1)} %bitcast.230), calls=%async_computation.1 | async-start | bytes 393216 | tf_op jit(solution)/shard_map/all_to_all | solution.py:58
  112.3 1.5 copy-start.4
  112.3 1.5 copy-start.12
  118.4 16.5 %all-to-all-start = ((bf16[4,96,256]{2,1,0:T(8,128)(2,1)}), bf16[4,96,256]{2,1,0:T(8,128)(2,1)}, u32[]{:S(2)}, u32[]{:S(2)}) async-start(bf16[4,96,256]{2,1,0:T(8,128)(2,1)} %all_to_all.26), calls=%async_computation | async-start | bytes 393216 | tf_op jit(solution)/shard_map/all_to_all | solution.py:79
  122.4 0.9 copy-start.14
  124.0 1.2 copy-start.9
  124.0 1.2 copy-start.6
  124.0 1.2 copy-start.13
  125.2 1.5 %collective-permute-start.3 = (f32[2,128,128]{2,1,0:T(8,128)S(1)}, f32[2,128,128]{2,1,0:T(8,128)S(1)}, u32[]{:S(2)}, u32[]{:S(2)}) collective-permute-start(f32[2,128,128]{2,1,0:T(8,128)S(1)} %copy-done.9), channel_id=1, source_target_pairs={{0,4},{4,0},{8,12},{12,8},{16,20},{20,16},{24,28},{28,24},{1,5},{5... | collective-permute-start | bytes 393224 | tf_op jit(solution)/shard_map/ppermute | solution.py:18
  126.4 1.9 %copy-start.5 = (f32[2,128,128]{2,1,0:T(8,128)S(1)}, f32[2,128,128]{2,1,0:T(8,128)}, u32[]{:S(2)}) copy-start(f32[2,128,128]{2,1,0:T(8,128)} %select_add_fusion.1) | copy-start | bytes 393220
  126.7 5.9 %collective-permute-start.4 = (f32[2,128,128]{2,1,0:T(8,128)S(1)}, f32[2,128,128]{2,1,0:T(8,128)S(1)}, u32[]{:S(2)}, u32[]{:S(2)}) collective-permute-start(f32[2,128,128]{2,1,0:T(8,128)S(1)} %add.90), channel_id=1, source_target_pairs={{0,8},{4,12},{8,0},{12,4},{16,24},{20,28},{24,16},{28,20},{1,9},{5... | collective-permute-start | bytes 393224 | tf_op jit(solution)/shard_map/ppermute | solution.py:18
  133.3 8.2 %collective-permute-start.5 = (f32[2,128,128]{2,1,0:T(8,128)}, f32[2,128,128]{2,1,0:T(8,128)S(1)}, u32[]{:S(2)}, u32[]{:S(2)}) collective-permute-start(f32[2,128,128]{2,1,0:T(8,128)} %add.92), channel_id=1, source_target_pairs={{0,16},{4,20},{8,24},{12,28},{16,0},{20,4},{24,8},{28,12},{1,17},{... | collective-permute-start | bytes 393224 | tf_op jit(solution)/shard_map/ppermute | solution.py:18
  135.8 5.8 %copy-start.10 = (f32[384,2,128]{0,2,1:T(8,128)S(1)}, f32[384,2,128]{0,2,1:T(8,128)}, u32[]{:S(2)}) copy-start(f32[384,2,128]{0,2,1:T(8,128)} %fusion.13) | copy-start | bytes 1179652
  141.5 1.3 copy-start.11
Sparse Core Ops, SparseCore 0:
  10.9 80.1 all-gather.1

commit v2 on v1

v2 whole, which is shorter than its diff:
```python
import functools
import math

import jax
import jax.numpy as jnp
from jax import lax
from jax.experimental import pallas as pl
from jax.experimental.pallas import tpu as pltpu
from jax.sharding import PartitionSpec as P

DH = 128
F32 = jnp.float32
BF16 = jnp.bfloat16
NN = ((1,), (0,))
NT = ((1,), (1,))
TN = ((0,), (0,))
MIB = 1 << 20


def dot(a, b, dims):
    return lax.dot_general(a, b, (dims, ((), ())), preferred_element_type=F32)


def dot_wide(a, b, dims):
    high = b.astype(BF16)
    low = (b - high.astype(F32)).astype(BF16)
    return dot(a, high, dims) + dot(a, low, dims)


def call(body, outs, args, flops, smem=(), scratch=()):
    moved = sum(a.size * a.dtype.itemsize for a in args)
    moved += sum(math.prod(s) * jnp.dtype(t).itemsize for s, t in outs)
    return pl.pallas_call(
        body,
        out_shape=[jax.ShapeDtypeStruct(s, t) for s, t in outs],
        in_specs=[pl.BlockSpec(memory_space=pltpu.SMEM) for _ in smem]
        + [pl.BlockSpec(memory_space=pltpu.VMEM) for _ in args],
        out_specs=[pl.BlockSpec(memory_space=pltpu.VMEM) for _ in outs],
        scratch_shapes=list(scratch),
        compiler_params=pltpu.CompilerParams(vmem_limit_bytes=40 * MIB),
        cost_estimate=pl.CostEstimate(
            flops=int(flops), bytes_accessed=int(moved), transcendentals=0
        ),
    )(*smem, *args)


def lower_triangle(blk):
    return lax.broadcasted_iota(jnp.int32, (blk, blk), 0) >= lax.broadcasted_iota(
        jnp.int32, (blk, blk), 1
    )


def forward_kernel(scale, mask, q_ref, k_ref, v_ref, probs_ref, inner_ref, soft_ref, pre_ref):
    rows, width = q_ref.shape
    count = mask.shape[0]
    blk = rows // count
    inv_root = 1.0 / math.sqrt(DH)
    triangle = lower_triangle(blk)
    for h in range(width // DH):
        cols = slice(h * DH, (h + 1) * DH)
        for i in range(count):
            here = slice(i * blk, (i + 1) * blk)
            upto = slice(0, (i + 1) * blk)
            raw = dot(q_ref[here, cols], k_ref[upto, cols], NT)
            scores, inner = [], []
            for j in range(i + 1):
                part = raw[:, j * blk : (j + 1) * blk]
                keep = triangle if j == i else mask[i, j] > 0
                scores.append(jnp.where(keep, part * inv_root, -1e30))
                inner.append(jnp.where(triangle, part, 0.0) if j == i else part)
            scores = jnp.concatenate(scores, 1)
            inner = jnp.concatenate(inner, 1).astype(BF16)
            expo = jnp.exp(scores - jnp.max(scores, -1, keepdims=True))
            probs = (expo / jnp.sum(expo, -1, keepdims=True)).astype(BF16)
            v = v_ref[upto, cols]
            soft = dot(probs, v, NN)
            probs_ref[h, here, upto] = probs
            inner_ref[h, here, upto] = inner
            soft_ref[here, cols] = soft
            pre_ref[here, cols] = soft + scale * dot(inner, v, NN)


def attn_kernel(scale, place, q_ref, pre_ref, state_ref, *out_refs):
    count = len(out_refs)
    own = out_refs[0].shape[0]
    for s in range(count):
        block = lax.rem(place[0] + s, count)
        here = pl.ds(pl.multiple_of(block * own, own), own)
        for h in range(q_ref.shape[1] // DH):
            cols = slice(h * DH, (h + 1) * DH)
            inter = dot_wide(q_ref[here, cols], state_ref[h], NN)
            out_refs[s][:, cols] = (pre_ref[here, cols] + scale * inter).astype(BF16)


def grad_kernel(places, mine_ref, mate_ref, *refs):
    chunks, (own_ref, other_ref) = refs[:-2], refs[-2:]
    own = mine_ref.shape[0]
    total = None
    for j, chunk in enumerate(chunks):
        cols = pl.ds(pl.multiple_of(places[j], DH), chunk.shape[1])
        left = jnp.concatenate([mine_ref[:, cols], mate_ref[:, cols]], 0)
        part = dot(left, chunk[...], NT)
        total = part if total is None else total + part
    total = total.astype(BF16)
    own_ref[...] = total[:own]
    other_ref[...] = total[own:]


def mixed_kernel(count, places, core, *refs):
    own_out, mate_out = refs[-2:]
    attn, mate, weight = refs[:count], refs[count], refs[count + 1]
    chunks = refs[count + 2 : -2]
    each = len(chunks) // (count - 1)
    own = own_out.shape[0]
    cols = pl.ds(pl.multiple_of(core[0] * DH, DH), DH)
    left = jnp.concatenate(
        [jnp.concatenate([attn[s][:, cols], mate[s]], 0) for s in range(count)], 1
    )
    for j in range(each):
        wide = chunks[j].shape[1]
        there = pl.ds(pl.multiple_of(places[j], DH), wide)
        right = jnp.concatenate(
            [weight[:, there]] + [chunks[s * each + j][...] for s in range(count - 1)], 0
        )
        part = dot(left, right, NN)
        own_out[:, there] = part[:own]
        mate_out[:, there] = part[own:]


def collect_kernel(scale, where, q_ref, *refs):
    g_ref, state_ref = refs[-2:]
    count = (len(refs) - 2) // 2
    own = refs[0].shape[0]
    place, core = where[0], where[1]
    mine = pl.ds(pl.multiple_of(core * DH, DH), DH)
    mate = pl.ds(pl.multiple_of((1 - core) * DH, DH), DH)
    for s in range(count):
        block = lax.rem(place + s, count)
        here = pl.ds(pl.multiple_of(block * own, own), own)
        g_ref[here, mine] = refs[s][...]
        g_ref[here, mate] = refs[count + s][...]
    for h in range(q_ref.shape[1] // DH):
        cols = slice(h * DH, (h + 1) * DH)
        state_ref[h] = scale * dot(q_ref[:, cols], g_ref[:, cols], TN)


def backward_kernel(
    scale,
    count,
    q_ref,
    k_ref,
    v_ref,
    g_ref,
    probs_ref,
    inner_ref,
    soft_ref,
    state_ref,
    dq_ref,
    dk_ref,
    dv_ref,
):
    rows, width = q_ref.shape
    blk = rows // count
    inv_root = 1.0 / math.sqrt(DH)
    triangle = lower_triangle(blk)
    for h in range(width // DH):
        cols = slice(h * DH, (h + 1) * DH)
        for i in reversed(range(count)):
            here = slice(i * blk, (i + 1) * blk)
            upto = slice(0, (i + 1) * blk)
            q, g = q_ref[here, cols], g_ref[here, cols]
            k = k_ref[upto, cols]
            probs = probs_ref[h, here, upto]
            dprod = dot(g, v_ref[upto, cols], NT)
            delta = jnp.sum(g.astype(F32) * soft_ref[here, cols], -1, keepdims=True)
            dscore = (probs.astype(F32) * (dprod - delta) * inv_root).astype(BF16)
            last = jnp.where(triangle, dprod[:, i * blk :], 0.0)
            dinner = jnp.concatenate([dprod[:, : i * blk], last], 1) if i else last
            dinner = dinner.astype(BF16)
            dq_ref[here, cols] = (
                dot(dscore, k, NN)
                + scale * (dot(dinner, k, NN) + dot_wide(g, state_ref[h], NT))
            ).astype(BF16)
            dk = dot(dscore, q, TN) + scale * dot(dinner, q, TN)
            dv = dot(probs, g, TN) + scale * dot(inner_ref[h, here, upto], g, TN)
            if i == count - 1:
                dk_ref[upto, cols] = dk
                dv_ref[upto, cols] = dv
            else:
                dk_ref[upto, cols] += dk
                dv_ref[upto, cols] += dv


def close_kernel(k_ref, v_ref, dk_ref, dv_ref, state_ref, gk_ref, gv_ref):
    for h in range(k_ref.shape[1] // DH):
        cols = slice(h * DH, (h + 1) * DH)
        state = state_ref[h]
        gk_ref[:, cols] = (dk_ref[:, cols] + dot_wide(v_ref[:, cols], state, NT)).astype(BF16)
        gv_ref[:, cols] = (dv_ref[:, cols] + dot_wide(k_ref[:, cols], state, NN)).astype(BF16)


def send(x, flip, shift):
    shards, heads = lax.axis_size("ctx"), lax.axis_size("head")
    pairs = [
        (c * heads + z, (c ^ flip) * heads + (z + shift) % heads)
        for c in range(shards)
        for z in range(heads)
    ]
    return lax.ppermute(x, ("ctx", "head"), pairs)


def carried_in(part, reverse):
    place = lax.axis_index("ctx")
    total = part
    carried = jnp.zeros_like(part)
    step = 1
    while step < lax.axis_size("ctx"):
        other = send(total, step, 0)
        upper = (place & step) > 0
        carried = carried + jnp.where(upper ^ reverse, other, 0.0)
        total = total + other
        step *= 2
    return carried


def spread(piece, chip, chips):
    wide = piece.shape[1]
    if chips != 4:
        shards = lax.axis_size("ctx")
        groups = [list(range(core, shards, 2)) for core in range(2)]
        whole = lax.all_gather(piece, "ctx", axis=1, tiled=True, axis_index_groups=groups)
        return [whole], [jnp.int32(0)]
    half = wide // 2
    along_x, along_y = send(piece, 2, 0), send(piece, 4, 0)
    first, second = send(along_x[:, :half], 4, 0), send(along_y[:, half:], 2, 0)
    far = (chip ^ 3) * wide
    return (
        [piece, along_x, along_y, first, second],
        [chip * wide, (chip ^ 1) * wide, (chip ^ 2) * wide, far, far + half],
    )


def on_device(query, key, value, block_mask, out_weight, cotangent):
    rows, width = query.shape
    heads = width // DH
    shards, count = lax.axis_size("ctx"), lax.axis_size("head")
    model = out_weight.shape[1]
    own = rows // count
    scale = 1.0 / math.sqrt(DH * rows * shards)
    blocks = block_mask.shape[0]
    ctx, place = lax.axis_index("ctx"), lax.axis_index("head")
    core, chip, chips = ctx & 1, ctx >> 1, shards // 2
    place1, core1 = place.reshape(1), core.reshape(1)
    square = rows * rows * DH * heads

    weight = lax.dynamic_slice_in_dim(out_weight, core * DH, DH, 0)
    wide = model // chips
    piece = lax.dynamic_slice_in_dim(weight, chip * wide, wide, 1)
    shifts = sorted(range(1, count), key=lambda s: min(s, count - s))
    arrived = {s: send(piece, 0, s) for s in shifts}
    mate_cotangent = send(cotangent, 1, 0)

    own_state = jnp.einsum(
        "jhd,jhe->hde",
        key.reshape(rows, heads, DH),
        value.reshape(rows, heads, DH),
        preferred_element_type=F32,
    )
    linear_state = carried_in(own_state, False)
    probs, inner, soft, pre = call(
        functools.partial(forward_kernel, scale),
        [((heads, rows, rows), BF16)] * 2 + [((rows, width), F32)] * 2,
        [query, key, value],
        6 * square,
        [block_mask],
    )

    def grads(chunks, places):
        return call(
            grad_kernel,
            [((own, DH), BF16)] * 2,
            [cotangent, mate_cotangent, *chunks],
            4 * own * DH * model,
            [jnp.stack(places)],
        )

    chunks = {}
    mine, mate = [None] * count, [None] * count
    mine[0], other = grads([weight], [jnp.int32(0)])
    mate[0] = send(other, 1, 0)
    for s in shifts:
        chunks[s], places = spread(arrived[s], chip, chips)
        here, other = grads(chunks[s], places)
        mine[s], mate[s] = send(here, 0, -s), send(other, 1, -s)

    attn = call(
        functools.partial(attn_kernel, scale),
        [((own, width), BF16)] * count,
        [query, pre, linear_state],
        4 * rows * width * DH,
        [place1],
    )
    attn = [attn[0]] + [send(attn[s], 0, s) for s in range(1, count)]
    across = jnp.stack([lax.dynamic_slice_in_dim(a, (1 - core) * DH, DH, 1) for a in attn])
    across = send(across, 1, 0)
    part, mate_part = call(
        functools.partial(mixed_kernel, count),
        [((own, model), F32)] * 2,
        [*attn, across, weight, *(a for s in range(1, count) for a in chunks[s])],
        4 * own * DH * count * model,
        [jnp.stack(places), core1],
    )
    mixed = (part + send(mate_part, 1, 0)).astype(BF16)

    g, own_grad = call(
        functools.partial(collect_kernel, scale),
        [((rows, width), BF16), ((heads, DH, DH), F32)],
        [query, *mine, *mate],
        2 * rows * width * DH,
        [jnp.stack([place, core])],
    )
    grad_state = carried_in(own_grad, True)
    grad_query, dk, dv = call(
        functools.partial(backward_kernel, scale, blocks),
        [((rows, width), BF16)] + [((rows, width), F32)] * 2,
        [query, key, value, g, probs, inner, soft, linear_state],
        14 * square,
    )
    grad_key, grad_value = call(
        close_kernel,
        [((rows, width), BF16)] * 2,
        [key, value, dk, dv, grad_state],
        8 * rows * width * DH,
    )
    return mixed, grad_query, grad_key, grad_value


def solution(mesh):
    return jax.shard_map(
        on_device,
        mesh=mesh,
        in_specs=(
            P("ctx", "head"),
            P("ctx", "head"),
            P("ctx", "head"),
            P("ctx", None),
            P("head", None),
            P(("ctx", "head"), None),
        ),
        out_specs=(P(("ctx", "head"), None), P("ctx", "head"), P("ctx", "head"), P("ctx", "head")),
        check_vma=False,
    )
```

time: 151 us -> 114 us (0.75)
  waiting for transfers between devices: 76.8 us -> 30.8 us
  starting transfers between devices: 15.2 us -> 44.8 us
  matrix products: 26.5 us -> 1.13 us
  Pallas kernels: 0 us -> 15.6 us
  between operations: 14.3 us -> 0.95 us
  local copies, waits for them, and re-layouts: 14.4 us -> 17.8 us
    all_gather x1 -> x0, waiting for transfers between devices: 65.3 us -> none  [on_device(): weight = lax.all_gather(part, ('head', 'ctx'), axis=0, tiled=True)]
    ppermute x6 -> x34, starting transfers between devices: 7.83 us -> 44.8 us  [send(): return lax.ppermute(x, ('ctx', 'head'), pairs)]
    ppermute x6 -> x34, waiting for transfers between devices: 6.31 us -> 30.8 us  [send(): return lax.ppermute(x, ('ctx', 'head'), pairs)]
    dot_general x18 -> x1, matrix products: 24.9 us -> 1.13 us  [on_device(): jnp.einsum('jhd,jhe->hde', key.reshape(rows, heads, DH), value.reshape(ro...]
    pallas_call x0 -> x10, Pallas kernels: none -> 15.6 us  [call(): pl.pallas_call(body, out_shape=[jax.ShapeDtypeStruct(s, t) for s, t in ou...]
    all_to_all x2 -> x0, starting transfers between devices: 7.36 us -> none  [the longest x1 3.99 us: on_device(): attn_own = lax.all_to_all(attn, 'head', 0, 1, tiled=True)]
    unnamed x35 -> x68, local copies, waits for them, and re-layouts: 5.29 us -> 12 us
    all_to_all x2 -> x0, waiting for transfers between devices: 5.22 us -> none  [the longest x1 5.22 us: on_device(): grad_attn = lax.all_to_all(grad_own, 'head', 1, 0, tiled=True)]
  transfers between devices with their start and end apart: 9 -> 34, of which waited for: 4 -> 17; matrix products, arithmetic and copies ran while one was open for 20% -> 4% of each run, Pallas kernels for 0% -> 14%
where the time goes in v2:
time: 114 us
  starting transfers between devices  44.8 us (39%)
  waiting for transfers between devices  30.8 us (27%)
  local copies, waits for them, and re-layouts  17.8 us (16%)
  Pallas kernels  15.6 us (14%)
  other arithmetic  2.64 us (2%)
    ppermute x34, starting transfers between devices, send(): return lax.ppermute(x, ('ctx', 'head'), pairs)  44.8 us
    ppermute x34, waiting for transfers between devices, send(): return lax.ppermute(x, ('ctx', 'head'), pairs)  30.8 us
    pallas_call x10, Pallas kernels, call(): pl.pallas_call(body, out_shape=[jax.ShapeDtypeStruct(s, t) for s, t in ou...  15.6 us
    unnamed x68, local copies, waits for them, and re-layouts  12 us
    convert_element_type x1, other arithmetic, on_device(): mixed = (part + send(mate_part, 1, 0)).astype(BF16)  2.44 us
  transfers between devices with their start and end apart: 34, of which 17 were waited for; matrix products, arithmetic and copies ran while one was open for 4% of the time, Pallas kernels for 14%

profile of v2, /device:TPU:0, one launch (start us, length us, event | category | flops | bytes accessed | tf_op | source)
XLA Modules:
  0.0 113.8 jit_solution(2925870508359083678)
XLA Ops:
  0.7 1.1 %copy.12 = bf16[384,256]{0,1:T(8,128)(2,1)S(1)} copy(bf16[384,256]{1,0:T(8,128)(2,1)} %k_ref.5) | data formatting | bytes 393216 | tf_op jit(solution)/shard_map/reshape | solution.py:265
  1.8 1.1 fusion
  3.5 1.1 dynamic_slice.23
  4.6 2.7 %collective-permute-start.7 = (bf16[128,1024]{1,0:T(8,128)(2,1)S(1)}, bf16[128,1024]{1,0:T(8,128)(2,1)S(1)}, u32[]{:S(2)}, u32[]{:S(2)}) collective-permute-start(bf16[128,1024]{1,0:T(8,128)(2,1)S(1)} %dynamic_slice.23), channel_id=1, source_target_pairs={{0,1},{1,2},{2,3},{3,0},{4,5},{5,6},{6,7},{7,4},{8,9},{9,10},{10,1... | collective-permute-start | bytes 786440 | tf_op jit(solution)/shard_map/ppermute | solution.py:209
  7.3 2.6 %collective-permute-start.12 = (bf16[128,1024]{1,0:T(8,128)(2,1)S(1)}, bf16[128,1024]{1,0:T(8,128)(2,1)S(1)}, u32[]{:S(2)}, u32[]{:S(2)}) collective-permute-start(bf16[128,1024]{1,0:T(8,128)(2,1)S(1)} %dynamic_slice.23), channel_id=1, source_target_pairs={{0,2},{1,3},{2,0},{3,1},{4,6},{5,7},{6,4},{7,5},{8,10},{9,11},{10,... | collective-permute-start | bytes 786440 | tf_op jit(solution)/shard_map/ppermute | solution.py:209
  9.9 1.6 %collective-permute-start.1 = (f32[2,128,128]{2,1,0:T(8,128)S(1)}, f32[2,128,128]{2,1,0:T(8,128)S(1)}, u32[]{:S(2)}, u32[]{:S(2)}) collective-permute-start(f32[2,128,128]{2,1,0:T(8,128)S(1)} %add.47), channel_id=1, source_target_pairs={{0,8},{1,9},{2,10},{3,11},{4,12},{5,13},{6,14},{7,15},{8,0},{9,1},... | collective-permute-start | bytes 393224 | tf_op jit(solution)/shard_map/ppermute | solution.py:209
  11.4 3.8 %collective-permute-done.1 = f32[2,128,128]{2,1,0:T(8,128)S(1)} collective-permute-done((f32[2,128,128]{2,1,0:T(8,128)S(1)}, f32[2,128,128]{2,1,0:T(8,128)S(1)}, u32[]{:S(2)}, u32[]{:S(2)}) %collective-permute-start.1) | collective-permute-done | bytes 131104 | tf_op jit(solution)/shard_map/ppermute | solution.py:209
  15.3 1.6 %collective-permute-start.2 = (f32[2,128,128]{2,1,0:T(8,128)S(1)}, f32[2,128,128]{2,1,0:T(8,128)S(1)}, u32[]{:S(2)}, u32[]{:S(2)}) collective-permute-start(f32[2,128,128]{2,1,0:T(8,128)S(1)} %add.49), channel_id=1, source_target_pairs={{0,16},{1,17},{2,18},{3,19},{4,20},{5,21},{6,22},{7,23},{8,24},{9,... | collective-permute-start | bytes 393224 | tf_op jit(solution)/shard_map/ppermute | solution.py:209
  16.9 1.4 %collective-permute-start.17 = (bf16[128,1024]{1,0:T(8,128)(2,1)S(1)}, bf16[128,1024]{1,0:T(8,128)(2,1)}, u32[]{:S(2)}, u32[]{:S(2)}) collective-permute-start(bf16[128,1024]{1,0:T(8,128)(2,1)S(1)} %dynamic_slice.23), channel_id=1, source_target_pairs={{0,3},{1,0},{2,1},{3,2},{4,7},{5,4},{6,5},{7,6},{8,11},{9,8},{10,9... | collective-permute-start | bytes 786440 | tf_op jit(solution)/shard_map/ppermute | solution.py:209
  18.2 2.3 %shard_map.93 = (bf16[2,384,384]{2,1,0:T(8,128)(2,1)S(1)}, bf16[2,384,384]{2,1,0:T(8,128)(2,1)S(1)}, f32[384,256]{1,0:T(8,128)S(1)}, f32[384,256]{1,0:T(8,128)S(1)}) custom-call(s32[3,3]{1,0:T(4,128)S(1)} %copy-done.32, bf16[384,256]{1,0:T(8,128)(2,1)S(1)} %copy-done.2, bf16[384,256]{1,0:T(8,128)(2,1)S(1)} %copy-done.1, bf16[384,256]{1,0:T(8,128)(2,1)S(1)} %copy-done.3), custom_call_target="tpu_custom_call" | custom-call | flops 226492416 | bytes 2555904 | tf_op jit(solution)/shard_map/pallas_call | solution.py:33
  22.2 1.5 %collective-permute-start.8 = (bf16[128,1024]{1,0:T(8,128)(2,1)S(1)}, bf16[128,1024]{1,0:T(8,128)(2,1)S(1)}, u32[]{:S(2)}, u32[]{:S(2)}) collective-permute-start(bf16[128,1024]{1,0:T(8,128)(2,1)S(1)} %collective-permute-done.7.refs_6_.refs_0_), channel_id=1, source_target_pairs={{0,8},{1,9},{2,10},{3,11},{4,12},{5,13},{6,14},{7,15},{8,0},{9,1},... | collective-permute-start | bytes 786440 | tf_op jit(solution)/shard_map/ppermute | solution.py:209
  24.3 3.3 %collective-permute-done.12.refs_11_.refs_0_ = bf16[128,1024]{1,0:T(8,128)(2,1)S(1)} collective-permute-done((bf16[128,1024]{1,0:T(8,128)(2,1)S(1)}, bf16[128,1024]{1,0:T(8,128)(2,1)S(1)}, u32[]{:S(2)}, u32[]{:S(2)}) %collective-permute-start.12) | collective-permute-done | bytes 262176 | tf_op jit(solution)/shard_map/ppermute | solution.py:209
  27.6 1.5 %collective-permute-start.13 = (bf16[128,1024]{1,0:T(8,128)(2,1)S(1)}, bf16[128,1024]{1,0:T(8,128)(2,1)S(1)}, u32[]{:S(2)}, u32[]{:S(2)}) collective-permute-start(bf16[128,1024]{1,0:T(8,128)(2,1)S(1)} %collective-permute-done.12.refs_11_.refs_0_), channel_id=1, source_target_pairs={{0,8},{1,9},{2,10},{3,11},{4,12},{5,13},{6,14},{7,15},{8,0},{9,1},... | collective-permute-start | bytes 786440 | tf_op jit(solution)/shard_map/ppermute | solution.py:209
  29.4 7.2 %collective-permute-start.5 = (bf16[96,256]{1,0:T(8,128)(2,1)S(1)}, bf16[96,256]{1,0:T(8,128)(2,1)S(1)}, u32[]{:S(2)}, u32[]{:S(2)}) collective-permute-start(bf16[96,256]{1,0:T(8,128)(2,1)S(1)} %get-tuple-element.33), channel_id=1, source_target_pairs={{0,3},{1,0},{2,1},{3,2},{4,7},{5,4},{6,5},{7,6},{8,11},{9,8},{10,9... | collective-permute-start | bytes 147464 | tf_op jit(solution)/shard_map/ppermute | solution.py:209
  36.6 1.7 %collective-permute-done.5.refs_3_ = bf16[96,256]{1,0:T(8,128)(2,1)S(1)} collective-permute-done((bf16[96,256]{1,0:T(8,128)(2,1)S(1)}, bf16[96,256]{1,0:T(8,128)(2,1)S(1)}, u32[]{:S(2)}, u32[]{:S(2)}) %collective-permute-start.5) | collective-permute-done | bytes 49184 | tf_op jit(solution)/shard_map/ppermute | solution.py:209
  39.2 4.1 %collective-permute-done.4.refs_2_ = bf16[96,256]{1,0:T(8,128)(2,1)S(1)} collective-permute-done((bf16[96,256]{1,0:T(8,128)(2,1)S(1)}, bf16[96,256]{1,0:T(8,128)(2,1)S(1)}, u32[]{:S(2)}, u32[]{:S(2)}) %collective-permute-start.4) | collective-permute-done | bytes 49184 | tf_op jit(solution)/shard_map/ppermute | solution.py:209
  43.3 1.9 %collective-permute-start.3 = (bf16[96,256]{1,0:T(8,128)(2,1)S(1)}, bf16[96,256]{1,0:T(8,128)(2,1)S(1)}, u32[]{:S(2)}, u32[]{:S(2)}) collective-permute-start(bf16[96,256]{1,0:T(8,128)(2,1)S(1)} %get-tuple-element.31), channel_id=1, source_target_pairs={{0,1},{1,2},{2,3},{3,0},{4,5},{5,6},{6,7},{7,4},{8,9},{9,10},{10,1... | collective-permute-start | bytes 147464 | tf_op jit(solution)/shard_map/ppermute | solution.py:209
  45.3 1.5 %collective-permute-start.14 = (bf16[128,1024]{1,0:T(8,128)(2,1)S(1)}, bf16[128,1024]{1,0:T(8,128)(2,1)S(1)}, u32[]{:S(2)}, u32[]{:S(2)}) collective-permute-start(bf16[128,1024]{1,0:T(8,128)(2,1)S(1)} %collective-permute-done.12.refs_11_.refs_0_), channel_id=1, source_target_pairs={{0,16},{1,17},{2,18},{3,19},{4,20},{5,21},{6,22},{7,23},{8,24},{9,... | collective-permute-start | bytes 786440 | tf_op jit(solution)/shard_map/ppermute | solution.py:209
  46.8 2.9 %collective-permute-done.3.refs_1_ = bf16[96,256]{1,0:T(8,128)(2,1)S(1)} collective-permute-done((bf16[96,256]{1,0:T(8,128)(2,1)S(1)}, bf16[96,256]{1,0:T(8,128)(2,1)S(1)}, u32[]{:S(2)}, u32[]{:S(2)}) %collective-permute-start.3) | collective-permute-done | bytes 49184 | tf_op jit(solution)/shard_map/ppermute | solution.py:209
  50.2 1.5 %collective-permute-start.19 = (bf16[128,1024]{1,0:T(8,128)(2,1)}, bf16[128,1024]{1,0:T(8,128)(2,1)S(1)}, u32[]{:S(2)}, u32[]{:S(2)}) collective-permute-start(bf16[128,1024]{1,0:T(8,128)(2,1)} %collective-permute-done.17.refs_16_.refs_0_), channel_id=1, source_target_pairs={{0,16},{1,17},{2,18},{3,19},{4,20},{5,21},{6,22},{7,23},{8,24},{9,... | collective-permute-start | bytes 786440 | tf_op jit(solution)/shard_map/ppermute | solution.py:209
  54.0 1.3 %collective-permute-start.11 = (bf16[128,512]{1,0:T(8,128)(2,1)}, bf16[128,512]{1,0:T(8,128)(2,1)}, u32[]{:S(2)}, u32[]{:S(2)}) collective-permute-start(bf16[128,512]{1,0:T(8,128)(2,1)} %slice.25), channel_id=1, source_target_pairs={{0,8},{1,9},{2,10},{3,11},{4,12},{5,13},{6,14},{7,15},{8,0},{9,1},... | collective-permute-start | bytes 393224 | tf_op jit(solution)/shard_map/ppermute | solution.py:209
  56.3 1.5 %collective-permute-start.15 = (bf16[128,512]{1,0:T(8,128)(2,1)}, bf16[128,512]{1,0:T(8,128)(2,1)}, u32[]{:S(2)}, u32[]{:S(2)}) collective-permute-start(bf16[128,512]{1,0:T(8,128)(2,1)} %slice.26), channel_id=1, source_target_pairs={{0,16},{1,17},{2,18},{3,19},{4,20},{5,21},{6,22},{7,23},{8,24},{9,... | collective-permute-start | bytes 393224 | tf_op jit(solution)/shard_map/ppermute | solution.py:209
  60.5 1.5 %collective-permute-start.20 = (bf16[128,512]{1,0:T(8,128)(2,1)}, bf16[128,512]{1,0:T(8,128)(2,1)}, u32[]{:S(2)}, u32[]{:S(2)}) collective-permute-start(bf16[128,512]{1,0:T(8,128)(2,1)} %slice.28), channel_id=1, source_target_pairs={{0,16},{1,17},{2,18},{3,19},{4,20},{5,21},{6,22},{7,23},{8,24},{9,... | collective-permute-start | bytes 393224 | tf_op jit(solution)/shard_map/ppermute | solution.py:209
  62.7 1.5 %collective-permute-start.21 = (bf16[128,512]{1,0:T(8,128)(2,1)}, bf16[128,512]{1,0:T(8,128)(2,1)}, u32[]{:S(2)}, u32[]{:S(2)}) collective-permute-start(bf16[128,512]{1,0:T(8,128)(2,1)} %slice.29), channel_id=1, source_target_pairs={{0,8},{1,9},{2,10},{3,11},{4,12},{5,13},{6,14},{7,15},{8,0},{9,1},... | collective-permute-start | bytes 393224 | tf_op jit(solution)/shard_map/ppermute | solution.py:209
  64.5 1.3 %collective-permute-done.20.refs_19_.refs_3_ = bf16[128,512]{1,0:T(8,128)(2,1)} collective-permute-done((bf16[128,512]{1,0:T(8,128)(2,1)}, bf16[128,512]{1,0:T(8,128)(2,1)}, u32[]{:S(2)}, u32[]{:S(2)}) %collective-permute-start.20) | collective-permute-done | bytes 131104 | tf_op jit(solution)/shard_map/ppermute | solution.py:209
  65.8 2.2 %collective-permute-done.21.refs_20_.refs_4_ = bf16[128,512]{1,0:T(8,128)(2,1)} collective-permute-done((bf16[128,512]{1,0:T(8,128)(2,1)}, bf16[128,512]{1,0:T(8,128)(2,1)}, u32[]{:S(2)}, u32[]{:S(2)}) %collective-permute-start.21) | collective-permute-done | bytes 131104 | tf_op jit(solution)/shard_map/ppermute | solution.py:209
  68.0 0.9 copy-done.5
  68.9 0.9 copy-done.7
  69.9 0.9 copy-done.13
  70.8 0.9 copy-done.15
  76.0 3.4 %shard_map.95 = (f32[96,4096]{1,0:T(8,128)S(1)}, f32[96,4096]{1,0:T(8,128)}) custom-call(s32[5]{0:T(128)S(1)} %stack.29.places, s32[1]{0:T(128)} %bitcast.5.core, bf16[96,256]{1,0:T(8,128)(2,1)S(1)} %get-tuple-element.30.refs_0_, bf16[96,256]{1,0:T(8,128)(2,1)S(1)} %copy-done.29, bf16[96,256]{1,0:T(8,128)(2,1)S(1)} %copy-done.27, ...), custom_call_target="tpu_custom_call" | custom-call | flops 805306368 | bytes 7634944 | tf_op jit(solution)/shard_map/pallas_call | solution.py:33
  79.4 1.7 %shard_map.97 = (bf16[96,128]{1,0:T(8,128)(2,1)S(1)}, bf16[96,128]{1,0:T(8,128)(2,1)S(1)}) custom-call(s32[5]{0:T(128)S(1)} %stack.29.places, bf16[96,4096]{1,0:T(8,128)(2,1)S(1)} %copy-done, bf16[96,4096]{1,0:T(8,128)(2,1)S(1)} %collective-permute-done.23.mate_ref, bf16[128,1024]{1,0:T(8,128)(2,1)S(1)} %copy-done.15, ...), custom_call_target="tpu_custom_call" | custom-call | flops 201326592 | bytes 2670592 | tf_op jit(solution)/shard_map/pallas_call | solution.py:33
  81.0 2.5 %collective-permute-start.24 = (bf16[96,128]{1,0:T(8,128)(2,1)S(1)}, bf16[96,128]{1,0:T(8,128)(2,1)S(1)}, u32[]{:S(2)}, u32[]{:S(2)}) collective-permute-start(bf16[96,128]{1,0:T(8,128)(2,1)S(1)} %get-tuple-element.37), channel_id=1, source_target_pairs={{0,3},{1,0},{2,1},{3,2},{4,7},{5,4},{6,5},{7,6},{8,11},{9,8},{10,9... | collective-permute-start | bytes 73736 | tf_op jit(solution)/shard_map/ppermute | solution.py:209
  83.5 1.5 %shard_map.98 = (bf16[96,128]{1,0:T(8,128)(2,1)S(1)}, bf16[96,128]{1,0:T(8,128)(2,1)S(1)}) custom-call(s32[5]{0:T(128)S(1)} %stack.29.places, bf16[96,4096]{1,0:T(8,128)(2,1)S(1)} %copy-done, bf16[96,4096]{1,0:T(8,128)(2,1)S(1)} %collective-permute-done.23.mate_ref, bf16[128,1024]{1,0:T(8,128)(2,1)S(1)} %copy-done.13, ...), custom_call_target="tpu_custom_call" | custom-call | flops 201326592 | bytes 2670592 | tf_op jit(solution)/shard_map/pallas_call | solution.py:33
  85.1 0.9 collective-permute-start.25
  86.0 1.6 %shard_map.99 = (bf16[96,128]{1,0:T(8,128)(2,1)S(1)}, bf16[96,128]{1,0:T(8,128)(2,1)S(1)}) custom-call(s32[5]{0:T(128)S(1)} %stack.29.places, bf16[96,4096]{1,0:T(8,128)(2,1)S(1)} %copy-done, bf16[96,4096]{1,0:T(8,128)(2,1)S(1)} %collective-permute-done.23.mate_ref, bf16[128,1024]{1,0:T(8,128)(2,1)} %collective-permute-done.17.refs_16_.refs_0_, ...), custom_call_target="tpu_custom_call" | custom-call | flops 201326592 | bytes 2670592 | tf_op jit(solution)/shard_map/pallas_call | solution.py:33
  87.7 2.1 %collective-permute-start.26 = (bf16[96,128]{1,0:T(8,128)(2,1)S(1)}, bf16[96,128]{1,0:T(8,128)(2,1)S(1)}, u32[]{:S(2)}, u32[]{:S(2)}) collective-permute-start(bf16[96,128]{1,0:T(8,128)(2,1)S(1)} %get-tuple-element.39), channel_id=1, source_target_pairs={{0,1},{1,2},{2,3},{3,0},{4,5},{5,6},{6,7},{7,4},{8,9},{9,10},{10,1... | collective-permute-start | bytes 73736 | tf_op jit(solution)/shard_map/ppermute | solution.py:209
  89.7 1.2 %collective-permute-start.28 = (bf16[96,128]{1,0:T(8,128)(2,1)S(1)}, bf16[96,128]{1,0:T(8,128)(2,1)S(1)}, u32[]{:S(2)}, u32[]{:S(2)}) collective-permute-start(bf16[96,128]{1,0:T(8,128)(2,1)S(1)} %get-tuple-element.41), channel_id=1, source_target_pairs={{0,7},{1,4},{2,5},{3,6},{4,3},{5,0},{6,1},{7,2},{8,15},{9,12},{10,... | collective-permute-start | bytes 73736 | tf_op jit(solution)/shard_map/ppermute | solution.py:209
  93.4 2.3 %collective-permute-done.29.refs_6_ = bf16[96,128]{1,0:T(8,128)(2,1)S(1)} collective-permute-done((bf16[96,128]{1,0:T(8,128)(2,1)S(1)}, bf16[96,128]{1,0:T(8,128)(2,1)S(1)}, u32[]{:S(2)}, u32[]{:S(2)}) %collective-permute-start.29) | collective-permute-done | bytes 24608 | tf_op jit(solution)/shard_map/ppermute | solution.py:209
  95.7 1.5 %collective-permute-done.30.refs_7_ = bf16[96,128]{1,0:T(8,128)(2,1)S(1)} collective-permute-done((bf16[96,128]{1,0:T(8,128)(2,1)S(1)}, bf16[96,128]{1,0:T(8,128)(2,1)S(1)}, u32[]{:S(2)}, u32[]{:S(2)}) %collective-permute-start.30) | collective-permute-done | bytes 24608 | tf_op jit(solution)/shard_map/ppermute | solution.py:209
  98.3 1.1 collective-permute-done.31
  99.5 1.4 %collective-permute-start.32 = (f32[2,128,128]{2,1,0:T(8,128)S(1)}, f32[2,128,128]{2,1,0:T(8,128)S(1)}, u32[]{:S(2)}, u32[]{:S(2)}) collective-permute-start(f32[2,128,128]{2,1,0:T(8,128)S(1)} %add.55), channel_id=1, source_target_pairs={{0,8},{1,9},{2,10},{3,11},{4,12},{5,13},{6,14},{7,15},{8,0},{9,1},... | collective-permute-start | bytes 393224 | tf_op jit(solution)/shard_map/ppermute | solution.py:209
  100.9 4.3 %collective-permute-done.32 = f32[2,128,128]{2,1,0:T(8,128)S(1)} collective-permute-done((f32[2,128,128]{2,1,0:T(8,128)S(1)}, f32[2,128,128]{2,1,0:T(8,128)S(1)}, u32[]{:S(2)}, u32[]{:S(2)}) %collective-permute-start.32) | collective-permute-done | bytes 131104 | tf_op jit(solution)/shard_map/ppermute | solution.py:209
  105.2 1.0 collective-permute-start.33
  106.2 1.1 copy-done.19
  107.3 2.4 %shard_map.101 = (bf16[384,256]{1,0:T(8,128)(2,1)}, f32[384,256]{1,0:T(8,128)S(1)}, f32[384,256]{1,0:T(8,128)S(1)}) custom-call(bf16[384,256]{1,0:T(8,128)(2,1)S(1)} %copy-done.2, bf16[384,256]{1,0:T(8,128)(2,1)S(1)} %copy-done.1, bf16[384,256]{1,0:T(8,128)(2,1)S(1)} %copy-done.3, bf16[384,256]{1,0:T(8,128)(2,1)S(1)} %get-tuple-element.44.g_ref, ...), custom_call_target="tpu_custom_call" | custom-call | flops 528482304 | bytes 3473408 | tf_op jit(solution)/shard_map/pallas_call | solution.py:33
  110.2 1.1 shard_map.102
  111.3 2.4 %add_convert_fusion = bf16[96,4096]{1,0:T(8,128)(2,1)} fusion(f32[96,4096]{1,0:T(8,128)S(1)} %copy-done.9, f32[96,4096]{1,0:T(8,128)} %collective-permute-done.22), kind=kLoop, calls=%fused_computation | loop fusion | flops 786432 | bytes 3932160 | tf_op jit(solution)/shard_map/convert_element_type | solution.py:313
  (122 shorter events, 19.7 us)
Async XLA Ops:
  0.6 17.6 %copy-start.1 = (bf16[384,256]{1,0:T(8,128)(2,1)S(1)}, bf16[384,256]{1,0:T(8,128)(2,1)}, u32[]{:S(2)}) copy-start(bf16[384,256]{1,0:T(8,128)(2,1)} %k_ref.5) | copy-start | bytes 589828
  0.6 17.6 %copy-start.3 = (bf16[384,256]{1,0:T(8,128)(2,1)S(1)}, bf16[384,256]{1,0:T(8,128)(2,1)}, u32[]{:S(2)}) copy-start(bf16[384,256]{1,0:T(8,128)(2,1)} %v_ref.5) | copy-start | bytes 589828
  0.7 17.6 %copy-start.2 = (bf16[384,256]{1,0:T(8,128)(2,1)S(1)}, bf16[384,256]{1,0:T(8,128)(2,1)}, u32[]{:S(2)}) copy-start(bf16[384,256]{1,0:T(8,128)(2,1)} %q_ref.7) | copy-start | bytes 589828
  0.7 17.6 %copy-start.32 = (s32[3,3]{1,0:T(4,128)S(1)}, s32[3,3]{1,0:T(4,128)}, u32[]{:S(2)}) copy-start(s32[3,3]{1,0:T(4,128)} %mask.1) | copy-start | bytes 112
  3.0 6.9 %collective-permute-start = (f32[2,128,128]{2,1,0:T(8,128)S(1)}, f32[2,128,128]{2,1,0:T(8,128)S(1)}, u32[]{:S(2)}, u32[]{:S(2)}) collective-permute-start(f32[2,128,128]{2,1,0:T(8,128)S(1)} %fusion), channel_id=1, source_target_pairs={{0,4},{1,5},{2,6},{3,7},{4,0},{5,1},{6,2},{7,3},{8,12},{9,13},{10,... | collective-permute-start | bytes 393224 | tf_op jit(solution)/shard_map/ppermute | solution.py:209
  4.6 17.6 %collective-permute-start.7 = (bf16[128,1024]{1,0:T(8,128)(2,1)S(1)}, bf16[128,1024]{1,0:T(8,128)(2,1)S(1)}, u32[]{:S(2)}, u32[]{:S(2)}) collective-permute-start(bf16[128,1024]{1,0:T(8,128)(2,1)S(1)} %dynamic_slice.23), channel_id=1, source_target_pairs={{0,1},{1,2},{2,3},{3,0},{4,5},{5,6},{6,7},{7,4},{8,9},{9,10},{10,1... | collective-permute-start | bytes 786440 | tf_op jit(solution)/shard_map/ppermute | solution.py:209
  7.3 20.3 %collective-permute-start.12 = (bf16[128,1024]{1,0:T(8,128)(2,1)S(1)}, bf16[128,1024]{1,0:T(8,128)(2,1)S(1)}, u32[]{:S(2)}, u32[]{:S(2)}) collective-permute-start(bf16[128,1024]{1,0:T(8,128)(2,1)S(1)} %dynamic_slice.23), channel_id=1, source_target_pairs={{0,2},{1,3},{2,0},{3,1},{4,6},{5,7},{6,4},{7,5},{8,10},{9,11},{10,... | collective-permute-start | bytes 786440 | tf_op jit(solution)/shard_map/ppermute | solution.py:209
  9.9 5.4 %collective-permute-start.1 = (f32[2,128,128]{2,1,0:T(8,128)S(1)}, f32[2,128,128]{2,1,0:T(8,128)S(1)}, u32[]{:S(2)}, u32[]{:S(2)}) collective-permute-start(f32[2,128,128]{2,1,0:T(8,128)S(1)} %add.47), channel_id=1, source_target_pairs={{0,8},{1,9},{2,10},{3,11},{4,12},{5,13},{6,14},{7,15},{8,0},{9,1},... | collective-permute-start | bytes 393224 | tf_op jit(solution)/shard_map/ppermute | solution.py:209
  15.3 13.8 %collective-permute-start.2 = (f32[2,128,128]{2,1,0:T(8,128)S(1)}, f32[2,128,128]{2,1,0:T(8,128)S(1)}, u32[]{:S(2)}, u32[]{:S(2)}) collective-permute-start(f32[2,128,128]{2,1,0:T(8,128)S(1)} %add.49), channel_id=1, source_target_pairs={{0,16},{1,17},{2,18},{3,19},{4,20},{5,21},{6,22},{7,23},{8,24},{9,... | collective-permute-start | bytes 393224 | tf_op jit(solution)/shard_map/ppermute | solution.py:209
  16.9 28.4 %collective-permute-start.17 = (bf16[128,1024]{1,0:T(8,128)(2,1)S(1)}, bf16[128,1024]{1,0:T(8,128)(2,1)}, u32[]{:S(2)}, u32[]{:S(2)}) collective-permute-start(bf16[128,1024]{1,0:T(8,128)(2,1)S(1)} %dynamic_slice.23), channel_id=1, source_target_pairs={{0,3},{1,0},{2,1},{3,2},{4,7},{5,4},{6,5},{7,6},{8,11},{9,8},{10,9... | collective-permute-start | bytes 786440 | tf_op jit(solution)/shard_map/ppermute | solution.py:209
  22.2 37.7 %copy-start.22 = (f32[384,256]{1,0:T(8,128)}, f32[384,256]{1,0:T(8,128)S(1)}, u32[]{:S(2)}) copy-start(f32[384,256]{1,0:T(8,128)S(1)} %get-tuple-element.47.soft_ref) | copy-start | bytes 1179652
  22.2 42.0 %copy-start.33 = (bf16[256,4096]{1,0:T(8,128)(2,1)S(1)}, bf16[256,4096]{1,0:T(8,128)(2,1)}, u32[]{:S(2)}) copy-start(bf16[256,4096]{1,0:T(8,128)(2,1)} %param.10) | copy-start | bytes 6291460
  22.2 37.6 %copy-start.14 = (bf16[128,1024]{1,0:T(8,128)(2,1)}, bf16[128,1024]{1,0:T(8,128)(2,1)S(1)}, u32[]{:S(2)}) copy-start(bf16[128,1024]{1,0:T(8,128)(2,1)S(1)} %collective-permute-done.7.refs_6_.refs_0_) | copy-start | bytes 786436
  22.2 28.0 %collective-permute-start.8 = (bf16[128,1024]{1,0:T(8,128)(2,1)S(1)}, bf16[128,1024]{1,0:T(8,128)(2,1)S(1)}, u32[]{:S(2)}, u32[]{:S(2)}) collective-permute-start(bf16[128,1024]{1,0:T(8,128)(2,1)S(1)} %collective-permute-done.7.refs_6_.refs_0_), channel_id=1, source_target_pairs={{0,8},{1,9},{2,10},{3,11},{4,12},{5,13},{6,14},{7,15},{8,0},{9,1},... | collective-permute-start | bytes 786440 | tf_op jit(solution)/shard_map/ppermute | solution.py:209
  23.7 28.0 %collective-permute-start.9 = (bf16[128,1024]{1,0:T(8,128)(2,1)S(1)}, bf16[128,1024]{1,0:T(8,128)(2,1)S(1)}, u32[]{:S(2)}, u32[]{:S(2)}) collective-permute-start(bf16[128,1024]{1,0:T(8,128)(2,1)S(1)} %collective-permute-done.7.refs_6_.refs_0_), channel_id=1, source_target_pairs={{0,16},{1,17},{2,18},{3,19},{4,20},{5,21},{6,22},{7,23},{8,24},{9,... | collective-permute-start | bytes 786440 | tf_op jit(solution)/shard_map/ppermute | solution.py:209
  27.6 32.3 %copy-start.12 = (bf16[128,1024]{1,0:T(8,128)(2,1)}, bf16[128,1024]{1,0:T(8,128)(2,1)S(1)}, u32[]{:S(2)}) copy-start(bf16[128,1024]{1,0:T(8,128)(2,1)S(1)} %collective-permute-done.12.refs_11_.refs_0_) | copy-start | bytes 786436
  27.6 24.8 %collective-permute-start.13 = (bf16[128,1024]{1,0:T(8,128)(2,1)S(1)}, bf16[128,1024]{1,0:T(8,128)(2,1)S(1)}, u32[]{:S(2)}, u32[]{:S(2)}) collective-permute-start(bf16[128,1024]{1,0:T(8,128)(2,1)S(1)} %collective-permute-done.12.refs_11_.refs_0_), channel_id=1, source_target_pairs={{0,8},{1,9},{2,10},{3,11},{4,12},{5,13},{6,14},{7,15},{8,0},{9,1},... | collective-permute-start | bytes 786440 | tf_op jit(solution)/shard_map/ppermute | solution.py:209
  29.1 35.0 %copy-start.10 = (f32[2,128,128]{2,1,0:T(8,128)}, f32[2,128,128]{2,1,0:T(8,128)S(1)}, u32[]{:S(2)}) copy-start(f32[2,128,128]{2,1,0:T(8,128)S(1)} %select_add_fusion.1.state_ref) | copy-start | bytes 393220
  29.4 8.9 %collective-permute-start.5 = (bf16[96,256]{1,0:T(8,128)(2,1)S(1)}, bf16[96,256]{1,0:T(8,128)(2,1)S(1)}, u32[]{:S(2)}, u32[]{:S(2)}) collective-permute-start(bf16[96,256]{1,0:T(8,128)(2,1)S(1)} %get-tuple-element.33), channel_id=1, source_target_pairs={{0,3},{1,0},{2,1},{3,2},{4,7},{5,4},{6,5},{7,6},{8,11},{9,8},{10,9... | collective-permute-start | bytes 147464 | tf_op jit(solution)/shard_map/ppermute | solution.py:209
  38.4 8.4 %copy-start.24 = (bf16[96,256]{1,0:T(8,128)(2,1)}, bf16[96,256]{1,0:T(8,128)(2,1)S(1)}, u32[]{:S(2)}) copy-start(bf16[96,256]{1,0:T(8,128)(2,1)S(1)} %collective-permute-done.5.refs_3_) | copy-start | bytes 147460
  38.4 5.0 %collective-permute-start.4 = (bf16[96,256]{1,0:T(8,128)(2,1)S(1)}, bf16[96,256]{1,0:T(8,128)(2,1)S(1)}, u32[]{:S(2)}, u32[]{:S(2)}) collective-permute-start(bf16[96,256]{1,0:T(8,128)(2,1)S(1)} %get-tuple-element.32), channel_id=1, source_target_pairs={{0,2},{1,3},{2,0},{3,1},{4,6},{5,7},{6,4},{7,5},{8,10},{9,11},{10,... | collective-permute-start | bytes 147464 | tf_op jit(solution)/shard_map/ppermute | solution.py:209
  43.3 6.3 %collective-permute-start.3 = (bf16[96,256]{1,0:T(8,128)(2,1)S(1)}, bf16[96,256]{1,0:T(8,128)(2,1)S(1)}, u32[]{:S(2)}, u32[]{:S(2)}) collective-permute-start(bf16[96,256]{1,0:T(8,128)(2,1)S(1)} %get-tuple-element.31), channel_id=1, source_target_pairs={{0,1},{1,2},{2,3},{3,0},{4,5},{5,6},{6,7},{7,4},{8,9},{9,10},{10,1... | collective-permute-start | bytes 147464 | tf_op jit(solution)/shard_map/ppermute | solution.py:209
  45.3 8.7 %collective-permute-start.14 = (bf16[128,1024]{1,0:T(8,128)(2,1)S(1)}, bf16[128,1024]{1,0:T(8,128)(2,1)S(1)}, u32[]{:S(2)}, u32[]{:S(2)}) collective-permute-start(bf16[128,1024]{1,0:T(8,128)(2,1)S(1)} %collective-permute-done.12.refs_11_.refs_0_), channel_id=1, source_target_pairs={{0,16},{1,17},{2,18},{3,19},{4,20},{5,21},{6,22},{7,23},{8,24},{9,... | collective-permute-start | bytes 786440 | tf_op jit(solution)/shard_map/ppermute | solution.py:209
  49.7 6.6 %collective-permute-start.18 = (bf16[128,1024]{1,0:T(8,128)(2,1)}, bf16[128,1024]{1,0:T(8,128)(2,1)S(1)}, u32[]{:S(2)}, u32[]{:S(2)}) collective-permute-start(bf16[128,1024]{1,0:T(8,128)(2,1)} %collective-permute-done.17.refs_16_.refs_0_), channel_id=1, source_target_pairs={{0,8},{1,9},{2,10},{3,11},{4,12},{5,13},{6,14},{7,15},{8,0},{9,1},... | collective-permute-start | bytes 786440 | tf_op jit(solution)/shard_map/ppermute | solution.py:209
  50.2 8.4 %collective-permute-start.19 = (bf16[128,1024]{1,0:T(8,128)(2,1)}, bf16[128,1024]{1,0:T(8,128)(2,1)S(1)}, u32[]{:S(2)}, u32[]{:S(2)}) collective-permute-start(bf16[128,1024]{1,0:T(8,128)(2,1)} %collective-permute-done.17.refs_16_.refs_0_), channel_id=1, source_target_pairs={{0,16},{1,17},{2,18},{3,19},{4,20},{5,21},{6,22},{7,23},{8,24},{9,... | collective-permute-start | bytes 786440 | tf_op jit(solution)/shard_map/ppermute | solution.py:209
  51.8 10.2 %collective-permute-start.10 = (bf16[128,512]{1,0:T(8,128)(2,1)S(1)}, bf16[128,512]{1,0:T(8,128)(2,1)S(1)}, u32[]{:S(2)}, u32[]{:S(2)}) collective-permute-start(bf16[128,512]{1,0:T(8,128)(2,1)S(1)} %slice.24), channel_id=1, source_target_pairs={{0,16},{1,17},{2,18},{3,19},{4,20},{5,21},{6,22},{7,23},{8,24},{9,... | collective-permute-start | bytes 393224 | tf_op jit(solution)/shard_map/ppermute | solution.py:209
  52.4 7.5 %collective-permute-start.6 = (bf16[4,96,128]{2,1,0:T(8,128)(2,1)S(1)}, bf16[4,96,128]{2,1,0:T(8,128)(2,1)S(1)}, u32[]{:S(2)}, u32[]{:S(2)}) collective-permute-start(bf16[4,96,128]{2,1,0:T(8,128)(2,1)S(1)} %pad_maximum_fusion), channel_id=1, source_target_pairs={{0,4},{1,5},{2,6},{3,7},{4,0},{5,1},{6,2},{7,3},{8,12},{9,13},{10,... | collective-permute-start | bytes 294920 | tf_op jit(solution)/shard_map/ppermute | solution.py:209
  53.1 11.2 %copy-start = (bf16[96,4096]{1,0:T(8,128)(2,1)S(1)}, bf16[96,4096]{1,0:T(8,128)(2,1)}, u32[]{:S(2)}) copy-start(bf16[96,4096]{1,0:T(8,128)(2,1)} %mine_ref.7) | copy-start | bytes 2359300
  54.0 10.4 %collective-permute-start.11 = (bf16[128,512]{1,0:T(8,128)(2,1)}, bf16[128,512]{1,0:T(8,128)(2,1)}, u32[]{:S(2)}, u32[]{:S(2)}) collective-permute-start(bf16[128,512]{1,0:T(8,128)(2,1)} %slice.25), channel_id=1, source_target_pairs={{0,8},{1,9},{2,10},{3,11},{4,12},{5,13},{6,14},{7,15},{8,0},{9,1},... | collective-permute-start | bytes 393224 | tf_op jit(solution)/shard_map/ppermute | solution.py:209
  56.3 8.2 %collective-permute-start.15 = (bf16[128,512]{1,0:T(8,128)(2,1)}, bf16[128,512]{1,0:T(8,128)(2,1)}, u32[]{:S(2)}, u32[]{:S(2)}) collective-permute-start(bf16[128,512]{1,0:T(8,128)(2,1)} %slice.26), channel_id=1, source_target_pairs={{0,16},{1,17},{2,18},{3,19},{4,20},{5,21},{6,22},{7,23},{8,24},{9,... | collective-permute-start | bytes 393224 | tf_op jit(solution)/shard_map/ppermute | solution.py:209
  58.6 5.8 %collective-permute-start.16 = (bf16[128,512]{1,0:T(8,128)(2,1)}, bf16[128,512]{1,0:T(8,128)(2,1)}, u32[]{:S(2)}, u32[]{:S(2)}) collective-permute-start(bf16[128,512]{1,0:T(8,128)(2,1)} %slice.27), channel_id=1, source_target_pairs={{0,8},{1,9},{2,10},{3,11},{4,12},{5,13},{6,14},{7,15},{8,0},{9,1},... | collective-permute-start | bytes 393224 | tf_op jit(solution)/shard_map/ppermute | solution.py:209
  60.5 5.3 %collective-permute-start.20 = (bf16[128,512]{1,0:T(8,128)(2,1)}, bf16[128,512]{1,0:T(8,128)(2,1)}, u32[]{:S(2)}, u32[]{:S(2)}) collective-permute-start(bf16[128,512]{1,0:T(8,128)(2,1)} %slice.28), channel_id=1, source_target_pairs={{0,16},{1,17},{2,18},{3,19},{4,20},{5,21},{6,22},{7,23},{8,24},{9,... | collective-permute-start | bytes 393224 | tf_op jit(solution)/shard_map/ppermute | solution.py:209
  62.7 5.3 %collective-permute-start.21 = (bf16[128,512]{1,0:T(8,128)(2,1)}, bf16[128,512]{1,0:T(8,128)(2,1)}, u32[]{:S(2)}, u32[]{:S(2)}) collective-permute-start(bf16[128,512]{1,0:T(8,128)(2,1)} %slice.29), channel_id=1, source_target_pairs={{0,8},{1,9},{2,10},{3,11},{4,12},{5,13},{6,14},{7,15},{8,0},{9,1},... | collective-permute-start | bytes 393224 | tf_op jit(solution)/shard_map/ppermute | solution.py:209
  64.3 15.0 %collective-permute-start.23 = (bf16[96,4096]{1,0:T(8,128)(2,1)S(1)}, bf16[96,4096]{1,0:T(8,128)(2,1)S(1)}, u32[]{:S(2)}, u32[]{:S(2)}) collective-permute-start(bf16[96,4096]{1,0:T(8,128)(2,1)S(1)} %copy-done), channel_id=1, source_target_pairs={{0,4},{1,5},{2,6},{3,7},{4,0},{5,1},{6,2},{7,3},{8,12},{9,13},{10,... | collective-permute-start | bytes 2359304 | tf_op jit(solution)/shard_map/ppermute | solution.py:209
  79.3 32.0 %collective-permute-start.22 = (f32[96,4096]{1,0:T(8,128)}, f32[96,4096]{1,0:T(8,128)}, u32[]{:S(2)}, u32[]{:S(2)}) collective-permute-start(f32[96,4096]{1,0:T(8,128)} %get-tuple-element.35), channel_id=1, source_target_pairs={{0,4},{1,5},{2,6},{3,7},{4,0},{5,1},{6,2},{7,3},{8,12},{9,13},{10,... | collective-permute-start | bytes 4718600 | tf_op jit(solution)/shard_map/ppermute | solution.py:209
  81.0 10.5 %collective-permute-start.24 = (bf16[96,128]{1,0:T(8,128)(2,1)S(1)}, bf16[96,128]{1,0:T(8,128)(2,1)S(1)}, u32[]{:S(2)}, u32[]{:S(2)}) collective-permute-start(bf16[96,128]{1,0:T(8,128)(2,1)S(1)} %get-tuple-element.37), channel_id=1, source_target_pairs={{0,3},{1,0},{2,1},{3,2},{4,7},{5,4},{6,5},{7,6},{8,11},{9,8},{10,9... | collective-permute-start | bytes 73736 | tf_op jit(solution)/shard_map/ppermute | solution.py:209
  85.1 7.1 %collective-permute-start.25 = (bf16[96,128]{1,0:T(8,128)(2,1)S(1)}, bf16[96,128]{1,0:T(8,128)(2,1)S(1)}, u32[]{:S(2)}, u32[]{:S(2)}) collective-permute-start(bf16[96,128]{1,0:T(8,128)(2,1)S(1)} %get-tuple-element.38), channel_id=1, source_target_pairs={{0,2},{1,3},{2,0},{3,1},{4,6},{5,7},{6,4},{7,5},{8,10},{9,11},{10,... | collective-permute-start | bytes 73736 | tf_op jit(solution)/shard_map/ppermute | solution.py:209
  87.7 5.7 %collective-permute-start.26 = (bf16[96,128]{1,0:T(8,128)(2,1)S(1)}, bf16[96,128]{1,0:T(8,128)(2,1)S(1)}, u32[]{:S(2)}, u32[]{:S(2)}) collective-permute-start(bf16[96,128]{1,0:T(8,128)(2,1)S(1)} %get-tuple-element.39), channel_id=1, source_target_pairs={{0,1},{1,2},{2,3},{3,0},{4,5},{5,6},{6,7},{7,4},{8,9},{9,10},{10,1... | collective-permute-start | bytes 73736 | tf_op jit(solution)/shard_map/ppermute | solution.py:209
  89.7 16.4 %copy-start.11 = (f32[2,128,128]{2,1,0:T(8,128)S(1)}, f32[2,128,128]{2,1,0:T(8,128)}, u32[]{:S(2)}) copy-start(f32[2,128,128]{2,1,0:T(8,128)} %copy-done.10) | copy-start | bytes 393220
  89.7 16.4 %copy-start.17 = (bf16[2,384,384]{2,1,0:T(8,128)(2,1)S(1)}, bf16[2,384,384]{2,1,0:T(8,128)(2,1)}, u32[]{:S(2)}) copy-start(bf16[2,384,384]{2,1,0:T(8,128)(2,1)} %copy-done.16) | copy-start | bytes 1769476
  89.7 16.4 %copy-start.23 = (f32[384,256]{1,0:T(8,128)S(1)}, f32[384,256]{1,0:T(8,128)}, u32[]{:S(2)}) copy-start(f32[384,256]{1,0:T(8,128)} %copy-done.22) | copy-start | bytes 1179652
  89.7 3.7 %collective-permute-start.28 = (bf16[96,128]{1,0:T(8,128)(2,1)S(1)}, bf16[96,128]{1,0:T(8,128)(2,1)S(1)}, u32[]{:S(2)}, u32[]{:S(2)}) collective-permute-start(bf16[96,128]{1,0:T(8,128)(2,1)S(1)} %get-tuple-element.41), channel_id=1, source_target_pairs={{0,7},{1,4},{2,5},{3,6},{4,3},{5,0},{6,1},{7,2},{8,15},{9,12},{10,... | collective-permute-start | bytes 73736 | tf_op jit(solution)/shard_map/ppermute | solution.py:209
  91.5 4.2 %collective-permute-start.29 = (bf16[96,128]{1,0:T(8,128)(2,1)S(1)}, bf16[96,128]{1,0:T(8,128)(2,1)S(1)}, u32[]{:S(2)}, u32[]{:S(2)}) collective-permute-start(bf16[96,128]{1,0:T(8,128)(2,1)S(1)} %get-tuple-element.42), channel_id=1, source_target_pairs={{0,6},{1,7},{2,4},{3,5},{4,2},{5,3},{6,0},{7,1},{8,14},{9,15},{10,... | collective-permute-start | bytes 73736 | tf_op jit(solution)/shard_map/ppermute | solution.py:209
  92.2 5.1 %collective-permute-start.30 = (bf16[96,128]{1,0:T(8,128)(2,1)S(1)}, bf16[96,128]{1,0:T(8,128)(2,1)S(1)}, u32[]{:S(2)}, u32[]{:S(2)}) collective-permute-start(bf16[96,128]{1,0:T(8,128)(2,1)S(1)} %get-tuple-element.43), channel_id=1, source_target_pairs={{0,5},{1,6},{2,7},{3,4},{4,1},{5,2},{6,3},{7,0},{8,13},{9,14},{10,... | collective-permute-start | bytes 73736 | tf_op jit(solution)/shard_map/ppermute | solution.py:209
  93.3 3.9 %collective-permute-start.27 = (bf16[96,128]{1,0:T(8,128)(2,1)S(1)}, bf16[96,128]{1,0:T(8,128)(2,1)S(1)}, u32[]{:S(2)}, u32[]{:S(2)}) collective-permute-start(bf16[96,128]{1,0:T(8,128)(2,1)S(1)} %get-tuple-element.40), channel_id=1, source_target_pairs={{0,4},{1,5},{2,6},{3,7},{4,0},{5,1},{6,2},{7,3},{8,12},{9,13},{10,... | collective-permute-start | bytes 73736 | tf_op jit(solution)/shard_map/ppermute | solution.py:209
  98.0 1.4 %collective-permute-start.31 = (f32[2,128,128]{2,1,0:T(8,128)S(1)}, f32[2,128,128]{2,1,0:T(8,128)S(1)}, u32[]{:S(2)}, u32[]{:S(2)}) collective-permute-start(f32[2,128,128]{2,1,0:T(8,128)S(1)} %get-tuple-element.51), channel_id=1, source_target_pairs={{0,4},{1,5},{2,6},{3,7},{4,0},{5,1},{6,2},{7,3},{8,12},{9,13},{10,... | collective-permute-start | bytes 393224 | tf_op jit(solution)/shard_map/ppermute | solution.py:209
  99.5 5.7 %collective-permute-start.32 = (f32[2,128,128]{2,1,0:T(8,128)S(1)}, f32[2,128,128]{2,1,0:T(8,128)S(1)}, u32[]{:S(2)}, u32[]{:S(2)}) collective-permute-start(f32[2,128,128]{2,1,0:T(8,128)S(1)} %add.55), channel_id=1, source_target_pairs={{0,8},{1,9},{2,10},{3,11},{4,12},{5,13},{6,14},{7,15},{8,0},{9,1},... | collective-permute-start | bytes 393224 | tf_op jit(solution)/shard_map/ppermute | solution.py:209
  105.2 5.0 %collective-permute-start.33 = (f32[2,128,128]{2,1,0:T(8,128)S(1)}, f32[2,128,128]{2,1,0:T(8,128)S(1)}, u32[]{:S(2)}, u32[]{:S(2)}) collective-permute-start(f32[2,128,128]{2,1,0:T(8,128)S(1)} %add.57), channel_id=1, source_target_pairs={{0,16},{1,17},{2,18},{3,19},{4,20},{5,21},{6,22},{7,23},{8,24},{9,... | collective-permute-start | bytes 393224 | tf_op jit(solution)/shard_map/ppermute | solution.py:209
  (20 other events, 38.7 us)

commit v3 on v2

--- a/solution.py
+++ b/solution.py
@@ -27,21 +27,21 @@
     return dot(a, high, dims) + dot(a, low, dims)
 
 
-def call(body, outs, args, flops, smem=(), scratch=()):
-    moved = sum(a.size * a.dtype.itemsize for a in args)
-    moved += sum(math.prod(s) * jnp.dtype(t).itemsize for s, t in outs)
+def call(body, outs, args, smem=(), after=(), room=8):
+    def kernel(*refs):
+        first = len(smem) + len(args)
+        body(*refs[:first], *refs[first + len(after) :])
+
     return pl.pallas_call(
-        body,
+        kernel,
         out_shape=[jax.ShapeDtypeStruct(s, t) for s, t in outs],
         in_specs=[pl.BlockSpec(memory_space=pltpu.SMEM) for _ in smem]
-        + [pl.BlockSpec(memory_space=pltpu.VMEM) for _ in args],
+        + [pl.BlockSpec(memory_space=pltpu.VMEM) for _ in args]
+        + [pl.BlockSpec(memory_space=pl.ANY) for _ in after],
         out_specs=[pl.BlockSpec(memory_space=pltpu.VMEM) for _ in outs],
-        scratch_shapes=list(scratch),
-        compiler_params=pltpu.CompilerParams(vmem_limit_bytes=40 * MIB),
-        cost_estimate=pl.CostEstimate(
-            flops=int(flops), bytes_accessed=int(moved), transcendentals=0
-        ),
-    )(*smem, *args)
+        compiler_params=pltpu.CompilerParams(vmem_limit_bytes=room * MIB),
+        cost_estimate=pl.CostEstimate(flops=1, bytes_accessed=1, transcendentals=0),
+    )(*smem, *args, *after)
 
 
 def lower_triangle(blk):
@@ -80,11 +80,23 @@
             pre_ref[here, cols] = soft + scale * dot(inner, v, NN)
 
 
-def attn_kernel(scale, place, q_ref, pre_ref, state_ref, *out_refs):
+def state_kernel(k_ref, v_ref, state_ref):
+    for h in range(k_ref.shape[1] // DH):
+        cols = slice(h * DH, (h + 1) * DH)
+        state_ref[h] = dot(k_ref[:, cols], v_ref[:, cols], TN)
+
+
+def attn_kernel(scale, where, q_ref, pre_ref, states_ref, *refs):
+    out_refs, state_ref = refs[:-1], refs[-1]
+    place, ctx = where[0], where[1]
     count = len(out_refs)
     own = out_refs[0].shape[0]
+    total = jnp.zeros(state_ref.shape, F32)
+    for c in range(states_ref.shape[0] - 1):
+        total = total + jnp.where(c < ctx, states_ref[c], 0.0)
+    state_ref[...] = total
     for s in range(count):
-        block = lax.rem(place[0] + s, count)
+        block = lax.rem(place + s, count)
         here = pl.ds(pl.multiple_of(block * own, own), own)
         for h in range(q_ref.shape[1] // DH):
             cols = slice(h * DH, (h + 1) * DH)
@@ -92,53 +104,56 @@
             out_refs[s][:, cols] = (pre_ref[here, cols] + scale * inter).astype(BF16)
 
 
-def grad_kernel(places, mine_ref, mate_ref, *refs):
-    chunks, (own_ref, other_ref) = refs[:-2], refs[-2:]
+def grad_kernel(whole, places, mine_ref, mate_ref, *refs):
+    chunks, outs = refs[:-2], refs[-2:]
     own = mine_ref.shape[0]
     total = None
     for j, chunk in enumerate(chunks):
-        cols = pl.ds(pl.multiple_of(places[j], DH), chunk.shape[1])
+        cols = slice(None) if whole else pl.ds(pl.multiple_of(places[j], DH), chunk.shape[1])
         left = jnp.concatenate([mine_ref[:, cols], mate_ref[:, cols]], 0)
         part = dot(left, chunk[...], NT)
         total = part if total is None else total + part
     total = total.astype(BF16)
-    own_ref[...] = total[:own]
-    other_ref[...] = total[own:]
-
-
-def mixed_kernel(count, places, core, *refs):
+    outs[0][...] = total[:own]
+    outs[1][...] = total[own:]
+
+
+def mixed_kernel(count, each, places, where, *refs):
     own_out, mate_out = refs[-2:]
     attn, mate, weight = refs[:count], refs[count], refs[count + 1]
-    chunks = refs[count + 2 : -2]
-    each = len(chunks) // (count - 1)
+    chunks = list(refs[count + 2 : -2])
+    sets = [[chunks.pop(0)[...] for _ in range(n)] for n in each]
     own = own_out.shape[0]
-    cols = pl.ds(pl.multiple_of(core[0] * DH, DH), DH)
+    cols = pl.ds(pl.multiple_of(where[2] * DH, DH), DH)
     left = jnp.concatenate(
         [jnp.concatenate([attn[s][:, cols], mate[s]], 0) for s in range(count)], 1
     )
-    for j in range(each):
-        wide = chunks[j].shape[1]
-        there = pl.ds(pl.multiple_of(places[j], DH), wide)
-        right = jnp.concatenate(
-            [weight[:, there]] + [chunks[s * each + j][...] for s in range(count - 1)], 0
-        )
+    few = min(each)
+    sets = [
+        some[: few - 1] + [jnp.concatenate(some[few - 1 :], 1) if len(some) > few else some[-1]]
+        for some in sets
+    ]
+    for j in range(few):
+        there = pl.ds(pl.multiple_of(places[j], DH), sets[0][j].shape[1])
+        right = jnp.concatenate([weight[:, there]] + [some[j] for some in sets], 0)
         part = dot(left, right, NN)
         own_out[:, there] = part[:own]
         mate_out[:, there] = part[own:]
 
 
-def collect_kernel(scale, where, q_ref, *refs):
+def collect_kernel(scale, shifts, where, q_ref, *refs):
     g_ref, state_ref = refs[-2:]
-    count = (len(refs) - 2) // 2
-    own = refs[0].shape[0]
-    place, core = where[0], where[1]
+    count = len(shifts)
+    direct, across, last = refs[:count], refs[count], refs[count + 1]
+    own = g_ref.shape[0] // count
+    place, core = where[0], where[2]
     mine = pl.ds(pl.multiple_of(core * DH, DH), DH)
     mate = pl.ds(pl.multiple_of((1 - core) * DH, DH), DH)
-    for s in range(count):
+    for n, s in enumerate(shifts):
         block = lax.rem(place + s, count)
         here = pl.ds(pl.multiple_of(block * own, own), own)
-        g_ref[here, mine] = refs[s][...]
-        g_ref[here, mate] = refs[count + s][...]
+        g_ref[here, mine] = direct[n][:own]
+        g_ref[here, mate] = across[n] if n < count - 1 else last[...]
     for h in range(q_ref.shape[1] // DH):
         cols = slice(h * DH, (h + 1) * DH)
         state_ref[h] = scale * dot(q_ref[:, cols], g_ref[:, cols], TN)
@@ -209,35 +224,45 @@
     return lax.ppermute(x, ("ctx", "head"), pairs)
 
 
-def carried_in(part, reverse):
-    place = lax.axis_index("ctx")
-    total = part
-    carried = jnp.zeros_like(part)
+def later_chips(total, chip, chips):
+    carried = jnp.zeros_like(total)
+    if chips == 4:
+        for flip in (3, 2, 1):
+            there = send(total, 2 * flip, 0)
+            carried = carried + jnp.where((chip ^ flip) > chip, there, 0.0)
+        return carried, there
     step = 1
-    while step < lax.axis_size("ctx"):
-        other = send(total, step, 0)
-        upper = (place & step) > 0
-        carried = carried + jnp.where(upper ^ reverse, other, 0.0)
-        total = total + other
+    while step < chips:
+        there = send(total, 2 * step, 0)
+        carried = carried + jnp.where((chip & step) == 0, there, 0.0)
+        total = total + there
         step *= 2
-    return carried
-
-
-def spread(piece, chip, chips):
+    return carried, there
+
+
+def spread(piece, chip, chips, way):
     wide = piece.shape[1]
     if chips != 4:
         shards = lax.axis_size("ctx")
         groups = [list(range(core, shards, 2)) for core in range(2)]
         whole = lax.all_gather(piece, "ctx", axis=1, tiled=True, axis_index_groups=groups)
         return [whole], [jnp.int32(0)]
-    half = wide // 2
-    along_x, along_y = send(piece, 2, 0), send(piece, 4, 0)
-    first, second = send(along_x[:, :half], 4, 0), send(along_y[:, half:], 2, 0)
     far = (chip ^ 3) * wide
-    return (
-        [piece, along_x, along_y, first, second],
-        [chip * wide, (chip ^ 1) * wide, (chip ^ 2) * wide, far, far + half],
-    )
+    if way == 0:
+        along_x = send(piece, 2, 0)
+        along_y = send(piece, 4, 0)
+        ends = [send(along_x, 4, 0)]
+    elif way == 1:
+        along_y = send(piece, 4, 0)
+        along_x = send(piece, 2, 0)
+        ends = [send(along_y, 2, 0)]
+    else:
+        half = wide // 2
+        along_x, along_y = send(piece, 2, 0), send(piece, 4, 0)
+        ends = [send(along_x[:, :half], 4, 0), send(along_y[:, half:], 2, 0)]
+    places = [chip * wide, (chip ^ 1) * wide, (chip ^ 2) * wide, far, far + wide // 2]
+    arrays = [piece, along_x, along_y, *ends]
+    return arrays, places[: len(arrays)]
 
 
 def on_device(query, key, value, block_mask, out_weight, cotangent):
@@ -250,87 +275,98 @@
     blocks = block_mask.shape[0]
     ctx, place = lax.axis_index("ctx"), lax.axis_index("head")
     core, chip, chips = ctx & 1, ctx >> 1, shards // 2
-    place1, core1 = place.reshape(1), core.reshape(1)
-    square = rows * rows * DH * heads
-
+    where = jnp.stack([place, ctx, core])
+    flat, states = (rows, width), (heads, DH, DH)
+
+    wide = model // chips
+    piece = lax.dynamic_slice(out_weight, (core * DH, chip * wide), (DH, wide))
     weight = lax.dynamic_slice_in_dim(out_weight, core * DH, DH, 0)
-    wide = model // chips
-    piece = lax.dynamic_slice_in_dim(weight, chip * wide, wide, 1)
     shifts = sorted(range(1, count), key=lambda s: min(s, count - s))
-    arrived = {s: send(piece, 0, s) for s in shifts}
+    arrived = {0: piece}
+    for s in shifts:
+        step = 1 if s <= count // 2 else -1
+        arrived[s] = send(arrived[(s - step) % count], 0, step)
     mate_cotangent = send(cotangent, 1, 0)
 
-    own_state = jnp.einsum(
-        "jhd,jhe->hde",
-        key.reshape(rows, heads, DH),
-        value.reshape(rows, heads, DH),
-        preferred_element_type=F32,
-    )
-    linear_state = carried_in(own_state, False)
+    (own_state,) = call(state_kernel, [(states, F32)], [key, value], after=[piece])
+    every_state = lax.all_gather(own_state, "ctx")
     probs, inner, soft, pre = call(
         functools.partial(forward_kernel, scale),
-        [((heads, rows, rows), BF16)] * 2 + [((rows, width), F32)] * 2,
+        [((heads, rows, rows), BF16)] * 2 + [(flat, F32)] * 2,
         [query, key, value],
-        6 * square,
         [block_mask],
     )
 
-    def grads(chunks, places):
+    chunks, places = {}, None
+    for n, s in enumerate(shifts):
+        chunks[s], starts = spread(arrived[s], chip, chips, min(n, 2))
+        if places is None or len(starts) > len(places):
+            places = starts
+    places = jnp.stack(places)
+
+    def grads(some, whole=False, after=()):
         return call(
-            grad_kernel,
+            functools.partial(grad_kernel, whole),
             [((own, DH), BF16)] * 2,
-            [cotangent, mate_cotangent, *chunks],
-            4 * own * DH * model,
-            [jnp.stack(places)],
+            [cotangent, mate_cotangent, *some],
+            [places],
+            after,
         )
 
-    chunks = {}
-    mine, mate = [None] * count, [None] * count
-    mine[0], other = grads([weight], [jnp.int32(0)])
-    mate[0] = send(other, 1, 0)
-    for s in shifts:
-        chunks[s], places = spread(arrived[s], chip, chips)
-        here, other = grads(chunks[s], places)
-        mine[s], mate[s] = send(here, 0, -s), send(other, 1, -s)
-
-    attn = call(
+    direct, across = [], []
+    for s in [0] + shifts[:-1]:
+        both = grads(chunks[s]) if s else grads([weight], True)
+        both = send(jnp.concatenate(both, 0), 0, -s) if s else jnp.concatenate(both, 0)
+        direct.append(both)
+        across.append(both[own:])
+    across = send(jnp.stack(across), 1, 0)
+    *attn, linear_state = call(
         functools.partial(attn_kernel, scale),
-        [((own, width), BF16)] * count,
-        [query, pre, linear_state],
-        4 * rows * width * DH,
-        [place1],
+        [((own, width), BF16)] * count + [(states, F32)],
+        [query, pre, every_state],
+        [where],
     )
     attn = [attn[0]] + [send(attn[s], 0, s) for s in range(1, count)]
-    across = jnp.stack([lax.dynamic_slice_in_dim(a, (1 - core) * DH, DH, 1) for a in attn])
-    across = send(across, 1, 0)
+    for_mate = jnp.stack([lax.dynamic_slice_in_dim(a, (1 - core) * DH, DH, 1) for a in attn])
+    for_mate = send(for_mate, 1, 0)
+
+    mine, other = grads(chunks[shifts[-1]], after=[for_mate])
+    direct.append(send(mine, 0, -shifts[-1]))
+    last = send(other, 1, -shifts[-1])
+
+    g, own_grad = call(
+        functools.partial(collect_kernel, scale, [0] + shifts),
+        [(flat, BF16), (states, F32)],
+        [query, *direct, across, last],
+        [where],
+    )
+    here = jnp.where(core == 0, own_grad[0], own_grad[1])
+    got = send(jnp.where(core == 0, own_grad[1], own_grad[0]), 1, 0)
+    total = here + got
+    later, neighbour = later_chips(total, chip, chips)
     part, mate_part = call(
-        functools.partial(mixed_kernel, count),
+        functools.partial(
+            mixed_kernel, count, [len(chunks[s]) for s in range(1, count)]
+        ),
         [((own, model), F32)] * 2,
-        [*attn, across, weight, *(a for s in range(1, count) for a in chunks[s])],
-        4 * own * DH * count * model,
-        [jnp.stack(places), core1],
+        [*attn, for_mate, weight, *(a for s in range(1, count) for a in chunks[s])],
+        [places, where],
+        after=[neighbour],
+        room=16,
     )
     mixed = (part + send(mate_part, 1, 0)).astype(BF16)
-
-    g, own_grad = call(
-        functools.partial(collect_kernel, scale),
-        [((rows, width), BF16), ((heads, DH, DH), F32)],
-        [query, *mine, *mate],
-        2 * rows * width * DH,
-        [jnp.stack([place, core])],
-    )
-    grad_state = carried_in(own_grad, True)
+    back = send(jnp.where(core == 0, later, later + here), 1, 0)
+    keep = jnp.where(core == 0, later + got, later)
+    grad_state = jnp.stack([jnp.where(core == 0, keep, back), jnp.where(core == 0, back, keep)])
+
     grad_query, dk, dv = call(
         functools.partial(backward_kernel, scale, blocks),
-        [((rows, width), BF16)] + [((rows, width), F32)] * 2,
+        [(flat, BF16)] + [(flat, F32)] * 2,
         [query, key, value, g, probs, inner, soft, linear_state],
-        14 * square,
+        after=[total],
     )
     grad_key, grad_value = call(
-        close_kernel,
-        [((rows, width), BF16)] * 2,
-        [key, value, dk, dv, grad_state],
-        8 * rows * width * DH,
+        close_kernel, [(flat, BF16)] * 2, [key, value, dk, dv, grad_state]
     )
     return mixed, grad_query, grad_key, grad_value
 

time: 114 us -> 129 us (1.13)
  between operations: 0.95 us -> 14.3 us
  starting transfers between devices: 44.8 us -> 34.6 us
  waiting for transfers between devices: 30.8 us -> 36.5 us
  local copies, waits for them, and re-layouts: 17.8 us -> 21.9 us
  Pallas kernels: 15.6 us -> 18.3 us
    ppermute x34 -> x29, starting transfers between devices: 44.8 us -> 34.5 us  [send(): return lax.ppermute(x, ('ctx', 'head'), pairs)]
    ppermute x34 -> x29, waiting for transfers between devices: 30.8 us -> 36.5 us  [send(): return lax.ppermute(x, ('ctx', 'head'), pairs)]
    unnamed x68 -> x64, local copies, waits for them, and re-layouts: 12 us -> 16.1 us
    pallas_call x10 -> x11, Pallas kernels: 15.6 us -> 18.3 us  [call(): pl.pallas_call(kernel, out_shape=[jax.ShapeDtypeStruct(s, t) for s, t in...]
    slice x6 -> x2, local copies, waits for them, and re-layouts: 3.3 us -> 2.23 us  [spread(): ends = [send(along_x[:, :half], 4, 0), send(along_y[:, half:], 2, 0)]]
  transfers between devices with their start and end apart: 34 -> 30, of which waited for: 17 -> 16; matrix products, arithmetic and copies ran while one was open for 4% -> 4% of each run, Pallas kernels for 14% -> 11%
where the time goes in v3:
time: 129 us; the launch traced here: 128 us
  waiting for transfers between devices  36.5 us (28%)
  starting transfers between devices  34.6 us (27%)
  local copies, waits for them, and re-layouts  21.9 us (17%)
  Pallas kernels  18.3 us (14%)
  between operations  14.3 us (11%)
  other arithmetic  2.63 us (2%)
    ppermute x29, waiting for transfers between devices, send(): return lax.ppermute(x, ('ctx', 'head'), pairs)  36.5 us
    ppermute x29, starting transfers between devices, send(): return lax.ppermute(x, ('ctx', 'head'), pairs)  34.5 us
    pallas_call x11, Pallas kernels, call(): pl.pallas_call(kernel, out_shape=[jax.ShapeDtypeStruct(s, t) for s, t in...  18.3 us
    unnamed x64, local copies, waits for them, and re-layouts  16.1 us
  transfers between devices with their start and end apart: 30, of which 16 were waited for; matrix products, arithmetic and copies ran while one was open for 4% of the time, Pallas kernels for 11%

profile of v3, /device:TPU:0, one launch (start us, length us, event | category | flops | bytes accessed | tf_op | source)
XLA Modules:
  0.0 128.2 jit_solution(4477546620340968667)
XLA Ops:
  7.2 1.0 dynamic_slice.18.refs_2_
  8.2 3.1 %collective-permute-start.4 = (bf16[128,1024]{1,0:T(8,128)(2,1)S(1)}, bf16[128,1024]{1,0:T(8,128)(2,1)}, u32[]{:S(2)}, u32[]{:S(2)}) collective-permute-start(bf16[128,1024]{1,0:T(8,128)(2,1)S(1)} %dynamic_slice.18.refs_2_), channel_id=1, source_target_pairs={{0,1},{1,2},{2,3},{3,0},{4,5},{5,6},{6,7},{7,4},{8,9},{9,10},{10,1... | collective-permute-start | bytes 786440 | tf_op jit(solution)/shard_map/ppermute | solution.py:224
  11.3 0.9 copy-done.2
  14.1 2.1 %collective-permute-start.13 = (bf16[128,1024]{1,0:T(8,128)(2,1)S(1)}, bf16[128,1024]{1,0:T(8,128)(2,1)}, u32[]{:S(2)}, u32[]{:S(2)}) collective-permute-start(bf16[128,1024]{1,0:T(8,128)(2,1)S(1)} %dynamic_slice.18.refs_2_), channel_id=1, source_target_pairs={{0,3},{1,0},{2,1},{3,2},{4,7},{5,4},{6,5},{7,6},{8,11},{9,8},{10,9... | collective-permute-start | bytes 786440 | tf_op jit(solution)/shard_map/ppermute | solution.py:224
  16.2 4.3 %collective-permute-done.4.refs_3_.refs_8_ = bf16[128,1024]{1,0:T(8,128)(2,1)} collective-permute-done((bf16[128,1024]{1,0:T(8,128)(2,1)S(1)}, bf16[128,1024]{1,0:T(8,128)(2,1)}, u32[]{:S(2)}, u32[]{:S(2)}) %collective-permute-start.4) | collective-permute-done | bytes 262176 | tf_op jit(solution)/shard_map/ppermute | solution.py:224
  20.6 5.6 %collective-permute-done.13.refs_3_.refs_17_ = bf16[128,1024]{1,0:T(8,128)(2,1)} collective-permute-done((bf16[128,1024]{1,0:T(8,128)(2,1)S(1)}, bf16[128,1024]{1,0:T(8,128)(2,1)}, u32[]{:S(2)}, u32[]{:S(2)}) %collective-permute-start.13) | collective-permute-done | bytes 262176 | tf_op jit(solution)/shard_map/ppermute | solution.py:224
  26.2 1.8 %collective-permute-start.15 = (bf16[128,1024]{1,0:T(8,128)(2,1)}, bf16[128,1024]{1,0:T(8,128)(2,1)}, u32[]{:S(2)}, u32[]{:S(2)}) collective-permute-start(bf16[128,1024]{1,0:T(8,128)(2,1)} %collective-permute-done.13.refs_3_.refs_17_), channel_id=1, source_target_pairs={{0,16},{1,17},{2,18},{3,19},{4,20},{5,21},{6,22},{7,23},{8,24},{9,... | collective-permute-start | bytes 786440 | tf_op jit(solution)/shard_map/ppermute | solution.py:224
  27.9 1.5 %collective-permute-start.5 = (bf16[128,1024]{1,0:T(8,128)(2,1)}, bf16[128,1024]{1,0:T(8,128)(2,1)}, u32[]{:S(2)}, u32[]{:S(2)}) collective-permute-start(bf16[128,1024]{1,0:T(8,128)(2,1)} %collective-permute-done.4.refs_3_.refs_8_), channel_id=1, source_target_pairs={{0,8},{1,9},{2,10},{3,11},{4,12},{5,13},{6,14},{7,15},{8,0},{9,1},... | collective-permute-start | bytes 786440 | tf_op jit(solution)/shard_map/ppermute | solution.py:224
  29.4 1.8 %collective-permute-done.8.refs_3_.refs_12_ = bf16[128,1024]{1,0:T(8,128)(2,1)S(1)} collective-permute-done((bf16[128,1024]{1,0:T(8,128)(2,1)}, bf16[128,1024]{1,0:T(8,128)(2,1)S(1)}, u32[]{:S(2)}, u32[]{:S(2)}) %collective-permute-start.8) | collective-permute-done | bytes 262176 | tf_op jit(solution)/shard_map/ppermute | solution.py:224
  31.2 1.5 %collective-permute-start.9 = (bf16[128,1024]{1,0:T(8,128)(2,1)S(1)}, bf16[128,1024]{1,0:T(8,128)(2,1)S(1)}, u32[]{:S(2)}, u32[]{:S(2)}) collective-permute-start(bf16[128,1024]{1,0:T(8,128)(2,1)S(1)} %collective-permute-done.8.refs_3_.refs_12_), channel_id=1, source_target_pairs={{0,8},{1,9},{2,10},{3,11},{4,12},{5,13},{6,14},{7,15},{8,0},{9,1},... | collective-permute-start | bytes 786440 | tf_op jit(solution)/shard_map/ppermute | solution.py:224
  32.7 1.5 %collective-permute-start.10 = (bf16[128,1024]{1,0:T(8,128)(2,1)S(1)}, bf16[128,1024]{1,0:T(8,128)(2,1)S(1)}, u32[]{:S(2)}, u32[]{:S(2)}) collective-permute-start(bf16[128,1024]{1,0:T(8,128)(2,1)S(1)} %collective-permute-done.8.refs_3_.refs_12_), channel_id=1, source_target_pairs={{0,16},{1,17},{2,18},{3,19},{4,20},{5,21},{6,22},{7,23},{8,24},{9,... | collective-permute-start | bytes 786440 | tf_op jit(solution)/shard_map/ppermute | solution.py:224
  34.9 2.8 %collective-permute-done.15.refs_5_.refs_19_ = bf16[128,1024]{1,0:T(8,128)(2,1)} collective-permute-done((bf16[128,1024]{1,0:T(8,128)(2,1)}, bf16[128,1024]{1,0:T(8,128)(2,1)}, u32[]{:S(2)}, u32[]{:S(2)}) %collective-permute-start.15) | collective-permute-done | bytes 262176 | tf_op jit(solution)/shard_map/ppermute | solution.py:224
  37.8 1.6 %collective-permute-start.14 = (bf16[128,1024]{1,0:T(8,128)(2,1)}, bf16[128,1024]{1,0:T(8,128)(2,1)}, u32[]{:S(2)}, u32[]{:S(2)}) collective-permute-start(bf16[128,1024]{1,0:T(8,128)(2,1)} %collective-permute-done.13.refs_3_.refs_17_), channel_id=1, source_target_pairs={{0,8},{1,9},{2,10},{3,11},{4,12},{5,13},{6,14},{7,15},{8,0},{9,1},... | collective-permute-start | bytes 786440 | tf_op jit(solution)/shard_map/ppermute | solution.py:224
  40.3 1.5 %collective-permute-start.6 = (bf16[128,1024]{1,0:T(8,128)(2,1)}, bf16[128,1024]{1,0:T(8,128)(2,1)}, u32[]{:S(2)}, u32[]{:S(2)}) collective-permute-start(bf16[128,1024]{1,0:T(8,128)(2,1)} %collective-permute-done.4.refs_3_.refs_8_), channel_id=1, source_target_pairs={{0,16},{1,17},{2,18},{3,19},{4,20},{5,21},{6,22},{7,23},{8,24},{9,... | collective-permute-start | bytes 786440 | tf_op jit(solution)/shard_map/ppermute | solution.py:224
  41.7 4.1 %collective-permute-done.9.refs_4_.refs_13_ = bf16[128,1024]{1,0:T(8,128)(2,1)S(1)} collective-permute-done((bf16[128,1024]{1,0:T(8,128)(2,1)S(1)}, bf16[128,1024]{1,0:T(8,128)(2,1)S(1)}, u32[]{:S(2)}, u32[]{:S(2)}) %collective-permute-start.9) | collective-permute-done | bytes 262176 | tf_op jit(solution)/shard_map/ppermute | solution.py:224
  45.8 1.5 %collective-permute-start.16 = (bf16[128,1024]{1,0:T(8,128)(2,1)}, bf16[128,1024]{1,0:T(8,128)(2,1)}, u32[]{:S(2)}, u32[]{:S(2)}) collective-permute-start(bf16[128,1024]{1,0:T(8,128)(2,1)} %collective-permute-done.15.refs_5_.refs_19_), channel_id=1, source_target_pairs={{0,8},{1,9},{2,10},{3,11},{4,12},{5,13},{6,14},{7,15},{8,0},{9,1},... | collective-permute-start | bytes 786440 | tf_op jit(solution)/shard_map/ppermute | solution.py:224
  48.5 1.3 %constant_dynamic-slice_fusion.refs_3_.refs_7_ = bf16[128,4096]{1,0:T(8,128)(2,1)S(1)} fusion(bf16[256,4096]{1,0:T(8,128)(2,1)} %param.10, s32[]{:T(128)S(6)} %select_n.69), kind=kLoop, calls=%fused_computation.21 | loop fusion | bytes 2097156 | tf_op jit(solution)/shard_map/dynamic_slice | solution.py:283
  49.9 2.3 %shard_map.93 = (bf16[2,384,384]{2,1,0:T(8,128)(2,1)S(1)}, bf16[2,384,384]{2,1,0:T(8,128)(2,1)S(1)}, f32[384,256]{1,0:T(8,128)S(1)}, f32[384,256]{1,0:T(8,128)S(1)}) custom-call(s32[3,3]{1,0:T(4,128)S(1)} %copy-done.29, bf16[384,256]{1,0:T(8,128)(2,1)S(1)} %copy-done.1, bf16[384,256]{1,0:T(8,128)(2,1)S(1)} %copy-done.3, bf16[384,256]{1,0:T(8,128)(2,1)S(1)} %copy-done.5), custom_call_target="tpu_custom_call" | custom-call | flops 1 | bytes 1 | tf_op jit(solution)/shard_map/pallas_call | solution.py:35
  56.1 1.6 %slice.27 = bf16[128,512]{1,0:T(8,128)(2,1)} slice(bf16[128,1024]{1,0:T(8,128)(2,1)} %copy-done.6), slice={[0:128], [512:1024]} | slice | bytes 262144 | tf_op jit(solution)/shard_map/slice | solution.py:262
  57.7 1.5 %collective-permute-start.11 = (bf16[128,512]{1,0:T(8,128)(2,1)}, bf16[128,512]{1,0:T(8,128)(2,1)}, u32[]{:S(2)}, u32[]{:S(2)}) collective-permute-start(bf16[128,512]{1,0:T(8,128)(2,1)} %slice.26), channel_id=1, source_target_pairs={{0,16},{1,17},{2,18},{3,19},{4,20},{5,21},{6,22},{7,23},{8,24},{9,... | collective-permute-start | bytes 393224 | tf_op jit(solution)/shard_map/ppermute | solution.py:224
  59.8 1.8 %shard_map.98 = (bf16[96,128]{1,0:T(8,128)(2,1)S(1)}, bf16[96,128]{1,0:T(8,128)(2,1)S(1)}) custom-call(s32[5]{0:T(128)S(1)} %stack.71.refs_0_, bf16[96,4096]{1,0:T(8,128)(2,1)S(1)} %copy-done, bf16[96,4096]{1,0:T(8,128)(2,1)S(1)} %collective-permute-done.17.refs_2_, bf16[128,1024]{1,0:T(8,128)(2,1)} %collective-permute-done.13.refs_3_.refs_17_, ...), custom_call_target="tpu_custom_call" | custom-call | flops 1 | bytes 1 | tf_op jit(solution)/shard_map/pallas_call | solution.py:35
  62.2 1.8 %shard_map.97 = (bf16[96,128]{1,0:T(8,128)(2,1)S(1)}, bf16[96,128]{1,0:T(8,128)(2,1)S(1)}) custom-call(s32[5]{0:T(128)S(1)} %stack.71.refs_0_, bf16[96,4096]{1,0:T(8,128)(2,1)S(1)} %copy-done, bf16[96,4096]{1,0:T(8,128)(2,1)S(1)} %collective-permute-done.17.refs_2_, bf16[128,1024]{1,0:T(8,128)(2,1)} %collective-permute-done.4.refs_3_.refs_8_, ...), custom_call_target="tpu_custom_call" | custom-call | flops 1 | bytes 1 | tf_op jit(solution)/shard_map/pallas_call | solution.py:35
  64.0 3.3 %collective-permute-start.18 = (bf16[192,128]{1,0:T(8,128)(2,1)S(1)}, bf16[192,128]{1,0:T(8,128)(2,1)S(1)}, u32[]{:S(2)}, u32[]{:S(2)}) collective-permute-start(bf16[192,128]{1,0:T(8,128)(2,1)S(1)} %pad_maximum_fusion.4), channel_id=1, source_target_pairs={{0,3},{1,0},{2,1},{3,2},{4,7},{5,4},{6,5},{7,6},{8,11},{9,8},{10,9... | collective-permute-start | bytes 147464 | tf_op jit(solution)/shard_map/ppermute | solution.py:224
  67.3 1.1 shard_map.96
  70.9 1.3 copy-done.12
  72.1 1.0 copy-done.20
  74.7 3.5 %collective-permute-start.2 = (bf16[96,256]{1,0:T(8,128)(2,1)S(1)}, bf16[96,256]{1,0:T(8,128)(2,1)S(1)}, u32[]{:S(2)}, u32[]{:S(2)}) collective-permute-start(bf16[96,256]{1,0:T(8,128)(2,1)S(1)} %get-tuple-element.34), channel_id=1, source_target_pairs={{0,3},{1,0},{2,1},{3,2},{4,7},{5,4},{6,5},{7,6},{8,11},{9,8},{10,9... | collective-permute-start | bytes 147464 | tf_op jit(solution)/shard_map/ppermute | solution.py:224
  78.8 1.2 collective-permute-done.2.refs_5_
  80.0 3.2 %collective-permute-done.1.refs_4_ = bf16[96,256]{1,0:T(8,128)(2,1)S(1)} collective-permute-done((bf16[96,256]{1,0:T(8,128)(2,1)S(1)}, bf16[96,256]{1,0:T(8,128)(2,1)S(1)}, u32[]{:S(2)}, u32[]{:S(2)}) %collective-permute-start.1) | collective-permute-done | bytes 49184 | tf_op jit(solution)/shard_map/ppermute | solution.py:224
  85.5 1.5 %shard_map.99 = (bf16[96,128]{1,0:T(8,128)(2,1)S(1)}, bf16[96,128]{1,0:T(8,128)(2,1)S(1)}) custom-call(s32[5]{0:T(128)S(1)} %stack.71.refs_0_, bf16[96,4096]{1,0:T(8,128)(2,1)S(1)} %copy-done, bf16[96,4096]{1,0:T(8,128)(2,1)S(1)} %collective-permute-done.17.refs_2_, bf16[128,1024]{1,0:T(8,128)(2,1)S(1)} %copy-done.11, ...), custom_call_target="tpu_custom_call" | custom-call | flops 1 | bytes 1 | tf_op jit(solution)/shard_map/pallas_call | solution.py:35
  87.1 1.2 collective-permute-start.20
  88.3 1.3 collective-permute-start.22
  89.5 3.0 %collective-permute-done.20.refs_5_ = bf16[96,128]{1,0:T(8,128)(2,1)S(1)} collective-permute-done((bf16[96,128]{1,0:T(8,128)(2,1)S(1)}, bf16[96,128]{1,0:T(8,128)(2,1)S(1)}, u32[]{:S(2)}, u32[]{:S(2)}) %collective-permute-start.20) | collective-permute-done | bytes 24608 | tf_op jit(solution)/shard_map/ppermute | solution.py:224
  93.7 1.1 collective-permute-done.23
  94.9 1.6 %collective-permute-start.24 = (f32[128,128]{1,0:T(8,128)S(1)}, f32[128,128]{1,0:T(8,128)S(1)}, u32[]{:S(2)}, u32[]{:S(2)}) collective-permute-start(f32[128,128]{1,0:T(8,128)S(1)} %bitcast_add_fusion.refs_8_), channel_id=1, source_target_pairs={{0,8},{1,9},{2,10},{3,11},{4,12},{5,13},{6,14},{7,15},{8,0},{9,1},... | collective-permute-start | bytes 196616 | tf_op jit(solution)/shard_map/ppermute | solution.py:224
  96.4 2.8 %collective-permute-done.24.refs_21_ = f32[128,128]{1,0:T(8,128)S(1)} collective-permute-done((f32[128,128]{1,0:T(8,128)S(1)}, f32[128,128]{1,0:T(8,128)S(1)}, u32[]{:S(2)}, u32[]{:S(2)}) %collective-permute-start.24) | collective-permute-done | bytes 65568 | tf_op jit(solution)/shard_map/ppermute | solution.py:224
  99.2 3.8 %shard_map.101 = (f32[96,4096]{1,0:T(8,128)S(1)}, f32[96,4096]{1,0:T(8,128)}) custom-call(s32[5]{0:T(128)S(1)} %stack.71.refs_0_, s32[3]{0:T(128)S(1)} %pad_add_fusion.refs_0_.refs_1_, bf16[96,256]{1,0:T(8,128)(2,1)S(1)} %get-tuple-element.31.refs_2_, bf16[96,256]{1,0:T(8,128)(2,1)S(1)} %collective-permute-done.refs_3_, ...), custom_call_target="tpu_custom_call" | custom-call | flops 1 | bytes 1 | tf_op jit(solution)/shard_map/pallas_call | solution.py:35
  103.0 1.2 copy-done.8
  104.1 1.4 %collective-permute-start.26 = (f32[128,128]{1,0:T(8,128)S(1)}, f32[128,128]{1,0:T(8,128)S(1)}, u32[]{:S(2)}, u32[]{:S(2)}) collective-permute-start(f32[128,128]{1,0:T(8,128)S(1)} %bitcast_add_fusion.refs_8_), channel_id=1, source_target_pairs={{0,24},{1,25},{2,26},{3,27},{4,28},{5,29},{6,30},{7,31},{8,16},{9,... | collective-permute-start | bytes 196616 | tf_op jit(solution)/shard_map/ppermute | solution.py:224
  105.6 1.5 %collective-permute-start.27 = (f32[128,128]{1,0:T(8,128)S(1)}, f32[128,128]{1,0:T(8,128)S(1)}, u32[]{:S(2)}, u32[]{:S(2)}) collective-permute-start(f32[128,128]{1,0:T(8,128)S(1)} %bitcast_add_fusion.refs_8_), channel_id=1, source_target_pairs={{0,16},{1,17},{2,18},{3,19},{4,20},{5,21},{6,22},{7,23},{8,24},{9,... | collective-permute-start | bytes 196616 | tf_op jit(solution)/shard_map/ppermute | solution.py:224
  107.1 2.6 %collective-permute-done.26 = f32[128,128]{1,0:T(8,128)S(1)} collective-permute-done((f32[128,128]{1,0:T(8,128)S(1)}, f32[128,128]{1,0:T(8,128)S(1)}, u32[]{:S(2)}, u32[]{:S(2)}) %collective-permute-start.26) | collective-permute-done | bytes 65568 | tf_op jit(solution)/shard_map/ppermute | solution.py:224
  109.6 1.3 %collective-permute-done.27 = f32[128,128]{1,0:T(8,128)S(1)} collective-permute-done((f32[128,128]{1,0:T(8,128)S(1)}, f32[128,128]{1,0:T(8,128)S(1)}, u32[]{:S(2)}, u32[]{:S(2)}) %collective-permute-start.27) | collective-permute-done | bytes 65568 | tf_op jit(solution)/shard_map/ppermute | solution.py:224
  111.1 1.1 copy-done.16
  112.2 1.0 copy-done.18
  113.1 0.9 copy-done.22
  115.0 2.4 %shard_map.102 = (bf16[384,256]{1,0:T(8,128)(2,1)}, f32[384,256]{1,0:T(8,128)S(1)}, f32[384,256]{1,0:T(8,128)S(1)}) custom-call(bf16[384,256]{1,0:T(8,128)(2,1)S(1)} %copy-done.1, bf16[384,256]{1,0:T(8,128)(2,1)S(1)} %copy-done.3, bf16[384,256]{1,0:T(8,128)(2,1)S(1)} %copy-done.5, bf16[384,256]{1,0:T(8,128)(2,1)S(1)} %copy-done.22, ...), custom_call_target="tpu_custom_call" | custom-call | flops 1 | bytes 1 | tf_op jit(solution)/shard_map/pallas_call | solution.py:35
  117.4 1.1 shard_map.103
  118.9 2.4 %add_convert_fusion = bf16[96,4096]{1,0:T(8,128)(2,1)} fusion(f32[96,4096]{1,0:T(8,128)S(1)} %copy-done.9, f32[96,4096]{1,0:T(8,128)} %collective-permute-done.25), kind=kLoop, calls=%fused_computation | loop fusion | flops 786432 | bytes 3932160 | tf_op jit(solution)/shard_map/convert_element_type | solution.py:357
  (111 shorter events, 19.3 us)
Async XLA Ops:
  7.2 63.7 %all-gather.3.cloned.1.call-start = ((), (), s32[]{:S(2)}) async-start(), calls=%async_computation | async-start | bytes 1179648 | tf_op jit(solution)/shard_map/all_gather | solution.py:292
  8.2 41.6 %copy-start.1 = (bf16[384,256]{1,0:T(8,128)(2,1)S(1)}, bf16[384,256]{1,0:T(8,128)(2,1)}, u32[]{:S(2)}) copy-start(bf16[384,256]{1,0:T(8,128)(2,1)} %refs_0_.6) | copy-start | bytes 589828
  8.2 12.3 %collective-permute-start.4 = (bf16[128,1024]{1,0:T(8,128)(2,1)S(1)}, bf16[128,1024]{1,0:T(8,128)(2,1)}, u32[]{:S(2)}, u32[]{:S(2)}) collective-permute-start(bf16[128,1024]{1,0:T(8,128)(2,1)S(1)} %dynamic_slice.18.refs_2_), channel_id=1, source_target_pairs={{0,1},{1,2},{2,3},{3,0},{4,5},{5,6},{6,7},{7,4},{8,9},{9,10},{10,1... | collective-permute-start | bytes 786440 | tf_op jit(solution)/shard_map/ppermute | solution.py:224
  13.1 36.7 %copy-start.3 = (bf16[384,256]{1,0:T(8,128)(2,1)S(1)}, bf16[384,256]{1,0:T(8,128)(2,1)}, u32[]{:S(2)}) copy-start(bf16[384,256]{1,0:T(8,128)(2,1)} %refs_0_.7) | copy-start | bytes 589828
  13.1 36.7 %copy-start.5 = (bf16[384,256]{1,0:T(8,128)(2,1)S(1)}, bf16[384,256]{1,0:T(8,128)(2,1)}, u32[]{:S(2)}) copy-start(bf16[384,256]{1,0:T(8,128)(2,1)} %refs_1_.19) | copy-start | bytes 589828
  13.1 36.7 %copy-start.29 = (s32[3,3]{1,0:T(4,128)S(1)}, s32[3,3]{1,0:T(4,128)}, u32[]{:S(2)}) copy-start(s32[3,3]{1,0:T(4,128)} %refs_0_.4) | copy-start | bytes 112
  14.1 45.7 %copy-start = (bf16[96,4096]{1,0:T(8,128)(2,1)S(1)}, bf16[96,4096]{1,0:T(8,128)(2,1)}, u32[]{:S(2)}) copy-start(bf16[96,4096]{1,0:T(8,128)(2,1)} %refs_1_.16) | copy-start | bytes 2359300
  14.1 12.1 %collective-permute-start.13 = (bf16[128,1024]{1,0:T(8,128)(2,1)S(1)}, bf16[128,1024]{1,0:T(8,128)(2,1)}, u32[]{:S(2)}, u32[]{:S(2)}) collective-permute-start(bf16[128,1024]{1,0:T(8,128)(2,1)S(1)} %dynamic_slice.18.refs_2_), channel_id=1, source_target_pairs={{0,3},{1,0},{2,1},{3,2},{4,7},{5,4},{6,5},{7,6},{8,11},{9,8},{10,9... | collective-permute-start | bytes 786440 | tf_op jit(solution)/shard_map/ppermute | solution.py:224
  20.5 10.6 %collective-permute-start.8 = (bf16[128,1024]{1,0:T(8,128)(2,1)}, bf16[128,1024]{1,0:T(8,128)(2,1)S(1)}, u32[]{:S(2)}, u32[]{:S(2)}) collective-permute-start(bf16[128,1024]{1,0:T(8,128)(2,1)} %collective-permute-done.4.refs_3_.refs_8_), channel_id=1, source_target_pairs={{0,1},{1,2},{2,3},{3,0},{4,5},{5,6},{6,7},{7,4},{8,9},{9,10},{10,1... | collective-permute-start | bytes 786440 | tf_op jit(solution)/shard_map/ppermute | solution.py:224
  26.2 11.6 %collective-permute-start.15 = (bf16[128,1024]{1,0:T(8,128)(2,1)}, bf16[128,1024]{1,0:T(8,128)(2,1)}, u32[]{:S(2)}, u32[]{:S(2)}) collective-permute-start(bf16[128,1024]{1,0:T(8,128)(2,1)} %collective-permute-done.13.refs_3_.refs_17_), channel_id=1, source_target_pairs={{0,16},{1,17},{2,18},{3,19},{4,20},{5,21},{6,22},{7,23},{8,24},{9,... | collective-permute-start | bytes 786440 | tf_op jit(solution)/shard_map/ppermute | solution.py:224
  27.9 12.3 %collective-permute-start.5 = (bf16[128,1024]{1,0:T(8,128)(2,1)}, bf16[128,1024]{1,0:T(8,128)(2,1)}, u32[]{:S(2)}, u32[]{:S(2)}) collective-permute-start(bf16[128,1024]{1,0:T(8,128)(2,1)} %collective-permute-done.4.refs_3_.refs_8_), channel_id=1, source_target_pairs={{0,8},{1,9},{2,10},{3,11},{4,12},{5,13},{6,14},{7,15},{8,0},{9,1},... | collective-permute-start | bytes 786440 | tf_op jit(solution)/shard_map/ppermute | solution.py:224
  31.2 14.6 %collective-permute-start.9 = (bf16[128,1024]{1,0:T(8,128)(2,1)S(1)}, bf16[128,1024]{1,0:T(8,128)(2,1)S(1)}, u32[]{:S(2)}, u32[]{:S(2)}) collective-permute-start(bf16[128,1024]{1,0:T(8,128)(2,1)S(1)} %collective-permute-done.8.refs_3_.refs_12_), channel_id=1, source_target_pairs={{0,8},{1,9},{2,10},{3,11},{4,12},{5,13},{6,14},{7,15},{8,0},{9,1},... | collective-permute-start | bytes 786440 | tf_op jit(solution)/shard_map/ppermute | solution.py:224
  32.7 14.6 %collective-permute-start.10 = (bf16[128,1024]{1,0:T(8,128)(2,1)S(1)}, bf16[128,1024]{1,0:T(8,128)(2,1)S(1)}, u32[]{:S(2)}, u32[]{:S(2)}) collective-permute-start(bf16[128,1024]{1,0:T(8,128)(2,1)S(1)} %collective-permute-done.8.refs_3_.refs_12_), channel_id=1, source_target_pairs={{0,16},{1,17},{2,18},{3,19},{4,20},{5,21},{6,22},{7,23},{8,24},{9,... | collective-permute-start | bytes 786440 | tf_op jit(solution)/shard_map/ppermute | solution.py:224
  34.9 24.9 %collective-permute-start.17 = (bf16[96,4096]{1,0:T(8,128)(2,1)}, bf16[96,4096]{1,0:T(8,128)(2,1)S(1)}, u32[]{:S(2)}, u32[]{:S(2)}) collective-permute-start(bf16[96,4096]{1,0:T(8,128)(2,1)} %refs_1_.16), channel_id=1, source_target_pairs={{0,4},{1,5},{2,6},{3,7},{4,0},{5,1},{6,2},{7,3},{8,12},{9,13},{10,... | collective-permute-start | bytes 2359304 | tf_op jit(solution)/shard_map/ppermute | solution.py:224
  37.8 20.0 %collective-permute-start.14 = (bf16[128,1024]{1,0:T(8,128)(2,1)}, bf16[128,1024]{1,0:T(8,128)(2,1)}, u32[]{:S(2)}, u32[]{:S(2)}) collective-permute-start(bf16[128,1024]{1,0:T(8,128)(2,1)} %collective-permute-done.13.refs_3_.refs_17_), channel_id=1, source_target_pairs={{0,8},{1,9},{2,10},{3,11},{4,12},{5,13},{6,14},{7,15},{8,0},{9,1},... | collective-permute-start | bytes 786440 | tf_op jit(solution)/shard_map/ppermute | solution.py:224
  40.3 21.9 %collective-permute-start.6 = (bf16[128,1024]{1,0:T(8,128)(2,1)}, bf16[128,1024]{1,0:T(8,128)(2,1)}, u32[]{:S(2)}, u32[]{:S(2)}) collective-permute-start(bf16[128,1024]{1,0:T(8,128)(2,1)} %collective-permute-done.4.refs_3_.refs_8_), channel_id=1, source_target_pairs={{0,16},{1,17},{2,18},{3,19},{4,20},{5,21},{6,22},{7,23},{8,24},{9,... | collective-permute-start | bytes 786440 | tf_op jit(solution)/shard_map/ppermute | solution.py:224
  45.8 13.4 %collective-permute-start.16 = (bf16[128,1024]{1,0:T(8,128)(2,1)}, bf16[128,1024]{1,0:T(8,128)(2,1)}, u32[]{:S(2)}, u32[]{:S(2)}) collective-permute-start(bf16[128,1024]{1,0:T(8,128)(2,1)} %collective-permute-done.15.refs_5_.refs_19_), channel_id=1, source_target_pairs={{0,8},{1,9},{2,10},{3,11},{4,12},{5,13},{6,14},{7,15},{8,0},{9,1},... | collective-permute-start | bytes 786440 | tf_op jit(solution)/shard_map/ppermute | solution.py:224
  48.0 14.2 %collective-permute-start.7 = (bf16[128,1024]{1,0:T(8,128)(2,1)}, bf16[128,1024]{1,0:T(8,128)(2,1)}, u32[]{:S(2)}, u32[]{:S(2)}) collective-permute-start(bf16[128,1024]{1,0:T(8,128)(2,1)} %collective-permute-done.5.refs_4_.refs_9_), channel_id=1, source_target_pairs={{0,16},{1,17},{2,18},{3,19},{4,20},{5,21},{6,22},{7,23},{8,24},{9,... | collective-permute-start | bytes 786440 | tf_op jit(solution)/shard_map/ppermute | solution.py:224
  57.7 27.1 %collective-permute-start.11 = (bf16[128,512]{1,0:T(8,128)(2,1)}, bf16[128,512]{1,0:T(8,128)(2,1)}, u32[]{:S(2)}, u32[]{:S(2)}) collective-permute-start(bf16[128,512]{1,0:T(8,128)(2,1)} %slice.26), channel_id=1, source_target_pairs={{0,16},{1,17},{2,18},{3,19},{4,20},{5,21},{6,22},{7,23},{8,24},{9,... | collective-permute-start | bytes 393224 | tf_op jit(solution)/shard_map/ppermute | solution.py:224
  59.2 25.6 %collective-permute-start.12 = (bf16[128,512]{1,0:T(8,128)(2,1)}, bf16[128,512]{1,0:T(8,128)(2,1)}, u32[]{:S(2)}, u32[]{:S(2)}) collective-permute-start(bf16[128,512]{1,0:T(8,128)(2,1)} %slice.27), channel_id=1, source_target_pairs={{0,8},{1,9},{2,10},{3,11},{4,12},{5,13},{6,14},{7,15},{8,0},{9,1},... | collective-permute-start | bytes 393224 | tf_op jit(solution)/shard_map/ppermute | solution.py:224
  61.6 7.4 %collective-permute-start.19 = (bf16[192,128]{1,0:T(8,128)(2,1)S(1)}, bf16[192,128]{1,0:T(8,128)(2,1)S(1)}, u32[]{:S(2)}, u32[]{:S(2)}) collective-permute-start(bf16[192,128]{1,0:T(8,128)(2,1)S(1)} %pad_maximum_fusion.5), channel_id=1, source_target_pairs={{0,1},{1,2},{2,3},{3,0},{4,5},{5,6},{6,7},{7,4},{8,9},{9,10},{10,1... | collective-permute-start | bytes 147464 | tf_op jit(solution)/shard_map/ppermute | solution.py:224
  64.0 5.7 %collective-permute-start.18 = (bf16[192,128]{1,0:T(8,128)(2,1)S(1)}, bf16[192,128]{1,0:T(8,128)(2,1)S(1)}, u32[]{:S(2)}, u32[]{:S(2)}) collective-permute-start(bf16[192,128]{1,0:T(8,128)(2,1)S(1)} %pad_maximum_fusion.4), channel_id=1, source_target_pairs={{0,3},{1,0},{2,1},{3,2},{4,7},{5,4},{6,5},{7,6},{8,11},{9,8},{10,9... | collective-permute-start | bytes 147464 | tf_op jit(solution)/shard_map/ppermute | solution.py:224
  70.8 14.7 %copy-start.7 = (bf16[128,1024]{1,0:T(8,128)(2,1)S(1)}, bf16[128,1024]{1,0:T(8,128)(2,1)}, u32[]{:S(2)}) copy-start(bf16[128,1024]{1,0:T(8,128)(2,1)} %copy-done.6) | copy-start | bytes 786436
  70.8 14.7 %copy-start.11 = (bf16[128,1024]{1,0:T(8,128)(2,1)S(1)}, bf16[128,1024]{1,0:T(8,128)(2,1)}, u32[]{:S(2)}) copy-start(bf16[128,1024]{1,0:T(8,128)(2,1)} %copy-done.10) | copy-start | bytes 786436
  70.8 1.3 %copy-start.12 = (f32[16,128,128]{2,1,0:T(8,128)S(1)}, f32[16,128,128]{2,1,0:T(8,128)}, u32[]{:S(2)}) copy-start(f32[16,128,128]{2,1,0:T(8,128)} %all-gather.3.cloned.1.call-done) | copy-start | bytes 3145732
  72.1 1.0 copy-start.20
  73.1 11.1 %copy-start.30 = (bf16[1,96,128]{2,1,0:T(8,128)(2,1)S(1)}, bf16[1,96,128]{2,1,0:T(8,128)(2,1)}, u32[]{:S(2)}) copy-start(bf16[1,96,128]{2,1,0:T(8,128)(2,1)} %slice_bitcast_fusion) | copy-start | bytes 73732
  73.1 11.1 %copy-start.31 = (bf16[1,96,128]{2,1,0:T(8,128)(2,1)S(1)}, bf16[1,96,128]{2,1,0:T(8,128)(2,1)}, u32[]{:S(2)}) copy-start(bf16[1,96,128]{2,1,0:T(8,128)(2,1)} %slice_bitcast_fusion.1) | copy-start | bytes 73732
  74.7 5.3 %collective-permute-start.2 = (bf16[96,256]{1,0:T(8,128)(2,1)S(1)}, bf16[96,256]{1,0:T(8,128)(2,1)S(1)}, u32[]{:S(2)}, u32[]{:S(2)}) collective-permute-start(bf16[96,256]{1,0:T(8,128)(2,1)S(1)} %get-tuple-element.34), channel_id=1, source_target_pairs={{0,3},{1,0},{2,1},{3,2},{4,7},{5,4},{6,5},{7,6},{8,11},{9,8},{10,9... | collective-permute-start | bytes 147464 | tf_op jit(solution)/shard_map/ppermute | solution.py:224
  78.2 5.0 %collective-permute-start.1 = (bf16[96,256]{1,0:T(8,128)(2,1)S(1)}, bf16[96,256]{1,0:T(8,128)(2,1)S(1)}, u32[]{:S(2)}, u32[]{:S(2)}) collective-permute-start(bf16[96,256]{1,0:T(8,128)(2,1)S(1)} %get-tuple-element.33), channel_id=1, source_target_pairs={{0,2},{1,3},{2,0},{3,1},{4,6},{5,7},{6,4},{7,5},{8,10},{9,11},{10,... | collective-permute-start | bytes 147464 | tf_op jit(solution)/shard_map/ppermute | solution.py:224
  78.2 5.9 %collective-permute-start = (bf16[96,256]{1,0:T(8,128)(2,1)S(1)}, bf16[96,256]{1,0:T(8,128)(2,1)S(1)}, u32[]{:S(2)}, u32[]{:S(2)}) collective-permute-start(bf16[96,256]{1,0:T(8,128)(2,1)S(1)} %get-tuple-element.32), channel_id=1, source_target_pairs={{0,1},{1,2},{2,3},{3,0},{4,5},{5,6},{6,7},{7,4},{8,9},{9,10},{10,1... | collective-permute-start | bytes 147464 | tf_op jit(solution)/shard_map/ppermute | solution.py:224
  83.2 6.3 %copy-start.28 = (bf16[96,128]{1,0:T(8,128)(2,1)S(1)}, bf16[96,128]{1,0:T(8,128)(2,1)}, u32[]{:S(2)}) copy-start(bf16[96,128]{1,0:T(8,128)(2,1)} %copy-done.27) | copy-start | bytes 73732
  84.1 8.6 %copy-start.26 = (bf16[192,128]{1,0:T(8,128)(2,1)S(1)}, bf16[192,128]{1,0:T(8,128)(2,1)}, u32[]{:S(2)}) copy-start(bf16[192,128]{1,0:T(8,128)(2,1)} %copy-done.25) | copy-start | bytes 147460
  84.1 1.4 %collective-permute-start.3 = (bf16[4,96,128]{2,1,0:T(8,128)(2,1)S(1)}, bf16[4,96,128]{2,1,0:T(8,128)(2,1)S(1)}, u32[]{:S(2)}, u32[]{:S(2)}) collective-permute-start(bf16[4,96,128]{2,1,0:T(8,128)(2,1)S(1)} %pad_maximum_fusion.1), channel_id=1, source_target_pairs={{0,4},{1,5},{2,6},{3,7},{4,0},{5,1},{6,2},{7,3},{8,12},{9,13},{10,... | collective-permute-start | bytes 294920 | tf_op jit(solution)/shard_map/ppermute | solution.py:224
  84.3 5.3 %collective-permute-start.21 = (bf16[3,96,128]{2,1,0:T(8,128)(2,1)S(1)}, bf16[3,96,128]{2,1,0:T(8,128)(2,1)S(1)}, u32[]{:S(2)}, u32[]{:S(2)}) collective-permute-start(bf16[3,96,128]{2,1,0:T(8,128)(2,1)S(1)} %pad_maximum_fusion.2), channel_id=1, source_target_pairs={{0,4},{1,5},{2,6},{3,7},{4,0},{5,1},{6,2},{7,3},{8,12},{9,13},{10,... | collective-permute-start | bytes 221192 | tf_op jit(solution)/shard_map/ppermute | solution.py:224
  87.1 5.5 %collective-permute-start.20 = (bf16[96,128]{1,0:T(8,128)(2,1)S(1)}, bf16[96,128]{1,0:T(8,128)(2,1)S(1)}, u32[]{:S(2)}, u32[]{:S(2)}) collective-permute-start(bf16[96,128]{1,0:T(8,128)(2,1)S(1)} %get-tuple-element.41), channel_id=1, source_target_pairs={{0,2},{1,3},{2,0},{3,1},{4,6},{5,7},{6,4},{7,5},{8,10},{9,11},{10,... | collective-permute-start | bytes 73736 | tf_op jit(solution)/shard_map/ppermute | solution.py:224
  88.3 4.4 %collective-permute-start.22 = (bf16[96,128]{1,0:T(8,128)(2,1)S(1)}, bf16[96,128]{1,0:T(8,128)(2,1)S(1)}, u32[]{:S(2)}, u32[]{:S(2)}) collective-permute-start(bf16[96,128]{1,0:T(8,128)(2,1)S(1)} %get-tuple-element.42), channel_id=1, source_target_pairs={{0,6},{1,7},{2,4},{3,5},{4,2},{5,3},{6,0},{7,1},{8,14},{9,15},{10,... | collective-permute-start | bytes 73736 | tf_op jit(solution)/shard_map/ppermute | solution.py:224
  93.5 2.9 %copy-start.21 = (bf16[384,256]{1,0:T(8,128)(2,1)}, bf16[384,256]{1,0:T(8,128)(2,1)S(1)}, u32[]{:S(2)}) copy-start(bf16[384,256]{1,0:T(8,128)(2,1)S(1)} %get-tuple-element.46.refs_3_) | copy-start | bytes 589828
  93.5 1.3 %collective-permute-start.23 = (f32[128,128]{1,0:T(8,128)S(1)}, f32[128,128]{1,0:T(8,128)S(1)}, u32[]{:S(2)}, u32[]{:S(2)}) collective-permute-start(f32[128,128]{1,0:T(8,128)S(1)} %select_bitcast_fusion.2), channel_id=1, source_target_pairs={{0,4},{1,5},{2,6},{3,7},{4,0},{5,1},{6,2},{7,3},{8,12},{9,13},{10,... | collective-permute-start | bytes 196616 | tf_op jit(solution)/shard_map/ppermute | solution.py:224
  94.9 16.2 %copy-start.14 = (bf16[2,384,384]{2,1,0:T(8,128)(2,1)S(1)}, bf16[2,384,384]{2,1,0:T(8,128)(2,1)}, u32[]{:S(2)}) copy-start(bf16[2,384,384]{2,1,0:T(8,128)(2,1)} %copy-done.13) | copy-start | bytes 1769476
  94.9 4.3 %collective-permute-start.24 = (f32[128,128]{1,0:T(8,128)S(1)}, f32[128,128]{1,0:T(8,128)S(1)}, u32[]{:S(2)}, u32[]{:S(2)}) collective-permute-start(f32[128,128]{1,0:T(8,128)S(1)} %bitcast_add_fusion.refs_8_), channel_id=1, source_target_pairs={{0,8},{1,9},{2,10},{3,11},{4,12},{5,13},{6,14},{7,15},{8,0},{9,1},... | collective-permute-start | bytes 196616 | tf_op jit(solution)/shard_map/ppermute | solution.py:224
  103.0 1.2 copy-start.8
  104.1 14.4 %collective-permute-start.25 = (f32[96,4096]{1,0:T(8,128)}, f32[96,4096]{1,0:T(8,128)}, u32[]{:S(2)}, u32[]{:S(2)}) collective-permute-start(f32[96,4096]{1,0:T(8,128)} %get-tuple-element.45), channel_id=1, source_target_pairs={{0,4},{1,5},{2,6},{3,7},{4,0},{5,1},{6,2},{7,3},{8,12},{9,13},{10,... | collective-permute-start | bytes 4718600 | tf_op jit(solution)/shard_map/ppermute | solution.py:224
  104.1 5.5 %collective-permute-start.26 = (f32[128,128]{1,0:T(8,128)S(1)}, f32[128,128]{1,0:T(8,128)S(1)}, u32[]{:S(2)}, u32[]{:S(2)}) collective-permute-start(f32[128,128]{1,0:T(8,128)S(1)} %bitcast_add_fusion.refs_8_), channel_id=1, source_target_pairs={{0,24},{1,25},{2,26},{3,27},{4,28},{5,29},{6,30},{7,31},{8,16},{9,... | collective-permute-start | bytes 196616 | tf_op jit(solution)/shard_map/ppermute | solution.py:224
  105.6 5.4 %collective-permute-start.27 = (f32[128,128]{1,0:T(8,128)S(1)}, f32[128,128]{1,0:T(8,128)S(1)}, u32[]{:S(2)}, u32[]{:S(2)}) collective-permute-start(f32[128,128]{1,0:T(8,128)S(1)} %bitcast_add_fusion.refs_8_), channel_id=1, source_target_pairs={{0,16},{1,17},{2,18},{3,19},{4,20},{5,21},{6,22},{7,23},{8,24},{9,... | collective-permute-start | bytes 196616 | tf_op jit(solution)/shard_map/ppermute | solution.py:224
  111.0 6.4 %collective-permute-start.28 = (f32[128,128]{1,0:T(8,128)S(1)}, f32[128,128]{1,0:T(8,128)S(1)}, u32[]{:S(2)}, u32[]{:S(2)}) collective-permute-start(f32[128,128]{1,0:T(8,128)S(1)} %get-tuple-element.56), channel_id=1, source_target_pairs={{0,4},{1,5},{2,6},{3,7},{4,0},{5,1},{6,2},{7,3},{8,12},{9,13},{10,... | collective-permute-start | bytes 196616 | tf_op jit(solution)/shard_map/ppermute | solution.py:224
  111.1 1.1 copy-start.16
  117.4 1.5 %copy-start.9 = (f32[96,4096]{1,0:T(8,128)S(1)}, f32[96,4096]{1,0:T(8,128)}, u32[]{:S(2)}) copy-start(f32[96,4096]{1,0:T(8,128)} %copy-done.8) | copy-start | bytes 4718596
  (14 other events, 11.1 us)
Sparse Core Ops, SparseCore 0:
  14.2 26.7 all-gather.2

commit v4 on v2

v4 whole, which is shorter than its diff:
```python
import functools
import math

import jax
import jax.numpy as jnp
from jax import lax
from jax.experimental import pallas as pl
from jax.experimental.pallas import tpu as pltpu
from jax.sharding import PartitionSpec as P

DH = 128
F32 = jnp.float32
BF16 = jnp.bfloat16
NN = ((1,), (0,))
NT = ((1,), (1,))
TN = ((0,), (0,))
MIB = 1 << 20


def dot(a, b, dims):
    return lax.dot_general(a, b, (dims, ((), ())), preferred_element_type=F32)


def dot_wide(a, b, dims):
    high = b.astype(BF16)
    low = (b - high.astype(F32)).astype(BF16)
    return dot(a, high, dims) + dot(a, low, dims)


def whole_block(shape):
    return pl.BlockSpec(shape, lambda i: (0,) * len(shape))


def call(body, outs, args, smem=(), after=(), steps=1, specs=None, scratch=(), room=16, flops=1):
    ins, results = specs or ([whole_block(a.shape) for a in args], [whole_block(o) for o, _ in outs])

    def kernel(*refs):
        first = len(smem) + len(args)
        body(*refs[:first], *refs[first + len(after) :])

    moved = sum(a.size * a.dtype.itemsize for a in args)
    moved += sum(math.prod(s) * jnp.dtype(t).itemsize for s, t in outs)
    return pl.pallas_call(
        kernel,
        grid=(steps,),
        out_shape=[jax.ShapeDtypeStruct(s, t) for s, t in outs],
        in_specs=[pl.BlockSpec(memory_space=pltpu.SMEM) for _ in smem]
        + list(ins)
        + [pl.BlockSpec(memory_space=pl.ANY) for _ in after],
        out_specs=list(results),
        scratch_shapes=list(scratch),
        compiler_params=pltpu.CompilerParams(vmem_limit_bytes=room * MIB),
        cost_estimate=pl.CostEstimate(
            flops=int(flops), bytes_accessed=int(moved), transcendentals=0
        ),
    )(*smem, *args, *after)


def lower_triangle(blk):
    return lax.broadcasted_iota(jnp.int32, (blk, blk), 0) >= lax.broadcasted_iota(
        jnp.int32, (blk, blk), 1
    )


def forward_kernel(scale, mask, q_ref, k_ref, v_ref, probs_ref, inner_ref, soft_ref, pre_ref):
    rows, width = q_ref.shape
    count = mask.shape[0]
    blk = rows // count
    inv_root = 1.0 / math.sqrt(DH)
    triangle = lower_triangle(blk)
    for h in range(width // DH):
        cols = slice(h * DH, (h + 1) * DH)
        for i in range(count):
            here = slice(i * blk, (i + 1) * blk)
            upto = slice(0, (i + 1) * blk)
            raw = dot(q_ref[here, cols], k_ref[upto, cols], NT)
            scores, inner = [], []
            for j in range(i + 1):
                part = raw[:, j * blk : (j + 1) * blk]
                keep = triangle if j == i else mask[i, j] > 0
                scores.append(jnp.where(keep, part * inv_root, -1e30))
                inner.append(jnp.where(triangle, part, 0.0) if j == i else part)
            scores = jnp.concatenate(scores, 1)
            inner = jnp.concatenate(inner, 1).astype(BF16)
            expo = jnp.exp(scores - jnp.max(scores, -1, keepdims=True))
            probs = (expo / jnp.sum(expo, -1, keepdims=True)).astype(BF16)
            v = v_ref[upto, cols]
            soft = dot(probs, v, NN)
            probs_ref[h, here, upto] = probs
            inner_ref[h, here, upto] = inner
            soft_ref[here, cols] = soft
            pre_ref[here, cols] = soft + scale * dot(inner, v, NN)


def split_heads(core, parts, mine_ref, other_ref):
    mine_ref[...] = jnp.where(core == 0, parts[0], parts[1])
    other_ref[...] = jnp.where(core == 0, parts[1], parts[0])


def both_heads(core, mine_ref, other_ref):
    mine, other = mine_ref[...], other_ref[...]
    return jnp.where(core == 0, mine, other), jnp.where(core == 0, other, mine)


def state_kernel(where, k_ref, v_ref, mine_ref, other_ref):
    heads = [slice(h * DH, (h + 1) * DH) for h in range(2)]
    parts = [dot(k_ref[:, cols], v_ref[:, cols], TN) for cols in heads]
    split_heads(where[2], parts, mine_ref, other_ref)


def carry_kernel(flags, here_ref, got_ref, *refs):
    totals, (keep_ref, back_ref) = refs[:-2], refs[-2:]
    carried = jnp.zeros(here_ref.shape, F32)
    for n, total in enumerate(totals):
        carried = carried + jnp.where(flags[n] > 0, total[...], 0.0)
    counts = flags[len(totals)] > 0
    keep_ref[...] = carried + jnp.where(counts, got_ref[...], 0.0)
    back_ref[...] = carried + jnp.where(counts, 0.0, here_ref[...])


def attn_kernel(scale, where, q_ref, pre_ref, mine_ref, other_ref, *out_refs):
    count = len(out_refs)
    states = both_heads(where[2], mine_ref, other_ref)
    own = out_refs[0].shape[0]
    for s in range(count):
        block = lax.rem(where[0] + s, count)
        here = pl.ds(pl.multiple_of(block * own, own), own)
        for h in range(q_ref.shape[1] // DH):
            cols = slice(h * DH, (h + 1) * DH)
            inter = dot_wide(q_ref[here, cols], states[h], NN)
            out_refs[s][:, cols] = (pre_ref[here, cols] + scale * inter).astype(BF16)


def grad_kernel(count, where, mine_ref, mate_ref, weight_ref, *refs):
    outs, total_ref = refs[:-1], refs[-1]
    own = mine_ref.shape[0]
    step = pl.program_id(0)
    part = dot(jnp.concatenate([mine_ref[...], mate_ref[...]], 0), weight_ref[0], NT)

    @pl.when(step == 0)
    def _():
        total_ref[...] = part

    @pl.when(step > 0)
    def _():
        total_ref[...] += part

    @pl.when(step == pl.num_programs(0) - 1)
    def _():
        for s in range(count):
            z = lax.rem(where[0] + s, count)
            block = total_ref[:, pl.ds(pl.multiple_of(z * DH, DH), DH)].astype(BF16)
            outs[s][...] = block


def mixed_kernel(count, where, *refs):
    attn, mate = refs[:count], refs[count : 2 * count]
    weight_ref, own_out, *mate_outs, left_ref = refs[2 * count :]
    step = pl.program_id(0)
    each = pl.num_programs(0) // len(mate_outs)
    own = own_out.shape[0]

    @pl.when(step == 0)
    def _():
        cols = pl.ds(pl.multiple_of(where[2] * DH, DH), DH)
        for s in range(count):
            z = lax.rem(where[0] - s + count, count)
            there = pl.ds(pl.multiple_of(z * DH, DH), DH)
            left_ref[:own, there] = attn[s][:, cols]
            left_ref[own:, there] = mate[s][:, cols]

    part = dot(left_ref[...], weight_ref[0], NN)
    own_out[...] = part[:own]
    for n, mate_out in enumerate(mate_outs):

        @pl.when(step // each == n)
        def _():
            mate_out[...] = part[own:]


def collect_kernel(scale, count, where, q_ref, *refs):
    direct, across = refs[:count], refs[count : 2 * count]
    g_ref, mine_ref, other_ref = refs[2 * count :]
    own = g_ref.shape[0] // count
    mine = pl.ds(pl.multiple_of(where[2] * DH, DH), DH)
    mate = pl.ds(pl.multiple_of((1 - where[2]) * DH, DH), DH)
    for s in range(count):
        block = lax.rem(where[0] - s + count, count)
        here = pl.ds(pl.multiple_of(block * own, own), own)
        g_ref[here, mine] = direct[s][:own]
        g_ref[here, mate] = across[s][own:]
    heads = [slice(h * DH, (h + 1) * DH) for h in range(2)]
    parts = [scale * dot(q_ref[:, cols], g_ref[:, cols], TN) for cols in heads]
    split_heads(where[2], parts, mine_ref, other_ref)


def backward_kernel(
    scale,
    count,
    where,
    q_ref,
    k_ref,
    v_ref,
    g_ref,
    probs_ref,
    inner_ref,
    soft_ref,
    mine_ref,
    other_ref,
    dq_ref,
    dk_ref,
    dv_ref,
):
    rows, width = q_ref.shape
    blk = rows // count
    inv_root = 1.0 / math.sqrt(DH)
    triangle = lower_triangle(blk)
    states = both_heads(where[2], mine_ref, other_ref)
    for h in range(width // DH):
        cols = slice(h * DH, (h + 1) * DH)
        for i in reversed(range(count)):
            here = slice(i * blk, (i + 1) * blk)
            upto = slice(0, (i + 1) * blk)
            q, g = q_ref[here, cols], g_ref[here, cols]
            k = k_ref[upto, cols]
            probs = probs_ref[h, here, upto]
            dprod = dot(g, v_ref[upto, cols], NT)
            delta = jnp.sum(g.astype(F32) * soft_ref[here, cols], -1, keepdims=True)
            dscore = (probs.astype(F32) * (dprod - delta) * inv_root).astype(BF16)
            last = jnp.where(triangle, dprod[:, i * blk :], 0.0)
            dinner = jnp.concatenate([dprod[:, : i * blk], last], 1) if i else last
            dinner = dinner.astype(BF16)
            dq_ref[here, cols] = (
                dot(dscore, k, NN)
                + scale * (dot(dinner, k, NN) + dot_wide(g, states[h], NT))
            ).astype(BF16)
            dk = dot(dscore, q, TN) + scale * dot(dinner, q, TN)
            dv = dot(probs, g, TN) + scale * dot(inner_ref[h, here, upto], g, TN)
            if i == count - 1:
                dk_ref[upto, cols] = dk
                dv_ref[upto, cols] = dv
            else:
                dk_ref[upto, cols] += dk
                dv_ref[upto, cols] += dv


def close_kernel(where, k_ref, v_ref, dk_ref, dv_ref, mine_ref, other_ref, gk_ref, gv_ref):
    states = both_heads(where[2], mine_ref, other_ref)
    for h in range(k_ref.shape[1] // DH):
        cols = slice(h * DH, (h + 1) * DH)
        state = states[h]
        gk_ref[:, cols] = (dk_ref[:, cols] + dot_wide(v_ref[:, cols], state, NT)).astype(BF16)
        gv_ref[:, cols] = (dv_ref[:, cols] + dot_wide(k_ref[:, cols], state, NN)).astype(BF16)


def send(x, flip, shift):
    shards, heads = lax.axis_size("ctx"), lax.axis_size("head")
    pairs = [
        (c * heads + z, (c ^ flip) * heads + (z + shift) % heads)
        for c in range(shards)
        for z in range(heads)
    ]
    return lax.ppermute(x, ("ctx", "head"), pairs)


def exchange(mine, other, core, chip, chips, later):
    got = send(other, 1, 0)
    total = mine + got
    totals, flags = [], []
    if chips == 4:
        for flip in (1, 2, 3):
            totals.append(send(total, 2 * flip, 0))
            flags.append(((chip ^ flip) > chip) == later)
    else:
        step = 1
        while step < chips:
            totals.append(send(total, 2 * step, 0))
            flags.append(((chip & step) == 0) == later)
            total = total + totals[-1]
            step *= 2
    flags.append((core == 0) == later)
    return jnp.stack(flags).astype(jnp.int32), [mine, got, *totals]


def on_device(query, key, value, block_mask, out_weight, cotangent):
    rows, width = query.shape
    heads = width // DH
    shards, count = lax.axis_size("ctx"), lax.axis_size("head")
    model = out_weight.shape[1]
    own = rows // count
    scale = 1.0 / math.sqrt(DH * rows * shards)
    blocks = block_mask.shape[0]
    ctx, place = lax.axis_index("ctx"), lax.axis_index("head")
    core, chip, chips = ctx & 1, ctx >> 1, shards // 2
    where = jnp.stack([place, ctx, core])
    flat, square = (rows, width), rows * rows * DH * heads
    pair = [((DH, DH), F32)] * 2

    wide = model // chips
    piece = lax.dynamic_slice(out_weight, (core * DH, chip * wide), (DH, wide))
    groups = [[c * count + z for c in range(k, shards, 2) for z in range(count)] for k in range(2)]
    weight = lax.all_gather(piece, ("ctx", "head"), axis_index_groups=groups)
    weight = weight.reshape(chips, count * DH, wide)
    mate_cotangent = send(cotangent, 1, 0)

    mine, other = call(state_kernel, pair, [key, value], [where], [piece])
    flags, parts = exchange(mine, other, core, chip, chips, False)
    keep, back = call(carry_kernel, pair, parts, [flags])
    linear = [keep, send(back, 1, 0)]
    probs, inner, soft, pre = call(
        functools.partial(forward_kernel, scale),
        [((heads, rows, rows), BF16)] * 2 + [(flat, F32)] * 2,
        [query, key, value],
        [block_mask],
        flops=6 * square,
    )
    attn = call(
        functools.partial(attn_kernel, scale),
        [((own, width), BF16)] * count,
        [query, pre, *linear],
        [where],
    )
    attn = [attn[0]] + [send(attn[s], 0, s) for s in range(1, count)]
    mate_attn = [send(a, 1, 0) for a in attn]

    part_of = pl.BlockSpec((own, wide), lambda i: (0, i))
    weight_of = pl.BlockSpec((1, count * DH, wide), lambda i: (i, 0, 0))
    both = call(
        functools.partial(grad_kernel, count),
        [((2 * own, DH), BF16)] * count,
        [cotangent, mate_cotangent, weight],
        [where],
        mate_attn,
        chips,
        ([part_of, part_of, weight_of], [whole_block((2 * own, DH))] * count),
        [pltpu.VMEM((2 * own, count * DH), F32)],
        flops=4 * own * count * DH * model,
    )
    both = [both[0]] + [send(both[s], 0, s) for s in range(1, count)]
    across = [send(b, 1, 0) for b in both]
    cut = 2
    each = chips // cut
    cuts = [
        pl.BlockSpec((own, wide), lambda i, n=n: (0, jnp.clip(i - n * each, 0, each - 1)))
        for n in range(cut)
    ]
    part, *mate_parts = call(
        functools.partial(mixed_kernel, count),
        [((own, model), F32)] + [((own, model // cut), F32)] * cut,
        [*attn, *mate_attn, weight],
        [where],
        both[1:],
        chips,
        ([whole_block((own, width))] * (2 * count) + [weight_of], [part_of, *cuts]),
        [pltpu.VMEM((2 * own, count * DH), BF16)],
        flops=4 * own * count * DH * model,
    )
    g, mine, other = call(
        functools.partial(collect_kernel, scale, count),
        [(flat, BF16), *pair],
        [query, *both, *across],
        [where],
        [part],
    )
    flags, parts = exchange(mine, other, core, chip, chips, True)

    mate_part = jnp.concatenate([send(p, 1, 0) for p in mate_parts], 1)

    grad_query, dk, dv = call(
        functools.partial(backward_kernel, scale, blocks),
        [(flat, BF16)] + [(flat, F32)] * 2,
        [query, key, value, g, probs, inner, soft, *linear],
        [where],
        flops=14 * square,
    )
    keep, back = call(carry_kernel, pair, parts, [flags], [dk])
    grad_key, grad_value = call(
        close_kernel, [(flat, BF16)] * 2, [key, value, dk, dv, keep, send(back, 1, 0)], [where]
    )
    mixed = (part + mate_part).astype(BF16)
    return mixed, grad_query, grad_key, grad_value


def solution(mesh):
    return jax.shard_map(
        on_device,
        mesh=mesh,
        in_specs=(
            P("ctx", "head"),
            P("ctx", "head"),
            P("ctx", "head"),
            P("ctx", None),
            P("head", None),
            P(("ctx", "head"), None),
        ),
        out_specs=(P(("ctx", "head"), None), P("ctx", "head"), P("ctx", "head"), P("ctx", "head")),
        check_vma=False,
    )
```

time: 114 us -> 135 us (1.18)
  waiting for transfers between devices: 30.8 us -> 68.4 us
  starting transfers between devices: 44.8 us -> 20.2 us
  between operations: 0.95 us -> 14.3 us
  local copies, waits for them, and re-layouts: 17.8 us -> 14.3 us
    all_gather x0 -> x1, waiting for transfers between devices: none -> 50.6 us  [on_device(): weight = lax.all_gather(piece, ('ctx', 'head'), axis_index_groups=groups)]
    ppermute x34 -> x27, starting transfers between devices: 44.8 us -> 20.2 us  [send(): return lax.ppermute(x, ('ctx', 'head'), pairs)]
    ppermute x34 -> x27, waiting for transfers between devices: 30.8 us -> 17.8 us  [send(): return lax.ppermute(x, ('ctx', 'head'), pairs)]
    slice x6 -> x0, local copies, waits for them, and re-layouts: 3.3 us -> none  [the longest x3 1.97 us: spread(): along_y[:, half:]]
    unnamed x68 -> x58, local copies, waits for them, and re-layouts: 12 us -> 12.5 us
  transfers between devices with their start and end apart: 34 -> 28, of which waited for: 17 -> 15; matrix products, arithmetic and copies ran while one was open for 4% -> 0% of each run, Pallas kernels for 14% -> 8%
where the time goes in v4:
time: 135 us
  waiting for transfers between devices  68.4 us (51%)
  starting transfers between devices  20.2 us (15%)
  Pallas kernels  16 us (12%)
  local copies, waits for them, and re-layouts  14.3 us (11%)
  between operations  14.3 us (11%)
  other arithmetic  1.36 us (1%)
    all_gather x1, waiting for transfers between devices, on_device(): weight = lax.all_gather(piece, ('ctx', 'head'), axis_index_groups=groups)  50.6 us
    ppermute x27, starting transfers between devices, send(): return lax.ppermute(x, ('ctx', 'head'), pairs)  20.2 us
    ppermute x27, waiting for transfers between devices, send(): return lax.ppermute(x, ('ctx', 'head'), pairs)  17.8 us
    pallas_call x10, Pallas kernels, call(): pl.pallas_call(kernel, grid=(steps,), out_shape=[jax.ShapeDtypeStruct(s,...  16 us
    unnamed x58, local copies, waits for them, and re-layouts  12.5 us
  transfers between devices with their start and end apart: 28, of which 15 were waited for; matrix products, arithmetic and copies ran while one was open for 0% of the time, Pallas kernels for 8%

profile of v4, /device:TPU:0, one launch (start us, length us, event | category | flops | bytes accessed | tf_op | source)
XLA Modules:
  0.0 134.7 jit_solution(11012802639695086313)
XLA Ops:
  7.3 1.8 %dynamic_slice.3.refs_3_ = bf16[128,1024]{1,0:T(8,128)(2,1)} dynamic-slice(bf16[256,4096]{1,0:T(8,128)(2,1)} %param.10, s32[]{:T(128)S(6)} %select_n.6, s32[]{:T(128)S(6)} %select_n.7), dynamic_slice_sizes={128,1024} | dynamic-slice | bytes 524292 | tf_op jit(solution)/shard_map/dynamic_slice | solution.py:300
  9.7 0.9 copy-done.2
  10.6 0.9 copy-done.4
  11.6 0.9 copy-done.6
  12.5 0.8 shard_map.94
  13.4 1.2 collective-permute-done.refs_2_
  14.6 2.7 %collective-permute-start.1 = (f32[128,128]{1,0:T(8,128)S(1)}, f32[128,128]{1,0:T(8,128)S(1)}, u32[]{:S(2)}, u32[]{:S(2)}) collective-permute-start(f32[128,128]{1,0:T(8,128)S(1)} %add.17), channel_id=1, source_target_pairs={{0,8},{1,9},{2,10},{3,11},{4,12},{5,13},{6,14},{7,15},{8,0},{9,1},... | collective-permute-start | bytes 196616 | tf_op jit(solution)/shard_map/ppermute | solution.py:263
  17.3 1.5 %collective-permute-start.2 = (f32[128,128]{1,0:T(8,128)S(1)}, f32[128,128]{1,0:T(8,128)S(1)}, u32[]{:S(2)}, u32[]{:S(2)}) collective-permute-start(f32[128,128]{1,0:T(8,128)S(1)} %add.17), channel_id=1, source_target_pairs={{0,16},{1,17},{2,18},{3,19},{4,20},{5,21},{6,22},{7,23},{8,24},{9,... | collective-permute-start | bytes 196616 | tf_op jit(solution)/shard_map/ppermute | solution.py:263
  18.9 1.0 collective-permute-done.1.refs_3_
  19.9 1.7 %collective-permute-done.2.refs_4_ = f32[128,128]{1,0:T(8,128)S(1)} collective-permute-done((f32[128,128]{1,0:T(8,128)S(1)}, f32[128,128]{1,0:T(8,128)S(1)}, u32[]{:S(2)}, u32[]{:S(2)}) %collective-permute-start.2) | collective-permute-done | bytes 65568 | tf_op jit(solution)/shard_map/ppermute | solution.py:263
  21.6 2.4 %collective-permute-done.3.refs_5_ = f32[128,128]{1,0:T(8,128)S(1)} collective-permute-done((f32[128,128]{1,0:T(8,128)S(1)}, f32[128,128]{1,0:T(8,128)S(1)}, u32[]{:S(2)}, u32[]{:S(2)}) %collective-permute-start.3) | collective-permute-done | bytes 65568 | tf_op jit(solution)/shard_map/ppermute | solution.py:263
  24.7 2.3 %shard_map.93 = (bf16[2,384,384]{2,1,0:T(8,128)(2,1)S(1)}, bf16[2,384,384]{2,1,0:T(8,128)(2,1)S(1)}, f32[384,256]{1,0:T(8,128)S(1)}, f32[384,256]{1,0:T(8,128)S(1)}) custom-call(s32[3,3]{1,0:T(4,128)S(1)} %copy-done.28, bf16[384,256]{1,0:T(8,128)(2,1)S(1)} %copy-done.3, bf16[384,256]{1,0:T(8,128)(2,1)S(1)} %copy-done.5, bf16[384,256]{1,0:T(8,128)(2,1)S(1)} %copy-done.7), custom_call_target="tpu_custom_call" | custom-call | flops 226492416 | bytes 2555904 | tf_op jit(solution)/shard_map/pallas_call | solution.py:43
  27.0 0.7 copy-done.9
  27.8 0.8 shard_map.96
  28.6 2.6 %collective-permute-start.6 = (bf16[96,256]{1,0:T(8,128)(2,1)S(1)}, bf16[96,256]{1,0:T(8,128)(2,1)S(1)}, u32[]{:S(2)}, u32[]{:S(2)}) collective-permute-start(bf16[96,256]{1,0:T(8,128)(2,1)S(1)} %get-tuple-element.40), channel_id=1, source_target_pairs={{0,2},{1,3},{2,0},{3,1},{4,6},{5,7},{6,4},{7,5},{8,10},{9,11},{10,... | collective-permute-start | bytes 147464 | tf_op jit(solution)/shard_map/ppermute | solution.py:263
  31.3 1.4 %collective-permute-start.7 = (bf16[96,256]{1,0:T(8,128)(2,1)S(1)}, bf16[96,256]{1,0:T(8,128)(2,1)S(1)}, u32[]{:S(2)}, u32[]{:S(2)}) collective-permute-start(bf16[96,256]{1,0:T(8,128)(2,1)S(1)} %get-tuple-element.41), channel_id=1, source_target_pairs={{0,3},{1,0},{2,1},{3,2},{4,7},{5,4},{6,5},{7,6},{8,11},{9,8},{10,9... | collective-permute-start | bytes 147464 | tf_op jit(solution)/shard_map/ppermute | solution.py:263
  32.6 0.7 collective-permute-start.5
  33.3 0.6 copy-done.20
  33.9 2.5 %collective-permute-done.6.refs_3_ = bf16[96,256]{1,0:T(8,128)(2,1)S(1)} collective-permute-done((bf16[96,256]{1,0:T(8,128)(2,1)S(1)}, bf16[96,256]{1,0:T(8,128)(2,1)S(1)}, u32[]{:S(2)}, u32[]{:S(2)}) %collective-permute-start.6) | collective-permute-done | bytes 49184 | tf_op jit(solution)/shard_map/ppermute | solution.py:263
  36.4 0.6 copy-done.22
  37.5 0.6 copy-done.24
  38.5 0.6 copy-done.26
  39.1 0.6 copy-done.11
  39.8 0.6 copy-done.14
  40.4 0.6 copy-done.17
  41.0 50.6 %all-gather.3.cloned.1.call-done = bf16[2048,1024]{1,0:T(8,128)(2,1)} async-done(((bf16[128,1024]{1,0:T(8,128)(2,1)}), bf16[2048,1024]{1,0:T(8,128)(2,1)}) %all-gather.3.cloned.1.call-update) | async-done | bytes 4194320 | tf_op jit(solution)/shard_map/all_gather | solution.py:302
  91.6 2.2 %copy-done = bf16[2048,1024]{1,0:T(8,128)(2,1)S(1)} copy-done((bf16[2048,1024]{1,0:T(8,128)(2,1)S(1)}, bf16[2048,1024]{1,0:T(8,128)(2,1)}, u32[]{:S(2)}) %copy-start) | copy-done | bytes 4194328
  93.8 0.8 copy-done.12
  94.6 0.8 copy-done.15
  95.4 0.8 copy-done.18
  96.2 3.0 %shard_map.97 = (bf16[192,128]{1,0:T(8,128)(2,1)S(1)}, bf16[192,128]{1,0:T(8,128)(2,1)S(1)}, bf16[192,128]{1,0:T(8,128)(2,1)S(1)}, bf16[192,128]{1,0:T(8,128)(2,1)S(1)}) custom-call(s32[3]{0:T(128)S(1)} %pad_add_fusion.refs_0_, bf16[96,4096]{1,0:T(8,128)(2,1)S(1)} %copy-done.8, bf16[96,4096]{1,0:T(8,128)(2,1)S(1)} %collective-permute-done.12.refs_2_, ...), custom_call_target="tpu_custom_call" | custom-call | flops 805306368 | bytes 5963776 | tf_op jit(solution)/shard_map/pallas_call | solution.py:43
  99.2 1.5 %collective-permute-start.13 = (bf16[192,128]{1,0:T(8,128)(2,1)S(1)}, bf16[192,128]{1,0:T(8,128)(2,1)S(1)}, u32[]{:S(2)}, u32[]{:S(2)}) collective-permute-start(bf16[192,128]{1,0:T(8,128)(2,1)S(1)} %get-tuple-element.42), channel_id=1, source_target_pairs={{0,1},{1,2},{2,3},{3,0},{4,5},{5,6},{6,7},{7,4},{8,9},{9,10},{10,1... | collective-permute-start | bytes 147464 | tf_op jit(solution)/shard_map/ppermute | solution.py:263
  100.7 1.0 collective-permute-start.14
  101.7 2.4 %collective-permute-start.15 = (bf16[192,128]{1,0:T(8,128)(2,1)S(1)}, bf16[192,128]{1,0:T(8,128)(2,1)S(1)}, u32[]{:S(2)}, u32[]{:S(2)}) collective-permute-start(bf16[192,128]{1,0:T(8,128)(2,1)S(1)} %get-tuple-element.44), channel_id=1, source_target_pairs={{0,3},{1,0},{2,1},{3,2},{4,7},{5,4},{6,5},{7,6},{8,11},{9,8},{10,9... | collective-permute-start | bytes 147464 | tf_op jit(solution)/shard_map/ppermute | solution.py:263
  104.1 1.0 collective-permute-done.13.refs_10_.refs_3_
  105.1 0.6 collective-permute-done.14.refs_11_.refs_4_
  106.3 2.7 %shard_map.98 = (f32[96,4096]{1,0:T(8,128)S(1)}, f32[96,2048]{1,0:T(8,128)S(1)}, f32[96,2048]{1,0:T(8,128)S(1)}) custom-call(s32[3]{0:T(128)S(1)} %pad_add_fusion.refs_0_, bf16[96,256]{1,0:T(8,128)(2,1)S(1)} %copy-done.21, bf16[96,256]{1,0:T(8,128)(2,1)S(1)} %copy-done.27, bf16[96,256]{1,0:T(8,128)(2,1)S(1)} %copy-done.23, bf16[96,256]{1,0:T(8,128)(2,1)S(1)} %copy-done.25, ...), custom_call_target="tpu_custom_call" | custom-call | flops 805306368 | bytes 7733248 | tf_op jit(solution)/shard_map/pallas_call | solution.py:43
  110.2 2.4 %collective-permute-done.18.refs_6_ = bf16[192,128]{1,0:T(8,128)(2,1)S(1)} collective-permute-done((bf16[192,128]{1,0:T(8,128)(2,1)S(1)}, bf16[192,128]{1,0:T(8,128)(2,1)S(1)}, u32[]{:S(2)}, u32[]{:S(2)}) %collective-permute-start.18) | collective-permute-done | bytes 49184 | tf_op jit(solution)/shard_map/ppermute | solution.py:263
  112.7 1.1 collective-permute-done.21.refs_9_
  113.8 0.8 shard_map.99
  114.8 1.1 collective-permute-done.22.refs_2_
  115.9 1.5 %collective-permute-start.23 = (f32[128,128]{1,0:T(8,128)S(1)}, f32[128,128]{1,0:T(8,128)S(1)}, u32[]{:S(2)}, u32[]{:S(2)}) collective-permute-start(f32[128,128]{1,0:T(8,128)S(1)} %add.19), channel_id=1, source_target_pairs={{0,8},{1,9},{2,10},{3,11},{4,12},{5,13},{6,14},{7,15},{8,0},{9,1},... | collective-permute-start | bytes 196616 | tf_op jit(solution)/shard_map/ppermute | solution.py:263
  118.0 1.5 %collective-permute-start.25 = (f32[128,128]{1,0:T(8,128)S(1)}, f32[128,128]{1,0:T(8,128)S(1)}, u32[]{:S(2)}, u32[]{:S(2)}) collective-permute-start(f32[128,128]{1,0:T(8,128)S(1)} %add.19), channel_id=1, source_target_pairs={{0,24},{1,25},{2,26},{3,27},{4,28},{5,29},{6,30},{7,31},{8,16},{9,... | collective-permute-start | bytes 196616 | tf_op jit(solution)/shard_map/ppermute | solution.py:263
  119.6 2.9 %shard_map.100 = (bf16[384,256]{1,0:T(8,128)(2,1)}, f32[384,256]{1,0:T(8,128)S(1)}, f32[384,256]{1,0:T(8,128)S(1)}) custom-call(s32[3]{0:T(128)S(1)} %pad_add_fusion.refs_0_, bf16[384,256]{1,0:T(8,128)(2,1)S(1)} %copy-done.3, bf16[384,256]{1,0:T(8,128)(2,1)S(1)} %copy-done.5, bf16[384,256]{1,0:T(8,128)(2,1)S(1)} %copy-done.7, ...), custom_call_target="tpu_custom_call" | custom-call | flops 528482304 | bytes 3473408 | tf_op jit(solution)/shard_map/pallas_call | solution.py:43
  122.5 0.7 collective-permute-done.25.refs_5_
  123.8 1.2 collective-permute-done.26.refs_6_
  125.1 1.6 %shard_map.102 = (bf16[384,256]{1,0:T(8,128)(2,1)}, bf16[384,256]{1,0:T(8,128)(2,1)}) custom-call(s32[3]{0:T(128)S(1)} %pad_add_fusion.refs_0_, bf16[384,256]{1,0:T(8,128)(2,1)S(1)} %copy-done.5, bf16[384,256]{1,0:T(8,128)(2,1)S(1)} %copy-done.7, f32[384,256]{1,0:T(8,128)S(1)} %get-tuple-element.54.refs_6_.refs_3_, ...), custom_call_target="tpu_custom_call" | custom-call | flops 1 | bytes 1703936 | tf_op jit(solution)/shard_map/pallas_call | solution.py:43
  126.7 1.1 fusion
  (84 shorter events, 5.8 us)
Async XLA Ops:
  7.2 17.5 %copy-start.5 = (bf16[384,256]{1,0:T(8,128)(2,1)S(1)}, bf16[384,256]{1,0:T(8,128)(2,1)}, u32[]{:S(2)}) copy-start(bf16[384,256]{1,0:T(8,128)(2,1)} %refs_1_.13) | copy-start | bytes 589828
  7.2 17.5 %copy-start.7 = (bf16[384,256]{1,0:T(8,128)(2,1)S(1)}, bf16[384,256]{1,0:T(8,128)(2,1)}, u32[]{:S(2)}) copy-start(bf16[384,256]{1,0:T(8,128)(2,1)} %refs_2_.7) | copy-start | bytes 589828
  7.2 17.5 %copy-start.3 = (bf16[384,256]{1,0:T(8,128)(2,1)S(1)}, bf16[384,256]{1,0:T(8,128)(2,1)}, u32[]{:S(2)}) copy-start(bf16[384,256]{1,0:T(8,128)(2,1)} %refs_1_.12) | copy-start | bytes 589828
  7.2 17.5 %copy-start.28 = (s32[3,3]{1,0:T(4,128)S(1)}, s32[3,3]{1,0:T(4,128)}, u32[]{:S(2)}) copy-start(s32[3,3]{1,0:T(4,128)} %refs_0_.1) | copy-start | bytes 112
  7.2 84.4 %all-gather.3.cloned.1.call-start = ((), (), s32[]{:S(2)}) async-start(), calls=%async_computation | async-start | bytes 4456448 | tf_op jit(solution)/shard_map/all_gather | solution.py:302
  9.1 31.9 %collective-permute-start.12 = (bf16[96,4096]{1,0:T(8,128)(2,1)}, bf16[96,4096]{1,0:T(8,128)(2,1)S(1)}, u32[]{:S(2)}, u32[]{:S(2)}) collective-permute-start(bf16[96,4096]{1,0:T(8,128)(2,1)} %refs_1_.10), channel_id=1, source_target_pairs={{0,4},{1,5},{2,6},{3,7},{4,0},{5,1},{6,2},{7,3},{8,12},{9,13},{10,... | collective-permute-start | bytes 2359304 | tf_op jit(solution)/shard_map/ppermute | solution.py:263
  9.7 1.0 copy-start.2
  10.6 0.9 copy-start.4
  11.6 0.9 copy-start.6
  12.5 79.1 %copy-start.8 = (bf16[96,4096]{1,0:T(8,128)(2,1)S(1)}, bf16[96,4096]{1,0:T(8,128)(2,1)}, u32[]{:S(2)}) copy-start(bf16[96,4096]{1,0:T(8,128)(2,1)} %refs_1_.10) | copy-start | bytes 2359300
  13.3 1.3 collective-permute-start
  14.6 5.3 %collective-permute-start.1 = (f32[128,128]{1,0:T(8,128)S(1)}, f32[128,128]{1,0:T(8,128)S(1)}, u32[]{:S(2)}, u32[]{:S(2)}) collective-permute-start(f32[128,128]{1,0:T(8,128)S(1)} %add.17), channel_id=1, source_target_pairs={{0,8},{1,9},{2,10},{3,11},{4,12},{5,13},{6,14},{7,15},{8,0},{9,1},... | collective-permute-start | bytes 196616 | tf_op jit(solution)/shard_map/ppermute | solution.py:263
  17.3 4.3 %collective-permute-start.2 = (f32[128,128]{1,0:T(8,128)S(1)}, f32[128,128]{1,0:T(8,128)S(1)}, u32[]{:S(2)}, u32[]{:S(2)}) collective-permute-start(f32[128,128]{1,0:T(8,128)S(1)} %add.17), channel_id=1, source_target_pairs={{0,16},{1,17},{2,18},{3,19},{4,20},{5,21},{6,22},{7,23},{8,24},{9,... | collective-permute-start | bytes 196616 | tf_op jit(solution)/shard_map/ppermute | solution.py:263
  18.8 5.2 %collective-permute-start.3 = (f32[128,128]{1,0:T(8,128)S(1)}, f32[128,128]{1,0:T(8,128)S(1)}, u32[]{:S(2)}, u32[]{:S(2)}) collective-permute-start(f32[128,128]{1,0:T(8,128)S(1)} %add.17), channel_id=1, source_target_pairs={{0,24},{1,25},{2,26},{3,27},{4,28},{5,29},{6,30},{7,31},{8,16},{9,... | collective-permute-start | bytes 196616 | tf_op jit(solution)/shard_map/ppermute | solution.py:263
  24.6 3.2 %collective-permute-start.4 = (f32[128,128]{1,0:T(8,128)S(1)}, f32[128,128]{1,0:T(8,128)S(1)}, u32[]{:S(2)}, u32[]{:S(2)}) collective-permute-start(f32[128,128]{1,0:T(8,128)S(1)} %get-tuple-element.37), channel_id=1, source_target_pairs={{0,4},{1,5},{2,6},{3,7},{4,0},{5,1},{6,2},{7,3},{8,12},{9,13},{10,... | collective-permute-start | bytes 196616 | tf_op jit(solution)/shard_map/ppermute | solution.py:263
  28.6 7.8 %collective-permute-start.6 = (bf16[96,256]{1,0:T(8,128)(2,1)S(1)}, bf16[96,256]{1,0:T(8,128)(2,1)S(1)}, u32[]{:S(2)}, u32[]{:S(2)}) collective-permute-start(bf16[96,256]{1,0:T(8,128)(2,1)S(1)} %get-tuple-element.40), channel_id=1, source_target_pairs={{0,2},{1,3},{2,0},{3,1},{4,6},{5,7},{6,4},{7,5},{8,10},{9,11},{10,... | collective-permute-start | bytes 147464 | tf_op jit(solution)/shard_map/ppermute | solution.py:263
  31.3 5.8 %collective-permute-start.7 = (bf16[96,256]{1,0:T(8,128)(2,1)S(1)}, bf16[96,256]{1,0:T(8,128)(2,1)S(1)}, u32[]{:S(2)}, u32[]{:S(2)}) collective-permute-start(bf16[96,256]{1,0:T(8,128)(2,1)S(1)} %get-tuple-element.41), channel_id=1, source_target_pairs={{0,3},{1,0},{2,1},{3,2},{4,7},{5,4},{6,5},{7,6},{8,11},{9,8},{10,9... | collective-permute-start | bytes 147464 | tf_op jit(solution)/shard_map/ppermute | solution.py:263
  32.6 5.9 %collective-permute-start.5 = (bf16[96,256]{1,0:T(8,128)(2,1)S(1)}, bf16[96,256]{1,0:T(8,128)(2,1)S(1)}, u32[]{:S(2)}, u32[]{:S(2)}) collective-permute-start(bf16[96,256]{1,0:T(8,128)(2,1)S(1)} %get-tuple-element.39), channel_id=1, source_target_pairs={{0,1},{1,2},{2,3},{3,0},{4,5},{5,6},{6,7},{7,4},{8,9},{9,10},{10,1... | collective-permute-start | bytes 147464 | tf_op jit(solution)/shard_map/ppermute | solution.py:263
  33.3 5.8 %collective-permute-start.8 = (bf16[96,256]{1,0:T(8,128)(2,1)S(1)}, bf16[96,256]{1,0:T(8,128)(2,1)S(1)}, u32[]{:S(2)}, u32[]{:S(2)}) collective-permute-start(bf16[96,256]{1,0:T(8,128)(2,1)S(1)} %get-tuple-element.38.refs_1_), channel_id=1, source_target_pairs={{0,4},{1,5},{2,6},{3,7},{4,0},{5,1},{6,2},{7,3},{8,12},{9,13},{10,... | collective-permute-start | bytes 147464 | tf_op jit(solution)/shard_map/ppermute | solution.py:263
  36.4 2.7 %collective-permute-start.10 = (bf16[96,256]{1,0:T(8,128)(2,1)S(1)}, bf16[96,256]{1,0:T(8,128)(2,1)S(1)}, u32[]{:S(2)}, u32[]{:S(2)}) collective-permute-start(bf16[96,256]{1,0:T(8,128)(2,1)S(1)} %collective-permute-done.6.refs_3_), channel_id=1, source_target_pairs={{0,4},{1,5},{2,6},{3,7},{4,0},{5,1},{6,2},{7,3},{8,12},{9,13},{10,... | collective-permute-start | bytes 147464 | tf_op jit(solution)/shard_map/ppermute | solution.py:263
  37.0 2.7 %collective-permute-start.11 = (bf16[96,256]{1,0:T(8,128)(2,1)S(1)}, bf16[96,256]{1,0:T(8,128)(2,1)S(1)}, u32[]{:S(2)}, u32[]{:S(2)}) collective-permute-start(bf16[96,256]{1,0:T(8,128)(2,1)S(1)} %collective-permute-done.7.refs_4_), channel_id=1, source_target_pairs={{0,4},{1,5},{2,6},{3,7},{4,0},{5,1},{6,2},{7,3},{8,12},{9,13},{10,... | collective-permute-start | bytes 147464 | tf_op jit(solution)/shard_map/ppermute | solution.py:263
  38.5 1.9 %collective-permute-start.9 = (bf16[96,256]{1,0:T(8,128)(2,1)S(1)}, bf16[96,256]{1,0:T(8,128)(2,1)S(1)}, u32[]{:S(2)}, u32[]{:S(2)}) collective-permute-start(bf16[96,256]{1,0:T(8,128)(2,1)S(1)} %collective-permute-done.5.refs_2_), channel_id=1, source_target_pairs={{0,4},{1,5},{2,6},{3,7},{4,0},{5,1},{6,2},{7,3},{8,12},{9,13},{10,... | collective-permute-start | bytes 147464 | tf_op jit(solution)/shard_map/ppermute | solution.py:263
  91.6 2.2 %copy-start = (bf16[2048,1024]{1,0:T(8,128)(2,1)S(1)}, bf16[2048,1024]{1,0:T(8,128)(2,1)}, u32[]{:S(2)}) copy-start(bf16[2048,1024]{1,0:T(8,128)(2,1)} %all-gather.3.cloned.1.call-done) | copy-start | bytes 12582916
  93.8 0.8 copy-start.12
  94.6 0.8 copy-start.15
  96.2 10.1 %copy-start.1 = (bf16[2048,1024]{1,0:T(8,128)(2,1)S(1)}, bf16[2048,1024]{1,0:T(8,128)(2,1)}, u32[]{:S(2)}) copy-start(bf16[2048,1024]{1,0:T(8,128)(2,1)} %all-gather.3.cloned.1.call-done) | copy-start | bytes 12582916
  96.2 10.1 %copy-start.13 = (bf16[96,256]{1,0:T(8,128)(2,1)S(1)}, bf16[96,256]{1,0:T(8,128)(2,1)}, u32[]{:S(2)}) copy-start(bf16[96,256]{1,0:T(8,128)(2,1)} %copy-done.11) | copy-start | bytes 147460
  96.2 10.1 %copy-start.16 = (bf16[96,256]{1,0:T(8,128)(2,1)S(1)}, bf16[96,256]{1,0:T(8,128)(2,1)}, u32[]{:S(2)}) copy-start(bf16[96,256]{1,0:T(8,128)(2,1)} %copy-done.14) | copy-start | bytes 147460
  96.2 10.1 %copy-start.19 = (bf16[96,256]{1,0:T(8,128)(2,1)S(1)}, bf16[96,256]{1,0:T(8,128)(2,1)}, u32[]{:S(2)}) copy-start(bf16[96,256]{1,0:T(8,128)(2,1)} %copy-done.17) | copy-start | bytes 147460
  96.2 10.1 %copy-start.21 = (bf16[96,256]{1,0:T(8,128)(2,1)S(1)}, bf16[96,256]{1,0:T(8,128)(2,1)}, u32[]{:S(2)}) copy-start(bf16[96,256]{1,0:T(8,128)(2,1)} %copy-done.20) | copy-start | bytes 147460
  96.2 10.1 %copy-start.23 = (bf16[96,256]{1,0:T(8,128)(2,1)S(1)}, bf16[96,256]{1,0:T(8,128)(2,1)}, u32[]{:S(2)}) copy-start(bf16[96,256]{1,0:T(8,128)(2,1)} %copy-done.22) | copy-start | bytes 147460
  96.2 10.1 %copy-start.25 = (bf16[96,256]{1,0:T(8,128)(2,1)S(1)}, bf16[96,256]{1,0:T(8,128)(2,1)}, u32[]{:S(2)}) copy-start(bf16[96,256]{1,0:T(8,128)(2,1)} %copy-done.24) | copy-start | bytes 147460
  96.2 10.1 %copy-start.27 = (bf16[96,256]{1,0:T(8,128)(2,1)S(1)}, bf16[96,256]{1,0:T(8,128)(2,1)}, u32[]{:S(2)}) copy-start(bf16[96,256]{1,0:T(8,128)(2,1)} %copy-done.26) | copy-start | bytes 147460
  99.2 5.9 %collective-permute-start.13 = (bf16[192,128]{1,0:T(8,128)(2,1)S(1)}, bf16[192,128]{1,0:T(8,128)(2,1)S(1)}, u32[]{:S(2)}, u32[]{:S(2)}) collective-permute-start(bf16[192,128]{1,0:T(8,128)(2,1)S(1)} %get-tuple-element.42), channel_id=1, source_target_pairs={{0,1},{1,2},{2,3},{3,0},{4,5},{5,6},{6,7},{7,4},{8,9},{9,10},{10,1... | collective-permute-start | bytes 147464 | tf_op jit(solution)/shard_map/ppermute | solution.py:263
  100.7 5.0 %collective-permute-start.14 = (bf16[192,128]{1,0:T(8,128)(2,1)S(1)}, bf16[192,128]{1,0:T(8,128)(2,1)S(1)}, u32[]{:S(2)}, u32[]{:S(2)}) collective-permute-start(bf16[192,128]{1,0:T(8,128)(2,1)S(1)} %get-tuple-element.43), channel_id=1, source_target_pairs={{0,2},{1,3},{2,0},{3,1},{4,6},{5,7},{6,4},{7,5},{8,10},{9,11},{10,... | collective-permute-start | bytes 147464 | tf_op jit(solution)/shard_map/ppermute | solution.py:263
  101.7 4.5 %collective-permute-start.15 = (bf16[192,128]{1,0:T(8,128)(2,1)S(1)}, bf16[192,128]{1,0:T(8,128)(2,1)S(1)}, u32[]{:S(2)}, u32[]{:S(2)}) collective-permute-start(bf16[192,128]{1,0:T(8,128)(2,1)S(1)} %get-tuple-element.44), channel_id=1, source_target_pairs={{0,3},{1,0},{2,1},{3,2},{4,7},{5,4},{6,5},{7,6},{8,11},{9,8},{10,9... | collective-permute-start | bytes 147464 | tf_op jit(solution)/shard_map/ppermute | solution.py:263
  109.0 10.6 %copy-start.10 = (f32[384,256]{1,0:T(8,128)S(1)}, f32[384,256]{1,0:T(8,128)}, u32[]{:S(2)}) copy-start(f32[384,256]{1,0:T(8,128)} %copy-done.9) | copy-start | bytes 1179652
  109.0 17.7 %collective-permute-start.16 = (f32[96,2048]{1,0:T(8,128)S(1)}, f32[96,2048]{1,0:T(8,128)S(1)}, u32[]{:S(2)}, u32[]{:S(2)}) collective-permute-start(f32[96,2048]{1,0:T(8,128)S(1)} %get-tuple-element.46), channel_id=1, source_target_pairs={{0,4},{1,5},{2,6},{3,7},{4,0},{5,1},{6,2},{7,3},{8,12},{9,13},{10,... | collective-permute-start | bytes 2359304 | tf_op jit(solution)/shard_map/ppermute | solution.py:263
  109.1 17.6 %collective-permute-start.17 = (f32[96,2048]{1,0:T(8,128)S(1)}, f32[96,2048]{1,0:T(8,128)S(1)}, u32[]{:S(2)}, u32[]{:S(2)}) collective-permute-start(f32[96,2048]{1,0:T(8,128)S(1)} %get-tuple-element.47), channel_id=1, source_target_pairs={{0,4},{1,5},{2,6},{3,7},{4,0},{5,1},{6,2},{7,3},{8,12},{9,13},{10,... | collective-permute-start | bytes 2359304 | tf_op jit(solution)/shard_map/ppermute | solution.py:263
  109.6 3.0 %collective-permute-start.18 = (bf16[192,128]{1,0:T(8,128)(2,1)S(1)}, bf16[192,128]{1,0:T(8,128)(2,1)S(1)}, u32[]{:S(2)}, u32[]{:S(2)}) collective-permute-start(bf16[192,128]{1,0:T(8,128)(2,1)S(1)} %get-tuple-element.48.refs_2_), channel_id=1, source_target_pairs={{0,4},{1,5},{2,6},{3,7},{4,0},{5,1},{6,2},{7,3},{8,12},{9,13},{10,... | collective-permute-start | bytes 147464 | tf_op jit(solution)/shard_map/ppermute | solution.py:263
  109.7 3.0 %collective-permute-start.19 = (bf16[192,128]{1,0:T(8,128)(2,1)S(1)}, bf16[192,128]{1,0:T(8,128)(2,1)S(1)}, u32[]{:S(2)}, u32[]{:S(2)}) collective-permute-start(bf16[192,128]{1,0:T(8,128)(2,1)S(1)} %collective-permute-done.13.refs_10_.refs_3_), channel_id=1, source_target_pairs={{0,4},{1,5},{2,6},{3,7},{4,0},{5,1},{6,2},{7,3},{8,12},{9,13},{10,... | collective-permute-start | bytes 147464 | tf_op jit(solution)/shard_map/ppermute | solution.py:263
  110.1 2.6 %collective-permute-start.20 = (bf16[192,128]{1,0:T(8,128)(2,1)S(1)}, bf16[192,128]{1,0:T(8,128)(2,1)S(1)}, u32[]{:S(2)}, u32[]{:S(2)}) collective-permute-start(bf16[192,128]{1,0:T(8,128)(2,1)S(1)} %collective-permute-done.14.refs_11_.refs_4_), channel_id=1, source_target_pairs={{0,4},{1,5},{2,6},{3,7},{4,0},{5,1},{6,2},{7,3},{8,12},{9,13},{10,... | collective-permute-start | bytes 147464 | tf_op jit(solution)/shard_map/ppermute | solution.py:263
  112.6 1.2 collective-permute-start.21
  114.6 1.3 collective-permute-start.22
  115.9 6.6 %collective-permute-start.23 = (f32[128,128]{1,0:T(8,128)S(1)}, f32[128,128]{1,0:T(8,128)S(1)}, u32[]{:S(2)}, u32[]{:S(2)}) collective-permute-start(f32[128,128]{1,0:T(8,128)S(1)} %add.19), channel_id=1, source_target_pairs={{0,8},{1,9},{2,10},{3,11},{4,12},{5,13},{6,14},{7,15},{8,0},{9,1},... | collective-permute-start | bytes 196616 | tf_op jit(solution)/shard_map/ppermute | solution.py:263
  117.4 5.1 %collective-permute-start.24 = (f32[128,128]{1,0:T(8,128)S(1)}, f32[128,128]{1,0:T(8,128)S(1)}, u32[]{:S(2)}, u32[]{:S(2)}) collective-permute-start(f32[128,128]{1,0:T(8,128)S(1)} %add.19), channel_id=1, source_target_pairs={{0,16},{1,17},{2,18},{3,19},{4,20},{5,21},{6,22},{7,23},{8,24},{9,... | collective-permute-start | bytes 196616 | tf_op jit(solution)/shard_map/ppermute | solution.py:263
  118.0 5.2 %collective-permute-start.25 = (f32[128,128]{1,0:T(8,128)S(1)}, f32[128,128]{1,0:T(8,128)S(1)}, u32[]{:S(2)}, u32[]{:S(2)}) collective-permute-start(f32[128,128]{1,0:T(8,128)S(1)} %add.19), channel_id=1, source_target_pairs={{0,24},{1,25},{2,26},{3,27},{4,28},{5,29},{6,30},{7,31},{8,16},{9,... | collective-permute-start | bytes 196616 | tf_op jit(solution)/shard_map/ppermute | solution.py:263
  123.8 1.3 collective-permute-start.26
  (9 other events, 5.9 us)
Sparse Core Ops, SparseCore 0:
  10.8 80.7 all-gather.2

commit v5 on v4

--- a/solution.py
+++ b/solution.py
@@ -27,13 +27,7 @@
     return dot(a, high, dims) + dot(a, low, dims)
 
 
-def whole_block(shape):
-    return pl.BlockSpec(shape, lambda i: (0,) * len(shape))
-
-
-def call(body, outs, args, smem=(), after=(), steps=1, specs=None, scratch=(), room=16, flops=1):
-    ins, results = specs or ([whole_block(a.shape) for a in args], [whole_block(o) for o, _ in outs])
-
+def call(body, outs, args, smem=(), after=(), room=8, flops=1):
     def kernel(*refs):
         first = len(smem) + len(args)
         body(*refs[:first], *refs[first + len(after) :])
@@ -42,13 +36,11 @@
     moved += sum(math.prod(s) * jnp.dtype(t).itemsize for s, t in outs)
     return pl.pallas_call(
         kernel,
-        grid=(steps,),
         out_shape=[jax.ShapeDtypeStruct(s, t) for s, t in outs],
         in_specs=[pl.BlockSpec(memory_space=pltpu.SMEM) for _ in smem]
-        + list(ins)
+        + [pl.BlockSpec(memory_space=pltpu.VMEM) for _ in args]
         + [pl.BlockSpec(memory_space=pl.ANY) for _ in after],
-        out_specs=list(results),
-        scratch_shapes=list(scratch),
+        out_specs=[pl.BlockSpec(memory_space=pltpu.VMEM) for _ in outs],
         compiler_params=pltpu.CompilerParams(vmem_limit_bytes=room * MIB),
         cost_estimate=pl.CostEstimate(
             flops=int(flops), bytes_accessed=int(moved), transcendentals=0
@@ -131,51 +123,46 @@
             out_refs[s][:, cols] = (pre_ref[here, cols] + scale * inter).astype(BF16)
 
 
-def grad_kernel(count, where, mine_ref, mate_ref, weight_ref, *refs):
-    outs, total_ref = refs[:-1], refs[-1]
-    own = mine_ref.shape[0]
-    step = pl.program_id(0)
-    part = dot(jnp.concatenate([mine_ref[...], mate_ref[...]], 0), weight_ref[0], NT)
-
-    @pl.when(step == 0)
-    def _():
-        total_ref[...] = part
-
-    @pl.when(step > 0)
-    def _():
-        total_ref[...] += part
-
-    @pl.when(step == pl.num_programs(0) - 1)
-    def _():
-        for s in range(count):
-            z = lax.rem(where[0] + s, count)
-            block = total_ref[:, pl.ds(pl.multiple_of(z * DH, DH), DH)].astype(BF16)
-            outs[s][...] = block
-
-
-def mixed_kernel(count, where, *refs):
-    attn, mate = refs[:count], refs[count : 2 * count]
-    weight_ref, own_out, *mate_outs, left_ref = refs[2 * count :]
-    step = pl.program_id(0)
-    each = pl.num_programs(0) // len(mate_outs)
+def cut_kernel(piece_ref, *out_refs):
+    wide = out_refs[0].shape[1]
+    for n, out_ref in enumerate(out_refs):
+        out_ref[...] = piece_ref[:, n * wide : (n + 1) * wide]
+
+
+def grad_kernel(whole, added, places, mine_ref, mate_ref, *refs):
+    chunks, out_ref = refs[added:-1], refs[-1]
+    total = refs[0][...] if added else None
+    for j, chunk in enumerate(chunks):
+        cols = slice(None) if whole else pl.ds(pl.multiple_of(places[j], DH), chunk.shape[1])
+        left = jnp.concatenate([mine_ref[:, cols], mate_ref[:, cols]], 0)
+        part = dot(left, chunk[...], NT)
+        total = part if total is None else total + part
+    out_ref[...] = total.astype(out_ref.dtype)
+
+
+def mixed_kernel(count, each, places, where, *refs):
+    attn, mate, weight = refs[:count], refs[count : 2 * count], refs[2 * count]
+    chunks, (own_out, mate_out) = list(refs[2 * count + 1 : -2]), refs[-2:]
     own = own_out.shape[0]
-
-    @pl.when(step == 0)
-    def _():
-        cols = pl.ds(pl.multiple_of(where[2] * DH, DH), DH)
-        for s in range(count):
-            z = lax.rem(where[0] - s + count, count)
-            there = pl.ds(pl.multiple_of(z * DH, DH), DH)
-            left_ref[:own, there] = attn[s][:, cols]
-            left_ref[own:, there] = mate[s][:, cols]
-
-    part = dot(left_ref[...], weight_ref[0], NN)
+    cols = pl.ds(pl.multiple_of(where[2] * DH, DH), DH)
+    left = jnp.concatenate(
+        [jnp.concatenate([attn[s][:, cols], mate[s][:, cols]], 0) for s in range(count)], 1
+    )
+    right = [weight[:, pl.ds(pl.multiple_of(places[0], DH), own_out.shape[1])]]
+    for n in each:
+        parts = [chunks.pop(0)[...] for _ in range(n)]
+        right.append(jnp.concatenate(parts, 1) if n > 1 else parts[0])
+    part = dot(left, jnp.concatenate(right, 0), NN)
     own_out[...] = part[:own]
-    for n, mate_out in enumerate(mate_outs):
-
-        @pl.when(step // each == n)
-        def _():
-            mate_out[...] = part[own:]
+    mate_out[...] = part[own:]
+
+
+def join_kernel(places, *refs):
+    out_ref = refs[-1]
+    for n in range(len(refs) // 2):
+        wide = refs[2 * n].shape[1]
+        there = pl.ds(pl.multiple_of(places[n], DH), wide)
+        out_ref[:, there] = (refs[2 * n][...] + refs[2 * n + 1][...]).astype(BF16)
 
 
 def collect_kernel(scale, count, where, q_ref, *refs):
@@ -185,7 +172,7 @@
     mine = pl.ds(pl.multiple_of(where[2] * DH, DH), DH)
     mate = pl.ds(pl.multiple_of((1 - where[2]) * DH, DH), DH)
     for s in range(count):
-        block = lax.rem(where[0] - s + count, count)
+        block = lax.rem(where[0] + s, count)
         here = pl.ds(pl.multiple_of(block * own, own), own)
         g_ref[here, mine] = direct[s][:own]
         g_ref[here, mate] = across[s][own:]
@@ -295,12 +282,20 @@
     where = jnp.stack([place, ctx, core])
     flat, square = (rows, width), rows * rows * DH * heads
     pair = [((DH, DH), F32)] * 2
-
-    wide = model // chips
-    piece = lax.dynamic_slice(out_weight, (core * DH, chip * wide), (DH, wide))
-    groups = [[c * count + z for c in range(k, shards, 2) for z in range(count)] for k in range(2)]
-    weight = lax.all_gather(piece, ("ctx", "head"), axis_index_groups=groups)
-    weight = weight.reshape(chips, count * DH, wide)
+    product = 4 * own * DH * model
+
+    board = chips == 4
+    wide = model // (2 if board else chips)
+    colour = (chip & 1) ^ (chip >> 1) if board else chip
+    piece = lax.dynamic_slice(out_weight, (core * DH, colour * wide), (DH, wide))
+    weight = lax.dynamic_slice_in_dim(out_weight, core * DH, DH, 0)
+    near = (colour * wide if board else jnp.int32(0)).reshape(1)
+    far = jnp.stack([(1 - colour) * wide, (1 - colour) * wide + wide // 2])
+    shifts = sorted(range(1, count), key=lambda s: min(s, count - s))
+    arrived = {0: piece}
+    for s in shifts:
+        step = 1 if s <= count // 2 else -1
+        arrived[s] = send(arrived[(s - step) % count], 0, step)
     mate_cotangent = send(cotangent, 1, 0)
 
     mine, other = call(state_kernel, pair, [key, value], [where], [piece])
@@ -323,49 +318,67 @@
     attn = [attn[0]] + [send(attn[s], 0, s) for s in range(1, count)]
     mate_attn = [send(a, 1, 0) for a in attn]
 
-    part_of = pl.BlockSpec((own, wide), lambda i: (0, i))
-    weight_of = pl.BlockSpec((1, count * DH, wide), lambda i: (i, 0, 0))
-    both = call(
-        functools.partial(grad_kernel, count),
-        [((2 * own, DH), BF16)] * count,
-        [cotangent, mate_cotangent, weight],
-        [where],
-        mate_attn,
-        chips,
-        ([part_of, part_of, weight_of], [whole_block((2 * own, DH))] * count),
-        [pltpu.VMEM((2 * own, count * DH), F32)],
-        flops=4 * own * count * DH * model,
-    )
-    both = [both[0]] + [send(both[s], 0, s) for s in range(1, count)]
-    across = [send(b, 1, 0) for b in both]
-    cut = 2
-    each = chips // cut
-    cuts = [
-        pl.BlockSpec((own, wide), lambda i, n=n: (0, jnp.clip(i - n * each, 0, each - 1)))
-        for n in range(cut)
-    ]
-    part, *mate_parts = call(
-        functools.partial(mixed_kernel, count),
-        [((own, model), F32)] + [((own, model // cut), F32)] * cut,
-        [*attn, *mate_attn, weight],
-        [where],
-        both[1:],
-        chips,
-        ([whole_block((own, width))] * (2 * count) + [weight_of], [part_of, *cuts]),
-        [pltpu.VMEM((2 * own, count * DH), BF16)],
-        flops=4 * own * count * DH * model,
-    )
+    first, second = {}, {}
+    for n, s in enumerate(shifts):
+        if not board:
+            groups = [list(range(k, shards, 2)) for k in range(2)]
+            whole = lax.all_gather(arrived[s], "ctx", axis=1, tiled=True, axis_index_groups=groups)
+            first[s], second[s] = whole, []
+        elif n < 2:
+            first[s], second[s] = arrived[s], [send(arrived[s], 2 + 2 * n, 0)]
+        else:
+            cut = [((DH, wide // 2), BF16)] * 2
+            left, right = call(cut_kernel, cut, [arrived[s]], after=mate_attn)
+            first[s], second[s] = arrived[s], [send(left, 2, 0), send(right, 4, 0)]
+
+    def grads(some, places, whole=False, earlier=(), last=True, after=()):
+        (both,) = call(
+            functools.partial(grad_kernel, whole, len(earlier)),
+            [((2 * own, DH), BF16 if last else F32)],
+            [cotangent, mate_cotangent, *earlier, *some],
+            [places],
+            after,
+            flops=product,
+        )
+        return both
+
+    def mix(each, places, after=()):
+        wide = sum(a.shape[1] for a in each[0])
+        return call(
+            functools.partial(mixed_kernel, count, [len(some) for some in each]),
+            [((own, wide), F32)] * 2,
+            [*attn, *mate_attn, weight, *(a for some in each for a in some)],
+            [places, where],
+            after,
+            room=16,
+            flops=count * product,
+        )
+
+    both = {0: grads([weight], near, True)}
+    end = shifts[-1]
+    for s in shifts[:-1]:
+        half = [grads([first[s]], near, last=False)] if board else []
+        some, places = (second[s], far) if board else ([first[s]], near)
+        both[s] = send(grads(some, places, earlier=half), 0, -s)
+    half = [grads([first[end]], near, last=False)] if board else []
+    part, mate_part = mix([[first[s]] for s in range(1, count)], near)
+    joins, starts = [part, send(mate_part, 1, 0)], [near]
+    some, places = (second[end], far) if board else ([first[end]], near)
+    early = [part, *(both[s] for s in [0] + shifts[:-1])]
+    both[end] = send(grads(some, places, earlier=half, after=early), 0, -end)
+    across = [send(both[s], 1, 0) for s in range(count)]
+    if board:
+        part, mate_part = mix([second[s] for s in range(1, count)], far, [both[end]])
+        joins, starts = [*joins, part, send(mate_part, 1, 0)], [near, far[:1]]
+
     g, mine, other = call(
         functools.partial(collect_kernel, scale, count),
         [(flat, BF16), *pair],
-        [query, *both, *across],
+        [query, *(both[s] for s in range(count)), *across],
         [where],
         [part],
     )
     flags, parts = exchange(mine, other, core, chip, chips, True)
-
-    mate_part = jnp.concatenate([send(p, 1, 0) for p in mate_parts], 1)
-
     grad_query, dk, dv = call(
         functools.partial(backward_kernel, scale, blocks),
         [(flat, BF16)] + [(flat, F32)] * 2,
@@ -377,7 +390,7 @@
     grad_key, grad_value = call(
         close_kernel, [(flat, BF16)] * 2, [key, value, dk, dv, keep, send(back, 1, 0)], [where]
     )
-    mixed = (part + mate_part).astype(BF16)
+    (mixed,) = call(join_kernel, [((own, model), BF16)], joins, [jnp.concatenate(starts)])
     return mixed, grad_query, grad_key, grad_value
 
 

time: 135 us -> 96.8 us (0.72)
  waiting for transfers between devices: 68.4 us -> 37.3 us
  between operations: 14.3 us -> 1.13 us
  Pallas kernels: 16 us -> 23.1 us
  local copies, waits for them, and re-layouts: 14.3 us -> 9.63 us
  starting transfers between devices: 20.2 us -> 24.7 us
    all_gather x1 -> x0, waiting for transfers between devices: 50.6 us -> none  [on_device(): weight = lax.all_gather(piece, ('ctx', 'head'), axis_index_groups=groups)]
    ppermute x27 -> x34, waiting for transfers between devices: 17.8 us -> 37.3 us  [send(): return lax.ppermute(x, ('ctx', 'head'), pairs)]
    pallas_call x10 -> x19, Pallas kernels: 16 us -> 23.1 us  [call(): pl.pallas_call(kernel, out_shape=[jax.ShapeDtypeStruct(s, t) for s, t in...]
    unnamed x58 -> x50, local copies, waits for them, and re-layouts: 12.5 us -> 7.18 us
    ppermute x27 -> x34, starting transfers between devices: 20.2 us -> 24.7 us  [send(): return lax.ppermute(x, ('ctx', 'head'), pairs)]
  transfers between devices with their start and end apart: 28 -> 34, of which waited for: 15 -> 15; matrix products, arithmetic and copies ran while one was open for 0% -> 2% of each run, Pallas kernels for 8% -> 21%
where the time goes in v5:
time: 96.8 us; the launch traced here: 96.4 us
  waiting for transfers between devices  37.3 us (39%)
  starting transfers between devices  24.7 us (26%)
  Pallas kernels  23.1 us (24%)
  local copies, waits for them, and re-layouts  9.63 us (10%)
  between operations  1.13 us (1%)
    ppermute x34, waiting for transfers between devices, send(): return lax.ppermute(x, ('ctx', 'head'), pairs)  37.3 us
    ppermute x34, starting transfers between devices, send(): return lax.ppermute(x, ('ctx', 'head'), pairs)  24.7 us
    pallas_call x19, Pallas kernels, call(): pl.pallas_call(kernel, out_shape=[jax.ShapeDtypeStruct(s, t) for s, t in...  23.1 us
    unnamed x50, local copies, waits for them, and re-layouts  7.18 us
  transfers between devices with their start and end apart: 34, of which 15 were waited for; matrix products, arithmetic and copies ran while one was open for 2% of the time, Pallas kernels for 21%

profile of v5, /device:TPU:0, one launch (start us, length us, event | category | flops | bytes accessed | tf_op | source)
XLA Modules:
  0.0 96.4 jit_solution(4076843398323210939)
XLA Ops:
  0.7 1.2 %dynamic_slice.6.refs_3_ = bf16[128,2048]{1,0:T(8,128)(2,1)S(1)} dynamic-slice(bf16[256,4096]{1,0:T(8,128)(2,1)} %param.10, s32[]{:T(128)S(6)} %select_n.7, s32[]{:T(128)S(6)} %select_n.8), dynamic_slice_sizes={128,2048} | dynamic-slice | bytes 1048580 | tf_op jit(solution)/shard_map/dynamic_slice | solution.py:290
  1.8 3.1 %collective-permute-start.12 = (bf16[128,2048]{1,0:T(8,128)(2,1)S(1)}, bf16[128,2048]{1,0:T(8,128)(2,1)}, u32[]{:S(2)}, u32[]{:S(2)}) collective-permute-start(bf16[128,2048]{1,0:T(8,128)(2,1)S(1)} %dynamic_slice.6.refs_3_), channel_id=1, source_target_pairs={{0,1},{1,2},{2,3},{3,0},{4,5},{5,6},{6,7},{7,4},{8,9},{9,10},{10,1... | collective-permute-start | bytes 1572872 | tf_op jit(solution)/shard_map/ppermute | solution.py:250
  4.9 2.1 %collective-permute-start.14 = (bf16[128,2048]{1,0:T(8,128)(2,1)S(1)}, bf16[128,2048]{1,0:T(8,128)(2,1)}, u32[]{:S(2)}, u32[]{:S(2)}) collective-permute-start(bf16[128,2048]{1,0:T(8,128)(2,1)S(1)} %dynamic_slice.6.refs_3_), channel_id=1, source_target_pairs={{0,3},{1,0},{2,1},{3,2},{4,7},{5,4},{6,5},{7,6},{8,11},{9,8},{10,9... | collective-permute-start | bytes 1572872 | tf_op jit(solution)/shard_map/ppermute | solution.py:250
  7.1 0.9 copy-done.2
  8.0 0.9 copy-done.5
  8.9 0.8 shard_map.94
  9.8 1.2 %collective-permute-done.refs_2_ = f32[128,128]{1,0:T(8,128)S(1)} collective-permute-done((f32[128,128]{1,0:T(8,128)S(1)}, f32[128,128]{1,0:T(8,128)S(1)}, u32[]{:S(2)}, u32[]{:S(2)}) %collective-permute-start) | collective-permute-done | bytes 65568 | tf_op jit(solution)/shard_map/ppermute | solution.py:250
  11.1 1.7 %collective-permute-start.1 = (f32[128,128]{1,0:T(8,128)S(1)}, f32[128,128]{1,0:T(8,128)S(1)}, u32[]{:S(2)}, u32[]{:S(2)}) collective-permute-start(f32[128,128]{1,0:T(8,128)S(1)} %add.18), channel_id=1, source_target_pairs={{0,8},{1,9},{2,10},{3,11},{4,12},{5,13},{6,14},{7,15},{8,0},{9,1},... | collective-permute-start | bytes 196616 | tf_op jit(solution)/shard_map/ppermute | solution.py:250
  12.8 1.5 %collective-permute-start.2 = (f32[128,128]{1,0:T(8,128)S(1)}, f32[128,128]{1,0:T(8,128)S(1)}, u32[]{:S(2)}, u32[]{:S(2)}) collective-permute-start(f32[128,128]{1,0:T(8,128)S(1)} %add.18), channel_id=1, source_target_pairs={{0,16},{1,17},{2,18},{3,19},{4,20},{5,21},{6,22},{7,23},{8,24},{9,... | collective-permute-start | bytes 196616 | tf_op jit(solution)/shard_map/ppermute | solution.py:250
  14.7 0.7 collective-permute-done.1.refs_3_
  15.4 1.6 %collective-permute-done.2.refs_4_ = f32[128,128]{1,0:T(8,128)S(1)} collective-permute-done((f32[128,128]{1,0:T(8,128)S(1)}, f32[128,128]{1,0:T(8,128)S(1)}, u32[]{:S(2)}, u32[]{:S(2)}) %collective-permute-start.2) | collective-permute-done | bytes 65568 | tf_op jit(solution)/shard_map/ppermute | solution.py:250
  17.0 2.4 %collective-permute-done.3.refs_5_ = f32[128,128]{1,0:T(8,128)S(1)} collective-permute-done((f32[128,128]{1,0:T(8,128)S(1)}, f32[128,128]{1,0:T(8,128)S(1)}, u32[]{:S(2)}, u32[]{:S(2)}) %collective-permute-start.3) | collective-permute-done | bytes 65568 | tf_op jit(solution)/shard_map/ppermute | solution.py:250
  20.6 0.9 copy-done.3
  21.6 0.9 copy-done.6
  22.5 2.3 %shard_map.93 = (bf16[2,384,384]{2,1,0:T(8,128)(2,1)S(1)}, bf16[2,384,384]{2,1,0:T(8,128)(2,1)S(1)}, f32[384,256]{1,0:T(8,128)S(1)}, f32[384,256]{1,0:T(8,128)S(1)}) custom-call(s32[3,3]{1,0:T(4,128)S(1)} %copy-done.24, bf16[384,256]{1,0:T(8,128)(2,1)S(1)} %copy-done.1, bf16[384,256]{1,0:T(8,128)(2,1)S(1)} %copy-done.3, bf16[384,256]{1,0:T(8,128)(2,1)S(1)} %copy-done.6), custom_call_target="tpu_custom_call" | custom-call | flops 226492416 | bytes 2555904 | tf_op jit(solution)/shard_map/pallas_call | solution.py:37
  24.8 0.8 copy-done.8
  25.6 0.8 copy-done.12
  26.4 0.8 shard_map.96
  27.2 0.9 collective-permute-start.6
  28.1 1.3 %collective-permute-start.7 = (bf16[96,256]{1,0:T(8,128)(2,1)S(1)}, bf16[96,256]{1,0:T(8,128)(2,1)S(1)}, u32[]{:S(2)}, u32[]{:S(2)}) collective-permute-start(bf16[96,256]{1,0:T(8,128)(2,1)S(1)} %get-tuple-element.40), channel_id=1, source_target_pairs={{0,3},{1,0},{2,1},{3,2},{4,7},{5,4},{6,5},{7,6},{8,11},{9,8},{10,9... | collective-permute-start | bytes 147464 | tf_op jit(solution)/shard_map/ppermute | solution.py:250
  29.4 3.4 %collective-permute-done.6.refs_4_ = bf16[96,256]{1,0:T(8,128)(2,1)S(1)} collective-permute-done((bf16[96,256]{1,0:T(8,128)(2,1)S(1)}, bf16[96,256]{1,0:T(8,128)(2,1)S(1)}, u32[]{:S(2)}, u32[]{:S(2)}) %collective-permute-start.6) | collective-permute-done | bytes 49184 | tf_op jit(solution)/shard_map/ppermute | solution.py:250
  33.6 5.2 %collective-permute-done.5.refs_3_ = bf16[96,256]{1,0:T(8,128)(2,1)} collective-permute-done((bf16[96,256]{1,0:T(8,128)(2,1)S(1)}, bf16[96,256]{1,0:T(8,128)(2,1)}, u32[]{:S(2)}, u32[]{:S(2)}) %collective-permute-start.5) | collective-permute-done | bytes 49184 | tf_op jit(solution)/shard_map/ppermute | solution.py:250
  40.9 1.1 %collective-permute-start.16 = (bf16[128,2048]{1,0:T(8,128)(2,1)}, bf16[128,2048]{1,0:T(8,128)(2,1)}, u32[]{:S(2)}, u32[]{:S(2)}) collective-permute-start(bf16[128,2048]{1,0:T(8,128)(2,1)} %collective-permute-done.12.refs_11_.refs_3_), channel_id=1, source_target_pairs={{0,8},{1,9},{2,10},{3,11},{4,12},{5,13},{6,14},{7,15},{8,0},{9,1},... | collective-permute-start | bytes 1572872 | tf_op jit(solution)/shard_map/ppermute | solution.py:250
  42.0 1.4 %collective-permute-start.19 = (bf16[128,2048]{1,0:T(8,128)(2,1)}, bf16[128,2048]{1,0:T(8,128)(2,1)}, u32[]{:S(2)}, u32[]{:S(2)}) collective-permute-start(bf16[128,2048]{1,0:T(8,128)(2,1)} %collective-permute-done.14.refs_13_.refs_3_), channel_id=1, source_target_pairs={{0,16},{1,17},{2,18},{3,19},{4,20},{5,21},{6,22},{7,23},{8,24},{9,... | collective-permute-start | bytes 1572872 | tf_op jit(solution)/shard_map/ppermute | solution.py:250
  43.4 1.3 %constant_dynamic-slice_fusion.refs_10_.refs_3_ = bf16[128,4096]{1,0:T(8,128)(2,1)S(1)} fusion(bf16[256,4096]{1,0:T(8,128)(2,1)} %param.10, s32[]{:T(128)S(6)} %select_n.7), kind=kLoop, calls=%fused_computation.5 | loop fusion | bytes 2097156 | tf_op jit(solution)/shard_map/dynamic_slice | solution.py:291
  44.7 11.0 %collective-permute-done.13.refs_12_.refs_0_.refs_3_ = bf16[128,2048]{1,0:T(8,128)(2,1)S(1)} collective-permute-done((bf16[128,2048]{1,0:T(8,128)(2,1)}, bf16[128,2048]{1,0:T(8,128)(2,1)S(1)}, u32[]{:S(2)}, u32[]{:S(2)}) %collective-permute-start.13) | collective-permute-done | bytes 524320 | tf_op jit(solution)/shard_map/ppermute | solution.py:250
  55.8 1.2 %collective-permute-start.17 = (bf16[128,1024]{1,0:T(8,128)(2,1)S(1)}, bf16[128,1024]{1,0:T(8,128)(2,1)S(1)}, u32[]{:S(2)}, u32[]{:S(2)}) collective-permute-start(bf16[128,1024]{1,0:T(8,128)(2,1)S(1)} %get-tuple-element.43), channel_id=1, source_target_pairs={{0,8},{1,9},{2,10},{3,11},{4,12},{5,13},{6,14},{7,15},{8,0},{9,1},... | collective-permute-start | bytes 786440 | tf_op jit(solution)/shard_map/ppermute | solution.py:250
  57.0 1.4 %collective-permute-start.18 = (bf16[128,1024]{1,0:T(8,128)(2,1)S(1)}, bf16[128,1024]{1,0:T(8,128)(2,1)S(1)}, u32[]{:S(2)}, u32[]{:S(2)}) collective-permute-start(bf16[128,1024]{1,0:T(8,128)(2,1)S(1)} %get-tuple-element.44), channel_id=1, source_target_pairs={{0,16},{1,17},{2,18},{3,19},{4,20},{5,21},{6,22},{7,23},{8,24},{9,... | collective-permute-start | bytes 786440 | tf_op jit(solution)/shard_map/ppermute | solution.py:250
  58.5 1.4 %shard_map.101.refs_3_ = f32[192,128]{1,0:T(8,128)S(1)} custom-call(s32[1]{0:T(128)} %bitcast.refs_0_, bf16[96,4096]{1,0:T(8,128)(2,1)S(1)} %copy-done, bf16[96,4096]{1,0:T(8,128)(2,1)S(1)} %collective-permute-done.20.refs_2_, bf16[128,2048]{1,0:T(8,128)(2,1)} %collective-permute-done.12.refs_11_.refs_3_), custom_call_target="tpu_custom_call" | custom-call | flops 201326592 | bytes 2195456 | tf_op jit(solution)/shard_map/pallas_call | solution.py:37
  59.9 1.4 %shard_map.103.refs_3_ = f32[192,128]{1,0:T(8,128)S(1)} custom-call(s32[1]{0:T(128)} %bitcast.refs_0_, bf16[96,4096]{1,0:T(8,128)(2,1)S(1)} %copy-done, bf16[96,4096]{1,0:T(8,128)(2,1)S(1)} %collective-permute-done.20.refs_2_, bf16[128,2048]{1,0:T(8,128)(2,1)} %collective-permute-done.14.refs_13_.refs_3_), custom_call_target="tpu_custom_call" | custom-call | flops 201326592 | bytes 2195456 | tf_op jit(solution)/shard_map/pallas_call | solution.py:37
  61.9 1.4 %shard_map.102 = bf16[192,128]{1,0:T(8,128)(2,1)S(1)} custom-call(s32[2]{0:T(128)S(1)} %pad_add_fusion.2.refs_0_, bf16[96,4096]{1,0:T(8,128)(2,1)S(1)} %copy-done, bf16[96,4096]{1,0:T(8,128)(2,1)S(1)} %collective-permute-done.20.refs_2_, f32[192,128]{1,0:T(8,128)S(1)} %shard_map.101.refs_3_, bf16[128,2048]{1,0:T(8,128)(2,1)} %collective-permute-done.16.refs_4_.refs_11_), custom_call_target="tpu_custom_call" | custom-call | flops 201326592 | bytes 2244608 | tf_op jit(solution)/shard_map/pallas_call | solution.py:37
  63.4 1.4 %shard_map.104 = bf16[192,128]{1,0:T(8,128)(2,1)S(1)} custom-call(s32[2]{0:T(128)S(1)} %pad_add_fusion.2.refs_0_, bf16[96,4096]{1,0:T(8,128)(2,1)S(1)} %copy-done, bf16[96,4096]{1,0:T(8,128)(2,1)S(1)} %collective-permute-done.20.refs_2_, f32[192,128]{1,0:T(8,128)S(1)} %shard_map.103.refs_3_, bf16[128,2048]{1,0:T(8,128)(2,1)} %collective-permute-done.19.refs_4_.refs_14_), custom_call_target="tpu_custom_call" | custom-call | flops 201326592 | bytes 2244608 | tf_op jit(solution)/shard_map/pallas_call | solution.py:37
  64.8 2.1 %collective-permute-start.22 = (bf16[192,128]{1,0:T(8,128)(2,1)S(1)}, bf16[192,128]{1,0:T(8,128)(2,1)S(1)}, u32[]{:S(2)}, u32[]{:S(2)}) collective-permute-start(bf16[192,128]{1,0:T(8,128)(2,1)S(1)} %shard_map.104), channel_id=1, source_target_pairs={{0,1},{1,2},{2,3},{3,0},{4,5},{5,6},{6,7},{7,4},{8,9},{9,10},{10,1... | collective-permute-start | bytes 147464 | tf_op jit(solution)/shard_map/ppermute | solution.py:250
  67.3 1.8 %shard_map.97 = (f32[96,2048]{1,0:T(8,128)S(1)}, f32[96,2048]{1,0:T(8,128)S(1)}) custom-call(s32[1]{0:T(128)} %bitcast.refs_0_, s32[3]{0:T(128)S(1)} %pad_add_fusion.1.refs_0_.refs_1_, bf16[96,256]{1,0:T(8,128)(2,1)S(1)} %copy-done.19, bf16[96,256]{1,0:T(8,128)(2,1)} %collective-permute-done.5.refs_3_, bf16[96,256]{1,0:T(8,128)(2,1)S(1)} %copy-done.21, ...), custom_call_target="tpu_custom_call" | custom-call | flops 805306368 | bytes 4587520 | tf_op jit(solution)/shard_map/pallas_call | solution.py:37
  69.1 1.7 %collective-permute-done.22.refs_9_.refs_5_ = bf16[192,128]{1,0:T(8,128)(2,1)S(1)} collective-permute-done((bf16[192,128]{1,0:T(8,128)(2,1)S(1)}, bf16[192,128]{1,0:T(8,128)(2,1)S(1)}, u32[]{:S(2)}, u32[]{:S(2)}) %collective-permute-start.22) | collective-permute-done | bytes 49184 | tf_op jit(solution)/shard_map/ppermute | solution.py:250
  70.8 0.9 shard_map.105
  71.9 5.0 %collective-permute-done.23.refs_15_.refs_4_ = bf16[192,128]{1,0:T(8,128)(2,1)S(1)} collective-permute-done((bf16[192,128]{1,0:T(8,128)(2,1)S(1)}, bf16[192,128]{1,0:T(8,128)(2,1)S(1)}, u32[]{:S(2)}, u32[]{:S(2)}) %collective-permute-start.23) | collective-permute-done | bytes 49184 | tf_op jit(solution)/shard_map/ppermute | solution.py:250
  76.9 1.8 %shard_map.106 = (f32[96,2048]{1,0:T(8,128)S(1)}, f32[96,2048]{1,0:T(8,128)S(1)}) custom-call(s32[2]{0:T(128)S(1)} %pad_add_fusion.2.refs_0_, s32[3]{0:T(128)S(1)} %pad_add_fusion.1.refs_0_.refs_1_, bf16[96,256]{1,0:T(8,128)(2,1)S(1)} %copy-done.19, bf16[96,256]{1,0:T(8,128)(2,1)} %collective-permute-done.5.refs_3_, bf16[96,256]{1,0:T(8,128)(2,1)S(1)} %copy-done.21, ...), custom_call_target="tpu_custom_call" | custom-call | flops 805306368 | bytes 4587520 | tf_op jit(solution)/shard_map/pallas_call | solution.py:37
  79.8 1.3 %collective-permute-done.25.refs_6_ = bf16[192,128]{1,0:T(8,128)(2,1)S(1)} collective-permute-done((bf16[192,128]{1,0:T(8,128)(2,1)S(1)}, bf16[192,128]{1,0:T(8,128)(2,1)S(1)}, u32[]{:S(2)}, u32[]{:S(2)}) %collective-permute-start.25) | collective-permute-done | bytes 49184 | tf_op jit(solution)/shard_map/ppermute | solution.py:250
  81.3 1.1 %collective-permute-done.27.refs_8_ = bf16[192,128]{1,0:T(8,128)(2,1)S(1)} collective-permute-done((bf16[192,128]{1,0:T(8,128)(2,1)S(1)}, bf16[192,128]{1,0:T(8,128)(2,1)S(1)}, u32[]{:S(2)}, u32[]{:S(2)}) %collective-permute-start.27) | collective-permute-done | bytes 49184 | tf_op jit(solution)/shard_map/ppermute | solution.py:250
  82.4 0.8 shard_map.108
  83.4 1.1 %collective-permute-done.29.refs_2_ = f32[128,128]{1,0:T(8,128)S(1)} collective-permute-done((f32[128,128]{1,0:T(8,128)S(1)}, f32[128,128]{1,0:T(8,128)S(1)}, u32[]{:S(2)}, u32[]{:S(2)}) %collective-permute-start.29) | collective-permute-done | bytes 65568 | tf_op jit(solution)/shard_map/ppermute | solution.py:250
  85.2 0.9 collective-permute-start.31
  86.1 2.0 %collective-permute-start.32 = (f32[128,128]{1,0:T(8,128)S(1)}, f32[128,128]{1,0:T(8,128)S(1)}, u32[]{:S(2)}, u32[]{:S(2)}) collective-permute-start(f32[128,128]{1,0:T(8,128)S(1)} %add.20), channel_id=1, source_target_pairs={{0,24},{1,25},{2,26},{3,27},{4,28},{5,29},{6,30},{7,31},{8,16},{9,... | collective-permute-start | bytes 196616 | tf_op jit(solution)/shard_map/ppermute | solution.py:250
  88.2 2.9 %shard_map.109 = (bf16[384,256]{1,0:T(8,128)(2,1)}, f32[384,256]{1,0:T(8,128)S(1)}, f32[384,256]{1,0:T(8,128)S(1)}) custom-call(s32[3]{0:T(128)S(1)} %pad_add_fusion.1.refs_0_.refs_1_, bf16[384,256]{1,0:T(8,128)(2,1)S(1)} %copy-done.1, bf16[384,256]{1,0:T(8,128)(2,1)S(1)} %copy-done.4, bf16[384,256]{1,0:T(8,128)(2,1)S(1)} %copy-done.7, ...), custom_call_target="tpu_custom_call" | custom-call | flops 528482304 | bytes 3473408 | tf_op jit(solution)/shard_map/pallas_call | solution.py:37
  92.0 1.2 %collective-permute-done.33.refs_6_ = f32[128,128]{1,0:T(8,128)S(1)} collective-permute-done((f32[128,128]{1,0:T(8,128)S(1)}, f32[128,128]{1,0:T(8,128)S(1)}, u32[]{:S(2)}, u32[]{:S(2)}) %collective-permute-start.33) | collective-permute-done | bytes 65568 | tf_op jit(solution)/shard_map/ppermute | solution.py:250
  93.2 1.6 %shard_map.111 = (bf16[384,256]{1,0:T(8,128)(2,1)}, bf16[384,256]{1,0:T(8,128)(2,1)}) custom-call(s32[3]{0:T(128)S(1)} %pad_add_fusion.1.refs_0_.refs_1_, bf16[384,256]{1,0:T(8,128)(2,1)S(1)} %copy-done.4, bf16[384,256]{1,0:T(8,128)(2,1)S(1)} %copy-done.7, f32[384,256]{1,0:T(8,128)S(1)} %get-tuple-element.52.refs_6_.refs_3_, ...), custom_call_target="tpu_custom_call" | custom-call | flops 1 | bytes 1703936 | tf_op jit(solution)/shard_map/pallas_call | solution.py:37
  94.8 1.6 %shard_map.107 = bf16[96,4096]{1,0:T(8,128)(2,1)} custom-call(s32[2]{0:T(128)S(1)} %pad_add_fusion.refs_0_, f32[96,2048]{1,0:T(8,128)S(1)} %get-tuple-element.41.refs_6_.refs_1_, f32[96,2048]{1,0:T(8,128)S(1)} %collective-permute-done.15.refs_2_, f32[96,2048]{1,0:T(8,128)S(1)} %get-tuple-element.45.refs_3_.refs_10_, ...), custom_call_target="tpu_custom_call" | custom-call | flops 1 | bytes 3932160 | tf_op jit(solution)/shard_map/pallas_call | solution.py:37
  (98 shorter events, 9.0 us)
Async XLA Ops:
  0.6 19.5 %copy-start = (bf16[96,4096]{1,0:T(8,128)(2,1)S(1)}, bf16[96,4096]{1,0:T(8,128)(2,1)}, u32[]{:S(2)}) copy-start(bf16[96,4096]{1,0:T(8,128)(2,1)} %refs_1_.22) | copy-start | bytes 2359300
  0.6 20.0 %copy-start.1 = (bf16[384,256]{1,0:T(8,128)(2,1)S(1)}, bf16[384,256]{1,0:T(8,128)(2,1)}, u32[]{:S(2)}) copy-start(bf16[384,256]{1,0:T(8,128)(2,1)} %refs_1_.24) | copy-start | bytes 589828
  0.7 20.0 %copy-start.24 = (s32[3,3]{1,0:T(4,128)S(1)}, s32[3,3]{1,0:T(4,128)}, u32[]{:S(2)}) copy-start(s32[3,3]{1,0:T(4,128)} %refs_0_.1) | copy-start | bytes 112
  1.8 37.6 %collective-permute-start.12 = (bf16[128,2048]{1,0:T(8,128)(2,1)S(1)}, bf16[128,2048]{1,0:T(8,128)(2,1)}, u32[]{:S(2)}, u32[]{:S(2)}) collective-permute-start(bf16[128,2048]{1,0:T(8,128)(2,1)S(1)} %dynamic_slice.6.refs_3_), channel_id=1, source_target_pairs={{0,1},{1,2},{2,3},{3,0},{4,5},{5,6},{6,7},{7,4},{8,9},{9,10},{10,1... | collective-permute-start | bytes 1572872 | tf_op jit(solution)/shard_map/ppermute | solution.py:250
  4.9 37.1 %collective-permute-start.14 = (bf16[128,2048]{1,0:T(8,128)(2,1)S(1)}, bf16[128,2048]{1,0:T(8,128)(2,1)}, u32[]{:S(2)}, u32[]{:S(2)}) collective-permute-start(bf16[128,2048]{1,0:T(8,128)(2,1)S(1)} %dynamic_slice.6.refs_3_), channel_id=1, source_target_pairs={{0,3},{1,0},{2,1},{3,2},{4,7},{5,4},{6,5},{7,6},{8,11},{9,8},{10,9... | collective-permute-start | bytes 1572872 | tf_op jit(solution)/shard_map/ppermute | solution.py:250
  9.7 1.3 %collective-permute-start = (f32[128,128]{1,0:T(8,128)S(1)}, f32[128,128]{1,0:T(8,128)S(1)}, u32[]{:S(2)}, u32[]{:S(2)}) collective-permute-start(f32[128,128]{1,0:T(8,128)S(1)} %get-tuple-element.34), channel_id=1, source_target_pairs={{0,4},{1,5},{2,6},{3,7},{4,0},{5,1},{6,2},{7,3},{8,12},{9,13},{10,... | collective-permute-start | bytes 196616 | tf_op jit(solution)/shard_map/ppermute | solution.py:250
  11.1 4.3 %collective-permute-start.1 = (f32[128,128]{1,0:T(8,128)S(1)}, f32[128,128]{1,0:T(8,128)S(1)}, u32[]{:S(2)}, u32[]{:S(2)}) collective-permute-start(f32[128,128]{1,0:T(8,128)S(1)} %add.18), channel_id=1, source_target_pairs={{0,8},{1,9},{2,10},{3,11},{4,12},{5,13},{6,14},{7,15},{8,0},{9,1},... | collective-permute-start | bytes 196616 | tf_op jit(solution)/shard_map/ppermute | solution.py:250
  12.8 4.3 %collective-permute-start.2 = (f32[128,128]{1,0:T(8,128)S(1)}, f32[128,128]{1,0:T(8,128)S(1)}, u32[]{:S(2)}, u32[]{:S(2)}) collective-permute-start(f32[128,128]{1,0:T(8,128)S(1)} %add.18), channel_id=1, source_target_pairs={{0,16},{1,17},{2,18},{3,19},{4,20},{5,21},{6,22},{7,23},{8,24},{9,... | collective-permute-start | bytes 196616 | tf_op jit(solution)/shard_map/ppermute | solution.py:250
  14.3 5.2 %collective-permute-start.3 = (f32[128,128]{1,0:T(8,128)S(1)}, f32[128,128]{1,0:T(8,128)S(1)}, u32[]{:S(2)}, u32[]{:S(2)}) collective-permute-start(f32[128,128]{1,0:T(8,128)S(1)} %add.18), channel_id=1, source_target_pairs={{0,24},{1,25},{2,26},{3,27},{4,28},{5,29},{6,30},{7,31},{8,16},{9,... | collective-permute-start | bytes 196616 | tf_op jit(solution)/shard_map/ppermute | solution.py:250
  20.0 18.7 %copy-start.14 = (f32[128,128]{1,0:T(8,128)}, f32[128,128]{1,0:T(8,128)S(1)}, u32[]{:S(2)}) copy-start(f32[128,128]{1,0:T(8,128)S(1)} %get-tuple-element.35.refs_3_.refs_8_) | copy-start | bytes 196612
  20.1 6.3 %collective-permute-start.4 = (f32[128,128]{1,0:T(8,128)S(1)}, f32[128,128]{1,0:T(8,128)S(1)}, u32[]{:S(2)}, u32[]{:S(2)}) collective-permute-start(f32[128,128]{1,0:T(8,128)S(1)} %get-tuple-element.36), channel_id=1, source_target_pairs={{0,4},{1,5},{2,6},{3,7},{4,0},{5,1},{6,2},{7,3},{8,12},{9,13},{10,... | collective-permute-start | bytes 196616 | tf_op jit(solution)/shard_map/ppermute | solution.py:250
  20.1 38.3 %collective-permute-start.20 = (bf16[96,4096]{1,0:T(8,128)(2,1)S(1)}, bf16[96,4096]{1,0:T(8,128)(2,1)S(1)}, u32[]{:S(2)}, u32[]{:S(2)}) collective-permute-start(bf16[96,4096]{1,0:T(8,128)(2,1)S(1)} %copy-done), channel_id=1, source_target_pairs={{0,4},{1,5},{2,6},{3,7},{4,0},{5,1},{6,2},{7,3},{8,12},{9,13},{10,... | collective-permute-start | bytes 2359304 | tf_op jit(solution)/shard_map/ppermute | solution.py:250
  26.4 15.6 %copy-start.10 = (bf16[2,384,384]{2,1,0:T(8,128)(2,1)}, bf16[2,384,384]{2,1,0:T(8,128)(2,1)S(1)}, u32[]{:S(2)}) copy-start(bf16[2,384,384]{2,1,0:T(8,128)(2,1)S(1)} %get-tuple-element.49.refs_6_) | copy-start | bytes 1769476
  26.4 12.4 %copy-start.16 = (f32[128,128]{1,0:T(8,128)}, f32[128,128]{1,0:T(8,128)S(1)}, u32[]{:S(2)}) copy-start(f32[128,128]{1,0:T(8,128)S(1)} %collective-permute-done.4.refs_4_.refs_9_) | copy-start | bytes 196612
  27.2 5.6 %collective-permute-start.6 = (bf16[96,256]{1,0:T(8,128)(2,1)S(1)}, bf16[96,256]{1,0:T(8,128)(2,1)S(1)}, u32[]{:S(2)}, u32[]{:S(2)}) collective-permute-start(bf16[96,256]{1,0:T(8,128)(2,1)S(1)} %get-tuple-element.39), channel_id=1, source_target_pairs={{0,2},{1,3},{2,0},{3,1},{4,6},{5,7},{6,4},{7,5},{8,10},{9,11},{10,... | collective-permute-start | bytes 147464 | tf_op jit(solution)/shard_map/ppermute | solution.py:250
  28.1 4.9 %collective-permute-start.7 = (bf16[96,256]{1,0:T(8,128)(2,1)S(1)}, bf16[96,256]{1,0:T(8,128)(2,1)S(1)}, u32[]{:S(2)}, u32[]{:S(2)}) collective-permute-start(bf16[96,256]{1,0:T(8,128)(2,1)S(1)} %get-tuple-element.40), channel_id=1, source_target_pairs={{0,3},{1,0},{2,1},{3,2},{4,7},{5,4},{6,5},{7,6},{8,11},{9,8},{10,9... | collective-permute-start | bytes 147464 | tf_op jit(solution)/shard_map/ppermute | solution.py:250
  32.8 6.0 %collective-permute-start.5 = (bf16[96,256]{1,0:T(8,128)(2,1)S(1)}, bf16[96,256]{1,0:T(8,128)(2,1)}, u32[]{:S(2)}, u32[]{:S(2)}) collective-permute-start(bf16[96,256]{1,0:T(8,128)(2,1)S(1)} %get-tuple-element.38), channel_id=1, source_target_pairs={{0,1},{1,2},{2,3},{3,0},{4,5},{5,6},{6,7},{7,4},{8,9},{9,10},{10,1... | collective-permute-start | bytes 147464 | tf_op jit(solution)/shard_map/ppermute | solution.py:250
  33.0 6.4 %collective-permute-start.8 = (bf16[96,256]{1,0:T(8,128)(2,1)S(1)}, bf16[96,256]{1,0:T(8,128)(2,1)S(1)}, u32[]{:S(2)}, u32[]{:S(2)}) collective-permute-start(bf16[96,256]{1,0:T(8,128)(2,1)S(1)} %get-tuple-element.37.refs_2_), channel_id=1, source_target_pairs={{0,4},{1,5},{2,6},{3,7},{4,0},{5,1},{6,2},{7,3},{8,12},{9,13},{10,... | collective-permute-start | bytes 147464 | tf_op jit(solution)/shard_map/ppermute | solution.py:250
  38.8 1.8 %collective-permute-start.10 = (bf16[96,256]{1,0:T(8,128)(2,1)S(1)}, bf16[96,256]{1,0:T(8,128)(2,1)S(1)}, u32[]{:S(2)}, u32[]{:S(2)}) collective-permute-start(bf16[96,256]{1,0:T(8,128)(2,1)S(1)} %collective-permute-done.6.refs_4_), channel_id=1, source_target_pairs={{0,4},{1,5},{2,6},{3,7},{4,0},{5,1},{6,2},{7,3},{8,12},{9,13},{10,... | collective-permute-start | bytes 147464 | tf_op jit(solution)/shard_map/ppermute | solution.py:250
  39.4 16.3 %collective-permute-start.13 = (bf16[128,2048]{1,0:T(8,128)(2,1)}, bf16[128,2048]{1,0:T(8,128)(2,1)S(1)}, u32[]{:S(2)}, u32[]{:S(2)}) collective-permute-start(bf16[128,2048]{1,0:T(8,128)(2,1)} %collective-permute-done.12.refs_11_.refs_3_), channel_id=1, source_target_pairs={{0,1},{1,2},{2,3},{3,0},{4,5},{5,6},{6,7},{7,4},{8,9},{9,10},{10,1... | collective-permute-start | bytes 1572872 | tf_op jit(solution)/shard_map/ppermute | solution.py:250
  39.4 1.5 %collective-permute-start.11 = (bf16[96,256]{1,0:T(8,128)(2,1)S(1)}, bf16[96,256]{1,0:T(8,128)(2,1)S(1)}, u32[]{:S(2)}, u32[]{:S(2)}) collective-permute-start(bf16[96,256]{1,0:T(8,128)(2,1)S(1)} %collective-permute-done.7.refs_5_), channel_id=1, source_target_pairs={{0,4},{1,5},{2,6},{3,7},{4,0},{5,1},{6,2},{7,3},{8,12},{9,13},{10,... | collective-permute-start | bytes 147464 | tf_op jit(solution)/shard_map/ppermute | solution.py:250
  40.6 4.1 %collective-permute-start.9 = (bf16[96,256]{1,0:T(8,128)(2,1)}, bf16[96,256]{1,0:T(8,128)(2,1)S(1)}, u32[]{:S(2)}, u32[]{:S(2)}) collective-permute-start(bf16[96,256]{1,0:T(8,128)(2,1)} %collective-permute-done.5.refs_3_), channel_id=1, source_target_pairs={{0,4},{1,5},{2,6},{3,7},{4,0},{5,1},{6,2},{7,3},{8,12},{9,13},{10,... | collective-permute-start | bytes 147464 | tf_op jit(solution)/shard_map/ppermute | solution.py:250
  40.9 21.0 %collective-permute-start.16 = (bf16[128,2048]{1,0:T(8,128)(2,1)}, bf16[128,2048]{1,0:T(8,128)(2,1)}, u32[]{:S(2)}, u32[]{:S(2)}) collective-permute-start(bf16[128,2048]{1,0:T(8,128)(2,1)} %collective-permute-done.12.refs_11_.refs_3_), channel_id=1, source_target_pairs={{0,8},{1,9},{2,10},{3,11},{4,12},{5,13},{6,14},{7,15},{8,0},{9,1},... | collective-permute-start | bytes 1572872 | tf_op jit(solution)/shard_map/ppermute | solution.py:250
  42.0 21.4 %collective-permute-start.19 = (bf16[128,2048]{1,0:T(8,128)(2,1)}, bf16[128,2048]{1,0:T(8,128)(2,1)}, u32[]{:S(2)}, u32[]{:S(2)}) collective-permute-start(bf16[128,2048]{1,0:T(8,128)(2,1)} %collective-permute-done.14.refs_13_.refs_3_), channel_id=1, source_target_pairs={{0,16},{1,17},{2,18},{3,19},{4,20},{5,21},{6,22},{7,23},{8,24},{9,... | collective-permute-start | bytes 1572872 | tf_op jit(solution)/shard_map/ppermute | solution.py:250
  55.8 15.0 %collective-permute-start.17 = (bf16[128,1024]{1,0:T(8,128)(2,1)S(1)}, bf16[128,1024]{1,0:T(8,128)(2,1)S(1)}, u32[]{:S(2)}, u32[]{:S(2)}) collective-permute-start(bf16[128,1024]{1,0:T(8,128)(2,1)S(1)} %get-tuple-element.43), channel_id=1, source_target_pairs={{0,8},{1,9},{2,10},{3,11},{4,12},{5,13},{6,14},{7,15},{8,0},{9,1},... | collective-permute-start | bytes 786440 | tf_op jit(solution)/shard_map/ppermute | solution.py:250
  57.0 13.8 %collective-permute-start.18 = (bf16[128,1024]{1,0:T(8,128)(2,1)S(1)}, bf16[128,1024]{1,0:T(8,128)(2,1)S(1)}, u32[]{:S(2)}, u32[]{:S(2)}) collective-permute-start(bf16[128,1024]{1,0:T(8,128)(2,1)S(1)} %get-tuple-element.44), channel_id=1, source_target_pairs={{0,16},{1,17},{2,18},{3,19},{4,20},{5,21},{6,22},{7,23},{8,24},{9,... | collective-permute-start | bytes 786440 | tf_op jit(solution)/shard_map/ppermute | solution.py:250
  63.3 4.0 %copy-start.19 = (bf16[96,256]{1,0:T(8,128)(2,1)S(1)}, bf16[96,256]{1,0:T(8,128)(2,1)}, u32[]{:S(2)}) copy-start(bf16[96,256]{1,0:T(8,128)(2,1)} %copy-done.18) | copy-start | bytes 147460
  63.3 5.8 %collective-permute-start.21 = (bf16[192,128]{1,0:T(8,128)(2,1)S(1)}, bf16[192,128]{1,0:T(8,128)(2,1)S(1)}, u32[]{:S(2)}, u32[]{:S(2)}) collective-permute-start(bf16[192,128]{1,0:T(8,128)(2,1)S(1)} %shard_map.102), channel_id=1, source_target_pairs={{0,3},{1,0},{2,1},{3,2},{4,7},{5,4},{6,5},{7,6},{8,11},{9,8},{10,9... | collective-permute-start | bytes 147464 | tf_op jit(solution)/shard_map/ppermute | solution.py:250
  64.8 5.9 %collective-permute-start.22 = (bf16[192,128]{1,0:T(8,128)(2,1)S(1)}, bf16[192,128]{1,0:T(8,128)(2,1)S(1)}, u32[]{:S(2)}, u32[]{:S(2)}) collective-permute-start(bf16[192,128]{1,0:T(8,128)(2,1)S(1)} %shard_map.104), channel_id=1, source_target_pairs={{0,1},{1,2},{2,3},{3,0},{4,5},{5,6},{6,7},{7,4},{8,9},{9,10},{10,1... | collective-permute-start | bytes 147464 | tf_op jit(solution)/shard_map/ppermute | solution.py:250
  71.7 5.2 %collective-permute-start.23 = (bf16[192,128]{1,0:T(8,128)(2,1)S(1)}, bf16[192,128]{1,0:T(8,128)(2,1)S(1)}, u32[]{:S(2)}, u32[]{:S(2)}) collective-permute-start(bf16[192,128]{1,0:T(8,128)(2,1)S(1)} %shard_map.105), channel_id=1, source_target_pairs={{0,2},{1,3},{2,0},{3,1},{4,6},{5,7},{6,4},{7,5},{8,10},{9,11},{10,... | collective-permute-start | bytes 147464 | tf_op jit(solution)/shard_map/ppermute | solution.py:250
  71.8 16.4 %copy-start.4 = (bf16[384,256]{1,0:T(8,128)(2,1)S(1)}, bf16[384,256]{1,0:T(8,128)(2,1)}, u32[]{:S(2)}) copy-start(bf16[384,256]{1,0:T(8,128)(2,1)} %refs_1_.25) | copy-start | bytes 589828
  71.8 16.4 %copy-start.7 = (bf16[384,256]{1,0:T(8,128)(2,1)S(1)}, bf16[384,256]{1,0:T(8,128)(2,1)}, u32[]{:S(2)}) copy-start(bf16[384,256]{1,0:T(8,128)(2,1)} %refs_2_.7) | copy-start | bytes 589828
  71.8 16.4 %copy-start.9 = (bf16[2,384,384]{2,1,0:T(8,128)(2,1)S(1)}, bf16[2,384,384]{2,1,0:T(8,128)(2,1)}, u32[]{:S(2)}) copy-start(bf16[2,384,384]{2,1,0:T(8,128)(2,1)} %copy-done.8) | copy-start | bytes 1769476
  71.8 16.4 %copy-start.11 = (bf16[2,384,384]{2,1,0:T(8,128)(2,1)S(1)}, bf16[2,384,384]{2,1,0:T(8,128)(2,1)}, u32[]{:S(2)}) copy-start(bf16[2,384,384]{2,1,0:T(8,128)(2,1)} %copy-done.10) | copy-start | bytes 1769476
  71.8 16.4 %copy-start.13 = (f32[384,256]{1,0:T(8,128)S(1)}, f32[384,256]{1,0:T(8,128)}, u32[]{:S(2)}) copy-start(f32[384,256]{1,0:T(8,128)} %copy-done.12) | copy-start | bytes 1179652
  71.8 16.4 %copy-start.15 = (f32[128,128]{1,0:T(8,128)S(1)}, f32[128,128]{1,0:T(8,128)}, u32[]{:S(2)}) copy-start(f32[128,128]{1,0:T(8,128)} %copy-done.14) | copy-start | bytes 196612
  71.8 16.3 %copy-start.17 = (f32[128,128]{1,0:T(8,128)S(1)}, f32[128,128]{1,0:T(8,128)}, u32[]{:S(2)}) copy-start(f32[128,128]{1,0:T(8,128)} %copy-done.16) | copy-start | bytes 196612
  71.8 23.0 %collective-permute-start.15 = (f32[96,2048]{1,0:T(8,128)S(1)}, f32[96,2048]{1,0:T(8,128)S(1)}, u32[]{:S(2)}, u32[]{:S(2)}) collective-permute-start(f32[96,2048]{1,0:T(8,128)S(1)} %get-tuple-element.42), channel_id=1, source_target_pairs={{0,4},{1,5},{2,6},{3,7},{4,0},{5,1},{6,2},{7,3},{8,12},{9,13},{10,... | collective-permute-start | bytes 2359304 | tf_op jit(solution)/shard_map/ppermute | solution.py:250
  78.7 16.1 %collective-permute-start.24 = (f32[96,2048]{1,0:T(8,128)S(1)}, f32[96,2048]{1,0:T(8,128)S(1)}, u32[]{:S(2)}, u32[]{:S(2)}) collective-permute-start(f32[96,2048]{1,0:T(8,128)S(1)} %get-tuple-element.46), channel_id=1, source_target_pairs={{0,4},{1,5},{2,6},{3,7},{4,0},{5,1},{6,2},{7,3},{8,12},{9,13},{10,... | collective-permute-start | bytes 2359304 | tf_op jit(solution)/shard_map/ppermute | solution.py:250
  78.8 2.3 %collective-permute-start.25 = (bf16[192,128]{1,0:T(8,128)(2,1)S(1)}, bf16[192,128]{1,0:T(8,128)(2,1)S(1)}, u32[]{:S(2)}, u32[]{:S(2)}) collective-permute-start(bf16[192,128]{1,0:T(8,128)(2,1)S(1)} %shard_map.100.refs_7_.refs_2_), channel_id=1, source_target_pairs={{0,4},{1,5},{2,6},{3,7},{4,0},{5,1},{6,2},{7,3},{8,12},{9,13},{10,... | collective-permute-start | bytes 147464 | tf_op jit(solution)/shard_map/ppermute | solution.py:250
  79.3 2.0 %collective-permute-start.26 = (bf16[192,128]{1,0:T(8,128)(2,1)S(1)}, bf16[192,128]{1,0:T(8,128)(2,1)S(1)}, u32[]{:S(2)}, u32[]{:S(2)}) collective-permute-start(bf16[192,128]{1,0:T(8,128)(2,1)S(1)} %collective-permute-done.21.refs_8_.refs_3_), channel_id=1, source_target_pairs={{0,4},{1,5},{2,6},{3,7},{4,0},{5,1},{6,2},{7,3},{8,12},{9,13},{10,... | collective-permute-start | bytes 147464 | tf_op jit(solution)/shard_map/ppermute | solution.py:250
  79.4 1.9 %collective-permute-start.28 = (bf16[192,128]{1,0:T(8,128)(2,1)S(1)}, bf16[192,128]{1,0:T(8,128)(2,1)S(1)}, u32[]{:S(2)}, u32[]{:S(2)}) collective-permute-start(bf16[192,128]{1,0:T(8,128)(2,1)S(1)} %collective-permute-done.22.refs_9_.refs_5_), channel_id=1, source_target_pairs={{0,4},{1,5},{2,6},{3,7},{4,0},{5,1},{6,2},{7,3},{8,12},{9,13},{10,... | collective-permute-start | bytes 147464 | tf_op jit(solution)/shard_map/ppermute | solution.py:250
  81.1 1.2 %collective-permute-start.27 = (bf16[192,128]{1,0:T(8,128)(2,1)S(1)}, bf16[192,128]{1,0:T(8,128)(2,1)S(1)}, u32[]{:S(2)}, u32[]{:S(2)}) collective-permute-start(bf16[192,128]{1,0:T(8,128)(2,1)S(1)} %collective-permute-done.23.refs_15_.refs_4_), channel_id=1, source_target_pairs={{0,4},{1,5},{2,6},{3,7},{4,0},{5,1},{6,2},{7,3},{8,12},{9,13},{10,... | collective-permute-start | bytes 147464 | tf_op jit(solution)/shard_map/ppermute | solution.py:250
  83.2 1.3 %collective-permute-start.29 = (f32[128,128]{1,0:T(8,128)S(1)}, f32[128,128]{1,0:T(8,128)S(1)}, u32[]{:S(2)}, u32[]{:S(2)}) collective-permute-start(f32[128,128]{1,0:T(8,128)S(1)} %get-tuple-element.55), channel_id=1, source_target_pairs={{0,4},{1,5},{2,6},{3,7},{4,0},{5,1},{6,2},{7,3},{8,12},{9,13},{10,... | collective-permute-start | bytes 196616 | tf_op jit(solution)/shard_map/ppermute | solution.py:250
  84.5 6.6 %collective-permute-start.30 = (f32[128,128]{1,0:T(8,128)S(1)}, f32[128,128]{1,0:T(8,128)S(1)}, u32[]{:S(2)}, u32[]{:S(2)}) collective-permute-start(f32[128,128]{1,0:T(8,128)S(1)} %add.20), channel_id=1, source_target_pairs={{0,8},{1,9},{2,10},{3,11},{4,12},{5,13},{6,14},{7,15},{8,0},{9,1},... | collective-permute-start | bytes 196616 | tf_op jit(solution)/shard_map/ppermute | solution.py:250
  85.2 6.0 %collective-permute-start.31 = (f32[128,128]{1,0:T(8,128)S(1)}, f32[128,128]{1,0:T(8,128)S(1)}, u32[]{:S(2)}, u32[]{:S(2)}) collective-permute-start(f32[128,128]{1,0:T(8,128)S(1)} %add.20), channel_id=1, source_target_pairs={{0,16},{1,17},{2,18},{3,19},{4,20},{5,21},{6,22},{7,23},{8,24},{9,... | collective-permute-start | bytes 196616 | tf_op jit(solution)/shard_map/ppermute | solution.py:250
  86.1 5.2 %collective-permute-start.32 = (f32[128,128]{1,0:T(8,128)S(1)}, f32[128,128]{1,0:T(8,128)S(1)}, u32[]{:S(2)}, u32[]{:S(2)}) collective-permute-start(f32[128,128]{1,0:T(8,128)S(1)} %add.20), channel_id=1, source_target_pairs={{0,24},{1,25},{2,26},{3,27},{4,28},{5,29},{6,30},{7,31},{8,16},{9,... | collective-permute-start | bytes 196616 | tf_op jit(solution)/shard_map/ppermute | solution.py:250
  91.8 1.3 %collective-permute-start.33 = (f32[128,128]{1,0:T(8,128)S(1)}, f32[128,128]{1,0:T(8,128)S(1)}, u32[]{:S(2)}, u32[]{:S(2)}) collective-permute-start(f32[128,128]{1,0:T(8,128)S(1)} %get-tuple-element.57), channel_id=1, source_target_pairs={{0,4},{1,5},{2,6},{3,7},{4,0},{5,1},{6,2},{7,3},{8,12},{9,13},{10,... | collective-permute-start | bytes 196616 | tf_op jit(solution)/shard_map/ppermute | solution.py:250
  (11 other events, 15.0 us)

commit v6 on v5

--- a/solution.py
+++ b/solution.py
@@ -111,22 +111,35 @@
 
 
 def attn_kernel(scale, where, q_ref, pre_ref, mine_ref, other_ref, *out_refs):
+    states = both_heads(where[2], mine_ref, other_ref)
+    parts = []
+    for h in range(2):
+        cols = slice(h * DH, (h + 1) * DH)
+        inter = dot_wide(q_ref[:, cols], states[h], NN)
+        parts.append((pre_ref[:, cols] + scale * inter).astype(BF16))
+    split_heads(where[2], parts, *out_refs)
+
+
+def pack_kernel(where, mine_ref, got_ref, *out_refs):
     count = len(out_refs)
-    states = both_heads(where[2], mine_ref, other_ref)
-    own = out_refs[0].shape[0]
-    for s in range(count):
+    own = mine_ref.shape[0] // count
+    for s, out_ref in enumerate(out_refs):
         block = lax.rem(where[0] + s, count)
         here = pl.ds(pl.multiple_of(block * own, own), own)
-        for h in range(q_ref.shape[1] // DH):
-            cols = slice(h * DH, (h + 1) * DH)
-            inter = dot_wide(q_ref[here, cols], states[h], NN)
-            out_refs[s][:, cols] = (pre_ref[here, cols] + scale * inter).astype(BF16)
-
-
-def cut_kernel(piece_ref, *out_refs):
+        out_ref[:own] = mine_ref[here]
+        out_ref[own:] = got_ref[here]
+
+
+def cut_kernel(left_ref, right_ref, *out_refs):
     wide = out_refs[0].shape[1]
-    for n, out_ref in enumerate(out_refs):
-        out_ref[...] = piece_ref[:, n * wide : (n + 1) * wide]
+    out_refs[0][...] = left_ref[:, :wide]
+    out_refs[1][...] = right_ref[:, wide:]
+
+
+def copy_kernel(*refs):
+    count = len(refs) // 2
+    for source, target in zip(refs[:count], refs[count:]):
+        target[...] = source[...]
 
 
 def grad_kernel(whole, added, places, mine_ref, mate_ref, *refs):
@@ -140,14 +153,11 @@
     out_ref[...] = total.astype(out_ref.dtype)
 
 
-def mixed_kernel(count, each, places, where, *refs):
-    attn, mate, weight = refs[:count], refs[count : 2 * count], refs[2 * count]
-    chunks, (own_out, mate_out) = list(refs[2 * count + 1 : -2]), refs[-2:]
+def mixed_kernel(count, each, places, *refs):
+    attn, weight = refs[:count], refs[count]
+    chunks, (own_out, mate_out) = list(refs[count + 1 : -2]), refs[-2:]
     own = own_out.shape[0]
-    cols = pl.ds(pl.multiple_of(where[2] * DH, DH), DH)
-    left = jnp.concatenate(
-        [jnp.concatenate([attn[s][:, cols], mate[s][:, cols]], 0) for s in range(count)], 1
-    )
+    left = jnp.concatenate([a[...] for a in attn], 1)
     right = [weight[:, pl.ds(pl.multiple_of(places[0], DH), own_out.shape[1])]]
     for n in each:
         parts = [chunks.pop(0)[...] for _ in range(n)]
@@ -284,24 +294,19 @@
     pair = [((DH, DH), F32)] * 2
     product = 4 * own * DH * model
 
-    board = chips == 4
+    board = chips == 4 and count == 4
     wide = model // (2 if board else chips)
     colour = (chip & 1) ^ (chip >> 1) if board else chip
     piece = lax.dynamic_slice(out_weight, (core * DH, colour * wide), (DH, wide))
     weight = lax.dynamic_slice_in_dim(out_weight, core * DH, DH, 0)
-    near = (colour * wide if board else jnp.int32(0)).reshape(1)
-    far = jnp.stack([(1 - colour) * wide, (1 - colour) * wide + wide // 2])
-    shifts = sorted(range(1, count), key=lambda s: min(s, count - s))
-    arrived = {0: piece}
-    for s in shifts:
-        step = 1 if s <= count // 2 else -1
-        arrived[s] = send(arrived[(s - step) % count], 0, step)
+    start, other = colour * wide, (1 - colour) * wide
+    near = jnp.stack([start, start + wide // 2]) if board else jnp.zeros((1,), jnp.int32)
+    far = jnp.stack([other, other + wide // 2])
+    arrived = {1: send(piece, 0, 1), count - 1: send(piece, 0, -1)}
     mate_cotangent = send(cotangent, 1, 0)
 
-    mine, other = call(state_kernel, pair, [key, value], [where], [piece])
+    mine, other = call(state_kernel, pair, [key, value], [where], [piece, mate_cotangent])
     flags, parts = exchange(mine, other, core, chip, chips, False)
-    keep, back = call(carry_kernel, pair, parts, [flags])
-    linear = [keep, send(back, 1, 0)]
     probs, inner, soft, pre = call(
         functools.partial(forward_kernel, scale),
         [((heads, rows, rows), BF16)] * 2 + [(flat, F32)] * 2,
@@ -309,27 +314,16 @@
         [block_mask],
         flops=6 * square,
     )
-    attn = call(
+    keep, back = call(carry_kernel, pair, parts, [flags], [pre])
+    linear = [keep, send(back, 1, 0)]
+    mine, other = call(
         functools.partial(attn_kernel, scale),
-        [((own, width), BF16)] * count,
+        [((rows, DH), BF16)] * 2,
         [query, pre, *linear],
         [where],
     )
+    attn = call(pack_kernel, [((2 * own, DH), BF16)] * count, [mine, send(other, 1, 0)], [where])
     attn = [attn[0]] + [send(attn[s], 0, s) for s in range(1, count)]
-    mate_attn = [send(a, 1, 0) for a in attn]
-
-    first, second = {}, {}
-    for n, s in enumerate(shifts):
-        if not board:
-            groups = [list(range(k, shards, 2)) for k in range(2)]
-            whole = lax.all_gather(arrived[s], "ctx", axis=1, tiled=True, axis_index_groups=groups)
-            first[s], second[s] = whole, []
-        elif n < 2:
-            first[s], second[s] = arrived[s], [send(arrived[s], 2 + 2 * n, 0)]
-        else:
-            cut = [((DH, wide // 2), BF16)] * 2
-            left, right = call(cut_kernel, cut, [arrived[s]], after=mate_attn)
-            first[s], second[s] = arrived[s], [send(left, 2, 0), send(right, 4, 0)]
 
     def grads(some, places, whole=False, earlier=(), last=True, after=()):
         (both,) = call(
@@ -347,34 +341,56 @@
         return call(
             functools.partial(mixed_kernel, count, [len(some) for some in each]),
             [((own, wide), F32)] * 2,
-            [*attn, *mate_attn, weight, *(a for some in each for a in some)],
-            [places, where],
+            [*attn, weight, *(a for some in each for a in some)],
+            [places],
             after,
             room=16,
             flops=count * product,
         )
 
+    end = count // 2
+    if board:
+        cut = [((DH, wide // 2), BF16)] * 2
+        left, right = call(cut_kernel, cut, [arrived[1], arrived[3]], after=attn[1:])
+        left, right = send(left, 0, 1), send(right, 0, -1)
+        first = {1: [arrived[1]], 2: [left, right], 3: [arrived[3]]}
+        second = {1: [send(arrived[1], 2, 0)], 3: [send(arrived[3], 4, 0)]}
+    else:
+        groups = [list(range(k, shards, 2)) for k in range(2)]
+        for s in range(2, count - 1):
+            arrived[s] = send(arrived[s - 1], 0, 1)
+        first = {
+            s: [lax.all_gather(a, "ctx", axis=1, tiled=True, axis_index_groups=groups)]
+            for s, a in arrived.items()
+        }
+    shifts = [s for s in range(1, count) if s != end] + [end]
+
     both = {0: grads([weight], near, True)}
-    end = shifts[-1]
+    across = {0: send(both[0], 1, 0)}
+    half = {s: [grads(first[s], near, last=False)] if board else [] for s in shifts}
+    if board:
+        before = [both[0], *half[1], *half[3], *second[1], *second[3]]
+        left, right = call(copy_kernel, cut, [left, right], after=before)
+        second[2] = [send(left, 2, 0), send(right, 4, 0)]
+    some, places = (second, far) if board else (first, near)
     for s in shifts[:-1]:
-        half = [grads([first[s]], near, last=False)] if board else []
-        some, places = (second[s], far) if board else ([first[s]], near)
-        both[s] = send(grads(some, places, earlier=half), 0, -s)
-    half = [grads([first[end]], near, last=False)] if board else []
-    part, mate_part = mix([[first[s]] for s in range(1, count)], near)
-    joins, starts = [part, send(mate_part, 1, 0)], [near]
-    some, places = (second[end], far) if board else ([first[end]], near)
-    early = [part, *(both[s] for s in [0] + shifts[:-1])]
-    both[end] = send(grads(some, places, earlier=half, after=early), 0, -end)
-    across = [send(both[s], 1, 0) for s in range(count)]
+        both[s] = send(grads(some[s], places, earlier=half[s]), 0, -s)
+        across[s] = send(both[s], 1, 0)
+    ahead = [across[s] for s in across]
+    joins, starts = [], []
     if board:
-        part, mate_part = mix([second[s] for s in range(1, count)], far, [both[end]])
-        joins, starts = [*joins, part, send(mate_part, 1, 0)], [near, far[:1]]
+        part, mate_part = mix([first[s] for s in range(1, count)], near)
+        joins, starts = [part, send(mate_part, 1, 0)], [near[:1]]
+        ahead += joins
+    both[end] = send(grads(some[end], places, earlier=half[end], after=ahead), 0, -end)
+    across[end] = send(both[end], 1, 0)
+    part, mate_part = mix([some[s] for s in range(1, count)], places, [both[end]])
+    joins, starts = [*joins, part, send(mate_part, 1, 0)], [*starts, places[:1]]
 
     g, mine, other = call(
         functools.partial(collect_kernel, scale, count),
         [(flat, BF16), *pair],
-        [query, *(both[s] for s in range(count)), *across],
+        [query, *(both[s] for s in range(count)), *(across[s] for s in range(count))],
         [where],
         [part],
     )

time: 96.8 us -> 106 us (1.095)
  starting transfers between devices: 24.7 us -> 30 us
  Pallas kernels: 23.1 us -> 28.4 us
  waiting for transfers between devices: 37.3 us -> 32.2 us
  local copies, waits for them, and re-layouts: 9.63 us -> 12.9 us
    ppermute x34 -> x32, starting transfers between devices: 24.7 us -> 30 us  [send(): return lax.ppermute(x, ('ctx', 'head'), pairs)]
    pallas_call x19 -> x21, Pallas kernels: 23.1 us -> 28.4 us  [call(): pl.pallas_call(kernel, out_shape=[jax.ShapeDtypeStruct(s, t) for s, t in...]
    ppermute x34 -> x32, waiting for transfers between devices: 37.3 us -> 32.2 us  [send(): return lax.ppermute(x, ('ctx', 'head'), pairs)]
    unnamed x50 -> x94, local copies, waits for them, and re-layouts: 7.18 us -> 11.7 us
    dynamic_slice x1, local copies, waits for them, and re-layouts: 1.29 us -> 0.09 us  [on_device(): weight = lax.dynamic_slice_in_dim(out_weight, core * DH, DH, 0)]
  transfers between devices with their start and end apart: 34 -> 32, of which waited for: 15 -> 16; matrix products, arithmetic and copies ran while one was open for 2% -> 2% of each run, Pallas kernels for 21% -> 20%
where the time goes in v6:
time: 106 us; the launch traced here: 105 us
  waiting for transfers between devices  32.2 us (30%)
  starting transfers between devices  30 us (28%)
  Pallas kernels  28.4 us (27%)
  local copies, waits for them, and re-layouts  12.9 us (12%)
  between operations  1.19 us (1%)
    ppermute x32, waiting for transfers between devices, send(): return lax.ppermute(x, ('ctx', 'head'), pairs)  32.2 us
    ppermute x32, starting transfers between devices, send(): return lax.ppermute(x, ('ctx', 'head'), pairs)  30 us
    pallas_call x21, Pallas kernels, call(): pl.pallas_call(kernel, out_shape=[jax.ShapeDtypeStruct(s, t) for s, t in...  28.4 us
    unnamed x94, local copies, waits for them, and re-layouts  11.7 us
  transfers between devices with their start and end apart: 32, of which 16 were waited for; matrix products, arithmetic and copies ran while one was open for 2% of the time, Pallas kernels for 20%

profile of v6, /device:TPU:0, one launch (start us, length us, event | category | flops | bytes accessed | tf_op | source)
XLA Modules:
  0.0 105.1 jit_solution(17103370272087504683)
XLA Ops:
  1.2 1.1 %dynamic_slice.6.refs_3_ = bf16[128,2048]{1,0:T(8,128)(2,1)S(1)} dynamic-slice(bf16[256,4096]{1,0:T(8,128)(2,1)} %param.10, s32[]{:T(128)S(6)} %select_n.7, s32[]{:T(128)S(6)} %select_n.8), dynamic_slice_sizes={128,2048} | dynamic-slice | bytes 1048580 | tf_op jit(solution)/shard_map/dynamic_slice | solution.py:300
  2.3 2.8 %collective-permute-start.10 = (bf16[128,2048]{1,0:T(8,128)(2,1)S(1)}, bf16[128,2048]{1,0:T(8,128)(2,1)}, u32[]{:S(2)}, u32[]{:S(2)}) collective-permute-start(bf16[128,2048]{1,0:T(8,128)(2,1)S(1)} %dynamic_slice.6.refs_3_), channel_id=1, source_target_pairs={{0,1},{1,2},{2,3},{3,0},{4,5},{5,6},{6,7},{7,4},{8,9},{9,10},{10,1... | collective-permute-start | bytes 1572872 | tf_op jit(solution)/shard_map/ppermute | solution.py:260
  5.1 2.1 %collective-permute-start.11 = (bf16[128,2048]{1,0:T(8,128)(2,1)S(1)}, bf16[128,2048]{1,0:T(8,128)(2,1)}, u32[]{:S(2)}, u32[]{:S(2)}) collective-permute-start(bf16[128,2048]{1,0:T(8,128)(2,1)S(1)} %dynamic_slice.6.refs_3_), channel_id=1, source_target_pairs={{0,3},{1,0},{2,1},{3,2},{4,7},{5,4},{6,5},{7,6},{8,11},{9,8},{10,9... | collective-permute-start | bytes 1572872 | tf_op jit(solution)/shard_map/ppermute | solution.py:260
  7.3 0.9 copy-done.6
  8.2 0.9 copy-done.9
  10.0 1.2 %collective-permute-done.1.refs_2_ = f32[128,128]{1,0:T(8,128)S(1)} collective-permute-done((f32[128,128]{1,0:T(8,128)S(1)}, f32[128,128]{1,0:T(8,128)S(1)}, u32[]{:S(2)}, u32[]{:S(2)}) %collective-permute-start.1) | collective-permute-done | bytes 65568 | tf_op jit(solution)/shard_map/ppermute | solution.py:260
  11.2 1.7 %collective-permute-start.2 = (f32[128,128]{1,0:T(8,128)S(1)}, f32[128,128]{1,0:T(8,128)S(1)}, u32[]{:S(2)}, u32[]{:S(2)}) collective-permute-start(f32[128,128]{1,0:T(8,128)S(1)} %add.22), channel_id=1, source_target_pairs={{0,8},{1,9},{2,10},{3,11},{4,12},{5,13},{6,14},{7,15},{8,0},{9,1},... | collective-permute-start | bytes 196616 | tf_op jit(solution)/shard_map/ppermute | solution.py:260
  13.0 1.5 %collective-permute-start.3 = (f32[128,128]{1,0:T(8,128)S(1)}, f32[128,128]{1,0:T(8,128)S(1)}, u32[]{:S(2)}, u32[]{:S(2)}) collective-permute-start(f32[128,128]{1,0:T(8,128)S(1)} %add.22), channel_id=1, source_target_pairs={{0,16},{1,17},{2,18},{3,19},{4,20},{5,21},{6,22},{7,23},{8,24},{9,... | collective-permute-start | bytes 196616 | tf_op jit(solution)/shard_map/ppermute | solution.py:260
  14.9 2.3 %shard_map.93 = (bf16[2,384,384]{2,1,0:T(8,128)(2,1)S(1)}, bf16[2,384,384]{2,1,0:T(8,128)(2,1)S(1)}, f32[384,256]{1,0:T(8,128)S(1)}, f32[384,256]{1,0:T(8,128)S(1)}) custom-call(s32[3,3]{1,0:T(4,128)S(1)} %copy-done.45, bf16[384,256]{1,0:T(8,128)(2,1)S(1)} %copy-done.12, bf16[384,256]{1,0:T(8,128)(2,1)S(1)} %copy-done.7, bf16[384,256]{1,0:T(8,128)(2,1)S(1)} %copy-done.10), custom_call_target="tpu_custom_call" | custom-call | flops 226492416 | bytes 2555904 | tf_op jit(solution)/shard_map/pallas_call | solution.py:37
  20.3 1.2 %collective-permute-done.5.refs_4_.refs_9_ = f32[128,128]{1,0:T(8,128)S(1)} collective-permute-done((f32[128,128]{1,0:T(8,128)S(1)}, f32[128,128]{1,0:T(8,128)S(1)}, u32[]{:S(2)}, u32[]{:S(2)}) %collective-permute-start.5) | collective-permute-done | bytes 65568 | tf_op jit(solution)/shard_map/ppermute | solution.py:260
  22.6 1.1 %collective-permute-done.6.refs_2_ = bf16[384,128]{1,0:T(8,128)(2,1)S(1)} collective-permute-done((bf16[384,128]{1,0:T(8,128)(2,1)S(1)}, bf16[384,128]{1,0:T(8,128)(2,1)S(1)}, u32[]{:S(2)}, u32[]{:S(2)}) %collective-permute-start.6) | collective-permute-done | bytes 98336 | tf_op jit(solution)/shard_map/ppermute | solution.py:260
  24.9 2.4 %collective-permute-start.8 = (bf16[192,128]{1,0:T(8,128)(2,1)S(1)}, bf16[192,128]{1,0:T(8,128)(2,1)S(1)}, u32[]{:S(2)}, u32[]{:S(2)}) collective-permute-start(bf16[192,128]{1,0:T(8,128)(2,1)S(1)} %get-tuple-element.45), channel_id=1, source_target_pairs={{0,2},{1,3},{2,0},{3,1},{4,6},{5,7},{6,4},{7,5},{8,10},{9,11},{10,... | collective-permute-start | bytes 147464 | tf_op jit(solution)/shard_map/ppermute | solution.py:260
  27.3 1.5 %collective-permute-start.9 = (bf16[192,128]{1,0:T(8,128)(2,1)S(1)}, bf16[192,128]{1,0:T(8,128)(2,1)S(1)}, u32[]{:S(2)}, u32[]{:S(2)}) collective-permute-start(bf16[192,128]{1,0:T(8,128)(2,1)S(1)} %get-tuple-element.46), channel_id=1, source_target_pairs={{0,3},{1,0},{2,1},{3,2},{4,7},{5,4},{6,5},{7,6},{8,11},{9,8},{10,9... | collective-permute-start | bytes 147464 | tf_op jit(solution)/shard_map/ppermute | solution.py:260
  28.8 1.9 %collective-permute-done.11.refs_1_.refs_9_.refs_3_ = bf16[128,2048]{1,0:T(8,128)(2,1)} collective-permute-done((bf16[128,2048]{1,0:T(8,128)(2,1)S(1)}, bf16[128,2048]{1,0:T(8,128)(2,1)}, u32[]{:S(2)}, u32[]{:S(2)}) %collective-permute-start.11) | collective-permute-done | bytes 524320 | tf_op jit(solution)/shard_map/ppermute | solution.py:260
  30.7 1.6 %collective-permute-done.7.refs_2_ = bf16[192,128]{1,0:T(8,128)(2,1)S(1)} collective-permute-done((bf16[192,128]{1,0:T(8,128)(2,1)S(1)}, bf16[192,128]{1,0:T(8,128)(2,1)S(1)}, u32[]{:S(2)}, u32[]{:S(2)}) %collective-permute-start.7) | collective-permute-done | bytes 49184 | tf_op jit(solution)/shard_map/ppermute | solution.py:260
  32.2 1.8 %collective-permute-done.8.refs_3_ = bf16[192,128]{1,0:T(8,128)(2,1)S(1)} collective-permute-done((bf16[192,128]{1,0:T(8,128)(2,1)S(1)}, bf16[192,128]{1,0:T(8,128)(2,1)S(1)}, u32[]{:S(2)}, u32[]{:S(2)}) %collective-permute-start.8) | collective-permute-done | bytes 49184 | tf_op jit(solution)/shard_map/ppermute | solution.py:260
  34.0 2.0 %shard_map.98 = (bf16[128,1024]{1,0:T(8,128)(2,1)}, bf16[128,1024]{1,0:T(8,128)(2,1)S(1)}) custom-call(bf16[128,2048]{1,0:T(8,128)(2,1)} %collective-permute-done.10.refs_0_.refs_6_.refs_3_, bf16[128,2048]{1,0:T(8,128)(2,1)} %collective-permute-done.11.refs_1_.refs_9_.refs_3_, bf16[192,128]{1,0:T(8,128)(2,1)S(1)} %collective-permute-done.7.refs_2_, ...), custom_call_target="tpu_custom_call" | custom-call | flops 1 | bytes 1572864 | tf_op jit(solution)/shard_map/pallas_call | solution.py:37
  36.0 1.5 %collective-permute-start.12 = (bf16[128,1024]{1,0:T(8,128)(2,1)}, bf16[128,1024]{1,0:T(8,128)(2,1)S(1)}, u32[]{:S(2)}, u32[]{:S(2)}) collective-permute-start(bf16[128,1024]{1,0:T(8,128)(2,1)} %get-tuple-element.47), channel_id=1, source_target_pairs={{0,1},{1,2},{2,3},{3,0},{4,5},{5,6},{6,7},{7,4},{8,9},{9,10},{10,1... | collective-permute-start | bytes 786440 | tf_op jit(solution)/shard_map/ppermute | solution.py:260
  37.5 2.3 %collective-permute-start.13 = (bf16[128,1024]{1,0:T(8,128)(2,1)S(1)}, bf16[128,1024]{1,0:T(8,128)(2,1)S(1)}, u32[]{:S(2)}, u32[]{:S(2)}) collective-permute-start(bf16[128,1024]{1,0:T(8,128)(2,1)S(1)} %get-tuple-element.48), channel_id=1, source_target_pairs={{0,3},{1,0},{2,1},{3,2},{4,7},{5,4},{6,5},{7,6},{8,11},{9,8},{10,9... | collective-permute-start | bytes 786440 | tf_op jit(solution)/shard_map/ppermute | solution.py:260
  40.0 1.5 %collective-permute-start.15 = (bf16[128,2048]{1,0:T(8,128)(2,1)}, bf16[128,2048]{1,0:T(8,128)(2,1)S(1)}, u32[]{:S(2)}, u32[]{:S(2)}) collective-permute-start(bf16[128,2048]{1,0:T(8,128)(2,1)} %collective-permute-done.10.refs_0_.refs_6_.refs_3_), channel_id=1, source_target_pairs={{0,8},{1,9},{2,10},{3,11},{4,12},{5,13},{6,14},{7,15},{8,0},{9,1},... | collective-permute-start | bytes 1572872 | tf_op jit(solution)/shard_map/ppermute | solution.py:260
  41.5 1.5 %collective-permute-start.16 = (bf16[128,2048]{1,0:T(8,128)(2,1)}, bf16[128,2048]{1,0:T(8,128)(2,1)S(1)}, u32[]{:S(2)}, u32[]{:S(2)}) collective-permute-start(bf16[128,2048]{1,0:T(8,128)(2,1)} %collective-permute-done.11.refs_1_.refs_9_.refs_3_), channel_id=1, source_target_pairs={{0,16},{1,17},{2,18},{3,19},{4,20},{5,21},{6,22},{7,23},{8,24},{9,... | collective-permute-start | bytes 1572872 | tf_op jit(solution)/shard_map/ppermute | solution.py:260
  43.0 4.2 %collective-permute-done.12.refs_7_.refs_0_.refs_3_ = bf16[128,1024]{1,0:T(8,128)(2,1)S(1)} collective-permute-done((bf16[128,1024]{1,0:T(8,128)(2,1)}, bf16[128,1024]{1,0:T(8,128)(2,1)S(1)}, u32[]{:S(2)}, u32[]{:S(2)}) %collective-permute-start.12) | collective-permute-done | bytes 262176 | tf_op jit(solution)/shard_map/ppermute | solution.py:260
  47.9 3.2 %collective-permute-done.13.refs_8_.refs_1_.refs_4_ = bf16[128,1024]{1,0:T(8,128)(2,1)S(1)} collective-permute-done((bf16[128,1024]{1,0:T(8,128)(2,1)S(1)}, bf16[128,1024]{1,0:T(8,128)(2,1)S(1)}, u32[]{:S(2)}, u32[]{:S(2)}) %collective-permute-start.13) | collective-permute-done | bytes 262176 | tf_op jit(solution)/shard_map/ppermute | solution.py:260
  51.8 0.9 copy-done.15
  52.7 0.9 copy-done.18
  54.5 2.7 %shard_map.99 = (f32[96,2048]{1,0:T(8,128)S(1)}, f32[96,2048]{1,0:T(8,128)}) custom-call(s32[2]{0:T(128)S(1)} %pad_add_fusion.1.refs_0_, bf16[192,128]{1,0:T(8,128)(2,1)S(1)} %copy-done.43, bf16[192,128]{1,0:T(8,128)(2,1)S(1)} %collective-permute-done.7.refs_2_, bf16[192,128]{1,0:T(8,128)(2,1)S(1)} %collective-permute-done.8.refs_3_, ...), custom_call_target="tpu_custom_call" | custom-call | flops 805306368 | bytes 4390912 | tf_op jit(solution)/shard_map/pallas_call | solution.py:37
  57.2 1.1 %shard_map.100.refs_2_ = bf16[192,128]{1,0:T(8,128)(2,1)S(1)} custom-call(s32[2]{0:T(128)S(1)} %pad_add_fusion.1.refs_0_, bf16[96,4096]{1,0:T(8,128)(2,1)S(1)} %copy-done, bf16[96,4096]{1,0:T(8,128)(2,1)S(1)} %collective-permute-done.refs_4_.refs_2_, bf16[128,4096]{1,0:T(8,128)(2,1)S(1)} %constant_dynamic-slice_fusion.refs_5_.refs_3_), custom_call_target="tpu_custom_call" | custom-call | flops 201326592 | bytes 2670592 | tf_op jit(solution)/shard_map/pallas_call | solution.py:37
  58.3 1.4 %shard_map.101.refs_3_ = f32[192,128]{1,0:T(8,128)S(1)} custom-call(s32[2]{0:T(128)S(1)} %pad_add_fusion.1.refs_0_, bf16[96,4096]{1,0:T(8,128)(2,1)S(1)} %copy-done, bf16[96,4096]{1,0:T(8,128)(2,1)S(1)} %collective-permute-done.refs_4_.refs_2_, bf16[128,2048]{1,0:T(8,128)(2,1)} %collective-permute-done.10.refs_0_.refs_6_.refs_3_), custom_call_target="tpu_custom_call" | custom-call | flops 201326592 | bytes 2195456 | tf_op jit(solution)/shard_map/pallas_call | solution.py:37
  59.8 1.5 %shard_map.102.refs_4_.refs_3_ = f32[192,128]{1,0:T(8,128)S(1)} custom-call(s32[2]{0:T(128)S(1)} %pad_add_fusion.1.refs_0_, bf16[96,4096]{1,0:T(8,128)(2,1)S(1)} %copy-done, bf16[96,4096]{1,0:T(8,128)(2,1)S(1)} %collective-permute-done.refs_4_.refs_2_, bf16[128,2048]{1,0:T(8,128)(2,1)} %collective-permute-done.11.refs_1_.refs_9_.refs_3_), custom_call_target="tpu_custom_call" | custom-call | flops 201326592 | bytes 2195456 | tf_op jit(solution)/shard_map/pallas_call | solution.py:37
  63.6 1.5 %collective-permute-start.17 = (bf16[128,1024]{1,0:T(8,128)(2,1)}, bf16[128,1024]{1,0:T(8,128)(2,1)}, u32[]{:S(2)}, u32[]{:S(2)}) collective-permute-start(bf16[128,1024]{1,0:T(8,128)(2,1)} %get-tuple-element.51), channel_id=1, source_target_pairs={{0,8},{1,9},{2,10},{3,11},{4,12},{5,13},{6,14},{7,15},{8,0},{9,1},... | collective-permute-start | bytes 786440 | tf_op jit(solution)/shard_map/ppermute | solution.py:260
  65.1 1.5 %collective-permute-start.18 = (bf16[128,1024]{1,0:T(8,128)(2,1)}, bf16[128,1024]{1,0:T(8,128)(2,1)}, u32[]{:S(2)}, u32[]{:S(2)}) collective-permute-start(bf16[128,1024]{1,0:T(8,128)(2,1)} %get-tuple-element.52), channel_id=1, source_target_pairs={{0,16},{1,17},{2,18},{3,19},{4,20},{5,21},{6,22},{7,23},{8,24},{9,... | collective-permute-start | bytes 786440 | tf_op jit(solution)/shard_map/ppermute | solution.py:260
  66.7 1.0 copy-done.2
  67.7 0.9 copy-done.21
  68.6 0.9 shard_map.105
  69.5 2.3 %collective-permute-start.20 = (bf16[192,128]{1,0:T(8,128)(2,1)S(1)}, bf16[192,128]{1,0:T(8,128)(2,1)S(1)}, u32[]{:S(2)}, u32[]{:S(2)}) collective-permute-start(bf16[192,128]{1,0:T(8,128)(2,1)S(1)} %shard_map.105), channel_id=1, source_target_pairs={{0,3},{1,0},{2,1},{3,2},{4,7},{5,4},{6,5},{7,6},{8,11},{9,8},{10,9... | collective-permute-start | bytes 147464 | tf_op jit(solution)/shard_map/ppermute | solution.py:260
  71.8 0.9 shard_map.106
  73.7 5.0 %collective-permute-done.22.refs_5_ = bf16[192,128]{1,0:T(8,128)(2,1)S(1)} collective-permute-done((bf16[192,128]{1,0:T(8,128)(2,1)S(1)}, bf16[192,128]{1,0:T(8,128)(2,1)S(1)}, u32[]{:S(2)}, u32[]{:S(2)}) %collective-permute-start.22) | collective-permute-done | bytes 49184 | tf_op jit(solution)/shard_map/ppermute | solution.py:260
  78.7 0.9 shard_map.104.refs_3_
  80.0 1.4 %shard_map.107 = bf16[192,128]{1,0:T(8,128)(2,1)S(1)} custom-call(s32[2]{0:T(128)S(1)} %pad_add_fusion.3.refs_0_, bf16[96,4096]{1,0:T(8,128)(2,1)S(1)} %copy-done, bf16[96,4096]{1,0:T(8,128)(2,1)S(1)} %collective-permute-done.refs_4_.refs_2_, f32[192,128]{1,0:T(8,128)S(1)} %shard_map.104.refs_3_, bf16[128,1024]{1,0:T(8,128)(2,1)} %collective-permute-done.17.refs_4_.refs_7_, ...), custom_call_target="tpu_custom_call" | custom-call | flops 201326592 | bytes 2244608 | tf_op jit(solution)/shard_map/pallas_call | solution.py:37
  81.5 5.0 %collective-permute-done.24.refs_10_.refs_4_ = bf16[192,128]{1,0:T(8,128)(2,1)S(1)} collective-permute-done((bf16[192,128]{1,0:T(8,128)(2,1)S(1)}, bf16[192,128]{1,0:T(8,128)(2,1)S(1)}, u32[]{:S(2)}, u32[]{:S(2)}) %collective-permute-start.24) | collective-permute-done | bytes 49184 | tf_op jit(solution)/shard_map/ppermute | solution.py:260
  86.6 1.6 %shard_map.108 = (f32[96,2048]{1,0:T(8,128)S(1)}, f32[96,2048]{1,0:T(8,128)S(1)}) custom-call(s32[2]{0:T(128)S(1)} %pad_add_fusion.3.refs_0_, bf16[192,128]{1,0:T(8,128)(2,1)S(1)} %copy-done.44, bf16[192,128]{1,0:T(8,128)(2,1)S(1)} %copy-done.33, bf16[192,128]{1,0:T(8,128)(2,1)S(1)} %copy-done.35, bf16[192,128]{1,0:T(8,128)(2,1)S(1)} %copy-done.37, ...), custom_call_target="tpu_custom_call" | custom-call | flops 805306368 | bytes 4390912 | tf_op jit(solution)/shard_map/pallas_call | solution.py:37
  88.8 1.8 %collective-permute-done.26.refs_8_ = bf16[192,128]{1,0:T(8,128)(2,1)S(1)} collective-permute-done((bf16[192,128]{1,0:T(8,128)(2,1)S(1)}, bf16[192,128]{1,0:T(8,128)(2,1)S(1)}, u32[]{:S(2)}, u32[]{:S(2)}) %collective-permute-start.26) | collective-permute-done | bytes 49184 | tf_op jit(solution)/shard_map/ppermute | solution.py:260
  91.6 1.1 %collective-permute-done.27.refs_2_ = f32[128,128]{1,0:T(8,128)S(1)} collective-permute-done((f32[128,128]{1,0:T(8,128)S(1)}, f32[128,128]{1,0:T(8,128)S(1)}, u32[]{:S(2)}, u32[]{:S(2)}) %collective-permute-start.27) | collective-permute-done | bytes 65568 | tf_op jit(solution)/shard_map/ppermute | solution.py:260
  93.9 2.4 %collective-permute-start.30 = (f32[128,128]{1,0:T(8,128)S(1)}, f32[128,128]{1,0:T(8,128)S(1)}, u32[]{:S(2)}, u32[]{:S(2)}) collective-permute-start(f32[128,128]{1,0:T(8,128)S(1)} %add.24), channel_id=1, source_target_pairs={{0,24},{1,25},{2,26},{3,27},{4,28},{5,29},{6,30},{7,31},{8,16},{9,... | collective-permute-start | bytes 196616 | tf_op jit(solution)/shard_map/ppermute | solution.py:260
  96.4 2.9 %shard_map.111 = (bf16[384,256]{1,0:T(8,128)(2,1)}, f32[384,256]{1,0:T(8,128)S(1)}, f32[384,256]{1,0:T(8,128)S(1)}) custom-call(s32[3]{0:T(128)S(1)} %copy-done.39, bf16[384,256]{1,0:T(8,128)(2,1)S(1)} %copy-done.13, bf16[384,256]{1,0:T(8,128)(2,1)S(1)} %copy-done.8, bf16[384,256]{1,0:T(8,128)(2,1)S(1)} %copy-done.11, ...), custom_call_target="tpu_custom_call" | custom-call | flops 528482304 | bytes 3473408 | tf_op jit(solution)/shard_map/pallas_call | solution.py:37
  100.1 1.2 %collective-permute-done.31.refs_6_ = f32[128,128]{1,0:T(8,128)S(1)} collective-permute-done((f32[128,128]{1,0:T(8,128)S(1)}, f32[128,128]{1,0:T(8,128)S(1)}, u32[]{:S(2)}, u32[]{:S(2)}) %collective-permute-start.31) | collective-permute-done | bytes 65568 | tf_op jit(solution)/shard_map/ppermute | solution.py:260
  101.3 1.6 %shard_map.113 = (bf16[384,256]{1,0:T(8,128)(2,1)}, bf16[384,256]{1,0:T(8,128)(2,1)}) custom-call(s32[3]{0:T(128)S(1)} %copy-done.39, bf16[384,256]{1,0:T(8,128)(2,1)S(1)} %copy-done.8, bf16[384,256]{1,0:T(8,128)(2,1)S(1)} %copy-done.11, f32[384,256]{1,0:T(8,128)S(1)} %get-tuple-element.60.refs_6_.refs_3_, f32[384,256]{1,0:T(8,128)S(1)} %get-tuple-element.61.refs_4_, ...), custom_call_target="tpu_custom_call" | custom-call | flops 1 | bytes 1703936 | tf_op jit(solution)/shard_map/pallas_call | solution.py:37
  102.9 2.2 %shard_map.109 = bf16[96,4096]{1,0:T(8,128)(2,1)} custom-call(s32[2]{0:T(128)S(1)} %pad_add_fusion.refs_0_, f32[96,2048]{1,0:T(8,128)S(1)} %get-tuple-element.49.refs_9_.refs_1_, f32[96,2048]{1,0:T(8,128)} %collective-permute-done.14.refs_10_.refs_2_, f32[96,2048]{1,0:T(8,128)S(1)} %get-tuple-element.53.refs_3_.refs_10_, ...), custom_call_target="tpu_custom_call" | custom-call | flops 1 | bytes 3932160 | tf_op jit(solution)/shard_map/pallas_call | solution.py:37
  (141 shorter events, 16.9 us)
Async XLA Ops:
  0.6 14.2 %copy-start.7 = (bf16[384,256]{1,0:T(8,128)(2,1)S(1)}, bf16[384,256]{1,0:T(8,128)(2,1)}, u32[]{:S(2)}) copy-start(bf16[384,256]{1,0:T(8,128)(2,1)} %refs_1_.25) | copy-start | bytes 589828
  0.6 14.2 %copy-start.10 = (bf16[384,256]{1,0:T(8,128)(2,1)S(1)}, bf16[384,256]{1,0:T(8,128)(2,1)}, u32[]{:S(2)}) copy-start(bf16[384,256]{1,0:T(8,128)(2,1)} %refs_2_.7) | copy-start | bytes 589828
  0.7 14.2 %copy-start.12 = (bf16[384,256]{1,0:T(8,128)(2,1)S(1)}, bf16[384,256]{1,0:T(8,128)(2,1)}, u32[]{:S(2)}) copy-start(bf16[384,256]{1,0:T(8,128)(2,1)} %refs_1_.24) | copy-start | bytes 589828
  0.7 6.6 %collective-permute-start = (bf16[96,4096]{1,0:T(8,128)(2,1)}, bf16[96,4096]{1,0:T(8,128)(2,1)S(1)}, u32[]{:S(2)}, u32[]{:S(2)}) collective-permute-start(bf16[96,4096]{1,0:T(8,128)(2,1)} %refs_1_.22), channel_id=1, source_target_pairs={{0,4},{1,5},{2,6},{3,7},{4,0},{5,1},{6,2},{7,3},{8,12},{9,13},{10,... | collective-permute-start | bytes 2359304 | tf_op jit(solution)/shard_map/ppermute | solution.py:260
  2.3 26.5 %collective-permute-start.10 = (bf16[128,2048]{1,0:T(8,128)(2,1)S(1)}, bf16[128,2048]{1,0:T(8,128)(2,1)}, u32[]{:S(2)}, u32[]{:S(2)}) collective-permute-start(bf16[128,2048]{1,0:T(8,128)(2,1)S(1)} %dynamic_slice.6.refs_3_), channel_id=1, source_target_pairs={{0,1},{1,2},{2,3},{3,0},{4,5},{5,6},{6,7},{7,4},{8,9},{9,10},{10,1... | collective-permute-start | bytes 1572872 | tf_op jit(solution)/shard_map/ppermute | solution.py:260
  5.1 25.6 %collective-permute-start.11 = (bf16[128,2048]{1,0:T(8,128)(2,1)S(1)}, bf16[128,2048]{1,0:T(8,128)(2,1)}, u32[]{:S(2)}, u32[]{:S(2)}) collective-permute-start(bf16[128,2048]{1,0:T(8,128)(2,1)S(1)} %dynamic_slice.6.refs_3_), channel_id=1, source_target_pairs={{0,3},{1,0},{2,1},{3,2},{4,7},{5,4},{6,5},{7,6},{8,11},{9,8},{10,9... | collective-permute-start | bytes 1572872 | tf_op jit(solution)/shard_map/ppermute | solution.py:260
  7.3 16.5 %copy-start.38 = (s32[3]{0:T(128)}, s32[3]{0:T(128)S(1)}, u32[]{:S(2)}) copy-start(s32[3]{0:T(128)S(1)} %pad_add_fusion.2.refs_0_) | copy-start | bytes 40
  9.9 1.3 %collective-permute-start.1 = (f32[128,128]{1,0:T(8,128)S(1)}, f32[128,128]{1,0:T(8,128)S(1)}, u32[]{:S(2)}, u32[]{:S(2)}) collective-permute-start(f32[128,128]{1,0:T(8,128)S(1)} %get-tuple-element.38), channel_id=1, source_target_pairs={{0,4},{1,5},{2,6},{3,7},{4,0},{5,1},{6,2},{7,3},{8,12},{9,13},{10,... | collective-permute-start | bytes 196616 | tf_op jit(solution)/shard_map/ppermute | solution.py:260
  10.0 29.8 %copy-start.46 = (bf16[256,4096]{1,0:T(8,128)(2,1)S(1)}, bf16[256,4096]{1,0:T(8,128)(2,1)}, u32[]{:S(2)}) copy-start(bf16[256,4096]{1,0:T(8,128)(2,1)} %param.10) | copy-start | bytes 6291460
  11.2 7.6 %collective-permute-start.2 = (f32[128,128]{1,0:T(8,128)S(1)}, f32[128,128]{1,0:T(8,128)S(1)}, u32[]{:S(2)}, u32[]{:S(2)}) collective-permute-start(f32[128,128]{1,0:T(8,128)S(1)} %add.22), channel_id=1, source_target_pairs={{0,8},{1,9},{2,10},{3,11},{4,12},{5,13},{6,14},{7,15},{8,0},{9,1},... | collective-permute-start | bytes 196616 | tf_op jit(solution)/shard_map/ppermute | solution.py:260
  13.0 5.9 %collective-permute-start.3 = (f32[128,128]{1,0:T(8,128)S(1)}, f32[128,128]{1,0:T(8,128)S(1)}, u32[]{:S(2)}, u32[]{:S(2)}) collective-permute-start(f32[128,128]{1,0:T(8,128)S(1)} %add.22), channel_id=1, source_target_pairs={{0,16},{1,17},{2,18},{3,19},{4,20},{5,21},{6,22},{7,23},{8,24},{9,... | collective-permute-start | bytes 196616 | tf_op jit(solution)/shard_map/ppermute | solution.py:260
  14.5 5.2 %collective-permute-start.4 = (f32[128,128]{1,0:T(8,128)S(1)}, f32[128,128]{1,0:T(8,128)S(1)}, u32[]{:S(2)}, u32[]{:S(2)}) collective-permute-start(f32[128,128]{1,0:T(8,128)S(1)} %add.22), channel_id=1, source_target_pairs={{0,24},{1,25},{2,26},{3,27},{4,28},{5,29},{6,30},{7,31},{8,16},{9,... | collective-permute-start | bytes 196616 | tf_op jit(solution)/shard_map/ppermute | solution.py:260
  20.2 1.3 %collective-permute-start.5 = (f32[128,128]{1,0:T(8,128)S(1)}, f32[128,128]{1,0:T(8,128)S(1)}, u32[]{:S(2)}, u32[]{:S(2)}) collective-permute-start(f32[128,128]{1,0:T(8,128)S(1)} %get-tuple-element.40), channel_id=1, source_target_pairs={{0,4},{1,5},{2,6},{3,7},{4,0},{5,1},{6,2},{7,3},{8,12},{9,13},{10,... | collective-permute-start | bytes 196616 | tf_op jit(solution)/shard_map/ppermute | solution.py:260
  22.4 1.4 %collective-permute-start.6 = (bf16[384,128]{1,0:T(8,128)(2,1)S(1)}, bf16[384,128]{1,0:T(8,128)(2,1)S(1)}, u32[]{:S(2)}, u32[]{:S(2)}) collective-permute-start(bf16[384,128]{1,0:T(8,128)(2,1)S(1)} %get-tuple-element.42), channel_id=1, source_target_pairs={{0,4},{1,5},{2,6},{3,7},{4,0},{5,1},{6,2},{7,3},{8,12},{9,13},{10,... | collective-permute-start | bytes 294920 | tf_op jit(solution)/shard_map/ppermute | solution.py:260
  24.9 7.3 %collective-permute-start.7 = (bf16[192,128]{1,0:T(8,128)(2,1)S(1)}, bf16[192,128]{1,0:T(8,128)(2,1)S(1)}, u32[]{:S(2)}, u32[]{:S(2)}) collective-permute-start(bf16[192,128]{1,0:T(8,128)(2,1)S(1)} %get-tuple-element.44), channel_id=1, source_target_pairs={{0,1},{1,2},{2,3},{3,0},{4,5},{5,6},{6,7},{7,4},{8,9},{9,10},{10,1... | collective-permute-start | bytes 147464 | tf_op jit(solution)/shard_map/ppermute | solution.py:260
  24.9 9.1 %collective-permute-start.8 = (bf16[192,128]{1,0:T(8,128)(2,1)S(1)}, bf16[192,128]{1,0:T(8,128)(2,1)S(1)}, u32[]{:S(2)}, u32[]{:S(2)}) collective-permute-start(bf16[192,128]{1,0:T(8,128)(2,1)S(1)} %get-tuple-element.45), channel_id=1, source_target_pairs={{0,2},{1,3},{2,0},{3,1},{4,6},{5,7},{6,4},{7,5},{8,10},{9,11},{10,... | collective-permute-start | bytes 147464 | tf_op jit(solution)/shard_map/ppermute | solution.py:260
  27.3 6.7 %collective-permute-start.9 = (bf16[192,128]{1,0:T(8,128)(2,1)S(1)}, bf16[192,128]{1,0:T(8,128)(2,1)S(1)}, u32[]{:S(2)}, u32[]{:S(2)}) collective-permute-start(bf16[192,128]{1,0:T(8,128)(2,1)S(1)} %get-tuple-element.46), channel_id=1, source_target_pairs={{0,3},{1,0},{2,1},{3,2},{4,7},{5,4},{6,5},{7,6},{8,11},{9,8},{10,9... | collective-permute-start | bytes 147464 | tf_op jit(solution)/shard_map/ppermute | solution.py:260
  32.2 24.9 %copy-start.32 = (bf16[192,128]{1,0:T(8,128)(2,1)}, bf16[192,128]{1,0:T(8,128)(2,1)S(1)}, u32[]{:S(2)}) copy-start(bf16[192,128]{1,0:T(8,128)(2,1)S(1)} %collective-permute-done.7.refs_2_) | copy-start | bytes 147460
  34.0 23.1 %copy-start.34 = (bf16[192,128]{1,0:T(8,128)(2,1)}, bf16[192,128]{1,0:T(8,128)(2,1)S(1)}, u32[]{:S(2)}) copy-start(bf16[192,128]{1,0:T(8,128)(2,1)S(1)} %collective-permute-done.8.refs_3_) | copy-start | bytes 147460
  34.0 23.1 %copy-start.36 = (bf16[192,128]{1,0:T(8,128)(2,1)}, bf16[192,128]{1,0:T(8,128)(2,1)S(1)}, u32[]{:S(2)}) copy-start(bf16[192,128]{1,0:T(8,128)(2,1)S(1)} %collective-permute-done.9.refs_4_) | copy-start | bytes 147460
  36.0 11.2 %collective-permute-start.12 = (bf16[128,1024]{1,0:T(8,128)(2,1)}, bf16[128,1024]{1,0:T(8,128)(2,1)S(1)}, u32[]{:S(2)}, u32[]{:S(2)}) collective-permute-start(bf16[128,1024]{1,0:T(8,128)(2,1)} %get-tuple-element.47), channel_id=1, source_target_pairs={{0,1},{1,2},{2,3},{3,0},{4,5},{5,6},{6,7},{7,4},{8,9},{9,10},{10,1... | collective-permute-start | bytes 786440 | tf_op jit(solution)/shard_map/ppermute | solution.py:260
  37.5 19.7 %copy-start = (bf16[96,4096]{1,0:T(8,128)(2,1)S(1)}, bf16[96,4096]{1,0:T(8,128)(2,1)}, u32[]{:S(2)}) copy-start(bf16[96,4096]{1,0:T(8,128)(2,1)} %refs_1_.22) | copy-start | bytes 2359300
  37.5 13.6 %collective-permute-start.13 = (bf16[128,1024]{1,0:T(8,128)(2,1)S(1)}, bf16[128,1024]{1,0:T(8,128)(2,1)S(1)}, u32[]{:S(2)}, u32[]{:S(2)}) collective-permute-start(bf16[128,1024]{1,0:T(8,128)(2,1)S(1)} %get-tuple-element.48), channel_id=1, source_target_pairs={{0,3},{1,0},{2,1},{3,2},{4,7},{5,4},{6,5},{7,6},{8,11},{9,8},{10,9... | collective-permute-start | bytes 786440 | tf_op jit(solution)/shard_map/ppermute | solution.py:260
  40.0 21.8 %collective-permute-start.15 = (bf16[128,2048]{1,0:T(8,128)(2,1)}, bf16[128,2048]{1,0:T(8,128)(2,1)S(1)}, u32[]{:S(2)}, u32[]{:S(2)}) collective-permute-start(bf16[128,2048]{1,0:T(8,128)(2,1)} %collective-permute-done.10.refs_0_.refs_6_.refs_3_), channel_id=1, source_target_pairs={{0,8},{1,9},{2,10},{3,11},{4,12},{5,13},{6,14},{7,15},{8,0},{9,1},... | collective-permute-start | bytes 1572872 | tf_op jit(solution)/shard_map/ppermute | solution.py:260
  41.5 20.3 %collective-permute-start.16 = (bf16[128,2048]{1,0:T(8,128)(2,1)}, bf16[128,2048]{1,0:T(8,128)(2,1)S(1)}, u32[]{:S(2)}, u32[]{:S(2)}) collective-permute-start(bf16[128,2048]{1,0:T(8,128)(2,1)} %collective-permute-done.11.refs_1_.refs_9_.refs_3_), channel_id=1, source_target_pairs={{0,16},{1,17},{2,18},{3,19},{4,20},{5,21},{6,22},{7,23},{8,24},{9,... | collective-permute-start | bytes 1572872 | tf_op jit(solution)/shard_map/ppermute | solution.py:260
  57.1 22.8 %collective-permute-start.14 = (f32[96,2048]{1,0:T(8,128)}, f32[96,2048]{1,0:T(8,128)}, u32[]{:S(2)}, u32[]{:S(2)}) collective-permute-start(f32[96,2048]{1,0:T(8,128)} %get-tuple-element.50), channel_id=1, source_target_pairs={{0,4},{1,5},{2,6},{3,7},{4,0},{5,1},{6,2},{7,3},{8,12},{9,13},{10,... | collective-permute-start | bytes 2359304 | tf_op jit(solution)/shard_map/ppermute | solution.py:260
  63.6 16.4 %collective-permute-start.17 = (bf16[128,1024]{1,0:T(8,128)(2,1)}, bf16[128,1024]{1,0:T(8,128)(2,1)}, u32[]{:S(2)}, u32[]{:S(2)}) collective-permute-start(bf16[128,1024]{1,0:T(8,128)(2,1)} %get-tuple-element.51), channel_id=1, source_target_pairs={{0,8},{1,9},{2,10},{3,11},{4,12},{5,13},{6,14},{7,15},{8,0},{9,1},... | collective-permute-start | bytes 786440 | tf_op jit(solution)/shard_map/ppermute | solution.py:260
  65.1 14.9 %collective-permute-start.18 = (bf16[128,1024]{1,0:T(8,128)(2,1)}, bf16[128,1024]{1,0:T(8,128)(2,1)}, u32[]{:S(2)}, u32[]{:S(2)}) collective-permute-start(bf16[128,1024]{1,0:T(8,128)(2,1)} %get-tuple-element.52), channel_id=1, source_target_pairs={{0,16},{1,17},{2,18},{3,19},{4,20},{5,21},{6,22},{7,23},{8,24},{9,... | collective-permute-start | bytes 786440 | tf_op jit(solution)/shard_map/ppermute | solution.py:260
  66.6 6.2 %collective-permute-start.19 = (bf16[192,128]{1,0:T(8,128)(2,1)S(1)}, bf16[192,128]{1,0:T(8,128)(2,1)S(1)}, u32[]{:S(2)}, u32[]{:S(2)}) collective-permute-start(bf16[192,128]{1,0:T(8,128)(2,1)S(1)} %shard_map.100.refs_2_), channel_id=1, source_target_pairs={{0,4},{1,5},{2,6},{3,7},{4,0},{5,1},{6,2},{7,3},{8,12},{9,13},{10,... | collective-permute-start | bytes 147464 | tf_op jit(solution)/shard_map/ppermute | solution.py:260
  69.5 4.2 %collective-permute-start.20 = (bf16[192,128]{1,0:T(8,128)(2,1)S(1)}, bf16[192,128]{1,0:T(8,128)(2,1)S(1)}, u32[]{:S(2)}, u32[]{:S(2)}) collective-permute-start(bf16[192,128]{1,0:T(8,128)(2,1)S(1)} %shard_map.105), channel_id=1, source_target_pairs={{0,3},{1,0},{2,1},{3,2},{4,7},{5,4},{6,5},{7,6},{8,11},{9,8},{10,9... | collective-permute-start | bytes 147464 | tf_op jit(solution)/shard_map/ppermute | solution.py:260
  72.8 5.9 %collective-permute-start.22 = (bf16[192,128]{1,0:T(8,128)(2,1)S(1)}, bf16[192,128]{1,0:T(8,128)(2,1)S(1)}, u32[]{:S(2)}, u32[]{:S(2)}) collective-permute-start(bf16[192,128]{1,0:T(8,128)(2,1)S(1)} %shard_map.106), channel_id=1, source_target_pairs={{0,1},{1,2},{2,3},{3,0},{4,5},{5,6},{6,7},{7,4},{8,9},{9,10},{10,1... | collective-permute-start | bytes 147464 | tf_op jit(solution)/shard_map/ppermute | solution.py:260
  73.7 6.0 %collective-permute-start.21 = (bf16[192,128]{1,0:T(8,128)(2,1)S(1)}, bf16[192,128]{1,0:T(8,128)(2,1)S(1)}, u32[]{:S(2)}, u32[]{:S(2)}) collective-permute-start(bf16[192,128]{1,0:T(8,128)(2,1)S(1)} %collective-permute-done.20.refs_3_), channel_id=1, source_target_pairs={{0,4},{1,5},{2,6},{3,7},{4,0},{5,1},{6,2},{7,3},{8,12},{9,13},{10,... | collective-permute-start | bytes 147464 | tf_op jit(solution)/shard_map/ppermute | solution.py:260
  78.7 1.2 %collective-permute-start.23 = (bf16[192,128]{1,0:T(8,128)(2,1)S(1)}, bf16[192,128]{1,0:T(8,128)(2,1)S(1)}, u32[]{:S(2)}, u32[]{:S(2)}) collective-permute-start(bf16[192,128]{1,0:T(8,128)(2,1)S(1)} %collective-permute-done.22.refs_5_), channel_id=1, source_target_pairs={{0,4},{1,5},{2,6},{3,7},{4,0},{5,1},{6,2},{7,3},{8,12},{9,13},{10,... | collective-permute-start | bytes 147464 | tf_op jit(solution)/shard_map/ppermute | solution.py:260
  81.4 15.0 %copy-start.8 = (bf16[384,256]{1,0:T(8,128)(2,1)S(1)}, bf16[384,256]{1,0:T(8,128)(2,1)}, u32[]{:S(2)}) copy-start(bf16[384,256]{1,0:T(8,128)(2,1)} %refs_1_.25) | copy-start | bytes 589828
  81.4 15.0 %copy-start.11 = (bf16[384,256]{1,0:T(8,128)(2,1)S(1)}, bf16[384,256]{1,0:T(8,128)(2,1)}, u32[]{:S(2)}) copy-start(bf16[384,256]{1,0:T(8,128)(2,1)} %refs_2_.7) | copy-start | bytes 589828
  81.4 15.0 %copy-start.23 = (bf16[2,384,384]{2,1,0:T(8,128)(2,1)S(1)}, bf16[2,384,384]{2,1,0:T(8,128)(2,1)}, u32[]{:S(2)}) copy-start(bf16[2,384,384]{2,1,0:T(8,128)(2,1)} %copy-done.22) | copy-start | bytes 1769476
  81.4 15.0 %copy-start.25 = (bf16[2,384,384]{2,1,0:T(8,128)(2,1)S(1)}, bf16[2,384,384]{2,1,0:T(8,128)(2,1)}, u32[]{:S(2)}) copy-start(bf16[2,384,384]{2,1,0:T(8,128)(2,1)} %copy-done.24) | copy-start | bytes 1769476
  81.4 15.0 %copy-start.27 = (f32[384,256]{1,0:T(8,128)S(1)}, f32[384,256]{1,0:T(8,128)}, u32[]{:S(2)}) copy-start(f32[384,256]{1,0:T(8,128)} %copy-done.26) | copy-start | bytes 1179652
  81.4 15.0 %copy-start.29 = (f32[128,128]{1,0:T(8,128)S(1)}, f32[128,128]{1,0:T(8,128)}, u32[]{:S(2)}) copy-start(f32[128,128]{1,0:T(8,128)} %copy-done.28) | copy-start | bytes 196612
  81.5 15.0 %copy-start.31 = (f32[128,128]{1,0:T(8,128)S(1)}, f32[128,128]{1,0:T(8,128)}, u32[]{:S(2)}) copy-start(f32[128,128]{1,0:T(8,128)} %copy-done.30) | copy-start | bytes 196612
  81.5 5.1 %collective-permute-start.24 = (bf16[192,128]{1,0:T(8,128)(2,1)S(1)}, bf16[192,128]{1,0:T(8,128)(2,1)S(1)}, u32[]{:S(2)}, u32[]{:S(2)}) collective-permute-start(bf16[192,128]{1,0:T(8,128)(2,1)S(1)} %shard_map.107), channel_id=1, source_target_pairs={{0,2},{1,3},{2,0},{3,1},{4,6},{5,7},{6,4},{7,5},{8,10},{9,11},{10,... | collective-permute-start | bytes 147464 | tf_op jit(solution)/shard_map/ppermute | solution.py:260
  88.2 14.7 %collective-permute-start.25 = (f32[96,2048]{1,0:T(8,128)S(1)}, f32[96,2048]{1,0:T(8,128)S(1)}, u32[]{:S(2)}, u32[]{:S(2)}) collective-permute-start(f32[96,2048]{1,0:T(8,128)S(1)} %get-tuple-element.54), channel_id=1, source_target_pairs={{0,4},{1,5},{2,6},{3,7},{4,0},{5,1},{6,2},{7,3},{8,12},{9,13},{10,... | collective-permute-start | bytes 2359304 | tf_op jit(solution)/shard_map/ppermute | solution.py:260
  88.3 2.3 %collective-permute-start.26 = (bf16[192,128]{1,0:T(8,128)(2,1)S(1)}, bf16[192,128]{1,0:T(8,128)(2,1)S(1)}, u32[]{:S(2)}, u32[]{:S(2)}) collective-permute-start(bf16[192,128]{1,0:T(8,128)(2,1)S(1)} %collective-permute-done.24.refs_10_.refs_4_), channel_id=1, source_target_pairs={{0,4},{1,5},{2,6},{3,7},{4,0},{5,1},{6,2},{7,3},{8,12},{9,13},{10,... | collective-permute-start | bytes 147464 | tf_op jit(solution)/shard_map/ppermute | solution.py:260
  91.4 1.3 %collective-permute-start.27 = (f32[128,128]{1,0:T(8,128)S(1)}, f32[128,128]{1,0:T(8,128)S(1)}, u32[]{:S(2)}, u32[]{:S(2)}) collective-permute-start(f32[128,128]{1,0:T(8,128)S(1)} %get-tuple-element.63), channel_id=1, source_target_pairs={{0,4},{1,5},{2,6},{3,7},{4,0},{5,1},{6,2},{7,3},{8,12},{9,13},{10,... | collective-permute-start | bytes 196616 | tf_op jit(solution)/shard_map/ppermute | solution.py:260
  92.7 6.6 %collective-permute-start.28 = (f32[128,128]{1,0:T(8,128)S(1)}, f32[128,128]{1,0:T(8,128)S(1)}, u32[]{:S(2)}, u32[]{:S(2)}) collective-permute-start(f32[128,128]{1,0:T(8,128)S(1)} %add.24), channel_id=1, source_target_pairs={{0,8},{1,9},{2,10},{3,11},{4,12},{5,13},{6,14},{7,15},{8,0},{9,1},... | collective-permute-start | bytes 196616 | tf_op jit(solution)/shard_map/ppermute | solution.py:260
  93.4 6.0 %collective-permute-start.29 = (f32[128,128]{1,0:T(8,128)S(1)}, f32[128,128]{1,0:T(8,128)S(1)}, u32[]{:S(2)}, u32[]{:S(2)}) collective-permute-start(f32[128,128]{1,0:T(8,128)S(1)} %add.24), channel_id=1, source_target_pairs={{0,16},{1,17},{2,18},{3,19},{4,20},{5,21},{6,22},{7,23},{8,24},{9,... | collective-permute-start | bytes 196616 | tf_op jit(solution)/shard_map/ppermute | solution.py:260
  93.9 5.5 %collective-permute-start.30 = (f32[128,128]{1,0:T(8,128)S(1)}, f32[128,128]{1,0:T(8,128)S(1)}, u32[]{:S(2)}, u32[]{:S(2)}) collective-permute-start(f32[128,128]{1,0:T(8,128)S(1)} %add.24), channel_id=1, source_target_pairs={{0,24},{1,25},{2,26},{3,27},{4,28},{5,29},{6,30},{7,31},{8,16},{9,... | collective-permute-start | bytes 196616 | tf_op jit(solution)/shard_map/ppermute | solution.py:260
  100.0 1.3 %collective-permute-start.31 = (f32[128,128]{1,0:T(8,128)S(1)}, f32[128,128]{1,0:T(8,128)S(1)}, u32[]{:S(2)}, u32[]{:S(2)}) collective-permute-start(f32[128,128]{1,0:T(8,128)S(1)} %get-tuple-element.65), channel_id=1, source_target_pairs={{0,4},{1,5},{2,6},{3,7},{4,0},{5,1},{6,2},{7,3},{8,12},{9,13},{10,... | collective-permute-start | bytes 196616 | tf_op jit(solution)/shard_map/ppermute | solution.py:260
  (31 other events, 153.2 us)

commit v7 on v6

v7 whole, which is shorter than its diff:
```python
import functools
import math

import jax
import jax.numpy as jnp
from jax import lax
from jax.experimental import pallas as pl
from jax.experimental.pallas import tpu as pltpu
from jax.sharding import PartitionSpec as P

DH = 128
F32 = jnp.float32
BF16 = jnp.bfloat16
NN = ((1,), (0,))
NT = ((1,), (1,))
TN = ((0,), (0,))
MIB = 1 << 20


def dot(a, b, dims):
    return lax.dot_general(a, b, (dims, ((), ())), preferred_element_type=F32)


def dot_wide(a, b, dims):
    high = b.astype(BF16)
    low = (b - high.astype(F32)).astype(BF16)
    return dot(a, high, dims) + dot(a, low, dims)


def fetch(shape, *parts):
    return (shape, parts)


def all_of(ref, *_):
    return ref


def columns(spot, wide, rows=slice(None)):
    def view(ref, spots, *_):
        return ref.at[rows, pl.ds(pl.multiple_of(spots[spot], DH), wide)]

    return view


def rows_at(first, count):
    return lambda ref, *_: ref.at[first : first + count]


def columns_at(first, count):
    return lambda ref, *_: ref.at[:, first : first + count]


def call(body, outs, args, smem=(), after=(), room=8, flops=1):
    arrays, specs, scratch = [], [], []
    for arg in args:
        if isinstance(arg, tuple):
            arrays += [part[0] for part in arg[1]]
            specs += [pl.BlockSpec(memory_space=pltpu.HBM) for _ in arg[1]]
            scratch.append(pltpu.VMEM(arg[0], arg[1][0][0].dtype))
        else:
            arrays.append(arg)
            specs.append(pl.BlockSpec(memory_space=pltpu.VMEM))
    copies = sum(len(arg[1]) for arg in args if isinstance(arg, tuple))
    held = len(scratch)
    if copies:
        scratch.append(pltpu.SemaphoreType.DMA((copies,)))

    def kernel(*refs):
        scalars, refs = refs[: len(smem)], list(refs[len(smem) :])
        ins, refs = refs[: len(arrays)], refs[len(arrays) + len(after) :]
        results, slots = refs[: len(outs)], refs[len(outs) :]
        given, started, slot = [], [], 0
        for arg in args:
            if not isinstance(arg, tuple):
                given.append(ins.pop(0))
                continue
            for _, source, target in arg[1]:
                copy = pltpu.make_async_copy(
                    source(ins.pop(0), *scalars),
                    target(slots[slot], *scalars),
                    slots[held].at[len(started)],
                )
                copy.start()
                started.append(copy)
            given.append(slots[slot])
            slot += 1
        for copy in started:
            copy.wait()
        body(*scalars, *given, *results)

    moved = sum(a.size * a.dtype.itemsize for a in arrays)
    moved += sum(math.prod(s) * jnp.dtype(t).itemsize for s, t in outs)
    return pl.pallas_call(
        kernel,
        out_shape=[jax.ShapeDtypeStruct(s, t) for s, t in outs],
        in_specs=[pl.BlockSpec(memory_space=pltpu.SMEM) for _ in smem]
        + specs
        + [pl.BlockSpec(memory_space=pl.ANY) for _ in after],
        out_specs=[pl.BlockSpec(memory_space=pltpu.VMEM) for _ in outs],
        scratch_shapes=scratch,
        compiler_params=pltpu.CompilerParams(vmem_limit_bytes=room * MIB),
        cost_estimate=pl.CostEstimate(
            flops=int(flops), bytes_accessed=int(moved), transcendentals=0
        ),
    )(*smem, *arrays, *after)


def hold(arrays, after):
    held = len(arrays)
    return pl.pallas_call(
        lambda *refs: None,
        out_shape=[jax.ShapeDtypeStruct(a.shape, a.dtype) for a in arrays],
        in_specs=[pl.BlockSpec(memory_space=pl.ANY) for _ in (*arrays, *after)],
        out_specs=[pl.BlockSpec(memory_space=pl.ANY) for _ in arrays],
        input_output_aliases={n: n for n in range(held)},
        cost_estimate=pl.CostEstimate(flops=1, bytes_accessed=1, transcendentals=0),
    )(*arrays, *after)


def lower_triangle(blk):
    return lax.broadcasted_iota(jnp.int32, (blk, blk), 0) >= lax.broadcasted_iota(
        jnp.int32, (blk, blk), 1
    )


def forward_kernel(
    scale,
    mask,
    where,
    q_ref,
    k_ref,
    v_ref,
    probs_ref,
    inner_ref,
    soft_ref,
    mine_ref,
    other_ref,
    far_ref,
):
    rows, width = q_ref.shape
    count = mask.shape[0]
    blk = rows // count
    inv_root = 1.0 / math.sqrt(DH)
    triangle = lower_triangle(blk)
    for i in range(count):
        here = slice(i * blk, (i + 1) * blk)
        upto = slice(0, (i + 1) * blk)
        sums = []
        for h in range(2):
            cols = slice(h * DH, (h + 1) * DH)
            raw = dot(q_ref[here, cols], k_ref[upto, cols], NT)
            scores, inner = [], []
            for j in range(i + 1):
                part = raw[:, j * blk : (j + 1) * blk]
                keep = triangle if j == i else mask[i, j] > 0
                scores.append(jnp.where(keep, part * inv_root, -1e30))
                inner.append(jnp.where(triangle, part, 0.0) if j == i else part)
            scores = jnp.concatenate(scores, 1)
            inner = jnp.concatenate(inner, 1).astype(BF16)
            expo = jnp.exp(scores - jnp.max(scores, -1, keepdims=True))
            probs = (expo / jnp.sum(expo, -1, keepdims=True)).astype(BF16)
            v = v_ref[upto, cols]
            soft = dot(probs, v, NN)
            probs_ref[h, here, upto] = probs
            inner_ref[h, here, upto] = inner
            soft_ref[here, cols] = soft
            sums.append(soft + scale * dot(inner, v, NN))
        mine_ref[here], other_ref[here] = pick(where[2], sums)
    far_ref[...] = q_ref[:, pl.ds(pl.multiple_of((1 - where[2]) * DH, DH), DH)]


def pick(core, parts):
    return jnp.where(core == 0, parts[0], parts[1]), jnp.where(core == 0, parts[1], parts[0])


def both_heads(core, mine_ref, other_ref):
    mine, other = mine_ref[...], other_ref[...]
    return jnp.where(core == 0, mine, other), jnp.where(core == 0, other, mine)


def state_kernel(where, k_ref, v_ref, mine_ref, other_ref):
    heads = [slice(h * DH, (h + 1) * DH) for h in range(2)]
    parts = [dot(k_ref[:, cols], v_ref[:, cols], TN) for cols in heads]
    mine_ref[...], other_ref[...] = pick(where[2], parts)


def carry(flags, here_ref, got_ref, totals):
    carried = jnp.zeros(here_ref.shape, F32)
    for n, total in enumerate(totals):
        carried = carried + jnp.where(flags[n] > 0, total[...], 0.0)
    counts = flags[len(totals)] > 0
    keep = carried + jnp.where(counts, got_ref[...], 0.0)
    return keep, carried + jnp.where(counts, 0.0, here_ref[...])


def carry_kernel(flags, here_ref, got_ref, *refs):
    totals, (keep_ref, back_ref) = refs[:-2], refs[-2:]
    keep_ref[...], back_ref[...] = carry(flags, here_ref, got_ref, totals)


def attn_kernel(scale, count, flags, where, here_ref, got_ref, *refs):
    totals, refs = refs[: -count - 6], refs[-count - 6 :]
    q_ref, far_ref, pre_ref, far_pre_ref = refs[:4]
    out_refs, (keep_ref, back_ref) = refs[4:-2], refs[-2:]
    keep, back = carry(flags, here_ref, got_ref, totals)
    keep_ref[...], back_ref[...] = keep, back
    own = pre_ref.shape[0] // count
    cols = pl.ds(pl.multiple_of(where[2] * DH, DH), DH)
    for s, out_ref in enumerate(out_refs):
        block = lax.rem(where[0] + s, count)
        here = pl.ds(pl.multiple_of(block * own, own), own)
        mine = pre_ref[here] + scale * dot_wide(q_ref[here, cols], keep, NN)
        mate = far_pre_ref[here] + scale * dot_wide(far_ref[here], back, NN)
        out_ref[:own] = mine.astype(BF16)
        out_ref[own:] = mate.astype(BF16)


def first_kernel(spots, left_ref, weight_ref, right_ref, own_ref, half_ref):
    own_ref[...] = dot(left_ref[...], weight_ref[...], NT).astype(BF16)
    near = left_ref[:, pl.ds(pl.multiple_of(spots[0], DH), right_ref.shape[1])]
    half_ref[...] = dot(near, right_ref[...], NT)


def second_kernel(spots, left_ref, right_ref, half_ref, piece_ref, one_ref, three_ref, *cut_refs):
    wide = cut_refs[0].shape[1]
    for n, cut_ref in enumerate(cut_refs):
        cut_ref[...] = piece_ref[:, n * wide : (n + 1) * wide]
    total = (half_ref[...] + dot(left_ref[...], right_ref[...], NT)).astype(BF16)
    one_ref[...], three_ref[...] = total[:, :DH], total[:, DH:]


def last_kernel(spots, left_ref, right_ref, half_ref, out_ref):
    out_ref[...] = (half_ref[...] + dot(left_ref[...], right_ref[...], NT)).astype(BF16)


def near_kernel(spots, left_ref, right_ref, *refs):
    attn, (half_ref, own_out, mate_out) = refs[:-3], refs[-3:]
    half_ref[...] = dot(left_ref[...], right_ref[2 * DH : 3 * DH], NT)
    far_kernel(spots, right_ref, *attn, own_out, mate_out)


def far_kernel(spots, right_ref, *refs):
    attn, (own_out, mate_out) = refs[:-2], refs[-2:]
    own = own_out.shape[0]
    part = dot(jnp.concatenate([a[...] for a in attn], 1), right_ref[...], NN)
    own_out[...] = part[:own]
    mate_out[...] = part[own:]


def grad_kernel(whole, added, places, mine_ref, mate_ref, *refs):
    chunks, out_ref = refs[added:-1], refs[-1]
    total = refs[0][...] if added else None
    for j, chunk in enumerate(chunks):
        cols = slice(None) if whole else pl.ds(pl.multiple_of(places[j], DH), chunk.shape[1])
        left = jnp.concatenate([mine_ref[:, cols], mate_ref[:, cols]], 0)
        part = dot(left, chunk[...], NT)
        total = part if total is None else total + part
    out_ref[...] = total.astype(out_ref.dtype)


def mixed_kernel(count, each, places, *refs):
    attn, weight = refs[:count], refs[count]
    chunks, (own_out, mate_out) = list(refs[count + 1 : -2]), refs[-2:]
    own = own_out.shape[0]
    left = jnp.concatenate([a[...] for a in attn], 1)
    right = [weight[:, pl.ds(pl.multiple_of(places[0], DH), own_out.shape[1])]]
    for n in each:
        parts = [chunks.pop(0)[...] for _ in range(n)]
        right.append(jnp.concatenate(parts, 1) if n > 1 else parts[0])
    part = dot(left, jnp.concatenate(right, 0), NN)
    own_out[...] = part[:own]
    mate_out[...] = part[own:]


def join_kernel(places, *refs):
    out_ref, done_ref = refs[-2:]
    done_ref[...] = jnp.zeros(done_ref.shape, F32)
    for n in range(len(refs) // 2 - 1):
        wide = refs[2 * n].shape[1]
        there = pl.ds(pl.multiple_of(places[n], DH), wide)
        out_ref[:, there] = (refs[2 * n][...] + refs[2 * n + 1][...]).astype(BF16)


def collect_kernel(scale, count, where, q_ref, *refs):
    direct, across = refs[:count], refs[count : 2 * count]
    g_ref, mine_ref, other_ref = refs[2 * count :]
    own = g_ref.shape[0] // count
    mine = pl.ds(pl.multiple_of(where[2] * DH, DH), DH)
    mate = pl.ds(pl.multiple_of((1 - where[2]) * DH, DH), DH)
    for s in range(count):
        block = lax.rem(where[0] + s, count)
        here = pl.ds(pl.multiple_of(block * own, own), own)
        g_ref[here, mine] = direct[s][:own]
        g_ref[here, mate] = across[s][own:]
    heads = [slice(h * DH, (h + 1) * DH) for h in range(2)]
    parts = [scale * dot(q_ref[:, cols], g_ref[:, cols], TN) for cols in heads]
    mine_ref[...], other_ref[...] = pick(where[2], parts)


def backward_kernel(
    scale,
    count,
    where,
    q_ref,
    k_ref,
    v_ref,
    g_ref,
    probs_ref,
    inner_ref,
    soft_ref,
    mine_ref,
    other_ref,
    dq_ref,
    dk_ref,
    dv_ref,
):
    rows, width = q_ref.shape
    blk = rows // count
    inv_root = 1.0 / math.sqrt(DH)
    triangle = lower_triangle(blk)
    states = both_heads(where[2], mine_ref, other_ref)
    for h in range(width // DH):
        cols = slice(h * DH, (h + 1) * DH)
        for i in reversed(range(count)):
            here = slice(i * blk, (i + 1) * blk)
            upto = slice(0, (i + 1) * blk)
            q, g = q_ref[here, cols], g_ref[here, cols]
            k = k_ref[upto, cols]
            probs = probs_ref[h, here, upto]
            dprod = dot(g, v_ref[upto, cols], NT)
            delta = jnp.sum(g.astype(F32) * soft_ref[here, cols], -1, keepdims=True)
            dscore = (probs.astype(F32) * (dprod - delta) * inv_root).astype(BF16)
            last = jnp.where(triangle, dprod[:, i * blk :], 0.0)
            dinner = jnp.concatenate([dprod[:, : i * blk], last], 1) if i else last
            dinner = dinner.astype(BF16)
            dq_ref[here, cols] = (
                dot(dscore, k, NN)
                + scale * (dot(dinner, k, NN) + dot_wide(g, states[h], NT))
            ).astype(BF16)
            dk = dot(dscore, q, TN) + scale * dot(dinner, q, TN)
            dv = dot(probs, g, TN) + scale * dot(inner_ref[h, here, upto], g, TN)
            if i == count - 1:
                dk_ref[upto, cols] = dk
                dv_ref[upto, cols] = dv
            else:
                dk_ref[upto, cols] += dk
                dv_ref[upto, cols] += dv


def close_kernel(where, k_ref, v_ref, dk_ref, dv_ref, mine_ref, other_ref, gk_ref, gv_ref):
    states = both_heads(where[2], mine_ref, other_ref)
    for h in range(k_ref.shape[1] // DH):
        cols = slice(h * DH, (h + 1) * DH)
        state = states[h]
        gk_ref[:, cols] = (dk_ref[:, cols] + dot_wide(v_ref[:, cols], state, NT)).astype(BF16)
        gv_ref[:, cols] = (dv_ref[:, cols] + dot_wide(k_ref[:, cols], state, NN)).astype(BF16)


def send(x, flip, shift):
    shards, heads = lax.axis_size("ctx"), lax.axis_size("head")
    pairs = [
        (c * heads + z, (c ^ flip) * heads + (z + shift) % heads)
        for c in range(shards)
        for z in range(heads)
    ]
    return lax.ppermute(x, ("ctx", "head"), pairs)


def exchange(mine, other, core, chip, chips, later):
    got = send(other, 1, 0)
    own = total = mine + got
    totals, flags = [], []
    if chips == 4:
        for flip in (1, 2, 3):
            totals.append(send(total, 2 * flip, 0))
            flags.append(((chip ^ flip) > chip) == later)
    else:
        step = 1
        while step < chips:
            totals.append(send(total, 2 * step, 0))
            flags.append(((chip & step) == 0) == later)
            total = total + totals[-1]
            step *= 2
    flags.append((core == 0) == later)
    return jnp.stack(flags).astype(jnp.int32), [mine, got, *totals], own


def on_device(query, key, value, block_mask, out_weight, cotangent):
    rows, width = query.shape
    heads = width // DH
    shards, count = lax.axis_size("ctx"), lax.axis_size("head")
    model = out_weight.shape[1]
    own = rows // count
    scale = 1.0 / math.sqrt(DH * rows * shards)
    blocks = block_mask.shape[0]
    ctx, place = lax.axis_index("ctx"), lax.axis_index("head")
    core, chip, chips = ctx & 1, ctx >> 1, shards // 2
    where = jnp.stack([place, ctx, core])
    flat, square = (rows, width), rows * rows * DH * heads
    pair = [((DH, DH), F32)] * 2
    tokens = ((2 * own, DH), BF16)
    product = 4 * own * DH * model

    board = chips == 4 and count == 4
    wide = model // (2 if board else chips)
    colour = (chip & 1) ^ (chip >> 1) if board else chip
    piece = lax.dynamic_slice(out_weight, (core * DH, colour * wide), (DH, wide))
    arrived = {1: send(piece, 0, 1), count - 1: send(piece, 0, -1)}
    mate_cotangent = send(cotangent, 1, 0)

    mine, other = call(
        state_kernel,
        pair,
        [fetch(flat, (a, all_of, all_of)) for a in (key, value)],
        [where],
        [mate_cotangent],
    )
    flags, parts, total = exchange(mine, other, core, chip, chips, False)
    probs, inner, soft, pre, other, far = call(
        functools.partial(forward_kernel, scale),
        [((heads, rows, rows), BF16)] * 2
        + [(flat, F32)]
        + [((rows, DH), F32)] * 2
        + [((rows, DH), BF16)],
        [query, key, value],
        [block_mask, where],
        [total],
        flops=6 * square,
    )
    *attn, keep, back = call(
        functools.partial(attn_kernel, scale, count),
        [tokens] * count + pair,
        [*parts, query, send(far, 1, 0), pre, send(other, 1, 0)],
        [flags, where],
    )
    linear = [keep, send(back, 1, 0)]
    attn = [attn[0]] + [send(attn[s], 0, s) for s in range(1, count)]

    work = near_and_far if board else by_gathers
    both, across, joins, starts = work(
        attn, arrived, cotangent, mate_cotangent, out_weight, core, chip, colour, product
    )
    mixed, done = call(
        join_kernel, [((own, model), BF16), ((8, DH), F32)], joins, [jnp.stack(starts)]
    )

    g, mine, other = call(
        functools.partial(collect_kernel, scale, count),
        [(flat, BF16), *pair],
        [query, *both, *across],
        [where],
    )
    flags, parts, total = exchange(mine, other, core, chip, chips, True)
    grad_query, dk, dv = call(
        functools.partial(backward_kernel, scale, blocks),
        [(flat, BF16)] + [(flat, F32)] * 2,
        [query, key, value, g, probs, inner, soft, *linear],
        [where],
        [total],
        flops=14 * square,
    )
    keep, back = call(carry_kernel, pair, parts, [flags], [dk])
    grad_key, grad_value = call(
        close_kernel,
        [(flat, BF16)] * 2,
        [key, value, dk, dv, keep, send(back, 1, 0)],
        [where],
        [done],
    )
    return mixed, grad_query, grad_key, grad_value


def near_and_far(attn, arrived, cotangent, mate_cotangent, weight, core, chip, colour, product):
    own, model = cotangent.shape
    wide = model // 2
    spots = jnp.stack([colour * wide, (1 - colour) * wide, core * DH])
    tokens = ((2 * own, DH), BF16)
    parts = [((own, wide), F32)] * 2
    all_arrays = [(cotangent, all_of, rows_at(0, own)), (mate_cotangent, all_of, rows_at(own, own))]
    whole = fetch((2 * own, model), *all_arrays)
    left = [
        fetch((2 * own, wide), *((a, columns(n, wide), put) for a, _, put in all_arrays))
        for n in range(2)
    ]

    def own_rows(ref, spots, *_):
        return ref.at[pl.ds(pl.multiple_of(spots[2], DH), DH)]

    def own_columns(n):
        return lambda ref, spots, *_: ref.at[
            pl.ds(pl.multiple_of(spots[2], DH), DH), pl.ds(pl.multiple_of(spots[n], DH), wide)
        ]

    def stacked(*arrays):
        return [(a, all_of, rows_at(n * DH, DH)) for n, a in enumerate(arrays)]

    arrived[1], arrived[3] = hold([arrived[1], arrived[3]], attn[1:])
    arrived[2] = send(arrived[1], 0, 1)
    second = {1: send(arrived[1], 2, 0), 3: send(arrived[3], 4, 0)}
    mine, half = call(
        first_kernel,
        [tokens, ((2 * own, 2 * DH), F32)],
        [
            whole,
            fetch((DH, model), (weight, own_rows, all_of)),
            fetch((2 * DH, wide), *stacked(arrived[1], arrived[3])),
        ],
        [spots],
        room=24,
        flops=2 * product,
    )
    one, three, *cuts = call(
        second_kernel,
        [tokens] * 2 + [((DH, wide // 2), BF16)] * 2,
        [
            left[1],
            fetch((2 * DH, wide), *stacked(second[1], second[3])),
            half,
            fetch((DH, wide), (arrived[2], all_of, all_of)),
        ],
        [spots],
        room=16,
        flops=product,
    )
    second[2] = [send(cuts[0], 2, 0), send(cuts[1], 4, 0)]
    both = {0: mine, 1: send(one, 0, -1), 3: send(three, 0, -3)}
    across = {s: send(both[s], 1, 0) for s in (0, 1, 3)}
    half, part, mate_part = call(
        near_kernel,
        [((2 * own, DH), F32), *parts],
        [
            left[0],
            fetch(
                (4 * DH, wide),
                (weight, own_columns(0), rows_at(0, DH)),
                *((arrived[s], all_of, rows_at(s * DH, DH)) for s in (1, 2, 3)),
            ),
            *attn,
        ],
        [spots],
        room=24,
        flops=2 * product,
    )
    joins = [part, send(mate_part, 1, 0)]
    quarters = [(a, all_of, columns_at(n * wide // 2, wide // 2)) for n, a in enumerate(second[2])]
    (two,) = call(
        last_kernel,
        [tokens],
        [left[1], fetch((DH, wide), *quarters), half],
        [spots],
        [across[0], across[1], across[3]],
        room=16,
        flops=product // 2,
    )
    both[2] = send(two, 0, -2)

    def quarter(n):
        return lambda ref, *_: ref.at[2 * DH : 3 * DH, n * wide // 2 : (n + 1) * wide // 2]

    part, mate_part = call(
        far_kernel,
        parts,
        [
            fetch(
                (4 * DH, wide),
                (weight, own_columns(1), rows_at(0, DH)),
                (second[1], all_of, rows_at(DH, DH)),
                (second[3], all_of, rows_at(3 * DH, DH)),
                *((a, all_of, quarter(n)) for n, a in enumerate(second[2])),
            ),
            *attn,
        ],
        [spots],
        [both[2]],
        room=24,
        flops=2 * product,
    )
    joins += [part, send(mate_part, 1, 0)]
    across[2] = send(both[2], 1, 0)
    return [both[s] for s in range(4)], [across[s] for s in range(4)], joins, [spots[0], spots[1]]


def by_gathers(attn, arrived, cotangent, mate_cotangent, out_weight, core, chip, colour, product):
    own, model = cotangent.shape
    shards, count = lax.axis_size("ctx"), lax.axis_size("head")
    weight = lax.dynamic_slice_in_dim(out_weight, core * DH, DH, 0)
    zero = jnp.zeros((1,), jnp.int32)
    groups = [list(range(k, shards, 2)) for k in range(2)]
    for s in range(2, count - 1):
        arrived[s] = send(arrived[s - 1], 0, 1)
    chunks = [weight] + [
        lax.all_gather(arrived[s], "ctx", axis=1, tiled=True, axis_index_groups=groups)
        for s in range(1, count)
    ]
    both = []
    for s in range(count):
        (block,) = call(
            functools.partial(grad_kernel, True, 0),
            [((2 * own, DH), BF16)],
            [cotangent, mate_cotangent, chunks[s]],
            [zero],
            flops=product,
        )
        both.append(send(block, 0, -s) if s else block)
    part, mate_part = call(
        functools.partial(mixed_kernel, count, [1] * (count - 1)),
        [((own, model), F32)] * 2,
        [*attn, *chunks],
        [zero],
        room=16,
        flops=count * product,
    )
    return both, [send(b, 1, 0) for b in both], [part, send(mate_part, 1, 0)], [jnp.int32(0)]


def solution(mesh):
    return jax.shard_map(
        on_device,
        mesh=mesh,
        in_specs=(
            P("ctx", "head"),
            P("ctx", "head"),
            P("ctx", "head"),
            P("ctx", None),
            P("head", None),
            P(("ctx", "head"), None),
        ),
        out_specs=(P(("ctx", "head"), None), P("ctx", "head"), P("ctx", "head"), P("ctx", "head")),
        check_vma=False,
    )
```

time: 106 us -> 99.6 us (0.940)
  waiting for transfers between devices: 32.2 us -> 25.6 us
  Pallas kernels: 28.4 us -> 24.1 us
  local copies, waits for them, and re-layouts: 12.9 us -> 16.9 us
    ppermute x32, waiting for transfers between devices: 32.2 us -> 25.6 us  [send(): return lax.ppermute(x, ('ctx', 'head'), pairs)]
    pallas_call x21 -> x13, Pallas kernels: 28.4 us -> 24 us  [call(): pl.pallas_call(kernel, out_shape=[jax.ShapeDtypeStruct(s, t) for s, t in...]
    unnamed x94 -> x76, local copies, waits for them, and re-layouts: 11.7 us -> 15.1 us
  transfers between devices with their start and end apart: 32 -> 32, of which waited for: 16 -> 14; matrix products, arithmetic and copies ran while one was open for 2% -> 3% of each run, Pallas kernels for 20% -> 19%
where the time goes in v7:
time: 99.6 us; the launch traced here: 99 us
  starting transfers between devices  30.4 us (31%)
  waiting for transfers between devices  25.6 us (26%)
  Pallas kernels  24.1 us (24%)
  local copies, waits for them, and re-layouts  16.9 us (17%)
  between operations  1.04 us (1%)
  other arithmetic  1.02 us (1%)
    ppermute x32, starting transfers between devices, send(): return lax.ppermute(x, ('ctx', 'head'), pairs)  30.4 us
    ppermute x32, waiting for transfers between devices, send(): return lax.ppermute(x, ('ctx', 'head'), pairs)  25.6 us
    pallas_call x13, Pallas kernels, call(): pl.pallas_call(kernel, out_shape=[jax.ShapeDtypeStruct(s, t) for s, t in...  24 us
    unnamed x76, local copies, waits for them, and re-layouts  15.1 us
  transfers between devices with their start and end apart: 32, of which 14 were waited for; matrix products, arithmetic and copies ran while one was open for 3% of the time, Pallas kernels for 19%

profile of v7, /device:TPU:0, one launch (start us, length us, event | category | flops | bytes accessed | tf_op | source)
XLA Modules:
  0.0 99.0 jit_solution(15199952500151018044)
XLA Ops:
  1.2 1.9 %dynamic_slice.3 = bf16[128,2048]{1,0:T(8,128)(2,1)} dynamic-slice(bf16[256,4096]{1,0:T(8,128)(2,1)} %refs_1_.14, s32[]{:T(128)S(6)} %select_n.6, s32[]{:T(128)S(6)} %select_n.7), dynamic_slice_sizes={128,2048} | dynamic-slice | bytes 1048580 | tf_op jit(solution)/shard_map/dynamic_slice | solution.py:407
  3.0 2.6 %collective-permute-start.1 = (bf16[128,2048]{1,0:T(8,128)(2,1)}, bf16[128,2048]{1,0:T(8,128)(2,1)S(1)}, u32[]{:S(2)}, u32[]{:S(2)}) collective-permute-start(bf16[128,2048]{1,0:T(8,128)(2,1)} %dynamic_slice.3), channel_id=1, source_target_pairs={{0,1},{1,2},{2,3},{3,0},{4,5},{5,6},{6,7},{7,4},{8,9},{9,10},{10,1... | collective-permute-start | bytes 1572872 | tf_op jit(solution)/shard_map/ppermute | solution.py:366
  5.6 2.0 %collective-permute-start.2 = (bf16[128,2048]{1,0:T(8,128)(2,1)}, bf16[128,2048]{1,0:T(8,128)(2,1)}, u32[]{:S(2)}, u32[]{:S(2)}) collective-permute-start(bf16[128,2048]{1,0:T(8,128)(2,1)} %dynamic_slice.3), channel_id=1, source_target_pairs={{0,3},{1,0},{2,1},{3,2},{4,7},{5,4},{6,5},{7,6},{8,11},{9,8},{10,9... | collective-permute-start | bytes 1572872 | tf_op jit(solution)/shard_map/ppermute | solution.py:366
  7.8 1.1 %copy-done.8 = bf16[384,256]{1,0:T(8,128)(2,1)S(1)} copy-done((bf16[384,256]{1,0:T(8,128)(2,1)S(1)}, bf16[384,256]{1,0:T(8,128)(2,1)}, u32[]{:S(2)}) %copy-start.8) | copy-done | bytes 196632
  8.8 0.9 copy-done.11
  9.8 1.3 %shard_map.93 = (f32[128,128]{1,0:T(8,128)S(1)}, f32[128,128]{1,0:T(8,128)S(1)}) custom-call(s32[3]{0:T(128)S(1)} %pad_add_fusion.2.refs_0_.refs_1_, bf16[384,256]{1,0:T(8,128)(2,1)S(1)} %copy-done.8, bf16[384,256]{1,0:T(8,128)(2,1)S(1)} %copy-done.11, bf16[96,4096]{1,0:T(8,128)(2,1)S(1)} %collective-permute-done.refs_3_.refs_2_), custom_call_target="tpu_custom_call" | custom-call | flops 1 | bytes 524288 | tf_op jit(solution)/shard_map/pallas_call | solution.py:93
  11.3 1.1 %collective-permute-done.3.refs_3_ = f32[128,128]{1,0:T(8,128)S(1)} collective-permute-done((f32[128,128]{1,0:T(8,128)S(1)}, f32[128,128]{1,0:T(8,128)S(1)}, u32[]{:S(2)}, u32[]{:S(2)}) %collective-permute-start.3) | collective-permute-done | bytes 65568 | tf_op jit(solution)/shard_map/ppermute | solution.py:366
  13.0 0.9 copy-done.5
  14.0 0.9 copy-done.9
  14.9 0.9 copy-done.12
  15.8 2.7 %shard_map.94 = (bf16[2,384,384]{2,1,0:T(8,128)(2,1)S(1)}, bf16[2,384,384]{2,1,0:T(8,128)(2,1)S(1)}, f32[384,256]{1,0:T(8,128)S(1)}, f32[384,128]{1,0:T(8,128)S(...) custom-call(s32[3,3]{1,0:T(4,128)S(1)} %copy-done.37, s32[3]{0:T(128)S(1)} %pad_add_fusion.2.refs_0_.refs_1_, ...), custom_call_target="tpu_custom_call" | custom-call | flops 226492416 | bytes 2654208 | tf_op jit(solution)/shard_map/pallas_call | solution.py:93
  18.6 0.8 copy-done.14
  19.4 0.8 copy-done.16
  22.5 1.7 %collective-permute-start.4 = (f32[128,128]{1,0:T(8,128)}, f32[128,128]{1,0:T(8,128)}, u32[]{:S(2)}, u32[]{:S(2)}) collective-permute-start(f32[128,128]{1,0:T(8,128)} %add.14.refs_5_), channel_id=1, source_target_pairs={{0,8},{1,9},{2,10},{3,11},{4,12},{5,13},{6,14},{7,15},{8,0},{9,1},... | collective-permute-start | bytes 196616 | tf_op jit(solution)/shard_map/ppermute | solution.py:366
  24.1 1.5 %collective-permute-start.5 = (f32[128,128]{1,0:T(8,128)}, f32[128,128]{1,0:T(8,128)}, u32[]{:S(2)}, u32[]{:S(2)}) collective-permute-start(f32[128,128]{1,0:T(8,128)} %add.14.refs_5_), channel_id=1, source_target_pairs={{0,16},{1,17},{2,18},{3,19},{4,20},{5,21},{6,22},{7,23},{8,24},{9,... | collective-permute-start | bytes 196616 | tf_op jit(solution)/shard_map/ppermute | solution.py:366
  25.7 1.4 %collective-permute-done.4.refs_4_ = f32[128,128]{1,0:T(8,128)} collective-permute-done((f32[128,128]{1,0:T(8,128)}, f32[128,128]{1,0:T(8,128)}, u32[]{:S(2)}, u32[]{:S(2)}) %collective-permute-start.4) | collective-permute-done | bytes 65568 | tf_op jit(solution)/shard_map/ppermute | solution.py:366
  27.1 2.7 %collective-permute-start.6 = (f32[128,128]{1,0:T(8,128)}, f32[128,128]{1,0:T(8,128)S(1)}, u32[]{:S(2)}, u32[]{:S(2)}) collective-permute-start(f32[128,128]{1,0:T(8,128)} %add.14.refs_5_), channel_id=1, source_target_pairs={{0,24},{1,25},{2,26},{3,27},{4,28},{5,29},{6,30},{7,31},{8,16},{9,... | collective-permute-start | bytes 196616 | tf_op jit(solution)/shard_map/ppermute | solution.py:366
  29.8 2.6 %collective-permute-done.6.refs_6_ = f32[128,128]{1,0:T(8,128)S(1)} collective-permute-done((f32[128,128]{1,0:T(8,128)}, f32[128,128]{1,0:T(8,128)S(1)}, u32[]{:S(2)}, u32[]{:S(2)}) %collective-permute-start.6) | collective-permute-done | bytes 65568 | tf_op jit(solution)/shard_map/ppermute | solution.py:366
  32.5 0.9 copy-done.6
  33.4 0.9 copy-done.29
  34.3 1.3 %shard_map.95 = (bf16[192,128]{1,0:T(8,128)(2,1)S(1)}, bf16[192,128]{1,0:T(8,128)(2,1)S(1)}, bf16[192,128]{1,0:T(8,128)(2,1)S(1)}, bf16[192,128]{1,0:T(8,128)(2,...) custom-call(s32[4]{0:T(128)S(1)} %add_convert_fusion.refs_0_, s32[3]{0:T(128)S(1)} %pad_add_fusion.2.refs_0_.refs_1_, ...), custom_call_target="tpu_custom_call" | custom-call | flops 1 | bytes 1343488 | tf_op jit(solution)/shard_map/pallas_call | solution.py:93
  37.5 2.6 %collective-permute-start.10 = (bf16[192,128]{1,0:T(8,128)(2,1)S(1)}, bf16[192,128]{1,0:T(8,128)(2,1)S(1)}, u32[]{:S(2)}, u32[]{:S(2)}) collective-permute-start(bf16[192,128]{1,0:T(8,128)(2,1)S(1)} %get-tuple-element.49), channel_id=1, source_target_pairs={{0,2},{1,3},{2,0},{3,1},{4,6},{5,7},{6,4},{7,5},{8,10},{9,11},{10,... | collective-permute-start | bytes 147464 | tf_op jit(solution)/shard_map/ppermute | solution.py:366
  40.1 1.4 %collective-permute-start.11 = (bf16[192,128]{1,0:T(8,128)(2,1)S(1)}, bf16[192,128]{1,0:T(8,128)(2,1)S(1)}, u32[]{:S(2)}, u32[]{:S(2)}) collective-permute-start(bf16[192,128]{1,0:T(8,128)(2,1)S(1)} %get-tuple-element.50), channel_id=1, source_target_pairs={{0,3},{1,0},{2,1},{3,2},{4,7},{5,4},{6,5},{7,6},{8,11},{9,8},{10,9... | collective-permute-start | bytes 147464 | tf_op jit(solution)/shard_map/ppermute | solution.py:366
  41.5 2.0 %collective-permute-done.9.refs_2_.refs_8_.refs_7_ = bf16[192,128]{1,0:T(8,128)(2,1)S(1)} collective-permute-done((bf16[192,128]{1,0:T(8,128)(2,1)S(1)}, bf16[192,128]{1,0:T(8,128)(2,1)S(1)}, u32[]{:S(2)}, u32[]{:S(2)}) %collective-permute-start.9) | collective-permute-done | bytes 49184 | tf_op jit(solution)/shard_map/ppermute | solution.py:366
  44.8 1.8 %collective-permute-start.12 = (bf16[128,2048]{1,0:T(8,128)(2,1)}, bf16[128,2048]{1,0:T(8,128)(2,1)}, u32[]{:S(2)}, u32[]{:S(2)}) collective-permute-start(bf16[128,2048]{1,0:T(8,128)(2,1)} %get-tuple-element.51.refs_4_), channel_id=1, source_target_pairs={{0,1},{1,2},{2,3},{3,0},{4,5},{5,6},{6,7},{7,4},{8,9},{9,10},{10,1... | collective-permute-start | bytes 1572872 | tf_op jit(solution)/shard_map/ppermute | solution.py:366
  46.6 1.7 %collective-permute-start.14 = (bf16[128,2048]{1,0:T(8,128)(2,1)}, bf16[128,2048]{1,0:T(8,128)(2,1)S(1)}, u32[]{:S(2)}, u32[]{:S(2)}) collective-permute-start(bf16[128,2048]{1,0:T(8,128)(2,1)} %get-tuple-element.51.refs_4_), channel_id=1, source_target_pairs={{0,8},{1,9},{2,10},{3,11},{4,12},{5,13},{6,14},{7,15},{8,0},{9,1},... | collective-permute-start | bytes 1572872 | tf_op jit(solution)/shard_map/ppermute | solution.py:366
  48.3 1.5 %collective-permute-start.15 = (bf16[128,2048]{1,0:T(8,128)(2,1)}, bf16[128,2048]{1,0:T(8,128)(2,1)}, u32[]{:S(2)}, u32[]{:S(2)}) collective-permute-start(bf16[128,2048]{1,0:T(8,128)(2,1)} %get-tuple-element.52.refs_6_.refs_5_), channel_id=1, source_target_pairs={{0,16},{1,17},{2,18},{3,19},{4,20},{5,21},{6,22},{7,23},{8,24},{9,... | collective-permute-start | bytes 1572872 | tf_op jit(solution)/shard_map/ppermute | solution.py:366
  49.9 1.1 %copy-done.1 = bf16[96,4096]{1,0:T(8,128)(2,1)S(1)} copy-done((bf16[96,4096]{1,0:T(8,128)(2,1)S(1)}, bf16[96,4096]{1,0:T(8,128)(2,1)}, u32[]{:S(2)}) %copy-start.1) | copy-done | bytes 786456
  51.1 1.0 %copy-done.3 = bf16[128,2048]{1,0:T(8,128)(2,1)S(1)} copy-done((bf16[128,2048]{1,0:T(8,128)(2,1)S(1)}, bf16[128,2048]{1,0:T(8,128)(2,1)}, u32[]{:S(2)}) %copy-start.3) | copy-done | bytes 524312
  52.1 2.7 %shard_map.98 = (bf16[192,128]{1,0:T(8,128)(2,1)S(1)}, f32[192,256]{1,0:T(8,128)S(1)}) custom-call(s32[3]{0:T(128)S(1)} %pad_add_fusion.1.refs_0_, bf16[96,4096]{1,0:T(8,128)(2,1)S(1)} %copy-done.1, bf16[96,4096]{1,0:T(8,128)(2,1)S(1)} %collective-permute-done.refs_3_.refs_2_, bf16[256,4096]{1,0:T(8,128)(2,1)S(1)} %copy-done, ...), custom_call_target="tpu_custom_call" | custom-call | flops 402653184 | bytes 4964352 | tf_op jit(solution)/shard_map/pallas_call | solution.py:93
  54.9 3.7 %collective-permute-done.12.refs_5_.refs_6_ = bf16[128,2048]{1,0:T(8,128)(2,1)} collective-permute-done((bf16[128,2048]{1,0:T(8,128)(2,1)}, bf16[128,2048]{1,0:T(8,128)(2,1)}, u32[]{:S(2)}, u32[]{:S(2)}) %collective-permute-start.12) | collective-permute-done | bytes 524320 | tf_op jit(solution)/shard_map/ppermute | solution.py:366
  59.1 2.4 %shard_map.99 = (bf16[192,128]{1,0:T(8,128)(2,1)S(1)}, bf16[192,128]{1,0:T(8,128)(2,1)S(1)}, bf16[128,1024]{1,0:T(8,128)(2,1)S(1)}, bf16[128,1024]{1,0:T(8,128)(2,1)S(1)}) custom-call(s32[3]{0:T(128)S(1)} %pad_add_fusion.1.refs_0_, bf16[96,4096]{1,0:T(8,128)(2,1)S(1)} %copy-done.1, bf16[96,4096]{1,0:T(8,128)(2,1)S(1)} %collective-permute-done.refs_3_.refs_2_, ...), custom_call_target="tpu_custom_call" | custom-call | flops 201326592 | bytes 3964928 | tf_op jit(solution)/shard_map/pallas_call | solution.py:93
  61.6 1.8 %collective-permute-start.16 = (bf16[128,1024]{1,0:T(8,128)(2,1)S(1)}, bf16[128,1024]{1,0:T(8,128)(2,1)S(1)}, u32[]{:S(2)}, u32[]{:S(2)}) collective-permute-start(bf16[128,1024]{1,0:T(8,128)(2,1)S(1)} %get-tuple-element.57), channel_id=1, source_target_pairs={{0,8},{1,9},{2,10},{3,11},{4,12},{5,13},{6,14},{7,15},{8,0},{9,1},... | collective-permute-start | bytes 786440 | tf_op jit(solution)/shard_map/ppermute | solution.py:366
  64.1 2.0 %collective-permute-start.19 = (bf16[192,128]{1,0:T(8,128)(2,1)S(1)}, bf16[192,128]{1,0:T(8,128)(2,1)S(1)}, u32[]{:S(2)}, u32[]{:S(2)}) collective-permute-start(bf16[192,128]{1,0:T(8,128)(2,1)S(1)} %get-tuple-element.61), channel_id=1, source_target_pairs={{0,3},{1,0},{2,1},{3,2},{4,7},{5,4},{6,5},{7,6},{8,11},{9,8},{10,9... | collective-permute-start | bytes 147464 | tf_op jit(solution)/shard_map/ppermute | solution.py:366
  66.1 2.1 %collective-permute-done.19.refs_3_ = bf16[192,128]{1,0:T(8,128)(2,1)S(1)} collective-permute-done((bf16[192,128]{1,0:T(8,128)(2,1)S(1)}, bf16[192,128]{1,0:T(8,128)(2,1)S(1)}, u32[]{:S(2)}, u32[]{:S(2)}) %collective-permute-start.19) | collective-permute-done | bytes 49184 | tf_op jit(solution)/shard_map/ppermute | solution.py:366
  68.2 3.8 %collective-permute-done.21.refs_5_ = bf16[192,128]{1,0:T(8,128)(2,1)S(1)} collective-permute-done((bf16[192,128]{1,0:T(8,128)(2,1)S(1)}, bf16[192,128]{1,0:T(8,128)(2,1)S(1)}, u32[]{:S(2)}, u32[]{:S(2)}) %collective-permute-start.21) | collective-permute-done | bytes 49184 | tf_op jit(solution)/shard_map/ppermute | solution.py:366
  72.0 2.7 %shard_map.97 = (f32[192,128]{1,0:T(8,128)S(1)}, f32[96,2048]{1,0:T(8,128)S(1)}, f32[96,2048]{1,0:T(8,128)S(1)}) custom-call(s32[3]{0:T(128)S(1)} %pad_add_fusion.1.refs_0_, bf16[96,4096]{1,0:T(8,128)(2,1)S(1)} %copy-done.1, bf16[96,4096]{1,0:T(8,128)(2,1)S(1)} %collective-permute-done.refs_3_.refs_2_, bf16[256,4096]{1,0:T(8,128)(2,1)S(1)} %copy-done, ...), custom_call_target="tpu_custom_call" | custom-call | flops 402653184 | bytes 7110656 | tf_op jit(solution)/shard_map/pallas_call | solution.py:93
  74.8 1.1 %shard_map.100 = bf16[192,128]{1,0:T(8,128)(2,1)S(1)} custom-call(s32[3]{0:T(128)S(1)} %pad_add_fusion.1.refs_0_, bf16[96,4096]{1,0:T(8,128)(2,1)S(1)} %copy-done.1, bf16[96,4096]{1,0:T(8,128)(2,1)S(1)} %collective-permute-done.refs_3_.refs_2_, bf16[128,1024]{1,0:T(8,128)(2,1)S(1)} %collective-permute-done.16.refs_3_.refs_4_, ...), custom_call_target="tpu_custom_call" | custom-call | flops 100663296 | bytes 2244608 | tf_op jit(solution)/shard_map/pallas_call | solution.py:93
  76.6 4.4 %collective-permute-done.23.refs_10_.refs_4_ = bf16[192,128]{1,0:T(8,128)(2,1)S(1)} collective-permute-done((bf16[192,128]{1,0:T(8,128)(2,1)S(1)}, bf16[192,128]{1,0:T(8,128)(2,1)S(1)}, u32[]{:S(2)}, u32[]{:S(2)}) %collective-permute-start.23) | collective-permute-done | bytes 49184 | tf_op jit(solution)/shard_map/ppermute | solution.py:366
  81.0 2.3 %shard_map.101 = (f32[96,2048]{1,0:T(8,128)S(1)}, f32[96,2048]{1,0:T(8,128)S(1)}) custom-call(s32[3]{0:T(128)S(1)} %pad_add_fusion.1.refs_0_, bf16[256,4096]{1,0:T(8,128)(2,1)S(1)} %copy-done, bf16[128,2048]{1,0:T(8,128)(2,1)S(1)} %collective-permute-done.14.refs_3_.refs_2_, bf16[128,2048]{1,0:T(8,128)(2,1)} %collective-permute-done.15.refs_4_.refs_3_, ...), custom_call_target="tpu_custom_call" | custom-call | flops 402653184 | bytes 5439488 | tf_op jit(solution)/shard_map/pallas_call | solution.py:93
  83.8 1.8 %collective-permute-done.25.refs_8_ = bf16[192,128]{1,0:T(8,128)(2,1)S(1)} collective-permute-done((bf16[192,128]{1,0:T(8,128)(2,1)S(1)}, bf16[192,128]{1,0:T(8,128)(2,1)S(1)}, u32[]{:S(2)}, u32[]{:S(2)}) %collective-permute-start.25) | collective-permute-done | bytes 49184 | tf_op jit(solution)/shard_map/ppermute | solution.py:366
  85.7 0.8 shard_map.103
  87.1 0.7 collective-permute-done.27.refs_2_
  87.8 1.5 %collective-permute-start.28 = (f32[128,128]{1,0:T(8,128)S(1)}, f32[128,128]{1,0:T(8,128)S(1)}, u32[]{:S(2)}, u32[]{:S(2)}) collective-permute-start(f32[128,128]{1,0:T(8,128)S(1)} %add.15.refs_10_), channel_id=1, source_target_pairs={{0,8},{1,9},{2,10},{3,11},{4,12},{5,13},{6,14},{7,15},{8,0},{9,1},... | collective-permute-start | bytes 196616 | tf_op jit(solution)/shard_map/ppermute | solution.py:366
  89.9 1.5 %collective-permute-start.30 = (f32[128,128]{1,0:T(8,128)S(1)}, f32[128,128]{1,0:T(8,128)S(1)}, u32[]{:S(2)}, u32[]{:S(2)}) collective-permute-start(f32[128,128]{1,0:T(8,128)S(1)} %add.15.refs_10_), channel_id=1, source_target_pairs={{0,24},{1,25},{2,26},{3,27},{4,28},{5,29},{6,30},{7,31},{8,16},{9,... | collective-permute-start | bytes 196616 | tf_op jit(solution)/shard_map/ppermute | solution.py:366
  91.5 2.9 %shard_map.104 = (bf16[384,256]{1,0:T(8,128)(2,1)}, f32[384,256]{1,0:T(8,128)S(1)}, f32[384,256]{1,0:T(8,128)S(1)}) custom-call(s32[3]{0:T(128)S(1)} %copy-done.33, bf16[384,256]{1,0:T(8,128)(2,1)S(1)} %copy-done.7, bf16[384,256]{1,0:T(8,128)(2,1)S(1)} %copy-done.10, bf16[384,256]{1,0:T(8,128)(2,1)S(1)} %copy-done.13, ...), custom_call_target="tpu_custom_call" | custom-call | flops 528482304 | bytes 3473408 | tf_op jit(solution)/shard_map/pallas_call | solution.py:93
  95.8 1.6 %shard_map.102 = (bf16[96,4096]{1,0:T(8,128)(2,1)}, f32[8,128]{1,0:T(8,128)S(1)}) custom-call(s32[2]{0:T(128)S(1)} %pad_add_fusion.refs_0_, f32[96,2048]{1,0:T(8,128)S(1)} %get-tuple-element.54.refs_1_, f32[96,2048]{1,0:T(8,128)S(1)} %collective-permute-done.13.refs_2_, f32[96,2048]{1,0:T(8,128)S(1)} %get-tuple-element.63.refs_3_, ...), custom_call_target="tpu_custom_call" | custom-call | flops 1 | bytes 3936256 | tf_op jit(solution)/shard_map/pallas_call | solution.py:93
  97.4 1.6 %shard_map.106 = (bf16[384,256]{1,0:T(8,128)(2,1)}, bf16[384,256]{1,0:T(8,128)(2,1)}) custom-call(s32[3]{0:T(128)S(1)} %copy-done.33, bf16[384,256]{1,0:T(8,128)(2,1)S(1)} %copy-done.10, bf16[384,256]{1,0:T(8,128)(2,1)S(1)} %copy-done.13, f32[384,256]{1,0:T(8,128)S(1)} %get-tuple-element.75.refs_6_.refs_3_, f32[384,256]{1,0:T(8,128)S(1)} %get-tuple-element.76.refs_4_, ...), custom_call_target="tpu_custom_call" | custom-call | flops 1 | bytes 1703936 | tf_op jit(solution)/shard_map/pallas_call | solution.py:93
  (114 shorter events, 12.2 us)
Async XLA Ops:
  0.6 12.4 %copy-start.37 = (s32[3,3]{1,0:T(4,128)S(1)}, s32[3,3]{1,0:T(4,128)}, u32[]{:S(2)}) copy-start(s32[3,3]{1,0:T(4,128)} %refs_0_.1) | copy-start | bytes 112
  0.6 7.1 %collective-permute-start = (bf16[96,4096]{1,0:T(8,128)(2,1)}, bf16[96,4096]{1,0:T(8,128)(2,1)S(1)}, u32[]{:S(2)}, u32[]{:S(2)}) collective-permute-start(bf16[96,4096]{1,0:T(8,128)(2,1)} %refs_1_.13), channel_id=1, source_target_pairs={{0,4},{1,5},{2,6},{3,7},{4,0},{5,1},{6,2},{7,3},{8,12},{9,13},{10,... | collective-permute-start | bytes 2359304 | tf_op jit(solution)/shard_map/ppermute | solution.py:366
  3.0 38.4 %collective-permute-start.1 = (bf16[128,2048]{1,0:T(8,128)(2,1)}, bf16[128,2048]{1,0:T(8,128)(2,1)S(1)}, u32[]{:S(2)}, u32[]{:S(2)}) collective-permute-start(bf16[128,2048]{1,0:T(8,128)(2,1)} %dynamic_slice.3), channel_id=1, source_target_pairs={{0,1},{1,2},{2,3},{3,0},{4,5},{5,6},{6,7},{7,4},{8,9},{9,10},{10,1... | collective-permute-start | bytes 1572872 | tf_op jit(solution)/shard_map/ppermute | solution.py:366
  5.6 35.8 %collective-permute-start.2 = (bf16[128,2048]{1,0:T(8,128)(2,1)}, bf16[128,2048]{1,0:T(8,128)(2,1)}, u32[]{:S(2)}, u32[]{:S(2)}) collective-permute-start(bf16[128,2048]{1,0:T(8,128)(2,1)} %dynamic_slice.3), channel_id=1, source_target_pairs={{0,3},{1,0},{2,1},{3,2},{4,7},{5,4},{6,5},{7,6},{8,11},{9,8},{10,9... | collective-permute-start | bytes 1572872 | tf_op jit(solution)/shard_map/ppermute | solution.py:366
  7.7 32.4 %copy-start.32 = (s32[3]{0:T(128)}, s32[3]{0:T(128)S(1)}, u32[]{:S(2)}) copy-start(s32[3]{0:T(128)S(1)} %pad_add_fusion.2.refs_0_.refs_1_) | copy-start | bytes 40
  7.8 42.2 %copy-start = (bf16[256,4096]{1,0:T(8,128)(2,1)S(1)}, bf16[256,4096]{1,0:T(8,128)(2,1)}, u32[]{:S(2)}) copy-start(bf16[256,4096]{1,0:T(8,128)(2,1)} %refs_1_.14) | copy-start | bytes 6291460
  11.1 1.3 %collective-permute-start.3 = (f32[128,128]{1,0:T(8,128)S(1)}, f32[128,128]{1,0:T(8,128)S(1)}, u32[]{:S(2)}, u32[]{:S(2)}) collective-permute-start(f32[128,128]{1,0:T(8,128)S(1)} %get-tuple-element.44), channel_id=1, source_target_pairs={{0,4},{1,5},{2,6},{3,7},{4,0},{5,1},{6,2},{7,3},{8,12},{9,13},{10,... | collective-permute-start | bytes 196616 | tf_op jit(solution)/shard_map/ppermute | solution.py:366
  22.3 10.2 %collective-permute-start.8 = (f32[384,128]{1,0:T(8,128)}, f32[384,128]{1,0:T(8,128)}, u32[]{:S(2)}, u32[]{:S(2)}) collective-permute-start(f32[384,128]{1,0:T(8,128)} %get-tuple-element.47), channel_id=1, source_target_pairs={{0,4},{1,5},{2,6},{3,7},{4,0},{5,1},{6,2},{7,3},{8,12},{9,13},{10,... | collective-permute-start | bytes 589832 | tf_op jit(solution)/shard_map/ppermute | solution.py:366
  22.5 4.6 %collective-permute-start.4 = (f32[128,128]{1,0:T(8,128)}, f32[128,128]{1,0:T(8,128)}, u32[]{:S(2)}, u32[]{:S(2)}) collective-permute-start(f32[128,128]{1,0:T(8,128)} %add.14.refs_5_), channel_id=1, source_target_pairs={{0,8},{1,9},{2,10},{3,11},{4,12},{5,13},{6,14},{7,15},{8,0},{9,1},... | collective-permute-start | bytes 196616 | tf_op jit(solution)/shard_map/ppermute | solution.py:366
  24.1 5.6 %collective-permute-start.5 = (f32[128,128]{1,0:T(8,128)}, f32[128,128]{1,0:T(8,128)}, u32[]{:S(2)}, u32[]{:S(2)}) collective-permute-start(f32[128,128]{1,0:T(8,128)} %add.14.refs_5_), channel_id=1, source_target_pairs={{0,16},{1,17},{2,18},{3,19},{4,20},{5,21},{6,22},{7,23},{8,24},{9,... | collective-permute-start | bytes 196616 | tf_op jit(solution)/shard_map/ppermute | solution.py:366
  27.1 5.4 %collective-permute-start.6 = (f32[128,128]{1,0:T(8,128)}, f32[128,128]{1,0:T(8,128)S(1)}, u32[]{:S(2)}, u32[]{:S(2)}) collective-permute-start(f32[128,128]{1,0:T(8,128)} %add.14.refs_5_), channel_id=1, source_target_pairs={{0,24},{1,25},{2,26},{3,27},{4,28},{5,29},{6,30},{7,31},{8,16},{9,... | collective-permute-start | bytes 196616 | tf_op jit(solution)/shard_map/ppermute | solution.py:366
  29.8 2.7 %collective-permute-start.7 = (bf16[384,128]{1,0:T(8,128)(2,1)}, bf16[384,128]{1,0:T(8,128)(2,1)S(1)}, u32[]{:S(2)}, u32[]{:S(2)}) collective-permute-start(bf16[384,128]{1,0:T(8,128)(2,1)} %copy-done.34), channel_id=1, source_target_pairs={{0,4},{1,5},{2,6},{3,7},{4,0},{5,1},{6,2},{7,3},{8,12},{9,13},{10,... | collective-permute-start | bytes 294920 | tf_op jit(solution)/shard_map/ppermute | solution.py:366
  37.5 6.0 %collective-permute-start.9 = (bf16[192,128]{1,0:T(8,128)(2,1)S(1)}, bf16[192,128]{1,0:T(8,128)(2,1)S(1)}, u32[]{:S(2)}, u32[]{:S(2)}) collective-permute-start(bf16[192,128]{1,0:T(8,128)(2,1)S(1)} %get-tuple-element.48), channel_id=1, source_target_pairs={{0,1},{1,2},{2,3},{3,0},{4,5},{5,6},{6,7},{7,4},{8,9},{9,10},{10,1... | collective-permute-start | bytes 147464 | tf_op jit(solution)/shard_map/ppermute | solution.py:366
  37.5 6.0 %collective-permute-start.10 = (bf16[192,128]{1,0:T(8,128)(2,1)S(1)}, bf16[192,128]{1,0:T(8,128)(2,1)S(1)}, u32[]{:S(2)}, u32[]{:S(2)}) collective-permute-start(bf16[192,128]{1,0:T(8,128)(2,1)S(1)} %get-tuple-element.49), channel_id=1, source_target_pairs={{0,2},{1,3},{2,0},{3,1},{4,6},{5,7},{6,4},{7,5},{8,10},{9,11},{10,... | collective-permute-start | bytes 147464 | tf_op jit(solution)/shard_map/ppermute | solution.py:366
  40.1 4.1 %collective-permute-start.11 = (bf16[192,128]{1,0:T(8,128)(2,1)S(1)}, bf16[192,128]{1,0:T(8,128)(2,1)S(1)}, u32[]{:S(2)}, u32[]{:S(2)}) collective-permute-start(bf16[192,128]{1,0:T(8,128)(2,1)S(1)} %get-tuple-element.50), channel_id=1, source_target_pairs={{0,3},{1,0},{2,1},{3,2},{4,7},{5,4},{6,5},{7,6},{8,11},{9,8},{10,9... | collective-permute-start | bytes 147464 | tf_op jit(solution)/shard_map/ppermute | solution.py:366
  44.8 13.7 %collective-permute-start.12 = (bf16[128,2048]{1,0:T(8,128)(2,1)}, bf16[128,2048]{1,0:T(8,128)(2,1)}, u32[]{:S(2)}, u32[]{:S(2)}) collective-permute-start(bf16[128,2048]{1,0:T(8,128)(2,1)} %get-tuple-element.51.refs_4_), channel_id=1, source_target_pairs={{0,1},{1,2},{2,3},{3,0},{4,5},{5,6},{6,7},{7,4},{8,9},{9,10},{10,1... | collective-permute-start | bytes 1572872 | tf_op jit(solution)/shard_map/ppermute | solution.py:366
  46.6 12.4 %collective-permute-start.14 = (bf16[128,2048]{1,0:T(8,128)(2,1)}, bf16[128,2048]{1,0:T(8,128)(2,1)S(1)}, u32[]{:S(2)}, u32[]{:S(2)}) collective-permute-start(bf16[128,2048]{1,0:T(8,128)(2,1)} %get-tuple-element.51.refs_4_), channel_id=1, source_target_pairs={{0,8},{1,9},{2,10},{3,11},{4,12},{5,13},{6,14},{7,15},{8,0},{9,1},... | collective-permute-start | bytes 1572872 | tf_op jit(solution)/shard_map/ppermute | solution.py:366
  48.3 10.8 %collective-permute-start.15 = (bf16[128,2048]{1,0:T(8,128)(2,1)}, bf16[128,2048]{1,0:T(8,128)(2,1)}, u32[]{:S(2)}, u32[]{:S(2)}) collective-permute-start(bf16[128,2048]{1,0:T(8,128)(2,1)} %get-tuple-element.52.refs_6_.refs_5_), channel_id=1, source_target_pairs={{0,16},{1,17},{2,18},{3,19},{4,20},{5,21},{6,22},{7,23},{8,24},{9,... | collective-permute-start | bytes 1572872 | tf_op jit(solution)/shard_map/ppermute | solution.py:366
  54.8 17.1 %copy-start.4 = (bf16[128,2048]{1,0:T(8,128)(2,1)S(1)}, bf16[128,2048]{1,0:T(8,128)(2,1)}, u32[]{:S(2)}) copy-start(bf16[128,2048]{1,0:T(8,128)(2,1)} %get-tuple-element.51.refs_4_) | copy-start | bytes 1572868
  54.8 17.1 %copy-start.19 = (bf16[192,128]{1,0:T(8,128)(2,1)S(1)}, bf16[192,128]{1,0:T(8,128)(2,1)}, u32[]{:S(2)}) copy-start(bf16[192,128]{1,0:T(8,128)(2,1)} %copy-done.18) | copy-start | bytes 147460
  54.9 17.1 %copy-start.21 = (bf16[192,128]{1,0:T(8,128)(2,1)S(1)}, bf16[192,128]{1,0:T(8,128)(2,1)}, u32[]{:S(2)}) copy-start(bf16[192,128]{1,0:T(8,128)(2,1)} %copy-done.20) | copy-start | bytes 147460
  54.9 17.1 %copy-start.23 = (bf16[192,128]{1,0:T(8,128)(2,1)S(1)}, bf16[192,128]{1,0:T(8,128)(2,1)}, u32[]{:S(2)}) copy-start(bf16[192,128]{1,0:T(8,128)(2,1)} %copy-done.22) | copy-start | bytes 147460
  54.9 17.1 %copy-start.27 = (bf16[192,128]{1,0:T(8,128)(2,1)S(1)}, bf16[192,128]{1,0:T(8,128)(2,1)}, u32[]{:S(2)}) copy-start(bf16[192,128]{1,0:T(8,128)(2,1)} %copy-done.26) | copy-start | bytes 147460
  61.6 13.2 %collective-permute-start.16 = (bf16[128,1024]{1,0:T(8,128)(2,1)S(1)}, bf16[128,1024]{1,0:T(8,128)(2,1)S(1)}, u32[]{:S(2)}, u32[]{:S(2)}) collective-permute-start(bf16[128,1024]{1,0:T(8,128)(2,1)S(1)} %get-tuple-element.57), channel_id=1, source_target_pairs={{0,8},{1,9},{2,10},{3,11},{4,12},{5,13},{6,14},{7,15},{8,0},{9,1},... | collective-permute-start | bytes 786440 | tf_op jit(solution)/shard_map/ppermute | solution.py:366
  63.4 11.4 %collective-permute-start.17 = (bf16[128,1024]{1,0:T(8,128)(2,1)S(1)}, bf16[128,1024]{1,0:T(8,128)(2,1)S(1)}, u32[]{:S(2)}, u32[]{:S(2)}) collective-permute-start(bf16[128,1024]{1,0:T(8,128)(2,1)S(1)} %get-tuple-element.58), channel_id=1, source_target_pairs={{0,16},{1,17},{2,18},{3,19},{4,20},{5,21},{6,22},{7,23},{8,24},{9,... | collective-permute-start | bytes 786440 | tf_op jit(solution)/shard_map/ppermute | solution.py:366
  64.1 4.1 %collective-permute-start.19 = (bf16[192,128]{1,0:T(8,128)(2,1)S(1)}, bf16[192,128]{1,0:T(8,128)(2,1)S(1)}, u32[]{:S(2)}, u32[]{:S(2)}) collective-permute-start(bf16[192,128]{1,0:T(8,128)(2,1)S(1)} %get-tuple-element.61), channel_id=1, source_target_pairs={{0,3},{1,0},{2,1},{3,2},{4,7},{5,4},{6,5},{7,6},{8,11},{9,8},{10,9... | collective-permute-start | bytes 147464 | tf_op jit(solution)/shard_map/ppermute | solution.py:366
  66.1 5.9 %collective-permute-start.21 = (bf16[192,128]{1,0:T(8,128)(2,1)S(1)}, bf16[192,128]{1,0:T(8,128)(2,1)S(1)}, u32[]{:S(2)}, u32[]{:S(2)}) collective-permute-start(bf16[192,128]{1,0:T(8,128)(2,1)S(1)} %get-tuple-element.62), channel_id=1, source_target_pairs={{0,1},{1,2},{2,3},{3,0},{4,5},{5,6},{6,7},{7,4},{8,9},{9,10},{10,1... | collective-permute-start | bytes 147464 | tf_op jit(solution)/shard_map/ppermute | solution.py:366
  66.1 8.6 %collective-permute-start.18 = (bf16[192,128]{1,0:T(8,128)(2,1)S(1)}, bf16[192,128]{1,0:T(8,128)(2,1)S(1)}, u32[]{:S(2)}, u32[]{:S(2)}) collective-permute-start(bf16[192,128]{1,0:T(8,128)(2,1)S(1)} %get-tuple-element.60.refs_2_), channel_id=1, source_target_pairs={{0,4},{1,5},{2,6},{3,7},{4,0},{5,1},{6,2},{7,3},{8,12},{9,13},{10,... | collective-permute-start | bytes 147464 | tf_op jit(solution)/shard_map/ppermute | solution.py:366
  68.2 6.6 %collective-permute-start.20 = (bf16[192,128]{1,0:T(8,128)(2,1)S(1)}, bf16[192,128]{1,0:T(8,128)(2,1)S(1)}, u32[]{:S(2)}, u32[]{:S(2)}) collective-permute-start(bf16[192,128]{1,0:T(8,128)(2,1)S(1)} %collective-permute-done.19.refs_3_), channel_id=1, source_target_pairs={{0,4},{1,5},{2,6},{3,7},{4,0},{5,1},{6,2},{7,3},{8,12},{9,13},{10,... | collective-permute-start | bytes 147464 | tf_op jit(solution)/shard_map/ppermute | solution.py:366
  72.0 2.8 %collective-permute-start.22 = (bf16[192,128]{1,0:T(8,128)(2,1)S(1)}, bf16[192,128]{1,0:T(8,128)(2,1)S(1)}, u32[]{:S(2)}, u32[]{:S(2)}) collective-permute-start(bf16[192,128]{1,0:T(8,128)(2,1)S(1)} %collective-permute-done.21.refs_5_), channel_id=1, source_target_pairs={{0,4},{1,5},{2,6},{3,7},{4,0},{5,1},{6,2},{7,3},{8,12},{9,13},{10,... | collective-permute-start | bytes 147464 | tf_op jit(solution)/shard_map/ppermute | solution.py:366
  75.8 9.9 %copy-start.7 = (bf16[384,256]{1,0:T(8,128)(2,1)S(1)}, bf16[384,256]{1,0:T(8,128)(2,1)}, u32[]{:S(2)}) copy-start(bf16[384,256]{1,0:T(8,128)(2,1)} %refs_1_.16) | copy-start | bytes 589828
  75.9 5.1 %collective-permute-start.23 = (bf16[192,128]{1,0:T(8,128)(2,1)S(1)}, bf16[192,128]{1,0:T(8,128)(2,1)S(1)}, u32[]{:S(2)}, u32[]{:S(2)}) collective-permute-start(bf16[192,128]{1,0:T(8,128)(2,1)S(1)} %shard_map.100), channel_id=1, source_target_pairs={{0,2},{1,3},{2,0},{3,1},{4,6},{5,7},{6,4},{7,5},{8,10},{9,11},{10,... | collective-permute-start | bytes 147464 | tf_op jit(solution)/shard_map/ppermute | solution.py:366
  75.9 10.8 %copy-start.36 = (f32[128,128]{1,0:T(8,128)S(1)}, f32[128,128]{1,0:T(8,128)}, u32[]{:S(2)}) copy-start(f32[128,128]{1,0:T(8,128)} %copy-done.35) | copy-start | bytes 196612
  76.0 15.5 %copy-start.10 = (bf16[384,256]{1,0:T(8,128)(2,1)S(1)}, bf16[384,256]{1,0:T(8,128)(2,1)}, u32[]{:S(2)}) copy-start(bf16[384,256]{1,0:T(8,128)(2,1)} %refs_1_.17) | copy-start | bytes 589828
  76.0 15.5 %copy-start.13 = (bf16[384,256]{1,0:T(8,128)(2,1)S(1)}, bf16[384,256]{1,0:T(8,128)(2,1)}, u32[]{:S(2)}) copy-start(bf16[384,256]{1,0:T(8,128)(2,1)} %refs_2_.7) | copy-start | bytes 589828
  76.0 15.5 %copy-start.15 = (bf16[2,384,384]{2,1,0:T(8,128)(2,1)S(1)}, bf16[2,384,384]{2,1,0:T(8,128)(2,1)}, u32[]{:S(2)}) copy-start(bf16[2,384,384]{2,1,0:T(8,128)(2,1)} %copy-done.14) | copy-start | bytes 1769476
  76.0 15.5 %copy-start.17 = (bf16[2,384,384]{2,1,0:T(8,128)(2,1)S(1)}, bf16[2,384,384]{2,1,0:T(8,128)(2,1)}, u32[]{:S(2)}) copy-start(bf16[2,384,384]{2,1,0:T(8,128)(2,1)} %copy-done.16) | copy-start | bytes 1769476
  76.0 15.5 %copy-start.25 = (f32[384,256]{1,0:T(8,128)S(1)}, f32[384,256]{1,0:T(8,128)}, u32[]{:S(2)}) copy-start(f32[384,256]{1,0:T(8,128)} %copy-done.24) | copy-start | bytes 1179652
  76.0 15.5 %copy-start.31 = (f32[128,128]{1,0:T(8,128)S(1)}, f32[128,128]{1,0:T(8,128)}, u32[]{:S(2)}) copy-start(f32[128,128]{1,0:T(8,128)} %copy-done.30) | copy-start | bytes 196612
  76.0 19.8 %collective-permute-start.13 = (f32[96,2048]{1,0:T(8,128)S(1)}, f32[96,2048]{1,0:T(8,128)S(1)}, u32[]{:S(2)}, u32[]{:S(2)}) collective-permute-start(f32[96,2048]{1,0:T(8,128)S(1)} %get-tuple-element.55), channel_id=1, source_target_pairs={{0,4},{1,5},{2,6},{3,7},{4,0},{5,1},{6,2},{7,3},{8,12},{9,13},{10,... | collective-permute-start | bytes 2359304 | tf_op jit(solution)/shard_map/ppermute | solution.py:366
  83.3 12.5 %collective-permute-start.24 = (f32[96,2048]{1,0:T(8,128)S(1)}, f32[96,2048]{1,0:T(8,128)S(1)}, u32[]{:S(2)}, u32[]{:S(2)}) collective-permute-start(f32[96,2048]{1,0:T(8,128)S(1)} %get-tuple-element.64), channel_id=1, source_target_pairs={{0,4},{1,5},{2,6},{3,7},{4,0},{5,1},{6,2},{7,3},{8,12},{9,13},{10,... | collective-permute-start | bytes 2359304 | tf_op jit(solution)/shard_map/ppermute | solution.py:366
  83.4 2.3 %collective-permute-start.25 = (bf16[192,128]{1,0:T(8,128)(2,1)S(1)}, bf16[192,128]{1,0:T(8,128)(2,1)S(1)}, u32[]{:S(2)}, u32[]{:S(2)}) collective-permute-start(bf16[192,128]{1,0:T(8,128)(2,1)S(1)} %collective-permute-done.23.refs_10_.refs_4_), channel_id=1, source_target_pairs={{0,4},{1,5},{2,6},{3,7},{4,0},{5,1},{6,2},{7,3},{8,12},{9,13},{10,... | collective-permute-start | bytes 147464 | tf_op jit(solution)/shard_map/ppermute | solution.py:366
  86.5 1.3 %collective-permute-start.27 = (f32[128,128]{1,0:T(8,128)S(1)}, f32[128,128]{1,0:T(8,128)S(1)}, u32[]{:S(2)}, u32[]{:S(2)}) collective-permute-start(f32[128,128]{1,0:T(8,128)S(1)} %get-tuple-element.73), channel_id=1, source_target_pairs={{0,4},{1,5},{2,6},{3,7},{4,0},{5,1},{6,2},{7,3},{8,12},{9,13},{10,... | collective-permute-start | bytes 196616 | tf_op jit(solution)/shard_map/ppermute | solution.py:366
  86.7 3.2 %collective-permute-start.26 = (f32[128,128]{1,0:T(8,128)S(1)}, f32[128,128]{1,0:T(8,128)S(1)}, u32[]{:S(2)}, u32[]{:S(2)}) collective-permute-start(f32[128,128]{1,0:T(8,128)S(1)} %copy-done.36), channel_id=1, source_target_pairs={{0,4},{1,5},{2,6},{3,7},{4,0},{5,1},{6,2},{7,3},{8,12},{9,13},{10,... | collective-permute-start | bytes 196616 | tf_op jit(solution)/shard_map/ppermute | solution.py:366
  87.8 6.6 %collective-permute-start.28 = (f32[128,128]{1,0:T(8,128)S(1)}, f32[128,128]{1,0:T(8,128)S(1)}, u32[]{:S(2)}, u32[]{:S(2)}) collective-permute-start(f32[128,128]{1,0:T(8,128)S(1)} %add.15.refs_10_), channel_id=1, source_target_pairs={{0,8},{1,9},{2,10},{3,11},{4,12},{5,13},{6,14},{7,15},{8,0},{9,1},... | collective-permute-start | bytes 196616 | tf_op jit(solution)/shard_map/ppermute | solution.py:366
  89.4 5.1 %collective-permute-start.29 = (f32[128,128]{1,0:T(8,128)S(1)}, f32[128,128]{1,0:T(8,128)S(1)}, u32[]{:S(2)}, u32[]{:S(2)}) collective-permute-start(f32[128,128]{1,0:T(8,128)S(1)} %add.15.refs_10_), channel_id=1, source_target_pairs={{0,16},{1,17},{2,18},{3,19},{4,20},{5,21},{6,22},{7,23},{8,24},{9,... | collective-permute-start | bytes 196616 | tf_op jit(solution)/shard_map/ppermute | solution.py:366
  89.9 5.2 %collective-permute-start.30 = (f32[128,128]{1,0:T(8,128)S(1)}, f32[128,128]{1,0:T(8,128)S(1)}, u32[]{:S(2)}, u32[]{:S(2)}) collective-permute-start(f32[128,128]{1,0:T(8,128)S(1)} %add.15.refs_10_), channel_id=1, source_target_pairs={{0,24},{1,25},{2,26},{3,27},{4,28},{5,29},{6,30},{7,31},{8,16},{9,... | collective-permute-start | bytes 196616 | tf_op jit(solution)/shard_map/ppermute | solution.py:366
  95.6 1.7 %collective-permute-start.31 = (f32[128,128]{1,0:T(8,128)S(1)}, f32[128,128]{1,0:T(8,128)S(1)}, u32[]{:S(2)}, u32[]{:S(2)}) collective-permute-start(f32[128,128]{1,0:T(8,128)S(1)} %get-tuple-element.78), channel_id=1, source_target_pairs={{0,4},{1,5},{2,6},{3,7},{4,0},{5,1},{6,2},{7,3},{8,12},{9,13},{10,... | collective-permute-start | bytes 196616 | tf_op jit(solution)/shard_map/ppermute | solution.py:366
  (22 other events, 29.0 us)

commit v8 on v7

--- a/solution.py
+++ b/solution.py
@@ -50,17 +50,24 @@
     return lambda ref, *_: ref.at[:, first : first + count]
 
 
-def call(body, outs, args, smem=(), after=(), room=8, flops=1):
+def here(*arrays):
+    return [fetch(a.shape, (a, all_of, all_of)) for a in arrays]
+
+
+def call(body, outs, args, smem=(), after=(), room=12):
     arrays, specs, scratch = [], [], []
     for arg in args:
         if isinstance(arg, tuple):
             arrays += [part[0] for part in arg[1]]
-            specs += [pl.BlockSpec(memory_space=pltpu.HBM) for _ in arg[1]]
+            specs += [pl.BlockSpec(memory_space=pl.ANY) for _ in arg[1]]
             scratch.append(pltpu.VMEM(arg[0], arg[1][0][0].dtype))
         else:
             arrays.append(arg)
             specs.append(pl.BlockSpec(memory_space=pltpu.VMEM))
-    copies = sum(len(arg[1]) for arg in args if isinstance(arg, tuple))
+    stored = [len(out) == 3 for out in outs]
+    fetched = len(scratch)
+    scratch += [pltpu.VMEM(out[0], out[1]) for out in outs if len(out) == 3]
+    copies = sum(len(arg[1]) for arg in args if isinstance(arg, tuple)) + sum(stored)
     held = len(scratch)
     if copies:
         scratch.append(pltpu.SemaphoreType.DMA((copies,)))
@@ -86,22 +93,30 @@
             slot += 1
         for copy in started:
             copy.wait()
-        body(*scalars, *given, *results)
-
-    moved = sum(a.size * a.dtype.itemsize for a in arrays)
-    moved += sum(math.prod(s) * jnp.dtype(t).itemsize for s, t in outs)
+        used, slot, targets = len(started), fetched, []
+        for ref, mark in zip(results, stored):
+            targets.append(slots[slot] if mark else ref)
+            slot += mark
+        body(*scalars, *given, *targets)
+        started = []
+        for ref, target, mark in zip(results, targets, stored):
+            if mark:
+                copy = pltpu.make_async_copy(target, ref, slots[held].at[used + len(started)])
+                copy.start()
+                started.append(copy)
+        for copy in started:
+            copy.wait()
+
     return pl.pallas_call(
         kernel,
-        out_shape=[jax.ShapeDtypeStruct(s, t) for s, t in outs],
+        out_shape=[jax.ShapeDtypeStruct(out[0], out[1]) for out in outs],
         in_specs=[pl.BlockSpec(memory_space=pltpu.SMEM) for _ in smem]
         + specs
         + [pl.BlockSpec(memory_space=pl.ANY) for _ in after],
-        out_specs=[pl.BlockSpec(memory_space=pltpu.VMEM) for _ in outs],
+        out_specs=[pl.BlockSpec(memory_space=pl.ANY if m else pltpu.VMEM) for m in stored],
         scratch_shapes=scratch,
         compiler_params=pltpu.CompilerParams(vmem_limit_bytes=room * MIB),
-        cost_estimate=pl.CostEstimate(
-            flops=int(flops), bytes_accessed=int(moved), transcendentals=0
-        ),
+        cost_estimate=pl.CostEstimate(flops=1, bytes_accessed=1, transcendentals=0),
     )(*smem, *arrays, *after)
 
 
@@ -396,10 +411,9 @@
     ctx, place = lax.axis_index("ctx"), lax.axis_index("head")
     core, chip, chips = ctx & 1, ctx >> 1, shards // 2
     where = jnp.stack([place, ctx, core])
-    flat, square = (rows, width), rows * rows * DH * heads
+    flat = (rows, width)
     pair = [((DH, DH), F32)] * 2
     tokens = ((2 * own, DH), BF16)
-    product = 4 * own * DH * model
 
     board = chips == 4 and count == 4
     wide = model // (2 if board else chips)
@@ -411,26 +425,25 @@
     mine, other = call(
         state_kernel,
         pair,
-        [fetch(flat, (a, all_of, all_of)) for a in (key, value)],
+        [*here(key, value)],
         [where],
         [mate_cotangent],
     )
     flags, parts, total = exchange(mine, other, core, chip, chips, False)
     probs, inner, soft, pre, other, far = call(
         functools.partial(forward_kernel, scale),
-        [((heads, rows, rows), BF16)] * 2
-        + [(flat, F32)]
-        + [((rows, DH), F32)] * 2
-        + [((rows, DH), BF16)],
-        [query, key, value],
+        [((heads, rows, rows), BF16, True)] * 2
+        + [(flat, F32, True)]
+        + [((rows, DH), F32, True)] * 2
+        + [((rows, DH), BF16, True)],
+        here(query, key, value),
         [block_mask, where],
         [total],
-        flops=6 * square,
     )
     *attn, keep, back = call(
         functools.partial(attn_kernel, scale, count),
-        [tokens] * count + pair,
-        [*parts, query, send(far, 1, 0), pre, send(other, 1, 0)],
+        [(*tokens, True)] + [tokens] * (count - 1) + [(*kept, True) for kept in pair],
+        [*parts, *here(query, send(far, 1, 0), pre, send(other, 1, 0))],
         [flags, where],
     )
     linear = [keep, send(back, 1, 0)]
@@ -438,44 +451,43 @@
 
     work = near_and_far if board else by_gathers
     both, across, joins, starts = work(
-        attn, arrived, cotangent, mate_cotangent, out_weight, core, chip, colour, product
+        attn, arrived, cotangent, mate_cotangent, out_weight, core, chip, colour
     )
     mixed, done = call(
-        join_kernel, [((own, model), BF16), ((8, DH), F32)], joins, [jnp.stack(starts)]
+        join_kernel, [((own, model), BF16, True), ((8, DH), F32)], here(*joins), [jnp.stack(starts)]
     )
 
     g, mine, other = call(
         functools.partial(collect_kernel, scale, count),
         [(flat, BF16), *pair],
-        [query, *both, *across],
+        [*here(query, *both, *across)],
         [where],
     )
     flags, parts, total = exchange(mine, other, core, chip, chips, True)
     grad_query, dk, dv = call(
         functools.partial(backward_kernel, scale, blocks),
-        [(flat, BF16)] + [(flat, F32)] * 2,
-        [query, key, value, g, probs, inner, soft, *linear],
+        [(flat, BF16, True)] + [(flat, F32)] * 2,
+        [*here(query, key, value), g, *here(probs, inner, soft, *linear)],
         [where],
         [total],
-        flops=14 * square,
     )
     keep, back = call(carry_kernel, pair, parts, [flags], [dk])
     grad_key, grad_value = call(
         close_kernel,
-        [(flat, BF16)] * 2,
-        [key, value, dk, dv, keep, send(back, 1, 0)],
+        [(flat, BF16, True)] * 2,
+        [*here(key, value), dk, dv, keep, send(back, 1, 0)],
         [where],
         [done],
     )
     return mixed, grad_query, grad_key, grad_value
 
 
-def near_and_far(attn, arrived, cotangent, mate_cotangent, weight, core, chip, colour, product):
+def near_and_far(attn, arrived, cotangent, mate_cotangent, weight, core, chip, colour):
     own, model = cotangent.shape
     wide = model // 2
     spots = jnp.stack([colour * wide, (1 - colour) * wide, core * DH])
     tokens = ((2 * own, DH), BF16)
-    parts = [((own, wide), F32)] * 2
+    parts = [((own, wide), F32, True)] * 2
     all_arrays = [(cotangent, all_of, rows_at(0, own)), (mate_cotangent, all_of, rows_at(own, own))]
     whole = fetch((2 * own, model), *all_arrays)
     left = [
@@ -499,15 +511,13 @@
     second = {1: send(arrived[1], 2, 0), 3: send(arrived[3], 4, 0)}
     mine, half = call(
         first_kernel,
-        [tokens, ((2 * own, 2 * DH), F32)],
+        [(*tokens, True), ((2 * own, 2 * DH), F32, True)],
         [
             whole,
             fetch((DH, model), (weight, own_rows, all_of)),
             fetch((2 * DH, wide), *stacked(arrived[1], arrived[3])),
         ],
         [spots],
-        room=24,
-        flops=2 * product,
     )
     one, three, *cuts = call(
         second_kernel,
@@ -515,12 +525,10 @@
         [
             left[1],
             fetch((2 * DH, wide), *stacked(second[1], second[3])),
-            half,
+            *here(half),
             fetch((DH, wide), (arrived[2], all_of, all_of)),
         ],
         [spots],
-        room=16,
-        flops=product,
     )
     second[2] = [send(cuts[0], 2, 0), send(cuts[1], 4, 0)]
     both = {0: mine, 1: send(one, 0, -1), 3: send(three, 0, -3)}
@@ -535,11 +543,9 @@
                 (weight, own_columns(0), rows_at(0, DH)),
                 *((arrived[s], all_of, rows_at(s * DH, DH)) for s in (1, 2, 3)),
             ),
-            *attn,
+            *here(*attn),
         ],
         [spots],
-        room=24,
-        flops=2 * product,
     )
     joins = [part, send(mate_part, 1, 0)]
     quarters = [(a, all_of, columns_at(n * wide // 2, wide // 2)) for n, a in enumerate(second[2])]
@@ -549,8 +555,6 @@
         [left[1], fetch((DH, wide), *quarters), half],
         [spots],
         [across[0], across[1], across[3]],
-        room=16,
-        flops=product // 2,
     )
     both[2] = send(two, 0, -2)
 
@@ -568,19 +572,17 @@
                 (second[3], all_of, rows_at(3 * DH, DH)),
                 *((a, all_of, quarter(n)) for n, a in enumerate(second[2])),
             ),
-            *attn,
+            *here(*attn),
         ],
         [spots],
         [both[2]],
-        room=24,
-        flops=2 * product,
     )
     joins += [part, send(mate_part, 1, 0)]
     across[2] = send(both[2], 1, 0)
     return [both[s] for s in range(4)], [across[s] for s in range(4)], joins, [spots[0], spots[1]]
 
 
-def by_gathers(attn, arrived, cotangent, mate_cotangent, out_weight, core, chip, colour, product):
+def by_gathers(attn, arrived, cotangent, mate_cotangent, out_weight, core, chip, colour):
     own, model = cotangent.shape
     shards, count = lax.axis_size("ctx"), lax.axis_size("head")
     weight = lax.dynamic_slice_in_dim(out_weight, core * DH, DH, 0)
@@ -597,18 +599,16 @@
         (block,) = call(
             functools.partial(grad_kernel, True, 0),
             [((2 * own, DH), BF16)],
-            [cotangent, mate_cotangent, chunks[s]],
+            here(cotangent, mate_cotangent, chunks[s]),
             [zero],
-            flops=product,
-        )
+            )
         both.append(send(block, 0, -s) if s else block)
     part, mate_part = call(
         functools.partial(mixed_kernel, count, [1] * (count - 1)),
-        [((own, model), F32)] * 2,
-        [*attn, *chunks],
+        [((own, model), F32, True)] * 2,
+        here(*attn, *chunks),
         [zero],
-        room=16,
-        flops=count * product,
+        room=40,
     )
     return both, [send(b, 1, 0) for b in both], [part, send(mate_part, 1, 0)], [jnp.int32(0)]
 

time: 99.6 us -> 106 us (1.064)
  Pallas kernels: 24.1 us -> 31.2 us
    pallas_call x13, Pallas kernels: 24 us -> 31.2 us  [call(): pl.pallas_call(kernel, out_shape=[jax.ShapeDtypeStruct(out[0], out[1]) fo...]
  transfers between devices with their start and end apart: 32 -> 32, of which waited for: 14 -> 13; matrix products, arithmetic and copies ran while one was open for 3% -> 3% of each run, Pallas kernels for 19% -> 24%
where the time goes in v8:
time: 106 us; the launch traced here: 105 us
  Pallas kernels  31.2 us (29%)
  starting transfers between devices  30 us (28%)
  waiting for transfers between devices  24.6 us (23%)
  local copies, waits for them, and re-layouts  16.9 us (16%)
  between operations  1.09 us (1%)
    pallas_call x13, Pallas kernels, call(): pl.pallas_call(kernel, out_shape=[jax.ShapeDtypeStruct(out[0], out[1]) fo...  31.2 us
    ppermute x32, starting transfers between devices, send(): return lax.ppermute(x, ('ctx', 'head'), pairs)  30 us
    ppermute x32, waiting for transfers between devices, send(): return lax.ppermute(x, ('ctx', 'head'), pairs)  24.6 us
    unnamed x76, local copies, waits for them, and re-layouts  15.1 us
  transfers between devices with their start and end apart: 32, of which 13 were waited for; matrix products, arithmetic and copies ran while one was open for 3% of the time, Pallas kernels for 24%

profile of v8, /device:TPU:0, one launch (start us, length us, event | category | flops | bytes accessed | tf_op | source)
XLA Modules:
  0.0 104.9 jit_solution(13471672810250836319)
XLA Ops:
  1.2 1.9 %dynamic_slice.3 = bf16[128,2048]{1,0:T(8,128)(2,1)} dynamic-slice(bf16[256,4096]{1,0:T(8,128)(2,1)} %refs_1_.14, s32[]{:T(128)S(6)} %select_n.6, s32[]{:T(128)S(6)} %select_n.7), dynamic_slice_sizes={128,2048} | dynamic-slice | bytes 1048580 | tf_op jit(solution)/shard_map/dynamic_slice | solution.py:421
  3.0 2.6 %collective-permute-start.1 = (bf16[128,2048]{1,0:T(8,128)(2,1)}, bf16[128,2048]{1,0:T(8,128)(2,1)S(1)}, u32[]{:S(2)}, u32[]{:S(2)}) collective-permute-start(bf16[128,2048]{1,0:T(8,128)(2,1)} %dynamic_slice.3), channel_id=1, source_target_pairs={{0,1},{1,2},{2,3},{3,0},{4,5},{5,6},{6,7},{7,4},{8,9},{9,10},{10,1... | collective-permute-start | bytes 1572872 | tf_op jit(solution)/shard_map/ppermute | solution.py:381
  5.6 2.0 %collective-permute-start.2 = (bf16[128,2048]{1,0:T(8,128)(2,1)}, bf16[128,2048]{1,0:T(8,128)(2,1)}, u32[]{:S(2)}, u32[]{:S(2)}) collective-permute-start(bf16[128,2048]{1,0:T(8,128)(2,1)} %dynamic_slice.3), channel_id=1, source_target_pairs={{0,3},{1,0},{2,1},{3,2},{4,7},{5,4},{6,5},{7,6},{8,11},{9,8},{10,9... | collective-permute-start | bytes 1572872 | tf_op jit(solution)/shard_map/ppermute | solution.py:381
  7.8 1.1 %copy-done.8 = bf16[384,256]{1,0:T(8,128)(2,1)S(1)} copy-done((bf16[384,256]{1,0:T(8,128)(2,1)S(1)}, bf16[384,256]{1,0:T(8,128)(2,1)}, u32[]{:S(2)}) %copy-start.8) | copy-done | bytes 196632
  8.8 0.9 copy-done.11
  9.8 1.3 %shard_map.93 = (f32[128,128]{1,0:T(8,128)S(1)}, f32[128,128]{1,0:T(8,128)S(1)}) custom-call(s32[3]{0:T(128)S(1)} %pad_add_fusion.2.refs_0_.refs_1_, bf16[384,256]{1,0:T(8,128)(2,1)S(1)} %copy-done.8, bf16[384,256]{1,0:T(8,128)(2,1)S(1)} %copy-done.11, bf16[96,4096]{1,0:T(8,128)(2,1)S(1)} %collective-permute-done.refs_3_.refs_2_), custom_call_target="tpu_custom_call" | custom-call | flops 1 | bytes 1 | tf_op jit(solution)/shard_map/pallas_call | solution.py:110
  11.3 1.1 %collective-permute-done.3.refs_3_ = f32[128,128]{1,0:T(8,128)S(1)} collective-permute-done((f32[128,128]{1,0:T(8,128)S(1)}, f32[128,128]{1,0:T(8,128)S(1)}, u32[]{:S(2)}, u32[]{:S(2)}) %collective-permute-start.3) | collective-permute-done | bytes 65568 | tf_op jit(solution)/shard_map/ppermute | solution.py:381
  13.0 0.9 copy-done.5
  14.0 0.9 copy-done.9
  14.9 0.9 copy-done.12
  15.8 4.3 %shard_map.94 = (bf16[2,384,384]{2,1,0:T(8,128)(2,1)S(1)}, bf16[2,384,384]{2,1,0:T(8,128)(2,1)S(1)}, f32[384,256]{1,0:T(8,128)S(1)}, f32[384,128]{1,0:T(8,128)S(...) custom-call(s32[3,3]{1,0:T(4,128)S(1)} %copy-done.34, s32[3]{0:T(128)S(1)} %pad_add_fusion.2.refs_0_.refs_1_, ...), custom_call_target="tpu_custom_call" | custom-call | flops 1 | bytes 1 | tf_op jit(solution)/shard_map/pallas_call | solution.py:110
  20.1 0.8 copy-done.14
  20.9 0.8 copy-done.16
  24.0 1.7 %collective-permute-start.4 = (f32[128,128]{1,0:T(8,128)}, f32[128,128]{1,0:T(8,128)}, u32[]{:S(2)}, u32[]{:S(2)}) collective-permute-start(f32[128,128]{1,0:T(8,128)} %add.14.refs_5_), channel_id=1, source_target_pairs={{0,8},{1,9},{2,10},{3,11},{4,12},{5,13},{6,14},{7,15},{8,0},{9,1},... | collective-permute-start | bytes 196616 | tf_op jit(solution)/shard_map/ppermute | solution.py:381
  25.7 1.5 %collective-permute-start.5 = (f32[128,128]{1,0:T(8,128)}, f32[128,128]{1,0:T(8,128)}, u32[]{:S(2)}, u32[]{:S(2)}) collective-permute-start(f32[128,128]{1,0:T(8,128)} %add.14.refs_5_), channel_id=1, source_target_pairs={{0,16},{1,17},{2,18},{3,19},{4,20},{5,21},{6,22},{7,23},{8,24},{9,... | collective-permute-start | bytes 196616 | tf_op jit(solution)/shard_map/ppermute | solution.py:381
  27.2 1.4 %collective-permute-done.4.refs_4_ = f32[128,128]{1,0:T(8,128)} collective-permute-done((f32[128,128]{1,0:T(8,128)}, f32[128,128]{1,0:T(8,128)}, u32[]{:S(2)}, u32[]{:S(2)}) %collective-permute-start.4) | collective-permute-done | bytes 65568 | tf_op jit(solution)/shard_map/ppermute | solution.py:381
  28.6 2.7 %collective-permute-start.6 = (f32[128,128]{1,0:T(8,128)}, f32[128,128]{1,0:T(8,128)S(1)}, u32[]{:S(2)}, u32[]{:S(2)}) collective-permute-start(f32[128,128]{1,0:T(8,128)} %add.14.refs_5_), channel_id=1, source_target_pairs={{0,24},{1,25},{2,26},{3,27},{4,28},{5,29},{6,30},{7,31},{8,16},{9,... | collective-permute-start | bytes 196616 | tf_op jit(solution)/shard_map/ppermute | solution.py:381
  31.4 2.6 %collective-permute-done.6.refs_6_ = f32[128,128]{1,0:T(8,128)S(1)} collective-permute-done((f32[128,128]{1,0:T(8,128)}, f32[128,128]{1,0:T(8,128)S(1)}, u32[]{:S(2)}, u32[]{:S(2)}) %collective-permute-start.6) | collective-permute-done | bytes 65568 | tf_op jit(solution)/shard_map/ppermute | solution.py:381
  34.0 0.9 copy-done.6
  34.9 0.9 copy-done.29
  35.9 3.0 %shard_map.95 = (bf16[192,128]{1,0:T(8,128)(2,1)S(1)}, bf16[192,128]{1,0:T(8,128)(2,1)S(1)}, bf16[192,128]{1,0:T(8,128)(2,1)S(1)}, bf16[192,128]{1,0:T(8,128)(2,...) custom-call(s32[4]{0:T(128)S(1)} %add_convert_fusion.refs_0_, s32[3]{0:T(128)S(1)} %pad_add_fusion.2.refs_0_.refs_1_, ...), custom_call_target="tpu_custom_call" | custom-call | flops 1 | bytes 1 | tf_op jit(solution)/shard_map/pallas_call | solution.py:110
  40.8 2.6 %collective-permute-start.10 = (bf16[192,128]{1,0:T(8,128)(2,1)S(1)}, bf16[192,128]{1,0:T(8,128)(2,1)S(1)}, u32[]{:S(2)}, u32[]{:S(2)}) collective-permute-start(bf16[192,128]{1,0:T(8,128)(2,1)S(1)} %get-tuple-element.49), channel_id=1, source_target_pairs={{0,2},{1,3},{2,0},{3,1},{4,6},{5,7},{6,4},{7,5},{8,10},{9,11},{10,... | collective-permute-start | bytes 147464 | tf_op jit(solution)/shard_map/ppermute | solution.py:381
  43.4 1.4 %collective-permute-start.11 = (bf16[192,128]{1,0:T(8,128)(2,1)S(1)}, bf16[192,128]{1,0:T(8,128)(2,1)S(1)}, u32[]{:S(2)}, u32[]{:S(2)}) collective-permute-start(bf16[192,128]{1,0:T(8,128)(2,1)S(1)} %get-tuple-element.50), channel_id=1, source_target_pairs={{0,3},{1,0},{2,1},{3,2},{4,7},{5,4},{6,5},{7,6},{8,11},{9,8},{10,9... | collective-permute-start | bytes 147464 | tf_op jit(solution)/shard_map/ppermute | solution.py:381
  44.7 2.0 %collective-permute-done.9.refs_2_.refs_8_.refs_7_ = bf16[192,128]{1,0:T(8,128)(2,1)S(1)} collective-permute-done((bf16[192,128]{1,0:T(8,128)(2,1)S(1)}, bf16[192,128]{1,0:T(8,128)(2,1)S(1)}, u32[]{:S(2)}, u32[]{:S(2)}) %collective-permute-start.9) | collective-permute-done | bytes 49184 | tf_op jit(solution)/shard_map/ppermute | solution.py:381
  48.1 1.8 %collective-permute-start.12 = (bf16[128,2048]{1,0:T(8,128)(2,1)}, bf16[128,2048]{1,0:T(8,128)(2,1)}, u32[]{:S(2)}, u32[]{:S(2)}) collective-permute-start(bf16[128,2048]{1,0:T(8,128)(2,1)} %get-tuple-element.51.refs_4_), channel_id=1, source_target_pairs={{0,1},{1,2},{2,3},{3,0},{4,5},{5,6},{6,7},{7,4},{8,9},{9,10},{10,1... | collective-permute-start | bytes 1572872 | tf_op jit(solution)/shard_map/ppermute | solution.py:381
  49.9 1.7 %collective-permute-start.14 = (bf16[128,2048]{1,0:T(8,128)(2,1)}, bf16[128,2048]{1,0:T(8,128)(2,1)S(1)}, u32[]{:S(2)}, u32[]{:S(2)}) collective-permute-start(bf16[128,2048]{1,0:T(8,128)(2,1)} %get-tuple-element.51.refs_4_), channel_id=1, source_target_pairs={{0,8},{1,9},{2,10},{3,11},{4,12},{5,13},{6,14},{7,15},{8,0},{9,1},... | collective-permute-start | bytes 1572872 | tf_op jit(solution)/shard_map/ppermute | solution.py:381
  51.6 1.5 %collective-permute-start.15 = (bf16[128,2048]{1,0:T(8,128)(2,1)}, bf16[128,2048]{1,0:T(8,128)(2,1)}, u32[]{:S(2)}, u32[]{:S(2)}) collective-permute-start(bf16[128,2048]{1,0:T(8,128)(2,1)} %get-tuple-element.52.refs_6_.refs_5_), channel_id=1, source_target_pairs={{0,16},{1,17},{2,18},{3,19},{4,20},{5,21},{6,22},{7,23},{8,24},{9,... | collective-permute-start | bytes 1572872 | tf_op jit(solution)/shard_map/ppermute | solution.py:381
  53.2 1.1 %copy-done.1 = bf16[96,4096]{1,0:T(8,128)(2,1)S(1)} copy-done((bf16[96,4096]{1,0:T(8,128)(2,1)S(1)}, bf16[96,4096]{1,0:T(8,128)(2,1)}, u32[]{:S(2)}) %copy-start.1) | copy-done | bytes 786456
  54.3 1.0 copy-done.3
  55.4 3.0 %shard_map.98 = (bf16[192,128]{1,0:T(8,128)(2,1)S(1)}, f32[192,256]{1,0:T(8,128)S(1)}) custom-call(s32[3]{0:T(128)S(1)} %pad_add_fusion.1.refs_0_, bf16[96,4096]{1,0:T(8,128)(2,1)S(1)} %copy-done.1, bf16[96,4096]{1,0:T(8,128)(2,1)S(1)} %collective-permute-done.refs_3_.refs_2_, bf16[256,4096]{1,0:T(8,128)(2,1)S(1)} %copy-done, ...), custom_call_target="tpu_custom_call" | custom-call | flops 1 | bytes 1 | tf_op jit(solution)/shard_map/pallas_call | solution.py:110
  58.5 3.3 %collective-permute-done.12.refs_5_.refs_6_ = bf16[128,2048]{1,0:T(8,128)(2,1)} collective-permute-done((bf16[128,2048]{1,0:T(8,128)(2,1)}, bf16[128,2048]{1,0:T(8,128)(2,1)}, u32[]{:S(2)}, u32[]{:S(2)}) %collective-permute-start.12) | collective-permute-done | bytes 524320 | tf_op jit(solution)/shard_map/ppermute | solution.py:381
  62.4 2.6 %shard_map.99 = (bf16[192,128]{1,0:T(8,128)(2,1)S(1)}, bf16[192,128]{1,0:T(8,128)(2,1)S(1)}, bf16[128,1024]{1,0:T(8,128)(2,1)S(1)}, bf16[128,1024]{1,0:T(8,128)(2,1)S(1)}) custom-call(s32[3]{0:T(128)S(1)} %pad_add_fusion.1.refs_0_, bf16[96,4096]{1,0:T(8,128)(2,1)S(1)} %copy-done.1, bf16[96,4096]{1,0:T(8,128)(2,1)S(1)} %collective-permute-done.refs_3_.refs_2_, ...), custom_call_target="tpu_custom_call" | custom-call | flops 1 | bytes 1 | tf_op jit(solution)/shard_map/pallas_call | solution.py:110
  65.0 1.8 %collective-permute-start.16 = (bf16[128,1024]{1,0:T(8,128)(2,1)S(1)}, bf16[128,1024]{1,0:T(8,128)(2,1)S(1)}, u32[]{:S(2)}, u32[]{:S(2)}) collective-permute-start(bf16[128,1024]{1,0:T(8,128)(2,1)S(1)} %get-tuple-element.57), channel_id=1, source_target_pairs={{0,8},{1,9},{2,10},{3,11},{4,12},{5,13},{6,14},{7,15},{8,0},{9,1},... | collective-permute-start | bytes 786440 | tf_op jit(solution)/shard_map/ppermute | solution.py:381
  67.1 2.0 %collective-permute-start.19 = (bf16[192,128]{1,0:T(8,128)(2,1)S(1)}, bf16[192,128]{1,0:T(8,128)(2,1)S(1)}, u32[]{:S(2)}, u32[]{:S(2)}) collective-permute-start(bf16[192,128]{1,0:T(8,128)(2,1)S(1)} %get-tuple-element.61), channel_id=1, source_target_pairs={{0,3},{1,0},{2,1},{3,2},{4,7},{5,4},{6,5},{7,6},{8,11},{9,8},{10,9... | collective-permute-start | bytes 147464 | tf_op jit(solution)/shard_map/ppermute | solution.py:381
  69.1 2.1 %collective-permute-done.19.refs_3_ = bf16[192,128]{1,0:T(8,128)(2,1)S(1)} collective-permute-done((bf16[192,128]{1,0:T(8,128)(2,1)S(1)}, bf16[192,128]{1,0:T(8,128)(2,1)S(1)}, u32[]{:S(2)}, u32[]{:S(2)}) %collective-permute-start.19) | collective-permute-done | bytes 49184 | tf_op jit(solution)/shard_map/ppermute | solution.py:381
  71.2 3.8 %collective-permute-done.21.refs_5_ = bf16[192,128]{1,0:T(8,128)(2,1)S(1)} collective-permute-done((bf16[192,128]{1,0:T(8,128)(2,1)S(1)}, bf16[192,128]{1,0:T(8,128)(2,1)S(1)}, u32[]{:S(2)}, u32[]{:S(2)}) %collective-permute-start.21) | collective-permute-done | bytes 49184 | tf_op jit(solution)/shard_map/ppermute | solution.py:381
  75.0 2.9 %shard_map.97 = (f32[192,128]{1,0:T(8,128)S(1)}, f32[96,2048]{1,0:T(8,128)S(1)}, f32[96,2048]{1,0:T(8,128)S(1)}) custom-call(s32[3]{0:T(128)S(1)} %pad_add_fusion.1.refs_0_, bf16[96,4096]{1,0:T(8,128)(2,1)S(1)} %copy-done.1, bf16[96,4096]{1,0:T(8,128)(2,1)S(1)} %collective-permute-done.refs_3_.refs_2_, bf16[256,4096]{1,0:T(8,128)(2,1)S(1)} %copy-done, ...), custom_call_target="tpu_custom_call" | custom-call | flops 1 | bytes 1 | tf_op jit(solution)/shard_map/pallas_call | solution.py:110
  78.0 1.1 %shard_map.100 = bf16[192,128]{1,0:T(8,128)(2,1)S(1)} custom-call(s32[3]{0:T(128)S(1)} %pad_add_fusion.1.refs_0_, bf16[96,4096]{1,0:T(8,128)(2,1)S(1)} %copy-done.1, bf16[96,4096]{1,0:T(8,128)(2,1)S(1)} %collective-permute-done.refs_3_.refs_2_, bf16[128,1024]{1,0:T(8,128)(2,1)S(1)} %collective-permute-done.16.refs_3_.refs_4_, ...), custom_call_target="tpu_custom_call" | custom-call | flops 1 | bytes 1 | tf_op jit(solution)/shard_map/pallas_call | solution.py:110
  79.8 4.4 %collective-permute-done.23.refs_10_.refs_4_ = bf16[192,128]{1,0:T(8,128)(2,1)S(1)} collective-permute-done((bf16[192,128]{1,0:T(8,128)(2,1)S(1)}, bf16[192,128]{1,0:T(8,128)(2,1)S(1)}, u32[]{:S(2)}, u32[]{:S(2)}) %collective-permute-start.23) | collective-permute-done | bytes 49184 | tf_op jit(solution)/shard_map/ppermute | solution.py:381
  84.2 2.5 %shard_map.101 = (f32[96,2048]{1,0:T(8,128)S(1)}, f32[96,2048]{1,0:T(8,128)S(1)}) custom-call(s32[3]{0:T(128)S(1)} %pad_add_fusion.1.refs_0_, bf16[256,4096]{1,0:T(8,128)(2,1)S(1)} %copy-done, bf16[128,2048]{1,0:T(8,128)(2,1)S(1)} %collective-permute-done.14.refs_3_.refs_2_, bf16[128,2048]{1,0:T(8,128)(2,1)} %collective-permute-done.15.refs_4_.refs_3_, ...), custom_call_target="tpu_custom_call" | custom-call | flops 1 | bytes 1 | tf_op jit(solution)/shard_map/pallas_call | solution.py:110
  87.2 1.8 %collective-permute-done.25.refs_8_ = bf16[192,128]{1,0:T(8,128)(2,1)S(1)} collective-permute-done((bf16[192,128]{1,0:T(8,128)(2,1)S(1)}, bf16[192,128]{1,0:T(8,128)(2,1)S(1)}, u32[]{:S(2)}, u32[]{:S(2)}) %collective-permute-start.25) | collective-permute-done | bytes 49184 | tf_op jit(solution)/shard_map/ppermute | solution.py:381
  89.1 1.6 %shard_map.103 = (bf16[384,256]{1,0:T(8,128)(2,1)S(1)}, f32[128,128]{1,0:T(8,128)S(1)}, f32[128,128]{1,0:T(8,128)S(1)}) custom-call(s32[3]{0:T(128)S(1)} %copy-done.33, bf16[384,256]{1,0:T(8,128)(2,1)S(1)} %copy-done.7, bf16[192,128]{1,0:T(8,128)(2,1)S(1)} %get-tuple-element.60.refs_2_, bf16[192,128]{1,0:T(8,128)(2,1)S(1)} %collective-permute-done.19.refs_3_, ...), custom_call_target="tpu_custom_call" | custom-call | flops 1 | bytes 1 | tf_op jit(solution)/shard_map/pallas_call | solution.py:110
  91.3 0.7 collective-permute-done.27.refs_2_
  92.0 1.6 %collective-permute-start.28 = (f32[128,128]{1,0:T(8,128)S(1)}, f32[128,128]{1,0:T(8,128)S(1)}, u32[]{:S(2)}, u32[]{:S(2)}) collective-permute-start(f32[128,128]{1,0:T(8,128)S(1)} %add.15.refs_10_), channel_id=1, source_target_pairs={{0,8},{1,9},{2,10},{3,11},{4,12},{5,13},{6,14},{7,15},{8,0},{9,1},... | collective-permute-start | bytes 196616 | tf_op jit(solution)/shard_map/ppermute | solution.py:381
  94.1 1.5 %collective-permute-start.30 = (f32[128,128]{1,0:T(8,128)S(1)}, f32[128,128]{1,0:T(8,128)S(1)}, u32[]{:S(2)}, u32[]{:S(2)}) collective-permute-start(f32[128,128]{1,0:T(8,128)S(1)} %add.15.refs_10_), channel_id=1, source_target_pairs={{0,24},{1,25},{2,26},{3,27},{4,28},{5,29},{6,30},{7,31},{8,16},{9,... | collective-permute-start | bytes 196616 | tf_op jit(solution)/shard_map/ppermute | solution.py:381
  95.7 4.4 %shard_map.104 = (bf16[384,256]{1,0:T(8,128)(2,1)}, f32[384,256]{1,0:T(8,128)S(1)}, f32[384,256]{1,0:T(8,128)S(1)}) custom-call(s32[3]{0:T(128)S(1)} %copy-done.33, bf16[384,256]{1,0:T(8,128)(2,1)S(1)} %copy-done.7, bf16[384,256]{1,0:T(8,128)(2,1)S(1)} %copy-done.10, bf16[384,256]{1,0:T(8,128)(2,1)S(1)} %copy-done.13, ...), custom_call_target="tpu_custom_call" | custom-call | flops 1 | bytes 1 | tf_op jit(solution)/shard_map/pallas_call | solution.py:110
  100.9 1.8 %shard_map.102 = (bf16[96,4096]{1,0:T(8,128)(2,1)}, f32[8,128]{1,0:T(8,128)S(1)}) custom-call(s32[2]{0:T(128)S(1)} %pad_add_fusion.refs_0_, f32[96,2048]{1,0:T(8,128)S(1)} %get-tuple-element.54.refs_1_, f32[96,2048]{1,0:T(8,128)S(1)} %collective-permute-done.13.refs_2_, f32[96,2048]{1,0:T(8,128)S(1)} %get-tuple-element.63.refs_3_, ...), custom_call_target="tpu_custom_call" | custom-call | flops 1 | bytes 1 | tf_op jit(solution)/shard_map/pallas_call | solution.py:110
  102.7 2.2 %shard_map.106 = (bf16[384,256]{1,0:T(8,128)(2,1)}, bf16[384,256]{1,0:T(8,128)(2,1)}) custom-call(s32[3]{0:T(128)S(1)} %copy-done.33, bf16[384,256]{1,0:T(8,128)(2,1)S(1)} %copy-done.10, bf16[384,256]{1,0:T(8,128)(2,1)S(1)} %copy-done.13, f32[384,256]{1,0:T(8,128)S(1)} %get-tuple-element.75.refs_6_.refs_3_, f32[384,256]{1,0:T(8,128)S(1)} %get-tuple-element.76.refs_4_, ...), custom_call_target="tpu_custom_call" | custom-call | flops 1 | bytes 1 | tf_op jit(solution)/shard_map/pallas_call | solution.py:110
  (114 shorter events, 11.2 us)
Async XLA Ops:
  0.6 12.4 %copy-start.34 = (s32[3,3]{1,0:T(4,128)S(1)}, s32[3,3]{1,0:T(4,128)}, u32[]{:S(2)}) copy-start(s32[3,3]{1,0:T(4,128)} %refs_0_.1) | copy-start | bytes 112
  0.6 7.1 %collective-permute-start = (bf16[96,4096]{1,0:T(8,128)(2,1)}, bf16[96,4096]{1,0:T(8,128)(2,1)S(1)}, u32[]{:S(2)}, u32[]{:S(2)}) collective-permute-start(bf16[96,4096]{1,0:T(8,128)(2,1)} %refs_1_.13), channel_id=1, source_target_pairs={{0,4},{1,5},{2,6},{3,7},{4,0},{5,1},{6,2},{7,3},{8,12},{9,13},{10,... | collective-permute-start | bytes 2359304 | tf_op jit(solution)/shard_map/ppermute | solution.py:381
  3.0 41.7 %collective-permute-start.1 = (bf16[128,2048]{1,0:T(8,128)(2,1)}, bf16[128,2048]{1,0:T(8,128)(2,1)S(1)}, u32[]{:S(2)}, u32[]{:S(2)}) collective-permute-start(bf16[128,2048]{1,0:T(8,128)(2,1)} %dynamic_slice.3), channel_id=1, source_target_pairs={{0,1},{1,2},{2,3},{3,0},{4,5},{5,6},{6,7},{7,4},{8,9},{9,10},{10,1... | collective-permute-start | bytes 1572872 | tf_op jit(solution)/shard_map/ppermute | solution.py:381
  5.6 39.1 %collective-permute-start.2 = (bf16[128,2048]{1,0:T(8,128)(2,1)}, bf16[128,2048]{1,0:T(8,128)(2,1)}, u32[]{:S(2)}, u32[]{:S(2)}) collective-permute-start(bf16[128,2048]{1,0:T(8,128)(2,1)} %dynamic_slice.3), channel_id=1, source_target_pairs={{0,3},{1,0},{2,1},{3,2},{4,7},{5,4},{6,5},{7,6},{8,11},{9,8},{10,9... | collective-permute-start | bytes 1572872 | tf_op jit(solution)/shard_map/ppermute | solution.py:381
  7.7 35.6 %copy-start.32 = (s32[3]{0:T(128)}, s32[3]{0:T(128)S(1)}, u32[]{:S(2)}) copy-start(s32[3]{0:T(128)S(1)} %pad_add_fusion.2.refs_0_.refs_1_) | copy-start | bytes 40
  7.8 45.4 %copy-start = (bf16[256,4096]{1,0:T(8,128)(2,1)S(1)}, bf16[256,4096]{1,0:T(8,128)(2,1)}, u32[]{:S(2)}) copy-start(bf16[256,4096]{1,0:T(8,128)(2,1)} %refs_1_.14) | copy-start | bytes 6291460
  11.1 1.3 %collective-permute-start.3 = (f32[128,128]{1,0:T(8,128)S(1)}, f32[128,128]{1,0:T(8,128)S(1)}, u32[]{:S(2)}, u32[]{:S(2)}) collective-permute-start(f32[128,128]{1,0:T(8,128)S(1)} %get-tuple-element.44), channel_id=1, source_target_pairs={{0,4},{1,5},{2,6},{3,7},{4,0},{5,1},{6,2},{7,3},{8,12},{9,13},{10,... | collective-permute-start | bytes 196616 | tf_op jit(solution)/shard_map/ppermute | solution.py:381
  23.8 10.2 %collective-permute-start.8 = (f32[384,128]{1,0:T(8,128)}, f32[384,128]{1,0:T(8,128)}, u32[]{:S(2)}, u32[]{:S(2)}) collective-permute-start(f32[384,128]{1,0:T(8,128)} %get-tuple-element.47), channel_id=1, source_target_pairs={{0,4},{1,5},{2,6},{3,7},{4,0},{5,1},{6,2},{7,3},{8,12},{9,13},{10,... | collective-permute-start | bytes 589832 | tf_op jit(solution)/shard_map/ppermute | solution.py:381
  24.0 4.6 %collective-permute-start.4 = (f32[128,128]{1,0:T(8,128)}, f32[128,128]{1,0:T(8,128)}, u32[]{:S(2)}, u32[]{:S(2)}) collective-permute-start(f32[128,128]{1,0:T(8,128)} %add.14.refs_5_), channel_id=1, source_target_pairs={{0,8},{1,9},{2,10},{3,11},{4,12},{5,13},{6,14},{7,15},{8,0},{9,1},... | collective-permute-start | bytes 196616 | tf_op jit(solution)/shard_map/ppermute | solution.py:381
  25.7 5.6 %collective-permute-start.5 = (f32[128,128]{1,0:T(8,128)}, f32[128,128]{1,0:T(8,128)}, u32[]{:S(2)}, u32[]{:S(2)}) collective-permute-start(f32[128,128]{1,0:T(8,128)} %add.14.refs_5_), channel_id=1, source_target_pairs={{0,16},{1,17},{2,18},{3,19},{4,20},{5,21},{6,22},{7,23},{8,24},{9,... | collective-permute-start | bytes 196616 | tf_op jit(solution)/shard_map/ppermute | solution.py:381
  28.6 5.4 %collective-permute-start.6 = (f32[128,128]{1,0:T(8,128)}, f32[128,128]{1,0:T(8,128)S(1)}, u32[]{:S(2)}, u32[]{:S(2)}) collective-permute-start(f32[128,128]{1,0:T(8,128)} %add.14.refs_5_), channel_id=1, source_target_pairs={{0,24},{1,25},{2,26},{3,27},{4,28},{5,29},{6,30},{7,31},{8,16},{9,... | collective-permute-start | bytes 196616 | tf_op jit(solution)/shard_map/ppermute | solution.py:381
  31.3 2.7 %collective-permute-start.7 = (bf16[384,128]{1,0:T(8,128)(2,1)}, bf16[384,128]{1,0:T(8,128)(2,1)S(1)}, u32[]{:S(2)}, u32[]{:S(2)}) collective-permute-start(bf16[384,128]{1,0:T(8,128)(2,1)} %copy-done.35), channel_id=1, source_target_pairs={{0,4},{1,5},{2,6},{3,7},{4,0},{5,1},{6,2},{7,3},{8,12},{9,13},{10,... | collective-permute-start | bytes 294920 | tf_op jit(solution)/shard_map/ppermute | solution.py:381
  40.8 6.0 %collective-permute-start.9 = (bf16[192,128]{1,0:T(8,128)(2,1)S(1)}, bf16[192,128]{1,0:T(8,128)(2,1)S(1)}, u32[]{:S(2)}, u32[]{:S(2)}) collective-permute-start(bf16[192,128]{1,0:T(8,128)(2,1)S(1)} %get-tuple-element.48), channel_id=1, source_target_pairs={{0,1},{1,2},{2,3},{3,0},{4,5},{5,6},{6,7},{7,4},{8,9},{9,10},{10,1... | collective-permute-start | bytes 147464 | tf_op jit(solution)/shard_map/ppermute | solution.py:381
  40.8 6.0 %collective-permute-start.10 = (bf16[192,128]{1,0:T(8,128)(2,1)S(1)}, bf16[192,128]{1,0:T(8,128)(2,1)S(1)}, u32[]{:S(2)}, u32[]{:S(2)}) collective-permute-start(bf16[192,128]{1,0:T(8,128)(2,1)S(1)} %get-tuple-element.49), channel_id=1, source_target_pairs={{0,2},{1,3},{2,0},{3,1},{4,6},{5,7},{6,4},{7,5},{8,10},{9,11},{10,... | collective-permute-start | bytes 147464 | tf_op jit(solution)/shard_map/ppermute | solution.py:381
  43.4 4.1 %collective-permute-start.11 = (bf16[192,128]{1,0:T(8,128)(2,1)S(1)}, bf16[192,128]{1,0:T(8,128)(2,1)S(1)}, u32[]{:S(2)}, u32[]{:S(2)}) collective-permute-start(bf16[192,128]{1,0:T(8,128)(2,1)S(1)} %get-tuple-element.50), channel_id=1, source_target_pairs={{0,3},{1,0},{2,1},{3,2},{4,7},{5,4},{6,5},{7,6},{8,11},{9,8},{10,9... | collective-permute-start | bytes 147464 | tf_op jit(solution)/shard_map/ppermute | solution.py:381
  48.1 13.7 %collective-permute-start.12 = (bf16[128,2048]{1,0:T(8,128)(2,1)}, bf16[128,2048]{1,0:T(8,128)(2,1)}, u32[]{:S(2)}, u32[]{:S(2)}) collective-permute-start(bf16[128,2048]{1,0:T(8,128)(2,1)} %get-tuple-element.51.refs_4_), channel_id=1, source_target_pairs={{0,1},{1,2},{2,3},{3,0},{4,5},{5,6},{6,7},{7,4},{8,9},{9,10},{10,1... | collective-permute-start | bytes 1572872 | tf_op jit(solution)/shard_map/ppermute | solution.py:381
  49.9 12.4 %collective-permute-start.14 = (bf16[128,2048]{1,0:T(8,128)(2,1)}, bf16[128,2048]{1,0:T(8,128)(2,1)S(1)}, u32[]{:S(2)}, u32[]{:S(2)}) collective-permute-start(bf16[128,2048]{1,0:T(8,128)(2,1)} %get-tuple-element.51.refs_4_), channel_id=1, source_target_pairs={{0,8},{1,9},{2,10},{3,11},{4,12},{5,13},{6,14},{7,15},{8,0},{9,1},... | collective-permute-start | bytes 1572872 | tf_op jit(solution)/shard_map/ppermute | solution.py:381
  51.6 10.8 %collective-permute-start.15 = (bf16[128,2048]{1,0:T(8,128)(2,1)}, bf16[128,2048]{1,0:T(8,128)(2,1)}, u32[]{:S(2)}, u32[]{:S(2)}) collective-permute-start(bf16[128,2048]{1,0:T(8,128)(2,1)} %get-tuple-element.52.refs_6_.refs_5_), channel_id=1, source_target_pairs={{0,16},{1,17},{2,18},{3,19},{4,20},{5,21},{6,22},{7,23},{8,24},{9,... | collective-permute-start | bytes 1572872 | tf_op jit(solution)/shard_map/ppermute | solution.py:381
  58.4 16.6 %copy-start.4 = (bf16[128,2048]{1,0:T(8,128)(2,1)S(1)}, bf16[128,2048]{1,0:T(8,128)(2,1)}, u32[]{:S(2)}) copy-start(bf16[128,2048]{1,0:T(8,128)(2,1)} %get-tuple-element.51.refs_4_) | copy-start | bytes 1572868
  58.4 16.6 %copy-start.19 = (bf16[192,128]{1,0:T(8,128)(2,1)S(1)}, bf16[192,128]{1,0:T(8,128)(2,1)}, u32[]{:S(2)}) copy-start(bf16[192,128]{1,0:T(8,128)(2,1)} %copy-done.18) | copy-start | bytes 147460
  58.4 16.6 %copy-start.21 = (bf16[192,128]{1,0:T(8,128)(2,1)S(1)}, bf16[192,128]{1,0:T(8,128)(2,1)}, u32[]{:S(2)}) copy-start(bf16[192,128]{1,0:T(8,128)(2,1)} %copy-done.20) | copy-start | bytes 147460
  58.4 16.6 %copy-start.23 = (bf16[192,128]{1,0:T(8,128)(2,1)S(1)}, bf16[192,128]{1,0:T(8,128)(2,1)}, u32[]{:S(2)}) copy-start(bf16[192,128]{1,0:T(8,128)(2,1)} %copy-done.22) | copy-start | bytes 147460
  58.5 16.6 %copy-start.27 = (bf16[192,128]{1,0:T(8,128)(2,1)S(1)}, bf16[192,128]{1,0:T(8,128)(2,1)}, u32[]{:S(2)}) copy-start(bf16[192,128]{1,0:T(8,128)(2,1)} %copy-done.26) | copy-start | bytes 147460
  65.0 13.0 %collective-permute-start.16 = (bf16[128,1024]{1,0:T(8,128)(2,1)S(1)}, bf16[128,1024]{1,0:T(8,128)(2,1)S(1)}, u32[]{:S(2)}, u32[]{:S(2)}) collective-permute-start(bf16[128,1024]{1,0:T(8,128)(2,1)S(1)} %get-tuple-element.57), channel_id=1, source_target_pairs={{0,8},{1,9},{2,10},{3,11},{4,12},{5,13},{6,14},{7,15},{8,0},{9,1},... | collective-permute-start | bytes 786440 | tf_op jit(solution)/shard_map/ppermute | solution.py:381
  66.8 11.2 %collective-permute-start.17 = (bf16[128,1024]{1,0:T(8,128)(2,1)S(1)}, bf16[128,1024]{1,0:T(8,128)(2,1)S(1)}, u32[]{:S(2)}, u32[]{:S(2)}) collective-permute-start(bf16[128,1024]{1,0:T(8,128)(2,1)S(1)} %get-tuple-element.58), channel_id=1, source_target_pairs={{0,16},{1,17},{2,18},{3,19},{4,20},{5,21},{6,22},{7,23},{8,24},{9,... | collective-permute-start | bytes 786440 | tf_op jit(solution)/shard_map/ppermute | solution.py:381
  67.1 4.1 %collective-permute-start.19 = (bf16[192,128]{1,0:T(8,128)(2,1)S(1)}, bf16[192,128]{1,0:T(8,128)(2,1)S(1)}, u32[]{:S(2)}, u32[]{:S(2)}) collective-permute-start(bf16[192,128]{1,0:T(8,128)(2,1)S(1)} %get-tuple-element.61), channel_id=1, source_target_pairs={{0,3},{1,0},{2,1},{3,2},{4,7},{5,4},{6,5},{7,6},{8,11},{9,8},{10,9... | collective-permute-start | bytes 147464 | tf_op jit(solution)/shard_map/ppermute | solution.py:381
  69.1 5.9 %collective-permute-start.21 = (bf16[192,128]{1,0:T(8,128)(2,1)S(1)}, bf16[192,128]{1,0:T(8,128)(2,1)S(1)}, u32[]{:S(2)}, u32[]{:S(2)}) collective-permute-start(bf16[192,128]{1,0:T(8,128)(2,1)S(1)} %get-tuple-element.62), channel_id=1, source_target_pairs={{0,1},{1,2},{2,3},{3,0},{4,5},{5,6},{6,7},{7,4},{8,9},{9,10},{10,1... | collective-permute-start | bytes 147464 | tf_op jit(solution)/shard_map/ppermute | solution.py:381
  69.1 8.8 %collective-permute-start.18 = (bf16[192,128]{1,0:T(8,128)(2,1)S(1)}, bf16[192,128]{1,0:T(8,128)(2,1)S(1)}, u32[]{:S(2)}, u32[]{:S(2)}) collective-permute-start(bf16[192,128]{1,0:T(8,128)(2,1)S(1)} %get-tuple-element.60.refs_2_), channel_id=1, source_target_pairs={{0,4},{1,5},{2,6},{3,7},{4,0},{5,1},{6,2},{7,3},{8,12},{9,13},{10,... | collective-permute-start | bytes 147464 | tf_op jit(solution)/shard_map/ppermute | solution.py:381
  71.2 6.7 %collective-permute-start.20 = (bf16[192,128]{1,0:T(8,128)(2,1)S(1)}, bf16[192,128]{1,0:T(8,128)(2,1)S(1)}, u32[]{:S(2)}, u32[]{:S(2)}) collective-permute-start(bf16[192,128]{1,0:T(8,128)(2,1)S(1)} %collective-permute-done.19.refs_3_), channel_id=1, source_target_pairs={{0,4},{1,5},{2,6},{3,7},{4,0},{5,1},{6,2},{7,3},{8,12},{9,13},{10,... | collective-permute-start | bytes 147464 | tf_op jit(solution)/shard_map/ppermute | solution.py:381
  75.0 3.0 %collective-permute-start.22 = (bf16[192,128]{1,0:T(8,128)(2,1)S(1)}, bf16[192,128]{1,0:T(8,128)(2,1)S(1)}, u32[]{:S(2)}, u32[]{:S(2)}) collective-permute-start(bf16[192,128]{1,0:T(8,128)(2,1)S(1)} %collective-permute-done.21.refs_5_), channel_id=1, source_target_pairs={{0,4},{1,5},{2,6},{3,7},{4,0},{5,1},{6,2},{7,3},{8,12},{9,13},{10,... | collective-permute-start | bytes 147464 | tf_op jit(solution)/shard_map/ppermute | solution.py:381
  79.0 10.0 %copy-start.7 = (bf16[384,256]{1,0:T(8,128)(2,1)S(1)}, bf16[384,256]{1,0:T(8,128)(2,1)}, u32[]{:S(2)}) copy-start(bf16[384,256]{1,0:T(8,128)(2,1)} %refs_1_.16) | copy-start | bytes 589828
  79.0 5.1 %collective-permute-start.23 = (bf16[192,128]{1,0:T(8,128)(2,1)S(1)}, bf16[192,128]{1,0:T(8,128)(2,1)S(1)}, u32[]{:S(2)}, u32[]{:S(2)}) collective-permute-start(bf16[192,128]{1,0:T(8,128)(2,1)S(1)} %shard_map.100), channel_id=1, source_target_pairs={{0,2},{1,3},{2,0},{3,1},{4,6},{5,7},{6,4},{7,5},{8,10},{9,11},{10,... | collective-permute-start | bytes 147464 | tf_op jit(solution)/shard_map/ppermute | solution.py:381
  79.1 11.8 %copy-start.37 = (f32[128,128]{1,0:T(8,128)S(1)}, f32[128,128]{1,0:T(8,128)}, u32[]{:S(2)}) copy-start(f32[128,128]{1,0:T(8,128)} %copy-done.36) | copy-start | bytes 196612
  79.1 16.5 %copy-start.10 = (bf16[384,256]{1,0:T(8,128)(2,1)S(1)}, bf16[384,256]{1,0:T(8,128)(2,1)}, u32[]{:S(2)}) copy-start(bf16[384,256]{1,0:T(8,128)(2,1)} %refs_1_.17) | copy-start | bytes 589828
  79.2 16.5 %copy-start.13 = (bf16[384,256]{1,0:T(8,128)(2,1)S(1)}, bf16[384,256]{1,0:T(8,128)(2,1)}, u32[]{:S(2)}) copy-start(bf16[384,256]{1,0:T(8,128)(2,1)} %refs_2_.7) | copy-start | bytes 589828
  79.2 16.5 %copy-start.15 = (bf16[2,384,384]{2,1,0:T(8,128)(2,1)S(1)}, bf16[2,384,384]{2,1,0:T(8,128)(2,1)}, u32[]{:S(2)}) copy-start(bf16[2,384,384]{2,1,0:T(8,128)(2,1)} %copy-done.14) | copy-start | bytes 1769476
  79.2 16.5 %copy-start.17 = (bf16[2,384,384]{2,1,0:T(8,128)(2,1)S(1)}, bf16[2,384,384]{2,1,0:T(8,128)(2,1)}, u32[]{:S(2)}) copy-start(bf16[2,384,384]{2,1,0:T(8,128)(2,1)} %copy-done.16) | copy-start | bytes 1769476
  79.2 16.5 %copy-start.25 = (f32[384,256]{1,0:T(8,128)S(1)}, f32[384,256]{1,0:T(8,128)}, u32[]{:S(2)}) copy-start(f32[384,256]{1,0:T(8,128)} %copy-done.24) | copy-start | bytes 1179652
  79.2 16.5 %copy-start.31 = (f32[128,128]{1,0:T(8,128)S(1)}, f32[128,128]{1,0:T(8,128)}, u32[]{:S(2)}) copy-start(f32[128,128]{1,0:T(8,128)} %copy-done.30) | copy-start | bytes 196612
  79.2 21.6 %collective-permute-start.13 = (f32[96,2048]{1,0:T(8,128)S(1)}, f32[96,2048]{1,0:T(8,128)S(1)}, u32[]{:S(2)}, u32[]{:S(2)}) collective-permute-start(f32[96,2048]{1,0:T(8,128)S(1)} %get-tuple-element.55), channel_id=1, source_target_pairs={{0,4},{1,5},{2,6},{3,7},{4,0},{5,1},{6,2},{7,3},{8,12},{9,13},{10,... | collective-permute-start | bytes 2359304 | tf_op jit(solution)/shard_map/ppermute | solution.py:381
  86.6 14.2 %collective-permute-start.24 = (f32[96,2048]{1,0:T(8,128)S(1)}, f32[96,2048]{1,0:T(8,128)S(1)}, u32[]{:S(2)}, u32[]{:S(2)}) collective-permute-start(f32[96,2048]{1,0:T(8,128)S(1)} %get-tuple-element.64), channel_id=1, source_target_pairs={{0,4},{1,5},{2,6},{3,7},{4,0},{5,1},{6,2},{7,3},{8,12},{9,13},{10,... | collective-permute-start | bytes 2359304 | tf_op jit(solution)/shard_map/ppermute | solution.py:381
  86.7 2.3 %collective-permute-start.25 = (bf16[192,128]{1,0:T(8,128)(2,1)S(1)}, bf16[192,128]{1,0:T(8,128)(2,1)S(1)}, u32[]{:S(2)}, u32[]{:S(2)}) collective-permute-start(bf16[192,128]{1,0:T(8,128)(2,1)S(1)} %collective-permute-done.23.refs_10_.refs_4_), channel_id=1, source_target_pairs={{0,4},{1,5},{2,6},{3,7},{4,0},{5,1},{6,2},{7,3},{8,12},{9,13},{10,... | collective-permute-start | bytes 147464 | tf_op jit(solution)/shard_map/ppermute | solution.py:381
  90.7 1.3 %collective-permute-start.27 = (f32[128,128]{1,0:T(8,128)S(1)}, f32[128,128]{1,0:T(8,128)S(1)}, u32[]{:S(2)}, u32[]{:S(2)}) collective-permute-start(f32[128,128]{1,0:T(8,128)S(1)} %get-tuple-element.73), channel_id=1, source_target_pairs={{0,4},{1,5},{2,6},{3,7},{4,0},{5,1},{6,2},{7,3},{8,12},{9,13},{10,... | collective-permute-start | bytes 196616 | tf_op jit(solution)/shard_map/ppermute | solution.py:381
  90.9 3.2 %collective-permute-start.26 = (f32[128,128]{1,0:T(8,128)S(1)}, f32[128,128]{1,0:T(8,128)S(1)}, u32[]{:S(2)}, u32[]{:S(2)}) collective-permute-start(f32[128,128]{1,0:T(8,128)S(1)} %copy-done.37), channel_id=1, source_target_pairs={{0,4},{1,5},{2,6},{3,7},{4,0},{5,1},{6,2},{7,3},{8,12},{9,13},{10,... | collective-permute-start | bytes 196616 | tf_op jit(solution)/shard_map/ppermute | solution.py:381
  92.0 8.0 %collective-permute-start.28 = (f32[128,128]{1,0:T(8,128)S(1)}, f32[128,128]{1,0:T(8,128)S(1)}, u32[]{:S(2)}, u32[]{:S(2)}) collective-permute-start(f32[128,128]{1,0:T(8,128)S(1)} %add.15.refs_10_), channel_id=1, source_target_pairs={{0,8},{1,9},{2,10},{3,11},{4,12},{5,13},{6,14},{7,15},{8,0},{9,1},... | collective-permute-start | bytes 196616 | tf_op jit(solution)/shard_map/ppermute | solution.py:381
  93.6 6.5 %collective-permute-start.29 = (f32[128,128]{1,0:T(8,128)S(1)}, f32[128,128]{1,0:T(8,128)S(1)}, u32[]{:S(2)}, u32[]{:S(2)}) collective-permute-start(f32[128,128]{1,0:T(8,128)S(1)} %add.15.refs_10_), channel_id=1, source_target_pairs={{0,16},{1,17},{2,18},{3,19},{4,20},{5,21},{6,22},{7,23},{8,24},{9,... | collective-permute-start | bytes 196616 | tf_op jit(solution)/shard_map/ppermute | solution.py:381
  94.1 6.0 %collective-permute-start.30 = (f32[128,128]{1,0:T(8,128)S(1)}, f32[128,128]{1,0:T(8,128)S(1)}, u32[]{:S(2)}, u32[]{:S(2)}) collective-permute-start(f32[128,128]{1,0:T(8,128)S(1)} %add.15.refs_10_), channel_id=1, source_target_pairs={{0,24},{1,25},{2,26},{3,27},{4,28},{5,29},{6,30},{7,31},{8,16},{9,... | collective-permute-start | bytes 196616 | tf_op jit(solution)/shard_map/ppermute | solution.py:381
  100.7 2.0 %collective-permute-start.31 = (f32[128,128]{1,0:T(8,128)S(1)}, f32[128,128]{1,0:T(8,128)S(1)}, u32[]{:S(2)}, u32[]{:S(2)}) collective-permute-start(f32[128,128]{1,0:T(8,128)S(1)} %get-tuple-element.78), channel_id=1, source_target_pairs={{0,4},{1,5},{2,6},{3,7},{4,0},{5,1},{6,2},{7,3},{8,12},{9,13},{10,... | collective-permute-start | bytes 196616 | tf_op jit(solution)/shard_map/ppermute | solution.py:381
  (22 other events, 29.1 us)

commit v9 on v7

--- a/solution.py
+++ b/solution.py
@@ -136,7 +136,12 @@
     mine_ref,
     other_ref,
     far_ref,
+    mine_state_ref,
+    other_state_ref,
 ):
+    heads = [slice(h * DH, (h + 1) * DH) for h in range(2)]
+    states = [dot(k_ref[:, cols], v_ref[:, cols], TN) for cols in heads]
+    mine_state_ref[...], other_state_ref[...] = pick(where[2], states)
     rows, width = q_ref.shape
     count = mask.shape[0]
     blk = rows // count
@@ -176,12 +181,6 @@
 def both_heads(core, mine_ref, other_ref):
     mine, other = mine_ref[...], other_ref[...]
     return jnp.where(core == 0, mine, other), jnp.where(core == 0, other, mine)
-
-
-def state_kernel(where, k_ref, v_ref, mine_ref, other_ref):
-    heads = [slice(h * DH, (h + 1) * DH) for h in range(2)]
-    parts = [dot(k_ref[:, cols], v_ref[:, cols], TN) for cols in heads]
-    mine_ref[...], other_ref[...] = pick(where[2], parts)
 
 
 def carry(flags, here_ref, got_ref, totals):
@@ -408,29 +407,23 @@
     arrived = {1: send(piece, 0, 1), count - 1: send(piece, 0, -1)}
     mate_cotangent = send(cotangent, 1, 0)
 
-    mine, other = call(
-        state_kernel,
-        pair,
-        [fetch(flat, (a, all_of, all_of)) for a in (key, value)],
-        [where],
-        [mate_cotangent],
-    )
-    flags, parts, total = exchange(mine, other, core, chip, chips, False)
-    probs, inner, soft, pre, other, far = call(
+    probs, inner, soft, pre, other_pre, far, mine, other = call(
         functools.partial(forward_kernel, scale),
         [((heads, rows, rows), BF16)] * 2
         + [(flat, F32)]
         + [((rows, DH), F32)] * 2
-        + [((rows, DH), BF16)],
+        + [((rows, DH), BF16)]
+        + pair,
         [query, key, value],
         [block_mask, where],
-        [total],
-        flops=6 * square,
-    )
+        [mate_cotangent],
+        flops=7 * square,
+    )
+    flags, parts, total = exchange(mine, other, core, chip, chips, False)
     *attn, keep, back = call(
         functools.partial(attn_kernel, scale, count),
         [tokens] * count + pair,
-        [*parts, query, send(far, 1, 0), pre, send(other, 1, 0)],
+        [*parts, query, send(far, 1, 0), pre, send(other_pre, 1, 0)],
         [flags, where],
     )
     linear = [keep, send(back, 1, 0)]
@@ -494,7 +487,7 @@
     def stacked(*arrays):
         return [(a, all_of, rows_at(n * DH, DH)) for n, a in enumerate(arrays)]
 
-    arrived[1], arrived[3] = hold([arrived[1], arrived[3]], attn[1:])
+    arrived[1], arrived[3] = hold([arrived[1], arrived[3]], attn[:1])
     arrived[2] = send(arrived[1], 0, 1)
     second = {1: send(arrived[1], 2, 0), 3: send(arrived[3], 4, 0)}
     mine, half = call(
@@ -519,6 +512,7 @@
             fetch((DH, wide), (arrived[2], all_of, all_of)),
         ],
         [spots],
+        attn[1:],
         room=16,
         flops=product,
     )
@@ -548,7 +542,7 @@
         [tokens],
         [left[1], fetch((DH, wide), *quarters), half],
         [spots],
-        [across[0], across[1], across[3]],
+        [both[1], both[3]],
         room=16,
         flops=product // 2,
     )
@@ -571,7 +565,7 @@
             *attn,
         ],
         [spots],
-        [both[2]],
+        [both[2], across[0], across[1], across[3]],
         room=24,
         flops=2 * product,
     )

time: 99.6 us -> 95.9 us (0.963)
  waiting for transfers between devices: 25.6 us -> 22.3 us
  Pallas kernels: 24.1 us -> 22.8 us
    ppermute x32, waiting for transfers between devices: 25.6 us -> 22.3 us  [send(): return lax.ppermute(x, ('ctx', 'head'), pairs)]
    pallas_call x13 -> x12, Pallas kernels: 24 us -> 22.8 us  [call(): pl.pallas_call(kernel, out_shape=[jax.ShapeDtypeStruct(s, t) for s, t in...]
    unnamed x76 -> x60, local copies, waits for them, and re-layouts: 15.1 us -> 15.2 us
  transfers between devices with their start and end apart: 32 -> 32, of which waited for: 14 -> 8; matrix products, arithmetic and copies ran while one was open for 3% -> 3% of each run, Pallas kernels for 19% -> 20%
where the time goes in v9:
time: 95.9 us; the launch traced here: 95.3 us
  starting transfers between devices  31.2 us (33%)
  Pallas kernels  22.8 us (24%)
  waiting for transfers between devices  22.3 us (23%)
  local copies, waits for them, and re-layouts  17.1 us (18%)
  other arithmetic  1.02 us (1%)
    ppermute x32, starting transfers between devices, send(): return lax.ppermute(x, ('ctx', 'head'), pairs)  31.2 us
    pallas_call x12, Pallas kernels, call(): pl.pallas_call(kernel, out_shape=[jax.ShapeDtypeStruct(s, t) for s, t in...  22.8 us
    ppermute x32, waiting for transfers between devices, send(): return lax.ppermute(x, ('ctx', 'head'), pairs)  22.3 us
    unnamed x60, local copies, waits for them, and re-layouts  15.2 us
  transfers between devices with their start and end apart: 32, of which 8 were waited for; matrix products, arithmetic and copies ran while one was open for 3% of the time, Pallas kernels for 20%

profile of v9, /device:TPU:0, one launch (start us, length us, event | category | flops | bytes accessed | tf_op | source)
XLA Modules:
  0.0 95.3 jit_solution(14730381911299978216)
XLA Ops:
  1.1 1.9 %dynamic_slice.3 = bf16[128,2048]{1,0:T(8,128)(2,1)} dynamic-slice(bf16[256,4096]{1,0:T(8,128)(2,1)} %refs_1_.12, s32[]{:T(128)S(6)} %select_n.6, s32[]{:T(128)S(6)} %select_n.7), dynamic_slice_sizes={128,2048} | dynamic-slice | bytes 1048580 | tf_op jit(solution)/shard_map/dynamic_slice | solution.py:406
  3.0 2.6 %collective-permute-start.1 = (bf16[128,2048]{1,0:T(8,128)(2,1)}, bf16[128,2048]{1,0:T(8,128)(2,1)S(1)}, u32[]{:S(2)}, u32[]{:S(2)}) collective-permute-start(bf16[128,2048]{1,0:T(8,128)(2,1)} %dynamic_slice.3), channel_id=1, source_target_pairs={{0,1},{1,2},{2,3},{3,0},{4,5},{5,6},{6,7},{7,4},{8,9},{9,10},{10,1... | collective-permute-start | bytes 1572872 | tf_op jit(solution)/shard_map/ppermute | solution.py:365
  5.6 2.0 %collective-permute-start.2 = (bf16[128,2048]{1,0:T(8,128)(2,1)}, bf16[128,2048]{1,0:T(8,128)(2,1)}, u32[]{:S(2)}, u32[]{:S(2)}) collective-permute-start(bf16[128,2048]{1,0:T(8,128)(2,1)} %dynamic_slice.3), channel_id=1, source_target_pairs={{0,3},{1,0},{2,1},{3,2},{4,7},{5,4},{6,5},{7,6},{8,11},{9,8},{10,9... | collective-permute-start | bytes 1572872 | tf_op jit(solution)/shard_map/ppermute | solution.py:365
  7.8 0.9 copy-done.5
  8.7 0.9 copy-done.8
  9.6 0.9 copy-done.10
  10.5 0.7 copy-done.24
  11.2 2.8 %shard_map.93 = (bf16[2,384,384]{2,1,0:T(8,128)(2,1)S(1)}, bf16[2,384,384]{2,1,0:T(8,128)(2,1)S(1)}, f32[384,256]{1,0:T(8,128)S(1)}, f32[384,128]{1,0:T(8,128)S(...) custom-call(s32[3,3]{1,0:T(4,128)S(1)} %copy-done.24, ...), custom_call_target="tpu_custom_call" | custom-call | flops 264241152 | bytes 2785280 | tf_op jit(solution)/shard_map/pallas_call | solution.py:93
  14.0 0.8 copy-done.12
  14.8 0.9 copy-done.14
  15.7 0.8 copy-done.18
  16.4 0.7 copy-done.20
  19.0 1.8 %collective-permute-start.4 = (f32[128,128]{1,0:T(8,128)}, f32[128,128]{1,0:T(8,128)}, u32[]{:S(2)}, u32[]{:S(2)}) collective-permute-start(f32[128,128]{1,0:T(8,128)} %add.14), channel_id=1, source_target_pairs={{0,8},{1,9},{2,10},{3,11},{4,12},{5,13},{6,14},{7,15},{8,0},{9,1},... | collective-permute-start | bytes 196616 | tf_op jit(solution)/shard_map/ppermute | solution.py:365
  20.8 1.5 %collective-permute-start.5 = (f32[128,128]{1,0:T(8,128)}, f32[128,128]{1,0:T(8,128)S(1)}, u32[]{:S(2)}, u32[]{:S(2)}) collective-permute-start(f32[128,128]{1,0:T(8,128)} %add.14), channel_id=1, source_target_pairs={{0,16},{1,17},{2,18},{3,19},{4,20},{5,21},{6,22},{7,23},{8,24},{9,... | collective-permute-start | bytes 196616 | tf_op jit(solution)/shard_map/ppermute | solution.py:365
  22.3 1.3 %collective-permute-done.4.refs_4_ = f32[128,128]{1,0:T(8,128)} collective-permute-done((f32[128,128]{1,0:T(8,128)}, f32[128,128]{1,0:T(8,128)}, u32[]{:S(2)}, u32[]{:S(2)}) %collective-permute-start.4) | collective-permute-done | bytes 65568 | tf_op jit(solution)/shard_map/ppermute | solution.py:365
  23.6 2.7 %collective-permute-start.6 = (f32[128,128]{1,0:T(8,128)}, f32[128,128]{1,0:T(8,128)S(1)}, u32[]{:S(2)}, u32[]{:S(2)}) collective-permute-start(f32[128,128]{1,0:T(8,128)} %add.14), channel_id=1, source_target_pairs={{0,24},{1,25},{2,26},{3,27},{4,28},{5,29},{6,30},{7,31},{8,16},{9,... | collective-permute-start | bytes 196616 | tf_op jit(solution)/shard_map/ppermute | solution.py:365
  26.4 2.6 %collective-permute-done.6.refs_6_ = f32[128,128]{1,0:T(8,128)S(1)} collective-permute-done((f32[128,128]{1,0:T(8,128)}, f32[128,128]{1,0:T(8,128)S(1)}, u32[]{:S(2)}, u32[]{:S(2)}) %collective-permute-start.6) | collective-permute-done | bytes 65568 | tf_op jit(solution)/shard_map/ppermute | solution.py:365
  29.0 0.9 copy-done.6
  29.9 0.9 copy-done.21
  30.8 1.3 %shard_map.94 = (bf16[192,128]{1,0:T(8,128)(2,1)S(1)}, bf16[192,128]{1,0:T(8,128)(2,1)S(1)}, bf16[192,128]{1,0:T(8,128)(2,1)S(1)}, bf16[192,128]{1,0:T(8,128)(2,...) custom-call(s32[4]{0:T(128)S(1)} %add_convert_fusion.refs_0_, s32[3]{0:T(128)S(1)} %pad_add_fusion.2.refs_1_.refs_0_, ...), custom_call_target="tpu_custom_call" | custom-call | flops 1 | bytes 1343488 | tf_op jit(solution)/shard_map/pallas_call | solution.py:93
  32.8 0.6 copy-done.22
  35.9 0.8 copy-done.2
  36.8 1.7 %collective-permute-start.14 = (bf16[128,2048]{1,0:T(8,128)(2,1)}, bf16[128,2048]{1,0:T(8,128)(2,1)S(1)}, u32[]{:S(2)}, u32[]{:S(2)}) collective-permute-start(bf16[128,2048]{1,0:T(8,128)(2,1)} %get-tuple-element.49.refs_4_), channel_id=1, source_target_pairs={{0,8},{1,9},{2,10},{3,11},{4,12},{5,13},{6,14},{7,15},{8,0},{9,1},... | collective-permute-start | bytes 1572872 | tf_op jit(solution)/shard_map/ppermute | solution.py:365
  38.5 1.5 %collective-permute-start.15 = (bf16[128,2048]{1,0:T(8,128)(2,1)}, bf16[128,2048]{1,0:T(8,128)(2,1)}, u32[]{:S(2)}, u32[]{:S(2)}) collective-permute-start(bf16[128,2048]{1,0:T(8,128)(2,1)} %get-tuple-element.50.refs_6_.refs_5_), channel_id=1, source_target_pairs={{0,16},{1,17},{2,18},{3,19},{4,20},{5,21},{6,22},{7,23},{8,24},{9,... | collective-permute-start | bytes 1572872 | tf_op jit(solution)/shard_map/ppermute | solution.py:365
  40.0 1.3 %collective-permute-start.10 = (bf16[192,128]{1,0:T(8,128)(2,1)}, bf16[192,128]{1,0:T(8,128)(2,1)S(1)}, u32[]{:S(2)}, u32[]{:S(2)}) collective-permute-start(bf16[192,128]{1,0:T(8,128)(2,1)} %copy-done.29), channel_id=1, source_target_pairs={{0,1},{1,2},{2,3},{3,0},{4,5},{5,6},{6,7},{7,4},{8,9},{9,10},{10,1... | collective-permute-start | bytes 147464 | tf_op jit(solution)/shard_map/ppermute | solution.py:365
  41.3 3.0 %collective-permute-start.11 = (bf16[192,128]{1,0:T(8,128)(2,1)}, bf16[192,128]{1,0:T(8,128)(2,1)S(1)}, u32[]{:S(2)}, u32[]{:S(2)}) collective-permute-start(bf16[192,128]{1,0:T(8,128)(2,1)} %copy-done.28), channel_id=1, source_target_pairs={{0,2},{1,3},{2,0},{3,1},{4,6},{5,7},{6,4},{7,5},{8,10},{9,11},{10,... | collective-permute-start | bytes 147464 | tf_op jit(solution)/shard_map/ppermute | solution.py:365
  44.4 8.6 %collective-permute-done.10.refs_8_.refs_7_ = bf16[192,128]{1,0:T(8,128)(2,1)S(1)} collective-permute-done((bf16[192,128]{1,0:T(8,128)(2,1)}, bf16[192,128]{1,0:T(8,128)(2,1)S(1)}, u32[]{:S(2)}, u32[]{:S(2)}) %collective-permute-start.10) | collective-permute-done | bytes 49184 | tf_op jit(solution)/shard_map/ppermute | solution.py:365
  53.1 1.1 %copy-done.1 = bf16[96,4096]{1,0:T(8,128)(2,1)S(1)} copy-done((bf16[96,4096]{1,0:T(8,128)(2,1)S(1)}, bf16[96,4096]{1,0:T(8,128)(2,1)}, u32[]{:S(2)}) %copy-start.1) | copy-done | bytes 786456
  54.2 1.0 %copy-done.3 = bf16[128,2048]{1,0:T(8,128)(2,1)S(1)} copy-done((bf16[128,2048]{1,0:T(8,128)(2,1)S(1)}, bf16[128,2048]{1,0:T(8,128)(2,1)}, u32[]{:S(2)}) %copy-start.3) | copy-done | bytes 524312
  55.3 2.7 %shard_map.97 = (bf16[192,128]{1,0:T(8,128)(2,1)S(1)}, f32[192,256]{1,0:T(8,128)S(1)}) custom-call(s32[3]{0:T(128)S(1)} %pad_add_fusion.1.refs_0_, bf16[96,4096]{1,0:T(8,128)(2,1)S(1)} %copy-done.1, bf16[96,4096]{1,0:T(8,128)(2,1)S(1)} %collective-permute-done.refs_5_.refs_2_, bf16[256,4096]{1,0:T(8,128)(2,1)S(1)} %copy-done, ...), custom_call_target="tpu_custom_call" | custom-call | flops 402653184 | bytes 4964352 | tf_op jit(solution)/shard_map/pallas_call | solution.py:93
  58.1 2.4 %shard_map.98 = (bf16[192,128]{1,0:T(8,128)(2,1)S(1)}, bf16[192,128]{1,0:T(8,128)(2,1)S(1)}, bf16[128,1024]{1,0:T(8,128)(2,1)S(1)}, bf16[128,1024]{1,0:T(8,128)(2,1)S(1)}) custom-call(s32[3]{0:T(128)S(1)} %pad_add_fusion.1.refs_0_, bf16[96,4096]{1,0:T(8,128)(2,1)S(1)} %copy-done.1, bf16[96,4096]{1,0:T(8,128)(2,1)S(1)} %collective-permute-done.refs_5_.refs_2_, ...), custom_call_target="tpu_custom_call" | custom-call | flops 201326592 | bytes 3964928 | tf_op jit(solution)/shard_map/pallas_call | solution.py:93
  60.5 1.8 %collective-permute-start.16 = (bf16[128,1024]{1,0:T(8,128)(2,1)S(1)}, bf16[128,1024]{1,0:T(8,128)(2,1)S(1)}, u32[]{:S(2)}, u32[]{:S(2)}) collective-permute-start(bf16[128,1024]{1,0:T(8,128)(2,1)S(1)} %get-tuple-element.57), channel_id=1, source_target_pairs={{0,8},{1,9},{2,10},{3,11},{4,12},{5,13},{6,14},{7,15},{8,0},{9,1},... | collective-permute-start | bytes 786440 | tf_op jit(solution)/shard_map/ppermute | solution.py:365
  62.2 1.5 %collective-permute-start.17 = (bf16[128,1024]{1,0:T(8,128)(2,1)S(1)}, bf16[128,1024]{1,0:T(8,128)(2,1)S(1)}, u32[]{:S(2)}, u32[]{:S(2)}) collective-permute-start(bf16[128,1024]{1,0:T(8,128)(2,1)S(1)} %get-tuple-element.58), channel_id=1, source_target_pairs={{0,16},{1,17},{2,18},{3,19},{4,20},{5,21},{6,22},{7,23},{8,24},{9,... | collective-permute-start | bytes 786440 | tf_op jit(solution)/shard_map/ppermute | solution.py:365
  63.8 1.1 %collective-permute-start.18 = (bf16[192,128]{1,0:T(8,128)(2,1)S(1)}, bf16[192,128]{1,0:T(8,128)(2,1)S(1)}, u32[]{:S(2)}, u32[]{:S(2)}) collective-permute-start(bf16[192,128]{1,0:T(8,128)(2,1)S(1)} %get-tuple-element.60), channel_id=1, source_target_pairs={{0,3},{1,0},{2,1},{3,2},{4,7},{5,4},{6,5},{7,6},{8,11},{9,8},{10,9... | collective-permute-start | bytes 147464 | tf_op jit(solution)/shard_map/ppermute | solution.py:365
  64.8 1.0 %collective-permute-start.19 = (bf16[192,128]{1,0:T(8,128)(2,1)S(1)}, bf16[192,128]{1,0:T(8,128)(2,1)S(1)}, u32[]{:S(2)}, u32[]{:S(2)}) collective-permute-start(bf16[192,128]{1,0:T(8,128)(2,1)S(1)} %get-tuple-element.61), channel_id=1, source_target_pairs={{0,1},{1,2},{2,3},{3,0},{4,5},{5,6},{6,7},{7,4},{8,9},{9,10},{10,1... | collective-permute-start | bytes 147464 | tf_op jit(solution)/shard_map/ppermute | solution.py:365
  65.8 2.7 %shard_map.96 = (f32[192,128]{1,0:T(8,128)S(1)}, f32[96,2048]{1,0:T(8,128)S(1)}, f32[96,2048]{1,0:T(8,128)S(1)}) custom-call(s32[3]{0:T(128)S(1)} %pad_add_fusion.1.refs_0_, bf16[96,4096]{1,0:T(8,128)(2,1)S(1)} %copy-done.1, bf16[96,4096]{1,0:T(8,128)(2,1)S(1)} %collective-permute-done.refs_5_.refs_2_, bf16[256,4096]{1,0:T(8,128)(2,1)S(1)} %copy-done, ...), custom_call_target="tpu_custom_call" | custom-call | flops 402653184 | bytes 7110656 | tf_op jit(solution)/shard_map/pallas_call | solution.py:93
  69.1 1.6 %collective-permute-done.19.refs_7_.refs_5_ = bf16[192,128]{1,0:T(8,128)(2,1)S(1)} collective-permute-done((bf16[192,128]{1,0:T(8,128)(2,1)S(1)}, bf16[192,128]{1,0:T(8,128)(2,1)S(1)}, u32[]{:S(2)}, u32[]{:S(2)}) %collective-permute-start.19) | collective-permute-done | bytes 49184 | tf_op jit(solution)/shard_map/ppermute | solution.py:365
  70.7 1.1 %shard_map.99 = bf16[192,128]{1,0:T(8,128)(2,1)S(1)} custom-call(s32[3]{0:T(128)S(1)} %pad_add_fusion.1.refs_0_, bf16[96,4096]{1,0:T(8,128)(2,1)S(1)} %copy-done.1, bf16[96,4096]{1,0:T(8,128)(2,1)S(1)} %collective-permute-done.refs_5_.refs_2_, bf16[128,1024]{1,0:T(8,128)(2,1)S(1)} %collective-permute-done.16.refs_3_.refs_4_, ...), custom_call_target="tpu_custom_call" | custom-call | flops 100663296 | bytes 2244608 | tf_op jit(solution)/shard_map/pallas_call | solution.py:93
  71.8 0.7 collective-permute-start.20
  72.8 5.0 %collective-permute-done.20.refs_10_.refs_4_ = bf16[192,128]{1,0:T(8,128)(2,1)S(1)} collective-permute-done((bf16[192,128]{1,0:T(8,128)(2,1)S(1)}, bf16[192,128]{1,0:T(8,128)(2,1)S(1)}, u32[]{:S(2)}, u32[]{:S(2)}) %collective-permute-start.20) | collective-permute-done | bytes 49184 | tf_op jit(solution)/shard_map/ppermute | solution.py:365
  77.8 2.3 %shard_map.100 = (f32[96,2048]{1,0:T(8,128)S(1)}, f32[96,2048]{1,0:T(8,128)S(1)}) custom-call(s32[3]{0:T(128)S(1)} %pad_add_fusion.1.refs_0_, bf16[256,4096]{1,0:T(8,128)(2,1)S(1)} %copy-done, bf16[128,2048]{1,0:T(8,128)(2,1)S(1)} %collective-permute-done.14.refs_3_.refs_2_, bf16[128,2048]{1,0:T(8,128)(2,1)} %collective-permute-done.15.refs_4_.refs_3_, ...), custom_call_target="tpu_custom_call" | custom-call | flops 402653184 | bytes 5439488 | tf_op jit(solution)/shard_map/pallas_call | solution.py:93
  80.7 1.8 %collective-permute-done.25.refs_8_ = bf16[192,128]{1,0:T(8,128)(2,1)S(1)} collective-permute-done((bf16[192,128]{1,0:T(8,128)(2,1)S(1)}, bf16[192,128]{1,0:T(8,128)(2,1)S(1)}, u32[]{:S(2)}, u32[]{:S(2)}) %collective-permute-start.25) | collective-permute-done | bytes 49184 | tf_op jit(solution)/shard_map/ppermute | solution.py:365
  82.6 0.8 shard_map.102
  83.9 0.7 collective-permute-done.27.refs_2_
  85.6 2.7 %collective-permute-start.30 = (f32[128,128]{1,0:T(8,128)S(1)}, f32[128,128]{1,0:T(8,128)S(1)}, u32[]{:S(2)}, u32[]{:S(2)}) collective-permute-start(f32[128,128]{1,0:T(8,128)S(1)} %add.15.refs_10_), channel_id=1, source_target_pairs={{0,24},{1,25},{2,26},{3,27},{4,28},{5,29},{6,30},{7,31},{8,16},{9,... | collective-permute-start | bytes 196616 | tf_op jit(solution)/shard_map/ppermute | solution.py:365
  88.4 2.9 %shard_map.103 = (bf16[384,256]{1,0:T(8,128)(2,1)}, f32[384,256]{1,0:T(8,128)S(1)}, f32[384,256]{1,0:T(8,128)S(1)}) custom-call(s32[3]{0:T(128)S(1)} %pad_add_fusion.2.refs_1_.refs_0_, bf16[384,256]{1,0:T(8,128)(2,1)S(1)} %copy-done.7, bf16[384,256]{1,0:T(8,128)(2,1)S(1)} %copy-done.9, bf16[384,256]{1,0:T(8,128)(2,1)S(1)} %copy-done.11, ...), custom_call_target="tpu_custom_call" | custom-call | flops 528482304 | bytes 3473408 | tf_op jit(solution)/shard_map/pallas_call | solution.py:93
  92.1 1.6 %shard_map.101 = (bf16[96,4096]{1,0:T(8,128)(2,1)}, f32[8,128]{1,0:T(8,128)S(1)}) custom-call(s32[2]{0:T(128)S(1)} %pad_add_fusion.refs_0_, f32[96,2048]{1,0:T(8,128)S(1)} %get-tuple-element.54.refs_1_, f32[96,2048]{1,0:T(8,128)S(1)} %collective-permute-done.13.refs_2_, f32[96,2048]{1,0:T(8,128)S(1)} %get-tuple-element.63.refs_3_, ...), custom_call_target="tpu_custom_call" | custom-call | flops 1 | bytes 3936256 | tf_op jit(solution)/shard_map/pallas_call | solution.py:93
  93.6 1.6 %shard_map.105 = (bf16[384,256]{1,0:T(8,128)(2,1)}, bf16[384,256]{1,0:T(8,128)(2,1)}) custom-call(s32[3]{0:T(128)S(1)} %pad_add_fusion.2.refs_1_.refs_0_, bf16[384,256]{1,0:T(8,128)(2,1)S(1)} %copy-done.9, bf16[384,256]{1,0:T(8,128)(2,1)S(1)} %copy-done.11, f32[384,256]{1,0:T(8,128)S(1)} %get-tuple-element.75.refs_6_.refs_3_, ...), custom_call_target="tpu_custom_call" | custom-call | flops 1 | bytes 1703936 | tf_op jit(solution)/shard_map/pallas_call | solution.py:93
  (97 shorter events, 9.6 us)
Async XLA Ops:
  0.6 7.1 %collective-permute-start = (bf16[96,4096]{1,0:T(8,128)(2,1)}, bf16[96,4096]{1,0:T(8,128)(2,1)S(1)}, u32[]{:S(2)}, u32[]{:S(2)}) collective-permute-start(bf16[96,4096]{1,0:T(8,128)(2,1)} %refs_1_.11), channel_id=1, source_target_pairs={{0,4},{1,5},{2,6},{3,7},{4,0},{5,1},{6,2},{7,3},{8,12},{9,13},{10,... | collective-permute-start | bytes 2359304 | tf_op jit(solution)/shard_map/ppermute | solution.py:365
  3.0 50.0 %copy-start = (bf16[256,4096]{1,0:T(8,128)(2,1)S(1)}, bf16[256,4096]{1,0:T(8,128)(2,1)}, u32[]{:S(2)}) copy-start(bf16[256,4096]{1,0:T(8,128)(2,1)} %refs_1_.12) | copy-start | bytes 6291460
  3.0 32.8 %collective-permute-start.1 = (bf16[128,2048]{1,0:T(8,128)(2,1)}, bf16[128,2048]{1,0:T(8,128)(2,1)S(1)}, u32[]{:S(2)}, u32[]{:S(2)}) collective-permute-start(bf16[128,2048]{1,0:T(8,128)(2,1)} %dynamic_slice.3), channel_id=1, source_target_pairs={{0,1},{1,2},{2,3},{3,0},{4,5},{5,6},{6,7},{7,4},{8,9},{9,10},{10,1... | collective-permute-start | bytes 1572872 | tf_op jit(solution)/shard_map/ppermute | solution.py:365
  5.6 30.2 %collective-permute-start.2 = (bf16[128,2048]{1,0:T(8,128)(2,1)}, bf16[128,2048]{1,0:T(8,128)(2,1)}, u32[]{:S(2)}, u32[]{:S(2)}) collective-permute-start(bf16[128,2048]{1,0:T(8,128)(2,1)} %dynamic_slice.3), channel_id=1, source_target_pairs={{0,3},{1,0},{2,1},{3,2},{4,7},{5,4},{6,5},{7,6},{8,11},{9,8},{10,9... | collective-permute-start | bytes 1572872 | tf_op jit(solution)/shard_map/ppermute | solution.py:365
  7.8 0.9 copy-start.5
  8.7 0.9 copy-start.8
  17.1 1.3 %collective-permute-start.3 = (f32[128,128]{1,0:T(8,128)S(1)}, f32[128,128]{1,0:T(8,128)S(1)}, u32[]{:S(2)}, u32[]{:S(2)}) collective-permute-start(f32[128,128]{1,0:T(8,128)S(1)} %get-tuple-element.44), channel_id=1, source_target_pairs={{0,4},{1,5},{2,6},{3,7},{4,0},{5,1},{6,2},{7,3},{8,12},{9,13},{10,... | collective-permute-start | bytes 196616 | tf_op jit(solution)/shard_map/ppermute | solution.py:365
  17.3 3.5 %collective-permute-start.7 = (bf16[384,128]{1,0:T(8,128)(2,1)}, bf16[384,128]{1,0:T(8,128)(2,1)}, u32[]{:S(2)}, u32[]{:S(2)}) collective-permute-start(bf16[384,128]{1,0:T(8,128)(2,1)} %get-tuple-element.45), channel_id=1, source_target_pairs={{0,4},{1,5},{2,6},{3,7},{4,0},{5,1},{6,2},{7,3},{8,12},{9,13},{10,... | collective-permute-start | bytes 294920 | tf_op jit(solution)/shard_map/ppermute | solution.py:365
  17.6 11.3 %collective-permute-start.8 = (f32[384,128]{1,0:T(8,128)}, f32[384,128]{1,0:T(8,128)}, u32[]{:S(2)}, u32[]{:S(2)}) collective-permute-start(f32[384,128]{1,0:T(8,128)} %get-tuple-element.47), channel_id=1, source_target_pairs={{0,4},{1,5},{2,6},{3,7},{4,0},{5,1},{6,2},{7,3},{8,12},{9,13},{10,... | collective-permute-start | bytes 589832 | tf_op jit(solution)/shard_map/ppermute | solution.py:365
  19.0 4.6 %collective-permute-start.4 = (f32[128,128]{1,0:T(8,128)}, f32[128,128]{1,0:T(8,128)}, u32[]{:S(2)}, u32[]{:S(2)}) collective-permute-start(f32[128,128]{1,0:T(8,128)} %add.14), channel_id=1, source_target_pairs={{0,8},{1,9},{2,10},{3,11},{4,12},{5,13},{6,14},{7,15},{8,0},{9,1},... | collective-permute-start | bytes 196616 | tf_op jit(solution)/shard_map/ppermute | solution.py:365
  20.8 5.6 %collective-permute-start.5 = (f32[128,128]{1,0:T(8,128)}, f32[128,128]{1,0:T(8,128)S(1)}, u32[]{:S(2)}, u32[]{:S(2)}) collective-permute-start(f32[128,128]{1,0:T(8,128)} %add.14), channel_id=1, source_target_pairs={{0,16},{1,17},{2,18},{3,19},{4,20},{5,21},{6,22},{7,23},{8,24},{9,... | collective-permute-start | bytes 196616 | tf_op jit(solution)/shard_map/ppermute | solution.py:365
  23.6 5.4 %collective-permute-start.6 = (f32[128,128]{1,0:T(8,128)}, f32[128,128]{1,0:T(8,128)S(1)}, u32[]{:S(2)}, u32[]{:S(2)}) collective-permute-start(f32[128,128]{1,0:T(8,128)} %add.14), channel_id=1, source_target_pairs={{0,24},{1,25},{2,26},{3,27},{4,28},{5,29},{6,30},{7,31},{8,16},{9,... | collective-permute-start | bytes 196616 | tf_op jit(solution)/shard_map/ppermute | solution.py:365
  29.0 0.9 copy-start.6
  36.7 21.3 %collective-permute-start.9 = (bf16[128,2048]{1,0:T(8,128)(2,1)}, bf16[128,2048]{1,0:T(8,128)(2,1)}, u32[]{:S(2)}, u32[]{:S(2)}) collective-permute-start(bf16[128,2048]{1,0:T(8,128)(2,1)} %get-tuple-element.49.refs_4_), channel_id=1, source_target_pairs={{0,1},{1,2},{2,3},{3,0},{4,5},{5,6},{6,7},{7,4},{8,9},{9,10},{10,1... | collective-permute-start | bytes 1572872 | tf_op jit(solution)/shard_map/ppermute | solution.py:365
  36.8 21.3 %collective-permute-start.14 = (bf16[128,2048]{1,0:T(8,128)(2,1)}, bf16[128,2048]{1,0:T(8,128)(2,1)S(1)}, u32[]{:S(2)}, u32[]{:S(2)}) collective-permute-start(bf16[128,2048]{1,0:T(8,128)(2,1)} %get-tuple-element.49.refs_4_), channel_id=1, source_target_pairs={{0,8},{1,9},{2,10},{3,11},{4,12},{5,13},{6,14},{7,15},{8,0},{9,1},... | collective-permute-start | bytes 1572872 | tf_op jit(solution)/shard_map/ppermute | solution.py:365
  38.5 19.6 %collective-permute-start.15 = (bf16[128,2048]{1,0:T(8,128)(2,1)}, bf16[128,2048]{1,0:T(8,128)(2,1)}, u32[]{:S(2)}, u32[]{:S(2)}) collective-permute-start(bf16[128,2048]{1,0:T(8,128)(2,1)} %get-tuple-element.50.refs_6_.refs_5_), channel_id=1, source_target_pairs={{0,16},{1,17},{2,18},{3,19},{4,20},{5,21},{6,22},{7,23},{8,24},{9,... | collective-permute-start | bytes 1572872 | tf_op jit(solution)/shard_map/ppermute | solution.py:365
  40.0 13.0 %collective-permute-start.10 = (bf16[192,128]{1,0:T(8,128)(2,1)}, bf16[192,128]{1,0:T(8,128)(2,1)S(1)}, u32[]{:S(2)}, u32[]{:S(2)}) collective-permute-start(bf16[192,128]{1,0:T(8,128)(2,1)} %copy-done.29), channel_id=1, source_target_pairs={{0,1},{1,2},{2,3},{3,0},{4,5},{5,6},{6,7},{7,4},{8,9},{9,10},{10,1... | collective-permute-start | bytes 147464 | tf_op jit(solution)/shard_map/ppermute | solution.py:365
  41.3 16.7 %collective-permute-start.11 = (bf16[192,128]{1,0:T(8,128)(2,1)}, bf16[192,128]{1,0:T(8,128)(2,1)S(1)}, u32[]{:S(2)}, u32[]{:S(2)}) collective-permute-start(bf16[192,128]{1,0:T(8,128)(2,1)} %copy-done.28), channel_id=1, source_target_pairs={{0,2},{1,3},{2,0},{3,1},{4,6},{5,7},{6,4},{7,5},{8,10},{9,11},{10,... | collective-permute-start | bytes 147464 | tf_op jit(solution)/shard_map/ppermute | solution.py:365
  53.0 5.0 %collective-permute-start.12 = (bf16[192,128]{1,0:T(8,128)(2,1)}, bf16[192,128]{1,0:T(8,128)(2,1)S(1)}, u32[]{:S(2)}, u32[]{:S(2)}) collective-permute-start(bf16[192,128]{1,0:T(8,128)(2,1)} %copy-done.27), channel_id=1, source_target_pairs={{0,3},{1,0},{2,1},{3,2},{4,7},{5,4},{6,5},{7,6},{8,11},{9,8},{10,9... | collective-permute-start | bytes 147464 | tf_op jit(solution)/shard_map/ppermute | solution.py:365
  53.1 1.1 %copy-start.1 = (bf16[96,4096]{1,0:T(8,128)(2,1)S(1)}, bf16[96,4096]{1,0:T(8,128)(2,1)}, u32[]{:S(2)}) copy-start(bf16[96,4096]{1,0:T(8,128)(2,1)} %refs_1_.11) | copy-start | bytes 2359300
  54.2 1.0 %copy-start.3 = (bf16[128,2048]{1,0:T(8,128)(2,1)S(1)}, bf16[128,2048]{1,0:T(8,128)(2,1)}, u32[]{:S(2)}) copy-start(bf16[128,2048]{1,0:T(8,128)(2,1)} %get-tuple-element.49.refs_4_) | copy-start | bytes 1572868
  58.0 7.8 %copy-start.4 = (bf16[128,2048]{1,0:T(8,128)(2,1)S(1)}, bf16[128,2048]{1,0:T(8,128)(2,1)}, u32[]{:S(2)}) copy-start(bf16[128,2048]{1,0:T(8,128)(2,1)} %get-tuple-element.49.refs_4_) | copy-start | bytes 1572868
  58.0 7.8 %copy-start.17 = (bf16[192,128]{1,0:T(8,128)(2,1)S(1)}, bf16[192,128]{1,0:T(8,128)(2,1)}, u32[]{:S(2)}) copy-start(bf16[192,128]{1,0:T(8,128)(2,1)} %copy-done.16) | copy-start | bytes 147460
  60.5 10.2 %collective-permute-start.16 = (bf16[128,1024]{1,0:T(8,128)(2,1)S(1)}, bf16[128,1024]{1,0:T(8,128)(2,1)S(1)}, u32[]{:S(2)}, u32[]{:S(2)}) collective-permute-start(bf16[128,1024]{1,0:T(8,128)(2,1)S(1)} %get-tuple-element.57), channel_id=1, source_target_pairs={{0,8},{1,9},{2,10},{3,11},{4,12},{5,13},{6,14},{7,15},{8,0},{9,1},... | collective-permute-start | bytes 786440 | tf_op jit(solution)/shard_map/ppermute | solution.py:365
  62.2 8.5 %collective-permute-start.17 = (bf16[128,1024]{1,0:T(8,128)(2,1)S(1)}, bf16[128,1024]{1,0:T(8,128)(2,1)S(1)}, u32[]{:S(2)}, u32[]{:S(2)}) collective-permute-start(bf16[128,1024]{1,0:T(8,128)(2,1)S(1)} %get-tuple-element.58), channel_id=1, source_target_pairs={{0,16},{1,17},{2,18},{3,19},{4,20},{5,21},{6,22},{7,23},{8,24},{9,... | collective-permute-start | bytes 786440 | tf_op jit(solution)/shard_map/ppermute | solution.py:365
  63.8 4.8 %collective-permute-start.18 = (bf16[192,128]{1,0:T(8,128)(2,1)S(1)}, bf16[192,128]{1,0:T(8,128)(2,1)S(1)}, u32[]{:S(2)}, u32[]{:S(2)}) collective-permute-start(bf16[192,128]{1,0:T(8,128)(2,1)S(1)} %get-tuple-element.60), channel_id=1, source_target_pairs={{0,3},{1,0},{2,1},{3,2},{4,7},{5,4},{6,5},{7,6},{8,11},{9,8},{10,9... | collective-permute-start | bytes 147464 | tf_op jit(solution)/shard_map/ppermute | solution.py:365
  64.8 5.9 %collective-permute-start.19 = (bf16[192,128]{1,0:T(8,128)(2,1)S(1)}, bf16[192,128]{1,0:T(8,128)(2,1)S(1)}, u32[]{:S(2)}, u32[]{:S(2)}) collective-permute-start(bf16[192,128]{1,0:T(8,128)(2,1)S(1)} %get-tuple-element.61), channel_id=1, source_target_pairs={{0,1},{1,2},{2,3},{3,0},{4,5},{5,6},{6,7},{7,4},{8,9},{9,10},{10,1... | collective-permute-start | bytes 147464 | tf_op jit(solution)/shard_map/ppermute | solution.py:365
  65.8 7.0 %collective-permute-start.21 = (bf16[192,128]{1,0:T(8,128)(2,1)S(1)}, bf16[192,128]{1,0:T(8,128)(2,1)S(1)}, u32[]{:S(2)}, u32[]{:S(2)}) collective-permute-start(bf16[192,128]{1,0:T(8,128)(2,1)S(1)} %get-tuple-element.62.refs_2_), channel_id=1, source_target_pairs={{0,4},{1,5},{2,6},{3,7},{4,0},{5,1},{6,2},{7,3},{8,12},{9,13},{10,... | collective-permute-start | bytes 147464 | tf_op jit(solution)/shard_map/ppermute | solution.py:365
  68.5 4.3 %collective-permute-start.22 = (bf16[192,128]{1,0:T(8,128)(2,1)S(1)}, bf16[192,128]{1,0:T(8,128)(2,1)S(1)}, u32[]{:S(2)}, u32[]{:S(2)}) collective-permute-start(bf16[192,128]{1,0:T(8,128)(2,1)S(1)} %collective-permute-done.18.refs_6_.refs_3_), channel_id=1, source_target_pairs={{0,4},{1,5},{2,6},{3,7},{4,0},{5,1},{6,2},{7,3},{8,12},{9,13},{10,... | collective-permute-start | bytes 147464 | tf_op jit(solution)/shard_map/ppermute | solution.py:365
  70.7 2.1 %collective-permute-start.23 = (bf16[192,128]{1,0:T(8,128)(2,1)S(1)}, bf16[192,128]{1,0:T(8,128)(2,1)S(1)}, u32[]{:S(2)}, u32[]{:S(2)}) collective-permute-start(bf16[192,128]{1,0:T(8,128)(2,1)S(1)} %collective-permute-done.19.refs_7_.refs_5_), channel_id=1, source_target_pairs={{0,4},{1,5},{2,6},{3,7},{4,0},{5,1},{6,2},{7,3},{8,12},{9,13},{10,... | collective-permute-start | bytes 147464 | tf_op jit(solution)/shard_map/ppermute | solution.py:365
  71.8 10.8 %copy-start.7 = (bf16[384,256]{1,0:T(8,128)(2,1)S(1)}, bf16[384,256]{1,0:T(8,128)(2,1)}, u32[]{:S(2)}) copy-start(bf16[384,256]{1,0:T(8,128)(2,1)} %refs_1_.14) | copy-start | bytes 589828
  71.8 6.0 %collective-permute-start.20 = (bf16[192,128]{1,0:T(8,128)(2,1)S(1)}, bf16[192,128]{1,0:T(8,128)(2,1)S(1)}, u32[]{:S(2)}, u32[]{:S(2)}) collective-permute-start(bf16[192,128]{1,0:T(8,128)(2,1)S(1)} %shard_map.99), channel_id=1, source_target_pairs={{0,2},{1,3},{2,0},{3,1},{4,6},{5,7},{6,4},{7,5},{8,10},{9,11},{10,... | collective-permute-start | bytes 147464 | tf_op jit(solution)/shard_map/ppermute | solution.py:365
  72.5 11.1 %copy-start.26 = (f32[128,128]{1,0:T(8,128)S(1)}, f32[128,128]{1,0:T(8,128)}, u32[]{:S(2)}) copy-start(f32[128,128]{1,0:T(8,128)} %copy-done.25) | copy-start | bytes 196612
  72.5 15.8 %copy-start.9 = (bf16[384,256]{1,0:T(8,128)(2,1)S(1)}, bf16[384,256]{1,0:T(8,128)(2,1)}, u32[]{:S(2)}) copy-start(bf16[384,256]{1,0:T(8,128)(2,1)} %refs_1_.15) | copy-start | bytes 589828
  72.5 15.8 %copy-start.11 = (bf16[384,256]{1,0:T(8,128)(2,1)S(1)}, bf16[384,256]{1,0:T(8,128)(2,1)}, u32[]{:S(2)}) copy-start(bf16[384,256]{1,0:T(8,128)(2,1)} %refs_2_.5) | copy-start | bytes 589828
  72.5 15.8 %copy-start.13 = (bf16[2,384,384]{2,1,0:T(8,128)(2,1)S(1)}, bf16[2,384,384]{2,1,0:T(8,128)(2,1)}, u32[]{:S(2)}) copy-start(bf16[2,384,384]{2,1,0:T(8,128)(2,1)} %copy-done.12) | copy-start | bytes 1769476
  72.5 15.8 %copy-start.15 = (bf16[2,384,384]{2,1,0:T(8,128)(2,1)S(1)}, bf16[2,384,384]{2,1,0:T(8,128)(2,1)}, u32[]{:S(2)}) copy-start(bf16[2,384,384]{2,1,0:T(8,128)(2,1)} %copy-done.14) | copy-start | bytes 1769476
  72.5 15.8 %copy-start.19 = (f32[384,256]{1,0:T(8,128)S(1)}, f32[384,256]{1,0:T(8,128)}, u32[]{:S(2)}) copy-start(f32[384,256]{1,0:T(8,128)} %copy-done.18) | copy-start | bytes 1179652
  72.5 15.8 %copy-start.23 = (f32[128,128]{1,0:T(8,128)S(1)}, f32[128,128]{1,0:T(8,128)}, u32[]{:S(2)}) copy-start(f32[128,128]{1,0:T(8,128)} %copy-done.22) | copy-start | bytes 196612
  72.5 19.5 %collective-permute-start.13 = (f32[96,2048]{1,0:T(8,128)S(1)}, f32[96,2048]{1,0:T(8,128)S(1)}, u32[]{:S(2)}, u32[]{:S(2)}) collective-permute-start(f32[96,2048]{1,0:T(8,128)S(1)} %get-tuple-element.55), channel_id=1, source_target_pairs={{0,4},{1,5},{2,6},{3,7},{4,0},{5,1},{6,2},{7,3},{8,12},{9,13},{10,... | collective-permute-start | bytes 2359304 | tf_op jit(solution)/shard_map/ppermute | solution.py:365
  80.1 11.9 %collective-permute-start.24 = (f32[96,2048]{1,0:T(8,128)S(1)}, f32[96,2048]{1,0:T(8,128)S(1)}, u32[]{:S(2)}, u32[]{:S(2)}) collective-permute-start(f32[96,2048]{1,0:T(8,128)S(1)} %get-tuple-element.64), channel_id=1, source_target_pairs={{0,4},{1,5},{2,6},{3,7},{4,0},{5,1},{6,2},{7,3},{8,12},{9,13},{10,... | collective-permute-start | bytes 2359304 | tf_op jit(solution)/shard_map/ppermute | solution.py:365
  80.3 2.3 %collective-permute-start.25 = (bf16[192,128]{1,0:T(8,128)(2,1)S(1)}, bf16[192,128]{1,0:T(8,128)(2,1)S(1)}, u32[]{:S(2)}, u32[]{:S(2)}) collective-permute-start(bf16[192,128]{1,0:T(8,128)(2,1)S(1)} %collective-permute-done.20.refs_10_.refs_4_), channel_id=1, source_target_pairs={{0,4},{1,5},{2,6},{3,7},{4,0},{5,1},{6,2},{7,3},{8,12},{9,13},{10,... | collective-permute-start | bytes 147464 | tf_op jit(solution)/shard_map/ppermute | solution.py:365
  83.4 1.3 %collective-permute-start.27 = (f32[128,128]{1,0:T(8,128)S(1)}, f32[128,128]{1,0:T(8,128)S(1)}, u32[]{:S(2)}, u32[]{:S(2)}) collective-permute-start(f32[128,128]{1,0:T(8,128)S(1)} %get-tuple-element.73), channel_id=1, source_target_pairs={{0,4},{1,5},{2,6},{3,7},{4,0},{5,1},{6,2},{7,3},{8,12},{9,13},{10,... | collective-permute-start | bytes 196616 | tf_op jit(solution)/shard_map/ppermute | solution.py:365
  83.6 2.0 %collective-permute-start.26 = (f32[128,128]{1,0:T(8,128)S(1)}, f32[128,128]{1,0:T(8,128)S(1)}, u32[]{:S(2)}, u32[]{:S(2)}) collective-permute-start(f32[128,128]{1,0:T(8,128)S(1)} %copy-done.26), channel_id=1, source_target_pairs={{0,4},{1,5},{2,6},{3,7},{4,0},{5,1},{6,2},{7,3},{8,12},{9,13},{10,... | collective-permute-start | bytes 196616 | tf_op jit(solution)/shard_map/ppermute | solution.py:365
  84.7 6.6 %collective-permute-start.28 = (f32[128,128]{1,0:T(8,128)S(1)}, f32[128,128]{1,0:T(8,128)S(1)}, u32[]{:S(2)}, u32[]{:S(2)}) collective-permute-start(f32[128,128]{1,0:T(8,128)S(1)} %add.15.refs_10_), channel_id=1, source_target_pairs={{0,8},{1,9},{2,10},{3,11},{4,12},{5,13},{6,14},{7,15},{8,0},{9,1},... | collective-permute-start | bytes 196616 | tf_op jit(solution)/shard_map/ppermute | solution.py:365
  85.3 6.0 %collective-permute-start.29 = (f32[128,128]{1,0:T(8,128)S(1)}, f32[128,128]{1,0:T(8,128)S(1)}, u32[]{:S(2)}, u32[]{:S(2)}) collective-permute-start(f32[128,128]{1,0:T(8,128)S(1)} %add.15.refs_10_), channel_id=1, source_target_pairs={{0,16},{1,17},{2,18},{3,19},{4,20},{5,21},{6,22},{7,23},{8,24},{9,... | collective-permute-start | bytes 196616 | tf_op jit(solution)/shard_map/ppermute | solution.py:365
  85.6 5.7 %collective-permute-start.30 = (f32[128,128]{1,0:T(8,128)S(1)}, f32[128,128]{1,0:T(8,128)S(1)}, u32[]{:S(2)}, u32[]{:S(2)}) collective-permute-start(f32[128,128]{1,0:T(8,128)S(1)} %add.15.refs_10_), channel_id=1, source_target_pairs={{0,24},{1,25},{2,26},{3,27},{4,28},{5,29},{6,30},{7,31},{8,16},{9,... | collective-permute-start | bytes 196616 | tf_op jit(solution)/shard_map/ppermute | solution.py:365
  91.9 1.7 %collective-permute-start.31 = (f32[128,128]{1,0:T(8,128)S(1)}, f32[128,128]{1,0:T(8,128)S(1)}, u32[]{:S(2)}, u32[]{:S(2)}) collective-permute-start(f32[128,128]{1,0:T(8,128)S(1)} %get-tuple-element.78), channel_id=1, source_target_pairs={{0,4},{1,5},{2,6},{3,7},{4,0},{5,1},{6,2},{7,3},{8,12},{9,13},{10,... | collective-permute-start | bytes 196616 | tf_op jit(solution)/shard_map/ppermute | solution.py:365
  (14 other events, 10.2 us)

commit v10 on v9

--- a/solution.py
+++ b/solution.py
@@ -420,6 +420,8 @@
         flops=7 * square,
     )
     flags, parts, total = exchange(mine, other, core, chip, chips, False)
+    if board:
+        arrived[1], arrived[3], parts[1] = hold([arrived[1], arrived[3], parts[1]], parts[2:])
     *attn, keep, back = call(
         functools.partial(attn_kernel, scale, count),
         [tokens] * count + pair,
@@ -487,7 +489,6 @@
     def stacked(*arrays):
         return [(a, all_of, rows_at(n * DH, DH)) for n, a in enumerate(arrays)]
 
-    arrived[1], arrived[3] = hold([arrived[1], arrived[3]], attn[:1])
     arrived[2] = send(arrived[1], 0, 1)
     second = {1: send(arrived[1], 2, 0), 3: send(arrived[3], 4, 0)}
     mine, half = call(

time: 95.9 us -> 93.8 us (0.978)
  starting transfers between devices: 31.2 us -> 26.7 us
  waiting for transfers between devices: 22.3 us -> 25.9 us
    ppermute x32, starting transfers between devices: 31.2 us -> 26.7 us  [send(): return lax.ppermute(x, ('ctx', 'head'), pairs)]
    ppermute x32, waiting for transfers between devices: 22.3 us -> 25.9 us  [send(): return lax.ppermute(x, ('ctx', 'head'), pairs)]
    unnamed x60 -> x66, local copies, waits for them, and re-layouts: 15.2 us -> 14.6 us
  transfers between devices with their start and end apart: 32 -> 32, of which waited for: 8 -> 10; matrix products, arithmetic and copies ran while one was open for 3% -> 2% of each run, Pallas kernels for 20% -> 20%
where the time goes in v10:
time: 93.8 us; the launch traced here: 93.2 us
  starting transfers between devices  26.7 us (28%)
  waiting for transfers between devices  25.9 us (28%)
  Pallas kernels  22.7 us (24%)
  local copies, waits for them, and re-layouts  16.5 us (18%)
  between operations  0.97 us (1%)
    ppermute x32, starting transfers between devices, send(): return lax.ppermute(x, ('ctx', 'head'), pairs)  26.7 us
    ppermute x32, waiting for transfers between devices, send(): return lax.ppermute(x, ('ctx', 'head'), pairs)  25.9 us
    pallas_call x12, Pallas kernels, call(): pl.pallas_call(kernel, out_shape=[jax.ShapeDtypeStruct(s, t) for s, t in...  22.7 us
    unnamed x66, local copies, waits for them, and re-layouts  14.6 us
    dynamic_slice x1, local copies, waits for them, and re-layouts, on_device(): lax.dynamic_slice(out_weight, (core * DH, colour * wide), (DH, wide))  1.91 us
  transfers between devices with their start and end apart: 32, of which 10 were waited for; matrix products, arithmetic and copies ran while one was open for 2% of the time, Pallas kernels for 20%

profile of v10, /device:TPU:0, one launch (start us, length us, event | category | flops | bytes accessed | tf_op | source)
XLA Modules:
  0.0 93.2 jit_solution(7800616964499670984)
XLA Ops:
  1.1 1.9 %dynamic_slice.3 = bf16[128,2048]{1,0:T(8,128)(2,1)} dynamic-slice(bf16[256,4096]{1,0:T(8,128)(2,1)} %refs_1_.12, s32[]{:T(128)S(6)} %select_n.6, s32[]{:T(128)S(6)} %select_n.7), dynamic_slice_sizes={128,2048} | dynamic-slice | bytes 1048580 | tf_op jit(solution)/shard_map/dynamic_slice | solution.py:406
  3.1 2.6 %collective-permute-start.1 = (bf16[128,2048]{1,0:T(8,128)(2,1)}, bf16[128,2048]{1,0:T(8,128)(2,1)S(1)}, u32[]{:S(2)}, u32[]{:S(2)}) collective-permute-start(bf16[128,2048]{1,0:T(8,128)(2,1)} %dynamic_slice.3), channel_id=1, source_target_pairs={{0,1},{1,2},{2,3},{3,0},{4,5},{5,6},{6,7},{7,4},{8,9},{9,10},{10,1... | collective-permute-start | bytes 1572872 | tf_op jit(solution)/shard_map/ppermute | solution.py:365
  5.7 2.0 %collective-permute-start.2 = (bf16[128,2048]{1,0:T(8,128)(2,1)}, bf16[128,2048]{1,0:T(8,128)(2,1)}, u32[]{:S(2)}, u32[]{:S(2)}) collective-permute-start(bf16[128,2048]{1,0:T(8,128)(2,1)} %dynamic_slice.3), channel_id=1, source_target_pairs={{0,3},{1,0},{2,1},{3,2},{4,7},{5,4},{6,5},{7,6},{8,11},{9,8},{10,9... | collective-permute-start | bytes 1572872 | tf_op jit(solution)/shard_map/ppermute | solution.py:365
  7.8 0.9 copy-done.5
  8.7 0.9 copy-done.8
  9.6 0.9 copy-done.10
  10.6 0.7 copy-done.26
  11.2 2.1 %shard_map.93 = (bf16[2,384,384]{2,1,0:T(8,128)(2,1)S(1)}, bf16[2,384,384]{2,1,0:T(8,128)(2,1)S(1)}, f32[384,256]{1,0:T(8,128)S(1)}, f32[384,128]{1,0:T(8,128)S(...) custom-call(s32[3,3]{1,0:T(4,128)S(1)} %copy-done.26, ...), custom_call_target="tpu_custom_call" | custom-call | flops 264241152 | bytes 2785280 | tf_op jit(solution)/shard_map/pallas_call | solution.py:93
  13.4 0.8 copy-done.14
  14.2 0.8 copy-done.16
  15.0 0.7 copy-done.18
  15.8 0.7 copy-done.22
  16.6 1.1 %collective-permute-done.3.refs_2_ = f32[128,128]{1,0:T(8,128)S(1)} collective-permute-done((f32[128,128]{1,0:T(8,128)S(1)}, f32[128,128]{1,0:T(8,128)S(1)}, u32[]{:S(2)}, u32[]{:S(2)}) %collective-permute-start.3) | collective-permute-done | bytes 65568 | tf_op jit(solution)/shard_map/ppermute | solution.py:365
  17.7 1.8 %collective-permute-start.4 = (f32[128,128]{1,0:T(8,128)S(1)}, f32[128,128]{1,0:T(8,128)}, u32[]{:S(2)}, u32[]{:S(2)}) collective-permute-start(f32[128,128]{1,0:T(8,128)S(1)} %add.14), channel_id=1, source_target_pairs={{0,8},{1,9},{2,10},{3,11},{4,12},{5,13},{6,14},{7,15},{8,0},{9,1},... | collective-permute-start | bytes 196616 | tf_op jit(solution)/shard_map/ppermute | solution.py:365
  19.5 1.5 %collective-permute-start.5 = (f32[128,128]{1,0:T(8,128)S(1)}, f32[128,128]{1,0:T(8,128)}, u32[]{:S(2)}, u32[]{:S(2)}) collective-permute-start(f32[128,128]{1,0:T(8,128)S(1)} %add.14), channel_id=1, source_target_pairs={{0,16},{1,17},{2,18},{3,19},{4,20},{5,21},{6,22},{7,23},{8,24},{9,... | collective-permute-start | bytes 196616 | tf_op jit(solution)/shard_map/ppermute | solution.py:365
  21.3 10.0 %collective-permute-done.2.refs_1_ = bf16[128,2048]{1,0:T(8,128)(2,1)} collective-permute-done((bf16[128,2048]{1,0:T(8,128)(2,1)}, bf16[128,2048]{1,0:T(8,128)(2,1)}, u32[]{:S(2)}, u32[]{:S(2)}) %collective-permute-start.2) | collective-permute-done | bytes 524320 | tf_op jit(solution)/shard_map/ppermute | solution.py:365
  31.3 1.2 %collective-permute-start.7 = (bf16[128,2048]{1,0:T(8,128)(2,1)}, bf16[128,2048]{1,0:T(8,128)(2,1)}, u32[]{:S(2)}, u32[]{:S(2)}) collective-permute-start(bf16[128,2048]{1,0:T(8,128)(2,1)} %get-tuple-element.46.refs_4_), channel_id=1, source_target_pairs={{0,1},{1,2},{2,3},{3,0},{4,5},{5,6},{6,7},{7,4},{8,9},{9,10},{10,1... | collective-permute-start | bytes 1572872 | tf_op jit(solution)/shard_map/ppermute | solution.py:365
  32.5 1.5 %collective-permute-start.14 = (bf16[128,2048]{1,0:T(8,128)(2,1)}, bf16[128,2048]{1,0:T(8,128)(2,1)S(1)}, u32[]{:S(2)}, u32[]{:S(2)}) collective-permute-start(bf16[128,2048]{1,0:T(8,128)(2,1)} %get-tuple-element.46.refs_4_), channel_id=1, source_target_pairs={{0,8},{1,9},{2,10},{3,11},{4,12},{5,13},{6,14},{7,15},{8,0},{9,1},... | collective-permute-start | bytes 1572872 | tf_op jit(solution)/shard_map/ppermute | solution.py:365
  34.0 1.5 %collective-permute-start.15 = (bf16[128,2048]{1,0:T(8,128)(2,1)}, bf16[128,2048]{1,0:T(8,128)(2,1)}, u32[]{:S(2)}, u32[]{:S(2)}) collective-permute-start(bf16[128,2048]{1,0:T(8,128)(2,1)} %get-tuple-element.47.refs_6_.refs_5_), channel_id=1, source_target_pairs={{0,16},{1,17},{2,18},{3,19},{4,20},{5,21},{6,22},{7,23},{8,24},{9,... | collective-permute-start | bytes 1572872 | tf_op jit(solution)/shard_map/ppermute | solution.py:365
  36.1 1.1 %collective-permute-done.8.refs_8_ = bf16[384,128]{1,0:T(8,128)(2,1)S(1)} collective-permute-done((bf16[384,128]{1,0:T(8,128)(2,1)}, bf16[384,128]{1,0:T(8,128)(2,1)S(1)}, u32[]{:S(2)}, u32[]{:S(2)}) %collective-permute-start.8) | collective-permute-done | bytes 98336 | tf_op jit(solution)/shard_map/ppermute | solution.py:365
  37.4 0.9 copy-done.6
  38.3 0.8 copy-done.13
  39.2 0.9 copy-done.23
  40.1 1.9 %shard_map.95 = (bf16[192,128]{1,0:T(8,128)(2,1)S(1)}, bf16[192,128]{1,0:T(8,128)(2,1)}, bf16[192,128]{1,0:T(8,128)(2,1)S(1)}, bf16[192,128]{1,0:T(8,128)(2,1)S(...) custom-call(s32[4]{0:T(128)S(1)} %add_convert_fusion.refs_0_, s32[3]{0:T(128)S(1)} %pad_add_fusion.2.refs_1_.refs_0_, ...), custom_call_target="tpu_custom_call" | custom-call | flops 1 | bytes 1343488 | tf_op jit(solution)/shard_map/pallas_call | solution.py:93
  45.1 1.3 %collective-permute-start.10 = (bf16[192,128]{1,0:T(8,128)(2,1)}, bf16[192,128]{1,0:T(8,128)(2,1)S(1)}, u32[]{:S(2)}, u32[]{:S(2)}) collective-permute-start(bf16[192,128]{1,0:T(8,128)(2,1)} %get-tuple-element.53), channel_id=1, source_target_pairs={{0,1},{1,2},{2,3},{3,0},{4,5},{5,6},{6,7},{7,4},{8,9},{9,10},{10,1... | collective-permute-start | bytes 147464 | tf_op jit(solution)/shard_map/ppermute | solution.py:365
  46.4 1.9 %collective-permute-start.11 = (bf16[192,128]{1,0:T(8,128)(2,1)}, bf16[192,128]{1,0:T(8,128)(2,1)S(1)}, u32[]{:S(2)}, u32[]{:S(2)}) collective-permute-start(bf16[192,128]{1,0:T(8,128)(2,1)} %copy-done.32), channel_id=1, source_target_pairs={{0,2},{1,3},{2,0},{3,1},{4,6},{5,7},{6,4},{7,5},{8,10},{9,11},{10,... | collective-permute-start | bytes 147464 | tf_op jit(solution)/shard_map/ppermute | solution.py:365
  48.4 3.0 %collective-permute-done.10.refs_8_.refs_7_ = bf16[192,128]{1,0:T(8,128)(2,1)S(1)} collective-permute-done((bf16[192,128]{1,0:T(8,128)(2,1)}, bf16[192,128]{1,0:T(8,128)(2,1)S(1)}, u32[]{:S(2)}, u32[]{:S(2)}) %collective-permute-start.10) | collective-permute-done | bytes 49184 | tf_op jit(solution)/shard_map/ppermute | solution.py:365
  51.4 0.7 collective-permute-start.12
  52.2 1.1 %copy-done.1 = bf16[96,4096]{1,0:T(8,128)(2,1)S(1)} copy-done((bf16[96,4096]{1,0:T(8,128)(2,1)S(1)}, bf16[96,4096]{1,0:T(8,128)(2,1)}, u32[]{:S(2)}) %copy-start.1) | copy-done | bytes 786456
  53.3 1.0 %copy-done.3 = bf16[128,2048]{1,0:T(8,128)(2,1)S(1)} copy-done((bf16[128,2048]{1,0:T(8,128)(2,1)S(1)}, bf16[128,2048]{1,0:T(8,128)(2,1)}, u32[]{:S(2)}) %copy-start.3) | copy-done | bytes 524312
  54.4 2.7 %shard_map.97 = (bf16[192,128]{1,0:T(8,128)(2,1)S(1)}, f32[192,256]{1,0:T(8,128)S(1)}) custom-call(s32[3]{0:T(128)S(1)} %pad_add_fusion.1.refs_0_, bf16[96,4096]{1,0:T(8,128)(2,1)S(1)} %copy-done.1, bf16[96,4096]{1,0:T(8,128)(2,1)S(1)} %collective-permute-done.refs_5_.refs_2_, bf16[256,4096]{1,0:T(8,128)(2,1)S(1)} %copy-done, ...), custom_call_target="tpu_custom_call" | custom-call | flops 402653184 | bytes 4964352 | tf_op jit(solution)/shard_map/pallas_call | solution.py:93
  57.1 2.4 %shard_map.98 = (bf16[192,128]{1,0:T(8,128)(2,1)S(1)}, bf16[192,128]{1,0:T(8,128)(2,1)S(1)}, bf16[128,1024]{1,0:T(8,128)(2,1)S(1)}, bf16[128,1024]{1,0:T(8,128)(2,1)S(1)}) custom-call(s32[3]{0:T(128)S(1)} %pad_add_fusion.1.refs_0_, bf16[96,4096]{1,0:T(8,128)(2,1)S(1)} %copy-done.1, bf16[96,4096]{1,0:T(8,128)(2,1)S(1)} %collective-permute-done.refs_5_.refs_2_, ...), custom_call_target="tpu_custom_call" | custom-call | flops 201326592 | bytes 3964928 | tf_op jit(solution)/shard_map/pallas_call | solution.py:93
  60.7 1.4 %collective-permute-start.18 = (bf16[192,128]{1,0:T(8,128)(2,1)S(1)}, bf16[192,128]{1,0:T(8,128)(2,1)S(1)}, u32[]{:S(2)}, u32[]{:S(2)}) collective-permute-start(bf16[192,128]{1,0:T(8,128)(2,1)S(1)} %get-tuple-element.62), channel_id=1, source_target_pairs={{0,3},{1,0},{2,1},{3,2},{4,7},{5,4},{6,5},{7,6},{8,11},{9,8},{10,9... | collective-permute-start | bytes 147464 | tf_op jit(solution)/shard_map/ppermute | solution.py:365
  62.7 2.7 %shard_map.96 = (f32[192,128]{1,0:T(8,128)S(1)}, f32[96,2048]{1,0:T(8,128)S(1)}, f32[96,2048]{1,0:T(8,128)S(1)}) custom-call(s32[3]{0:T(128)S(1)} %pad_add_fusion.1.refs_0_, bf16[96,4096]{1,0:T(8,128)(2,1)S(1)} %copy-done.1, bf16[96,4096]{1,0:T(8,128)(2,1)S(1)} %collective-permute-done.refs_5_.refs_2_, bf16[256,4096]{1,0:T(8,128)(2,1)S(1)} %copy-done, ...), custom_call_target="tpu_custom_call" | custom-call | flops 402653184 | bytes 7110656 | tf_op jit(solution)/shard_map/pallas_call | solution.py:93
  66.0 1.9 %collective-permute-done.19.refs_7_.refs_5_ = bf16[192,128]{1,0:T(8,128)(2,1)S(1)} collective-permute-done((bf16[192,128]{1,0:T(8,128)(2,1)S(1)}, bf16[192,128]{1,0:T(8,128)(2,1)S(1)}, u32[]{:S(2)}, u32[]{:S(2)}) %collective-permute-start.19) | collective-permute-done | bytes 49184 | tf_op jit(solution)/shard_map/ppermute | solution.py:365
  68.0 1.1 %shard_map.99 = bf16[192,128]{1,0:T(8,128)(2,1)S(1)} custom-call(s32[3]{0:T(128)S(1)} %pad_add_fusion.1.refs_0_, bf16[96,4096]{1,0:T(8,128)(2,1)S(1)} %copy-done.1, bf16[96,4096]{1,0:T(8,128)(2,1)S(1)} %collective-permute-done.refs_5_.refs_2_, bf16[128,1024]{1,0:T(8,128)(2,1)S(1)} %collective-permute-done.16.refs_3_.refs_4_, ...), custom_call_target="tpu_custom_call" | custom-call | flops 100663296 | bytes 2244608 | tf_op jit(solution)/shard_map/pallas_call | solution.py:93
  69.8 4.8 %collective-permute-done.20.refs_10_.refs_4_ = bf16[192,128]{1,0:T(8,128)(2,1)S(1)} collective-permute-done((bf16[192,128]{1,0:T(8,128)(2,1)S(1)}, bf16[192,128]{1,0:T(8,128)(2,1)S(1)}, u32[]{:S(2)}, u32[]{:S(2)}) %collective-permute-start.20) | collective-permute-done | bytes 49184 | tf_op jit(solution)/shard_map/ppermute | solution.py:365
  74.6 2.3 %shard_map.100 = (f32[96,2048]{1,0:T(8,128)S(1)}, f32[96,2048]{1,0:T(8,128)S(1)}) custom-call(s32[3]{0:T(128)S(1)} %pad_add_fusion.1.refs_0_, bf16[256,4096]{1,0:T(8,128)(2,1)S(1)} %copy-done, bf16[128,2048]{1,0:T(8,128)(2,1)S(1)} %collective-permute-done.14.refs_3_.refs_2_, bf16[128,2048]{1,0:T(8,128)(2,1)} %collective-permute-done.15.refs_4_.refs_3_, ...), custom_call_target="tpu_custom_call" | custom-call | flops 402653184 | bytes 5439488 | tf_op jit(solution)/shard_map/pallas_call | solution.py:93
  77.5 1.8 %collective-permute-done.25.refs_8_ = bf16[192,128]{1,0:T(8,128)(2,1)S(1)} collective-permute-done((bf16[192,128]{1,0:T(8,128)(2,1)S(1)}, bf16[192,128]{1,0:T(8,128)(2,1)S(1)}, u32[]{:S(2)}, u32[]{:S(2)}) %collective-permute-start.25) | collective-permute-done | bytes 49184 | tf_op jit(solution)/shard_map/ppermute | solution.py:365
  79.3 0.8 shard_map.102
  80.7 0.7 collective-permute-done.27.refs_2_
  81.5 1.6 %collective-permute-start.28 = (f32[128,128]{1,0:T(8,128)S(1)}, f32[128,128]{1,0:T(8,128)S(1)}, u32[]{:S(2)}, u32[]{:S(2)}) collective-permute-start(f32[128,128]{1,0:T(8,128)S(1)} %add.15.refs_10_), channel_id=1, source_target_pairs={{0,8},{1,9},{2,10},{3,11},{4,12},{5,13},{6,14},{7,15},{8,0},{9,1},... | collective-permute-start | bytes 196616 | tf_op jit(solution)/shard_map/ppermute | solution.py:365
  83.0 1.0 %collective-permute-start.29 = (f32[128,128]{1,0:T(8,128)S(1)}, f32[128,128]{1,0:T(8,128)S(1)}, u32[]{:S(2)}, u32[]{:S(2)}) collective-permute-start(f32[128,128]{1,0:T(8,128)S(1)} %add.15.refs_10_), channel_id=1, source_target_pairs={{0,16},{1,17},{2,18},{3,19},{4,20},{5,21},{6,22},{7,23},{8,24},{9,... | collective-permute-start | bytes 196616 | tf_op jit(solution)/shard_map/ppermute | solution.py:365
  84.1 1.0 %collective-permute-start.30 = (f32[128,128]{1,0:T(8,128)S(1)}, f32[128,128]{1,0:T(8,128)S(1)}, u32[]{:S(2)}, u32[]{:S(2)}) collective-permute-start(f32[128,128]{1,0:T(8,128)S(1)} %add.15.refs_10_), channel_id=1, source_target_pairs={{0,24},{1,25},{2,26},{3,27},{4,28},{5,29},{6,30},{7,31},{8,16},{9,... | collective-permute-start | bytes 196616 | tf_op jit(solution)/shard_map/ppermute | solution.py:365
  85.1 2.9 %shard_map.103 = (bf16[384,256]{1,0:T(8,128)(2,1)}, f32[384,256]{1,0:T(8,128)S(1)}, f32[384,256]{1,0:T(8,128)S(1)}) custom-call(s32[3]{0:T(128)S(1)} %pad_add_fusion.2.refs_1_.refs_0_, bf16[384,256]{1,0:T(8,128)(2,1)S(1)} %copy-done.7, bf16[384,256]{1,0:T(8,128)(2,1)S(1)} %copy-done.9, bf16[384,256]{1,0:T(8,128)(2,1)S(1)} %copy-done.11, ...), custom_call_target="tpu_custom_call" | custom-call | flops 528482304 | bytes 3473408 | tf_op jit(solution)/shard_map/pallas_call | solution.py:93
  88.1 1.2 %collective-permute-done.30.refs_5_ = f32[128,128]{1,0:T(8,128)S(1)} collective-permute-done((f32[128,128]{1,0:T(8,128)S(1)}, f32[128,128]{1,0:T(8,128)S(1)}, u32[]{:S(2)}, u32[]{:S(2)}) %collective-permute-start.30) | collective-permute-done | bytes 65568 | tf_op jit(solution)/shard_map/ppermute | solution.py:365
  90.0 1.6 %shard_map.101 = (bf16[96,4096]{1,0:T(8,128)(2,1)}, f32[8,128]{1,0:T(8,128)S(1)}) custom-call(s32[2]{0:T(128)S(1)} %pad_add_fusion.refs_0_, f32[96,2048]{1,0:T(8,128)S(1)} %get-tuple-element.56.refs_1_, f32[96,2048]{1,0:T(8,128)S(1)} %collective-permute-done.13.refs_2_, f32[96,2048]{1,0:T(8,128)S(1)} %get-tuple-element.65.refs_3_, ...), custom_call_target="tpu_custom_call" | custom-call | flops 1 | bytes 3936256 | tf_op jit(solution)/shard_map/pallas_call | solution.py:93
  91.5 1.6 %shard_map.105 = (bf16[384,256]{1,0:T(8,128)(2,1)}, bf16[384,256]{1,0:T(8,128)(2,1)}) custom-call(s32[3]{0:T(128)S(1)} %pad_add_fusion.2.refs_1_.refs_0_, bf16[384,256]{1,0:T(8,128)(2,1)S(1)} %copy-done.9, bf16[384,256]{1,0:T(8,128)(2,1)S(1)} %copy-done.11, f32[384,256]{1,0:T(8,128)S(1)} %get-tuple-element.77.refs_6_.refs_3_, ...), custom_call_target="tpu_custom_call" | custom-call | flops 1 | bytes 1703936 | tf_op jit(solution)/shard_map/pallas_call | solution.py:93
  (103 shorter events, 10.1 us)
Async XLA Ops:
  0.6 7.2 %collective-permute-start = (bf16[96,4096]{1,0:T(8,128)(2,1)}, bf16[96,4096]{1,0:T(8,128)(2,1)S(1)}, u32[]{:S(2)}, u32[]{:S(2)}) collective-permute-start(bf16[96,4096]{1,0:T(8,128)(2,1)} %refs_1_.11), channel_id=1, source_target_pairs={{0,4},{1,5},{2,6},{3,7},{4,0},{5,1},{6,2},{7,3},{8,12},{9,13},{10,... | collective-permute-start | bytes 2359304 | tf_op jit(solution)/shard_map/ppermute | solution.py:365
  3.1 49.1 %copy-start = (bf16[256,4096]{1,0:T(8,128)(2,1)S(1)}, bf16[256,4096]{1,0:T(8,128)(2,1)}, u32[]{:S(2)}) copy-start(bf16[256,4096]{1,0:T(8,128)(2,1)} %refs_1_.12) | copy-start | bytes 6291460
  3.1 18.2 %collective-permute-start.1 = (bf16[128,2048]{1,0:T(8,128)(2,1)}, bf16[128,2048]{1,0:T(8,128)(2,1)S(1)}, u32[]{:S(2)}, u32[]{:S(2)}) collective-permute-start(bf16[128,2048]{1,0:T(8,128)(2,1)} %dynamic_slice.3), channel_id=1, source_target_pairs={{0,1},{1,2},{2,3},{3,0},{4,5},{5,6},{6,7},{7,4},{8,9},{9,10},{10,1... | collective-permute-start | bytes 1572872 | tf_op jit(solution)/shard_map/ppermute | solution.py:365
  5.7 25.6 %collective-permute-start.2 = (bf16[128,2048]{1,0:T(8,128)(2,1)}, bf16[128,2048]{1,0:T(8,128)(2,1)}, u32[]{:S(2)}, u32[]{:S(2)}) collective-permute-start(bf16[128,2048]{1,0:T(8,128)(2,1)} %dynamic_slice.3), channel_id=1, source_target_pairs={{0,3},{1,0},{2,1},{3,2},{4,7},{5,4},{6,5},{7,6},{8,11},{9,8},{10,9... | collective-permute-start | bytes 1572872 | tf_op jit(solution)/shard_map/ppermute | solution.py:365
  16.4 1.3 %copy-start.27 = (f32[384,128]{1,0:T(8,128)}, f32[384,128]{1,0:T(8,128)S(1)}, u32[]{:S(2)}) copy-start(f32[384,128]{1,0:T(8,128)S(1)} %get-tuple-element.51) | copy-start | bytes 589828
  16.5 1.3 %copy-start.28 = (bf16[384,128]{1,0:T(8,128)(2,1)}, bf16[384,128]{1,0:T(8,128)(2,1)S(1)}, u32[]{:S(2)}) copy-start(bf16[384,128]{1,0:T(8,128)(2,1)S(1)} %get-tuple-element.49) | copy-start | bytes 294916
  16.5 1.3 %collective-permute-start.3 = (f32[128,128]{1,0:T(8,128)S(1)}, f32[128,128]{1,0:T(8,128)S(1)}, u32[]{:S(2)}, u32[]{:S(2)}) collective-permute-start(f32[128,128]{1,0:T(8,128)S(1)} %get-tuple-element.44), channel_id=1, source_target_pairs={{0,4},{1,5},{2,6},{3,7},{4,0},{5,1},{6,2},{7,3},{8,12},{9,13},{10,... | collective-permute-start | bytes 196616 | tf_op jit(solution)/shard_map/ppermute | solution.py:365
  17.7 13.5 %copy-start.12 = (f32[128,128]{1,0:T(8,128)}, f32[128,128]{1,0:T(8,128)S(1)}, u32[]{:S(2)}) copy-start(f32[128,128]{1,0:T(8,128)S(1)} %collective-permute-done.3.refs_2_) | copy-start | bytes 196612
  17.7 13.5 %collective-permute-start.4 = (f32[128,128]{1,0:T(8,128)S(1)}, f32[128,128]{1,0:T(8,128)}, u32[]{:S(2)}, u32[]{:S(2)}) collective-permute-start(f32[128,128]{1,0:T(8,128)S(1)} %add.14), channel_id=1, source_target_pairs={{0,8},{1,9},{2,10},{3,11},{4,12},{5,13},{6,14},{7,15},{8,0},{9,1},... | collective-permute-start | bytes 196616 | tf_op jit(solution)/shard_map/ppermute | solution.py:365
  19.5 11.7 %collective-permute-start.5 = (f32[128,128]{1,0:T(8,128)S(1)}, f32[128,128]{1,0:T(8,128)}, u32[]{:S(2)}, u32[]{:S(2)}) collective-permute-start(f32[128,128]{1,0:T(8,128)S(1)} %add.14), channel_id=1, source_target_pairs={{0,16},{1,17},{2,18},{3,19},{4,20},{5,21},{6,22},{7,23},{8,24},{9,... | collective-permute-start | bytes 196616 | tf_op jit(solution)/shard_map/ppermute | solution.py:365
  21.0 10.2 %collective-permute-start.6 = (f32[128,128]{1,0:T(8,128)S(1)}, f32[128,128]{1,0:T(8,128)}, u32[]{:S(2)}, u32[]{:S(2)}) collective-permute-start(f32[128,128]{1,0:T(8,128)S(1)} %add.14), channel_id=1, source_target_pairs={{0,24},{1,25},{2,26},{3,27},{4,28},{5,29},{6,30},{7,31},{8,16},{9,... | collective-permute-start | bytes 196616 | tf_op jit(solution)/shard_map/ppermute | solution.py:365
  21.3 10.0 %copy-start.2 = (bf16[128,2048]{1,0:T(8,128)(2,1)}, bf16[128,2048]{1,0:T(8,128)(2,1)S(1)}, u32[]{:S(2)}) copy-start(bf16[128,2048]{1,0:T(8,128)(2,1)S(1)} %collective-permute-done.1.refs_0_) | copy-start | bytes 1572868
  31.3 25.8 %collective-permute-start.7 = (bf16[128,2048]{1,0:T(8,128)(2,1)}, bf16[128,2048]{1,0:T(8,128)(2,1)}, u32[]{:S(2)}, u32[]{:S(2)}) collective-permute-start(bf16[128,2048]{1,0:T(8,128)(2,1)} %get-tuple-element.46.refs_4_), channel_id=1, source_target_pairs={{0,1},{1,2},{2,3},{3,0},{4,5},{5,6},{6,7},{7,4},{8,9},{9,10},{10,1... | collective-permute-start | bytes 1572872 | tf_op jit(solution)/shard_map/ppermute | solution.py:365
  32.5 24.7 %collective-permute-start.14 = (bf16[128,2048]{1,0:T(8,128)(2,1)}, bf16[128,2048]{1,0:T(8,128)(2,1)S(1)}, u32[]{:S(2)}, u32[]{:S(2)}) collective-permute-start(bf16[128,2048]{1,0:T(8,128)(2,1)} %get-tuple-element.46.refs_4_), channel_id=1, source_target_pairs={{0,8},{1,9},{2,10},{3,11},{4,12},{5,13},{6,14},{7,15},{8,0},{9,1},... | collective-permute-start | bytes 1572872 | tf_op jit(solution)/shard_map/ppermute | solution.py:365
  34.0 23.2 %collective-permute-start.15 = (bf16[128,2048]{1,0:T(8,128)(2,1)}, bf16[128,2048]{1,0:T(8,128)(2,1)}, u32[]{:S(2)}, u32[]{:S(2)}) collective-permute-start(bf16[128,2048]{1,0:T(8,128)(2,1)} %get-tuple-element.47.refs_6_.refs_5_), channel_id=1, source_target_pairs={{0,16},{1,17},{2,18},{3,19},{4,20},{5,21},{6,22},{7,23},{8,24},{9,... | collective-permute-start | bytes 1572872 | tf_op jit(solution)/shard_map/ppermute | solution.py:365
  35.5 1.9 %collective-permute-start.9 = (f32[384,128]{1,0:T(8,128)}, f32[384,128]{1,0:T(8,128)}, u32[]{:S(2)}, u32[]{:S(2)}) collective-permute-start(f32[384,128]{1,0:T(8,128)} %copy-done.27), channel_id=1, source_target_pairs={{0,4},{1,5},{2,6},{3,7},{4,0},{5,1},{6,2},{7,3},{8,12},{9,13},{10,... | collective-permute-start | bytes 589832 | tf_op jit(solution)/shard_map/ppermute | solution.py:365
  35.5 1.7 %collective-permute-start.8 = (bf16[384,128]{1,0:T(8,128)(2,1)}, bf16[384,128]{1,0:T(8,128)(2,1)S(1)}, u32[]{:S(2)}, u32[]{:S(2)}) collective-permute-start(bf16[384,128]{1,0:T(8,128)(2,1)} %copy-done.28), channel_id=1, source_target_pairs={{0,4},{1,5},{2,6},{3,7},{4,0},{5,1},{6,2},{7,3},{8,12},{9,13},{10,... | collective-permute-start | bytes 294920 | tf_op jit(solution)/shard_map/ppermute | solution.py:365
  45.1 6.3 %collective-permute-start.10 = (bf16[192,128]{1,0:T(8,128)(2,1)}, bf16[192,128]{1,0:T(8,128)(2,1)S(1)}, u32[]{:S(2)}, u32[]{:S(2)}) collective-permute-start(bf16[192,128]{1,0:T(8,128)(2,1)} %get-tuple-element.53), channel_id=1, source_target_pairs={{0,1},{1,2},{2,3},{3,0},{4,5},{5,6},{6,7},{7,4},{8,9},{9,10},{10,1... | collective-permute-start | bytes 147464 | tf_op jit(solution)/shard_map/ppermute | solution.py:365
  46.4 10.7 %collective-permute-start.11 = (bf16[192,128]{1,0:T(8,128)(2,1)}, bf16[192,128]{1,0:T(8,128)(2,1)S(1)}, u32[]{:S(2)}, u32[]{:S(2)}) collective-permute-start(bf16[192,128]{1,0:T(8,128)(2,1)} %copy-done.32), channel_id=1, source_target_pairs={{0,2},{1,3},{2,0},{3,1},{4,6},{5,7},{6,4},{7,5},{8,10},{9,11},{10,... | collective-permute-start | bytes 147464 | tf_op jit(solution)/shard_map/ppermute | solution.py:365
  51.4 5.7 %collective-permute-start.12 = (bf16[192,128]{1,0:T(8,128)(2,1)}, bf16[192,128]{1,0:T(8,128)(2,1)S(1)}, u32[]{:S(2)}, u32[]{:S(2)}) collective-permute-start(bf16[192,128]{1,0:T(8,128)(2,1)} %copy-done.31), channel_id=1, source_target_pairs={{0,3},{1,0},{2,1},{3,2},{4,7},{5,4},{6,5},{7,6},{8,11},{9,8},{10,9... | collective-permute-start | bytes 147464 | tf_op jit(solution)/shard_map/ppermute | solution.py:365
  52.2 1.1 %copy-start.1 = (bf16[96,4096]{1,0:T(8,128)(2,1)S(1)}, bf16[96,4096]{1,0:T(8,128)(2,1)}, u32[]{:S(2)}) copy-start(bf16[96,4096]{1,0:T(8,128)(2,1)} %refs_1_.11) | copy-start | bytes 2359300
  57.1 5.6 %copy-start.4 = (bf16[128,2048]{1,0:T(8,128)(2,1)S(1)}, bf16[128,2048]{1,0:T(8,128)(2,1)}, u32[]{:S(2)}) copy-start(bf16[128,2048]{1,0:T(8,128)(2,1)} %get-tuple-element.46.refs_4_) | copy-start | bytes 1572868
  57.1 5.6 %copy-start.21 = (bf16[192,128]{1,0:T(8,128)(2,1)S(1)}, bf16[192,128]{1,0:T(8,128)(2,1)}, u32[]{:S(2)}) copy-start(bf16[192,128]{1,0:T(8,128)(2,1)} %copy-done.20) | copy-start | bytes 147460
  59.6 8.4 %collective-permute-start.16 = (bf16[128,1024]{1,0:T(8,128)(2,1)S(1)}, bf16[128,1024]{1,0:T(8,128)(2,1)S(1)}, u32[]{:S(2)}, u32[]{:S(2)}) collective-permute-start(bf16[128,1024]{1,0:T(8,128)(2,1)S(1)} %get-tuple-element.59), channel_id=1, source_target_pairs={{0,8},{1,9},{2,10},{3,11},{4,12},{5,13},{6,14},{7,15},{8,0},{9,1},... | collective-permute-start | bytes 786440 | tf_op jit(solution)/shard_map/ppermute | solution.py:365
  60.2 7.8 %collective-permute-start.17 = (bf16[128,1024]{1,0:T(8,128)(2,1)S(1)}, bf16[128,1024]{1,0:T(8,128)(2,1)S(1)}, u32[]{:S(2)}, u32[]{:S(2)}) collective-permute-start(bf16[128,1024]{1,0:T(8,128)(2,1)S(1)} %get-tuple-element.60), channel_id=1, source_target_pairs={{0,16},{1,17},{2,18},{3,19},{4,20},{5,21},{6,22},{7,23},{8,24},{9,... | collective-permute-start | bytes 786440 | tf_op jit(solution)/shard_map/ppermute | solution.py:365
  60.7 4.8 %collective-permute-start.18 = (bf16[192,128]{1,0:T(8,128)(2,1)S(1)}, bf16[192,128]{1,0:T(8,128)(2,1)S(1)}, u32[]{:S(2)}, u32[]{:S(2)}) collective-permute-start(bf16[192,128]{1,0:T(8,128)(2,1)S(1)} %get-tuple-element.62), channel_id=1, source_target_pairs={{0,3},{1,0},{2,1},{3,2},{4,7},{5,4},{6,5},{7,6},{8,11},{9,8},{10,9... | collective-permute-start | bytes 147464 | tf_op jit(solution)/shard_map/ppermute | solution.py:365
  62.1 5.9 %collective-permute-start.19 = (bf16[192,128]{1,0:T(8,128)(2,1)S(1)}, bf16[192,128]{1,0:T(8,128)(2,1)S(1)}, u32[]{:S(2)}, u32[]{:S(2)}) collective-permute-start(bf16[192,128]{1,0:T(8,128)(2,1)S(1)} %get-tuple-element.63), channel_id=1, source_target_pairs={{0,1},{1,2},{2,3},{3,0},{4,5},{5,6},{6,7},{7,4},{8,9},{9,10},{10,1... | collective-permute-start | bytes 147464 | tf_op jit(solution)/shard_map/ppermute | solution.py:365
  62.7 7.0 %collective-permute-start.21 = (bf16[192,128]{1,0:T(8,128)(2,1)S(1)}, bf16[192,128]{1,0:T(8,128)(2,1)S(1)}, u32[]{:S(2)}, u32[]{:S(2)}) collective-permute-start(bf16[192,128]{1,0:T(8,128)(2,1)S(1)} %get-tuple-element.64.refs_2_), channel_id=1, source_target_pairs={{0,4},{1,5},{2,6},{3,7},{4,0},{5,1},{6,2},{7,3},{8,12},{9,13},{10,... | collective-permute-start | bytes 147464 | tf_op jit(solution)/shard_map/ppermute | solution.py:365
  65.5 4.3 %collective-permute-start.22 = (bf16[192,128]{1,0:T(8,128)(2,1)S(1)}, bf16[192,128]{1,0:T(8,128)(2,1)S(1)}, u32[]{:S(2)}, u32[]{:S(2)}) collective-permute-start(bf16[192,128]{1,0:T(8,128)(2,1)S(1)} %collective-permute-done.18.refs_6_.refs_3_), channel_id=1, source_target_pairs={{0,4},{1,5},{2,6},{3,7},{4,0},{5,1},{6,2},{7,3},{8,12},{9,13},{10,... | collective-permute-start | bytes 147464 | tf_op jit(solution)/shard_map/ppermute | solution.py:365
  67.9 1.8 %collective-permute-start.23 = (bf16[192,128]{1,0:T(8,128)(2,1)S(1)}, bf16[192,128]{1,0:T(8,128)(2,1)S(1)}, u32[]{:S(2)}, u32[]{:S(2)}) collective-permute-start(bf16[192,128]{1,0:T(8,128)(2,1)S(1)} %collective-permute-done.19.refs_7_.refs_5_), channel_id=1, source_target_pairs={{0,4},{1,5},{2,6},{3,7},{4,0},{5,1},{6,2},{7,3},{8,12},{9,13},{10,... | collective-permute-start | bytes 147464 | tf_op jit(solution)/shard_map/ppermute | solution.py:365
  69.0 10.3 %copy-start.7 = (bf16[384,256]{1,0:T(8,128)(2,1)S(1)}, bf16[384,256]{1,0:T(8,128)(2,1)}, u32[]{:S(2)}) copy-start(bf16[384,256]{1,0:T(8,128)(2,1)} %refs_1_.14) | copy-start | bytes 589828
  69.0 5.6 %collective-permute-start.20 = (bf16[192,128]{1,0:T(8,128)(2,1)S(1)}, bf16[192,128]{1,0:T(8,128)(2,1)S(1)}, u32[]{:S(2)}, u32[]{:S(2)}) collective-permute-start(bf16[192,128]{1,0:T(8,128)(2,1)S(1)} %shard_map.99), channel_id=1, source_target_pairs={{0,2},{1,3},{2,0},{3,1},{4,6},{5,7},{6,4},{7,5},{8,10},{9,11},{10,... | collective-permute-start | bytes 147464 | tf_op jit(solution)/shard_map/ppermute | solution.py:365
  69.1 11.2 %copy-start.30 = (f32[128,128]{1,0:T(8,128)S(1)}, f32[128,128]{1,0:T(8,128)}, u32[]{:S(2)}) copy-start(f32[128,128]{1,0:T(8,128)} %copy-done.29) | copy-start | bytes 196612
  69.1 16.0 %copy-start.9 = (bf16[384,256]{1,0:T(8,128)(2,1)S(1)}, bf16[384,256]{1,0:T(8,128)(2,1)}, u32[]{:S(2)}) copy-start(bf16[384,256]{1,0:T(8,128)(2,1)} %refs_1_.15) | copy-start | bytes 589828
  69.1 16.0 %copy-start.11 = (bf16[384,256]{1,0:T(8,128)(2,1)S(1)}, bf16[384,256]{1,0:T(8,128)(2,1)}, u32[]{:S(2)}) copy-start(bf16[384,256]{1,0:T(8,128)(2,1)} %refs_2_.5) | copy-start | bytes 589828
  69.1 16.0 %copy-start.15 = (bf16[2,384,384]{2,1,0:T(8,128)(2,1)S(1)}, bf16[2,384,384]{2,1,0:T(8,128)(2,1)}, u32[]{:S(2)}) copy-start(bf16[2,384,384]{2,1,0:T(8,128)(2,1)} %copy-done.14) | copy-start | bytes 1769476
  69.2 16.0 %copy-start.17 = (bf16[2,384,384]{2,1,0:T(8,128)(2,1)S(1)}, bf16[2,384,384]{2,1,0:T(8,128)(2,1)}, u32[]{:S(2)}) copy-start(bf16[2,384,384]{2,1,0:T(8,128)(2,1)} %copy-done.16) | copy-start | bytes 1769476
  69.2 16.0 %copy-start.19 = (f32[384,256]{1,0:T(8,128)S(1)}, f32[384,256]{1,0:T(8,128)}, u32[]{:S(2)}) copy-start(f32[384,256]{1,0:T(8,128)} %copy-done.18) | copy-start | bytes 1179652
  69.2 16.0 %copy-start.25 = (f32[128,128]{1,0:T(8,128)S(1)}, f32[128,128]{1,0:T(8,128)}, u32[]{:S(2)}) copy-start(f32[128,128]{1,0:T(8,128)} %copy-done.24) | copy-start | bytes 196612
  69.2 20.8 %collective-permute-start.13 = (f32[96,2048]{1,0:T(8,128)S(1)}, f32[96,2048]{1,0:T(8,128)S(1)}, u32[]{:S(2)}, u32[]{:S(2)}) collective-permute-start(f32[96,2048]{1,0:T(8,128)S(1)} %get-tuple-element.57), channel_id=1, source_target_pairs={{0,4},{1,5},{2,6},{3,7},{4,0},{5,1},{6,2},{7,3},{8,12},{9,13},{10,... | collective-permute-start | bytes 2359304 | tf_op jit(solution)/shard_map/ppermute | solution.py:365
  76.9 13.1 %collective-permute-start.24 = (f32[96,2048]{1,0:T(8,128)S(1)}, f32[96,2048]{1,0:T(8,128)S(1)}, u32[]{:S(2)}, u32[]{:S(2)}) collective-permute-start(f32[96,2048]{1,0:T(8,128)S(1)} %get-tuple-element.66), channel_id=1, source_target_pairs={{0,4},{1,5},{2,6},{3,7},{4,0},{5,1},{6,2},{7,3},{8,12},{9,13},{10,... | collective-permute-start | bytes 2359304 | tf_op jit(solution)/shard_map/ppermute | solution.py:365
  77.0 2.3 %collective-permute-start.25 = (bf16[192,128]{1,0:T(8,128)(2,1)S(1)}, bf16[192,128]{1,0:T(8,128)(2,1)S(1)}, u32[]{:S(2)}, u32[]{:S(2)}) collective-permute-start(bf16[192,128]{1,0:T(8,128)(2,1)S(1)} %collective-permute-done.20.refs_10_.refs_4_), channel_id=1, source_target_pairs={{0,4},{1,5},{2,6},{3,7},{4,0},{5,1},{6,2},{7,3},{8,12},{9,13},{10,... | collective-permute-start | bytes 147464 | tf_op jit(solution)/shard_map/ppermute | solution.py:365
  80.1 1.3 %collective-permute-start.27 = (f32[128,128]{1,0:T(8,128)S(1)}, f32[128,128]{1,0:T(8,128)S(1)}, u32[]{:S(2)}, u32[]{:S(2)}) collective-permute-start(f32[128,128]{1,0:T(8,128)S(1)} %get-tuple-element.75), channel_id=1, source_target_pairs={{0,4},{1,5},{2,6},{3,7},{4,0},{5,1},{6,2},{7,3},{8,12},{9,13},{10,... | collective-permute-start | bytes 196616 | tf_op jit(solution)/shard_map/ppermute | solution.py:365
  80.3 3.7 %collective-permute-start.26 = (f32[128,128]{1,0:T(8,128)S(1)}, f32[128,128]{1,0:T(8,128)S(1)}, u32[]{:S(2)}, u32[]{:S(2)}) collective-permute-start(f32[128,128]{1,0:T(8,128)S(1)} %copy-done.30), channel_id=1, source_target_pairs={{0,4},{1,5},{2,6},{3,7},{4,0},{5,1},{6,2},{7,3},{8,12},{9,13},{10,... | collective-permute-start | bytes 196616 | tf_op jit(solution)/shard_map/ppermute | solution.py:365
  81.5 6.6 %collective-permute-start.28 = (f32[128,128]{1,0:T(8,128)S(1)}, f32[128,128]{1,0:T(8,128)S(1)}, u32[]{:S(2)}, u32[]{:S(2)}) collective-permute-start(f32[128,128]{1,0:T(8,128)S(1)} %add.15.refs_10_), channel_id=1, source_target_pairs={{0,8},{1,9},{2,10},{3,11},{4,12},{5,13},{6,14},{7,15},{8,0},{9,1},... | collective-permute-start | bytes 196616 | tf_op jit(solution)/shard_map/ppermute | solution.py:365
  83.0 5.1 %collective-permute-start.29 = (f32[128,128]{1,0:T(8,128)S(1)}, f32[128,128]{1,0:T(8,128)S(1)}, u32[]{:S(2)}, u32[]{:S(2)}) collective-permute-start(f32[128,128]{1,0:T(8,128)S(1)} %add.15.refs_10_), channel_id=1, source_target_pairs={{0,16},{1,17},{2,18},{3,19},{4,20},{5,21},{6,22},{7,23},{8,24},{9,... | collective-permute-start | bytes 196616 | tf_op jit(solution)/shard_map/ppermute | solution.py:365
  84.1 5.2 %collective-permute-start.30 = (f32[128,128]{1,0:T(8,128)S(1)}, f32[128,128]{1,0:T(8,128)S(1)}, u32[]{:S(2)}, u32[]{:S(2)}) collective-permute-start(f32[128,128]{1,0:T(8,128)S(1)} %add.15.refs_10_), channel_id=1, source_target_pairs={{0,24},{1,25},{2,26},{3,27},{4,28},{5,29},{6,30},{7,31},{8,16},{9,... | collective-permute-start | bytes 196616 | tf_op jit(solution)/shard_map/ppermute | solution.py:365
  89.8 1.7 %collective-permute-start.31 = (f32[128,128]{1,0:T(8,128)S(1)}, f32[128,128]{1,0:T(8,128)S(1)}, u32[]{:S(2)}, u32[]{:S(2)}) collective-permute-start(f32[128,128]{1,0:T(8,128)S(1)} %get-tuple-element.80), channel_id=1, source_target_pairs={{0,4},{1,5},{2,6},{3,7},{4,0},{5,1},{6,2},{7,3},{8,12},{9,13},{10,... | collective-permute-start | bytes 196616 | tf_op jit(solution)/shard_map/ppermute | solution.py:365
  (17 other events, 13.4 us)

commit v11 on v9

--- a/solution.py
+++ b/solution.py
@@ -419,11 +419,13 @@
         [mate_cotangent],
         flops=7 * square,
     )
+    far, other_pre = send(far, 1, 0), send(other_pre, 1, 0)
+    (mine,) = hold([mine], [far, other_pre])
     flags, parts, total = exchange(mine, other, core, chip, chips, False)
     *attn, keep, back = call(
         functools.partial(attn_kernel, scale, count),
         [tokens] * count + pair,
-        [*parts, query, send(far, 1, 0), pre, send(other_pre, 1, 0)],
+        [*parts, query, far, pre, other_pre],
         [flags, where],
     )
     linear = [keep, send(back, 1, 0)]
@@ -512,7 +514,6 @@
             fetch((DH, wide), (arrived[2], all_of, all_of)),
         ],
         [spots],
-        attn[1:],
         room=16,
         flops=product,
     )

time: 95.9 us -> 94.9 us (0.990)
  starting transfers between devices: 31.2 us -> 24.4 us
  waiting for transfers between devices: 22.3 us -> 25.5 us
  local copies, waits for them, and re-layouts: 17.1 us -> 19.4 us
    ppermute x32, starting transfers between devices: 31.2 us -> 24.4 us  [send(): return lax.ppermute(x, ('ctx', 'head'), pairs)]
    ppermute x32, waiting for transfers between devices: 22.3 us -> 25.5 us  [send(): return lax.ppermute(x, ('ctx', 'head'), pairs)]
    unnamed x60 -> x70, local copies, waits for them, and re-layouts: 15.2 us -> 17.5 us
  transfers between devices with their start and end apart: 32 -> 32, of which waited for: 8 -> 11; matrix products, arithmetic and copies ran while one was open for 3% -> 3% of each run, Pallas kernels for 20% -> 20%
where the time goes in v11:
time: 94.9 us; the launch traced here: 94.2 us
  waiting for transfers between devices  25.5 us (27%)
  starting transfers between devices  24.4 us (26%)
  Pallas kernels  22.8 us (24%)
  local copies, waits for them, and re-layouts  19.4 us (20%)
  other arithmetic  1.27 us (1%)
    ppermute x32, waiting for transfers between devices, send(): return lax.ppermute(x, ('ctx', 'head'), pairs)  25.5 us
    ppermute x32, starting transfers between devices, send(): return lax.ppermute(x, ('ctx', 'head'), pairs)  24.4 us
    pallas_call x12, Pallas kernels, call(): pl.pallas_call(kernel, out_shape=[jax.ShapeDtypeStruct(s, t) for s, t in...  22.8 us
    unnamed x70, local copies, waits for them, and re-layouts  17.5 us
  transfers between devices with their start and end apart: 32, of which 11 were waited for; matrix products, arithmetic and copies ran while one was open for 3% of the time, Pallas kernels for 20%

profile of v11, /device:TPU:0, one launch (start us, length us, event | category | flops | bytes accessed | tf_op | source)
XLA Modules:
  0.0 94.2 jit_solution(10319041122594576008)
XLA Ops:
  1.1 1.9 %dynamic_slice.3 = bf16[128,2048]{1,0:T(8,128)(2,1)} dynamic-slice(bf16[256,4096]{1,0:T(8,128)(2,1)} %refs_1_.12, s32[]{:T(128)S(6)} %select_n.6, s32[]{:T(128)S(6)} %select_n.7), dynamic_slice_sizes={128,2048} | dynamic-slice | bytes 1048580 | tf_op jit(solution)/shard_map/dynamic_slice | solution.py:406
  3.0 2.6 %collective-permute-start.1 = (bf16[128,2048]{1,0:T(8,128)(2,1)}, bf16[128,2048]{1,0:T(8,128)(2,1)S(1)}, u32[]{:S(2)}, u32[]{:S(2)}) collective-permute-start(bf16[128,2048]{1,0:T(8,128)(2,1)} %dynamic_slice.3), channel_id=1, source_target_pairs={{0,1},{1,2},{2,3},{3,0},{4,5},{5,6},{6,7},{7,4},{8,9},{9,10},{10,1... | collective-permute-start | bytes 1572872 | tf_op jit(solution)/shard_map/ppermute | solution.py:365
  5.7 2.0 %collective-permute-start.2 = (bf16[128,2048]{1,0:T(8,128)(2,1)}, bf16[128,2048]{1,0:T(8,128)(2,1)}, u32[]{:S(2)}, u32[]{:S(2)}) collective-permute-start(bf16[128,2048]{1,0:T(8,128)(2,1)} %dynamic_slice.3), channel_id=1, source_target_pairs={{0,3},{1,0},{2,1},{3,2},{4,7},{5,4},{6,5},{7,6},{8,11},{9,8},{10,9... | collective-permute-start | bytes 1572872 | tf_op jit(solution)/shard_map/ppermute | solution.py:365
  7.8 0.9 copy-done.5
  8.7 0.9 copy-done.8
  9.6 0.9 copy-done.10
  11.2 2.8 %shard_map.93 = (bf16[2,384,384]{2,1,0:T(8,128)(2,1)S(1)}, bf16[2,384,384]{2,1,0:T(8,128)(2,1)S(1)}, f32[384,256]{1,0:T(8,128)S(1)}, f32[384,128]{1,0:T(8,128)S(...) custom-call(s32[3,3]{1,0:T(4,128)S(1)} %copy-done.26, ...), custom_call_target="tpu_custom_call" | custom-call | flops 264241152 | bytes 2785280 | tf_op jit(solution)/shard_map/pallas_call | solution.py:93
  14.7 0.8 copy-done.14
  15.5 0.9 copy-done.16
  16.3 0.7 copy-done.22
  18.4 1.1 %collective-permute-done.3.refs_1_.refs_8_ = bf16[384,128]{1,0:T(8,128)(2,1)S(1)} collective-permute-done((bf16[384,128]{1,0:T(8,128)(2,1)}, bf16[384,128]{1,0:T(8,128)(2,1)S(1)}, u32[]{:S(2)}, u32[]{:S(2)}) %collective-permute-start.3) | collective-permute-done | bytes 98336 | tf_op jit(solution)/shard_map/ppermute | solution.py:365
  20.2 0.9 add.14
  21.1 1.7 %collective-permute-start.6 = (f32[128,128]{1,0:T(8,128)S(1)}, f32[128,128]{1,0:T(8,128)S(1)}, u32[]{:S(2)}, u32[]{:S(2)}) collective-permute-start(f32[128,128]{1,0:T(8,128)S(1)} %add.14), channel_id=1, source_target_pairs={{0,8},{1,9},{2,10},{3,11},{4,12},{5,13},{6,14},{7,15},{8,0},{9,1},... | collective-permute-start | bytes 196616 | tf_op jit(solution)/shard_map/ppermute | solution.py:365
  22.8 1.5 %collective-permute-start.7 = (f32[128,128]{1,0:T(8,128)S(1)}, f32[128,128]{1,0:T(8,128)S(1)}, u32[]{:S(2)}, u32[]{:S(2)}) collective-permute-start(f32[128,128]{1,0:T(8,128)S(1)} %add.14), channel_id=1, source_target_pairs={{0,16},{1,17},{2,18},{3,19},{4,20},{5,21},{6,22},{7,23},{8,24},{9,... | collective-permute-start | bytes 196616 | tf_op jit(solution)/shard_map/ppermute | solution.py:365
  24.7 0.7 collective-permute-done.6.refs_4_
  25.4 1.6 %collective-permute-done.7.refs_5_ = f32[128,128]{1,0:T(8,128)S(1)} collective-permute-done((f32[128,128]{1,0:T(8,128)S(1)}, f32[128,128]{1,0:T(8,128)S(1)}, u32[]{:S(2)}, u32[]{:S(2)}) %collective-permute-start.7) | collective-permute-done | bytes 65568 | tf_op jit(solution)/shard_map/ppermute | solution.py:365
  27.1 2.4 %collective-permute-done.8.refs_6_ = f32[128,128]{1,0:T(8,128)S(1)} collective-permute-done((f32[128,128]{1,0:T(8,128)S(1)}, f32[128,128]{1,0:T(8,128)S(1)}, u32[]{:S(2)}, u32[]{:S(2)}) %collective-permute-start.8) | collective-permute-done | bytes 65568 | tf_op jit(solution)/shard_map/ppermute | solution.py:365
  29.5 0.9 copy-done.6
  30.4 0.8 copy-done.13
  31.3 0.9 copy-done.21
  32.1 0.9 copy-done.25
  33.1 1.3 %shard_map.95 = (bf16[192,128]{1,0:T(8,128)(2,1)S(1)}, bf16[192,128]{1,0:T(8,128)(2,1)S(1)}, bf16[192,128]{1,0:T(8,128)(2,1)S(1)}, bf16[192,128]{1,0:T(8,128)(2,...) custom-call(s32[4]{0:T(128)S(1)} %add_convert_fusion.refs_0_, s32[3]{0:T(128)S(1)} %pad_add_fusion.2.refs_1_.refs_0_, ...), custom_call_target="tpu_custom_call" | custom-call | flops 1 | bytes 1343488 | tf_op jit(solution)/shard_map/pallas_call | solution.py:93
  37.5 0.8 copy-done.2
  39.4 1.1 %copy-done.1 = bf16[96,4096]{1,0:T(8,128)(2,1)S(1)} copy-done((bf16[96,4096]{1,0:T(8,128)(2,1)S(1)}, bf16[96,4096]{1,0:T(8,128)(2,1)}, u32[]{:S(2)}) %copy-start.1) | copy-done | bytes 786456
  40.5 1.0 %copy-done.3 = bf16[128,2048]{1,0:T(8,128)(2,1)S(1)} copy-done((bf16[128,2048]{1,0:T(8,128)(2,1)S(1)}, bf16[128,2048]{1,0:T(8,128)(2,1)}, u32[]{:S(2)}) %copy-start.3) | copy-done | bytes 524312
  41.6 2.7 %shard_map.98 = (bf16[192,128]{1,0:T(8,128)(2,1)S(1)}, f32[192,256]{1,0:T(8,128)S(1)}) custom-call(s32[3]{0:T(128)S(1)} %pad_add_fusion.1.refs_0_, bf16[96,4096]{1,0:T(8,128)(2,1)S(1)} %copy-done.1, bf16[96,4096]{1,0:T(8,128)(2,1)S(1)} %collective-permute-done.refs_5_.refs_2_, bf16[256,4096]{1,0:T(8,128)(2,1)S(1)} %copy-done, ...), custom_call_target="tpu_custom_call" | custom-call | flops 402653184 | bytes 4964352 | tf_op jit(solution)/shard_map/pallas_call | solution.py:93
  44.3 8.5 %collective-permute-done.9.refs_5_.refs_6_ = bf16[128,2048]{1,0:T(8,128)(2,1)} collective-permute-done((bf16[128,2048]{1,0:T(8,128)(2,1)}, bf16[128,2048]{1,0:T(8,128)(2,1)}, u32[]{:S(2)}, u32[]{:S(2)}) %collective-permute-start.9) | collective-permute-done | bytes 524320 | tf_op jit(solution)/shard_map/ppermute | solution.py:365
  52.9 2.4 %shard_map.99 = (bf16[192,128]{1,0:T(8,128)(2,1)S(1)}, bf16[192,128]{1,0:T(8,128)(2,1)S(1)}, bf16[128,1024]{1,0:T(8,128)(2,1)S(1)}, bf16[128,1024]{1,0:T(8,128)(2,1)S(1)}) custom-call(s32[3]{0:T(128)S(1)} %pad_add_fusion.1.refs_0_, bf16[96,4096]{1,0:T(8,128)(2,1)S(1)} %copy-done.1, bf16[96,4096]{1,0:T(8,128)(2,1)S(1)} %collective-permute-done.refs_5_.refs_2_, ...), custom_call_target="tpu_custom_call" | custom-call | flops 201326592 | bytes 3964928 | tf_op jit(solution)/shard_map/pallas_call | solution.py:93
  57.0 3.0 %collective-permute-start.11 = (bf16[192,128]{1,0:T(8,128)(2,1)S(1)}, bf16[192,128]{1,0:T(8,128)(2,1)S(1)}, u32[]{:S(2)}, u32[]{:S(2)}) collective-permute-start(bf16[192,128]{1,0:T(8,128)(2,1)S(1)} %copy-done.32), channel_id=1, source_target_pairs={{0,2},{1,3},{2,0},{3,1},{4,6},{5,7},{6,4},{7,5},{8,10},{9,11},{10,... | collective-permute-start | bytes 147464 | tf_op jit(solution)/shard_map/ppermute | solution.py:365
  60.0 1.2 %collective-permute-start.12 = (bf16[192,128]{1,0:T(8,128)(2,1)S(1)}, bf16[192,128]{1,0:T(8,128)(2,1)S(1)}, u32[]{:S(2)}, u32[]{:S(2)}) collective-permute-start(bf16[192,128]{1,0:T(8,128)(2,1)S(1)} %copy-done.30), channel_id=1, source_target_pairs={{0,3},{1,0},{2,1},{3,2},{4,7},{5,4},{6,5},{7,6},{8,11},{9,8},{10,9... | collective-permute-start | bytes 147464 | tf_op jit(solution)/shard_map/ppermute | solution.py:365
  61.2 1.2 %collective-permute-done.10.refs_8_.refs_7_ = bf16[192,128]{1,0:T(8,128)(2,1)S(1)} collective-permute-done((bf16[192,128]{1,0:T(8,128)(2,1)S(1)}, bf16[192,128]{1,0:T(8,128)(2,1)S(1)}, u32[]{:S(2)}, u32[]{:S(2)}) %collective-permute-start.10) | collective-permute-done | bytes 49184 | tf_op jit(solution)/shard_map/ppermute | solution.py:365
  62.4 1.1 %collective-permute-start.18 = (bf16[192,128]{1,0:T(8,128)(2,1)S(1)}, bf16[192,128]{1,0:T(8,128)(2,1)S(1)}, u32[]{:S(2)}, u32[]{:S(2)}) collective-permute-start(bf16[192,128]{1,0:T(8,128)(2,1)S(1)} %get-tuple-element.60), channel_id=1, source_target_pairs={{0,3},{1,0},{2,1},{3,2},{4,7},{5,4},{6,5},{7,6},{8,11},{9,8},{10,9... | collective-permute-start | bytes 147464 | tf_op jit(solution)/shard_map/ppermute | solution.py:365
  63.6 0.9 collective-permute-start.19
  64.5 2.7 %shard_map.97 = (f32[192,128]{1,0:T(8,128)S(1)}, f32[96,2048]{1,0:T(8,128)S(1)}, f32[96,2048]{1,0:T(8,128)S(1)}) custom-call(s32[3]{0:T(128)S(1)} %pad_add_fusion.1.refs_0_, bf16[96,4096]{1,0:T(8,128)(2,1)S(1)} %copy-done.1, bf16[96,4096]{1,0:T(8,128)(2,1)S(1)} %collective-permute-done.refs_5_.refs_2_, bf16[256,4096]{1,0:T(8,128)(2,1)S(1)} %copy-done, ...), custom_call_target="tpu_custom_call" | custom-call | flops 402653184 | bytes 7110656 | tf_op jit(solution)/shard_map/pallas_call | solution.py:93
  67.8 1.7 %collective-permute-done.19.refs_7_.refs_5_ = bf16[192,128]{1,0:T(8,128)(2,1)S(1)} collective-permute-done((bf16[192,128]{1,0:T(8,128)(2,1)S(1)}, bf16[192,128]{1,0:T(8,128)(2,1)S(1)}, u32[]{:S(2)}, u32[]{:S(2)}) %collective-permute-start.19) | collective-permute-done | bytes 49184 | tf_op jit(solution)/shard_map/ppermute | solution.py:365
  69.5 1.1 %shard_map.100 = bf16[192,128]{1,0:T(8,128)(2,1)S(1)} custom-call(s32[3]{0:T(128)S(1)} %pad_add_fusion.1.refs_0_, bf16[96,4096]{1,0:T(8,128)(2,1)S(1)} %copy-done.1, bf16[96,4096]{1,0:T(8,128)(2,1)S(1)} %collective-permute-done.refs_5_.refs_2_, bf16[128,1024]{1,0:T(8,128)(2,1)S(1)} %collective-permute-done.16.refs_3_.refs_4_, ...), custom_call_target="tpu_custom_call" | custom-call | flops 100663296 | bytes 2244608 | tf_op jit(solution)/shard_map/pallas_call | solution.py:93
  71.3 4.4 %collective-permute-done.20.refs_10_.refs_4_ = bf16[192,128]{1,0:T(8,128)(2,1)S(1)} collective-permute-done((bf16[192,128]{1,0:T(8,128)(2,1)S(1)}, bf16[192,128]{1,0:T(8,128)(2,1)S(1)}, u32[]{:S(2)}, u32[]{:S(2)}) %collective-permute-start.20) | collective-permute-done | bytes 49184 | tf_op jit(solution)/shard_map/ppermute | solution.py:365
  75.6 2.3 %shard_map.101 = (f32[96,2048]{1,0:T(8,128)S(1)}, f32[96,2048]{1,0:T(8,128)S(1)}) custom-call(s32[3]{0:T(128)S(1)} %pad_add_fusion.1.refs_0_, bf16[256,4096]{1,0:T(8,128)(2,1)S(1)} %copy-done, bf16[128,2048]{1,0:T(8,128)(2,1)S(1)} %collective-permute-done.14.refs_3_.refs_2_, bf16[128,2048]{1,0:T(8,128)(2,1)} %collective-permute-done.15.refs_4_.refs_3_, ...), custom_call_target="tpu_custom_call" | custom-call | flops 402653184 | bytes 5439488 | tf_op jit(solution)/shard_map/pallas_call | solution.py:93
  78.5 1.8 %collective-permute-done.25.refs_8_ = bf16[192,128]{1,0:T(8,128)(2,1)S(1)} collective-permute-done((bf16[192,128]{1,0:T(8,128)(2,1)S(1)}, bf16[192,128]{1,0:T(8,128)(2,1)S(1)}, u32[]{:S(2)}, u32[]{:S(2)}) %collective-permute-start.25) | collective-permute-done | bytes 49184 | tf_op jit(solution)/shard_map/ppermute | solution.py:365
  80.4 0.8 shard_map.103
  81.8 0.7 collective-permute-done.27.refs_2_
  82.5 1.2 %collective-permute-start.28 = (f32[128,128]{1,0:T(8,128)S(1)}, f32[128,128]{1,0:T(8,128)S(1)}, u32[]{:S(2)}, u32[]{:S(2)}) collective-permute-start(f32[128,128]{1,0:T(8,128)S(1)} %add.15.refs_10_), channel_id=1, source_target_pairs={{0,8},{1,9},{2,10},{3,11},{4,12},{5,13},{6,14},{7,15},{8,0},{9,1},... | collective-permute-start | bytes 196616 | tf_op jit(solution)/shard_map/ppermute | solution.py:365
  83.7 1.4 %collective-permute-start.29 = (f32[128,128]{1,0:T(8,128)S(1)}, f32[128,128]{1,0:T(8,128)S(1)}, u32[]{:S(2)}, u32[]{:S(2)}) collective-permute-start(f32[128,128]{1,0:T(8,128)S(1)} %add.15.refs_10_), channel_id=1, source_target_pairs={{0,16},{1,17},{2,18},{3,19},{4,20},{5,21},{6,22},{7,23},{8,24},{9,... | collective-permute-start | bytes 196616 | tf_op jit(solution)/shard_map/ppermute | solution.py:365
  85.1 1.0 %collective-permute-start.30 = (f32[128,128]{1,0:T(8,128)S(1)}, f32[128,128]{1,0:T(8,128)S(1)}, u32[]{:S(2)}, u32[]{:S(2)}) collective-permute-start(f32[128,128]{1,0:T(8,128)S(1)} %add.15.refs_10_), channel_id=1, source_target_pairs={{0,24},{1,25},{2,26},{3,27},{4,28},{5,29},{6,30},{7,31},{8,16},{9,... | collective-permute-start | bytes 196616 | tf_op jit(solution)/shard_map/ppermute | solution.py:365
  86.2 2.9 %shard_map.104 = (bf16[384,256]{1,0:T(8,128)(2,1)}, f32[384,256]{1,0:T(8,128)S(1)}, f32[384,256]{1,0:T(8,128)S(1)}) custom-call(s32[3]{0:T(128)S(1)} %pad_add_fusion.2.refs_1_.refs_0_, bf16[384,256]{1,0:T(8,128)(2,1)S(1)} %copy-done.7, bf16[384,256]{1,0:T(8,128)(2,1)S(1)} %copy-done.9, bf16[384,256]{1,0:T(8,128)(2,1)S(1)} %copy-done.11, ...), custom_call_target="tpu_custom_call" | custom-call | flops 528482304 | bytes 3473408 | tf_op jit(solution)/shard_map/pallas_call | solution.py:93
  89.1 1.1 %collective-permute-done.30.refs_5_ = f32[128,128]{1,0:T(8,128)S(1)} collective-permute-done((f32[128,128]{1,0:T(8,128)S(1)}, f32[128,128]{1,0:T(8,128)S(1)}, u32[]{:S(2)}, u32[]{:S(2)}) %collective-permute-start.30) | collective-permute-done | bytes 65568 | tf_op jit(solution)/shard_map/ppermute | solution.py:365
  91.0 1.6 %shard_map.102 = (bf16[96,4096]{1,0:T(8,128)(2,1)}, f32[8,128]{1,0:T(8,128)S(1)}) custom-call(s32[2]{0:T(128)S(1)} %pad_add_fusion.refs_0_, f32[96,2048]{1,0:T(8,128)S(1)} %get-tuple-element.54.refs_1_, f32[96,2048]{1,0:T(8,128)S(1)} %collective-permute-done.13.refs_2_, f32[96,2048]{1,0:T(8,128)S(1)} %get-tuple-element.63.refs_3_, ...), custom_call_target="tpu_custom_call" | custom-call | flops 1 | bytes 3936256 | tf_op jit(solution)/shard_map/pallas_call | solution.py:93
  92.6 1.6 %shard_map.106 = (bf16[384,256]{1,0:T(8,128)(2,1)}, bf16[384,256]{1,0:T(8,128)(2,1)}) custom-call(s32[3]{0:T(128)S(1)} %pad_add_fusion.2.refs_1_.refs_0_, bf16[384,256]{1,0:T(8,128)(2,1)S(1)} %copy-done.9, bf16[384,256]{1,0:T(8,128)(2,1)S(1)} %copy-done.11, f32[384,256]{1,0:T(8,128)S(1)} %get-tuple-element.75.refs_6_.refs_3_, ...), custom_call_target="tpu_custom_call" | custom-call | flops 1 | bytes 1703936 | tf_op jit(solution)/shard_map/pallas_call | solution.py:93
  (108 shorter events, 13.5 us)
Async XLA Ops:
  0.6 7.1 %collective-permute-start = (bf16[96,4096]{1,0:T(8,128)(2,1)}, bf16[96,4096]{1,0:T(8,128)(2,1)S(1)}, u32[]{:S(2)}, u32[]{:S(2)}) collective-permute-start(bf16[96,4096]{1,0:T(8,128)(2,1)} %refs_1_.11), channel_id=1, source_target_pairs={{0,4},{1,5},{2,6},{3,7},{4,0},{5,1},{6,2},{7,3},{8,12},{9,13},{10,... | collective-permute-start | bytes 2359304 | tf_op jit(solution)/shard_map/ppermute | solution.py:365
  3.0 36.3 %copy-start = (bf16[256,4096]{1,0:T(8,128)(2,1)S(1)}, bf16[256,4096]{1,0:T(8,128)(2,1)}, u32[]{:S(2)}) copy-start(bf16[256,4096]{1,0:T(8,128)(2,1)} %refs_1_.12) | copy-start | bytes 6291460
  3.0 34.4 %collective-permute-start.1 = (bf16[128,2048]{1,0:T(8,128)(2,1)}, bf16[128,2048]{1,0:T(8,128)(2,1)S(1)}, u32[]{:S(2)}, u32[]{:S(2)}) collective-permute-start(bf16[128,2048]{1,0:T(8,128)(2,1)} %dynamic_slice.3), channel_id=1, source_target_pairs={{0,1},{1,2},{2,3},{3,0},{4,5},{5,6},{6,7},{7,4},{8,9},{9,10},{10,1... | collective-permute-start | bytes 1572872 | tf_op jit(solution)/shard_map/ppermute | solution.py:365
  5.7 31.8 %collective-permute-start.2 = (bf16[128,2048]{1,0:T(8,128)(2,1)}, bf16[128,2048]{1,0:T(8,128)(2,1)}, u32[]{:S(2)}, u32[]{:S(2)}) collective-permute-start(bf16[128,2048]{1,0:T(8,128)(2,1)} %dynamic_slice.3), channel_id=1, source_target_pairs={{0,3},{1,0},{2,1},{3,2},{4,7},{5,4},{6,5},{7,6},{8,11},{9,8},{10,9... | collective-permute-start | bytes 1572872 | tf_op jit(solution)/shard_map/ppermute | solution.py:365
  7.8 0.9 copy-start.5
  17.7 1.8 %collective-permute-start.4 = (f32[384,128]{1,0:T(8,128)}, f32[384,128]{1,0:T(8,128)}, u32[]{:S(2)}, u32[]{:S(2)}) collective-permute-start(f32[384,128]{1,0:T(8,128)} %get-tuple-element.45), channel_id=1, source_target_pairs={{0,4},{1,5},{2,6},{3,7},{4,0},{5,1},{6,2},{7,3},{8,12},{9,13},{10,... | collective-permute-start | bytes 589832 | tf_op jit(solution)/shard_map/ppermute | solution.py:365
  17.9 1.6 %collective-permute-start.3 = (bf16[384,128]{1,0:T(8,128)(2,1)}, bf16[384,128]{1,0:T(8,128)(2,1)S(1)}, u32[]{:S(2)}, u32[]{:S(2)}) collective-permute-start(bf16[384,128]{1,0:T(8,128)(2,1)} %get-tuple-element.44), channel_id=1, source_target_pairs={{0,4},{1,5},{2,6},{3,7},{4,0},{5,1},{6,2},{7,3},{8,12},{9,13},{10,... | collective-permute-start | bytes 294920 | tf_op jit(solution)/shard_map/ppermute | solution.py:365
  18.3 1.9 %collective-permute-start.5 = (f32[128,128]{1,0:T(8,128)}, f32[128,128]{1,0:T(8,128)}, u32[]{:S(2)}, u32[]{:S(2)}) collective-permute-start(f32[128,128]{1,0:T(8,128)} %get-tuple-element.46), channel_id=1, source_target_pairs={{0,4},{1,5},{2,6},{3,7},{4,0},{5,1},{6,2},{7,3},{8,12},{9,13},{10,... | collective-permute-start | bytes 196616 | tf_op jit(solution)/shard_map/ppermute | solution.py:365
  21.1 4.4 %collective-permute-start.6 = (f32[128,128]{1,0:T(8,128)S(1)}, f32[128,128]{1,0:T(8,128)S(1)}, u32[]{:S(2)}, u32[]{:S(2)}) collective-permute-start(f32[128,128]{1,0:T(8,128)S(1)} %add.14), channel_id=1, source_target_pairs={{0,8},{1,9},{2,10},{3,11},{4,12},{5,13},{6,14},{7,15},{8,0},{9,1},... | collective-permute-start | bytes 196616 | tf_op jit(solution)/shard_map/ppermute | solution.py:365
  22.8 4.3 %collective-permute-start.7 = (f32[128,128]{1,0:T(8,128)S(1)}, f32[128,128]{1,0:T(8,128)S(1)}, u32[]{:S(2)}, u32[]{:S(2)}) collective-permute-start(f32[128,128]{1,0:T(8,128)S(1)} %add.14), channel_id=1, source_target_pairs={{0,16},{1,17},{2,18},{3,19},{4,20},{5,21},{6,22},{7,23},{8,24},{9,... | collective-permute-start | bytes 196616 | tf_op jit(solution)/shard_map/ppermute | solution.py:365
  24.3 5.2 %collective-permute-start.8 = (f32[128,128]{1,0:T(8,128)S(1)}, f32[128,128]{1,0:T(8,128)S(1)}, u32[]{:S(2)}, u32[]{:S(2)}) collective-permute-start(f32[128,128]{1,0:T(8,128)S(1)} %add.14), channel_id=1, source_target_pairs={{0,24},{1,25},{2,26},{3,27},{4,28},{5,29},{6,30},{7,31},{8,16},{9,... | collective-permute-start | bytes 196616 | tf_op jit(solution)/shard_map/ppermute | solution.py:365
  38.3 14.6 %collective-permute-start.9 = (bf16[128,2048]{1,0:T(8,128)(2,1)}, bf16[128,2048]{1,0:T(8,128)(2,1)}, u32[]{:S(2)}, u32[]{:S(2)}) collective-permute-start(bf16[128,2048]{1,0:T(8,128)(2,1)} %get-tuple-element.49.refs_4_), channel_id=1, source_target_pairs={{0,1},{1,2},{2,3},{3,0},{4,5},{5,6},{6,7},{7,4},{8,9},{9,10},{10,1... | collective-permute-start | bytes 1572872 | tf_op jit(solution)/shard_map/ppermute | solution.py:365
  38.3 14.6 %collective-permute-start.14 = (bf16[128,2048]{1,0:T(8,128)(2,1)}, bf16[128,2048]{1,0:T(8,128)(2,1)S(1)}, u32[]{:S(2)}, u32[]{:S(2)}) collective-permute-start(bf16[128,2048]{1,0:T(8,128)(2,1)} %get-tuple-element.49.refs_4_), channel_id=1, source_target_pairs={{0,8},{1,9},{2,10},{3,11},{4,12},{5,13},{6,14},{7,15},{8,0},{9,1},... | collective-permute-start | bytes 1572872 | tf_op jit(solution)/shard_map/ppermute | solution.py:365
  38.8 14.1 %collective-permute-start.15 = (bf16[128,2048]{1,0:T(8,128)(2,1)}, bf16[128,2048]{1,0:T(8,128)(2,1)}, u32[]{:S(2)}, u32[]{:S(2)}) collective-permute-start(bf16[128,2048]{1,0:T(8,128)(2,1)} %get-tuple-element.50.refs_6_.refs_5_), channel_id=1, source_target_pairs={{0,16},{1,17},{2,18},{3,19},{4,20},{5,21},{6,22},{7,23},{8,24},{9,... | collective-permute-start | bytes 1572872 | tf_op jit(solution)/shard_map/ppermute | solution.py:365
  39.4 1.1 %copy-start.1 = (bf16[96,4096]{1,0:T(8,128)(2,1)S(1)}, bf16[96,4096]{1,0:T(8,128)(2,1)}, u32[]{:S(2)}) copy-start(bf16[96,4096]{1,0:T(8,128)(2,1)} %refs_1_.11) | copy-start | bytes 2359300
  40.5 1.0 %copy-start.3 = (bf16[128,2048]{1,0:T(8,128)(2,1)S(1)}, bf16[128,2048]{1,0:T(8,128)(2,1)}, u32[]{:S(2)}) copy-start(bf16[128,2048]{1,0:T(8,128)(2,1)} %get-tuple-element.49.refs_4_) | copy-start | bytes 1572868
  44.3 12.1 %copy-start.34 = (bf16[192,128]{1,0:T(8,128)(2,1)S(1)}, bf16[192,128]{1,0:T(8,128)(2,1)}, u32[]{:S(2)}) copy-start(bf16[192,128]{1,0:T(8,128)(2,1)} %copy-done.33) | copy-start | bytes 147460
  44.3 12.7 %copy-start.32 = (bf16[192,128]{1,0:T(8,128)(2,1)S(1)}, bf16[192,128]{1,0:T(8,128)(2,1)}, u32[]{:S(2)}) copy-start(bf16[192,128]{1,0:T(8,128)(2,1)} %copy-done.31) | copy-start | bytes 147460
  44.3 15.7 %copy-start.30 = (bf16[192,128]{1,0:T(8,128)(2,1)S(1)}, bf16[192,128]{1,0:T(8,128)(2,1)}, u32[]{:S(2)}) copy-start(bf16[192,128]{1,0:T(8,128)(2,1)} %copy-done.29) | copy-start | bytes 147460
  44.3 20.1 %copy-start.4 = (bf16[128,2048]{1,0:T(8,128)(2,1)S(1)}, bf16[128,2048]{1,0:T(8,128)(2,1)}, u32[]{:S(2)}) copy-start(bf16[128,2048]{1,0:T(8,128)(2,1)} %get-tuple-element.49.refs_4_) | copy-start | bytes 1572868
  44.3 20.1 %copy-start.19 = (bf16[192,128]{1,0:T(8,128)(2,1)S(1)}, bf16[192,128]{1,0:T(8,128)(2,1)}, u32[]{:S(2)}) copy-start(bf16[192,128]{1,0:T(8,128)(2,1)} %copy-done.18) | copy-start | bytes 147460
  55.3 14.2 %collective-permute-start.16 = (bf16[128,1024]{1,0:T(8,128)(2,1)S(1)}, bf16[128,1024]{1,0:T(8,128)(2,1)S(1)}, u32[]{:S(2)}, u32[]{:S(2)}) collective-permute-start(bf16[128,1024]{1,0:T(8,128)(2,1)S(1)} %get-tuple-element.57), channel_id=1, source_target_pairs={{0,8},{1,9},{2,10},{3,11},{4,12},{5,13},{6,14},{7,15},{8,0},{9,1},... | collective-permute-start | bytes 786440 | tf_op jit(solution)/shard_map/ppermute | solution.py:365
  55.9 13.6 %collective-permute-start.17 = (bf16[128,1024]{1,0:T(8,128)(2,1)S(1)}, bf16[128,1024]{1,0:T(8,128)(2,1)S(1)}, u32[]{:S(2)}, u32[]{:S(2)}) collective-permute-start(bf16[128,1024]{1,0:T(8,128)(2,1)S(1)} %get-tuple-element.58), channel_id=1, source_target_pairs={{0,16},{1,17},{2,18},{3,19},{4,20},{5,21},{6,22},{7,23},{8,24},{9,... | collective-permute-start | bytes 786440 | tf_op jit(solution)/shard_map/ppermute | solution.py:365
  56.4 6.0 %collective-permute-start.10 = (bf16[192,128]{1,0:T(8,128)(2,1)S(1)}, bf16[192,128]{1,0:T(8,128)(2,1)S(1)}, u32[]{:S(2)}, u32[]{:S(2)}) collective-permute-start(bf16[192,128]{1,0:T(8,128)(2,1)S(1)} %copy-done.34), channel_id=1, source_target_pairs={{0,1},{1,2},{2,3},{3,0},{4,5},{5,6},{6,7},{7,4},{8,9},{9,10},{10,1... | collective-permute-start | bytes 147464 | tf_op jit(solution)/shard_map/ppermute | solution.py:365
  57.0 6.6 %collective-permute-start.11 = (bf16[192,128]{1,0:T(8,128)(2,1)S(1)}, bf16[192,128]{1,0:T(8,128)(2,1)S(1)}, u32[]{:S(2)}, u32[]{:S(2)}) collective-permute-start(bf16[192,128]{1,0:T(8,128)(2,1)S(1)} %copy-done.32), channel_id=1, source_target_pairs={{0,2},{1,3},{2,0},{3,1},{4,6},{5,7},{6,4},{7,5},{8,10},{9,11},{10,... | collective-permute-start | bytes 147464 | tf_op jit(solution)/shard_map/ppermute | solution.py:365
  60.0 4.4 %collective-permute-start.12 = (bf16[192,128]{1,0:T(8,128)(2,1)S(1)}, bf16[192,128]{1,0:T(8,128)(2,1)S(1)}, u32[]{:S(2)}, u32[]{:S(2)}) collective-permute-start(bf16[192,128]{1,0:T(8,128)(2,1)S(1)} %copy-done.30), channel_id=1, source_target_pairs={{0,3},{1,0},{2,1},{3,2},{4,7},{5,4},{6,5},{7,6},{8,11},{9,8},{10,9... | collective-permute-start | bytes 147464 | tf_op jit(solution)/shard_map/ppermute | solution.py:365
  62.4 4.8 %collective-permute-start.18 = (bf16[192,128]{1,0:T(8,128)(2,1)S(1)}, bf16[192,128]{1,0:T(8,128)(2,1)S(1)}, u32[]{:S(2)}, u32[]{:S(2)}) collective-permute-start(bf16[192,128]{1,0:T(8,128)(2,1)S(1)} %get-tuple-element.60), channel_id=1, source_target_pairs={{0,3},{1,0},{2,1},{3,2},{4,7},{5,4},{6,5},{7,6},{8,11},{9,8},{10,9... | collective-permute-start | bytes 147464 | tf_op jit(solution)/shard_map/ppermute | solution.py:365
  63.6 5.9 %collective-permute-start.19 = (bf16[192,128]{1,0:T(8,128)(2,1)S(1)}, bf16[192,128]{1,0:T(8,128)(2,1)S(1)}, u32[]{:S(2)}, u32[]{:S(2)}) collective-permute-start(bf16[192,128]{1,0:T(8,128)(2,1)S(1)} %get-tuple-element.61), channel_id=1, source_target_pairs={{0,1},{1,2},{2,3},{3,0},{4,5},{5,6},{6,7},{7,4},{8,9},{9,10},{10,1... | collective-permute-start | bytes 147464 | tf_op jit(solution)/shard_map/ppermute | solution.py:365
  64.4 6.8 %collective-permute-start.21 = (bf16[192,128]{1,0:T(8,128)(2,1)S(1)}, bf16[192,128]{1,0:T(8,128)(2,1)S(1)}, u32[]{:S(2)}, u32[]{:S(2)}) collective-permute-start(bf16[192,128]{1,0:T(8,128)(2,1)S(1)} %get-tuple-element.62.refs_2_), channel_id=1, source_target_pairs={{0,4},{1,5},{2,6},{3,7},{4,0},{5,1},{6,2},{7,3},{8,12},{9,13},{10,... | collective-permute-start | bytes 147464 | tf_op jit(solution)/shard_map/ppermute | solution.py:365
  67.2 4.1 %collective-permute-start.22 = (bf16[192,128]{1,0:T(8,128)(2,1)S(1)}, bf16[192,128]{1,0:T(8,128)(2,1)S(1)}, u32[]{:S(2)}, u32[]{:S(2)}) collective-permute-start(bf16[192,128]{1,0:T(8,128)(2,1)S(1)} %collective-permute-done.18.refs_6_.refs_3_), channel_id=1, source_target_pairs={{0,4},{1,5},{2,6},{3,7},{4,0},{5,1},{6,2},{7,3},{8,12},{9,13},{10,... | collective-permute-start | bytes 147464 | tf_op jit(solution)/shard_map/ppermute | solution.py:365
  69.4 1.8 %collective-permute-start.23 = (bf16[192,128]{1,0:T(8,128)(2,1)S(1)}, bf16[192,128]{1,0:T(8,128)(2,1)S(1)}, u32[]{:S(2)}, u32[]{:S(2)}) collective-permute-start(bf16[192,128]{1,0:T(8,128)(2,1)S(1)} %collective-permute-done.19.refs_7_.refs_5_), channel_id=1, source_target_pairs={{0,4},{1,5},{2,6},{3,7},{4,0},{5,1},{6,2},{7,3},{8,12},{9,13},{10,... | collective-permute-start | bytes 147464 | tf_op jit(solution)/shard_map/ppermute | solution.py:365
  70.5 9.8 %copy-start.7 = (bf16[384,256]{1,0:T(8,128)(2,1)S(1)}, bf16[384,256]{1,0:T(8,128)(2,1)}, u32[]{:S(2)}) copy-start(bf16[384,256]{1,0:T(8,128)(2,1)} %refs_1_.14) | copy-start | bytes 589828
  70.5 5.1 %collective-permute-start.20 = (bf16[192,128]{1,0:T(8,128)(2,1)S(1)}, bf16[192,128]{1,0:T(8,128)(2,1)S(1)}, u32[]{:S(2)}, u32[]{:S(2)}) collective-permute-start(bf16[192,128]{1,0:T(8,128)(2,1)S(1)} %shard_map.100), channel_id=1, source_target_pairs={{0,2},{1,3},{2,0},{3,1},{4,6},{5,7},{6,4},{7,5},{8,10},{9,11},{10,... | collective-permute-start | bytes 147464 | tf_op jit(solution)/shard_map/ppermute | solution.py:365
  70.6 10.8 %copy-start.28 = (f32[128,128]{1,0:T(8,128)S(1)}, f32[128,128]{1,0:T(8,128)}, u32[]{:S(2)}) copy-start(f32[128,128]{1,0:T(8,128)} %copy-done.27) | copy-start | bytes 196612
  70.6 15.5 %copy-start.9 = (bf16[384,256]{1,0:T(8,128)(2,1)S(1)}, bf16[384,256]{1,0:T(8,128)(2,1)}, u32[]{:S(2)}) copy-start(bf16[384,256]{1,0:T(8,128)(2,1)} %refs_1_.15) | copy-start | bytes 589828
  70.6 15.5 %copy-start.11 = (bf16[384,256]{1,0:T(8,128)(2,1)S(1)}, bf16[384,256]{1,0:T(8,128)(2,1)}, u32[]{:S(2)}) copy-start(bf16[384,256]{1,0:T(8,128)(2,1)} %refs_2_.5) | copy-start | bytes 589828
  70.6 15.5 %copy-start.15 = (bf16[2,384,384]{2,1,0:T(8,128)(2,1)S(1)}, bf16[2,384,384]{2,1,0:T(8,128)(2,1)}, u32[]{:S(2)}) copy-start(bf16[2,384,384]{2,1,0:T(8,128)(2,1)} %copy-done.14) | copy-start | bytes 1769476
  70.7 15.5 %copy-start.17 = (bf16[2,384,384]{2,1,0:T(8,128)(2,1)S(1)}, bf16[2,384,384]{2,1,0:T(8,128)(2,1)}, u32[]{:S(2)}) copy-start(bf16[2,384,384]{2,1,0:T(8,128)(2,1)} %copy-done.16) | copy-start | bytes 1769476
  70.7 15.5 %copy-start.23 = (f32[384,256]{1,0:T(8,128)S(1)}, f32[384,256]{1,0:T(8,128)}, u32[]{:S(2)}) copy-start(f32[384,256]{1,0:T(8,128)} %copy-done.22) | copy-start | bytes 1179652
  70.7 20.3 %collective-permute-start.13 = (f32[96,2048]{1,0:T(8,128)S(1)}, f32[96,2048]{1,0:T(8,128)S(1)}, u32[]{:S(2)}, u32[]{:S(2)}) collective-permute-start(f32[96,2048]{1,0:T(8,128)S(1)} %get-tuple-element.55), channel_id=1, source_target_pairs={{0,4},{1,5},{2,6},{3,7},{4,0},{5,1},{6,2},{7,3},{8,12},{9,13},{10,... | collective-permute-start | bytes 2359304 | tf_op jit(solution)/shard_map/ppermute | solution.py:365
  77.9 13.1 %collective-permute-start.24 = (f32[96,2048]{1,0:T(8,128)S(1)}, f32[96,2048]{1,0:T(8,128)S(1)}, u32[]{:S(2)}, u32[]{:S(2)}) collective-permute-start(f32[96,2048]{1,0:T(8,128)S(1)} %get-tuple-element.64), channel_id=1, source_target_pairs={{0,4},{1,5},{2,6},{3,7},{4,0},{5,1},{6,2},{7,3},{8,12},{9,13},{10,... | collective-permute-start | bytes 2359304 | tf_op jit(solution)/shard_map/ppermute | solution.py:365
  78.0 2.3 %collective-permute-start.25 = (bf16[192,128]{1,0:T(8,128)(2,1)S(1)}, bf16[192,128]{1,0:T(8,128)(2,1)S(1)}, u32[]{:S(2)}, u32[]{:S(2)}) collective-permute-start(bf16[192,128]{1,0:T(8,128)(2,1)S(1)} %collective-permute-done.20.refs_10_.refs_4_), channel_id=1, source_target_pairs={{0,4},{1,5},{2,6},{3,7},{4,0},{5,1},{6,2},{7,3},{8,12},{9,13},{10,... | collective-permute-start | bytes 147464 | tf_op jit(solution)/shard_map/ppermute | solution.py:365
  81.2 1.3 %collective-permute-start.27 = (f32[128,128]{1,0:T(8,128)S(1)}, f32[128,128]{1,0:T(8,128)S(1)}, u32[]{:S(2)}, u32[]{:S(2)}) collective-permute-start(f32[128,128]{1,0:T(8,128)S(1)} %get-tuple-element.73), channel_id=1, source_target_pairs={{0,4},{1,5},{2,6},{3,7},{4,0},{5,1},{6,2},{7,3},{8,12},{9,13},{10,... | collective-permute-start | bytes 196616 | tf_op jit(solution)/shard_map/ppermute | solution.py:365
  81.4 3.7 %collective-permute-start.26 = (f32[128,128]{1,0:T(8,128)S(1)}, f32[128,128]{1,0:T(8,128)S(1)}, u32[]{:S(2)}, u32[]{:S(2)}) collective-permute-start(f32[128,128]{1,0:T(8,128)S(1)} %copy-done.28), channel_id=1, source_target_pairs={{0,4},{1,5},{2,6},{3,7},{4,0},{5,1},{6,2},{7,3},{8,12},{9,13},{10,... | collective-permute-start | bytes 196616 | tf_op jit(solution)/shard_map/ppermute | solution.py:365
  82.5 6.6 %collective-permute-start.28 = (f32[128,128]{1,0:T(8,128)S(1)}, f32[128,128]{1,0:T(8,128)S(1)}, u32[]{:S(2)}, u32[]{:S(2)}) collective-permute-start(f32[128,128]{1,0:T(8,128)S(1)} %add.15.refs_10_), channel_id=1, source_target_pairs={{0,8},{1,9},{2,10},{3,11},{4,12},{5,13},{6,14},{7,15},{8,0},{9,1},... | collective-permute-start | bytes 196616 | tf_op jit(solution)/shard_map/ppermute | solution.py:365
  83.7 5.4 %collective-permute-start.29 = (f32[128,128]{1,0:T(8,128)S(1)}, f32[128,128]{1,0:T(8,128)S(1)}, u32[]{:S(2)}, u32[]{:S(2)}) collective-permute-start(f32[128,128]{1,0:T(8,128)S(1)} %add.15.refs_10_), channel_id=1, source_target_pairs={{0,16},{1,17},{2,18},{3,19},{4,20},{5,21},{6,22},{7,23},{8,24},{9,... | collective-permute-start | bytes 196616 | tf_op jit(solution)/shard_map/ppermute | solution.py:365
  85.1 5.2 %collective-permute-start.30 = (f32[128,128]{1,0:T(8,128)S(1)}, f32[128,128]{1,0:T(8,128)S(1)}, u32[]{:S(2)}, u32[]{:S(2)}) collective-permute-start(f32[128,128]{1,0:T(8,128)S(1)} %add.15.refs_10_), channel_id=1, source_target_pairs={{0,24},{1,25},{2,26},{3,27},{4,28},{5,29},{6,30},{7,31},{8,16},{9,... | collective-permute-start | bytes 196616 | tf_op jit(solution)/shard_map/ppermute | solution.py:365
  90.8 1.7 %collective-permute-start.31 = (f32[128,128]{1,0:T(8,128)S(1)}, f32[128,128]{1,0:T(8,128)S(1)}, u32[]{:S(2)}, u32[]{:S(2)}) collective-permute-start(f32[128,128]{1,0:T(8,128)S(1)} %get-tuple-element.78), channel_id=1, source_target_pairs={{0,4},{1,5},{2,6},{3,7},{4,0},{5,1},{6,2},{7,3},{8,12},{9,13},{10,... | collective-permute-start | bytes 196616 | tf_op jit(solution)/shard_map/ppermute | solution.py:365
  (19 other events, 14.4 us)

commit v12 on v11

--- a/solution.py
+++ b/solution.py
@@ -50,7 +50,7 @@
     return lambda ref, *_: ref.at[:, first : first + count]
 
 
-def call(body, outs, args, smem=(), after=(), room=8, flops=1):
+def call(body, outs, args, smem=(), after=(), room=2, flops=1):
     arrays, specs, scratch = [], [], []
     for arg in args:
         if isinstance(arg, tuple):
@@ -501,7 +501,7 @@
             fetch((2 * DH, wide), *stacked(arrived[1], arrived[3])),
         ],
         [spots],
-        room=24,
+        room=6,
         flops=2 * product,
     )
     one, three, *cuts = call(
@@ -514,7 +514,7 @@
             fetch((DH, wide), (arrived[2], all_of, all_of)),
         ],
         [spots],
-        room=16,
+        room=6,
         flops=product,
     )
     second[2] = [send(cuts[0], 2, 0), send(cuts[1], 4, 0)]
@@ -533,7 +533,7 @@
             *attn,
         ],
         [spots],
-        room=24,
+        room=6,
         flops=2 * product,
     )
     joins = [part, send(mate_part, 1, 0)]
@@ -544,7 +544,7 @@
         [left[1], fetch((DH, wide), *quarters), half],
         [spots],
         [both[1], both[3]],
-        room=16,
+        room=6,
         flops=product // 2,
     )
     both[2] = send(two, 0, -2)
@@ -567,7 +567,7 @@
         ],
         [spots],
         [both[2], across[0], across[1], across[3]],
-        room=24,
+        room=6,
         flops=2 * product,
     )
     joins += [part, send(mate_part, 1, 0)]
@@ -602,7 +602,7 @@
         [((own, model), F32)] * 2,
         [*attn, *chunks],
         [zero],
-        room=16,
+        room=6,
         flops=count * product,
     )
     return both, [send(b, 1, 0) for b in both], [part, send(mate_part, 1, 0)], [jnp.int32(0)]

time: 94.9 us -> 94.9 us (level)
  no operation moved by 1% of the time
where the time goes in v12:
time: 94.9 us; the launch traced here: 94.2 us
  waiting for transfers between devices  25.4 us (27%)
  starting transfers between devices  24.4 us (26%)
  Pallas kernels  22.8 us (24%)
  local copies, waits for them, and re-layouts  19.4 us (20%)
  other arithmetic  1.27 us (1%)
    ppermute x32, waiting for transfers between devices, send(): return lax.ppermute(x, ('ctx', 'head'), pairs)  25.4 us
    ppermute x32, starting transfers between devices, send(): return lax.ppermute(x, ('ctx', 'head'), pairs)  24.4 us
    pallas_call x12, Pallas kernels, call(): pl.pallas_call(kernel, out_shape=[jax.ShapeDtypeStruct(s, t) for s, t in...  22.8 us
    unnamed x70, local copies, waits for them, and re-layouts  17.5 us
  transfers between devices with their start and end apart: 32, of which 11 were waited for; matrix products, arithmetic and copies ran while one was open for 3% of the time, Pallas kernels for 20%

profile of v12, /device:TPU:0, one launch (start us, length us, event | category | flops | bytes accessed | tf_op | source)
XLA Modules:
  0.0 94.2 jit_solution(5898512828561436029)
XLA Ops:
  1.1 1.9 %dynamic_slice.3 = bf16[128,2048]{1,0:T(8,128)(2,1)} dynamic-slice(bf16[256,4096]{1,0:T(8,128)(2,1)} %refs_1_.12, s32[]{:T(128)S(6)} %select_n.6, s32[]{:T(128)S(6)} %select_n.7), dynamic_slice_sizes={128,2048} | dynamic-slice | bytes 1048580 | tf_op jit(solution)/shard_map/dynamic_slice | solution.py:406
  3.0 2.6 %collective-permute-start.1 = (bf16[128,2048]{1,0:T(8,128)(2,1)}, bf16[128,2048]{1,0:T(8,128)(2,1)S(1)}, u32[]{:S(2)}, u32[]{:S(2)}) collective-permute-start(bf16[128,2048]{1,0:T(8,128)(2,1)} %dynamic_slice.3), channel_id=1, source_target_pairs={{0,1},{1,2},{2,3},{3,0},{4,5},{5,6},{6,7},{7,4},{8,9},{9,10},{10,1... | collective-permute-start | bytes 1572872 | tf_op jit(solution)/shard_map/ppermute | solution.py:365
  5.7 2.0 %collective-permute-start.2 = (bf16[128,2048]{1,0:T(8,128)(2,1)}, bf16[128,2048]{1,0:T(8,128)(2,1)}, u32[]{:S(2)}, u32[]{:S(2)}) collective-permute-start(bf16[128,2048]{1,0:T(8,128)(2,1)} %dynamic_slice.3), channel_id=1, source_target_pairs={{0,3},{1,0},{2,1},{3,2},{4,7},{5,4},{6,5},{7,6},{8,11},{9,8},{10,9... | collective-permute-start | bytes 1572872 | tf_op jit(solution)/shard_map/ppermute | solution.py:365
  7.8 0.9 copy-done.5
  8.7 0.9 copy-done.8
  9.6 0.9 copy-done.10
  11.2 2.8 %shard_map.93 = (bf16[2,384,384]{2,1,0:T(8,128)(2,1)S(1)}, bf16[2,384,384]{2,1,0:T(8,128)(2,1)S(1)}, f32[384,256]{1,0:T(8,128)S(1)}, f32[384,128]{1,0:T(8,128)S(...) custom-call(s32[3,3]{1,0:T(4,128)S(1)} %copy-done.26, ...), custom_call_target="tpu_custom_call" | custom-call | flops 264241152 | bytes 2785280 | tf_op jit(solution)/shard_map/pallas_call | solution.py:93
  14.7 0.8 copy-done.14
  15.5 0.9 copy-done.16
  16.3 0.7 copy-done.22
  18.4 1.1 %collective-permute-done.3.refs_1_.refs_8_ = bf16[384,128]{1,0:T(8,128)(2,1)S(1)} collective-permute-done((bf16[384,128]{1,0:T(8,128)(2,1)}, bf16[384,128]{1,0:T(8,128)(2,1)S(1)}, u32[]{:S(2)}, u32[]{:S(2)}) %collective-permute-start.3) | collective-permute-done | bytes 98336 | tf_op jit(solution)/shard_map/ppermute | solution.py:365
  20.2 0.9 add.14
  21.1 1.7 %collective-permute-start.6 = (f32[128,128]{1,0:T(8,128)S(1)}, f32[128,128]{1,0:T(8,128)S(1)}, u32[]{:S(2)}, u32[]{:S(2)}) collective-permute-start(f32[128,128]{1,0:T(8,128)S(1)} %add.14), channel_id=1, source_target_pairs={{0,8},{1,9},{2,10},{3,11},{4,12},{5,13},{6,14},{7,15},{8,0},{9,1},... | collective-permute-start | bytes 196616 | tf_op jit(solution)/shard_map/ppermute | solution.py:365
  22.8 1.5 %collective-permute-start.7 = (f32[128,128]{1,0:T(8,128)S(1)}, f32[128,128]{1,0:T(8,128)S(1)}, u32[]{:S(2)}, u32[]{:S(2)}) collective-permute-start(f32[128,128]{1,0:T(8,128)S(1)} %add.14), channel_id=1, source_target_pairs={{0,16},{1,17},{2,18},{3,19},{4,20},{5,21},{6,22},{7,23},{8,24},{9,... | collective-permute-start | bytes 196616 | tf_op jit(solution)/shard_map/ppermute | solution.py:365
  24.7 0.7 collective-permute-done.6.refs_4_
  25.4 1.6 %collective-permute-done.7.refs_5_ = f32[128,128]{1,0:T(8,128)S(1)} collective-permute-done((f32[128,128]{1,0:T(8,128)S(1)}, f32[128,128]{1,0:T(8,128)S(1)}, u32[]{:S(2)}, u32[]{:S(2)}) %collective-permute-start.7) | collective-permute-done | bytes 65568 | tf_op jit(solution)/shard_map/ppermute | solution.py:365
  27.1 2.4 %collective-permute-done.8.refs_6_ = f32[128,128]{1,0:T(8,128)S(1)} collective-permute-done((f32[128,128]{1,0:T(8,128)S(1)}, f32[128,128]{1,0:T(8,128)S(1)}, u32[]{:S(2)}, u32[]{:S(2)}) %collective-permute-start.8) | collective-permute-done | bytes 65568 | tf_op jit(solution)/shard_map/ppermute | solution.py:365
  29.5 0.9 copy-done.6
  30.4 0.8 copy-done.13
  31.3 0.9 copy-done.21
  32.1 0.9 copy-done.25
  33.1 1.3 %shard_map.95 = (bf16[192,128]{1,0:T(8,128)(2,1)S(1)}, bf16[192,128]{1,0:T(8,128)(2,1)S(1)}, bf16[192,128]{1,0:T(8,128)(2,1)S(1)}, bf16[192,128]{1,0:T(8,128)(2,...) custom-call(s32[4]{0:T(128)S(1)} %add_convert_fusion.refs_0_, s32[3]{0:T(128)S(1)} %pad_add_fusion.2.refs_1_.refs_0_, ...), custom_call_target="tpu_custom_call" | custom-call | flops 1 | bytes 1343488 | tf_op jit(solution)/shard_map/pallas_call | solution.py:93
  37.5 0.8 copy-done.2
  39.4 1.1 %copy-done.1 = bf16[96,4096]{1,0:T(8,128)(2,1)S(1)} copy-done((bf16[96,4096]{1,0:T(8,128)(2,1)S(1)}, bf16[96,4096]{1,0:T(8,128)(2,1)}, u32[]{:S(2)}) %copy-start.1) | copy-done | bytes 786456
  40.5 1.0 %copy-done.3 = bf16[128,2048]{1,0:T(8,128)(2,1)S(1)} copy-done((bf16[128,2048]{1,0:T(8,128)(2,1)S(1)}, bf16[128,2048]{1,0:T(8,128)(2,1)}, u32[]{:S(2)}) %copy-start.3) | copy-done | bytes 524312
  41.6 2.7 %shard_map.98 = (bf16[192,128]{1,0:T(8,128)(2,1)S(1)}, f32[192,256]{1,0:T(8,128)S(1)}) custom-call(s32[3]{0:T(128)S(1)} %pad_add_fusion.1.refs_0_, bf16[96,4096]{1,0:T(8,128)(2,1)S(1)} %copy-done.1, bf16[96,4096]{1,0:T(8,128)(2,1)S(1)} %collective-permute-done.refs_5_.refs_2_, bf16[256,4096]{1,0:T(8,128)(2,1)S(1)} %copy-done, ...), custom_call_target="tpu_custom_call" | custom-call | flops 402653184 | bytes 4964352 | tf_op jit(solution)/shard_map/pallas_call | solution.py:93
  44.3 8.5 %collective-permute-done.9.refs_5_.refs_6_ = bf16[128,2048]{1,0:T(8,128)(2,1)} collective-permute-done((bf16[128,2048]{1,0:T(8,128)(2,1)}, bf16[128,2048]{1,0:T(8,128)(2,1)}, u32[]{:S(2)}, u32[]{:S(2)}) %collective-permute-start.9) | collective-permute-done | bytes 524320 | tf_op jit(solution)/shard_map/ppermute | solution.py:365
  52.9 2.4 %shard_map.99 = (bf16[192,128]{1,0:T(8,128)(2,1)S(1)}, bf16[192,128]{1,0:T(8,128)(2,1)S(1)}, bf16[128,1024]{1,0:T(8,128)(2,1)S(1)}, bf16[128,1024]{1,0:T(8,128)(2,1)S(1)}) custom-call(s32[3]{0:T(128)S(1)} %pad_add_fusion.1.refs_0_, bf16[96,4096]{1,0:T(8,128)(2,1)S(1)} %copy-done.1, bf16[96,4096]{1,0:T(8,128)(2,1)S(1)} %collective-permute-done.refs_5_.refs_2_, ...), custom_call_target="tpu_custom_call" | custom-call | flops 201326592 | bytes 3964928 | tf_op jit(solution)/shard_map/pallas_call | solution.py:93
  57.0 3.0 %collective-permute-start.11 = (bf16[192,128]{1,0:T(8,128)(2,1)S(1)}, bf16[192,128]{1,0:T(8,128)(2,1)S(1)}, u32[]{:S(2)}, u32[]{:S(2)}) collective-permute-start(bf16[192,128]{1,0:T(8,128)(2,1)S(1)} %copy-done.32), channel_id=1, source_target_pairs={{0,2},{1,3},{2,0},{3,1},{4,6},{5,7},{6,4},{7,5},{8,10},{9,11},{10,... | collective-permute-start | bytes 147464 | tf_op jit(solution)/shard_map/ppermute | solution.py:365
  60.0 1.2 %collective-permute-start.12 = (bf16[192,128]{1,0:T(8,128)(2,1)S(1)}, bf16[192,128]{1,0:T(8,128)(2,1)S(1)}, u32[]{:S(2)}, u32[]{:S(2)}) collective-permute-start(bf16[192,128]{1,0:T(8,128)(2,1)S(1)} %copy-done.30), channel_id=1, source_target_pairs={{0,3},{1,0},{2,1},{3,2},{4,7},{5,4},{6,5},{7,6},{8,11},{9,8},{10,9... | collective-permute-start | bytes 147464 | tf_op jit(solution)/shard_map/ppermute | solution.py:365
  61.2 1.2 %collective-permute-done.10.refs_8_.refs_7_ = bf16[192,128]{1,0:T(8,128)(2,1)S(1)} collective-permute-done((bf16[192,128]{1,0:T(8,128)(2,1)S(1)}, bf16[192,128]{1,0:T(8,128)(2,1)S(1)}, u32[]{:S(2)}, u32[]{:S(2)}) %collective-permute-start.10) | collective-permute-done | bytes 49184 | tf_op jit(solution)/shard_map/ppermute | solution.py:365
  62.4 1.1 %collective-permute-start.18 = (bf16[192,128]{1,0:T(8,128)(2,1)S(1)}, bf16[192,128]{1,0:T(8,128)(2,1)S(1)}, u32[]{:S(2)}, u32[]{:S(2)}) collective-permute-start(bf16[192,128]{1,0:T(8,128)(2,1)S(1)} %get-tuple-element.60), channel_id=1, source_target_pairs={{0,3},{1,0},{2,1},{3,2},{4,7},{5,4},{6,5},{7,6},{8,11},{9,8},{10,9... | collective-permute-start | bytes 147464 | tf_op jit(solution)/shard_map/ppermute | solution.py:365
  63.6 0.9 collective-permute-start.19
  64.5 2.7 %shard_map.97 = (f32[192,128]{1,0:T(8,128)S(1)}, f32[96,2048]{1,0:T(8,128)S(1)}, f32[96,2048]{1,0:T(8,128)S(1)}) custom-call(s32[3]{0:T(128)S(1)} %pad_add_fusion.1.refs_0_, bf16[96,4096]{1,0:T(8,128)(2,1)S(1)} %copy-done.1, bf16[96,4096]{1,0:T(8,128)(2,1)S(1)} %collective-permute-done.refs_5_.refs_2_, bf16[256,4096]{1,0:T(8,128)(2,1)S(1)} %copy-done, ...), custom_call_target="tpu_custom_call" | custom-call | flops 402653184 | bytes 7110656 | tf_op jit(solution)/shard_map/pallas_call | solution.py:93
  67.8 1.7 %collective-permute-done.19.refs_7_.refs_5_ = bf16[192,128]{1,0:T(8,128)(2,1)S(1)} collective-permute-done((bf16[192,128]{1,0:T(8,128)(2,1)S(1)}, bf16[192,128]{1,0:T(8,128)(2,1)S(1)}, u32[]{:S(2)}, u32[]{:S(2)}) %collective-permute-start.19) | collective-permute-done | bytes 49184 | tf_op jit(solution)/shard_map/ppermute | solution.py:365
  69.5 1.1 %shard_map.100 = bf16[192,128]{1,0:T(8,128)(2,1)S(1)} custom-call(s32[3]{0:T(128)S(1)} %pad_add_fusion.1.refs_0_, bf16[96,4096]{1,0:T(8,128)(2,1)S(1)} %copy-done.1, bf16[96,4096]{1,0:T(8,128)(2,1)S(1)} %collective-permute-done.refs_5_.refs_2_, bf16[128,1024]{1,0:T(8,128)(2,1)S(1)} %collective-permute-done.16.refs_3_.refs_4_, ...), custom_call_target="tpu_custom_call" | custom-call | flops 100663296 | bytes 2244608 | tf_op jit(solution)/shard_map/pallas_call | solution.py:93
  71.3 4.4 %collective-permute-done.20.refs_10_.refs_4_ = bf16[192,128]{1,0:T(8,128)(2,1)S(1)} collective-permute-done((bf16[192,128]{1,0:T(8,128)(2,1)S(1)}, bf16[192,128]{1,0:T(8,128)(2,1)S(1)}, u32[]{:S(2)}, u32[]{:S(2)}) %collective-permute-start.20) | collective-permute-done | bytes 49184 | tf_op jit(solution)/shard_map/ppermute | solution.py:365
  75.6 2.3 %shard_map.101 = (f32[96,2048]{1,0:T(8,128)S(1)}, f32[96,2048]{1,0:T(8,128)S(1)}) custom-call(s32[3]{0:T(128)S(1)} %pad_add_fusion.1.refs_0_, bf16[256,4096]{1,0:T(8,128)(2,1)S(1)} %copy-done, bf16[128,2048]{1,0:T(8,128)(2,1)S(1)} %collective-permute-done.14.refs_3_.refs_2_, bf16[128,2048]{1,0:T(8,128)(2,1)} %collective-permute-done.15.refs_4_.refs_3_, ...), custom_call_target="tpu_custom_call" | custom-call | flops 402653184 | bytes 5439488 | tf_op jit(solution)/shard_map/pallas_call | solution.py:93
  78.5 1.8 %collective-permute-done.25.refs_8_ = bf16[192,128]{1,0:T(8,128)(2,1)S(1)} collective-permute-done((bf16[192,128]{1,0:T(8,128)(2,1)S(1)}, bf16[192,128]{1,0:T(8,128)(2,1)S(1)}, u32[]{:S(2)}, u32[]{:S(2)}) %collective-permute-start.25) | collective-permute-done | bytes 49184 | tf_op jit(solution)/shard_map/ppermute | solution.py:365
  80.4 0.8 shard_map.103
  81.8 0.7 collective-permute-done.27.refs_2_
  82.5 1.2 %collective-permute-start.28 = (f32[128,128]{1,0:T(8,128)S(1)}, f32[128,128]{1,0:T(8,128)S(1)}, u32[]{:S(2)}, u32[]{:S(2)}) collective-permute-start(f32[128,128]{1,0:T(8,128)S(1)} %add.15.refs_10_), channel_id=1, source_target_pairs={{0,8},{1,9},{2,10},{3,11},{4,12},{5,13},{6,14},{7,15},{8,0},{9,1},... | collective-permute-start | bytes 196616 | tf_op jit(solution)/shard_map/ppermute | solution.py:365
  83.7 1.4 %collective-permute-start.29 = (f32[128,128]{1,0:T(8,128)S(1)}, f32[128,128]{1,0:T(8,128)S(1)}, u32[]{:S(2)}, u32[]{:S(2)}) collective-permute-start(f32[128,128]{1,0:T(8,128)S(1)} %add.15.refs_10_), channel_id=1, source_target_pairs={{0,16},{1,17},{2,18},{3,19},{4,20},{5,21},{6,22},{7,23},{8,24},{9,... | collective-permute-start | bytes 196616 | tf_op jit(solution)/shard_map/ppermute | solution.py:365
  85.1 1.0 %collective-permute-start.30 = (f32[128,128]{1,0:T(8,128)S(1)}, f32[128,128]{1,0:T(8,128)S(1)}, u32[]{:S(2)}, u32[]{:S(2)}) collective-permute-start(f32[128,128]{1,0:T(8,128)S(1)} %add.15.refs_10_), channel_id=1, source_target_pairs={{0,24},{1,25},{2,26},{3,27},{4,28},{5,29},{6,30},{7,31},{8,16},{9,... | collective-permute-start | bytes 196616 | tf_op jit(solution)/shard_map/ppermute | solution.py:365
  86.2 2.9 %shard_map.104 = (bf16[384,256]{1,0:T(8,128)(2,1)}, f32[384,256]{1,0:T(8,128)S(1)}, f32[384,256]{1,0:T(8,128)S(1)}) custom-call(s32[3]{0:T(128)S(1)} %pad_add_fusion.2.refs_1_.refs_0_, bf16[384,256]{1,0:T(8,128)(2,1)S(1)} %copy-done.7, bf16[384,256]{1,0:T(8,128)(2,1)S(1)} %copy-done.9, bf16[384,256]{1,0:T(8,128)(2,1)S(1)} %copy-done.11, ...), custom_call_target="tpu_custom_call" | custom-call | flops 528482304 | bytes 3473408 | tf_op jit(solution)/shard_map/pallas_call | solution.py:93
  89.1 1.1 %collective-permute-done.30.refs_5_ = f32[128,128]{1,0:T(8,128)S(1)} collective-permute-done((f32[128,128]{1,0:T(8,128)S(1)}, f32[128,128]{1,0:T(8,128)S(1)}, u32[]{:S(2)}, u32[]{:S(2)}) %collective-permute-start.30) | collective-permute-done | bytes 65568 | tf_op jit(solution)/shard_map/ppermute | solution.py:365
  91.0 1.6 %shard_map.102 = (bf16[96,4096]{1,0:T(8,128)(2,1)}, f32[8,128]{1,0:T(8,128)S(1)}) custom-call(s32[2]{0:T(128)S(1)} %pad_add_fusion.refs_0_, f32[96,2048]{1,0:T(8,128)S(1)} %get-tuple-element.54.refs_1_, f32[96,2048]{1,0:T(8,128)S(1)} %collective-permute-done.13.refs_2_, f32[96,2048]{1,0:T(8,128)S(1)} %get-tuple-element.63.refs_3_, ...), custom_call_target="tpu_custom_call" | custom-call | flops 1 | bytes 3936256 | tf_op jit(solution)/shard_map/pallas_call | solution.py:93
  92.6 1.6 %shard_map.106 = (bf16[384,256]{1,0:T(8,128)(2,1)}, bf16[384,256]{1,0:T(8,128)(2,1)}) custom-call(s32[3]{0:T(128)S(1)} %pad_add_fusion.2.refs_1_.refs_0_, bf16[384,256]{1,0:T(8,128)(2,1)S(1)} %copy-done.9, bf16[384,256]{1,0:T(8,128)(2,1)S(1)} %copy-done.11, f32[384,256]{1,0:T(8,128)S(1)} %get-tuple-element.75.refs_6_.refs_3_, ...), custom_call_target="tpu_custom_call" | custom-call | flops 1 | bytes 1703936 | tf_op jit(solution)/shard_map/pallas_call | solution.py:93
  (108 shorter events, 13.5 us)
Async XLA Ops:
  0.6 7.1 %collective-permute-start = (bf16[96,4096]{1,0:T(8,128)(2,1)}, bf16[96,4096]{1,0:T(8,128)(2,1)S(1)}, u32[]{:S(2)}, u32[]{:S(2)}) collective-permute-start(bf16[96,4096]{1,0:T(8,128)(2,1)} %refs_1_.11), channel_id=1, source_target_pairs={{0,4},{1,5},{2,6},{3,7},{4,0},{5,1},{6,2},{7,3},{8,12},{9,13},{10,... | collective-permute-start | bytes 2359304 | tf_op jit(solution)/shard_map/ppermute | solution.py:365
  3.0 36.3 %copy-start = (bf16[256,4096]{1,0:T(8,128)(2,1)S(1)}, bf16[256,4096]{1,0:T(8,128)(2,1)}, u32[]{:S(2)}) copy-start(bf16[256,4096]{1,0:T(8,128)(2,1)} %refs_1_.12) | copy-start | bytes 6291460
  3.0 34.4 %collective-permute-start.1 = (bf16[128,2048]{1,0:T(8,128)(2,1)}, bf16[128,2048]{1,0:T(8,128)(2,1)S(1)}, u32[]{:S(2)}, u32[]{:S(2)}) collective-permute-start(bf16[128,2048]{1,0:T(8,128)(2,1)} %dynamic_slice.3), channel_id=1, source_target_pairs={{0,1},{1,2},{2,3},{3,0},{4,5},{5,6},{6,7},{7,4},{8,9},{9,10},{10,1... | collective-permute-start | bytes 1572872 | tf_op jit(solution)/shard_map/ppermute | solution.py:365
  5.7 31.8 %collective-permute-start.2 = (bf16[128,2048]{1,0:T(8,128)(2,1)}, bf16[128,2048]{1,0:T(8,128)(2,1)}, u32[]{:S(2)}, u32[]{:S(2)}) collective-permute-start(bf16[128,2048]{1,0:T(8,128)(2,1)} %dynamic_slice.3), channel_id=1, source_target_pairs={{0,3},{1,0},{2,1},{3,2},{4,7},{5,4},{6,5},{7,6},{8,11},{9,8},{10,9... | collective-permute-start | bytes 1572872 | tf_op jit(solution)/shard_map/ppermute | solution.py:365
  7.8 0.9 copy-start.5
  17.7 1.8 %collective-permute-start.4 = (f32[384,128]{1,0:T(8,128)}, f32[384,128]{1,0:T(8,128)}, u32[]{:S(2)}, u32[]{:S(2)}) collective-permute-start(f32[384,128]{1,0:T(8,128)} %get-tuple-element.45), channel_id=1, source_target_pairs={{0,4},{1,5},{2,6},{3,7},{4,0},{5,1},{6,2},{7,3},{8,12},{9,13},{10,... | collective-permute-start | bytes 589832 | tf_op jit(solution)/shard_map/ppermute | solution.py:365
  17.9 1.6 %collective-permute-start.3 = (bf16[384,128]{1,0:T(8,128)(2,1)}, bf16[384,128]{1,0:T(8,128)(2,1)S(1)}, u32[]{:S(2)}, u32[]{:S(2)}) collective-permute-start(bf16[384,128]{1,0:T(8,128)(2,1)} %get-tuple-element.44), channel_id=1, source_target_pairs={{0,4},{1,5},{2,6},{3,7},{4,0},{5,1},{6,2},{7,3},{8,12},{9,13},{10,... | collective-permute-start | bytes 294920 | tf_op jit(solution)/shard_map/ppermute | solution.py:365
  18.3 1.9 %collective-permute-start.5 = (f32[128,128]{1,0:T(8,128)}, f32[128,128]{1,0:T(8,128)}, u32[]{:S(2)}, u32[]{:S(2)}) collective-permute-start(f32[128,128]{1,0:T(8,128)} %get-tuple-element.46), channel_id=1, source_target_pairs={{0,4},{1,5},{2,6},{3,7},{4,0},{5,1},{6,2},{7,3},{8,12},{9,13},{10,... | collective-permute-start | bytes 196616 | tf_op jit(solution)/shard_map/ppermute | solution.py:365
  21.1 4.4 %collective-permute-start.6 = (f32[128,128]{1,0:T(8,128)S(1)}, f32[128,128]{1,0:T(8,128)S(1)}, u32[]{:S(2)}, u32[]{:S(2)}) collective-permute-start(f32[128,128]{1,0:T(8,128)S(1)} %add.14), channel_id=1, source_target_pairs={{0,8},{1,9},{2,10},{3,11},{4,12},{5,13},{6,14},{7,15},{8,0},{9,1},... | collective-permute-start | bytes 196616 | tf_op jit(solution)/shard_map/ppermute | solution.py:365
  22.8 4.3 %collective-permute-start.7 = (f32[128,128]{1,0:T(8,128)S(1)}, f32[128,128]{1,0:T(8,128)S(1)}, u32[]{:S(2)}, u32[]{:S(2)}) collective-permute-start(f32[128,128]{1,0:T(8,128)S(1)} %add.14), channel_id=1, source_target_pairs={{0,16},{1,17},{2,18},{3,19},{4,20},{5,21},{6,22},{7,23},{8,24},{9,... | collective-permute-start | bytes 196616 | tf_op jit(solution)/shard_map/ppermute | solution.py:365
  24.3 5.2 %collective-permute-start.8 = (f32[128,128]{1,0:T(8,128)S(1)}, f32[128,128]{1,0:T(8,128)S(1)}, u32[]{:S(2)}, u32[]{:S(2)}) collective-permute-start(f32[128,128]{1,0:T(8,128)S(1)} %add.14), channel_id=1, source_target_pairs={{0,24},{1,25},{2,26},{3,27},{4,28},{5,29},{6,30},{7,31},{8,16},{9,... | collective-permute-start | bytes 196616 | tf_op jit(solution)/shard_map/ppermute | solution.py:365
  38.3 14.6 %collective-permute-start.9 = (bf16[128,2048]{1,0:T(8,128)(2,1)}, bf16[128,2048]{1,0:T(8,128)(2,1)}, u32[]{:S(2)}, u32[]{:S(2)}) collective-permute-start(bf16[128,2048]{1,0:T(8,128)(2,1)} %get-tuple-element.49.refs_4_), channel_id=1, source_target_pairs={{0,1},{1,2},{2,3},{3,0},{4,5},{5,6},{6,7},{7,4},{8,9},{9,10},{10,1... | collective-permute-start | bytes 1572872 | tf_op jit(solution)/shard_map/ppermute | solution.py:365
  38.3 14.6 %collective-permute-start.14 = (bf16[128,2048]{1,0:T(8,128)(2,1)}, bf16[128,2048]{1,0:T(8,128)(2,1)S(1)}, u32[]{:S(2)}, u32[]{:S(2)}) collective-permute-start(bf16[128,2048]{1,0:T(8,128)(2,1)} %get-tuple-element.49.refs_4_), channel_id=1, source_target_pairs={{0,8},{1,9},{2,10},{3,11},{4,12},{5,13},{6,14},{7,15},{8,0},{9,1},... | collective-permute-start | bytes 1572872 | tf_op jit(solution)/shard_map/ppermute | solution.py:365
  38.8 14.1 %collective-permute-start.15 = (bf16[128,2048]{1,0:T(8,128)(2,1)}, bf16[128,2048]{1,0:T(8,128)(2,1)}, u32[]{:S(2)}, u32[]{:S(2)}) collective-permute-start(bf16[128,2048]{1,0:T(8,128)(2,1)} %get-tuple-element.50.refs_6_.refs_5_), channel_id=1, source_target_pairs={{0,16},{1,17},{2,18},{3,19},{4,20},{5,21},{6,22},{7,23},{8,24},{9,... | collective-permute-start | bytes 1572872 | tf_op jit(solution)/shard_map/ppermute | solution.py:365
  39.4 1.1 %copy-start.1 = (bf16[96,4096]{1,0:T(8,128)(2,1)S(1)}, bf16[96,4096]{1,0:T(8,128)(2,1)}, u32[]{:S(2)}) copy-start(bf16[96,4096]{1,0:T(8,128)(2,1)} %refs_1_.11) | copy-start | bytes 2359300
  40.5 1.0 %copy-start.3 = (bf16[128,2048]{1,0:T(8,128)(2,1)S(1)}, bf16[128,2048]{1,0:T(8,128)(2,1)}, u32[]{:S(2)}) copy-start(bf16[128,2048]{1,0:T(8,128)(2,1)} %get-tuple-element.49.refs_4_) | copy-start | bytes 1572868
  44.3 12.1 %copy-start.34 = (bf16[192,128]{1,0:T(8,128)(2,1)S(1)}, bf16[192,128]{1,0:T(8,128)(2,1)}, u32[]{:S(2)}) copy-start(bf16[192,128]{1,0:T(8,128)(2,1)} %copy-done.33) | copy-start | bytes 147460
  44.3 12.7 %copy-start.32 = (bf16[192,128]{1,0:T(8,128)(2,1)S(1)}, bf16[192,128]{1,0:T(8,128)(2,1)}, u32[]{:S(2)}) copy-start(bf16[192,128]{1,0:T(8,128)(2,1)} %copy-done.31) | copy-start | bytes 147460
  44.3 15.7 %copy-start.30 = (bf16[192,128]{1,0:T(8,128)(2,1)S(1)}, bf16[192,128]{1,0:T(8,128)(2,1)}, u32[]{:S(2)}) copy-start(bf16[192,128]{1,0:T(8,128)(2,1)} %copy-done.29) | copy-start | bytes 147460
  44.3 20.1 %copy-start.4 = (bf16[128,2048]{1,0:T(8,128)(2,1)S(1)}, bf16[128,2048]{1,0:T(8,128)(2,1)}, u32[]{:S(2)}) copy-start(bf16[128,2048]{1,0:T(8,128)(2,1)} %get-tuple-element.49.refs_4_) | copy-start | bytes 1572868
  44.3 20.1 %copy-start.19 = (bf16[192,128]{1,0:T(8,128)(2,1)S(1)}, bf16[192,128]{1,0:T(8,128)(2,1)}, u32[]{:S(2)}) copy-start(bf16[192,128]{1,0:T(8,128)(2,1)} %copy-done.18) | copy-start | bytes 147460
  55.3 14.2 %collective-permute-start.16 = (bf16[128,1024]{1,0:T(8,128)(2,1)S(1)}, bf16[128,1024]{1,0:T(8,128)(2,1)S(1)}, u32[]{:S(2)}, u32[]{:S(2)}) collective-permute-start(bf16[128,1024]{1,0:T(8,128)(2,1)S(1)} %get-tuple-element.57), channel_id=1, source_target_pairs={{0,8},{1,9},{2,10},{3,11},{4,12},{5,13},{6,14},{7,15},{8,0},{9,1},... | collective-permute-start | bytes 786440 | tf_op jit(solution)/shard_map/ppermute | solution.py:365
  55.9 13.6 %collective-permute-start.17 = (bf16[128,1024]{1,0:T(8,128)(2,1)S(1)}, bf16[128,1024]{1,0:T(8,128)(2,1)S(1)}, u32[]{:S(2)}, u32[]{:S(2)}) collective-permute-start(bf16[128,1024]{1,0:T(8,128)(2,1)S(1)} %get-tuple-element.58), channel_id=1, source_target_pairs={{0,16},{1,17},{2,18},{3,19},{4,20},{5,21},{6,22},{7,23},{8,24},{9,... | collective-permute-start | bytes 786440 | tf_op jit(solution)/shard_map/ppermute | solution.py:365
  56.4 6.0 %collective-permute-start.10 = (bf16[192,128]{1,0:T(8,128)(2,1)S(1)}, bf16[192,128]{1,0:T(8,128)(2,1)S(1)}, u32[]{:S(2)}, u32[]{:S(2)}) collective-permute-start(bf16[192,128]{1,0:T(8,128)(2,1)S(1)} %copy-done.34), channel_id=1, source_target_pairs={{0,1},{1,2},{2,3},{3,0},{4,5},{5,6},{6,7},{7,4},{8,9},{9,10},{10,1... | collective-permute-start | bytes 147464 | tf_op jit(solution)/shard_map/ppermute | solution.py:365
  57.0 6.6 %collective-permute-start.11 = (bf16[192,128]{1,0:T(8,128)(2,1)S(1)}, bf16[192,128]{1,0:T(8,128)(2,1)S(1)}, u32[]{:S(2)}, u32[]{:S(2)}) collective-permute-start(bf16[192,128]{1,0:T(8,128)(2,1)S(1)} %copy-done.32), channel_id=1, source_target_pairs={{0,2},{1,3},{2,0},{3,1},{4,6},{5,7},{6,4},{7,5},{8,10},{9,11},{10,... | collective-permute-start | bytes 147464 | tf_op jit(solution)/shard_map/ppermute | solution.py:365
  60.0 4.4 %collective-permute-start.12 = (bf16[192,128]{1,0:T(8,128)(2,1)S(1)}, bf16[192,128]{1,0:T(8,128)(2,1)S(1)}, u32[]{:S(2)}, u32[]{:S(2)}) collective-permute-start(bf16[192,128]{1,0:T(8,128)(2,1)S(1)} %copy-done.30), channel_id=1, source_target_pairs={{0,3},{1,0},{2,1},{3,2},{4,7},{5,4},{6,5},{7,6},{8,11},{9,8},{10,9... | collective-permute-start | bytes 147464 | tf_op jit(solution)/shard_map/ppermute | solution.py:365
  62.4 4.8 %collective-permute-start.18 = (bf16[192,128]{1,0:T(8,128)(2,1)S(1)}, bf16[192,128]{1,0:T(8,128)(2,1)S(1)}, u32[]{:S(2)}, u32[]{:S(2)}) collective-permute-start(bf16[192,128]{1,0:T(8,128)(2,1)S(1)} %get-tuple-element.60), channel_id=1, source_target_pairs={{0,3},{1,0},{2,1},{3,2},{4,7},{5,4},{6,5},{7,6},{8,11},{9,8},{10,9... | collective-permute-start | bytes 147464 | tf_op jit(solution)/shard_map/ppermute | solution.py:365
  63.6 5.9 %collective-permute-start.19 = (bf16[192,128]{1,0:T(8,128)(2,1)S(1)}, bf16[192,128]{1,0:T(8,128)(2,1)S(1)}, u32[]{:S(2)}, u32[]{:S(2)}) collective-permute-start(bf16[192,128]{1,0:T(8,128)(2,1)S(1)} %get-tuple-element.61), channel_id=1, source_target_pairs={{0,1},{1,2},{2,3},{3,0},{4,5},{5,6},{6,7},{7,4},{8,9},{9,10},{10,1... | collective-permute-start | bytes 147464 | tf_op jit(solution)/shard_map/ppermute | solution.py:365
  64.4 6.8 %collective-permute-start.21 = (bf16[192,128]{1,0:T(8,128)(2,1)S(1)}, bf16[192,128]{1,0:T(8,128)(2,1)S(1)}, u32[]{:S(2)}, u32[]{:S(2)}) collective-permute-start(bf16[192,128]{1,0:T(8,128)(2,1)S(1)} %get-tuple-element.62.refs_2_), channel_id=1, source_target_pairs={{0,4},{1,5},{2,6},{3,7},{4,0},{5,1},{6,2},{7,3},{8,12},{9,13},{10,... | collective-permute-start | bytes 147464 | tf_op jit(solution)/shard_map/ppermute | solution.py:365
  67.2 4.0 %collective-permute-start.22 = (bf16[192,128]{1,0:T(8,128)(2,1)S(1)}, bf16[192,128]{1,0:T(8,128)(2,1)S(1)}, u32[]{:S(2)}, u32[]{:S(2)}) collective-permute-start(bf16[192,128]{1,0:T(8,128)(2,1)S(1)} %collective-permute-done.18.refs_6_.refs_3_), channel_id=1, source_target_pairs={{0,4},{1,5},{2,6},{3,7},{4,0},{5,1},{6,2},{7,3},{8,12},{9,13},{10,... | collective-permute-start | bytes 147464 | tf_op jit(solution)/shard_map/ppermute | solution.py:365
  69.4 1.8 %collective-permute-start.23 = (bf16[192,128]{1,0:T(8,128)(2,1)S(1)}, bf16[192,128]{1,0:T(8,128)(2,1)S(1)}, u32[]{:S(2)}, u32[]{:S(2)}) collective-permute-start(bf16[192,128]{1,0:T(8,128)(2,1)S(1)} %collective-permute-done.19.refs_7_.refs_5_), channel_id=1, source_target_pairs={{0,4},{1,5},{2,6},{3,7},{4,0},{5,1},{6,2},{7,3},{8,12},{9,13},{10,... | collective-permute-start | bytes 147464 | tf_op jit(solution)/shard_map/ppermute | solution.py:365
  70.5 9.9 %copy-start.7 = (bf16[384,256]{1,0:T(8,128)(2,1)S(1)}, bf16[384,256]{1,0:T(8,128)(2,1)}, u32[]{:S(2)}) copy-start(bf16[384,256]{1,0:T(8,128)(2,1)} %refs_1_.14) | copy-start | bytes 589828
  70.5 5.1 %collective-permute-start.20 = (bf16[192,128]{1,0:T(8,128)(2,1)S(1)}, bf16[192,128]{1,0:T(8,128)(2,1)S(1)}, u32[]{:S(2)}, u32[]{:S(2)}) collective-permute-start(bf16[192,128]{1,0:T(8,128)(2,1)S(1)} %shard_map.100), channel_id=1, source_target_pairs={{0,2},{1,3},{2,0},{3,1},{4,6},{5,7},{6,4},{7,5},{8,10},{9,11},{10,... | collective-permute-start | bytes 147464 | tf_op jit(solution)/shard_map/ppermute | solution.py:365
  70.6 10.8 %copy-start.28 = (f32[128,128]{1,0:T(8,128)S(1)}, f32[128,128]{1,0:T(8,128)}, u32[]{:S(2)}) copy-start(f32[128,128]{1,0:T(8,128)} %copy-done.27) | copy-start | bytes 196612
  70.6 15.5 %copy-start.9 = (bf16[384,256]{1,0:T(8,128)(2,1)S(1)}, bf16[384,256]{1,0:T(8,128)(2,1)}, u32[]{:S(2)}) copy-start(bf16[384,256]{1,0:T(8,128)(2,1)} %refs_1_.15) | copy-start | bytes 589828
  70.6 15.5 %copy-start.11 = (bf16[384,256]{1,0:T(8,128)(2,1)S(1)}, bf16[384,256]{1,0:T(8,128)(2,1)}, u32[]{:S(2)}) copy-start(bf16[384,256]{1,0:T(8,128)(2,1)} %refs_2_.5) | copy-start | bytes 589828
  70.6 15.5 %copy-start.15 = (bf16[2,384,384]{2,1,0:T(8,128)(2,1)S(1)}, bf16[2,384,384]{2,1,0:T(8,128)(2,1)}, u32[]{:S(2)}) copy-start(bf16[2,384,384]{2,1,0:T(8,128)(2,1)} %copy-done.14) | copy-start | bytes 1769476
  70.7 15.5 %copy-start.17 = (bf16[2,384,384]{2,1,0:T(8,128)(2,1)S(1)}, bf16[2,384,384]{2,1,0:T(8,128)(2,1)}, u32[]{:S(2)}) copy-start(bf16[2,384,384]{2,1,0:T(8,128)(2,1)} %copy-done.16) | copy-start | bytes 1769476
  70.7 15.5 %copy-start.23 = (f32[384,256]{1,0:T(8,128)S(1)}, f32[384,256]{1,0:T(8,128)}, u32[]{:S(2)}) copy-start(f32[384,256]{1,0:T(8,128)} %copy-done.22) | copy-start | bytes 1179652
  70.7 20.3 %collective-permute-start.13 = (f32[96,2048]{1,0:T(8,128)S(1)}, f32[96,2048]{1,0:T(8,128)S(1)}, u32[]{:S(2)}, u32[]{:S(2)}) collective-permute-start(f32[96,2048]{1,0:T(8,128)S(1)} %get-tuple-element.55), channel_id=1, source_target_pairs={{0,4},{1,5},{2,6},{3,7},{4,0},{5,1},{6,2},{7,3},{8,12},{9,13},{10,... | collective-permute-start | bytes 2359304 | tf_op jit(solution)/shard_map/ppermute | solution.py:365
  78.0 13.1 %collective-permute-start.24 = (f32[96,2048]{1,0:T(8,128)S(1)}, f32[96,2048]{1,0:T(8,128)S(1)}, u32[]{:S(2)}, u32[]{:S(2)}) collective-permute-start(f32[96,2048]{1,0:T(8,128)S(1)} %get-tuple-element.64), channel_id=1, source_target_pairs={{0,4},{1,5},{2,6},{3,7},{4,0},{5,1},{6,2},{7,3},{8,12},{9,13},{10,... | collective-permute-start | bytes 2359304 | tf_op jit(solution)/shard_map/ppermute | solution.py:365
  78.0 2.3 %collective-permute-start.25 = (bf16[192,128]{1,0:T(8,128)(2,1)S(1)}, bf16[192,128]{1,0:T(8,128)(2,1)S(1)}, u32[]{:S(2)}, u32[]{:S(2)}) collective-permute-start(bf16[192,128]{1,0:T(8,128)(2,1)S(1)} %collective-permute-done.20.refs_10_.refs_4_), channel_id=1, source_target_pairs={{0,4},{1,5},{2,6},{3,7},{4,0},{5,1},{6,2},{7,3},{8,12},{9,13},{10,... | collective-permute-start | bytes 147464 | tf_op jit(solution)/shard_map/ppermute | solution.py:365
  81.2 1.3 %collective-permute-start.27 = (f32[128,128]{1,0:T(8,128)S(1)}, f32[128,128]{1,0:T(8,128)S(1)}, u32[]{:S(2)}, u32[]{:S(2)}) collective-permute-start(f32[128,128]{1,0:T(8,128)S(1)} %get-tuple-element.73), channel_id=1, source_target_pairs={{0,4},{1,5},{2,6},{3,7},{4,0},{5,1},{6,2},{7,3},{8,12},{9,13},{10,... | collective-permute-start | bytes 196616 | tf_op jit(solution)/shard_map/ppermute | solution.py:365
  81.4 3.7 %collective-permute-start.26 = (f32[128,128]{1,0:T(8,128)S(1)}, f32[128,128]{1,0:T(8,128)S(1)}, u32[]{:S(2)}, u32[]{:S(2)}) collective-permute-start(f32[128,128]{1,0:T(8,128)S(1)} %copy-done.28), channel_id=1, source_target_pairs={{0,4},{1,5},{2,6},{3,7},{4,0},{5,1},{6,2},{7,3},{8,12},{9,13},{10,... | collective-permute-start | bytes 196616 | tf_op jit(solution)/shard_map/ppermute | solution.py:365
  82.5 6.6 %collective-permute-start.28 = (f32[128,128]{1,0:T(8,128)S(1)}, f32[128,128]{1,0:T(8,128)S(1)}, u32[]{:S(2)}, u32[]{:S(2)}) collective-permute-start(f32[128,128]{1,0:T(8,128)S(1)} %add.15.refs_10_), channel_id=1, source_target_pairs={{0,8},{1,9},{2,10},{3,11},{4,12},{5,13},{6,14},{7,15},{8,0},{9,1},... | collective-permute-start | bytes 196616 | tf_op jit(solution)/shard_map/ppermute | solution.py:365
  83.7 5.4 %collective-permute-start.29 = (f32[128,128]{1,0:T(8,128)S(1)}, f32[128,128]{1,0:T(8,128)S(1)}, u32[]{:S(2)}, u32[]{:S(2)}) collective-permute-start(f32[128,128]{1,0:T(8,128)S(1)} %add.15.refs_10_), channel_id=1, source_target_pairs={{0,16},{1,17},{2,18},{3,19},{4,20},{5,21},{6,22},{7,23},{8,24},{9,... | collective-permute-start | bytes 196616 | tf_op jit(solution)/shard_map/ppermute | solution.py:365
  85.1 5.2 %collective-permute-start.30 = (f32[128,128]{1,0:T(8,128)S(1)}, f32[128,128]{1,0:T(8,128)S(1)}, u32[]{:S(2)}, u32[]{:S(2)}) collective-permute-start(f32[128,128]{1,0:T(8,128)S(1)} %add.15.refs_10_), channel_id=1, source_target_pairs={{0,24},{1,25},{2,26},{3,27},{4,28},{5,29},{6,30},{7,31},{8,16},{9,... | collective-permute-start | bytes 196616 | tf_op jit(solution)/shard_map/ppermute | solution.py:365
  90.8 1.7 %collective-permute-start.31 = (f32[128,128]{1,0:T(8,128)S(1)}, f32[128,128]{1,0:T(8,128)S(1)}, u32[]{:S(2)}, u32[]{:S(2)}) collective-permute-start(f32[128,128]{1,0:T(8,128)S(1)} %get-tuple-element.78), channel_id=1, source_target_pairs={{0,4},{1,5},{2,6},{3,7},{4,0},{5,1},{6,2},{7,3},{8,12},{9,13},{10,... | collective-permute-start | bytes 196616 | tf_op jit(solution)/shard_map/ppermute | solution.py:365
  (19 other events, 14.4 us)

commit v13 on v12

--- a/solution.py
+++ b/solution.py
@@ -130,9 +130,7 @@
     q_ref,
     k_ref,
     v_ref,
-    probs_ref,
-    inner_ref,
-    soft_ref,
+    store_ref,
     mine_ref,
     other_ref,
     far_ref,
@@ -166,9 +164,8 @@
             probs = (expo / jnp.sum(expo, -1, keepdims=True)).astype(BF16)
             v = v_ref[upto, cols]
             soft = dot(probs, v, NN)
-            probs_ref[h, here, upto] = probs
-            inner_ref[h, here, upto] = inner
-            soft_ref[here, cols] = soft
+            store_ref[h, here, upto] = probs
+            store_ref[2 + h, here, upto] = inner
             sums.append(soft + scale * dot(inner, v, NN))
         mine_ref[here], other_ref[here] = pick(where[2], sums)
     far_ref[...] = q_ref[:, pl.ds(pl.multiple_of((1 - where[2]) * DH, DH), DH)]
@@ -197,21 +194,24 @@
     keep_ref[...], back_ref[...] = carry(flags, here_ref, got_ref, totals)
 
 
-def attn_kernel(scale, count, flags, where, here_ref, got_ref, *refs):
-    totals, refs = refs[: -count - 6], refs[-count - 6 :]
-    q_ref, far_ref, pre_ref, far_pre_ref = refs[:4]
-    out_refs, (keep_ref, back_ref) = refs[4:-2], refs[-2:]
+def attn_kernel(scale, flags, where, here_ref, got_ref, *refs):
+    totals, refs = refs[:-7], refs[-7:]
+    q_ref, far_ref, pre_ref, far_pre_ref, out_ref, keep_ref, back_ref = refs
     keep, back = carry(flags, here_ref, got_ref, totals)
     keep_ref[...], back_ref[...] = keep, back
+    count = out_ref.shape[0]
     own = pre_ref.shape[0] // count
     cols = pl.ds(pl.multiple_of(where[2] * DH, DH), DH)
-    for s, out_ref in enumerate(out_refs):
-        block = lax.rem(where[0] + s, count)
-        here = pl.ds(pl.multiple_of(block * own, own), own)
-        mine = pre_ref[here] + scale * dot_wide(q_ref[here, cols], keep, NN)
-        mate = far_pre_ref[here] + scale * dot_wide(far_ref[here], back, NN)
-        out_ref[:own] = mine.astype(BF16)
-        out_ref[own:] = mate.astype(BF16)
+    mine = pre_ref[...] + scale * dot_wide(q_ref[:, cols], keep, NN)
+    mate = far_pre_ref[...] + scale * dot_wide(far_ref[...], back, NN)
+    for z in range(count):
+        out_ref[z, :own] = mine[z * own : (z + 1) * own].astype(BF16)
+        out_ref[z, own:] = mate[z * own : (z + 1) * own].astype(BF16)
+
+
+def back_along(attn_ref, place):
+    count = attn_ref.shape[0]
+    return jnp.concatenate([attn_ref[lax.rem(place - s + count, count)] for s in range(count)], 1)
 
 
 def first_kernel(spots, left_ref, weight_ref, right_ref, own_ref, half_ref):
@@ -232,16 +232,14 @@
     out_ref[...] = (half_ref[...] + dot(left_ref[...], right_ref[...], NT)).astype(BF16)
 
 
-def near_kernel(spots, left_ref, right_ref, *refs):
-    attn, (half_ref, own_out, mate_out) = refs[:-3], refs[-3:]
+def near_kernel(spots, left_ref, right_ref, attn_ref, half_ref, own_out, mate_out):
     half_ref[...] = dot(left_ref[...], right_ref[2 * DH : 3 * DH], NT)
-    far_kernel(spots, right_ref, *attn, own_out, mate_out)
-
-
-def far_kernel(spots, right_ref, *refs):
-    attn, (own_out, mate_out) = refs[:-2], refs[-2:]
+    far_kernel(spots, right_ref, attn_ref, own_out, mate_out)
+
+
+def far_kernel(spots, right_ref, attn_ref, own_out, mate_out):
     own = own_out.shape[0]
-    part = dot(jnp.concatenate([a[...] for a in attn], 1), right_ref[...], NN)
+    part = dot(back_along(attn_ref, spots[3]), right_ref[...], NN)
     own_out[...] = part[:own]
     mate_out[...] = part[own:]
 
@@ -257,16 +255,11 @@
     out_ref[...] = total.astype(out_ref.dtype)
 
 
-def mixed_kernel(count, each, places, *refs):
-    attn, weight = refs[:count], refs[count]
-    chunks, (own_out, mate_out) = list(refs[count + 1 : -2]), refs[-2:]
+def mixed_kernel(where, attn_ref, *refs):
+    chunks, (own_out, mate_out) = refs[:-2], refs[-2:]
     own = own_out.shape[0]
-    left = jnp.concatenate([a[...] for a in attn], 1)
-    right = [weight[:, pl.ds(pl.multiple_of(places[0], DH), own_out.shape[1])]]
-    for n in each:
-        parts = [chunks.pop(0)[...] for _ in range(n)]
-        right.append(jnp.concatenate(parts, 1) if n > 1 else parts[0])
-    part = dot(left, jnp.concatenate(right, 0), NN)
+    right = jnp.concatenate([chunk[...] for chunk in chunks], 0)
+    part = dot(back_along(attn_ref, where[0]), right, NN)
     own_out[...] = part[:own]
     mate_out[...] = part[own:]
 
@@ -304,9 +297,7 @@
     k_ref,
     v_ref,
     g_ref,
-    probs_ref,
-    inner_ref,
-    soft_ref,
+    store_ref,
     mine_ref,
     other_ref,
     dq_ref,
@@ -325,9 +316,9 @@
             upto = slice(0, (i + 1) * blk)
             q, g = q_ref[here, cols], g_ref[here, cols]
             k = k_ref[upto, cols]
-            probs = probs_ref[h, here, upto]
-            dprod = dot(g, v_ref[upto, cols], NT)
-            delta = jnp.sum(g.astype(F32) * soft_ref[here, cols], -1, keepdims=True)
+            probs, v = store_ref[h, here, upto], v_ref[upto, cols]
+            dprod = dot(g, v, NT)
+            delta = jnp.sum(g.astype(F32) * dot(probs, v, NN), -1, keepdims=True)
             dscore = (probs.astype(F32) * (dprod - delta) * inv_root).astype(BF16)
             last = jnp.where(triangle, dprod[:, i * blk :], 0.0)
             dinner = jnp.concatenate([dprod[:, : i * blk], last], 1) if i else last
@@ -337,7 +328,7 @@
                 + scale * (dot(dinner, k, NN) + dot_wide(g, states[h], NT))
             ).astype(BF16)
             dk = dot(dscore, q, TN) + scale * dot(dinner, q, TN)
-            dv = dot(probs, g, TN) + scale * dot(inner_ref[h, here, upto], g, TN)
+            dv = dot(probs, g, TN) + scale * dot(store_ref[2 + h, here, upto], g, TN)
             if i == count - 1:
                 dk_ref[upto, cols] = dk
                 dv_ref[upto, cols] = dv
@@ -407,10 +398,9 @@
     arrived = {1: send(piece, 0, 1), count - 1: send(piece, 0, -1)}
     mate_cotangent = send(cotangent, 1, 0)
 
-    probs, inner, soft, pre, other_pre, far, mine, other = call(
+    store, pre, other_pre, far, mine, other = call(
         functools.partial(forward_kernel, scale),
-        [((heads, rows, rows), BF16)] * 2
-        + [(flat, F32)]
+        [((2 * heads, rows, rows), BF16)]
         + [((rows, DH), F32)] * 2
         + [((rows, DH), BF16)]
         + pair,
@@ -422,14 +412,16 @@
     far, other_pre = send(far, 1, 0), send(other_pre, 1, 0)
     (mine,) = hold([mine], [far, other_pre])
     flags, parts, total = exchange(mine, other, core, chip, chips, False)
-    *attn, keep, back = call(
-        functools.partial(attn_kernel, scale, count),
-        [tokens] * count + pair,
+    attn, keep, back = call(
+        functools.partial(attn_kernel, scale),
+        [((count, *tokens[0]), BF16), *pair],
         [*parts, query, far, pre, other_pre],
         [flags, where],
     )
     linear = [keep, send(back, 1, 0)]
-    attn = [attn[0]] + [send(attn[s], 0, s) for s in range(1, count)]
+    if board:
+        arrived[1], arrived[3] = hold([arrived[1], arrived[3]], [keep])
+    attn = lax.all_to_all(attn, "head", 0, 0, tiled=True)
 
     work = near_and_far if board else by_gathers
     both, across, joins, starts = work(
@@ -449,7 +441,7 @@
     grad_query, dk, dv = call(
         functools.partial(backward_kernel, scale, blocks),
         [(flat, BF16)] + [(flat, F32)] * 2,
-        [query, key, value, g, probs, inner, soft, *linear],
+        [query, key, value, g, store, *linear],
         [where],
         [total],
         flops=14 * square,
@@ -468,7 +460,8 @@
 def near_and_far(attn, arrived, cotangent, mate_cotangent, weight, core, chip, colour, product):
     own, model = cotangent.shape
     wide = model // 2
-    spots = jnp.stack([colour * wide, (1 - colour) * wide, core * DH])
+    place = lax.axis_index("head")
+    spots = jnp.stack([colour * wide, (1 - colour) * wide, core * DH, place])
     tokens = ((2 * own, DH), BF16)
     parts = [((own, wide), F32)] * 2
     all_arrays = [(cotangent, all_of, rows_at(0, own)), (mate_cotangent, all_of, rows_at(own, own))]
@@ -489,7 +482,6 @@
     def stacked(*arrays):
         return [(a, all_of, rows_at(n * DH, DH)) for n, a in enumerate(arrays)]
 
-    arrived[1], arrived[3] = hold([arrived[1], arrived[3]], attn[:1])
     arrived[2] = send(arrived[1], 0, 1)
     second = {1: send(arrived[1], 2, 0), 3: send(arrived[3], 4, 0)}
     mine, half = call(
@@ -530,7 +522,7 @@
                 (weight, own_columns(0), rows_at(0, DH)),
                 *((arrived[s], all_of, rows_at(s * DH, DH)) for s in (1, 2, 3)),
             ),
-            *attn,
+            attn,
         ],
         [spots],
         room=6,
@@ -563,7 +555,7 @@
                 (second[3], all_of, rows_at(3 * DH, DH)),
                 *((a, all_of, quarter(n)) for n, a in enumerate(second[2])),
             ),
-            *attn,
+            attn,
         ],
         [spots],
         [both[2], across[0], across[1], across[3]],
@@ -598,10 +590,10 @@
         )
         both.append(send(block, 0, -s) if s else block)
     part, mate_part = call(
-        functools.partial(mixed_kernel, count, [1] * (count - 1)),
+        mixed_kernel,
         [((own, model), F32)] * 2,
-        [*attn, *chunks],
-        [zero],
+        [attn, *chunks],
+        [lax.axis_index("head").reshape(1)],
         room=6,
         flops=count * product,
     )

time: 94.9 us -> 92.6 us (0.976)
  waiting for transfers between devices: 25.4 us -> 19.2 us
  Pallas kernels: 22.8 us -> 26.8 us
    ppermute x32 -> x29, waiting for transfers between devices: 25.4 us -> 19.2 us  [send(): return lax.ppermute(x, ('ctx', 'head'), pairs)]
    all_to_all x0 -> x1, starting transfers between devices: none -> 5.09 us  [on_device(): attn = lax.all_to_all(attn, 'head', 0, 0, tiled=True)]
    ppermute x32 -> x29, starting transfers between devices: 24.4 us -> 19.7 us  [send(): return lax.ppermute(x, ('ctx', 'head'), pairs)]
    pallas_call x12, Pallas kernels: 22.8 us -> 26.8 us  [call(): pl.pallas_call(kernel, out_shape=[jax.ShapeDtypeStruct(s, t) for s, t in...]
    unnamed x70 -> x62, local copies, waits for them, and re-layouts: 17.5 us -> 16.9 us
  transfers between devices with their start and end apart: 32 -> 30, of which waited for: 11 -> 9; matrix products, arithmetic and copies ran while one was open for 3% -> 3% of each run, Pallas kernels for 20% -> 27%
where the time goes in v13:
time: 92.6 us; the launch traced here: 91.6 us
  Pallas kernels  26.8 us (29%)
  starting transfers between devices  24.8 us (27%)
  waiting for transfers between devices  19.2 us (21%)
  local copies, waits for them, and re-layouts  18.7 us (20%)
  other arithmetic  1.27 us (1%)
    pallas_call x12, Pallas kernels, call(): pl.pallas_call(kernel, out_shape=[jax.ShapeDtypeStruct(s, t) for s, t in...  26.8 us
    ppermute x29, starting transfers between devices, send(): return lax.ppermute(x, ('ctx', 'head'), pairs)  19.7 us
    ppermute x29, waiting for transfers between devices, send(): return lax.ppermute(x, ('ctx', 'head'), pairs)  19.2 us
    unnamed x62, local copies, waits for them, and re-layouts  16.9 us
    all_to_all x1, starting transfers between devices, on_device(): attn = lax.all_to_all(attn, 'head', 0, 0, tiled=True)  5.09 us
    dynamic_slice x1, local copies, waits for them, and re-layouts, on_device(): lax.dynamic_slice(out_weight, (core * DH, colour * wide), (DH, wide))  1.88 us
  transfers between devices with their start and end apart: 30, of which 9 were waited for; matrix products, arithmetic and copies ran while one was open for 3% of the time, Pallas kernels for 27%

profile of v13, /device:TPU:0, one launch (start us, length us, event | category | flops | bytes accessed | tf_op | source)
XLA Modules:
  0.0 91.6 jit_solution(5407075309021821242)
XLA Ops:
  1.1 1.9 %dynamic_slice.3 = bf16[128,2048]{1,0:T(8,128)(2,1)} dynamic-slice(bf16[256,4096]{1,0:T(8,128)(2,1)} %refs_1_.12, s32[]{:T(128)S(6)} %select_n.6, s32[]{:T(128)S(6)} %select_n.7), dynamic_slice_sizes={128,2048} | dynamic-slice | bytes 1048580 | tf_op jit(solution)/shard_map/dynamic_slice | solution.py:397
  3.0 2.6 %collective-permute-start.1 = (bf16[128,2048]{1,0:T(8,128)(2,1)}, bf16[128,2048]{1,0:T(8,128)(2,1)S(1)}, u32[]{:S(2)}, u32[]{:S(2)}) collective-permute-start(bf16[128,2048]{1,0:T(8,128)(2,1)} %dynamic_slice.3), channel_id=1, source_target_pairs={{0,1},{1,2},{2,3},{3,0},{4,5},{5,6},{6,7},{7,4},{8,9},{9,10},{10,1... | collective-permute-start | bytes 1572872 | tf_op jit(solution)/shard_map/ppermute | solution.py:356
  5.6 2.0 %collective-permute-start.2 = (bf16[128,2048]{1,0:T(8,128)(2,1)}, bf16[128,2048]{1,0:T(8,128)(2,1)}, u32[]{:S(2)}, u32[]{:S(2)}) collective-permute-start(bf16[128,2048]{1,0:T(8,128)(2,1)} %dynamic_slice.3), channel_id=1, source_target_pairs={{0,3},{1,0},{2,1},{3,2},{4,7},{5,4},{6,5},{7,6},{8,11},{9,8},{10,9... | collective-permute-start | bytes 1572872 | tf_op jit(solution)/shard_map/ppermute | solution.py:356
  7.8 1.1 %copy-done.6 = bf16[384,256]{1,0:T(8,128)(2,1)S(1)} copy-done((bf16[384,256]{1,0:T(8,128)(2,1)S(1)}, bf16[384,256]{1,0:T(8,128)(2,1)}, u32[]{:S(2)}) %copy-start.6) | copy-done | bytes 196632
  8.8 0.9 %copy-done.9 = bf16[384,256]{1,0:T(8,128)(2,1)S(1)} copy-done((bf16[384,256]{1,0:T(8,128)(2,1)S(1)}, bf16[384,256]{1,0:T(8,128)(2,1)}, u32[]{:S(2)}) %copy-start.9) | copy-done | bytes 196632
  9.8 0.9 %copy-done.11 = bf16[384,256]{1,0:T(8,128)(2,1)S(1)} copy-done((bf16[384,256]{1,0:T(8,128)(2,1)S(1)}, bf16[384,256]{1,0:T(8,128)(2,1)}, u32[]{:S(2)}) %copy-start.11) | copy-done | bytes 196632
  10.7 0.7 copy-done.28
  11.4 2.7 %shard_map.93 = (bf16[4,384,384]{2,1,0:T(8,128)(2,1)S(1)}, f32[384,128]{1,0:T(8,128)S(1)}, f32[384,128]{1,0:T(8,128)}, bf16[384,128]{1,0:T(8,128)(2,1)}, f32[128,128]{1,0:T(8,128)S(1)}, /*index=5*/f32[128,128]{1,0:T(8,128)}) custom-call(s32[3,3]{1,0:T(4,128)S(1)} %copy-done.28, s32[3]{0:T(128)S(1)} %pad_add_fusion.2.refs_1_.refs_0_, ...), custom_call_target="tpu_custom_call" | custom-call | flops 264241152 | bytes 2392064 | tf_op jit(solution)/shard_map/pallas_call | solution.py:93
  14.1 1.1 %copy-done.13 = bf16[4,384,384]{2,1,0:T(8,128)(2,1)} copy-done((bf16[4,384,384]{2,1,0:T(8,128)(2,1)}, bf16[4,384,384]{2,1,0:T(8,128)(2,1)S(1)}, u32[]{:S(2)}) %copy-start.13) | copy-done | bytes 1179672
  15.8 0.7 copy-done.21
  17.1 1.1 %collective-permute-done.3.refs_1_.refs_8_ = bf16[384,128]{1,0:T(8,128)(2,1)S(1)} collective-permute-done((bf16[384,128]{1,0:T(8,128)(2,1)}, bf16[384,128]{1,0:T(8,128)(2,1)S(1)}, u32[]{:S(2)}, u32[]{:S(2)}) %collective-permute-start.3) | collective-permute-done | bytes 98336 | tf_op jit(solution)/shard_map/ppermute | solution.py:356
  18.2 0.6 copy-done.17
  18.9 0.9 add.14
  19.8 1.7 %collective-permute-start.6 = (f32[128,128]{1,0:T(8,128)S(1)}, f32[128,128]{1,0:T(8,128)S(1)}, u32[]{:S(2)}, u32[]{:S(2)}) collective-permute-start(f32[128,128]{1,0:T(8,128)S(1)} %add.14), channel_id=1, source_target_pairs={{0,8},{1,9},{2,10},{3,11},{4,12},{5,13},{6,14},{7,15},{8,0},{9,1},... | collective-permute-start | bytes 196616 | tf_op jit(solution)/shard_map/ppermute | solution.py:356
  21.5 1.5 %collective-permute-start.7 = (f32[128,128]{1,0:T(8,128)S(1)}, f32[128,128]{1,0:T(8,128)S(1)}, u32[]{:S(2)}, u32[]{:S(2)}) collective-permute-start(f32[128,128]{1,0:T(8,128)S(1)} %add.14), channel_id=1, source_target_pairs={{0,16},{1,17},{2,18},{3,19},{4,20},{5,21},{6,22},{7,23},{8,24},{9,... | collective-permute-start | bytes 196616 | tf_op jit(solution)/shard_map/ppermute | solution.py:356
  23.4 0.7 collective-permute-done.6.refs_4_
  24.1 1.6 %collective-permute-done.7.refs_5_ = f32[128,128]{1,0:T(8,128)S(1)} collective-permute-done((f32[128,128]{1,0:T(8,128)S(1)}, f32[128,128]{1,0:T(8,128)S(1)}, u32[]{:S(2)}, u32[]{:S(2)}) %collective-permute-start.7) | collective-permute-done | bytes 65568 | tf_op jit(solution)/shard_map/ppermute | solution.py:356
  25.8 2.4 %collective-permute-done.8.refs_6_ = f32[128,128]{1,0:T(8,128)S(1)} collective-permute-done((f32[128,128]{1,0:T(8,128)S(1)}, f32[128,128]{1,0:T(8,128)S(1)}, u32[]{:S(2)}, u32[]{:S(2)}) %collective-permute-start.8) | collective-permute-done | bytes 65568 | tf_op jit(solution)/shard_map/ppermute | solution.py:356
  28.2 0.9 %copy-done.7 = bf16[384,256]{1,0:T(8,128)(2,1)S(1)} copy-done((bf16[384,256]{1,0:T(8,128)(2,1)S(1)}, bf16[384,256]{1,0:T(8,128)(2,1)}, u32[]{:S(2)}) %copy-start.7) | copy-done | bytes 196632
  29.1 0.8 copy-done.16
  30.0 0.9 copy-done.18
  30.9 0.9 %copy-done.22 = f32[384,128]{1,0:T(8,128)S(1)} copy-done((f32[384,128]{1,0:T(8,128)S(1)}, f32[384,128]{1,0:T(8,128)}, u32[]{:S(2)}) %copy-start.22) | copy-done | bytes 196632
  31.8 1.2 %shard_map.95 = (bf16[4,192,128]{2,1,0:T(8,128)(2,1)S(1)}, f32[128,128]{1,0:T(8,128)S(1)}, f32[128,128]{1,0:T(8,128)S(1)}) custom-call(s32[4]{0:T(128)S(1)} %add_convert_fusion.refs_0_, s32[3]{0:T(128)S(1)} %pad_add_fusion.2.refs_1_.refs_0_, f32[128,128]{1,0:T(8,128)S(1)} %copy-done.16, f32[128,128]{1,0:T(8,128)} %collective-permute-done.5.refs_3_, ...), custom_call_target="tpu_custom_call" | custom-call | flops 1 | bytes 1343488 | tf_op jit(solution)/shard_map/pallas_call | solution.py:93
  33.7 0.7 copy-done.23
  35.0 0.8 copy-done.3
  36.8 5.1 %all-to-all-start = ((bf16[4,192,128]{2,1,0:T(8,128)(2,1)}), bf16[4,192,128]{2,1,0:T(8,128)(2,1)}, u32[]{:S(2)}, u32[]{:S(2)}) async-start(bf16[4,192,128]{2,1,0:T(8,128)(2,1)} %copy-done.23), calls=%async_computation | async-start | bytes 393216 | tf_op jit(solution)/shard_map/all_to_all | solution.py:424
  42.0 1.1 %copy-done.1 = bf16[96,4096]{1,0:T(8,128)(2,1)S(1)} copy-done((bf16[96,4096]{1,0:T(8,128)(2,1)S(1)}, bf16[96,4096]{1,0:T(8,128)(2,1)}, u32[]{:S(2)}) %copy-start.1) | copy-done | bytes 786456
  43.1 1.0 %copy-done.4 = bf16[128,2048]{1,0:T(8,128)(2,1)S(1)} copy-done((bf16[128,2048]{1,0:T(8,128)(2,1)S(1)}, bf16[128,2048]{1,0:T(8,128)(2,1)}, u32[]{:S(2)}) %copy-start.4) | copy-done | bytes 524312
  44.2 3.3 %shard_map.98 = (bf16[192,128]{1,0:T(8,128)(2,1)}, f32[192,256]{1,0:T(8,128)S(1)}) custom-call(s32[4]{0:T(128)S(1)} %pad_add_fusion.1.refs_0_, bf16[96,4096]{1,0:T(8,128)(2,1)S(1)} %copy-done.1, bf16[96,4096]{1,0:T(8,128)(2,1)S(1)} %collective-permute-done.refs_5_.refs_2_, bf16[256,4096]{1,0:T(8,128)(2,1)S(1)} %copy-done, bf16[128,2048]{1,0:T(8,128)(2,1)S(1)} %copy-done.4, ...), custom_call_target="tpu_custom_call" | custom-call | flops 402653184 | bytes 4964352 | tf_op jit(solution)/shard_map/pallas_call | solution.py:93
  47.5 4.6 %collective-permute-done.9.refs_5_.refs_6_ = bf16[128,2048]{1,0:T(8,128)(2,1)} collective-permute-done((bf16[128,2048]{1,0:T(8,128)(2,1)}, bf16[128,2048]{1,0:T(8,128)(2,1)}, u32[]{:S(2)}, u32[]{:S(2)}) %collective-permute-start.9) | collective-permute-done | bytes 524320 | tf_op jit(solution)/shard_map/ppermute | solution.py:356
  52.0 3.3 %shard_map.99 = (bf16[192,128]{1,0:T(8,128)(2,1)}, bf16[192,128]{1,0:T(8,128)(2,1)}, bf16[128,1024]{1,0:T(8,128)(2,1)}, bf16[128,1024]{1,0:T(8,128)(2,1)}) custom-call(s32[4]{0:T(128)S(1)} %pad_add_fusion.1.refs_0_, bf16[96,4096]{1,0:T(8,128)(2,1)S(1)} %copy-done.1, bf16[96,4096]{1,0:T(8,128)(2,1)S(1)} %collective-permute-done.refs_5_.refs_2_, ...), custom_call_target="tpu_custom_call" | custom-call | flops 201326592 | bytes 3964928 | tf_op jit(solution)/shard_map/pallas_call | solution.py:93
  56.5 1.4 %collective-permute-start.15 = (bf16[192,128]{1,0:T(8,128)(2,1)}, bf16[192,128]{1,0:T(8,128)(2,1)S(1)}, u32[]{:S(2)}, u32[]{:S(2)}) collective-permute-start(bf16[192,128]{1,0:T(8,128)(2,1)} %get-tuple-element.53), channel_id=1, source_target_pairs={{0,3},{1,0},{2,1},{3,2},{4,7},{5,4},{6,5},{7,6},{8,11},{9,8},{10,9... | collective-permute-start | bytes 147464 | tf_op jit(solution)/shard_map/ppermute | solution.py:356
  57.8 0.7 collective-permute-start.16
  58.5 1.1 %copy-done.2 = bf16[96,4096]{1,0:T(8,128)(2,1)S(1)} copy-done((bf16[96,4096]{1,0:T(8,128)(2,1)S(1)}, bf16[96,4096]{1,0:T(8,128)(2,1)}, u32[]{:S(2)}) %copy-start.2) | copy-done | bytes 786456
  60.3 3.1 %shard_map.97 = (f32[192,128]{1,0:T(8,128)S(1)}, f32[96,2048]{1,0:T(8,128)S(1)}, f32[96,2048]{1,0:T(8,128)S(1)}) custom-call(s32[4]{0:T(128)S(1)} %copy-done.27, bf16[96,4096]{1,0:T(8,128)(2,1)S(1)} %copy-done.2, bf16[96,4096]{1,0:T(8,128)(2,1)S(1)} %collective-permute-done.refs_5_.refs_2_, bf16[256,4096]{1,0:T(8,128)(2,1)S(1)} %copy-done, ...), custom_call_target="tpu_custom_call" | custom-call | flops 402653184 | bytes 7110656 | tf_op jit(solution)/shard_map/pallas_call | solution.py:93
  64.1 2.0 %shard_map.100 = bf16[192,128]{1,0:T(8,128)(2,1)S(1)} custom-call(s32[4]{0:T(128)S(1)} %copy-done.27, bf16[96,4096]{1,0:T(8,128)(2,1)S(1)} %copy-done.2, bf16[96,4096]{1,0:T(8,128)(2,1)S(1)} %collective-permute-done.refs_5_.refs_2_, bf16[128,1024]{1,0:T(8,128)(2,1)} %collective-permute-done.13.refs_3_.refs_4_, ...), custom_call_target="tpu_custom_call" | custom-call | flops 100663296 | bytes 2244608 | tf_op jit(solution)/shard_map/pallas_call | solution.py:93
  66.8 5.4 %collective-permute-done.17.refs_7_.refs_4_ = bf16[192,128]{1,0:T(8,128)(2,1)S(1)} collective-permute-done((bf16[192,128]{1,0:T(8,128)(2,1)S(1)}, bf16[192,128]{1,0:T(8,128)(2,1)S(1)}, u32[]{:S(2)}, u32[]{:S(2)}) %collective-permute-start.17) | collective-permute-done | bytes 49184 | tf_op jit(solution)/shard_map/ppermute | solution.py:356
  72.2 3.0 %shard_map.101 = (f32[96,2048]{1,0:T(8,128)S(1)}, f32[96,2048]{1,0:T(8,128)S(1)}) custom-call(s32[4]{0:T(128)S(1)} %copy-done.27, bf16[256,4096]{1,0:T(8,128)(2,1)S(1)} %copy-done, bf16[128,2048]{1,0:T(8,128)(2,1)} %collective-permute-done.11.refs_3_.refs_2_, bf16[128,2048]{1,0:T(8,128)(2,1)} %collective-permute-done.12.refs_4_.refs_3_, ...), custom_call_target="tpu_custom_call" | custom-call | flops 402653184 | bytes 5439488 | tf_op jit(solution)/shard_map/pallas_call | solution.py:93
  75.8 1.8 %collective-permute-done.22.refs_8_ = bf16[192,128]{1,0:T(8,128)(2,1)S(1)} collective-permute-done((bf16[192,128]{1,0:T(8,128)(2,1)S(1)}, bf16[192,128]{1,0:T(8,128)(2,1)S(1)}, u32[]{:S(2)}, u32[]{:S(2)}) %collective-permute-start.22) | collective-permute-done | bytes 49184 | tf_op jit(solution)/shard_map/ppermute | solution.py:356
  77.6 1.1 %shard_map.103 = (bf16[384,256]{1,0:T(8,128)(2,1)S(1)}, f32[128,128]{1,0:T(8,128)S(1)}, f32[128,128]{1,0:T(8,128)S(1)}) custom-call(s32[3]{0:T(128)S(1)} %copy-done.25, bf16[384,256]{1,0:T(8,128)(2,1)S(1)} %copy-done.8, bf16[192,128]{1,0:T(8,128)(2,1)} %get-tuple-element.55.refs_2_, bf16[192,128]{1,0:T(8,128)(2,1)S(1)} %collective-permute-done.15.refs_6_.refs_3_, ...), custom_call_target="tpu_custom_call" | custom-call | flops 1 | bytes 917504 | tf_op jit(solution)/shard_map/pallas_call | solution.py:93
  79.3 0.7 collective-permute-done.24.refs_2_
  80.0 1.1 %collective-permute-start.25 = (f32[128,128]{1,0:T(8,128)S(1)}, f32[128,128]{1,0:T(8,128)S(1)}, u32[]{:S(2)}, u32[]{:S(2)}) collective-permute-start(f32[128,128]{1,0:T(8,128)S(1)} %add.15.refs_8_), channel_id=1, source_target_pairs={{0,8},{1,9},{2,10},{3,11},{4,12},{5,13},{6,14},{7,15},{8,0},{9,1},... | collective-permute-start | bytes 196616 | tf_op jit(solution)/shard_map/ppermute | solution.py:356
  81.1 1.4 %collective-permute-start.26 = (f32[128,128]{1,0:T(8,128)S(1)}, f32[128,128]{1,0:T(8,128)S(1)}, u32[]{:S(2)}, u32[]{:S(2)}) collective-permute-start(f32[128,128]{1,0:T(8,128)S(1)} %add.15.refs_8_), channel_id=1, source_target_pairs={{0,16},{1,17},{2,18},{3,19},{4,20},{5,21},{6,22},{7,23},{8,24},{9,... | collective-permute-start | bytes 196616 | tf_op jit(solution)/shard_map/ppermute | solution.py:356
  82.5 1.0 %collective-permute-start.27 = (f32[128,128]{1,0:T(8,128)S(1)}, f32[128,128]{1,0:T(8,128)S(1)}, u32[]{:S(2)}, u32[]{:S(2)}) collective-permute-start(f32[128,128]{1,0:T(8,128)S(1)} %add.15.refs_8_), channel_id=1, source_target_pairs={{0,24},{1,25},{2,26},{3,27},{4,28},{5,29},{6,30},{7,31},{8,16},{9,... | collective-permute-start | bytes 196616 | tf_op jit(solution)/shard_map/ppermute | solution.py:356
  83.7 3.3 %shard_map.104 = (bf16[384,256]{1,0:T(8,128)(2,1)}, f32[384,256]{1,0:T(8,128)S(1)}, f32[384,256]{1,0:T(8,128)S(1)}) custom-call(s32[3]{0:T(128)S(1)} %copy-done.25, bf16[384,256]{1,0:T(8,128)(2,1)S(1)} %copy-done.8, bf16[384,256]{1,0:T(8,128)(2,1)S(1)} %copy-done.10, bf16[384,256]{1,0:T(8,128)(2,1)S(1)} %copy-done.12, ...), custom_call_target="tpu_custom_call" | custom-call | flops 528482304 | bytes 3080192 | tf_op jit(solution)/shard_map/pallas_call | solution.py:93
  87.0 0.7 collective-permute-done.27.refs_5_
  88.4 1.6 %shard_map.102 = (bf16[96,4096]{1,0:T(8,128)(2,1)}, f32[8,128]{1,0:T(8,128)S(1)}) custom-call(s32[2]{0:T(128)S(1)} %pad_add_fusion.refs_0_, f32[96,2048]{1,0:T(8,128)S(1)} %get-tuple-element.47.refs_1_, f32[96,2048]{1,0:T(8,128)S(1)} %collective-permute-done.10.refs_2_, f32[96,2048]{1,0:T(8,128)S(1)} %get-tuple-element.56.refs_3_, ...), custom_call_target="tpu_custom_call" | custom-call | flops 1 | bytes 3936256 | tf_op jit(solution)/shard_map/pallas_call | solution.py:93
  90.0 1.6 %shard_map.106 = (bf16[384,256]{1,0:T(8,128)(2,1)}, bf16[384,256]{1,0:T(8,128)(2,1)}) custom-call(s32[3]{0:T(128)S(1)} %copy-done.25, bf16[384,256]{1,0:T(8,128)(2,1)S(1)} %copy-done.10, bf16[384,256]{1,0:T(8,128)(2,1)S(1)} %copy-done.12, f32[384,256]{1,0:T(8,128)S(1)} %get-tuple-element.65.refs_6_.refs_3_, f32[384,256]{1,0:T(8,128)S(1)} %get-tuple-element.66.refs_4_, ...), custom_call_target="tpu_custom_call" | custom-call | flops 1 | bytes 1703936 | tf_op jit(solution)/shard_map/pallas_call | solution.py:93
  (96 shorter events, 9.8 us)
Async XLA Ops:
  0.6 7.1 %collective-permute-start = (bf16[96,4096]{1,0:T(8,128)(2,1)}, bf16[96,4096]{1,0:T(8,128)(2,1)S(1)}, u32[]{:S(2)}, u32[]{:S(2)}) collective-permute-start(bf16[96,4096]{1,0:T(8,128)(2,1)} %refs_1_.11), channel_id=1, source_target_pairs={{0,4},{1,5},{2,6},{3,7},{4,0},{5,1},{6,2},{7,3},{8,12},{9,13},{10,... | collective-permute-start | bytes 2359304 | tf_op jit(solution)/shard_map/ppermute | solution.py:356
  3.0 31.9 %collective-permute-start.1 = (bf16[128,2048]{1,0:T(8,128)(2,1)}, bf16[128,2048]{1,0:T(8,128)(2,1)S(1)}, u32[]{:S(2)}, u32[]{:S(2)}) collective-permute-start(bf16[128,2048]{1,0:T(8,128)(2,1)} %dynamic_slice.3), channel_id=1, source_target_pairs={{0,1},{1,2},{2,3},{3,0},{4,5},{5,6},{6,7},{7,4},{8,9},{9,10},{10,1... | collective-permute-start | bytes 1572872 | tf_op jit(solution)/shard_map/ppermute | solution.py:356
  5.6 29.3 %collective-permute-start.2 = (bf16[128,2048]{1,0:T(8,128)(2,1)}, bf16[128,2048]{1,0:T(8,128)(2,1)}, u32[]{:S(2)}, u32[]{:S(2)}) collective-permute-start(bf16[128,2048]{1,0:T(8,128)(2,1)} %dynamic_slice.3), channel_id=1, source_target_pairs={{0,3},{1,0},{2,1},{3,2},{4,7},{5,4},{6,5},{7,6},{8,11},{9,8},{10,9... | collective-permute-start | bytes 1572872 | tf_op jit(solution)/shard_map/ppermute | solution.py:356
  7.7 29.1 %copy-start.24 = (s32[3]{0:T(128)}, s32[3]{0:T(128)S(1)}, u32[]{:S(2)}) copy-start(s32[3]{0:T(128)S(1)} %pad_add_fusion.2.refs_1_.refs_0_) | copy-start | bytes 40
  7.7 34.2 %copy-start = (bf16[256,4096]{1,0:T(8,128)(2,1)S(1)}, bf16[256,4096]{1,0:T(8,128)(2,1)}, u32[]{:S(2)}) copy-start(bf16[256,4096]{1,0:T(8,128)(2,1)} %refs_1_.12) | copy-start | bytes 6291460
  7.8 1.1 %copy-start.6 = (bf16[384,256]{1,0:T(8,128)(2,1)S(1)}, bf16[384,256]{1,0:T(8,128)(2,1)}, u32[]{:S(2)}) copy-start(bf16[384,256]{1,0:T(8,128)(2,1)} %refs_1_.14) | copy-start | bytes 589828
  8.8 0.9 %copy-start.9 = (bf16[384,256]{1,0:T(8,128)(2,1)S(1)}, bf16[384,256]{1,0:T(8,128)(2,1)}, u32[]{:S(2)}) copy-start(bf16[384,256]{1,0:T(8,128)(2,1)} %refs_1_.15) | copy-start | bytes 589828
  14.1 1.1 %copy-start.13 = (bf16[4,384,384]{2,1,0:T(8,128)(2,1)}, bf16[4,384,384]{2,1,0:T(8,128)(2,1)S(1)}, u32[]{:S(2)}) copy-start(bf16[4,384,384]{2,1,0:T(8,128)(2,1)S(1)} %get-tuple-element.60.refs_5_) | copy-start | bytes 3538948
  16.4 1.8 %collective-permute-start.4 = (f32[384,128]{1,0:T(8,128)}, f32[384,128]{1,0:T(8,128)}, u32[]{:S(2)}, u32[]{:S(2)}) collective-permute-start(f32[384,128]{1,0:T(8,128)} %get-tuple-element.40), channel_id=1, source_target_pairs={{0,4},{1,5},{2,6},{3,7},{4,0},{5,1},{6,2},{7,3},{8,12},{9,13},{10,... | collective-permute-start | bytes 589832 | tf_op jit(solution)/shard_map/ppermute | solution.py:356
  16.6 1.6 %collective-permute-start.3 = (bf16[384,128]{1,0:T(8,128)(2,1)}, bf16[384,128]{1,0:T(8,128)(2,1)S(1)}, u32[]{:S(2)}, u32[]{:S(2)}) collective-permute-start(bf16[384,128]{1,0:T(8,128)(2,1)} %get-tuple-element.39), channel_id=1, source_target_pairs={{0,4},{1,5},{2,6},{3,7},{4,0},{5,1},{6,2},{7,3},{8,12},{9,13},{10,... | collective-permute-start | bytes 294920 | tf_op jit(solution)/shard_map/ppermute | solution.py:356
  17.0 1.9 %collective-permute-start.5 = (f32[128,128]{1,0:T(8,128)}, f32[128,128]{1,0:T(8,128)}, u32[]{:S(2)}, u32[]{:S(2)}) collective-permute-start(f32[128,128]{1,0:T(8,128)} %get-tuple-element.41), channel_id=1, source_target_pairs={{0,4},{1,5},{2,6},{3,7},{4,0},{5,1},{6,2},{7,3},{8,12},{9,13},{10,... | collective-permute-start | bytes 196616 | tf_op jit(solution)/shard_map/ppermute | solution.py:356
  19.8 4.4 %collective-permute-start.6 = (f32[128,128]{1,0:T(8,128)S(1)}, f32[128,128]{1,0:T(8,128)S(1)}, u32[]{:S(2)}, u32[]{:S(2)}) collective-permute-start(f32[128,128]{1,0:T(8,128)S(1)} %add.14), channel_id=1, source_target_pairs={{0,8},{1,9},{2,10},{3,11},{4,12},{5,13},{6,14},{7,15},{8,0},{9,1},... | collective-permute-start | bytes 196616 | tf_op jit(solution)/shard_map/ppermute | solution.py:356
  21.5 4.3 %collective-permute-start.7 = (f32[128,128]{1,0:T(8,128)S(1)}, f32[128,128]{1,0:T(8,128)S(1)}, u32[]{:S(2)}, u32[]{:S(2)}) collective-permute-start(f32[128,128]{1,0:T(8,128)S(1)} %add.14), channel_id=1, source_target_pairs={{0,16},{1,17},{2,18},{3,19},{4,20},{5,21},{6,22},{7,23},{8,24},{9,... | collective-permute-start | bytes 196616 | tf_op jit(solution)/shard_map/ppermute | solution.py:356
  23.0 5.2 %collective-permute-start.8 = (f32[128,128]{1,0:T(8,128)S(1)}, f32[128,128]{1,0:T(8,128)S(1)}, u32[]{:S(2)}, u32[]{:S(2)}) collective-permute-start(f32[128,128]{1,0:T(8,128)S(1)} %add.14), channel_id=1, source_target_pairs={{0,24},{1,25},{2,26},{3,27},{4,28},{5,29},{6,30},{7,31},{8,16},{9,... | collective-permute-start | bytes 196616 | tf_op jit(solution)/shard_map/ppermute | solution.py:356
  28.2 0.9 %copy-start.7 = (bf16[384,256]{1,0:T(8,128)(2,1)S(1)}, bf16[384,256]{1,0:T(8,128)(2,1)}, u32[]{:S(2)}) copy-start(bf16[384,256]{1,0:T(8,128)(2,1)} %refs_1_.14) | copy-start | bytes 589828
  35.8 16.3 %collective-permute-start.9 = (bf16[128,2048]{1,0:T(8,128)(2,1)}, bf16[128,2048]{1,0:T(8,128)(2,1)}, u32[]{:S(2)}, u32[]{:S(2)}) collective-permute-start(bf16[128,2048]{1,0:T(8,128)(2,1)} %get-tuple-element.44.refs_4_), channel_id=1, source_target_pairs={{0,1},{1,2},{2,3},{3,0},{4,5},{5,6},{6,7},{7,4},{8,9},{9,10},{10,1... | collective-permute-start | bytes 1572872 | tf_op jit(solution)/shard_map/ppermute | solution.py:356
  35.8 16.3 %collective-permute-start.11 = (bf16[128,2048]{1,0:T(8,128)(2,1)}, bf16[128,2048]{1,0:T(8,128)(2,1)}, u32[]{:S(2)}, u32[]{:S(2)}) collective-permute-start(bf16[128,2048]{1,0:T(8,128)(2,1)} %get-tuple-element.44.refs_4_), channel_id=1, source_target_pairs={{0,8},{1,9},{2,10},{3,11},{4,12},{5,13},{6,14},{7,15},{8,0},{9,1},... | collective-permute-start | bytes 1572872 | tf_op jit(solution)/shard_map/ppermute | solution.py:356
  36.3 15.7 %collective-permute-start.12 = (bf16[128,2048]{1,0:T(8,128)(2,1)}, bf16[128,2048]{1,0:T(8,128)(2,1)}, u32[]{:S(2)}, u32[]{:S(2)}) collective-permute-start(bf16[128,2048]{1,0:T(8,128)(2,1)} %get-tuple-element.45.refs_6_.refs_5_), channel_id=1, source_target_pairs={{0,16},{1,17},{2,18},{3,19},{4,20},{5,21},{6,22},{7,23},{8,24},{9,... | collective-permute-start | bytes 1572872 | tf_op jit(solution)/shard_map/ppermute | solution.py:356
  36.8 21.7 %all-to-all-start = ((bf16[4,192,128]{2,1,0:T(8,128)(2,1)}), bf16[4,192,128]{2,1,0:T(8,128)(2,1)}, u32[]{:S(2)}, u32[]{:S(2)}) async-start(bf16[4,192,128]{2,1,0:T(8,128)(2,1)} %copy-done.23), calls=%async_computation | async-start | bytes 393216 | tf_op jit(solution)/shard_map/all_to_all | solution.py:424
  42.0 1.1 %copy-start.1 = (bf16[96,4096]{1,0:T(8,128)(2,1)S(1)}, bf16[96,4096]{1,0:T(8,128)(2,1)}, u32[]{:S(2)}) copy-start(bf16[96,4096]{1,0:T(8,128)(2,1)} %refs_1_.11) | copy-start | bytes 2359300
  43.1 1.0 %copy-start.4 = (bf16[128,2048]{1,0:T(8,128)(2,1)S(1)}, bf16[128,2048]{1,0:T(8,128)(2,1)}, u32[]{:S(2)}) copy-start(bf16[128,2048]{1,0:T(8,128)(2,1)} %get-tuple-element.44.refs_4_) | copy-start | bytes 1572868
  44.2 7.9 %copy-start.26 = (s32[4]{0:T(128)}, s32[4]{0:T(128)S(1)}, u32[]{:S(2)}) copy-start(s32[4]{0:T(128)S(1)} %pad_add_fusion.1.refs_0_) | copy-start | bytes 52
  47.5 11.0 %copy-start.5 = (bf16[128,2048]{1,0:T(8,128)(2,1)S(1)}, bf16[128,2048]{1,0:T(8,128)(2,1)}, u32[]{:S(2)}) copy-start(bf16[128,2048]{1,0:T(8,128)(2,1)} %get-tuple-element.44.refs_4_) | copy-start | bytes 1572868
  55.3 8.7 %collective-permute-start.13 = (bf16[128,1024]{1,0:T(8,128)(2,1)}, bf16[128,1024]{1,0:T(8,128)(2,1)}, u32[]{:S(2)}, u32[]{:S(2)}) collective-permute-start(bf16[128,1024]{1,0:T(8,128)(2,1)} %get-tuple-element.50), channel_id=1, source_target_pairs={{0,8},{1,9},{2,10},{3,11},{4,12},{5,13},{6,14},{7,15},{8,0},{9,1},... | collective-permute-start | bytes 786440 | tf_op jit(solution)/shard_map/ppermute | solution.py:356
  55.9 8.1 %collective-permute-start.14 = (bf16[128,1024]{1,0:T(8,128)(2,1)}, bf16[128,1024]{1,0:T(8,128)(2,1)}, u32[]{:S(2)}, u32[]{:S(2)}) collective-permute-start(bf16[128,1024]{1,0:T(8,128)(2,1)} %get-tuple-element.51), channel_id=1, source_target_pairs={{0,16},{1,17},{2,18},{3,19},{4,20},{5,21},{6,22},{7,23},{8,24},{9,... | collective-permute-start | bytes 786440 | tf_op jit(solution)/shard_map/ppermute | solution.py:356
  56.5 6.9 %collective-permute-start.15 = (bf16[192,128]{1,0:T(8,128)(2,1)}, bf16[192,128]{1,0:T(8,128)(2,1)S(1)}, u32[]{:S(2)}, u32[]{:S(2)}) collective-permute-start(bf16[192,128]{1,0:T(8,128)(2,1)} %get-tuple-element.53), channel_id=1, source_target_pairs={{0,3},{1,0},{2,1},{3,2},{4,7},{5,4},{6,5},{7,6},{8,11},{9,8},{10,9... | collective-permute-start | bytes 147464 | tf_op jit(solution)/shard_map/ppermute | solution.py:356
  57.8 6.1 %collective-permute-start.16 = (bf16[192,128]{1,0:T(8,128)(2,1)}, bf16[192,128]{1,0:T(8,128)(2,1)S(1)}, u32[]{:S(2)}, u32[]{:S(2)}) collective-permute-start(bf16[192,128]{1,0:T(8,128)(2,1)} %get-tuple-element.54), channel_id=1, source_target_pairs={{0,1},{1,2},{2,3},{3,0},{4,5},{5,6},{6,7},{7,4},{8,9},{9,10},{10,1... | collective-permute-start | bytes 147464 | tf_op jit(solution)/shard_map/ppermute | solution.py:356
  58.5 8.3 %collective-permute-start.18 = (bf16[192,128]{1,0:T(8,128)(2,1)}, bf16[192,128]{1,0:T(8,128)(2,1)S(1)}, u32[]{:S(2)}, u32[]{:S(2)}) collective-permute-start(bf16[192,128]{1,0:T(8,128)(2,1)} %get-tuple-element.55.refs_2_), channel_id=1, source_target_pairs={{0,4},{1,5},{2,6},{3,7},{4,0},{5,1},{6,2},{7,3},{8,12},{9,13},{10,... | collective-permute-start | bytes 147464 | tf_op jit(solution)/shard_map/ppermute | solution.py:356
  58.5 1.1 %copy-start.2 = (bf16[96,4096]{1,0:T(8,128)(2,1)S(1)}, bf16[96,4096]{1,0:T(8,128)(2,1)}, u32[]{:S(2)}) copy-start(bf16[96,4096]{1,0:T(8,128)(2,1)} %refs_1_.11) | copy-start | bytes 2359300
  63.4 3.4 %collective-permute-start.19 = (bf16[192,128]{1,0:T(8,128)(2,1)S(1)}, bf16[192,128]{1,0:T(8,128)(2,1)S(1)}, u32[]{:S(2)}, u32[]{:S(2)}) collective-permute-start(bf16[192,128]{1,0:T(8,128)(2,1)S(1)} %collective-permute-done.15.refs_6_.refs_3_), channel_id=1, source_target_pairs={{0,4},{1,5},{2,6},{3,7},{4,0},{5,1},{6,2},{7,3},{8,12},{9,13},{10,... | collective-permute-start | bytes 147464 | tf_op jit(solution)/shard_map/ppermute | solution.py:356
  64.0 2.8 %collective-permute-start.20 = (bf16[192,128]{1,0:T(8,128)(2,1)S(1)}, bf16[192,128]{1,0:T(8,128)(2,1)S(1)}, u32[]{:S(2)}, u32[]{:S(2)}) collective-permute-start(bf16[192,128]{1,0:T(8,128)(2,1)S(1)} %collective-permute-done.16.refs_7_.refs_5_), channel_id=1, source_target_pairs={{0,4},{1,5},{2,6},{3,7},{4,0},{5,1},{6,2},{7,3},{8,12},{9,13},{10,... | collective-permute-start | bytes 147464 | tf_op jit(solution)/shard_map/ppermute | solution.py:356
  66.1 11.5 %copy-start.8 = (bf16[384,256]{1,0:T(8,128)(2,1)S(1)}, bf16[384,256]{1,0:T(8,128)(2,1)}, u32[]{:S(2)}) copy-start(bf16[384,256]{1,0:T(8,128)(2,1)} %refs_1_.14) | copy-start | bytes 589828
  66.1 11.5 %copy-start.25 = (s32[3]{0:T(128)S(1)}, s32[3]{0:T(128)}, u32[]{:S(2)}) copy-start(s32[3]{0:T(128)} %copy-done.24) | copy-start | bytes 40
  66.1 6.1 %collective-permute-start.17 = (bf16[192,128]{1,0:T(8,128)(2,1)S(1)}, bf16[192,128]{1,0:T(8,128)(2,1)S(1)}, u32[]{:S(2)}, u32[]{:S(2)}) collective-permute-start(bf16[192,128]{1,0:T(8,128)(2,1)S(1)} %shard_map.100), channel_id=1, source_target_pairs={{0,2},{1,3},{2,0},{3,1},{4,6},{5,7},{6,4},{7,5},{8,10},{9,11},{10,... | collective-permute-start | bytes 147464 | tf_op jit(solution)/shard_map/ppermute | solution.py:356
  66.5 12.4 %copy-start.30 = (f32[128,128]{1,0:T(8,128)S(1)}, f32[128,128]{1,0:T(8,128)}, u32[]{:S(2)}) copy-start(f32[128,128]{1,0:T(8,128)} %copy-done.29) | copy-start | bytes 196612
  66.5 17.1 %copy-start.10 = (bf16[384,256]{1,0:T(8,128)(2,1)S(1)}, bf16[384,256]{1,0:T(8,128)(2,1)}, u32[]{:S(2)}) copy-start(bf16[384,256]{1,0:T(8,128)(2,1)} %refs_1_.15) | copy-start | bytes 589828
  66.5 17.1 %copy-start.12 = (bf16[384,256]{1,0:T(8,128)(2,1)S(1)}, bf16[384,256]{1,0:T(8,128)(2,1)}, u32[]{:S(2)}) copy-start(bf16[384,256]{1,0:T(8,128)(2,1)} %refs_2_.5) | copy-start | bytes 589828
  66.5 17.1 %copy-start.14 = (bf16[4,384,384]{2,1,0:T(8,128)(2,1)S(1)}, bf16[4,384,384]{2,1,0:T(8,128)(2,1)}, u32[]{:S(2)}) copy-start(bf16[4,384,384]{2,1,0:T(8,128)(2,1)} %copy-done.13) | copy-start | bytes 3538948
  66.5 17.1 %copy-start.20 = (f32[128,128]{1,0:T(8,128)S(1)}, f32[128,128]{1,0:T(8,128)}, u32[]{:S(2)}) copy-start(f32[128,128]{1,0:T(8,128)} %copy-done.19) | copy-start | bytes 196612
  66.6 21.9 %collective-permute-start.10 = (f32[96,2048]{1,0:T(8,128)S(1)}, f32[96,2048]{1,0:T(8,128)S(1)}, u32[]{:S(2)}, u32[]{:S(2)}) collective-permute-start(f32[96,2048]{1,0:T(8,128)S(1)} %get-tuple-element.48), channel_id=1, source_target_pairs={{0,4},{1,5},{2,6},{3,7},{4,0},{5,1},{6,2},{7,3},{8,12},{9,13},{10,... | collective-permute-start | bytes 2359304 | tf_op jit(solution)/shard_map/ppermute | solution.py:356
  75.2 13.3 %collective-permute-start.21 = (f32[96,2048]{1,0:T(8,128)S(1)}, f32[96,2048]{1,0:T(8,128)S(1)}, u32[]{:S(2)}, u32[]{:S(2)}) collective-permute-start(f32[96,2048]{1,0:T(8,128)S(1)} %get-tuple-element.57), channel_id=1, source_target_pairs={{0,4},{1,5},{2,6},{3,7},{4,0},{5,1},{6,2},{7,3},{8,12},{9,13},{10,... | collective-permute-start | bytes 2359304 | tf_op jit(solution)/shard_map/ppermute | solution.py:356
  75.3 2.3 %collective-permute-start.22 = (bf16[192,128]{1,0:T(8,128)(2,1)S(1)}, bf16[192,128]{1,0:T(8,128)(2,1)S(1)}, u32[]{:S(2)}, u32[]{:S(2)}) collective-permute-start(bf16[192,128]{1,0:T(8,128)(2,1)S(1)} %collective-permute-done.17.refs_7_.refs_4_), channel_id=1, source_target_pairs={{0,4},{1,5},{2,6},{3,7},{4,0},{5,1},{6,2},{7,3},{8,12},{9,13},{10,... | collective-permute-start | bytes 147464 | tf_op jit(solution)/shard_map/ppermute | solution.py:356
  78.7 1.3 %collective-permute-start.24 = (f32[128,128]{1,0:T(8,128)S(1)}, f32[128,128]{1,0:T(8,128)S(1)}, u32[]{:S(2)}, u32[]{:S(2)}) collective-permute-start(f32[128,128]{1,0:T(8,128)S(1)} %get-tuple-element.63), channel_id=1, source_target_pairs={{0,4},{1,5},{2,6},{3,7},{4,0},{5,1},{6,2},{7,3},{8,12},{9,13},{10,... | collective-permute-start | bytes 196616 | tf_op jit(solution)/shard_map/ppermute | solution.py:356
  78.9 3.6 %collective-permute-start.23 = (f32[128,128]{1,0:T(8,128)S(1)}, f32[128,128]{1,0:T(8,128)S(1)}, u32[]{:S(2)}, u32[]{:S(2)}) collective-permute-start(f32[128,128]{1,0:T(8,128)S(1)} %copy-done.30), channel_id=1, source_target_pairs={{0,4},{1,5},{2,6},{3,7},{4,0},{5,1},{6,2},{7,3},{8,12},{9,13},{10,... | collective-permute-start | bytes 196616 | tf_op jit(solution)/shard_map/ppermute | solution.py:356
  80.0 7.0 %collective-permute-start.25 = (f32[128,128]{1,0:T(8,128)S(1)}, f32[128,128]{1,0:T(8,128)S(1)}, u32[]{:S(2)}, u32[]{:S(2)}) collective-permute-start(f32[128,128]{1,0:T(8,128)S(1)} %add.15.refs_8_), channel_id=1, source_target_pairs={{0,8},{1,9},{2,10},{3,11},{4,12},{5,13},{6,14},{7,15},{8,0},{9,1},... | collective-permute-start | bytes 196616 | tf_op jit(solution)/shard_map/ppermute | solution.py:356
  81.1 5.9 %collective-permute-start.26 = (f32[128,128]{1,0:T(8,128)S(1)}, f32[128,128]{1,0:T(8,128)S(1)}, u32[]{:S(2)}, u32[]{:S(2)}) collective-permute-start(f32[128,128]{1,0:T(8,128)S(1)} %add.15.refs_8_), channel_id=1, source_target_pairs={{0,16},{1,17},{2,18},{3,19},{4,20},{5,21},{6,22},{7,23},{8,24},{9,... | collective-permute-start | bytes 196616 | tf_op jit(solution)/shard_map/ppermute | solution.py:356
  82.5 5.2 %collective-permute-start.27 = (f32[128,128]{1,0:T(8,128)S(1)}, f32[128,128]{1,0:T(8,128)S(1)}, u32[]{:S(2)}, u32[]{:S(2)}) collective-permute-start(f32[128,128]{1,0:T(8,128)S(1)} %add.15.refs_8_), channel_id=1, source_target_pairs={{0,24},{1,25},{2,26},{3,27},{4,28},{5,29},{6,30},{7,31},{8,16},{9,... | collective-permute-start | bytes 196616 | tf_op jit(solution)/shard_map/ppermute | solution.py:356
  88.3 1.7 %collective-permute-start.28 = (f32[128,128]{1,0:T(8,128)S(1)}, f32[128,128]{1,0:T(8,128)S(1)}, u32[]{:S(2)}, u32[]{:S(2)}) collective-permute-start(f32[128,128]{1,0:T(8,128)S(1)} %get-tuple-element.68), channel_id=1, source_target_pairs={{0,4},{1,5},{2,6},{3,7},{4,0},{5,1},{6,2},{7,3},{8,12},{9,13},{10,... | collective-permute-start | bytes 196616 | tf_op jit(solution)/shard_map/ppermute | solution.py:356
  (13 other events, 9.6 us)

commit v14 on v13

--- a/solution.py
+++ b/solution.py
@@ -24,7 +24,8 @@
 def dot_wide(a, b, dims):
     high = b.astype(BF16)
     low = (b - high.astype(F32)).astype(BF16)
-    return dot(a, high, dims) + dot(a, low, dims)
+    both = dot(a, jnp.concatenate([high, low], 1 - dims[1][0]), dims)
+    return both[:, :DH] + both[:, DH:]
 
 
 def fetch(shape, *parts):
@@ -127,9 +128,7 @@
     scale,
     mask,
     where,
-    q_ref,
-    k_ref,
-    v_ref,
+    all_ref,
     store_ref,
     mine_ref,
     other_ref,
@@ -137,6 +136,7 @@
     mine_state_ref,
     other_state_ref,
 ):
+    q_ref, k_ref, v_ref = (all_ref.at[n] for n in range(3))
     heads = [slice(h * DH, (h + 1) * DH) for h in range(2)]
     states = [dot(k_ref[:, cols], v_ref[:, cols], TN) for cols in heads]
     mine_state_ref[...], other_state_ref[...] = pick(where[2], states)
@@ -162,11 +162,10 @@
             inner = jnp.concatenate(inner, 1).astype(BF16)
             expo = jnp.exp(scores - jnp.max(scores, -1, keepdims=True))
             probs = (expo / jnp.sum(expo, -1, keepdims=True)).astype(BF16)
-            v = v_ref[upto, cols]
-            soft = dot(probs, v, NN)
             store_ref[h, here, upto] = probs
             store_ref[2 + h, here, upto] = inner
-            sums.append(soft + scale * dot(inner, v, NN))
+            both = dot(jnp.concatenate([probs, inner], 0), v_ref[upto, cols], NN)
+            sums.append(both[:blk] + scale * both[blk:])
         mine_ref[here], other_ref[here] = pick(where[2], sums)
     far_ref[...] = q_ref[:, pl.ds(pl.multiple_of((1 - where[2]) * DH, DH), DH)]
 
@@ -323,12 +322,15 @@
             last = jnp.where(triangle, dprod[:, i * blk :], 0.0)
             dinner = jnp.concatenate([dprod[:, : i * blk], last], 1) if i else last
             dinner = dinner.astype(BF16)
-            dq_ref[here, cols] = (
-                dot(dscore, k, NN)
-                + scale * (dot(dinner, k, NN) + dot_wide(g, states[h], NT))
-            ).astype(BF16)
-            dk = dot(dscore, q, TN) + scale * dot(dinner, q, TN)
-            dv = dot(probs, g, TN) + scale * dot(store_ref[2 + h, here, upto], g, TN)
+            far = slice(upto.stop, 2 * upto.stop)
+            inner = store_ref[2 + h, here, upto]
+            left = dot(jnp.concatenate([dscore, dinner], 0), k, NN)
+            linear = left[blk:] + dot_wide(g, states[h], NT)
+            dq_ref[here, cols] = (left[:blk] + scale * linear).astype(BF16)
+            dk = dot(jnp.concatenate([dscore, dinner], 1), q, TN)
+            dk = dk[upto] + scale * dk[far]
+            dv = dot(jnp.concatenate([probs, inner], 1), g, TN)
+            dv = dv[upto] + scale * dv[far]
             if i == count - 1:
                 dk_ref[upto, cols] = dk
                 dv_ref[upto, cols] = dv
@@ -404,7 +406,7 @@
         + [((rows, DH), F32)] * 2
         + [((rows, DH), BF16)]
         + pair,
-        [query, key, value],
+        [jnp.stack([query, key, value])],
         [block_mask, where],
         [mate_cotangent],
         flops=7 * square,

time: 92.6 us -> 90.6 us (0.978)
  local copies, waits for them, and re-layouts: 18.7 us -> 15.2 us
  other arithmetic: 1.27 us -> 2.45 us
    unnamed x62 -> x56, local copies, waits for them, and re-layouts: 16.9 us -> 13.3 us
    another operation x0 -> x1, other arithmetic: none -> 1.18 us  [on_device(): jnp.stack([query, key, value])]
  transfers between devices with their start and end apart: 30 -> 30, of which waited for: 9 -> 9; matrix products, arithmetic and copies ran while one was open for 3% -> 5% of each run, Pallas kernels for 27% -> 28%
where the time goes in v14:
time: 90.6 us; the launch traced here: 89.7 us
  Pallas kernels  27 us (30%)
  starting transfers between devices  25 us (28%)
  waiting for transfers between devices  19.1 us (21%)
  local copies, waits for them, and re-layouts  15.2 us (17%)
  other arithmetic  2.45 us (3%)
    pallas_call x12, Pallas kernels, call(): pl.pallas_call(kernel, out_shape=[jax.ShapeDtypeStruct(s, t) for s, t in...  27 us
    ppermute x29, starting transfers between devices, send(): return lax.ppermute(x, ('ctx', 'head'), pairs)  20.4 us
    ppermute x29, waiting for transfers between devices, send(): return lax.ppermute(x, ('ctx', 'head'), pairs)  19.1 us
    unnamed x56, local copies, waits for them, and re-layouts  13.3 us
    all_to_all x1, starting transfers between devices, on_device(): attn = lax.all_to_all(attn, 'head', 0, 0, tiled=True)  4.55 us
    dynamic_slice x1, local copies, waits for them, and re-layouts, on_device(): lax.dynamic_slice(out_weight, (core * DH, colour * wide), (DH, wide))  1.88 us
  transfers between devices with their start and end apart: 30, of which 9 were waited for; matrix products, arithmetic and copies ran while one was open for 5% of the time, Pallas kernels for 28%

profile of v14, /device:TPU:0, one launch (start us, length us, event | category | flops | bytes accessed | tf_op | source)
XLA Modules:
  0.0 89.7 jit_solution(10828285756712121858)
XLA Ops:
  1.2 1.9 %dynamic_slice.3 = bf16[128,2048]{1,0:T(8,128)(2,1)} dynamic-slice(bf16[256,4096]{1,0:T(8,128)(2,1)} %refs_1_.12, s32[]{:T(128)S(6)} %select_n.6, s32[]{:T(128)S(6)} %select_n.7), dynamic_slice_sizes={128,2048} | dynamic-slice | bytes 1048580 | tf_op jit(solution)/shard_map/dynamic_slice | solution.py:399
  3.0 2.6 %collective-permute-start.1 = (bf16[128,2048]{1,0:T(8,128)(2,1)}, bf16[128,2048]{1,0:T(8,128)(2,1)S(1)}, u32[]{:S(2)}, u32[]{:S(2)}) collective-permute-start(bf16[128,2048]{1,0:T(8,128)(2,1)} %dynamic_slice.3), channel_id=1, source_target_pairs={{0,1},{1,2},{2,3},{3,0},{4,5},{5,6},{6,7},{7,4},{8,9},{9,10},{10,1... | collective-permute-start | bytes 1572872 | tf_op jit(solution)/shard_map/ppermute | solution.py:358
  5.7 2.0 %collective-permute-start.2 = (bf16[128,2048]{1,0:T(8,128)(2,1)}, bf16[128,2048]{1,0:T(8,128)(2,1)}, u32[]{:S(2)}, u32[]{:S(2)}) collective-permute-start(bf16[128,2048]{1,0:T(8,128)(2,1)} %dynamic_slice.3), channel_id=1, source_target_pairs={{0,3},{1,0},{2,1},{3,2},{4,7},{5,4},{6,5},{7,6},{8,11},{9,8},{10,9... | collective-permute-start | bytes 1572872 | tf_op jit(solution)/shard_map/ppermute | solution.py:358
  7.8 1.2 %pad_maximum_fusion.refs_2_ = bf16[3,384,256]{2,1,0:T(8,128)(2,1)S(1)} fusion(bf16[1,384,256]{2,1,0:T(8,128)(2,1)} %bitcast.18, bf16[1,384,256]{2,1,0:T(8,128)(2,1)} %bitcast.19, bf16[1,384,256]{2,1,0:T(8,128)(2,1)} %bitcast.17), kind=kLoop, calls=%fused_computation | loop fusion | flops 589824 | bytes 1179648 | tf_op jit(solution)/shard_map/stack | solution.py:409
  9.0 3.1 %shard_map.93 = (bf16[4,384,384]{2,1,0:T(8,128)(2,1)S(1)}, f32[384,128]{1,0:T(8,128)S(1)}, f32[384,128]{1,0:T(8,128)}, bf16[384,128]{1,0:T(8,128)(2,1)}, f32[128,128]{1,0:T(8,128)S(1)}, /*index=5*/f32[128,128]{1,0:T(8,128)}) custom-call(s32[3,3]{1,0:T(4,128)S(1)} %copy-done.25, s32[3]{0:T(128)S(1)} %pad_add_fusion.2.refs_1_.refs_0_, ...), custom_call_target="tpu_custom_call" | custom-call | flops 264241152 | bytes 2392064 | tf_op jit(solution)/shard_map/pallas_call | solution.py:94
  12.1 1.1 %copy-done.10 = bf16[4,384,384]{2,1,0:T(8,128)(2,1)} copy-done((bf16[4,384,384]{2,1,0:T(8,128)(2,1)}, bf16[4,384,384]{2,1,0:T(8,128)(2,1)S(1)}, u32[]{:S(2)}) %copy-start.10) | copy-done | bytes 1179672
  13.8 0.7 copy-done.18
  15.1 1.1 %collective-permute-done.3.refs_1_.refs_8_ = bf16[384,128]{1,0:T(8,128)(2,1)S(1)} collective-permute-done((bf16[384,128]{1,0:T(8,128)(2,1)}, bf16[384,128]{1,0:T(8,128)(2,1)S(1)}, u32[]{:S(2)}, u32[]{:S(2)}) %collective-permute-start.3) | collective-permute-done | bytes 98336 | tf_op jit(solution)/shard_map/ppermute | solution.py:358
  16.2 0.6 copy-done.14
  16.9 0.9 add.14
  17.8 1.7 %collective-permute-start.6 = (f32[128,128]{1,0:T(8,128)S(1)}, f32[128,128]{1,0:T(8,128)S(1)}, u32[]{:S(2)}, u32[]{:S(2)}) collective-permute-start(f32[128,128]{1,0:T(8,128)S(1)} %add.14), channel_id=1, source_target_pairs={{0,8},{1,9},{2,10},{3,11},{4,12},{5,13},{6,14},{7,15},{8,0},{9,1},... | collective-permute-start | bytes 196616 | tf_op jit(solution)/shard_map/ppermute | solution.py:358
  19.5 1.5 %collective-permute-start.7 = (f32[128,128]{1,0:T(8,128)S(1)}, f32[128,128]{1,0:T(8,128)S(1)}, u32[]{:S(2)}, u32[]{:S(2)}) collective-permute-start(f32[128,128]{1,0:T(8,128)S(1)} %add.14), channel_id=1, source_target_pairs={{0,16},{1,17},{2,18},{3,19},{4,20},{5,21},{6,22},{7,23},{8,24},{9,... | collective-permute-start | bytes 196616 | tf_op jit(solution)/shard_map/ppermute | solution.py:358
  21.4 0.7 collective-permute-done.6.refs_4_
  22.1 1.6 %collective-permute-done.7.refs_5_ = f32[128,128]{1,0:T(8,128)S(1)} collective-permute-done((f32[128,128]{1,0:T(8,128)S(1)}, f32[128,128]{1,0:T(8,128)S(1)}, u32[]{:S(2)}, u32[]{:S(2)}) %collective-permute-start.7) | collective-permute-done | bytes 65568 | tf_op jit(solution)/shard_map/ppermute | solution.py:358
  23.8 2.4 %collective-permute-done.8.refs_6_ = f32[128,128]{1,0:T(8,128)S(1)} collective-permute-done((f32[128,128]{1,0:T(8,128)S(1)}, f32[128,128]{1,0:T(8,128)S(1)}, u32[]{:S(2)}, u32[]{:S(2)}) %collective-permute-start.8) | collective-permute-done | bytes 65568 | tf_op jit(solution)/shard_map/ppermute | solution.py:358
  26.2 0.9 %copy-done.6 = bf16[384,256]{1,0:T(8,128)(2,1)S(1)} copy-done((bf16[384,256]{1,0:T(8,128)(2,1)S(1)}, bf16[384,256]{1,0:T(8,128)(2,1)}, u32[]{:S(2)}) %copy-start.6) | copy-done | bytes 196632
  27.1 0.8 copy-done.13
  27.9 0.9 copy-done.15
  28.8 0.9 %copy-done.19 = f32[384,128]{1,0:T(8,128)S(1)} copy-done((f32[384,128]{1,0:T(8,128)S(1)}, f32[384,128]{1,0:T(8,128)}, u32[]{:S(2)}) %copy-start.19) | copy-done | bytes 196632
  29.8 1.2 %shard_map.95 = (bf16[4,192,128]{2,1,0:T(8,128)(2,1)S(1)}, f32[128,128]{1,0:T(8,128)S(1)}, f32[128,128]{1,0:T(8,128)S(1)}) custom-call(s32[4]{0:T(128)S(1)} %add_convert_fusion.refs_0_, s32[3]{0:T(128)S(1)} %pad_add_fusion.2.refs_1_.refs_0_, f32[128,128]{1,0:T(8,128)S(1)} %copy-done.13, f32[128,128]{1,0:T(8,128)} %collective-permute-done.5.refs_3_, ...), custom_call_target="tpu_custom_call" | custom-call | flops 1 | bytes 1343488 | tf_op jit(solution)/shard_map/pallas_call | solution.py:94
  31.7 0.7 copy-done.20
  32.3 0.6 copy-done.26
  33.0 0.8 copy-done.3
  34.3 1.0 %collective-permute-start.12 = (bf16[128,2048]{1,0:T(8,128)(2,1)}, bf16[128,2048]{1,0:T(8,128)(2,1)}, u32[]{:S(2)}, u32[]{:S(2)}) collective-permute-start(bf16[128,2048]{1,0:T(8,128)(2,1)} %get-tuple-element.45.refs_6_.refs_5_), channel_id=1, source_target_pairs={{0,16},{1,17},{2,18},{3,19},{4,20},{5,21},{6,22},{7,23},{8,24},{9,... | collective-permute-start | bytes 1572872 | tf_op jit(solution)/shard_map/ppermute | solution.py:358
  35.4 4.6 %all-to-all-start = ((bf16[4,192,128]{2,1,0:T(8,128)(2,1)}), bf16[4,192,128]{2,1,0:T(8,128)(2,1)}, u32[]{:S(2)}, u32[]{:S(2)}) async-start(bf16[4,192,128]{2,1,0:T(8,128)(2,1)} %copy-done.20), calls=%async_computation | async-start | bytes 393216 | tf_op jit(solution)/shard_map/all_to_all | solution.py:426
  40.0 1.1 %copy-done.1 = bf16[96,4096]{1,0:T(8,128)(2,1)S(1)} copy-done((bf16[96,4096]{1,0:T(8,128)(2,1)S(1)}, bf16[96,4096]{1,0:T(8,128)(2,1)}, u32[]{:S(2)}) %copy-start.1) | copy-done | bytes 786456
  41.1 1.0 %copy-done.4 = bf16[128,2048]{1,0:T(8,128)(2,1)S(1)} copy-done((bf16[128,2048]{1,0:T(8,128)(2,1)S(1)}, bf16[128,2048]{1,0:T(8,128)(2,1)}, u32[]{:S(2)}) %copy-start.4) | copy-done | bytes 524312
  42.2 3.3 %shard_map.98 = (bf16[192,128]{1,0:T(8,128)(2,1)}, f32[192,256]{1,0:T(8,128)S(1)}) custom-call(s32[4]{0:T(128)S(1)} %pad_add_fusion.1.refs_0_, bf16[96,4096]{1,0:T(8,128)(2,1)S(1)} %copy-done.1, bf16[96,4096]{1,0:T(8,128)(2,1)S(1)} %collective-permute-done.refs_3_.refs_2_, bf16[256,4096]{1,0:T(8,128)(2,1)S(1)} %copy-done, bf16[128,2048]{1,0:T(8,128)(2,1)S(1)} %copy-done.4, ...), custom_call_target="tpu_custom_call" | custom-call | flops 402653184 | bytes 4964352 | tf_op jit(solution)/shard_map/pallas_call | solution.py:94
  45.5 4.6 %collective-permute-done.9.refs_5_.refs_6_ = bf16[128,2048]{1,0:T(8,128)(2,1)} collective-permute-done((bf16[128,2048]{1,0:T(8,128)(2,1)}, bf16[128,2048]{1,0:T(8,128)(2,1)}, u32[]{:S(2)}, u32[]{:S(2)}) %collective-permute-start.9) | collective-permute-done | bytes 524320 | tf_op jit(solution)/shard_map/ppermute | solution.py:358
  50.1 3.3 %shard_map.99 = (bf16[192,128]{1,0:T(8,128)(2,1)}, bf16[192,128]{1,0:T(8,128)(2,1)}, bf16[128,1024]{1,0:T(8,128)(2,1)}, bf16[128,1024]{1,0:T(8,128)(2,1)}) custom-call(s32[4]{0:T(128)S(1)} %pad_add_fusion.1.refs_0_, bf16[96,4096]{1,0:T(8,128)(2,1)S(1)} %copy-done.1, bf16[96,4096]{1,0:T(8,128)(2,1)S(1)} %collective-permute-done.refs_3_.refs_2_, ...), custom_call_target="tpu_custom_call" | custom-call | flops 201326592 | bytes 3964928 | tf_op jit(solution)/shard_map/pallas_call | solution.py:94
  53.9 0.8 collective-permute-start.14
  54.7 1.1 %collective-permute-start.15 = (bf16[192,128]{1,0:T(8,128)(2,1)}, bf16[192,128]{1,0:T(8,128)(2,1)S(1)}, u32[]{:S(2)}, u32[]{:S(2)}) collective-permute-start(bf16[192,128]{1,0:T(8,128)(2,1)} %get-tuple-element.53), channel_id=1, source_target_pairs={{0,3},{1,0},{2,1},{3,2},{4,7},{5,4},{6,5},{7,6},{8,11},{9,8},{10,9... | collective-permute-start | bytes 147464 | tf_op jit(solution)/shard_map/ppermute | solution.py:358
  55.8 0.9 collective-permute-start.16
  56.7 1.1 %copy-done.2 = bf16[96,4096]{1,0:T(8,128)(2,1)S(1)} copy-done((bf16[96,4096]{1,0:T(8,128)(2,1)S(1)}, bf16[96,4096]{1,0:T(8,128)(2,1)}, u32[]{:S(2)}) %copy-start.2) | copy-done | bytes 786456
  57.9 0.7 copy-done.24
  58.5 3.1 %shard_map.97 = (f32[192,128]{1,0:T(8,128)S(1)}, f32[96,2048]{1,0:T(8,128)S(1)}, f32[96,2048]{1,0:T(8,128)S(1)}) custom-call(s32[4]{0:T(128)S(1)} %copy-done.24, bf16[96,4096]{1,0:T(8,128)(2,1)S(1)} %copy-done.2, bf16[96,4096]{1,0:T(8,128)(2,1)S(1)} %collective-permute-done.refs_3_.refs_2_, bf16[256,4096]{1,0:T(8,128)(2,1)S(1)} %copy-done, ...), custom_call_target="tpu_custom_call" | custom-call | flops 402653184 | bytes 7110656 | tf_op jit(solution)/shard_map/pallas_call | solution.py:94
  62.3 2.0 %shard_map.100 = bf16[192,128]{1,0:T(8,128)(2,1)S(1)} custom-call(s32[4]{0:T(128)S(1)} %copy-done.24, bf16[96,4096]{1,0:T(8,128)(2,1)S(1)} %copy-done.2, bf16[96,4096]{1,0:T(8,128)(2,1)S(1)} %collective-permute-done.refs_3_.refs_2_, bf16[128,1024]{1,0:T(8,128)(2,1)} %collective-permute-done.13.refs_3_.refs_4_, ...), custom_call_target="tpu_custom_call" | custom-call | flops 100663296 | bytes 2244608 | tf_op jit(solution)/shard_map/pallas_call | solution.py:94
  65.0 5.5 %collective-permute-done.17.refs_7_.refs_4_ = bf16[192,128]{1,0:T(8,128)(2,1)S(1)} collective-permute-done((bf16[192,128]{1,0:T(8,128)(2,1)S(1)}, bf16[192,128]{1,0:T(8,128)(2,1)S(1)}, u32[]{:S(2)}, u32[]{:S(2)}) %collective-permute-start.17) | collective-permute-done | bytes 49184 | tf_op jit(solution)/shard_map/ppermute | solution.py:358
  70.5 3.0 %shard_map.101 = (f32[96,2048]{1,0:T(8,128)S(1)}, f32[96,2048]{1,0:T(8,128)S(1)}) custom-call(s32[4]{0:T(128)S(1)} %copy-done.24, bf16[256,4096]{1,0:T(8,128)(2,1)S(1)} %copy-done, bf16[128,2048]{1,0:T(8,128)(2,1)} %collective-permute-done.11.refs_3_.refs_2_, bf16[128,2048]{1,0:T(8,128)(2,1)} %collective-permute-done.12.refs_4_.refs_3_, ...), custom_call_target="tpu_custom_call" | custom-call | flops 402653184 | bytes 5439488 | tf_op jit(solution)/shard_map/pallas_call | solution.py:94
  74.0 1.8 %collective-permute-done.22.refs_8_ = bf16[192,128]{1,0:T(8,128)(2,1)S(1)} collective-permute-done((bf16[192,128]{1,0:T(8,128)(2,1)S(1)}, bf16[192,128]{1,0:T(8,128)(2,1)S(1)}, u32[]{:S(2)}, u32[]{:S(2)}) %collective-permute-start.22) | collective-permute-done | bytes 49184 | tf_op jit(solution)/shard_map/ppermute | solution.py:358
  75.9 1.1 %shard_map.103 = (bf16[384,256]{1,0:T(8,128)(2,1)S(1)}, f32[128,128]{1,0:T(8,128)S(1)}, f32[128,128]{1,0:T(8,128)S(1)}) custom-call(s32[3]{0:T(128)S(1)} %copy-done.22, bf16[384,256]{1,0:T(8,128)(2,1)S(1)} %copy-done.7, bf16[192,128]{1,0:T(8,128)(2,1)} %get-tuple-element.55.refs_2_, bf16[192,128]{1,0:T(8,128)(2,1)S(1)} %collective-permute-done.15.refs_6_.refs_3_, ...), custom_call_target="tpu_custom_call" | custom-call | flops 1 | bytes 917504 | tf_op jit(solution)/shard_map/pallas_call | solution.py:94
  77.5 0.7 collective-permute-done.24.refs_2_
  78.3 1.0 %collective-permute-start.25 = (f32[128,128]{1,0:T(8,128)S(1)}, f32[128,128]{1,0:T(8,128)S(1)}, u32[]{:S(2)}, u32[]{:S(2)}) collective-permute-start(f32[128,128]{1,0:T(8,128)S(1)} %add.15.refs_8_), channel_id=1, source_target_pairs={{0,8},{1,9},{2,10},{3,11},{4,12},{5,13},{6,14},{7,15},{8,0},{9,1},... | collective-permute-start | bytes 196616 | tf_op jit(solution)/shard_map/ppermute | solution.py:358
  79.3 1.3 %collective-permute-start.26 = (f32[128,128]{1,0:T(8,128)S(1)}, f32[128,128]{1,0:T(8,128)S(1)}, u32[]{:S(2)}, u32[]{:S(2)}) collective-permute-start(f32[128,128]{1,0:T(8,128)S(1)} %add.15.refs_8_), channel_id=1, source_target_pairs={{0,16},{1,17},{2,18},{3,19},{4,20},{5,21},{6,22},{7,23},{8,24},{9,... | collective-permute-start | bytes 196616 | tf_op jit(solution)/shard_map/ppermute | solution.py:358
  80.6 1.3 %collective-permute-start.27 = (f32[128,128]{1,0:T(8,128)S(1)}, f32[128,128]{1,0:T(8,128)S(1)}, u32[]{:S(2)}, u32[]{:S(2)}) collective-permute-start(f32[128,128]{1,0:T(8,128)S(1)} %add.15.refs_8_), channel_id=1, source_target_pairs={{0,24},{1,25},{2,26},{3,27},{4,28},{5,29},{6,30},{7,31},{8,16},{9,... | collective-permute-start | bytes 196616 | tf_op jit(solution)/shard_map/ppermute | solution.py:358
  81.9 3.2 %shard_map.104 = (bf16[384,256]{1,0:T(8,128)(2,1)}, f32[384,256]{1,0:T(8,128)S(1)}, f32[384,256]{1,0:T(8,128)S(1)}) custom-call(s32[3]{0:T(128)S(1)} %copy-done.22, bf16[384,256]{1,0:T(8,128)(2,1)S(1)} %copy-done.7, bf16[384,256]{1,0:T(8,128)(2,1)S(1)} %copy-done.9, bf16[384,256]{1,0:T(8,128)(2,1)S(1)} %copy-done.8, ...), custom_call_target="tpu_custom_call" | custom-call | flops 528482304 | bytes 3080192 | tf_op jit(solution)/shard_map/pallas_call | solution.py:94
  86.5 1.6 %shard_map.102 = (bf16[96,4096]{1,0:T(8,128)(2,1)}, f32[8,128]{1,0:T(8,128)S(1)}) custom-call(s32[2]{0:T(128)S(1)} %pad_add_fusion.refs_0_, f32[96,2048]{1,0:T(8,128)S(1)} %get-tuple-element.47.refs_1_, f32[96,2048]{1,0:T(8,128)S(1)} %collective-permute-done.10.refs_2_, f32[96,2048]{1,0:T(8,128)S(1)} %get-tuple-element.56.refs_3_, ...), custom_call_target="tpu_custom_call" | custom-call | flops 1 | bytes 3936256 | tf_op jit(solution)/shard_map/pallas_call | solution.py:94
  88.0 1.6 %shard_map.106 = (bf16[384,256]{1,0:T(8,128)(2,1)}, bf16[384,256]{1,0:T(8,128)(2,1)}) custom-call(s32[3]{0:T(128)S(1)} %copy-done.22, bf16[384,256]{1,0:T(8,128)(2,1)S(1)} %copy-done.9, bf16[384,256]{1,0:T(8,128)(2,1)S(1)} %copy-done.8, f32[384,256]{1,0:T(8,128)S(1)} %get-tuple-element.65.refs_6_.refs_3_, f32[384,256]{1,0:T(8,128)S(1)} %get-tuple-element.66.refs_4_, ...), custom_call_target="tpu_custom_call" | custom-call | flops 1 | bytes 1703936 | tf_op jit(solution)/shard_map/pallas_call | solution.py:94
  (91 shorter events, 8.1 us)
Async XLA Ops:
  0.6 8.3 %copy-start.25 = (s32[3,3]{1,0:T(4,128)S(1)}, s32[3,3]{1,0:T(4,128)}, u32[]{:S(2)}) copy-start(s32[3,3]{1,0:T(4,128)} %refs_0_.1) | copy-start | bytes 112
  0.6 8.3 %collective-permute-start = (bf16[96,4096]{1,0:T(8,128)(2,1)}, bf16[96,4096]{1,0:T(8,128)(2,1)S(1)}, u32[]{:S(2)}, u32[]{:S(2)}) collective-permute-start(bf16[96,4096]{1,0:T(8,128)(2,1)} %refs_1_.11), channel_id=1, source_target_pairs={{0,4},{1,5},{2,6},{3,7},{4,0},{5,1},{6,2},{7,3},{8,12},{9,13},{10,... | collective-permute-start | bytes 2359304 | tf_op jit(solution)/shard_map/ppermute | solution.py:358
  3.0 29.9 %collective-permute-start.1 = (bf16[128,2048]{1,0:T(8,128)(2,1)}, bf16[128,2048]{1,0:T(8,128)(2,1)S(1)}, u32[]{:S(2)}, u32[]{:S(2)}) collective-permute-start(bf16[128,2048]{1,0:T(8,128)(2,1)} %dynamic_slice.3), channel_id=1, source_target_pairs={{0,1},{1,2},{2,3},{3,0},{4,5},{5,6},{6,7},{7,4},{8,9},{9,10},{10,1... | collective-permute-start | bytes 1572872 | tf_op jit(solution)/shard_map/ppermute | solution.py:358
  5.7 27.3 %collective-permute-start.2 = (bf16[128,2048]{1,0:T(8,128)(2,1)}, bf16[128,2048]{1,0:T(8,128)(2,1)}, u32[]{:S(2)}, u32[]{:S(2)}) collective-permute-start(bf16[128,2048]{1,0:T(8,128)(2,1)} %dynamic_slice.3), channel_id=1, source_target_pairs={{0,3},{1,0},{2,1},{3,2},{4,7},{5,4},{6,5},{7,6},{8,11},{9,8},{10,9... | collective-permute-start | bytes 1572872 | tf_op jit(solution)/shard_map/ppermute | solution.py:358
  7.8 23.3 %copy-start.21 = (s32[3]{0:T(128)}, s32[3]{0:T(128)S(1)}, u32[]{:S(2)}) copy-start(s32[3]{0:T(128)S(1)} %pad_add_fusion.2.refs_1_.refs_0_) | copy-start | bytes 40
  8.9 31.1 %copy-start = (bf16[256,4096]{1,0:T(8,128)(2,1)S(1)}, bf16[256,4096]{1,0:T(8,128)(2,1)}, u32[]{:S(2)}) copy-start(bf16[256,4096]{1,0:T(8,128)(2,1)} %refs_1_.12) | copy-start | bytes 6291460
  12.1 1.1 %copy-start.10 = (bf16[4,384,384]{2,1,0:T(8,128)(2,1)}, bf16[4,384,384]{2,1,0:T(8,128)(2,1)S(1)}, u32[]{:S(2)}) copy-start(bf16[4,384,384]{2,1,0:T(8,128)(2,1)S(1)} %get-tuple-element.60.refs_5_) | copy-start | bytes 3538948
  14.4 1.8 %collective-permute-start.4 = (f32[384,128]{1,0:T(8,128)}, f32[384,128]{1,0:T(8,128)}, u32[]{:S(2)}, u32[]{:S(2)}) collective-permute-start(f32[384,128]{1,0:T(8,128)} %get-tuple-element.40), channel_id=1, source_target_pairs={{0,4},{1,5},{2,6},{3,7},{4,0},{5,1},{6,2},{7,3},{8,12},{9,13},{10,... | collective-permute-start | bytes 589832 | tf_op jit(solution)/shard_map/ppermute | solution.py:358
  14.6 1.6 %collective-permute-start.3 = (bf16[384,128]{1,0:T(8,128)(2,1)}, bf16[384,128]{1,0:T(8,128)(2,1)S(1)}, u32[]{:S(2)}, u32[]{:S(2)}) collective-permute-start(bf16[384,128]{1,0:T(8,128)(2,1)} %get-tuple-element.39), channel_id=1, source_target_pairs={{0,4},{1,5},{2,6},{3,7},{4,0},{5,1},{6,2},{7,3},{8,12},{9,13},{10,... | collective-permute-start | bytes 294920 | tf_op jit(solution)/shard_map/ppermute | solution.py:358
  14.9 1.9 %collective-permute-start.5 = (f32[128,128]{1,0:T(8,128)}, f32[128,128]{1,0:T(8,128)}, u32[]{:S(2)}, u32[]{:S(2)}) collective-permute-start(f32[128,128]{1,0:T(8,128)} %get-tuple-element.41), channel_id=1, source_target_pairs={{0,4},{1,5},{2,6},{3,7},{4,0},{5,1},{6,2},{7,3},{8,12},{9,13},{10,... | collective-permute-start | bytes 196616 | tf_op jit(solution)/shard_map/ppermute | solution.py:358
  17.8 4.4 %collective-permute-start.6 = (f32[128,128]{1,0:T(8,128)S(1)}, f32[128,128]{1,0:T(8,128)S(1)}, u32[]{:S(2)}, u32[]{:S(2)}) collective-permute-start(f32[128,128]{1,0:T(8,128)S(1)} %add.14), channel_id=1, source_target_pairs={{0,8},{1,9},{2,10},{3,11},{4,12},{5,13},{6,14},{7,15},{8,0},{9,1},... | collective-permute-start | bytes 196616 | tf_op jit(solution)/shard_map/ppermute | solution.py:358
  19.5 4.3 %collective-permute-start.7 = (f32[128,128]{1,0:T(8,128)S(1)}, f32[128,128]{1,0:T(8,128)S(1)}, u32[]{:S(2)}, u32[]{:S(2)}) collective-permute-start(f32[128,128]{1,0:T(8,128)S(1)} %add.14), channel_id=1, source_target_pairs={{0,16},{1,17},{2,18},{3,19},{4,20},{5,21},{6,22},{7,23},{8,24},{9,... | collective-permute-start | bytes 196616 | tf_op jit(solution)/shard_map/ppermute | solution.py:358
  21.0 5.2 %collective-permute-start.8 = (f32[128,128]{1,0:T(8,128)S(1)}, f32[128,128]{1,0:T(8,128)S(1)}, u32[]{:S(2)}, u32[]{:S(2)}) collective-permute-start(f32[128,128]{1,0:T(8,128)S(1)} %add.14), channel_id=1, source_target_pairs={{0,24},{1,25},{2,26},{3,27},{4,28},{5,29},{6,30},{7,31},{8,16},{9,... | collective-permute-start | bytes 196616 | tf_op jit(solution)/shard_map/ppermute | solution.py:358
  26.2 0.9 %copy-start.6 = (bf16[384,256]{1,0:T(8,128)(2,1)S(1)}, bf16[384,256]{1,0:T(8,128)(2,1)}, u32[]{:S(2)}) copy-start(bf16[384,256]{1,0:T(8,128)(2,1)} %refs_1_.14) | copy-start | bytes 589828
  28.8 0.9 %copy-start.19 = (f32[384,128]{1,0:T(8,128)S(1)}, f32[384,128]{1,0:T(8,128)}, u32[]{:S(2)}) copy-start(f32[384,128]{1,0:T(8,128)} %copy-done.18) | copy-start | bytes 589828
  33.8 16.3 %collective-permute-start.9 = (bf16[128,2048]{1,0:T(8,128)(2,1)}, bf16[128,2048]{1,0:T(8,128)(2,1)}, u32[]{:S(2)}, u32[]{:S(2)}) collective-permute-start(bf16[128,2048]{1,0:T(8,128)(2,1)} %get-tuple-element.44.refs_4_), channel_id=1, source_target_pairs={{0,1},{1,2},{2,3},{3,0},{4,5},{5,6},{6,7},{7,4},{8,9},{9,10},{10,1... | collective-permute-start | bytes 1572872 | tf_op jit(solution)/shard_map/ppermute | solution.py:358
  33.8 16.3 %collective-permute-start.11 = (bf16[128,2048]{1,0:T(8,128)(2,1)}, bf16[128,2048]{1,0:T(8,128)(2,1)}, u32[]{:S(2)}, u32[]{:S(2)}) collective-permute-start(bf16[128,2048]{1,0:T(8,128)(2,1)} %get-tuple-element.44.refs_4_), channel_id=1, source_target_pairs={{0,8},{1,9},{2,10},{3,11},{4,12},{5,13},{6,14},{7,15},{8,0},{9,1},... | collective-permute-start | bytes 1572872 | tf_op jit(solution)/shard_map/ppermute | solution.py:358
  34.3 15.7 %collective-permute-start.12 = (bf16[128,2048]{1,0:T(8,128)(2,1)}, bf16[128,2048]{1,0:T(8,128)(2,1)}, u32[]{:S(2)}, u32[]{:S(2)}) collective-permute-start(bf16[128,2048]{1,0:T(8,128)(2,1)} %get-tuple-element.45.refs_6_.refs_5_), channel_id=1, source_target_pairs={{0,16},{1,17},{2,18},{3,19},{4,20},{5,21},{6,22},{7,23},{8,24},{9,... | collective-permute-start | bytes 1572872 | tf_op jit(solution)/shard_map/ppermute | solution.py:358
  35.4 21.4 %all-to-all-start = ((bf16[4,192,128]{2,1,0:T(8,128)(2,1)}), bf16[4,192,128]{2,1,0:T(8,128)(2,1)}, u32[]{:S(2)}, u32[]{:S(2)}) async-start(bf16[4,192,128]{2,1,0:T(8,128)(2,1)} %copy-done.20), calls=%async_computation | async-start | bytes 393216 | tf_op jit(solution)/shard_map/all_to_all | solution.py:426
  40.0 1.1 %copy-start.1 = (bf16[96,4096]{1,0:T(8,128)(2,1)S(1)}, bf16[96,4096]{1,0:T(8,128)(2,1)}, u32[]{:S(2)}) copy-start(bf16[96,4096]{1,0:T(8,128)(2,1)} %refs_1_.11) | copy-start | bytes 2359300
  41.1 1.0 %copy-start.4 = (bf16[128,2048]{1,0:T(8,128)(2,1)S(1)}, bf16[128,2048]{1,0:T(8,128)(2,1)}, u32[]{:S(2)}) copy-start(bf16[128,2048]{1,0:T(8,128)(2,1)} %get-tuple-element.44.refs_4_) | copy-start | bytes 1572868
  42.2 7.9 %copy-start.23 = (s32[4]{0:T(128)}, s32[4]{0:T(128)S(1)}, u32[]{:S(2)}) copy-start(s32[4]{0:T(128)S(1)} %pad_add_fusion.1.refs_0_) | copy-start | bytes 52
  45.5 11.3 %copy-start.5 = (bf16[128,2048]{1,0:T(8,128)(2,1)S(1)}, bf16[128,2048]{1,0:T(8,128)(2,1)}, u32[]{:S(2)}) copy-start(bf16[128,2048]{1,0:T(8,128)(2,1)} %get-tuple-element.44.refs_4_) | copy-start | bytes 1572868
  53.3 9.0 %collective-permute-start.13 = (bf16[128,1024]{1,0:T(8,128)(2,1)}, bf16[128,1024]{1,0:T(8,128)(2,1)}, u32[]{:S(2)}, u32[]{:S(2)}) collective-permute-start(bf16[128,1024]{1,0:T(8,128)(2,1)} %get-tuple-element.50), channel_id=1, source_target_pairs={{0,8},{1,9},{2,10},{3,11},{4,12},{5,13},{6,14},{7,15},{8,0},{9,1},... | collective-permute-start | bytes 786440 | tf_op jit(solution)/shard_map/ppermute | solution.py:358
  53.9 8.4 %collective-permute-start.14 = (bf16[128,1024]{1,0:T(8,128)(2,1)}, bf16[128,1024]{1,0:T(8,128)(2,1)}, u32[]{:S(2)}, u32[]{:S(2)}) collective-permute-start(bf16[128,1024]{1,0:T(8,128)(2,1)} %get-tuple-element.51), channel_id=1, source_target_pairs={{0,16},{1,17},{2,18},{3,19},{4,20},{5,21},{6,22},{7,23},{8,24},{9,... | collective-permute-start | bytes 786440 | tf_op jit(solution)/shard_map/ppermute | solution.py:358
  54.7 7.0 %collective-permute-start.15 = (bf16[192,128]{1,0:T(8,128)(2,1)}, bf16[192,128]{1,0:T(8,128)(2,1)S(1)}, u32[]{:S(2)}, u32[]{:S(2)}) collective-permute-start(bf16[192,128]{1,0:T(8,128)(2,1)} %get-tuple-element.53), channel_id=1, source_target_pairs={{0,3},{1,0},{2,1},{3,2},{4,7},{5,4},{6,5},{7,6},{8,11},{9,8},{10,9... | collective-permute-start | bytes 147464 | tf_op jit(solution)/shard_map/ppermute | solution.py:358
  55.8 6.4 %collective-permute-start.16 = (bf16[192,128]{1,0:T(8,128)(2,1)}, bf16[192,128]{1,0:T(8,128)(2,1)S(1)}, u32[]{:S(2)}, u32[]{:S(2)}) collective-permute-start(bf16[192,128]{1,0:T(8,128)(2,1)} %get-tuple-element.54), channel_id=1, source_target_pairs={{0,1},{1,2},{2,3},{3,0},{4,5},{5,6},{6,7},{7,4},{8,9},{9,10},{10,1... | collective-permute-start | bytes 147464 | tf_op jit(solution)/shard_map/ppermute | solution.py:358
  56.7 8.3 %collective-permute-start.18 = (bf16[192,128]{1,0:T(8,128)(2,1)}, bf16[192,128]{1,0:T(8,128)(2,1)S(1)}, u32[]{:S(2)}, u32[]{:S(2)}) collective-permute-start(bf16[192,128]{1,0:T(8,128)(2,1)} %get-tuple-element.55.refs_2_), channel_id=1, source_target_pairs={{0,4},{1,5},{2,6},{3,7},{4,0},{5,1},{6,2},{7,3},{8,12},{9,13},{10,... | collective-permute-start | bytes 147464 | tf_op jit(solution)/shard_map/ppermute | solution.py:358
  56.7 1.1 %copy-start.2 = (bf16[96,4096]{1,0:T(8,128)(2,1)S(1)}, bf16[96,4096]{1,0:T(8,128)(2,1)}, u32[]{:S(2)}) copy-start(bf16[96,4096]{1,0:T(8,128)(2,1)} %refs_1_.11) | copy-start | bytes 2359300
  61.7 3.4 %collective-permute-start.19 = (bf16[192,128]{1,0:T(8,128)(2,1)S(1)}, bf16[192,128]{1,0:T(8,128)(2,1)S(1)}, u32[]{:S(2)}, u32[]{:S(2)}) collective-permute-start(bf16[192,128]{1,0:T(8,128)(2,1)S(1)} %collective-permute-done.15.refs_6_.refs_3_), channel_id=1, source_target_pairs={{0,4},{1,5},{2,6},{3,7},{4,0},{5,1},{6,2},{7,3},{8,12},{9,13},{10,... | collective-permute-start | bytes 147464 | tf_op jit(solution)/shard_map/ppermute | solution.py:358
  62.2 2.8 %collective-permute-start.20 = (bf16[192,128]{1,0:T(8,128)(2,1)S(1)}, bf16[192,128]{1,0:T(8,128)(2,1)S(1)}, u32[]{:S(2)}, u32[]{:S(2)}) collective-permute-start(bf16[192,128]{1,0:T(8,128)(2,1)S(1)} %collective-permute-done.16.refs_7_.refs_5_), channel_id=1, source_target_pairs={{0,4},{1,5},{2,6},{3,7},{4,0},{5,1},{6,2},{7,3},{8,12},{9,13},{10,... | collective-permute-start | bytes 147464 | tf_op jit(solution)/shard_map/ppermute | solution.py:358
  64.4 11.5 %copy-start.7 = (bf16[384,256]{1,0:T(8,128)(2,1)S(1)}, bf16[384,256]{1,0:T(8,128)(2,1)}, u32[]{:S(2)}) copy-start(bf16[384,256]{1,0:T(8,128)(2,1)} %refs_1_.14) | copy-start | bytes 589828
  64.4 11.5 %copy-start.22 = (s32[3]{0:T(128)S(1)}, s32[3]{0:T(128)}, u32[]{:S(2)}) copy-start(s32[3]{0:T(128)} %copy-done.21) | copy-start | bytes 40
  64.4 6.1 %collective-permute-start.17 = (bf16[192,128]{1,0:T(8,128)(2,1)S(1)}, bf16[192,128]{1,0:T(8,128)(2,1)S(1)}, u32[]{:S(2)}, u32[]{:S(2)}) collective-permute-start(bf16[192,128]{1,0:T(8,128)(2,1)S(1)} %shard_map.100), channel_id=1, source_target_pairs={{0,2},{1,3},{2,0},{3,1},{4,6},{5,7},{6,4},{7,5},{8,10},{9,11},{10,... | collective-permute-start | bytes 147464 | tf_op jit(solution)/shard_map/ppermute | solution.py:358
  64.6 12.6 %copy-start.27 = (f32[128,128]{1,0:T(8,128)S(1)}, f32[128,128]{1,0:T(8,128)}, u32[]{:S(2)}) copy-start(f32[128,128]{1,0:T(8,128)} %copy-done.26) | copy-start | bytes 196612
  64.6 17.3 %copy-start.8 = (bf16[384,256]{1,0:T(8,128)(2,1)S(1)}, bf16[384,256]{1,0:T(8,128)(2,1)}, u32[]{:S(2)}) copy-start(bf16[384,256]{1,0:T(8,128)(2,1)} %refs_2_.3) | copy-start | bytes 589828
  64.6 17.3 %copy-start.9 = (bf16[384,256]{1,0:T(8,128)(2,1)S(1)}, bf16[384,256]{1,0:T(8,128)(2,1)}, u32[]{:S(2)}) copy-start(bf16[384,256]{1,0:T(8,128)(2,1)} %refs_1_.15) | copy-start | bytes 589828
  64.6 17.3 %copy-start.11 = (bf16[4,384,384]{2,1,0:T(8,128)(2,1)S(1)}, bf16[4,384,384]{2,1,0:T(8,128)(2,1)}, u32[]{:S(2)}) copy-start(bf16[4,384,384]{2,1,0:T(8,128)(2,1)} %copy-done.10) | copy-start | bytes 3538948
  64.6 17.3 %copy-start.17 = (f32[128,128]{1,0:T(8,128)S(1)}, f32[128,128]{1,0:T(8,128)}, u32[]{:S(2)}) copy-start(f32[128,128]{1,0:T(8,128)} %copy-done.16) | copy-start | bytes 196612
  64.6 21.9 %collective-permute-start.10 = (f32[96,2048]{1,0:T(8,128)S(1)}, f32[96,2048]{1,0:T(8,128)S(1)}, u32[]{:S(2)}, u32[]{:S(2)}) collective-permute-start(f32[96,2048]{1,0:T(8,128)S(1)} %get-tuple-element.48), channel_id=1, source_target_pairs={{0,4},{1,5},{2,6},{3,7},{4,0},{5,1},{6,2},{7,3},{8,12},{9,13},{10,... | collective-permute-start | bytes 2359304 | tf_op jit(solution)/shard_map/ppermute | solution.py:358
  73.5 13.0 %collective-permute-start.21 = (f32[96,2048]{1,0:T(8,128)S(1)}, f32[96,2048]{1,0:T(8,128)S(1)}, u32[]{:S(2)}, u32[]{:S(2)}) collective-permute-start(f32[96,2048]{1,0:T(8,128)S(1)} %get-tuple-element.57), channel_id=1, source_target_pairs={{0,4},{1,5},{2,6},{3,7},{4,0},{5,1},{6,2},{7,3},{8,12},{9,13},{10,... | collective-permute-start | bytes 2359304 | tf_op jit(solution)/shard_map/ppermute | solution.py:358
  73.5 2.3 %collective-permute-start.22 = (bf16[192,128]{1,0:T(8,128)(2,1)S(1)}, bf16[192,128]{1,0:T(8,128)(2,1)S(1)}, u32[]{:S(2)}, u32[]{:S(2)}) collective-permute-start(bf16[192,128]{1,0:T(8,128)(2,1)S(1)} %collective-permute-done.17.refs_7_.refs_4_), channel_id=1, source_target_pairs={{0,4},{1,5},{2,6},{3,7},{4,0},{5,1},{6,2},{7,3},{8,12},{9,13},{10,... | collective-permute-start | bytes 147464 | tf_op jit(solution)/shard_map/ppermute | solution.py:358
  77.0 1.3 %collective-permute-start.24 = (f32[128,128]{1,0:T(8,128)S(1)}, f32[128,128]{1,0:T(8,128)S(1)}, u32[]{:S(2)}, u32[]{:S(2)}) collective-permute-start(f32[128,128]{1,0:T(8,128)S(1)} %get-tuple-element.63), channel_id=1, source_target_pairs={{0,4},{1,5},{2,6},{3,7},{4,0},{5,1},{6,2},{7,3},{8,12},{9,13},{10,... | collective-permute-start | bytes 196616 | tf_op jit(solution)/shard_map/ppermute | solution.py:358
  77.2 3.4 %collective-permute-start.23 = (f32[128,128]{1,0:T(8,128)S(1)}, f32[128,128]{1,0:T(8,128)S(1)}, u32[]{:S(2)}, u32[]{:S(2)}) collective-permute-start(f32[128,128]{1,0:T(8,128)S(1)} %copy-done.27), channel_id=1, source_target_pairs={{0,4},{1,5},{2,6},{3,7},{4,0},{5,1},{6,2},{7,3},{8,12},{9,13},{10,... | collective-permute-start | bytes 196616 | tf_op jit(solution)/shard_map/ppermute | solution.py:358
  78.3 6.8 %collective-permute-start.25 = (f32[128,128]{1,0:T(8,128)S(1)}, f32[128,128]{1,0:T(8,128)S(1)}, u32[]{:S(2)}, u32[]{:S(2)}) collective-permute-start(f32[128,128]{1,0:T(8,128)S(1)} %add.15.refs_8_), channel_id=1, source_target_pairs={{0,8},{1,9},{2,10},{3,11},{4,12},{5,13},{6,14},{7,15},{8,0},{9,1},... | collective-permute-start | bytes 196616 | tf_op jit(solution)/shard_map/ppermute | solution.py:358
  79.3 5.8 %collective-permute-start.26 = (f32[128,128]{1,0:T(8,128)S(1)}, f32[128,128]{1,0:T(8,128)S(1)}, u32[]{:S(2)}, u32[]{:S(2)}) collective-permute-start(f32[128,128]{1,0:T(8,128)S(1)} %add.15.refs_8_), channel_id=1, source_target_pairs={{0,16},{1,17},{2,18},{3,19},{4,20},{5,21},{6,22},{7,23},{8,24},{9,... | collective-permute-start | bytes 196616 | tf_op jit(solution)/shard_map/ppermute | solution.py:358
  80.6 5.2 %collective-permute-start.27 = (f32[128,128]{1,0:T(8,128)S(1)}, f32[128,128]{1,0:T(8,128)S(1)}, u32[]{:S(2)}, u32[]{:S(2)}) collective-permute-start(f32[128,128]{1,0:T(8,128)S(1)} %add.15.refs_8_), channel_id=1, source_target_pairs={{0,24},{1,25},{2,26},{3,27},{4,28},{5,29},{6,30},{7,31},{8,16},{9,... | collective-permute-start | bytes 196616 | tf_op jit(solution)/shard_map/ppermute | solution.py:358
  86.3 1.7 %collective-permute-start.28 = (f32[128,128]{1,0:T(8,128)S(1)}, f32[128,128]{1,0:T(8,128)S(1)}, u32[]{:S(2)}, u32[]{:S(2)}) collective-permute-start(f32[128,128]{1,0:T(8,128)S(1)} %get-tuple-element.68), channel_id=1, source_target_pairs={{0,4},{1,5},{2,6},{3,7},{4,0},{5,1},{6,2},{7,3},{8,12},{9,13},{10,... | collective-permute-start | bytes 196616 | tf_op jit(solution)/shard_map/ppermute | solution.py:358
  (10 other events, 7.1 us)

commit v15 on v14

--- a/solution.py
+++ b/solution.py
@@ -145,28 +145,29 @@
     blk = rows // count
     inv_root = 1.0 / math.sqrt(DH)
     triangle = lower_triangle(blk)
-    for i in range(count):
-        here = slice(i * blk, (i + 1) * blk)
-        upto = slice(0, (i + 1) * blk)
-        sums = []
-        for h in range(2):
-            cols = slice(h * DH, (h + 1) * DH)
-            raw = dot(q_ref[here, cols], k_ref[upto, cols], NT)
-            scores, inner = [], []
+    sums = []
+    for h in range(2):
+        raw = dot(q_ref[:, heads[h]], k_ref[:, heads[h]], NT)
+        probs, inner = [], []
+        for i in range(count):
+            own = raw[i * blk : (i + 1) * blk]
+            scores, linear = [], []
             for j in range(i + 1):
-                part = raw[:, j * blk : (j + 1) * blk]
+                part = own[:, j * blk : (j + 1) * blk]
                 keep = triangle if j == i else mask[i, j] > 0
                 scores.append(jnp.where(keep, part * inv_root, -1e30))
-                inner.append(jnp.where(triangle, part, 0.0) if j == i else part)
+                linear.append(jnp.where(triangle, part, 0.0) if j == i else part)
+            empty = [jnp.zeros((blk, blk), F32)] * (count - 1 - i)
             scores = jnp.concatenate(scores, 1)
-            inner = jnp.concatenate(inner, 1).astype(BF16)
             expo = jnp.exp(scores - jnp.max(scores, -1, keepdims=True))
-            probs = (expo / jnp.sum(expo, -1, keepdims=True)).astype(BF16)
-            store_ref[h, here, upto] = probs
-            store_ref[2 + h, here, upto] = inner
-            both = dot(jnp.concatenate([probs, inner], 0), v_ref[upto, cols], NN)
-            sums.append(both[:blk] + scale * both[blk:])
-        mine_ref[here], other_ref[here] = pick(where[2], sums)
+            share = expo / jnp.sum(expo, -1, keepdims=True)
+            probs.append(jnp.concatenate([share, *empty], 1).astype(BF16))
+            inner.append(jnp.concatenate([*linear, *empty], 1).astype(BF16))
+        stacked = jnp.concatenate(probs + inner, 0)
+        store_ref[h], store_ref[2 + h] = stacked[:rows], stacked[rows:]
+        both = dot(stacked, v_ref[:, heads[h]], NN)
+        sums.append(both[:rows] + scale * both[rows:])
+    mine_ref[...], other_ref[...] = pick(where[2], sums)
     far_ref[...] = q_ref[:, pl.ds(pl.multiple_of((1 - where[2]) * DH, DH), DH)]
 
 
@@ -289,54 +290,27 @@
 
 
 def backward_kernel(
-    scale,
-    count,
-    where,
-    q_ref,
-    k_ref,
-    v_ref,
-    g_ref,
-    store_ref,
-    mine_ref,
-    other_ref,
-    dq_ref,
-    dk_ref,
-    dv_ref,
+    scale, where, q_ref, k_ref, v_ref, g_ref, store_ref, mine_ref, other_ref, dq_ref, dk_ref, dv_ref
 ):
     rows, width = q_ref.shape
-    blk = rows // count
     inv_root = 1.0 / math.sqrt(DH)
-    triangle = lower_triangle(blk)
+    triangle = lower_triangle(rows)
     states = both_heads(where[2], mine_ref, other_ref)
     for h in range(width // DH):
         cols = slice(h * DH, (h + 1) * DH)
-        for i in reversed(range(count)):
-            here = slice(i * blk, (i + 1) * blk)
-            upto = slice(0, (i + 1) * blk)
-            q, g = q_ref[here, cols], g_ref[here, cols]
-            k = k_ref[upto, cols]
-            probs, v = store_ref[h, here, upto], v_ref[upto, cols]
-            dprod = dot(g, v, NT)
-            delta = jnp.sum(g.astype(F32) * dot(probs, v, NN), -1, keepdims=True)
-            dscore = (probs.astype(F32) * (dprod - delta) * inv_root).astype(BF16)
-            last = jnp.where(triangle, dprod[:, i * blk :], 0.0)
-            dinner = jnp.concatenate([dprod[:, : i * blk], last], 1) if i else last
-            dinner = dinner.astype(BF16)
-            far = slice(upto.stop, 2 * upto.stop)
-            inner = store_ref[2 + h, here, upto]
-            left = dot(jnp.concatenate([dscore, dinner], 0), k, NN)
-            linear = left[blk:] + dot_wide(g, states[h], NT)
-            dq_ref[here, cols] = (left[:blk] + scale * linear).astype(BF16)
-            dk = dot(jnp.concatenate([dscore, dinner], 1), q, TN)
-            dk = dk[upto] + scale * dk[far]
-            dv = dot(jnp.concatenate([probs, inner], 1), g, TN)
-            dv = dv[upto] + scale * dv[far]
-            if i == count - 1:
-                dk_ref[upto, cols] = dk
-                dv_ref[upto, cols] = dv
-            else:
-                dk_ref[upto, cols] += dk
-                dv_ref[upto, cols] += dv
+        q, k, v, g = q_ref[:, cols], k_ref[:, cols], v_ref[:, cols], g_ref[:, cols]
+        probs, inner = store_ref[h], store_ref[2 + h]
+        dprod = dot(g, v, NT)
+        delta = jnp.sum(g.astype(F32) * dot(probs, v, NN), -1, keepdims=True)
+        dscore = (probs.astype(F32) * (dprod - delta) * inv_root).astype(BF16)
+        dinner = jnp.where(triangle, dprod, 0.0).astype(BF16)
+        left = dot(jnp.concatenate([dscore, dinner], 0), k, NN)
+        linear = left[rows:] + dot_wide(g, states[h], NT)
+        dq_ref[:, cols] = (left[:rows] + scale * linear).astype(BF16)
+        dk = dot(jnp.concatenate([dscore, dinner], 1), q, TN)
+        dk_ref[:, cols] = dk[:rows] + scale * dk[rows:]
+        dv = dot(jnp.concatenate([probs, inner], 1), g, TN)
+        dv_ref[:, cols] = dv[:rows] + scale * dv[rows:]
 
 
 def close_kernel(where, k_ref, v_ref, dk_ref, dv_ref, mine_ref, other_ref, gk_ref, gv_ref):
@@ -384,7 +358,6 @@
     model = out_weight.shape[1]
     own = rows // count
     scale = 1.0 / math.sqrt(DH * rows * shards)
-    blocks = block_mask.shape[0]
     ctx, place = lax.axis_index("ctx"), lax.axis_index("head")
     core, chip, chips = ctx & 1, ctx >> 1, shards // 2
     where = jnp.stack([place, ctx, core])
@@ -441,7 +414,7 @@
     )
     flags, parts, total = exchange(mine, other, core, chip, chips, True)
     grad_query, dk, dv = call(
-        functools.partial(backward_kernel, scale, blocks),
+        functools.partial(backward_kernel, scale),
         [(flat, BF16)] + [(flat, F32)] * 2,
         [query, key, value, g, store, *linear],
         [where],

time: 90.6 us -> 90 us (level)
    ppermute x29, starting transfers between devices: 20.4 us -> 21.5 us  [send(): return lax.ppermute(x, ('ctx', 'head'), pairs)]
where the time goes in v15:
time: 90 us; the launch traced here: 89.1 us
  Pallas kernels  26.3 us (29%)
  starting transfers between devices  25.5 us (28%)
  waiting for transfers between devices  18.8 us (21%)
  local copies, waits for them, and re-layouts  15.2 us (17%)
  other arithmetic  2.45 us (3%)
  between operations  0.92 us (1%)
    pallas_call x12, Pallas kernels, call(): pl.pallas_call(kernel, out_shape=[jax.ShapeDtypeStruct(s, t) for s, t in...  26.3 us
    ppermute x29, starting transfers between devices, send(): return lax.ppermute(x, ('ctx', 'head'), pairs)  21.5 us
    ppermute x29, waiting for transfers between devices, send(): return lax.ppermute(x, ('ctx', 'head'), pairs)  18.8 us
    unnamed x56, local copies, waits for them, and re-layouts  13.3 us
    all_to_all x1, starting transfers between devices, on_device(): attn = lax.all_to_all(attn, 'head', 0, 0, tiled=True)  4.01 us
    dynamic_slice x1, local copies, waits for them, and re-layouts, on_device(): lax.dynamic_slice(out_weight, (core * DH, colour * wide), (DH, wide))  1.88 us
  transfers between devices with their start and end apart: 30, of which 9 were waited for; matrix products, arithmetic and copies ran while one was open for 5% of the time, Pallas kernels for 28%

profile of v15, /device:TPU:0, one launch (start us, length us, event | category | flops | bytes accessed | tf_op | source)
XLA Modules:
  0.0 89.1 jit_solution(12443303564598825769)
XLA Ops:
  1.2 1.9 %dynamic_slice.3 = bf16[128,2048]{1,0:T(8,128)(2,1)} dynamic-slice(bf16[256,4096]{1,0:T(8,128)(2,1)} %refs_1_.12, s32[]{:T(128)S(6)} %select_n.6, s32[]{:T(128)S(6)} %select_n.7), dynamic_slice_sizes={128,2048} | dynamic-slice | bytes 1048580 | tf_op jit(solution)/shard_map/dynamic_slice | solution.py:372
  3.0 2.6 %collective-permute-start.1 = (bf16[128,2048]{1,0:T(8,128)(2,1)}, bf16[128,2048]{1,0:T(8,128)(2,1)S(1)}, u32[]{:S(2)}, u32[]{:S(2)}) collective-permute-start(bf16[128,2048]{1,0:T(8,128)(2,1)} %dynamic_slice.3), channel_id=1, source_target_pairs={{0,1},{1,2},{2,3},{3,0},{4,5},{5,6},{6,7},{7,4},{8,9},{9,10},{10,1... | collective-permute-start | bytes 1572872 | tf_op jit(solution)/shard_map/ppermute | solution.py:332
  5.7 2.0 %collective-permute-start.2 = (bf16[128,2048]{1,0:T(8,128)(2,1)}, bf16[128,2048]{1,0:T(8,128)(2,1)}, u32[]{:S(2)}, u32[]{:S(2)}) collective-permute-start(bf16[128,2048]{1,0:T(8,128)(2,1)} %dynamic_slice.3), channel_id=1, source_target_pairs={{0,3},{1,0},{2,1},{3,2},{4,7},{5,4},{6,5},{7,6},{8,11},{9,8},{10,9... | collective-permute-start | bytes 1572872 | tf_op jit(solution)/shard_map/ppermute | solution.py:332
  7.8 1.2 %pad_maximum_fusion.refs_2_ = bf16[3,384,256]{2,1,0:T(8,128)(2,1)S(1)} fusion(bf16[1,384,256]{2,1,0:T(8,128)(2,1)} %bitcast.18, bf16[1,384,256]{2,1,0:T(8,128)(2,1)} %bitcast.19, bf16[1,384,256]{2,1,0:T(8,128)(2,1)} %bitcast.17), kind=kLoop, calls=%fused_computation | loop fusion | flops 589824 | bytes 1179648 | tf_op jit(solution)/shard_map/stack | solution.py:382
  9.0 2.6 %shard_map.93 = (bf16[4,384,384]{2,1,0:T(8,128)(2,1)S(1)}, f32[384,128]{1,0:T(8,128)S(1)}, f32[384,128]{1,0:T(8,128)}, bf16[384,128]{1,0:T(8,128)(2,1)}, f32[128,128]{1,0:T(8,128)S(1)}, /*index=5*/f32[128,128]{1,0:T(8,128)}) custom-call(s32[3,3]{1,0:T(4,128)S(1)} %copy-done.25, s32[3]{0:T(128)S(1)} %pad_add_fusion.2.refs_1_.refs_0_, ...), custom_call_target="tpu_custom_call" | custom-call | flops 264241152 | bytes 2392064 | tf_op jit(solution)/shard_map/pallas_call | solution.py:94
  11.5 1.1 %copy-done.10 = bf16[4,384,384]{2,1,0:T(8,128)(2,1)} copy-done((bf16[4,384,384]{2,1,0:T(8,128)(2,1)}, bf16[4,384,384]{2,1,0:T(8,128)(2,1)S(1)}, u32[]{:S(2)}) %copy-start.10) | copy-done | bytes 1179672
  13.2 0.7 copy-done.18
  14.6 1.1 %collective-permute-done.3.refs_1_.refs_8_ = bf16[384,128]{1,0:T(8,128)(2,1)S(1)} collective-permute-done((bf16[384,128]{1,0:T(8,128)(2,1)}, bf16[384,128]{1,0:T(8,128)(2,1)S(1)}, u32[]{:S(2)}, u32[]{:S(2)}) %collective-permute-start.3) | collective-permute-done | bytes 98336 | tf_op jit(solution)/shard_map/ppermute | solution.py:332
  15.7 0.6 copy-done.14
  16.3 0.9 add.14
  17.2 1.7 %collective-permute-start.6 = (f32[128,128]{1,0:T(8,128)S(1)}, f32[128,128]{1,0:T(8,128)S(1)}, u32[]{:S(2)}, u32[]{:S(2)}) collective-permute-start(f32[128,128]{1,0:T(8,128)S(1)} %add.14), channel_id=1, source_target_pairs={{0,8},{1,9},{2,10},{3,11},{4,12},{5,13},{6,14},{7,15},{8,0},{9,1},... | collective-permute-start | bytes 196616 | tf_op jit(solution)/shard_map/ppermute | solution.py:332
  18.9 1.5 %collective-permute-start.7 = (f32[128,128]{1,0:T(8,128)S(1)}, f32[128,128]{1,0:T(8,128)S(1)}, u32[]{:S(2)}, u32[]{:S(2)}) collective-permute-start(f32[128,128]{1,0:T(8,128)S(1)} %add.14), channel_id=1, source_target_pairs={{0,16},{1,17},{2,18},{3,19},{4,20},{5,21},{6,22},{7,23},{8,24},{9,... | collective-permute-start | bytes 196616 | tf_op jit(solution)/shard_map/ppermute | solution.py:332
  20.8 0.7 collective-permute-done.6.refs_4_
  21.6 1.6 %collective-permute-done.7.refs_5_ = f32[128,128]{1,0:T(8,128)S(1)} collective-permute-done((f32[128,128]{1,0:T(8,128)S(1)}, f32[128,128]{1,0:T(8,128)S(1)}, u32[]{:S(2)}, u32[]{:S(2)}) %collective-permute-start.7) | collective-permute-done | bytes 65568 | tf_op jit(solution)/shard_map/ppermute | solution.py:332
  23.2 2.4 %collective-permute-done.8.refs_6_ = f32[128,128]{1,0:T(8,128)S(1)} collective-permute-done((f32[128,128]{1,0:T(8,128)S(1)}, f32[128,128]{1,0:T(8,128)S(1)}, u32[]{:S(2)}, u32[]{:S(2)}) %collective-permute-start.8) | collective-permute-done | bytes 65568 | tf_op jit(solution)/shard_map/ppermute | solution.py:332
  25.6 0.9 %copy-done.6 = bf16[384,256]{1,0:T(8,128)(2,1)S(1)} copy-done((bf16[384,256]{1,0:T(8,128)(2,1)S(1)}, bf16[384,256]{1,0:T(8,128)(2,1)}, u32[]{:S(2)}) %copy-start.6) | copy-done | bytes 196632
  26.6 0.8 copy-done.13
  27.4 0.9 copy-done.15
  28.3 0.9 %copy-done.19 = f32[384,128]{1,0:T(8,128)S(1)} copy-done((f32[384,128]{1,0:T(8,128)S(1)}, f32[384,128]{1,0:T(8,128)}, u32[]{:S(2)}) %copy-start.19) | copy-done | bytes 196632
  29.2 1.2 %shard_map.95 = (bf16[4,192,128]{2,1,0:T(8,128)(2,1)S(1)}, f32[128,128]{1,0:T(8,128)S(1)}, f32[128,128]{1,0:T(8,128)S(1)}) custom-call(s32[4]{0:T(128)S(1)} %add_convert_fusion.refs_0_, s32[3]{0:T(128)S(1)} %pad_add_fusion.2.refs_1_.refs_0_, f32[128,128]{1,0:T(8,128)S(1)} %copy-done.13, f32[128,128]{1,0:T(8,128)} %collective-permute-done.5.refs_3_, ...), custom_call_target="tpu_custom_call" | custom-call | flops 1 | bytes 1343488 | tf_op jit(solution)/shard_map/pallas_call | solution.py:94
  30.5 0.6 copy-done.16
  31.1 0.7 copy-done.20
  31.8 0.6 copy-done.26
  32.4 0.8 copy-done.3
  33.8 1.5 %collective-permute-start.12 = (bf16[128,2048]{1,0:T(8,128)(2,1)}, bf16[128,2048]{1,0:T(8,128)(2,1)}, u32[]{:S(2)}, u32[]{:S(2)}) collective-permute-start(bf16[128,2048]{1,0:T(8,128)(2,1)} %get-tuple-element.45.refs_6_.refs_5_), channel_id=1, source_target_pairs={{0,16},{1,17},{2,18},{3,19},{4,20},{5,21},{6,22},{7,23},{8,24},{9,... | collective-permute-start | bytes 1572872 | tf_op jit(solution)/shard_map/ppermute | solution.py:332
  35.4 4.0 %all-to-all-start = ((bf16[4,192,128]{2,1,0:T(8,128)(2,1)}), bf16[4,192,128]{2,1,0:T(8,128)(2,1)}, u32[]{:S(2)}, u32[]{:S(2)}) async-start(bf16[4,192,128]{2,1,0:T(8,128)(2,1)} %copy-done.20), calls=%async_computation | async-start | bytes 393216 | tf_op jit(solution)/shard_map/all_to_all | solution.py:399
  39.5 1.1 %copy-done.1 = bf16[96,4096]{1,0:T(8,128)(2,1)S(1)} copy-done((bf16[96,4096]{1,0:T(8,128)(2,1)S(1)}, bf16[96,4096]{1,0:T(8,128)(2,1)}, u32[]{:S(2)}) %copy-start.1) | copy-done | bytes 786456
  40.6 1.0 %copy-done.4 = bf16[128,2048]{1,0:T(8,128)(2,1)S(1)} copy-done((bf16[128,2048]{1,0:T(8,128)(2,1)S(1)}, bf16[128,2048]{1,0:T(8,128)(2,1)}, u32[]{:S(2)}) %copy-start.4) | copy-done | bytes 524312
  41.6 3.3 %shard_map.98 = (bf16[192,128]{1,0:T(8,128)(2,1)}, f32[192,256]{1,0:T(8,128)S(1)}) custom-call(s32[4]{0:T(128)S(1)} %pad_add_fusion.1.refs_0_, bf16[96,4096]{1,0:T(8,128)(2,1)S(1)} %copy-done.1, bf16[96,4096]{1,0:T(8,128)(2,1)S(1)} %collective-permute-done.refs_3_.refs_2_, bf16[256,4096]{1,0:T(8,128)(2,1)S(1)} %copy-done, bf16[128,2048]{1,0:T(8,128)(2,1)S(1)} %copy-done.4, ...), custom_call_target="tpu_custom_call" | custom-call | flops 402653184 | bytes 4964352 | tf_op jit(solution)/shard_map/pallas_call | solution.py:94
  44.9 4.5 %collective-permute-done.9.refs_5_.refs_6_ = bf16[128,2048]{1,0:T(8,128)(2,1)} collective-permute-done((bf16[128,2048]{1,0:T(8,128)(2,1)}, bf16[128,2048]{1,0:T(8,128)(2,1)}, u32[]{:S(2)}, u32[]{:S(2)}) %collective-permute-start.9) | collective-permute-done | bytes 524320 | tf_op jit(solution)/shard_map/ppermute | solution.py:332
  49.5 3.3 %shard_map.99 = (bf16[192,128]{1,0:T(8,128)(2,1)}, bf16[192,128]{1,0:T(8,128)(2,1)}, bf16[128,1024]{1,0:T(8,128)(2,1)}, bf16[128,1024]{1,0:T(8,128)(2,1)}) custom-call(s32[4]{0:T(128)S(1)} %pad_add_fusion.1.refs_0_, bf16[96,4096]{1,0:T(8,128)(2,1)S(1)} %copy-done.1, bf16[96,4096]{1,0:T(8,128)(2,1)S(1)} %collective-permute-done.refs_3_.refs_2_, ...), custom_call_target="tpu_custom_call" | custom-call | flops 201326592 | bytes 3964928 | tf_op jit(solution)/shard_map/pallas_call | solution.py:94
  53.4 1.3 %collective-permute-start.14 = (bf16[128,1024]{1,0:T(8,128)(2,1)}, bf16[128,1024]{1,0:T(8,128)(2,1)}, u32[]{:S(2)}, u32[]{:S(2)}) collective-permute-start(bf16[128,1024]{1,0:T(8,128)(2,1)} %get-tuple-element.51), channel_id=1, source_target_pairs={{0,16},{1,17},{2,18},{3,19},{4,20},{5,21},{6,22},{7,23},{8,24},{9,... | collective-permute-start | bytes 786440 | tf_op jit(solution)/shard_map/ppermute | solution.py:332
  55.3 1.4 %collective-permute-start.16 = (bf16[192,128]{1,0:T(8,128)(2,1)}, bf16[192,128]{1,0:T(8,128)(2,1)S(1)}, u32[]{:S(2)}, u32[]{:S(2)}) collective-permute-start(bf16[192,128]{1,0:T(8,128)(2,1)} %get-tuple-element.54), channel_id=1, source_target_pairs={{0,1},{1,2},{2,3},{3,0},{4,5},{5,6},{6,7},{7,4},{8,9},{9,10},{10,1... | collective-permute-start | bytes 147464 | tf_op jit(solution)/shard_map/ppermute | solution.py:332
  56.7 1.1 %copy-done.2 = bf16[96,4096]{1,0:T(8,128)(2,1)S(1)} copy-done((bf16[96,4096]{1,0:T(8,128)(2,1)S(1)}, bf16[96,4096]{1,0:T(8,128)(2,1)}, u32[]{:S(2)}) %copy-start.2) | copy-done | bytes 786456
  57.9 0.7 copy-done.24
  58.5 3.1 %shard_map.97 = (f32[192,128]{1,0:T(8,128)S(1)}, f32[96,2048]{1,0:T(8,128)S(1)}, f32[96,2048]{1,0:T(8,128)S(1)}) custom-call(s32[4]{0:T(128)S(1)} %copy-done.24, bf16[96,4096]{1,0:T(8,128)(2,1)S(1)} %copy-done.2, bf16[96,4096]{1,0:T(8,128)(2,1)S(1)} %collective-permute-done.refs_3_.refs_2_, bf16[256,4096]{1,0:T(8,128)(2,1)S(1)} %copy-done, ...), custom_call_target="tpu_custom_call" | custom-call | flops 402653184 | bytes 7110656 | tf_op jit(solution)/shard_map/pallas_call | solution.py:94
  62.3 2.0 %shard_map.100 = bf16[192,128]{1,0:T(8,128)(2,1)S(1)} custom-call(s32[4]{0:T(128)S(1)} %copy-done.24, bf16[96,4096]{1,0:T(8,128)(2,1)S(1)} %copy-done.2, bf16[96,4096]{1,0:T(8,128)(2,1)S(1)} %collective-permute-done.refs_3_.refs_2_, bf16[128,1024]{1,0:T(8,128)(2,1)} %collective-permute-done.13.refs_3_.refs_4_, ...), custom_call_target="tpu_custom_call" | custom-call | flops 100663296 | bytes 2244608 | tf_op jit(solution)/shard_map/pallas_call | solution.py:94
  65.0 5.2 %collective-permute-done.17.refs_7_.refs_4_ = bf16[192,128]{1,0:T(8,128)(2,1)S(1)} collective-permute-done((bf16[192,128]{1,0:T(8,128)(2,1)S(1)}, bf16[192,128]{1,0:T(8,128)(2,1)S(1)}, u32[]{:S(2)}, u32[]{:S(2)}) %collective-permute-start.17) | collective-permute-done | bytes 49184 | tf_op jit(solution)/shard_map/ppermute | solution.py:332
  70.2 3.0 %shard_map.101 = (f32[96,2048]{1,0:T(8,128)S(1)}, f32[96,2048]{1,0:T(8,128)S(1)}) custom-call(s32[4]{0:T(128)S(1)} %copy-done.24, bf16[256,4096]{1,0:T(8,128)(2,1)S(1)} %copy-done, bf16[128,2048]{1,0:T(8,128)(2,1)} %collective-permute-done.11.refs_3_.refs_2_, bf16[128,2048]{1,0:T(8,128)(2,1)} %collective-permute-done.12.refs_4_.refs_3_, ...), custom_call_target="tpu_custom_call" | custom-call | flops 402653184 | bytes 5439488 | tf_op jit(solution)/shard_map/pallas_call | solution.py:94
  73.8 1.8 %collective-permute-done.22.refs_8_ = bf16[192,128]{1,0:T(8,128)(2,1)S(1)} collective-permute-done((bf16[192,128]{1,0:T(8,128)(2,1)S(1)}, bf16[192,128]{1,0:T(8,128)(2,1)S(1)}, u32[]{:S(2)}, u32[]{:S(2)}) %collective-permute-start.22) | collective-permute-done | bytes 49184 | tf_op jit(solution)/shard_map/ppermute | solution.py:332
  75.6 1.1 %shard_map.103 = (bf16[384,256]{1,0:T(8,128)(2,1)S(1)}, f32[128,128]{1,0:T(8,128)S(1)}, f32[128,128]{1,0:T(8,128)S(1)}) custom-call(s32[3]{0:T(128)S(1)} %copy-done.22, bf16[384,256]{1,0:T(8,128)(2,1)S(1)} %copy-done.7, bf16[192,128]{1,0:T(8,128)(2,1)} %get-tuple-element.55.refs_2_, bf16[192,128]{1,0:T(8,128)(2,1)S(1)} %collective-permute-done.15.refs_6_.refs_3_, ...), custom_call_target="tpu_custom_call" | custom-call | flops 1 | bytes 917504 | tf_op jit(solution)/shard_map/pallas_call | solution.py:94
  77.3 0.7 collective-permute-done.24.refs_2_
  78.0 1.1 %collective-permute-start.25 = (f32[128,128]{1,0:T(8,128)S(1)}, f32[128,128]{1,0:T(8,128)S(1)}, u32[]{:S(2)}, u32[]{:S(2)}) collective-permute-start(f32[128,128]{1,0:T(8,128)S(1)} %add.15.refs_8_), channel_id=1, source_target_pairs={{0,8},{1,9},{2,10},{3,11},{4,12},{5,13},{6,14},{7,15},{8,0},{9,1},... | collective-permute-start | bytes 196616 | tf_op jit(solution)/shard_map/ppermute | solution.py:332
  79.2 0.9 collective-permute-start.26
  80.0 1.5 %collective-permute-start.27 = (f32[128,128]{1,0:T(8,128)S(1)}, f32[128,128]{1,0:T(8,128)S(1)}, u32[]{:S(2)}, u32[]{:S(2)}) collective-permute-start(f32[128,128]{1,0:T(8,128)S(1)} %add.15.refs_8_), channel_id=1, source_target_pairs={{0,24},{1,25},{2,26},{3,27},{4,28},{5,29},{6,30},{7,31},{8,16},{9,... | collective-permute-start | bytes 196616 | tf_op jit(solution)/shard_map/ppermute | solution.py:332
  81.7 3.0 %shard_map.104 = (bf16[384,256]{1,0:T(8,128)(2,1)}, f32[384,256]{1,0:T(8,128)S(1)}, f32[384,256]{1,0:T(8,128)S(1)}) custom-call(s32[3]{0:T(128)S(1)} %copy-done.22, bf16[384,256]{1,0:T(8,128)(2,1)S(1)} %copy-done.7, bf16[384,256]{1,0:T(8,128)(2,1)S(1)} %copy-done.9, bf16[384,256]{1,0:T(8,128)(2,1)S(1)} %copy-done.8, ...), custom_call_target="tpu_custom_call" | custom-call | flops 528482304 | bytes 3080192 | tf_op jit(solution)/shard_map/pallas_call | solution.py:94
  85.9 1.6 %shard_map.102 = (bf16[96,4096]{1,0:T(8,128)(2,1)}, f32[8,128]{1,0:T(8,128)S(1)}) custom-call(s32[2]{0:T(128)S(1)} %pad_add_fusion.refs_0_, f32[96,2048]{1,0:T(8,128)S(1)} %get-tuple-element.47.refs_1_, f32[96,2048]{1,0:T(8,128)S(1)} %collective-permute-done.10.refs_2_, f32[96,2048]{1,0:T(8,128)S(1)} %get-tuple-element.56.refs_3_, ...), custom_call_target="tpu_custom_call" | custom-call | flops 1 | bytes 3936256 | tf_op jit(solution)/shard_map/pallas_call | solution.py:94
  87.5 1.6 %shard_map.106 = (bf16[384,256]{1,0:T(8,128)(2,1)}, bf16[384,256]{1,0:T(8,128)(2,1)}) custom-call(s32[3]{0:T(128)S(1)} %copy-done.22, bf16[384,256]{1,0:T(8,128)(2,1)S(1)} %copy-done.9, bf16[384,256]{1,0:T(8,128)(2,1)S(1)} %copy-done.8, f32[384,256]{1,0:T(8,128)S(1)} %get-tuple-element.65.refs_6_.refs_3_, f32[384,256]{1,0:T(8,128)S(1)} %get-tuple-element.66.refs_4_, ...), custom_call_target="tpu_custom_call" | custom-call | flops 1 | bytes 1703936 | tf_op jit(solution)/shard_map/pallas_call | solution.py:94
  (91 shorter events, 8.0 us)
Async XLA Ops:
  0.6 8.3 %copy-start.25 = (s32[3,3]{1,0:T(4,128)S(1)}, s32[3,3]{1,0:T(4,128)}, u32[]{:S(2)}) copy-start(s32[3,3]{1,0:T(4,128)} %refs_0_.1) | copy-start | bytes 112
  0.6 8.3 %collective-permute-start = (bf16[96,4096]{1,0:T(8,128)(2,1)}, bf16[96,4096]{1,0:T(8,128)(2,1)S(1)}, u32[]{:S(2)}, u32[]{:S(2)}) collective-permute-start(bf16[96,4096]{1,0:T(8,128)(2,1)} %refs_1_.11), channel_id=1, source_target_pairs={{0,4},{1,5},{2,6},{3,7},{4,0},{5,1},{6,2},{7,3},{8,12},{9,13},{10,... | collective-permute-start | bytes 2359304 | tf_op jit(solution)/shard_map/ppermute | solution.py:332
  3.0 29.4 %collective-permute-start.1 = (bf16[128,2048]{1,0:T(8,128)(2,1)}, bf16[128,2048]{1,0:T(8,128)(2,1)S(1)}, u32[]{:S(2)}, u32[]{:S(2)}) collective-permute-start(bf16[128,2048]{1,0:T(8,128)(2,1)} %dynamic_slice.3), channel_id=1, source_target_pairs={{0,1},{1,2},{2,3},{3,0},{4,5},{5,6},{6,7},{7,4},{8,9},{9,10},{10,1... | collective-permute-start | bytes 1572872 | tf_op jit(solution)/shard_map/ppermute | solution.py:332
  5.7 26.8 %collective-permute-start.2 = (bf16[128,2048]{1,0:T(8,128)(2,1)}, bf16[128,2048]{1,0:T(8,128)(2,1)}, u32[]{:S(2)}, u32[]{:S(2)}) collective-permute-start(bf16[128,2048]{1,0:T(8,128)(2,1)} %dynamic_slice.3), channel_id=1, source_target_pairs={{0,3},{1,0},{2,1},{3,2},{4,7},{5,4},{6,5},{7,6},{8,11},{9,8},{10,9... | collective-permute-start | bytes 1572872 | tf_op jit(solution)/shard_map/ppermute | solution.py:332
  7.8 22.7 %copy-start.21 = (s32[3]{0:T(128)}, s32[3]{0:T(128)S(1)}, u32[]{:S(2)}) copy-start(s32[3]{0:T(128)S(1)} %pad_add_fusion.2.refs_1_.refs_0_) | copy-start | bytes 40
  8.9 30.5 %copy-start = (bf16[256,4096]{1,0:T(8,128)(2,1)S(1)}, bf16[256,4096]{1,0:T(8,128)(2,1)}, u32[]{:S(2)}) copy-start(bf16[256,4096]{1,0:T(8,128)(2,1)} %refs_1_.12) | copy-start | bytes 6291460
  11.5 1.1 %copy-start.10 = (bf16[4,384,384]{2,1,0:T(8,128)(2,1)}, bf16[4,384,384]{2,1,0:T(8,128)(2,1)S(1)}, u32[]{:S(2)}) copy-start(bf16[4,384,384]{2,1,0:T(8,128)(2,1)S(1)} %get-tuple-element.60.refs_5_) | copy-start | bytes 3538948
  13.9 1.8 %collective-permute-start.4 = (f32[384,128]{1,0:T(8,128)}, f32[384,128]{1,0:T(8,128)}, u32[]{:S(2)}, u32[]{:S(2)}) collective-permute-start(f32[384,128]{1,0:T(8,128)} %get-tuple-element.40), channel_id=1, source_target_pairs={{0,4},{1,5},{2,6},{3,7},{4,0},{5,1},{6,2},{7,3},{8,12},{9,13},{10,... | collective-permute-start | bytes 589832 | tf_op jit(solution)/shard_map/ppermute | solution.py:332
  14.1 1.6 %collective-permute-start.3 = (bf16[384,128]{1,0:T(8,128)(2,1)}, bf16[384,128]{1,0:T(8,128)(2,1)S(1)}, u32[]{:S(2)}, u32[]{:S(2)}) collective-permute-start(bf16[384,128]{1,0:T(8,128)(2,1)} %get-tuple-element.39), channel_id=1, source_target_pairs={{0,4},{1,5},{2,6},{3,7},{4,0},{5,1},{6,2},{7,3},{8,12},{9,13},{10,... | collective-permute-start | bytes 294920 | tf_op jit(solution)/shard_map/ppermute | solution.py:332
  14.4 1.9 %collective-permute-start.5 = (f32[128,128]{1,0:T(8,128)}, f32[128,128]{1,0:T(8,128)}, u32[]{:S(2)}, u32[]{:S(2)}) collective-permute-start(f32[128,128]{1,0:T(8,128)} %get-tuple-element.41), channel_id=1, source_target_pairs={{0,4},{1,5},{2,6},{3,7},{4,0},{5,1},{6,2},{7,3},{8,12},{9,13},{10,... | collective-permute-start | bytes 196616 | tf_op jit(solution)/shard_map/ppermute | solution.py:332
  17.2 4.4 %collective-permute-start.6 = (f32[128,128]{1,0:T(8,128)S(1)}, f32[128,128]{1,0:T(8,128)S(1)}, u32[]{:S(2)}, u32[]{:S(2)}) collective-permute-start(f32[128,128]{1,0:T(8,128)S(1)} %add.14), channel_id=1, source_target_pairs={{0,8},{1,9},{2,10},{3,11},{4,12},{5,13},{6,14},{7,15},{8,0},{9,1},... | collective-permute-start | bytes 196616 | tf_op jit(solution)/shard_map/ppermute | solution.py:332
  18.9 4.3 %collective-permute-start.7 = (f32[128,128]{1,0:T(8,128)S(1)}, f32[128,128]{1,0:T(8,128)S(1)}, u32[]{:S(2)}, u32[]{:S(2)}) collective-permute-start(f32[128,128]{1,0:T(8,128)S(1)} %add.14), channel_id=1, source_target_pairs={{0,16},{1,17},{2,18},{3,19},{4,20},{5,21},{6,22},{7,23},{8,24},{9,... | collective-permute-start | bytes 196616 | tf_op jit(solution)/shard_map/ppermute | solution.py:332
  20.5 5.2 %collective-permute-start.8 = (f32[128,128]{1,0:T(8,128)S(1)}, f32[128,128]{1,0:T(8,128)S(1)}, u32[]{:S(2)}, u32[]{:S(2)}) collective-permute-start(f32[128,128]{1,0:T(8,128)S(1)} %add.14), channel_id=1, source_target_pairs={{0,24},{1,25},{2,26},{3,27},{4,28},{5,29},{6,30},{7,31},{8,16},{9,... | collective-permute-start | bytes 196616 | tf_op jit(solution)/shard_map/ppermute | solution.py:332
  25.6 0.9 %copy-start.6 = (bf16[384,256]{1,0:T(8,128)(2,1)S(1)}, bf16[384,256]{1,0:T(8,128)(2,1)}, u32[]{:S(2)}) copy-start(bf16[384,256]{1,0:T(8,128)(2,1)} %refs_1_.14) | copy-start | bytes 589828
  28.3 0.9 %copy-start.19 = (f32[384,128]{1,0:T(8,128)S(1)}, f32[384,128]{1,0:T(8,128)}, u32[]{:S(2)}) copy-start(f32[384,128]{1,0:T(8,128)} %copy-done.18) | copy-start | bytes 589828
  33.2 16.3 %collective-permute-start.9 = (bf16[128,2048]{1,0:T(8,128)(2,1)}, bf16[128,2048]{1,0:T(8,128)(2,1)}, u32[]{:S(2)}, u32[]{:S(2)}) collective-permute-start(bf16[128,2048]{1,0:T(8,128)(2,1)} %get-tuple-element.44.refs_4_), channel_id=1, source_target_pairs={{0,1},{1,2},{2,3},{3,0},{4,5},{5,6},{6,7},{7,4},{8,9},{9,10},{10,1... | collective-permute-start | bytes 1572872 | tf_op jit(solution)/shard_map/ppermute | solution.py:332
  33.2 16.3 %collective-permute-start.11 = (bf16[128,2048]{1,0:T(8,128)(2,1)}, bf16[128,2048]{1,0:T(8,128)(2,1)}, u32[]{:S(2)}, u32[]{:S(2)}) collective-permute-start(bf16[128,2048]{1,0:T(8,128)(2,1)} %get-tuple-element.44.refs_4_), channel_id=1, source_target_pairs={{0,8},{1,9},{2,10},{3,11},{4,12},{5,13},{6,14},{7,15},{8,0},{9,1},... | collective-permute-start | bytes 1572872 | tf_op jit(solution)/shard_map/ppermute | solution.py:332
  33.8 15.7 %collective-permute-start.12 = (bf16[128,2048]{1,0:T(8,128)(2,1)}, bf16[128,2048]{1,0:T(8,128)(2,1)}, u32[]{:S(2)}, u32[]{:S(2)}) collective-permute-start(bf16[128,2048]{1,0:T(8,128)(2,1)} %get-tuple-element.45.refs_6_.refs_5_), channel_id=1, source_target_pairs={{0,16},{1,17},{2,18},{3,19},{4,20},{5,21},{6,22},{7,23},{8,24},{9,... | collective-permute-start | bytes 1572872 | tf_op jit(solution)/shard_map/ppermute | solution.py:332
  35.4 21.4 %all-to-all-start = ((bf16[4,192,128]{2,1,0:T(8,128)(2,1)}), bf16[4,192,128]{2,1,0:T(8,128)(2,1)}, u32[]{:S(2)}, u32[]{:S(2)}) async-start(bf16[4,192,128]{2,1,0:T(8,128)(2,1)} %copy-done.20), calls=%async_computation | async-start | bytes 393216 | tf_op jit(solution)/shard_map/all_to_all | solution.py:399
  39.4 1.1 %copy-start.1 = (bf16[96,4096]{1,0:T(8,128)(2,1)S(1)}, bf16[96,4096]{1,0:T(8,128)(2,1)}, u32[]{:S(2)}) copy-start(bf16[96,4096]{1,0:T(8,128)(2,1)} %refs_1_.11) | copy-start | bytes 2359300
  40.6 1.0 %copy-start.4 = (bf16[128,2048]{1,0:T(8,128)(2,1)S(1)}, bf16[128,2048]{1,0:T(8,128)(2,1)}, u32[]{:S(2)}) copy-start(bf16[128,2048]{1,0:T(8,128)(2,1)} %get-tuple-element.44.refs_4_) | copy-start | bytes 1572868
  41.6 7.9 %copy-start.23 = (s32[4]{0:T(128)}, s32[4]{0:T(128)S(1)}, u32[]{:S(2)}) copy-start(s32[4]{0:T(128)S(1)} %pad_add_fusion.1.refs_0_) | copy-start | bytes 52
  44.9 11.8 %copy-start.5 = (bf16[128,2048]{1,0:T(8,128)(2,1)S(1)}, bf16[128,2048]{1,0:T(8,128)(2,1)}, u32[]{:S(2)}) copy-start(bf16[128,2048]{1,0:T(8,128)(2,1)} %get-tuple-element.44.refs_4_) | copy-start | bytes 1572868
  52.8 9.5 %collective-permute-start.13 = (bf16[128,1024]{1,0:T(8,128)(2,1)}, bf16[128,1024]{1,0:T(8,128)(2,1)}, u32[]{:S(2)}, u32[]{:S(2)}) collective-permute-start(bf16[128,1024]{1,0:T(8,128)(2,1)} %get-tuple-element.50), channel_id=1, source_target_pairs={{0,8},{1,9},{2,10},{3,11},{4,12},{5,13},{6,14},{7,15},{8,0},{9,1},... | collective-permute-start | bytes 786440 | tf_op jit(solution)/shard_map/ppermute | solution.py:332
  53.4 8.9 %collective-permute-start.14 = (bf16[128,1024]{1,0:T(8,128)(2,1)}, bf16[128,1024]{1,0:T(8,128)(2,1)}, u32[]{:S(2)}, u32[]{:S(2)}) collective-permute-start(bf16[128,1024]{1,0:T(8,128)(2,1)} %get-tuple-element.51), channel_id=1, source_target_pairs={{0,16},{1,17},{2,18},{3,19},{4,20},{5,21},{6,22},{7,23},{8,24},{9,... | collective-permute-start | bytes 786440 | tf_op jit(solution)/shard_map/ppermute | solution.py:332
  54.7 7.0 %collective-permute-start.15 = (bf16[192,128]{1,0:T(8,128)(2,1)}, bf16[192,128]{1,0:T(8,128)(2,1)S(1)}, u32[]{:S(2)}, u32[]{:S(2)}) collective-permute-start(bf16[192,128]{1,0:T(8,128)(2,1)} %get-tuple-element.53), channel_id=1, source_target_pairs={{0,3},{1,0},{2,1},{3,2},{4,7},{5,4},{6,5},{7,6},{8,11},{9,8},{10,9... | collective-permute-start | bytes 147464 | tf_op jit(solution)/shard_map/ppermute | solution.py:332
  55.3 7.0 %collective-permute-start.16 = (bf16[192,128]{1,0:T(8,128)(2,1)}, bf16[192,128]{1,0:T(8,128)(2,1)S(1)}, u32[]{:S(2)}, u32[]{:S(2)}) collective-permute-start(bf16[192,128]{1,0:T(8,128)(2,1)} %get-tuple-element.54), channel_id=1, source_target_pairs={{0,1},{1,2},{2,3},{3,0},{4,5},{5,6},{6,7},{7,4},{8,9},{9,10},{10,1... | collective-permute-start | bytes 147464 | tf_op jit(solution)/shard_map/ppermute | solution.py:332
  56.7 8.3 %collective-permute-start.18 = (bf16[192,128]{1,0:T(8,128)(2,1)}, bf16[192,128]{1,0:T(8,128)(2,1)S(1)}, u32[]{:S(2)}, u32[]{:S(2)}) collective-permute-start(bf16[192,128]{1,0:T(8,128)(2,1)} %get-tuple-element.55.refs_2_), channel_id=1, source_target_pairs={{0,4},{1,5},{2,6},{3,7},{4,0},{5,1},{6,2},{7,3},{8,12},{9,13},{10,... | collective-permute-start | bytes 147464 | tf_op jit(solution)/shard_map/ppermute | solution.py:332
  56.7 1.1 %copy-start.2 = (bf16[96,4096]{1,0:T(8,128)(2,1)S(1)}, bf16[96,4096]{1,0:T(8,128)(2,1)}, u32[]{:S(2)}) copy-start(bf16[96,4096]{1,0:T(8,128)(2,1)} %refs_1_.11) | copy-start | bytes 2359300
  61.7 3.4 %collective-permute-start.19 = (bf16[192,128]{1,0:T(8,128)(2,1)S(1)}, bf16[192,128]{1,0:T(8,128)(2,1)S(1)}, u32[]{:S(2)}, u32[]{:S(2)}) collective-permute-start(bf16[192,128]{1,0:T(8,128)(2,1)S(1)} %collective-permute-done.15.refs_6_.refs_3_), channel_id=1, source_target_pairs={{0,4},{1,5},{2,6},{3,7},{4,0},{5,1},{6,2},{7,3},{8,12},{9,13},{10,... | collective-permute-start | bytes 147464 | tf_op jit(solution)/shard_map/ppermute | solution.py:332
  62.2 2.8 %collective-permute-start.20 = (bf16[192,128]{1,0:T(8,128)(2,1)S(1)}, bf16[192,128]{1,0:T(8,128)(2,1)S(1)}, u32[]{:S(2)}, u32[]{:S(2)}) collective-permute-start(bf16[192,128]{1,0:T(8,128)(2,1)S(1)} %collective-permute-done.16.refs_7_.refs_5_), channel_id=1, source_target_pairs={{0,4},{1,5},{2,6},{3,7},{4,0},{5,1},{6,2},{7,3},{8,12},{9,13},{10,... | collective-permute-start | bytes 147464 | tf_op jit(solution)/shard_map/ppermute | solution.py:332
  64.4 11.2 %copy-start.7 = (bf16[384,256]{1,0:T(8,128)(2,1)S(1)}, bf16[384,256]{1,0:T(8,128)(2,1)}, u32[]{:S(2)}) copy-start(bf16[384,256]{1,0:T(8,128)(2,1)} %refs_1_.14) | copy-start | bytes 589828
  64.4 11.2 %copy-start.22 = (s32[3]{0:T(128)S(1)}, s32[3]{0:T(128)}, u32[]{:S(2)}) copy-start(s32[3]{0:T(128)} %copy-done.21) | copy-start | bytes 40
  64.4 5.8 %collective-permute-start.17 = (bf16[192,128]{1,0:T(8,128)(2,1)S(1)}, bf16[192,128]{1,0:T(8,128)(2,1)S(1)}, u32[]{:S(2)}, u32[]{:S(2)}) collective-permute-start(bf16[192,128]{1,0:T(8,128)(2,1)S(1)} %shard_map.100), channel_id=1, source_target_pairs={{0,2},{1,3},{2,0},{3,1},{4,6},{5,7},{6,4},{7,5},{8,10},{9,11},{10,... | collective-permute-start | bytes 147464 | tf_op jit(solution)/shard_map/ppermute | solution.py:332
  64.5 12.4 %copy-start.27 = (f32[128,128]{1,0:T(8,128)S(1)}, f32[128,128]{1,0:T(8,128)}, u32[]{:S(2)}) copy-start(f32[128,128]{1,0:T(8,128)} %copy-done.26) | copy-start | bytes 196612
  64.5 17.2 %copy-start.8 = (bf16[384,256]{1,0:T(8,128)(2,1)S(1)}, bf16[384,256]{1,0:T(8,128)(2,1)}, u32[]{:S(2)}) copy-start(bf16[384,256]{1,0:T(8,128)(2,1)} %refs_2_.3) | copy-start | bytes 589828
  64.5 17.2 %copy-start.9 = (bf16[384,256]{1,0:T(8,128)(2,1)S(1)}, bf16[384,256]{1,0:T(8,128)(2,1)}, u32[]{:S(2)}) copy-start(bf16[384,256]{1,0:T(8,128)(2,1)} %refs_1_.15) | copy-start | bytes 589828
  64.5 17.1 %copy-start.11 = (bf16[4,384,384]{2,1,0:T(8,128)(2,1)S(1)}, bf16[4,384,384]{2,1,0:T(8,128)(2,1)}, u32[]{:S(2)}) copy-start(bf16[4,384,384]{2,1,0:T(8,128)(2,1)} %copy-done.10) | copy-start | bytes 3538948
  64.5 17.1 %copy-start.17 = (f32[128,128]{1,0:T(8,128)S(1)}, f32[128,128]{1,0:T(8,128)}, u32[]{:S(2)}) copy-start(f32[128,128]{1,0:T(8,128)} %copy-done.16) | copy-start | bytes 196612
  64.5 21.4 %collective-permute-start.10 = (f32[96,2048]{1,0:T(8,128)S(1)}, f32[96,2048]{1,0:T(8,128)S(1)}, u32[]{:S(2)}, u32[]{:S(2)}) collective-permute-start(f32[96,2048]{1,0:T(8,128)S(1)} %get-tuple-element.48), channel_id=1, source_target_pairs={{0,4},{1,5},{2,6},{3,7},{4,0},{5,1},{6,2},{7,3},{8,12},{9,13},{10,... | collective-permute-start | bytes 2359304 | tf_op jit(solution)/shard_map/ppermute | solution.py:332
  73.2 12.8 %collective-permute-start.21 = (f32[96,2048]{1,0:T(8,128)S(1)}, f32[96,2048]{1,0:T(8,128)S(1)}, u32[]{:S(2)}, u32[]{:S(2)}) collective-permute-start(f32[96,2048]{1,0:T(8,128)S(1)} %get-tuple-element.57), channel_id=1, source_target_pairs={{0,4},{1,5},{2,6},{3,7},{4,0},{5,1},{6,2},{7,3},{8,12},{9,13},{10,... | collective-permute-start | bytes 2359304 | tf_op jit(solution)/shard_map/ppermute | solution.py:332
  73.3 2.3 %collective-permute-start.22 = (bf16[192,128]{1,0:T(8,128)(2,1)S(1)}, bf16[192,128]{1,0:T(8,128)(2,1)S(1)}, u32[]{:S(2)}, u32[]{:S(2)}) collective-permute-start(bf16[192,128]{1,0:T(8,128)(2,1)S(1)} %collective-permute-done.17.refs_7_.refs_4_), channel_id=1, source_target_pairs={{0,4},{1,5},{2,6},{3,7},{4,0},{5,1},{6,2},{7,3},{8,12},{9,13},{10,... | collective-permute-start | bytes 147464 | tf_op jit(solution)/shard_map/ppermute | solution.py:332
  76.7 1.3 %collective-permute-start.24 = (f32[128,128]{1,0:T(8,128)S(1)}, f32[128,128]{1,0:T(8,128)S(1)}, u32[]{:S(2)}, u32[]{:S(2)}) collective-permute-start(f32[128,128]{1,0:T(8,128)S(1)} %get-tuple-element.63), channel_id=1, source_target_pairs={{0,4},{1,5},{2,6},{3,7},{4,0},{5,1},{6,2},{7,3},{8,12},{9,13},{10,... | collective-permute-start | bytes 196616 | tf_op jit(solution)/shard_map/ppermute | solution.py:332
  76.9 3.1 %collective-permute-start.23 = (f32[128,128]{1,0:T(8,128)S(1)}, f32[128,128]{1,0:T(8,128)S(1)}, u32[]{:S(2)}, u32[]{:S(2)}) collective-permute-start(f32[128,128]{1,0:T(8,128)S(1)} %copy-done.27), channel_id=1, source_target_pairs={{0,4},{1,5},{2,6},{3,7},{4,0},{5,1},{6,2},{7,3},{8,12},{9,13},{10,... | collective-permute-start | bytes 196616 | tf_op jit(solution)/shard_map/ppermute | solution.py:332
  78.0 6.7 %collective-permute-start.25 = (f32[128,128]{1,0:T(8,128)S(1)}, f32[128,128]{1,0:T(8,128)S(1)}, u32[]{:S(2)}, u32[]{:S(2)}) collective-permute-start(f32[128,128]{1,0:T(8,128)S(1)} %add.15.refs_8_), channel_id=1, source_target_pairs={{0,8},{1,9},{2,10},{3,11},{4,12},{5,13},{6,14},{7,15},{8,0},{9,1},... | collective-permute-start | bytes 196616 | tf_op jit(solution)/shard_map/ppermute | solution.py:332
  79.2 5.5 %collective-permute-start.26 = (f32[128,128]{1,0:T(8,128)S(1)}, f32[128,128]{1,0:T(8,128)S(1)}, u32[]{:S(2)}, u32[]{:S(2)}) collective-permute-start(f32[128,128]{1,0:T(8,128)S(1)} %add.15.refs_8_), channel_id=1, source_target_pairs={{0,16},{1,17},{2,18},{3,19},{4,20},{5,21},{6,22},{7,23},{8,24},{9,... | collective-permute-start | bytes 196616 | tf_op jit(solution)/shard_map/ppermute | solution.py:332
  80.0 5.2 %collective-permute-start.27 = (f32[128,128]{1,0:T(8,128)S(1)}, f32[128,128]{1,0:T(8,128)S(1)}, u32[]{:S(2)}, u32[]{:S(2)}) collective-permute-start(f32[128,128]{1,0:T(8,128)S(1)} %add.15.refs_8_), channel_id=1, source_target_pairs={{0,24},{1,25},{2,26},{3,27},{4,28},{5,29},{6,30},{7,31},{8,16},{9,... | collective-permute-start | bytes 196616 | tf_op jit(solution)/shard_map/ppermute | solution.py:332
  85.8 1.7 %collective-permute-start.28 = (f32[128,128]{1,0:T(8,128)S(1)}, f32[128,128]{1,0:T(8,128)S(1)}, u32[]{:S(2)}, u32[]{:S(2)}) collective-permute-start(f32[128,128]{1,0:T(8,128)S(1)} %get-tuple-element.68), channel_id=1, source_target_pairs={{0,4},{1,5},{2,6},{3,7},{4,0},{5,1},{6,2},{7,3},{8,12},{9,13},{10,... | collective-permute-start | bytes 196616 | tf_op jit(solution)/shard_map/ppermute | solution.py:332
  (10 other events, 7.1 us)

commit v16 on v15

--- a/solution.py
+++ b/solution.py
@@ -51,7 +51,7 @@
     return lambda ref, *_: ref.at[:, first : first + count]
 
 
-def call(body, outs, args, smem=(), after=(), room=2, flops=1):
+def call(body, outs, args, smem=(), after=(), room=2, flops=1, lazy=False):
     arrays, specs, scratch = [], [], []
     for arg in args:
         if isinstance(arg, tuple):
@@ -70,7 +70,7 @@
         scalars, refs = refs[: len(smem)], list(refs[len(smem) :])
         ins, refs = refs[: len(arrays)], refs[len(arrays) + len(after) :]
         results, slots = refs[: len(outs)], refs[len(outs) :]
-        given, started, slot = [], [], 0
+        given, started, slot, groups = [], [], 0, []
         for arg in args:
             if not isinstance(arg, tuple):
                 given.append(ins.pop(0))
@@ -84,9 +84,18 @@
                 copy.start()
                 started.append(copy)
             given.append(slots[slot])
+            groups.append(started[sum(len(group) for group in groups) :])
             slot += 1
-        for copy in started:
-            copy.wait()
+
+        def ready(n):
+            for copy in groups[n]:
+                copy.wait()
+
+        if lazy:
+            body(ready, *scalars, *given, *results)
+            return
+        for n in range(len(groups)):
+            ready(n)
         body(*scalars, *given, *results)
 
     moved = sum(a.size * a.dtype.itemsize for a in arrays)
@@ -214,8 +223,11 @@
     return jnp.concatenate([attn_ref[lax.rem(place - s + count, count)] for s in range(count)], 1)
 
 
-def first_kernel(spots, left_ref, weight_ref, right_ref, own_ref, half_ref):
+def first_kernel(ready, spots, left_ref, weight_ref, right_ref, own_ref, half_ref):
+    ready(0)
+    ready(1)
     own_ref[...] = dot(left_ref[...], weight_ref[...], NT).astype(BF16)
+    ready(2)
     near = left_ref[:, pl.ds(pl.multiple_of(spots[0], DH), right_ref.shape[1])]
     half_ref[...] = dot(near, right_ref[...], NT)
 
@@ -232,16 +244,20 @@
     out_ref[...] = (half_ref[...] + dot(left_ref[...], right_ref[...], NT)).astype(BF16)
 
 
-def near_kernel(spots, left_ref, right_ref, attn_ref, half_ref, own_out, mate_out):
-    half_ref[...] = dot(left_ref[...], right_ref[2 * DH : 3 * DH], NT)
-    far_kernel(spots, right_ref, attn_ref, own_out, mate_out)
-
-
-def far_kernel(spots, right_ref, attn_ref, own_out, mate_out):
-    own = own_out.shape[0]
-    part = dot(back_along(attn_ref, spots[3]), right_ref[...], NN)
-    own_out[...] = part[:own]
-    mate_out[...] = part[own:]
+def half_kernel(spots, left_ref, right_ref, half_ref):
+    half_ref[...] = dot(left_ref[...], right_ref[...], NT)
+
+
+def halves_kernel(ready, spots, attn_ref, *refs):
+    rights, outs = refs[:2], refs[2:]
+    own = outs[0].shape[0]
+    ready(0)
+    left = back_along(attn_ref, spots[3])
+    for n, right_ref in enumerate(rights):
+        ready(1 + n)
+        part = dot(left, right_ref[...], NN)
+        outs[2 * n][...] = part[:own]
+        outs[2 * n + 1][...] = part[own:]
 
 
 def grad_kernel(whole, added, places, mine_ref, mate_ref, *refs):
@@ -396,8 +412,6 @@
     linear = [keep, send(back, 1, 0)]
     if board:
         arrived[1], arrived[3] = hold([arrived[1], arrived[3]], [keep])
-    attn = lax.all_to_all(attn, "head", 0, 0, tiled=True)
-
     work = near_and_far if board else by_gathers
     both, across, joins, starts = work(
         attn, arrived, cotangent, mate_cotangent, out_weight, core, chip, colour, product
@@ -468,6 +482,7 @@
             fetch((2 * DH, wide), *stacked(arrived[1], arrived[3])),
         ],
         [spots],
+        lazy=True,
         room=6,
         flops=2 * product,
     )
@@ -487,23 +502,15 @@
     second[2] = [send(cuts[0], 2, 0), send(cuts[1], 4, 0)]
     both = {0: mine, 1: send(one, 0, -1), 3: send(three, 0, -3)}
     across = {s: send(both[s], 1, 0) for s in (0, 1, 3)}
-    half, part, mate_part = call(
-        near_kernel,
-        [((2 * own, DH), F32), *parts],
-        [
-            left[0],
-            fetch(
-                (4 * DH, wide),
-                (weight, own_columns(0), rows_at(0, DH)),
-                *((arrived[s], all_of, rows_at(s * DH, DH)) for s in (1, 2, 3)),
-            ),
-            attn,
-        ],
+    attn = lax.all_to_all(*hold([attn], [both[1], both[3]]), "head", 0, 0, tiled=True)
+    (half,) = call(
+        half_kernel,
+        [((2 * own, DH), F32)],
+        [left[0], fetch((DH, wide), (arrived[2], all_of, all_of))],
         [spots],
         room=6,
-        flops=2 * product,
-    )
-    joins = [part, send(mate_part, 1, 0)]
+        flops=product // 2,
+    )
     quarters = [(a, all_of, columns_at(n * wide // 2, wide // 2)) for n, a in enumerate(second[2])]
     (two,) = call(
         last_kernel,
@@ -519,10 +526,16 @@
     def quarter(n):
         return lambda ref, *_: ref.at[2 * DH : 3 * DH, n * wide // 2 : (n + 1) * wide // 2]
 
-    part, mate_part = call(
-        far_kernel,
-        parts,
+    parts = call(
+        halves_kernel,
+        parts * 2,
         [
+            fetch(attn.shape, (attn, all_of, all_of)),
+            fetch(
+                (4 * DH, wide),
+                (weight, own_columns(0), rows_at(0, DH)),
+                *((arrived[s], all_of, rows_at(s * DH, DH)) for s in (1, 2, 3)),
+            ),
             fetch(
                 (4 * DH, wide),
                 (weight, own_columns(1), rows_at(0, DH)),
@@ -530,14 +543,14 @@
                 (second[3], all_of, rows_at(3 * DH, DH)),
                 *((a, all_of, quarter(n)) for n, a in enumerate(second[2])),
             ),
-            attn,
         ],
         [spots],
         [both[2], across[0], across[1], across[3]],
-        room=6,
-        flops=2 * product,
-    )
-    joins += [part, send(mate_part, 1, 0)]
+        room=16,
+        flops=4 * product,
+        lazy=True,
+    )
+    joins = [parts[0], send(parts[1], 1, 0), parts[2], send(parts[3], 1, 0)]
     across[2] = send(both[2], 1, 0)
     return [both[s] for s in range(4)], [across[s] for s in range(4)], joins, [spots[0], spots[1]]
 
@@ -545,6 +558,7 @@
 def by_gathers(attn, arrived, cotangent, mate_cotangent, out_weight, core, chip, colour, product):
     own, model = cotangent.shape
     shards, count = lax.axis_size("ctx"), lax.axis_size("head")
+    attn = lax.all_to_all(attn, "head", 0, 0, tiled=True)
     weight = lax.dynamic_slice_in_dim(out_weight, core * DH, DH, 0)
     zero = jnp.zeros((1,), jnp.int32)
     groups = [list(range(k, shards, 2)) for k in range(2)]

time: 90 us -> 106 us (1.18)
  local copies, waits for them, and re-layouts: 15.2 us -> 27.4 us
  starting transfers between devices: 25.5 us -> 28.9 us
  Pallas kernels: 26.3 us -> 23.1 us
  waiting for transfers between devices: 18.8 us -> 21.9 us
    unnamed x56 -> x92, local copies, waits for them, and re-layouts: 13.3 us -> 25.5 us
    ppermute x29, starting transfers between devices: 21.5 us -> 24.7 us  [send(): return lax.ppermute(x, ('ctx', 'head'), pairs)]
    pallas_call x12, Pallas kernels: 26.3 us -> 23.1 us  [call(): pl.pallas_call(kernel, out_shape=[jax.ShapeDtypeStruct(s, t) for s, t in...]
    ppermute x29, waiting for transfers between devices: 18.8 us -> 21.9 us  [send(): return lax.ppermute(x, ('ctx', 'head'), pairs)]
  transfers between devices with their start and end apart: 30 -> 30, of which waited for: 9 -> 11; matrix products, arithmetic and copies ran while one was open for 5% -> 4% of each run, Pallas kernels for 28% -> 15%
where the time goes in v16:
time: 106 us; the launch traced here: 105 us
  starting transfers between devices  28.9 us (27%)
  local copies, waits for them, and re-layouts  27.4 us (26%)
  Pallas kernels  23.1 us (22%)
  waiting for transfers between devices  21.9 us (21%)
  other arithmetic  2.45 us (2%)
    unnamed x92, local copies, waits for them, and re-layouts  25.5 us
    ppermute x29, starting transfers between devices, send(): return lax.ppermute(x, ('ctx', 'head'), pairs)  24.7 us
    pallas_call x12, Pallas kernels, call(): pl.pallas_call(kernel, out_shape=[jax.ShapeDtypeStruct(s, t) for s, t in...  23.1 us
    ppermute x29, waiting for transfers between devices, send(): return lax.ppermute(x, ('ctx', 'head'), pairs)  21.9 us
    all_to_all x1, starting transfers between devices, near_and_far(): lax.all_to_all(*hold([attn], [both[1], both[3]]), 'head', 0, 0, tiled=True)  4.14 us
  transfers between devices with their start and end apart: 30, of which 11 were waited for; matrix products, arithmetic and copies ran while one was open for 4% of the time, Pallas kernels for 15%

profile of v16, /device:TPU:0, one launch (start us, length us, event | category | flops | bytes accessed | tf_op | source)
XLA Modules:
  0.0 104.6 jit_solution(7326966156136422317)
XLA Ops:
  1.2 1.9 %dynamic_slice.3 = bf16[128,2048]{1,0:T(8,128)(2,1)} dynamic-slice(bf16[256,4096]{1,0:T(8,128)(2,1)} %refs_6_.1, s32[]{:T(128)S(6)} %select_n.6, s32[]{:T(128)S(6)} %select_n.7), dynamic_slice_sizes={128,2048} | dynamic-slice | bytes 1048580 | tf_op jit(solution)/shard_map/dynamic_slice | solution.py:388
  3.0 2.6 %collective-permute-start.7 = (bf16[128,2048]{1,0:T(8,128)(2,1)}, bf16[128,2048]{1,0:T(8,128)(2,1)S(1)}, u32[]{:S(2)}, u32[]{:S(2)}) collective-permute-start(bf16[128,2048]{1,0:T(8,128)(2,1)} %dynamic_slice.3), channel_id=1, source_target_pairs={{0,1},{1,2},{2,3},{3,0},{4,5},{5,6},{6,7},{7,4},{8,9},{9,10},{10,1... | collective-permute-start | bytes 1572872 | tf_op jit(solution)/shard_map/ppermute | solution.py:348
  5.7 2.0 %collective-permute-start.8 = (bf16[128,2048]{1,0:T(8,128)(2,1)}, bf16[128,2048]{1,0:T(8,128)(2,1)}, u32[]{:S(2)}, u32[]{:S(2)}) collective-permute-start(bf16[128,2048]{1,0:T(8,128)(2,1)} %dynamic_slice.3), channel_id=1, source_target_pairs={{0,3},{1,0},{2,1},{3,2},{4,7},{5,4},{6,5},{7,6},{8,11},{9,8},{10,9... | collective-permute-start | bytes 1572872 | tf_op jit(solution)/shard_map/ppermute | solution.py:348
  7.8 1.2 %pad_maximum_fusion.refs_2_ = bf16[3,384,256]{2,1,0:T(8,128)(2,1)S(1)} fusion(bf16[1,384,256]{2,1,0:T(8,128)(2,1)} %bitcast.18, bf16[1,384,256]{2,1,0:T(8,128)(2,1)} %bitcast.19, bf16[1,384,256]{2,1,0:T(8,128)(2,1)} %bitcast.17), kind=kLoop, calls=%fused_computation | loop fusion | flops 589824 | bytes 1179648 | tf_op jit(solution)/shard_map/stack | solution.py:398
  9.0 2.6 %shard_map.93 = (bf16[4,384,384]{2,1,0:T(8,128)(2,1)S(1)}, f32[384,128]{1,0:T(8,128)S(1)}, f32[384,128]{1,0:T(8,128)}, bf16[384,128]{1,0:T(8,128)(2,1)}, f32[128,128]{1,0:T(8,128)S(1)}, /*index=5*/f32[128,128]{1,0:T(8,128)}) custom-call(s32[3,3]{1,0:T(4,128)S(1)} %copy-done.44, s32[3]{0:T(128)S(1)} %pad_add_fusion.2.refs_1_.refs_0_, ...), custom_call_target="tpu_custom_call" | custom-call | flops 264241152 | bytes 2392064 | tf_op jit(solution)/shard_map/pallas_call | solution.py:103
  11.5 1.0 copy-done.16
  14.5 1.1 %collective-permute-done.1.refs_1_.refs_8_ = bf16[384,128]{1,0:T(8,128)(2,1)S(1)} collective-permute-done((bf16[384,128]{1,0:T(8,128)(2,1)}, bf16[384,128]{1,0:T(8,128)(2,1)S(1)}, u32[]{:S(2)}, u32[]{:S(2)}) %collective-permute-start.1) | collective-permute-done | bytes 98336 | tf_op jit(solution)/shard_map/ppermute | solution.py:348
  16.3 0.9 add.12
  17.2 1.7 %collective-permute-start.4 = (f32[128,128]{1,0:T(8,128)S(1)}, f32[128,128]{1,0:T(8,128)S(1)}, u32[]{:S(2)}, u32[]{:S(2)}) collective-permute-start(f32[128,128]{1,0:T(8,128)S(1)} %add.12), channel_id=1, source_target_pairs={{0,8},{1,9},{2,10},{3,11},{4,12},{5,13},{6,14},{7,15},{8,0},{9,1},... | collective-permute-start | bytes 196616 | tf_op jit(solution)/shard_map/ppermute | solution.py:348
  18.9 1.5 %collective-permute-start.5 = (f32[128,128]{1,0:T(8,128)S(1)}, f32[128,128]{1,0:T(8,128)S(1)}, u32[]{:S(2)}, u32[]{:S(2)}) collective-permute-start(f32[128,128]{1,0:T(8,128)S(1)} %add.12), channel_id=1, source_target_pairs={{0,16},{1,17},{2,18},{3,19},{4,20},{5,21},{6,22},{7,23},{8,24},{9,... | collective-permute-start | bytes 196616 | tf_op jit(solution)/shard_map/ppermute | solution.py:348
  21.5 1.6 %collective-permute-done.5.refs_5_ = f32[128,128]{1,0:T(8,128)S(1)} collective-permute-done((f32[128,128]{1,0:T(8,128)S(1)}, f32[128,128]{1,0:T(8,128)S(1)}, u32[]{:S(2)}, u32[]{:S(2)}) %collective-permute-start.5) | collective-permute-done | bytes 65568 | tf_op jit(solution)/shard_map/ppermute | solution.py:348
  23.2 2.4 %collective-permute-done.6.refs_6_ = f32[128,128]{1,0:T(8,128)S(1)} collective-permute-done((f32[128,128]{1,0:T(8,128)S(1)}, f32[128,128]{1,0:T(8,128)S(1)}, u32[]{:S(2)}, u32[]{:S(2)}) %collective-permute-start.6) | collective-permute-done | bytes 65568 | tf_op jit(solution)/shard_map/ppermute | solution.py:348
  25.6 0.9 copy-done.9
  26.5 0.8 copy-done.20
  27.4 0.9 copy-done.26
  28.2 0.9 copy-done.34
  29.2 1.2 %shard_map.95 = (bf16[4,192,128]{2,1,0:T(8,128)(2,1)S(1)}, f32[128,128]{1,0:T(8,128)S(1)}, f32[128,128]{1,0:T(8,128)S(1)}) custom-call(s32[4]{0:T(128)S(1)} %add_convert_fusion.refs_0_, s32[3]{0:T(128)S(1)} %pad_add_fusion.2.refs_1_.refs_0_, f32[128,128]{1,0:T(8,128)S(1)} %copy-done.20, f32[128,128]{1,0:T(8,128)} %collective-permute-done.3.refs_3_, ...), custom_call_target="tpu_custom_call" | custom-call | flops 1 | bytes 1343488 | tf_op jit(solution)/shard_map/pallas_call | solution.py:103
  31.8 0.8 copy-done.3
  33.9 1.5 %collective-permute-start.9 = (bf16[128,2048]{1,0:T(8,128)(2,1)}, bf16[128,2048]{1,0:T(8,128)(2,1)}, u32[]{:S(2)}, u32[]{:S(2)}) collective-permute-start(bf16[128,2048]{1,0:T(8,128)(2,1)} %get-tuple-element.44.refs_4_.refs_3_), channel_id=1, source_target_pairs={{0,8},{1,9},{2,10},{3,11},{4,12},{5,13},{6,14},{7,15},{8,0},{9,1},... | collective-permute-start | bytes 1572872 | tf_op jit(solution)/shard_map/ppermute | solution.py:348
  35.4 1.1 %copy-done.1 = bf16[96,4096]{1,0:T(8,128)(2,1)S(1)} copy-done((bf16[96,4096]{1,0:T(8,128)(2,1)S(1)}, bf16[96,4096]{1,0:T(8,128)(2,1)}, u32[]{:S(2)}) %copy-start.1) | copy-done | bytes 786456
  36.6 1.0 copy-done.4
  37.6 2.6 %shard_map.97 = (bf16[192,128]{1,0:T(8,128)(2,1)S(1)}, f32[192,256]{1,0:T(8,128)S(1)}) custom-call(s32[4]{0:T(128)S(1)} %pad_add_fusion.1.refs_0_, bf16[96,4096]{1,0:T(8,128)(2,1)S(1)} %copy-done.1, bf16[96,4096]{1,0:T(8,128)(2,1)S(1)} %collective-permute-done.refs_3_.refs_2_, bf16[256,4096]{1,0:T(8,128)(2,1)S(1)} %copy-done, ...), custom_call_target="tpu_custom_call" | custom-call | flops 402653184 | bytes 4964352 | tf_op jit(solution)/shard_map/pallas_call | solution.py:103
  40.2 5.2 %collective-permute-done.10.refs_4_.refs_8_ = bf16[128,2048]{1,0:T(8,128)(2,1)} collective-permute-done((bf16[128,2048]{1,0:T(8,128)(2,1)}, bf16[128,2048]{1,0:T(8,128)(2,1)}, u32[]{:S(2)}, u32[]{:S(2)}) %collective-permute-start.10) | collective-permute-done | bytes 524320 | tf_op jit(solution)/shard_map/ppermute | solution.py:348
  45.3 2.4 %collective-permute-done.11.refs_6_.refs_3_.refs_4_ = bf16[128,2048]{1,0:T(8,128)(2,1)S(1)} collective-permute-done((bf16[128,2048]{1,0:T(8,128)(2,1)}, bf16[128,2048]{1,0:T(8,128)(2,1)S(1)}, u32[]{:S(2)}, u32[]{:S(2)}) %collective-permute-start.11) | collective-permute-done | bytes 524320 | tf_op jit(solution)/shard_map/ppermute | solution.py:348
  47.8 3.0 %shard_map.98 = (bf16[192,128]{1,0:T(8,128)(2,1)S(1)}, bf16[192,128]{1,0:T(8,128)(2,1)S(1)}, bf16[128,1024]{1,0:T(8,128)(2,1)}, bf16[128,1024]{1,0:T(8,128)(2,1)}) custom-call(s32[4]{0:T(128)S(1)} %pad_add_fusion.1.refs_0_, bf16[96,4096]{1,0:T(8,128)(2,1)S(1)} %copy-done.1, bf16[96,4096]{1,0:T(8,128)(2,1)S(1)} %collective-permute-done.refs_3_.refs_2_, ...), custom_call_target="tpu_custom_call" | custom-call | flops 201326592 | bytes 3964928 | tf_op jit(solution)/shard_map/pallas_call | solution.py:103
  50.9 1.9 %collective-permute-start.12 = (bf16[192,128]{1,0:T(8,128)(2,1)S(1)}, bf16[192,128]{1,0:T(8,128)(2,1)S(1)}, u32[]{:S(2)}, u32[]{:S(2)}) collective-permute-start(bf16[192,128]{1,0:T(8,128)(2,1)S(1)} %get-tuple-element.47), channel_id=1, source_target_pairs={{0,3},{1,0},{2,1},{3,2},{4,7},{5,4},{6,5},{7,6},{8,11},{9,8},{10,9... | collective-permute-start | bytes 147464 | tf_op jit(solution)/shard_map/ppermute | solution.py:348
  52.9 1.5 %collective-permute-start.14 = (bf16[128,1024]{1,0:T(8,128)(2,1)}, bf16[128,1024]{1,0:T(8,128)(2,1)}, u32[]{:S(2)}, u32[]{:S(2)}) collective-permute-start(bf16[128,1024]{1,0:T(8,128)(2,1)} %get-tuple-element.49), channel_id=1, source_target_pairs={{0,8},{1,9},{2,10},{3,11},{4,12},{5,13},{6,14},{7,15},{8,0},{9,1},... | collective-permute-start | bytes 786440 | tf_op jit(solution)/shard_map/ppermute | solution.py:348
  55.5 3.1 %collective-permute-done.13.refs_2_.refs_7_.refs_5_ = bf16[192,128]{1,0:T(8,128)(2,1)S(1)} collective-permute-done((bf16[192,128]{1,0:T(8,128)(2,1)S(1)}, bf16[192,128]{1,0:T(8,128)(2,1)S(1)}, u32[]{:S(2)}, u32[]{:S(2)}) %collective-permute-start.13) | collective-permute-done | bytes 49184 | tf_op jit(solution)/shard_map/ppermute | solution.py:348
  59.3 4.1 %all-to-all-start = ((bf16[4,192,128]{2,1,0:T(8,128)(2,1)}), bf16[4,192,128]{2,1,0:T(8,128)(2,1)}, u32[]{:S(2)}, u32[]{:S(2)}) async-start(bf16[4,192,128]{2,1,0:T(8,128)(2,1)} %shard_map.99), calls=%async_computation | async-start | bytes 393216 | tf_op jit(solution)/shard_map/all_to_all | solution.py:505
  63.5 1.1 %copy-done.2 = bf16[96,4096]{1,0:T(8,128)(2,1)S(1)} copy-done((bf16[96,4096]{1,0:T(8,128)(2,1)S(1)}, bf16[96,4096]{1,0:T(8,128)(2,1)}, u32[]{:S(2)}) %copy-start.2) | copy-done | bytes 786456
  64.6 1.0 copy-done.7
  66.3 1.0 shard_map.100.refs_5_
  68.0 2.0 %shard_map.101 = bf16[192,128]{1,0:T(8,128)(2,1)S(1)} custom-call(s32[4]{0:T(128)S(1)} %copy-done.42, bf16[96,4096]{1,0:T(8,128)(2,1)S(1)} %copy-done.2, bf16[96,4096]{1,0:T(8,128)(2,1)S(1)} %collective-permute-done.refs_3_.refs_2_, bf16[128,1024]{1,0:T(8,128)(2,1)} %collective-permute-done.14.refs_3_.refs_9_, ...), custom_call_target="tpu_custom_call" | custom-call | flops 100663296 | bytes 2244608 | tf_op jit(solution)/shard_map/pallas_call | solution.py:103
  70.1 2.9 %collective-permute-start.16 = (bf16[192,128]{1,0:T(8,128)(2,1)S(1)}, bf16[192,128]{1,0:T(8,128)(2,1)S(1)}, u32[]{:S(2)}, u32[]{:S(2)}) collective-permute-start(bf16[192,128]{1,0:T(8,128)(2,1)S(1)} %shard_map.101), channel_id=1, source_target_pairs={{0,2},{1,3},{2,0},{3,1},{4,6},{5,7},{6,4},{7,5},{8,10},{9,11},{10,... | collective-permute-start | bytes 147464 | tf_op jit(solution)/shard_map/ppermute | solution.py:348
  74.2 1.1 %collective-permute-done.16.refs_11_.refs_4_ = bf16[192,128]{1,0:T(8,128)(2,1)S(1)} collective-permute-done((bf16[192,128]{1,0:T(8,128)(2,1)S(1)}, bf16[192,128]{1,0:T(8,128)(2,1)S(1)}, u32[]{:S(2)}, u32[]{:S(2)}) %collective-permute-start.16) | collective-permute-done | bytes 49184 | tf_op jit(solution)/shard_map/ppermute | solution.py:348
  75.3 1.0 copy-done.8
  78.5 3.0 %shard_map.102 = (f32[96,2048]{1,0:T(8,128)S(1)}, f32[96,2048]{1,0:T(8,128)S(1)}, f32[96,2048]{1,0:T(8,128)S(1)}, f32[96,2048]{1,0:T(8,128)S(1)}) custom-call(s32[4]{0:T(128)S(1)} %copy-done.43, bf16[4,192,128]{2,1,0:T(8,128)(2,1)} %all-to-all-done.refs_1_, bf16[256,4096]{1,0:T(8,128)(2,1)S(1)} %copy-done, bf16[128,2048]{1,0:T(8,128)(2,1)S(1)} %copy-done.5, ...), custom_call_target="tpu_custom_call" | custom-call | flops 805306368 | bytes 10682368 | tf_op jit(solution)/shard_map/pallas_call | solution.py:103
  82.2 2.9 %collective-permute-done.22.refs_8_ = bf16[192,128]{1,0:T(8,128)(2,1)S(1)} collective-permute-done((bf16[192,128]{1,0:T(8,128)(2,1)S(1)}, bf16[192,128]{1,0:T(8,128)(2,1)S(1)}, u32[]{:S(2)}, u32[]{:S(2)}) %collective-permute-start.22) | collective-permute-done | bytes 49184 | tf_op jit(solution)/shard_map/ppermute | solution.py:348
  85.1 0.9 copy-done.10
  89.6 1.6 %collective-permute-start.25 = (f32[128,128]{1,0:T(8,128)S(1)}, f32[128,128]{1,0:T(8,128)S(1)}, u32[]{:S(2)}, u32[]{:S(2)}) collective-permute-start(f32[128,128]{1,0:T(8,128)S(1)} %add.15.refs_8_), channel_id=1, source_target_pairs={{0,8},{1,9},{2,10},{3,11},{4,12},{5,13},{6,14},{7,15},{8,0},{9,1},... | collective-permute-start | bytes 196616 | tf_op jit(solution)/shard_map/ppermute | solution.py:348
  91.7 1.5 %collective-permute-start.27 = (f32[128,128]{1,0:T(8,128)S(1)}, f32[128,128]{1,0:T(8,128)S(1)}, u32[]{:S(2)}, u32[]{:S(2)}) collective-permute-start(f32[128,128]{1,0:T(8,128)S(1)} %add.15.refs_8_), channel_id=1, source_target_pairs={{0,24},{1,25},{2,26},{3,27},{4,28},{5,29},{6,30},{7,31},{8,16},{9,... | collective-permute-start | bytes 196616 | tf_op jit(solution)/shard_map/ppermute | solution.py:348
  93.3 0.9 copy-done.11
  94.2 0.9 copy-done.12
  95.1 0.9 copy-done.14
  96.0 0.8 copy-done.28
  97.6 3.0 %shard_map.105 = (bf16[384,256]{1,0:T(8,128)(2,1)}, f32[384,256]{1,0:T(8,128)S(1)}, f32[384,256]{1,0:T(8,128)S(1)}) custom-call(s32[3]{0:T(128)S(1)} %copy-done.39, bf16[384,256]{1,0:T(8,128)(2,1)S(1)} %copy-done.11, bf16[384,256]{1,0:T(8,128)(2,1)S(1)} %copy-done.14, bf16[384,256]{1,0:T(8,128)(2,1)S(1)} %copy-done.12, ...), custom_call_target="tpu_custom_call" | custom-call | flops 528482304 | bytes 3080192 | tf_op jit(solution)/shard_map/pallas_call | solution.py:103
  101.3 1.6 %shard_map.103 = (bf16[96,4096]{1,0:T(8,128)(2,1)}, f32[8,128]{1,0:T(8,128)S(1)}) custom-call(s32[2]{0:T(128)S(1)} %pad_add_fusion.refs_0_, f32[96,2048]{1,0:T(8,128)S(1)} %get-tuple-element.52.refs_1_, f32[96,2048]{1,0:T(8,128)S(1)} %collective-permute-done.20.refs_2_, f32[96,2048]{1,0:T(8,128)S(1)} %get-tuple-element.54.refs_3_, ...), custom_call_target="tpu_custom_call" | custom-call | flops 1 | bytes 3936256 | tf_op jit(solution)/shard_map/pallas_call | solution.py:103
  103.0 1.6 %shard_map.107 = (bf16[384,256]{1,0:T(8,128)(2,1)}, bf16[384,256]{1,0:T(8,128)(2,1)}) custom-call(s32[3]{0:T(128)S(1)} %copy-done.39, bf16[384,256]{1,0:T(8,128)(2,1)S(1)} %copy-done.15, bf16[384,256]{1,0:T(8,128)(2,1)S(1)} %copy-done.13, f32[384,256]{1,0:T(8,128)S(1)} %get-tuple-element.63.refs_6_.refs_3_, f32[384,256]{1,0:T(8,128)S(1)} %get-tuple-element.64.refs_4_, ...), custom_call_target="tpu_custom_call" | custom-call | flops 1 | bytes 1703936 | tf_op jit(solution)/shard_map/pallas_call | solution.py:103
  (128 shorter events, 20.1 us)
Async XLA Ops:
  0.6 8.3 %copy-start.44 = (s32[3,3]{1,0:T(4,128)S(1)}, s32[3,3]{1,0:T(4,128)}, u32[]{:S(2)}) copy-start(s32[3,3]{1,0:T(4,128)} %refs_0_.1) | copy-start | bytes 112
  0.6 8.3 %collective-permute-start = (bf16[96,4096]{1,0:T(8,128)(2,1)}, bf16[96,4096]{1,0:T(8,128)(2,1)S(1)}, u32[]{:S(2)}, u32[]{:S(2)}) collective-permute-start(bf16[96,4096]{1,0:T(8,128)(2,1)} %refs_1_.10), channel_id=1, source_target_pairs={{0,4},{1,5},{2,6},{3,7},{4,0},{5,1},{6,2},{7,3},{8,12},{9,13},{10,... | collective-permute-start | bytes 2359304 | tf_op jit(solution)/shard_map/ppermute | solution.py:348
  3.0 28.7 %collective-permute-start.7 = (bf16[128,2048]{1,0:T(8,128)(2,1)}, bf16[128,2048]{1,0:T(8,128)(2,1)S(1)}, u32[]{:S(2)}, u32[]{:S(2)}) collective-permute-start(bf16[128,2048]{1,0:T(8,128)(2,1)} %dynamic_slice.3), channel_id=1, source_target_pairs={{0,1},{1,2},{2,3},{3,0},{4,5},{5,6},{6,7},{7,4},{8,9},{9,10},{10,1... | collective-permute-start | bytes 1572872 | tf_op jit(solution)/shard_map/ppermute | solution.py:348
  5.7 26.1 %collective-permute-start.8 = (bf16[128,2048]{1,0:T(8,128)(2,1)}, bf16[128,2048]{1,0:T(8,128)(2,1)}, u32[]{:S(2)}, u32[]{:S(2)}) collective-permute-start(bf16[128,2048]{1,0:T(8,128)(2,1)} %dynamic_slice.3), channel_id=1, source_target_pairs={{0,3},{1,0},{2,1},{3,2},{4,7},{5,4},{6,5},{7,6},{8,11},{9,8},{10,9... | collective-permute-start | bytes 1572872 | tf_op jit(solution)/shard_map/ppermute | solution.py:348
  7.8 22.7 %copy-start.37 = (s32[3]{0:T(128)}, s32[3]{0:T(128)S(1)}, u32[]{:S(2)}) copy-start(s32[3]{0:T(128)S(1)} %pad_add_fusion.2.refs_1_.refs_0_) | copy-start | bytes 40
  8.9 26.5 %copy-start = (bf16[256,4096]{1,0:T(8,128)(2,1)S(1)}, bf16[256,4096]{1,0:T(8,128)(2,1)}, u32[]{:S(2)}) copy-start(bf16[256,4096]{1,0:T(8,128)(2,1)} %refs_6_.1) | copy-start | bytes 6291460
  13.8 1.8 %collective-permute-start.2 = (f32[384,128]{1,0:T(8,128)}, f32[384,128]{1,0:T(8,128)}, u32[]{:S(2)}, u32[]{:S(2)}) collective-permute-start(f32[384,128]{1,0:T(8,128)} %get-tuple-element.39), channel_id=1, source_target_pairs={{0,4},{1,5},{2,6},{3,7},{4,0},{5,1},{6,2},{7,3},{8,12},{9,13},{10,... | collective-permute-start | bytes 589832 | tf_op jit(solution)/shard_map/ppermute | solution.py:348
  14.0 1.6 %collective-permute-start.1 = (bf16[384,128]{1,0:T(8,128)(2,1)}, bf16[384,128]{1,0:T(8,128)(2,1)S(1)}, u32[]{:S(2)}, u32[]{:S(2)}) collective-permute-start(bf16[384,128]{1,0:T(8,128)(2,1)} %get-tuple-element.38), channel_id=1, source_target_pairs={{0,4},{1,5},{2,6},{3,7},{4,0},{5,1},{6,2},{7,3},{8,12},{9,13},{10,... | collective-permute-start | bytes 294920 | tf_op jit(solution)/shard_map/ppermute | solution.py:348
  14.4 1.9 %collective-permute-start.3 = (f32[128,128]{1,0:T(8,128)}, f32[128,128]{1,0:T(8,128)}, u32[]{:S(2)}, u32[]{:S(2)}) collective-permute-start(f32[128,128]{1,0:T(8,128)} %get-tuple-element.40), channel_id=1, source_target_pairs={{0,4},{1,5},{2,6},{3,7},{4,0},{5,1},{6,2},{7,3},{8,12},{9,13},{10,... | collective-permute-start | bytes 196616 | tf_op jit(solution)/shard_map/ppermute | solution.py:348
  17.2 4.4 %collective-permute-start.4 = (f32[128,128]{1,0:T(8,128)S(1)}, f32[128,128]{1,0:T(8,128)S(1)}, u32[]{:S(2)}, u32[]{:S(2)}) collective-permute-start(f32[128,128]{1,0:T(8,128)S(1)} %add.12), channel_id=1, source_target_pairs={{0,8},{1,9},{2,10},{3,11},{4,12},{5,13},{6,14},{7,15},{8,0},{9,1},... | collective-permute-start | bytes 196616 | tf_op jit(solution)/shard_map/ppermute | solution.py:348
  18.9 4.3 %collective-permute-start.5 = (f32[128,128]{1,0:T(8,128)S(1)}, f32[128,128]{1,0:T(8,128)S(1)}, u32[]{:S(2)}, u32[]{:S(2)}) collective-permute-start(f32[128,128]{1,0:T(8,128)S(1)} %add.12), channel_id=1, source_target_pairs={{0,16},{1,17},{2,18},{3,19},{4,20},{5,21},{6,22},{7,23},{8,24},{9,... | collective-permute-start | bytes 196616 | tf_op jit(solution)/shard_map/ppermute | solution.py:348
  20.4 5.2 %collective-permute-start.6 = (f32[128,128]{1,0:T(8,128)S(1)}, f32[128,128]{1,0:T(8,128)S(1)}, u32[]{:S(2)}, u32[]{:S(2)}) collective-permute-start(f32[128,128]{1,0:T(8,128)S(1)} %add.12), channel_id=1, source_target_pairs={{0,24},{1,25},{2,26},{3,27},{4,28},{5,29},{6,30},{7,31},{8,16},{9,... | collective-permute-start | bytes 196616 | tf_op jit(solution)/shard_map/ppermute | solution.py:348
  31.7 19.1 %copy-start.45 = (f32[128,128]{1,0:T(8,128)}, f32[128,128]{1,0:T(8,128)S(1)}, u32[]{:S(2)}) copy-start(f32[128,128]{1,0:T(8,128)S(1)} %get-tuple-element.59) | copy-start | bytes 196612
  32.6 12.8 %collective-permute-start.10 = (bf16[128,2048]{1,0:T(8,128)(2,1)}, bf16[128,2048]{1,0:T(8,128)(2,1)}, u32[]{:S(2)}, u32[]{:S(2)}) collective-permute-start(bf16[128,2048]{1,0:T(8,128)(2,1)} %get-tuple-element.45.refs_5_), channel_id=1, source_target_pairs={{0,16},{1,17},{2,18},{3,19},{4,20},{5,21},{6,22},{7,23},{8,24},{9,... | collective-permute-start | bytes 1572872 | tf_op jit(solution)/shard_map/ppermute | solution.py:348
  33.1 14.7 %collective-permute-start.11 = (bf16[128,2048]{1,0:T(8,128)(2,1)}, bf16[128,2048]{1,0:T(8,128)(2,1)S(1)}, u32[]{:S(2)}, u32[]{:S(2)}) collective-permute-start(bf16[128,2048]{1,0:T(8,128)(2,1)} %get-tuple-element.44.refs_4_.refs_3_), channel_id=1, source_target_pairs={{0,1},{1,2},{2,3},{3,0},{4,5},{5,6},{6,7},{7,4},{8,9},{9,10},{10,1... | collective-permute-start | bytes 1572872 | tf_op jit(solution)/shard_map/ppermute | solution.py:348
  33.9 13.9 %collective-permute-start.9 = (bf16[128,2048]{1,0:T(8,128)(2,1)}, bf16[128,2048]{1,0:T(8,128)(2,1)}, u32[]{:S(2)}, u32[]{:S(2)}) collective-permute-start(bf16[128,2048]{1,0:T(8,128)(2,1)} %get-tuple-element.44.refs_4_.refs_3_), channel_id=1, source_target_pairs={{0,8},{1,9},{2,10},{3,11},{4,12},{5,13},{6,14},{7,15},{8,0},{9,1},... | collective-permute-start | bytes 1572872 | tf_op jit(solution)/shard_map/ppermute | solution.py:348
  35.4 1.1 %copy-start.1 = (bf16[96,4096]{1,0:T(8,128)(2,1)S(1)}, bf16[96,4096]{1,0:T(8,128)(2,1)}, u32[]{:S(2)}) copy-start(bf16[96,4096]{1,0:T(8,128)(2,1)} %refs_1_.10) | copy-start | bytes 2359300
  37.6 10.2 %copy-start.40 = (s32[4]{0:T(128)}, s32[4]{0:T(128)S(1)}, u32[]{:S(2)}) copy-start(s32[4]{0:T(128)S(1)} %pad_add_fusion.1.refs_0_) | copy-start | bytes 52
  40.2 7.6 %copy-start.35 = (bf16[192,128]{1,0:T(8,128)(2,1)}, bf16[192,128]{1,0:T(8,128)(2,1)S(1)}, u32[]{:S(2)}) copy-start(bf16[192,128]{1,0:T(8,128)(2,1)S(1)} %get-tuple-element.51.refs_2_) | copy-start | bytes 147460
  47.8 11.5 %copy-start.6 = (bf16[128,2048]{1,0:T(8,128)(2,1)}, bf16[128,2048]{1,0:T(8,128)(2,1)S(1)}, u32[]{:S(2)}) copy-start(bf16[128,2048]{1,0:T(8,128)(2,1)S(1)} %collective-permute-done.11.refs_6_.refs_3_.refs_4_) | copy-start | bytes 1572868
  50.9 4.7 %collective-permute-start.12 = (bf16[192,128]{1,0:T(8,128)(2,1)S(1)}, bf16[192,128]{1,0:T(8,128)(2,1)S(1)}, u32[]{:S(2)}, u32[]{:S(2)}) collective-permute-start(bf16[192,128]{1,0:T(8,128)(2,1)S(1)} %get-tuple-element.47), channel_id=1, source_target_pairs={{0,3},{1,0},{2,1},{3,2},{4,7},{5,4},{6,5},{7,6},{8,11},{9,8},{10,9... | collective-permute-start | bytes 147464 | tf_op jit(solution)/shard_map/ppermute | solution.py:348
  52.7 5.9 %collective-permute-start.13 = (bf16[192,128]{1,0:T(8,128)(2,1)S(1)}, bf16[192,128]{1,0:T(8,128)(2,1)S(1)}, u32[]{:S(2)}, u32[]{:S(2)}) collective-permute-start(bf16[192,128]{1,0:T(8,128)(2,1)S(1)} %get-tuple-element.48), channel_id=1, source_target_pairs={{0,1},{1,2},{2,3},{3,0},{4,5},{5,6},{6,7},{7,4},{8,9},{9,10},{10,1... | collective-permute-start | bytes 147464 | tf_op jit(solution)/shard_map/ppermute | solution.py:348
  52.9 15.1 %collective-permute-start.14 = (bf16[128,1024]{1,0:T(8,128)(2,1)}, bf16[128,1024]{1,0:T(8,128)(2,1)}, u32[]{:S(2)}, u32[]{:S(2)}) collective-permute-start(bf16[128,1024]{1,0:T(8,128)(2,1)} %get-tuple-element.49), channel_id=1, source_target_pairs={{0,8},{1,9},{2,10},{3,11},{4,12},{5,13},{6,14},{7,15},{8,0},{9,1},... | collective-permute-start | bytes 786440 | tf_op jit(solution)/shard_map/ppermute | solution.py:348
  54.4 13.6 %collective-permute-start.15 = (bf16[128,1024]{1,0:T(8,128)(2,1)}, bf16[128,1024]{1,0:T(8,128)(2,1)}, u32[]{:S(2)}, u32[]{:S(2)}) collective-permute-start(bf16[128,1024]{1,0:T(8,128)(2,1)} %get-tuple-element.50), channel_id=1, source_target_pairs={{0,16},{1,17},{2,18},{3,19},{4,20},{5,21},{6,22},{7,23},{8,24},{9,... | collective-permute-start | bytes 786440 | tf_op jit(solution)/shard_map/ppermute | solution.py:348
  55.5 3.1 %copy-start.21 = (bf16[192,128]{1,0:T(8,128)(2,1)}, bf16[192,128]{1,0:T(8,128)(2,1)S(1)}, u32[]{:S(2)}) copy-start(bf16[192,128]{1,0:T(8,128)(2,1)S(1)} %collective-permute-done.12.refs_1_.refs_6_.refs_3_) | copy-start | bytes 147460
  59.3 8.1 %copy-start.22 = (bf16[192,128]{1,0:T(8,128)(2,1)S(1)}, bf16[192,128]{1,0:T(8,128)(2,1)}, u32[]{:S(2)}) copy-start(bf16[192,128]{1,0:T(8,128)(2,1)} %copy-done.21) | copy-start | bytes 147460
  59.3 8.7 %copy-start.24 = (bf16[192,128]{1,0:T(8,128)(2,1)S(1)}, bf16[192,128]{1,0:T(8,128)(2,1)}, u32[]{:S(2)}) copy-start(bf16[192,128]{1,0:T(8,128)(2,1)} %copy-done.23) | copy-start | bytes 147460
  59.3 16.0 %all-to-all-start = ((bf16[4,192,128]{2,1,0:T(8,128)(2,1)}), bf16[4,192,128]{2,1,0:T(8,128)(2,1)}, u32[]{:S(2)}, u32[]{:S(2)}) async-start(bf16[4,192,128]{2,1,0:T(8,128)(2,1)} %shard_map.99), calls=%async_computation | async-start | bytes 393216 | tf_op jit(solution)/shard_map/all_to_all | solution.py:505
  63.4 4.6 %copy-start.42 = (s32[4]{0:T(128)S(1)}, s32[4]{0:T(128)}, u32[]{:S(2)}) copy-start(s32[4]{0:T(128)} %copy-done.40) | copy-start | bytes 52
  63.4 9.5 %collective-permute-start.17 = (bf16[192,128]{1,0:T(8,128)(2,1)}, bf16[192,128]{1,0:T(8,128)(2,1)S(1)}, u32[]{:S(2)}, u32[]{:S(2)}) collective-permute-start(bf16[192,128]{1,0:T(8,128)(2,1)} %copy-done.35), channel_id=1, source_target_pairs={{0,4},{1,5},{2,6},{3,7},{4,0},{5,1},{6,2},{7,3},{8,12},{9,13},{10,... | collective-permute-start | bytes 147464 | tf_op jit(solution)/shard_map/ppermute | solution.py:348
  63.5 1.1 %copy-start.2 = (bf16[96,4096]{1,0:T(8,128)(2,1)S(1)}, bf16[96,4096]{1,0:T(8,128)(2,1)}, u32[]{:S(2)}) copy-start(bf16[96,4096]{1,0:T(8,128)(2,1)} %refs_1_.10) | copy-start | bytes 2359300
  66.3 9.0 %copy-start.5 = (bf16[128,2048]{1,0:T(8,128)(2,1)S(1)}, bf16[128,2048]{1,0:T(8,128)(2,1)}, u32[]{:S(2)}) copy-start(bf16[128,2048]{1,0:T(8,128)(2,1)} %get-tuple-element.44.refs_4_.refs_3_) | copy-start | bytes 1572868
  67.4 5.6 %collective-permute-start.18 = (bf16[192,128]{1,0:T(8,128)(2,1)S(1)}, bf16[192,128]{1,0:T(8,128)(2,1)S(1)}, u32[]{:S(2)}, u32[]{:S(2)}) collective-permute-start(bf16[192,128]{1,0:T(8,128)(2,1)S(1)} %copy-done.22), channel_id=1, source_target_pairs={{0,4},{1,5},{2,6},{3,7},{4,0},{5,1},{6,2},{7,3},{8,12},{9,13},{10,... | collective-permute-start | bytes 147464 | tf_op jit(solution)/shard_map/ppermute | solution.py:348
  67.9 5.6 %collective-permute-start.19 = (bf16[192,128]{1,0:T(8,128)(2,1)S(1)}, bf16[192,128]{1,0:T(8,128)(2,1)S(1)}, u32[]{:S(2)}, u32[]{:S(2)}) collective-permute-start(bf16[192,128]{1,0:T(8,128)(2,1)S(1)} %copy-done.24), channel_id=1, source_target_pairs={{0,4},{1,5},{2,6},{3,7},{4,0},{5,1},{6,2},{7,3},{8,12},{9,13},{10,... | collective-permute-start | bytes 147464 | tf_op jit(solution)/shard_map/ppermute | solution.py:348
  70.1 5.2 %collective-permute-start.16 = (bf16[192,128]{1,0:T(8,128)(2,1)S(1)}, bf16[192,128]{1,0:T(8,128)(2,1)S(1)}, u32[]{:S(2)}, u32[]{:S(2)}) collective-permute-start(bf16[192,128]{1,0:T(8,128)(2,1)S(1)} %shard_map.101), channel_id=1, source_target_pairs={{0,2},{1,3},{2,0},{3,1},{4,6},{5,7},{6,4},{7,5},{8,10},{9,11},{10,... | collective-permute-start | bytes 147464 | tf_op jit(solution)/shard_map/ppermute | solution.py:348
  75.3 1.0 copy-start.8
  78.5 14.7 %copy-start.17 = (bf16[4,384,384]{2,1,0:T(8,128)(2,1)S(1)}, bf16[4,384,384]{2,1,0:T(8,128)(2,1)}, u32[]{:S(2)}) copy-start(bf16[4,384,384]{2,1,0:T(8,128)(2,1)} %copy-done.16) | copy-start | bytes 3538948
  81.5 19.8 %collective-permute-start.20 = (f32[96,2048]{1,0:T(8,128)S(1)}, f32[96,2048]{1,0:T(8,128)S(1)}, u32[]{:S(2)}, u32[]{:S(2)}) collective-permute-start(f32[96,2048]{1,0:T(8,128)S(1)} %get-tuple-element.53), channel_id=1, source_target_pairs={{0,4},{1,5},{2,6},{3,7},{4,0},{5,1},{6,2},{7,3},{8,12},{9,13},{10,... | collective-permute-start | bytes 2359304 | tf_op jit(solution)/shard_map/ppermute | solution.py:348
  81.6 19.7 %collective-permute-start.21 = (f32[96,2048]{1,0:T(8,128)S(1)}, f32[96,2048]{1,0:T(8,128)S(1)}, u32[]{:S(2)}, u32[]{:S(2)}) collective-permute-start(f32[96,2048]{1,0:T(8,128)S(1)} %get-tuple-element.55), channel_id=1, source_target_pairs={{0,4},{1,5},{2,6},{3,7},{4,0},{5,1},{6,2},{7,3},{8,12},{9,13},{10,... | collective-permute-start | bytes 2359304 | tf_op jit(solution)/shard_map/ppermute | solution.py:348
  82.1 3.0 %collective-permute-start.22 = (bf16[192,128]{1,0:T(8,128)(2,1)S(1)}, bf16[192,128]{1,0:T(8,128)(2,1)S(1)}, u32[]{:S(2)}, u32[]{:S(2)}) collective-permute-start(bf16[192,128]{1,0:T(8,128)(2,1)S(1)} %collective-permute-done.16.refs_11_.refs_4_), channel_id=1, source_target_pairs={{0,4},{1,5},{2,6},{3,7},{4,0},{5,1},{6,2},{7,3},{8,12},{9,13},{10,... | collective-permute-start | bytes 147464 | tf_op jit(solution)/shard_map/ppermute | solution.py:348
  88.3 1.3 %collective-permute-start.24 = (f32[128,128]{1,0:T(8,128)S(1)}, f32[128,128]{1,0:T(8,128)S(1)}, u32[]{:S(2)}, u32[]{:S(2)}) collective-permute-start(f32[128,128]{1,0:T(8,128)S(1)} %get-tuple-element.61), channel_id=1, source_target_pairs={{0,4},{1,5},{2,6},{3,7},{4,0},{5,1},{6,2},{7,3},{8,12},{9,13},{10,... | collective-permute-start | bytes 196616 | tf_op jit(solution)/shard_map/ppermute | solution.py:348
  88.5 3.2 %collective-permute-start.23 = (f32[128,128]{1,0:T(8,128)}, f32[128,128]{1,0:T(8,128)S(1)}, u32[]{:S(2)}, u32[]{:S(2)}) collective-permute-start(f32[128,128]{1,0:T(8,128)} %copy-done.45), channel_id=1, source_target_pairs={{0,4},{1,5},{2,6},{3,7},{4,0},{5,1},{6,2},{7,3},{8,12},{9,13},{10,... | collective-permute-start | bytes 196616 | tf_op jit(solution)/shard_map/ppermute | solution.py:348
  89.6 11.0 %collective-permute-start.25 = (f32[128,128]{1,0:T(8,128)S(1)}, f32[128,128]{1,0:T(8,128)S(1)}, u32[]{:S(2)}, u32[]{:S(2)}) collective-permute-start(f32[128,128]{1,0:T(8,128)S(1)} %add.15.refs_8_), channel_id=1, source_target_pairs={{0,8},{1,9},{2,10},{3,11},{4,12},{5,13},{6,14},{7,15},{8,0},{9,1},... | collective-permute-start | bytes 196616 | tf_op jit(solution)/shard_map/ppermute | solution.py:348
  91.2 9.4 %collective-permute-start.26 = (f32[128,128]{1,0:T(8,128)S(1)}, f32[128,128]{1,0:T(8,128)S(1)}, u32[]{:S(2)}, u32[]{:S(2)}) collective-permute-start(f32[128,128]{1,0:T(8,128)S(1)} %add.15.refs_8_), channel_id=1, source_target_pairs={{0,16},{1,17},{2,18},{3,19},{4,20},{5,21},{6,22},{7,23},{8,24},{9,... | collective-permute-start | bytes 196616 | tf_op jit(solution)/shard_map/ppermute | solution.py:348
  91.7 8.9 %collective-permute-start.27 = (f32[128,128]{1,0:T(8,128)S(1)}, f32[128,128]{1,0:T(8,128)S(1)}, u32[]{:S(2)}, u32[]{:S(2)}) collective-permute-start(f32[128,128]{1,0:T(8,128)S(1)} %add.15.refs_8_), channel_id=1, source_target_pairs={{0,24},{1,25},{2,26},{3,27},{4,28},{5,29},{6,30},{7,31},{8,16},{9,... | collective-permute-start | bytes 196616 | tf_op jit(solution)/shard_map/ppermute | solution.py:348
  100.6 2.4 %copy-start.13 = (bf16[384,256]{1,0:T(8,128)(2,1)S(1)}, bf16[384,256]{1,0:T(8,128)(2,1)}, u32[]{:S(2)}) copy-start(bf16[384,256]{1,0:T(8,128)(2,1)} %refs_2_.5) | copy-start | bytes 589828
  100.6 2.4 %copy-start.15 = (bf16[384,256]{1,0:T(8,128)(2,1)S(1)}, bf16[384,256]{1,0:T(8,128)(2,1)}, u32[]{:S(2)}) copy-start(bf16[384,256]{1,0:T(8,128)(2,1)} %refs_1_.13) | copy-start | bytes 589828
  101.2 1.8 %collective-permute-start.28 = (f32[128,128]{1,0:T(8,128)S(1)}, f32[128,128]{1,0:T(8,128)S(1)}, u32[]{:S(2)}, u32[]{:S(2)}) collective-permute-start(f32[128,128]{1,0:T(8,128)S(1)} %get-tuple-element.66), channel_id=1, source_target_pairs={{0,4},{1,5},{2,6},{3,7},{4,0},{5,1},{6,2},{7,3},{8,12},{9,13},{10,... | collective-permute-start | bytes 196616 | tf_op jit(solution)/shard_map/ppermute | solution.py:348
  (28 other events, 22.2 us)

commit v17 on v16

--- a/solution.py
+++ b/solution.py
@@ -412,6 +412,8 @@
     linear = [keep, send(back, 1, 0)]
     if board:
         arrived[1], arrived[3] = hold([arrived[1], arrived[3]], [keep])
+    attn = lax.all_to_all(attn, "head", 0, 0, tiled=True)
+
     work = near_and_far if board else by_gathers
     both, across, joins, starts = work(
         attn, arrived, cotangent, mate_cotangent, out_weight, core, chip, colour, product
@@ -502,12 +504,12 @@
     second[2] = [send(cuts[0], 2, 0), send(cuts[1], 4, 0)]
     both = {0: mine, 1: send(one, 0, -1), 3: send(three, 0, -3)}
     across = {s: send(both[s], 1, 0) for s in (0, 1, 3)}
-    attn = lax.all_to_all(*hold([attn], [both[1], both[3]]), "head", 0, 0, tiled=True)
     (half,) = call(
         half_kernel,
         [((2 * own, DH), F32)],
         [left[0], fetch((DH, wide), (arrived[2], all_of, all_of))],
         [spots],
+        [attn],
         room=6,
         flops=product // 2,
     )
@@ -546,7 +548,7 @@
         ],
         [spots],
         [both[2], across[0], across[1], across[3]],
-        room=16,
+        room=8,
         flops=4 * product,
         lazy=True,
     )
@@ -558,7 +560,6 @@
 def by_gathers(attn, arrived, cotangent, mate_cotangent, out_weight, core, chip, colour, product):
     own, model = cotangent.shape
     shards, count = lax.axis_size("ctx"), lax.axis_size("head")
-    attn = lax.all_to_all(attn, "head", 0, 0, tiled=True)
     weight = lax.dynamic_slice_in_dim(out_weight, core * DH, DH, 0)
     zero = jnp.zeros((1,), jnp.int32)
     groups = [list(range(k, shards, 2)) for k in range(2)]

time: 106 us -> 89.6 us (0.85)
  local copies, waits for them, and re-layouts: 27.4 us -> 15.1 us
  starting transfers between devices: 28.9 us -> 25 us
    unnamed x92 -> x58, local copies, waits for them, and re-layouts: 25.5 us -> 13.3 us
    ppermute x29, starting transfers between devices: 24.7 us -> 21 us  [send(): return lax.ppermute(x, ('ctx', 'head'), pairs)]
  transfers between devices with their start and end apart: 30 -> 30, of which waited for: 11 -> 10; matrix products, arithmetic and copies ran while one was open for 4% -> 5% of each run, Pallas kernels for 15% -> 21%
where the time goes in v17:
time: 89.6 us; the launch traced here: 88.8 us
  starting transfers between devices  25 us (28%)
  Pallas kernels  23.4 us (26%)
  waiting for transfers between devices  21.9 us (24%)
  local copies, waits for them, and re-layouts  15.1 us (17%)
  other arithmetic  2.45 us (3%)
  between operations  0.97 us (1%)
    pallas_call x12, Pallas kernels, call(): pl.pallas_call(kernel, out_shape=[jax.ShapeDtypeStruct(s, t) for s, t in...  23.4 us
    ppermute x29, waiting for transfers between devices, send(): return lax.ppermute(x, ('ctx', 'head'), pairs)  21.9 us
    ppermute x29, starting transfers between devices, send(): return lax.ppermute(x, ('ctx', 'head'), pairs)  21 us
    unnamed x58, local copies, waits for them, and re-layouts  13.3 us
    all_to_all x1, starting transfers between devices, on_device(): attn = lax.all_to_all(attn, 'head', 0, 0, tiled=True)  3.99 us
    dynamic_slice x1, local copies, waits for them, and re-layouts, on_device(): lax.dynamic_slice(out_weight, (core * DH, colour * wide), (DH, wide))  1.88 us
  transfers between devices with their start and end apart: 30, of which 10 were waited for; matrix products, arithmetic and copies ran while one was open for 5% of the time, Pallas kernels for 21%

profile of v17, /device:TPU:0, one launch (start us, length us, event | category | flops | bytes accessed | tf_op | source)
XLA Modules:
  0.0 88.8 jit_solution(4880417382870488810)
XLA Ops:
  1.2 1.9 %dynamic_slice.3 = bf16[128,2048]{1,0:T(8,128)(2,1)} dynamic-slice(bf16[256,4096]{1,0:T(8,128)(2,1)} %refs_6_.1, s32[]{:T(128)S(6)} %select_n.6, s32[]{:T(128)S(6)} %select_n.7), dynamic_slice_sizes={128,2048} | dynamic-slice | bytes 1048580 | tf_op jit(solution)/shard_map/dynamic_slice | solution.py:388
  3.0 2.6 %collective-permute-start.7 = (bf16[128,2048]{1,0:T(8,128)(2,1)}, bf16[128,2048]{1,0:T(8,128)(2,1)S(1)}, u32[]{:S(2)}, u32[]{:S(2)}) collective-permute-start(bf16[128,2048]{1,0:T(8,128)(2,1)} %dynamic_slice.3), channel_id=1, source_target_pairs={{0,1},{1,2},{2,3},{3,0},{4,5},{5,6},{6,7},{7,4},{8,9},{9,10},{10,1... | collective-permute-start | bytes 1572872 | tf_op jit(solution)/shard_map/ppermute | solution.py:348
  5.7 2.0 %collective-permute-start.8 = (bf16[128,2048]{1,0:T(8,128)(2,1)}, bf16[128,2048]{1,0:T(8,128)(2,1)}, u32[]{:S(2)}, u32[]{:S(2)}) collective-permute-start(bf16[128,2048]{1,0:T(8,128)(2,1)} %dynamic_slice.3), channel_id=1, source_target_pairs={{0,3},{1,0},{2,1},{3,2},{4,7},{5,4},{6,5},{7,6},{8,11},{9,8},{10,9... | collective-permute-start | bytes 1572872 | tf_op jit(solution)/shard_map/ppermute | solution.py:348
  7.8 1.2 %pad_maximum_fusion.refs_2_ = bf16[3,384,256]{2,1,0:T(8,128)(2,1)S(1)} fusion(bf16[1,384,256]{2,1,0:T(8,128)(2,1)} %bitcast.18, bf16[1,384,256]{2,1,0:T(8,128)(2,1)} %bitcast.19, bf16[1,384,256]{2,1,0:T(8,128)(2,1)} %bitcast.17), kind=kLoop, calls=%fused_computation | loop fusion | flops 589824 | bytes 1179648 | tf_op jit(solution)/shard_map/stack | solution.py:398
  9.0 2.6 %shard_map.93 = (bf16[4,384,384]{2,1,0:T(8,128)(2,1)S(1)}, f32[384,128]{1,0:T(8,128)S(1)}, f32[384,128]{1,0:T(8,128)}, bf16[384,128]{1,0:T(8,128)(2,1)}, f32[128,128]{1,0:T(8,128)S(1)}, /*index=5*/f32[128,128]{1,0:T(8,128)}) custom-call(s32[3,3]{1,0:T(4,128)S(1)} %copy-done.26, s32[3]{0:T(128)S(1)} %pad_add_fusion.2.refs_1_.refs_0_, ...), custom_call_target="tpu_custom_call" | custom-call | flops 264241152 | bytes 2392064 | tf_op jit(solution)/shard_map/pallas_call | solution.py:103
  11.5 1.1 %copy-done.10 = bf16[4,384,384]{2,1,0:T(8,128)(2,1)} copy-done((bf16[4,384,384]{2,1,0:T(8,128)(2,1)}, bf16[4,384,384]{2,1,0:T(8,128)(2,1)S(1)}, u32[]{:S(2)}) %copy-start.10) | copy-done | bytes 1179672
  13.2 0.7 copy-done.18
  14.6 1.1 %collective-permute-done.1.refs_1_.refs_8_ = bf16[384,128]{1,0:T(8,128)(2,1)S(1)} collective-permute-done((bf16[384,128]{1,0:T(8,128)(2,1)}, bf16[384,128]{1,0:T(8,128)(2,1)S(1)}, u32[]{:S(2)}, u32[]{:S(2)}) %collective-permute-start.1) | collective-permute-done | bytes 98336 | tf_op jit(solution)/shard_map/ppermute | solution.py:348
  15.7 0.6 copy-done.14
  16.3 0.9 add.12
  17.2 1.7 %collective-permute-start.4 = (f32[128,128]{1,0:T(8,128)S(1)}, f32[128,128]{1,0:T(8,128)S(1)}, u32[]{:S(2)}, u32[]{:S(2)}) collective-permute-start(f32[128,128]{1,0:T(8,128)S(1)} %add.12), channel_id=1, source_target_pairs={{0,8},{1,9},{2,10},{3,11},{4,12},{5,13},{6,14},{7,15},{8,0},{9,1},... | collective-permute-start | bytes 196616 | tf_op jit(solution)/shard_map/ppermute | solution.py:348
  18.9 1.5 %collective-permute-start.5 = (f32[128,128]{1,0:T(8,128)S(1)}, f32[128,128]{1,0:T(8,128)S(1)}, u32[]{:S(2)}, u32[]{:S(2)}) collective-permute-start(f32[128,128]{1,0:T(8,128)S(1)} %add.12), channel_id=1, source_target_pairs={{0,16},{1,17},{2,18},{3,19},{4,20},{5,21},{6,22},{7,23},{8,24},{9,... | collective-permute-start | bytes 196616 | tf_op jit(solution)/shard_map/ppermute | solution.py:348
  20.8 0.7 collective-permute-done.4.refs_4_
  21.6 1.6 %collective-permute-done.5.refs_5_ = f32[128,128]{1,0:T(8,128)S(1)} collective-permute-done((f32[128,128]{1,0:T(8,128)S(1)}, f32[128,128]{1,0:T(8,128)S(1)}, u32[]{:S(2)}, u32[]{:S(2)}) %collective-permute-start.5) | collective-permute-done | bytes 65568 | tf_op jit(solution)/shard_map/ppermute | solution.py:348
  23.2 2.4 %collective-permute-done.6.refs_6_ = f32[128,128]{1,0:T(8,128)S(1)} collective-permute-done((f32[128,128]{1,0:T(8,128)S(1)}, f32[128,128]{1,0:T(8,128)S(1)}, u32[]{:S(2)}, u32[]{:S(2)}) %collective-permute-start.6) | collective-permute-done | bytes 65568 | tf_op jit(solution)/shard_map/ppermute | solution.py:348
  25.6 0.9 %copy-done.6 = bf16[384,256]{1,0:T(8,128)(2,1)S(1)} copy-done((bf16[384,256]{1,0:T(8,128)(2,1)S(1)}, bf16[384,256]{1,0:T(8,128)(2,1)}, u32[]{:S(2)}) %copy-start.6) | copy-done | bytes 196632
  26.6 0.8 copy-done.13
  27.4 0.9 %copy-done.15 = bf16[384,128]{1,0:T(8,128)(2,1)S(1)} copy-done((bf16[384,128]{1,0:T(8,128)(2,1)S(1)}, bf16[384,128]{1,0:T(8,128)(2,1)}, u32[]{:S(2)}) %copy-start.15) | copy-done | bytes 98328
  28.3 0.9 %copy-done.19 = f32[384,128]{1,0:T(8,128)S(1)} copy-done((f32[384,128]{1,0:T(8,128)S(1)}, f32[384,128]{1,0:T(8,128)}, u32[]{:S(2)}) %copy-start.19) | copy-done | bytes 196632
  29.2 1.2 %shard_map.95 = (bf16[4,192,128]{2,1,0:T(8,128)(2,1)S(1)}, f32[128,128]{1,0:T(8,128)S(1)}, f32[128,128]{1,0:T(8,128)S(1)}) custom-call(s32[4]{0:T(128)S(1)} %add_convert_fusion.refs_0_, s32[3]{0:T(128)S(1)} %pad_add_fusion.2.refs_1_.refs_0_, f32[128,128]{1,0:T(8,128)S(1)} %copy-done.13, f32[128,128]{1,0:T(8,128)} %collective-permute-done.3.refs_3_, ...), custom_call_target="tpu_custom_call" | custom-call | flops 1 | bytes 1343488 | tf_op jit(solution)/shard_map/pallas_call | solution.py:103
  31.1 0.7 copy-done.20
  32.4 0.8 copy-done.3
  33.8 1.5 %collective-permute-start.11 = (bf16[128,2048]{1,0:T(8,128)(2,1)}, bf16[128,2048]{1,0:T(8,128)(2,1)}, u32[]{:S(2)}, u32[]{:S(2)}) collective-permute-start(bf16[128,2048]{1,0:T(8,128)(2,1)} %get-tuple-element.45.refs_5_), channel_id=1, source_target_pairs={{0,16},{1,17},{2,18},{3,19},{4,20},{5,21},{6,22},{7,23},{8,24},{9,... | collective-permute-start | bytes 1572872 | tf_op jit(solution)/shard_map/ppermute | solution.py:348
  35.4 4.0 %all-to-all-start = ((bf16[4,192,128]{2,1,0:T(8,128)(2,1)}), bf16[4,192,128]{2,1,0:T(8,128)(2,1)}, u32[]{:S(2)}, u32[]{:S(2)}) async-start(bf16[4,192,128]{2,1,0:T(8,128)(2,1)} %copy-done.20), calls=%async_computation | async-start | bytes 393216 | tf_op jit(solution)/shard_map/all_to_all | solution.py:415
  39.5 1.1 %copy-done.1 = bf16[96,4096]{1,0:T(8,128)(2,1)S(1)} copy-done((bf16[96,4096]{1,0:T(8,128)(2,1)S(1)}, bf16[96,4096]{1,0:T(8,128)(2,1)}, u32[]{:S(2)}) %copy-start.1) | copy-done | bytes 786456
  40.6 1.0 %copy-done.4 = bf16[128,2048]{1,0:T(8,128)(2,1)S(1)} copy-done((bf16[128,2048]{1,0:T(8,128)(2,1)S(1)}, bf16[128,2048]{1,0:T(8,128)(2,1)}, u32[]{:S(2)}) %copy-start.4) | copy-done | bytes 524312
  41.6 2.6 %shard_map.97 = (bf16[192,128]{1,0:T(8,128)(2,1)}, f32[192,256]{1,0:T(8,128)S(1)}) custom-call(s32[4]{0:T(128)S(1)} %pad_add_fusion.1.refs_0_, bf16[96,4096]{1,0:T(8,128)(2,1)S(1)} %copy-done.1, bf16[96,4096]{1,0:T(8,128)(2,1)S(1)} %collective-permute-done.refs_3_.refs_2_, bf16[256,4096]{1,0:T(8,128)(2,1)S(1)} %copy-done, bf16[128,2048]{1,0:T(8,128)(2,1)S(1)} %copy-done.4, ...), custom_call_target="tpu_custom_call" | custom-call | flops 402653184 | bytes 4964352 | tf_op jit(solution)/shard_map/pallas_call | solution.py:103
  44.2 5.2 %collective-permute-done.9.refs_6_.refs_3_.refs_4_ = bf16[128,2048]{1,0:T(8,128)(2,1)S(1)} collective-permute-done((bf16[128,2048]{1,0:T(8,128)(2,1)}, bf16[128,2048]{1,0:T(8,128)(2,1)S(1)}, u32[]{:S(2)}, u32[]{:S(2)}) %collective-permute-start.9) | collective-permute-done | bytes 524320 | tf_op jit(solution)/shard_map/ppermute | solution.py:348
  49.4 3.1 %shard_map.98 = (bf16[192,128]{1,0:T(8,128)(2,1)}, bf16[192,128]{1,0:T(8,128)(2,1)}, bf16[128,1024]{1,0:T(8,128)(2,1)}, bf16[128,1024]{1,0:T(8,128)(2,1)}) custom-call(s32[4]{0:T(128)S(1)} %pad_add_fusion.1.refs_0_, bf16[96,4096]{1,0:T(8,128)(2,1)S(1)} %copy-done.1, bf16[96,4096]{1,0:T(8,128)(2,1)S(1)} %collective-permute-done.refs_3_.refs_2_, ...), custom_call_target="tpu_custom_call" | custom-call | flops 201326592 | bytes 3964928 | tf_op jit(solution)/shard_map/pallas_call | solution.py:103
  53.1 1.3 %collective-permute-start.13 = (bf16[128,1024]{1,0:T(8,128)(2,1)}, bf16[128,1024]{1,0:T(8,128)(2,1)}, u32[]{:S(2)}, u32[]{:S(2)}) collective-permute-start(bf16[128,1024]{1,0:T(8,128)(2,1)} %get-tuple-element.48), channel_id=1, source_target_pairs={{0,16},{1,17},{2,18},{3,19},{4,20},{5,21},{6,22},{7,23},{8,24},{9,... | collective-permute-start | bytes 786440 | tf_op jit(solution)/shard_map/ppermute | solution.py:348
  54.4 0.7 collective-permute-start.14
  55.1 1.4 %collective-permute-start.15 = (bf16[192,128]{1,0:T(8,128)(2,1)}, bf16[192,128]{1,0:T(8,128)(2,1)S(1)}, u32[]{:S(2)}, u32[]{:S(2)}) collective-permute-start(bf16[192,128]{1,0:T(8,128)(2,1)} %get-tuple-element.50), channel_id=1, source_target_pairs={{0,1},{1,2},{2,3},{3,0},{4,5},{5,6},{6,7},{7,4},{8,9},{9,10},{10,1... | collective-permute-start | bytes 147464 | tf_op jit(solution)/shard_map/ppermute | solution.py:348
  56.5 1.1 %copy-done.2 = bf16[96,4096]{1,0:T(8,128)(2,1)S(1)} copy-done((bf16[96,4096]{1,0:T(8,128)(2,1)S(1)}, bf16[96,4096]{1,0:T(8,128)(2,1)}, u32[]{:S(2)}) %copy-start.2) | copy-done | bytes 786456
  58.2 1.0 %shard_map.99.refs_5_ = f32[192,128]{1,0:T(8,128)S(1)} custom-call(s32[4]{0:T(128)S(1)} %copy-done.24, bf16[96,4096]{1,0:T(8,128)(2,1)S(1)} %copy-done.2, bf16[96,4096]{1,0:T(8,128)(2,1)S(1)} %collective-permute-done.refs_3_.refs_2_, bf16[128,2048]{1,0:T(8,128)(2,1)S(1)} %collective-permute-done.9.refs_6_.refs_3_.refs_4_, ...), custom_call_target="tpu_custom_call" | custom-call | flops 100663296 | bytes 2195456 | tf_op jit(solution)/shard_map/pallas_call | solution.py:103
  59.8 1.4 %collective-permute-done.15.refs_7_.refs_5_ = bf16[192,128]{1,0:T(8,128)(2,1)S(1)} collective-permute-done((bf16[192,128]{1,0:T(8,128)(2,1)}, bf16[192,128]{1,0:T(8,128)(2,1)S(1)}, u32[]{:S(2)}, u32[]{:S(2)}) %collective-permute-start.15) | collective-permute-done | bytes 49184 | tf_op jit(solution)/shard_map/ppermute | solution.py:348
  61.2 2.0 %shard_map.100 = bf16[192,128]{1,0:T(8,128)(2,1)S(1)} custom-call(s32[4]{0:T(128)S(1)} %copy-done.25, bf16[96,4096]{1,0:T(8,128)(2,1)S(1)} %copy-done.2, bf16[96,4096]{1,0:T(8,128)(2,1)S(1)} %collective-permute-done.refs_3_.refs_2_, bf16[128,1024]{1,0:T(8,128)(2,1)} %collective-permute-done.12.refs_3_.refs_9_, ...), custom_call_target="tpu_custom_call" | custom-call | flops 100663296 | bytes 2244608 | tf_op jit(solution)/shard_map/pallas_call | solution.py:103
  63.5 5.0 %collective-permute-done.16.refs_11_.refs_4_ = bf16[192,128]{1,0:T(8,128)(2,1)S(1)} collective-permute-done((bf16[192,128]{1,0:T(8,128)(2,1)S(1)}, bf16[192,128]{1,0:T(8,128)(2,1)S(1)}, u32[]{:S(2)}, u32[]{:S(2)}) %collective-permute-start.16) | collective-permute-done | bytes 49184 | tf_op jit(solution)/shard_map/ppermute | solution.py:348
  68.5 3.0 %shard_map.101 = (f32[96,2048]{1,0:T(8,128)S(1)}, f32[96,2048]{1,0:T(8,128)S(1)}, f32[96,2048]{1,0:T(8,128)S(1)}, f32[96,2048]{1,0:T(8,128)S(1)}) custom-call(s32[4]{0:T(128)S(1)} %copy-done.25, bf16[4,192,128]{2,1,0:T(8,128)(2,1)} %all-to-all-done.refs_4_.refs_1_, bf16[256,4096]{1,0:T(8,128)(2,1)S(1)} %copy-done, bf16[128,2048]{1,0:T(8,128)(2,1)S(1)} %copy-done.5, ...), custom_call_target="tpu_custom_call" | custom-call | flops 805306368 | bytes 10682368 | tf_op jit(solution)/shard_map/pallas_call | solution.py:103
  72.2 2.9 %collective-permute-done.22.refs_8_ = bf16[192,128]{1,0:T(8,128)(2,1)S(1)} collective-permute-done((bf16[192,128]{1,0:T(8,128)(2,1)S(1)}, bf16[192,128]{1,0:T(8,128)(2,1)S(1)}, u32[]{:S(2)}, u32[]{:S(2)}) %collective-permute-start.22) | collective-permute-done | bytes 49184 | tf_op jit(solution)/shard_map/ppermute | solution.py:348
  75.0 1.1 %shard_map.103 = (bf16[384,256]{1,0:T(8,128)(2,1)S(1)}, f32[128,128]{1,0:T(8,128)S(1)}, f32[128,128]{1,0:T(8,128)S(1)}) custom-call(s32[3]{0:T(128)S(1)} %copy-done.22, bf16[384,256]{1,0:T(8,128)(2,1)S(1)} %copy-done.7, bf16[192,128]{1,0:T(8,128)(2,1)} %get-tuple-element.51.refs_2_, bf16[192,128]{1,0:T(8,128)(2,1)S(1)} %collective-permute-done.14.refs_6_.refs_3_, ...), custom_call_target="tpu_custom_call" | custom-call | flops 1 | bytes 917504 | tf_op jit(solution)/shard_map/pallas_call | solution.py:103
  76.7 0.7 collective-permute-done.24.refs_2_
  77.5 1.3 %collective-permute-start.25 = (f32[128,128]{1,0:T(8,128)S(1)}, f32[128,128]{1,0:T(8,128)S(1)}, u32[]{:S(2)}, u32[]{:S(2)}) collective-permute-start(f32[128,128]{1,0:T(8,128)S(1)} %add.15.refs_8_), channel_id=1, source_target_pairs={{0,8},{1,9},{2,10},{3,11},{4,12},{5,13},{6,14},{7,15},{8,0},{9,1},... | collective-permute-start | bytes 196616 | tf_op jit(solution)/shard_map/ppermute | solution.py:348
  78.7 1.0 %collective-permute-start.26 = (f32[128,128]{1,0:T(8,128)S(1)}, f32[128,128]{1,0:T(8,128)S(1)}, u32[]{:S(2)}, u32[]{:S(2)}) collective-permute-start(f32[128,128]{1,0:T(8,128)S(1)} %add.15.refs_8_), channel_id=1, source_target_pairs={{0,16},{1,17},{2,18},{3,19},{4,20},{5,21},{6,22},{7,23},{8,24},{9,... | collective-permute-start | bytes 196616 | tf_op jit(solution)/shard_map/ppermute | solution.py:348
  79.7 1.3 %collective-permute-start.27 = (f32[128,128]{1,0:T(8,128)S(1)}, f32[128,128]{1,0:T(8,128)S(1)}, u32[]{:S(2)}, u32[]{:S(2)}) collective-permute-start(f32[128,128]{1,0:T(8,128)S(1)} %add.15.refs_8_), channel_id=1, source_target_pairs={{0,24},{1,25},{2,26},{3,27},{4,28},{5,29},{6,30},{7,31},{8,16},{9,... | collective-permute-start | bytes 196616 | tf_op jit(solution)/shard_map/ppermute | solution.py:348
  81.1 3.0 %shard_map.104 = (bf16[384,256]{1,0:T(8,128)(2,1)}, f32[384,256]{1,0:T(8,128)S(1)}, f32[384,256]{1,0:T(8,128)S(1)}) custom-call(s32[3]{0:T(128)S(1)} %copy-done.22, bf16[384,256]{1,0:T(8,128)(2,1)S(1)} %copy-done.7, bf16[384,256]{1,0:T(8,128)(2,1)S(1)} %copy-done.9, bf16[384,256]{1,0:T(8,128)(2,1)S(1)} %copy-done.8, ...), custom_call_target="tpu_custom_call" | custom-call | flops 528482304 | bytes 3080192 | tf_op jit(solution)/shard_map/pallas_call | solution.py:103
  84.1 0.8 collective-permute-done.27.refs_5_
  85.6 1.6 %shard_map.102 = (bf16[96,4096]{1,0:T(8,128)(2,1)}, f32[8,128]{1,0:T(8,128)S(1)}) custom-call(s32[2]{0:T(128)S(1)} %pad_add_fusion.refs_0_, f32[96,2048]{1,0:T(8,128)S(1)} %get-tuple-element.52.refs_1_, f32[96,2048]{1,0:T(8,128)S(1)} %collective-permute-done.20.refs_2_, f32[96,2048]{1,0:T(8,128)S(1)} %get-tuple-element.54.refs_3_, ...), custom_call_target="tpu_custom_call" | custom-call | flops 1 | bytes 3936256 | tf_op jit(solution)/shard_map/pallas_call | solution.py:103
  87.2 1.6 %shard_map.106 = (bf16[384,256]{1,0:T(8,128)(2,1)}, bf16[384,256]{1,0:T(8,128)(2,1)}) custom-call(s32[3]{0:T(128)S(1)} %copy-done.22, bf16[384,256]{1,0:T(8,128)(2,1)S(1)} %copy-done.9, bf16[384,256]{1,0:T(8,128)(2,1)S(1)} %copy-done.8, f32[384,256]{1,0:T(8,128)S(1)} %get-tuple-element.63.refs_6_.refs_3_, f32[384,256]{1,0:T(8,128)S(1)} %get-tuple-element.64.refs_4_, ...), custom_call_target="tpu_custom_call" | custom-call | flops 1 | bytes 1703936 | tf_op jit(solution)/shard_map/pallas_call | solution.py:103
  (93 shorter events, 8.3 us)
Async XLA Ops:
  0.6 8.3 %copy-start.26 = (s32[3,3]{1,0:T(4,128)S(1)}, s32[3,3]{1,0:T(4,128)}, u32[]{:S(2)}) copy-start(s32[3,3]{1,0:T(4,128)} %refs_0_.1) | copy-start | bytes 112
  0.6 8.3 %collective-permute-start = (bf16[96,4096]{1,0:T(8,128)(2,1)}, bf16[96,4096]{1,0:T(8,128)(2,1)S(1)}, u32[]{:S(2)}, u32[]{:S(2)}) collective-permute-start(bf16[96,4096]{1,0:T(8,128)(2,1)} %refs_1_.10), channel_id=1, source_target_pairs={{0,4},{1,5},{2,6},{3,7},{4,0},{5,1},{6,2},{7,3},{8,12},{9,13},{10,... | collective-permute-start | bytes 2359304 | tf_op jit(solution)/shard_map/ppermute | solution.py:348
  3.0 29.4 %collective-permute-start.7 = (bf16[128,2048]{1,0:T(8,128)(2,1)}, bf16[128,2048]{1,0:T(8,128)(2,1)S(1)}, u32[]{:S(2)}, u32[]{:S(2)}) collective-permute-start(bf16[128,2048]{1,0:T(8,128)(2,1)} %dynamic_slice.3), channel_id=1, source_target_pairs={{0,1},{1,2},{2,3},{3,0},{4,5},{5,6},{6,7},{7,4},{8,9},{9,10},{10,1... | collective-permute-start | bytes 1572872 | tf_op jit(solution)/shard_map/ppermute | solution.py:348
  5.7 26.8 %collective-permute-start.8 = (bf16[128,2048]{1,0:T(8,128)(2,1)}, bf16[128,2048]{1,0:T(8,128)(2,1)}, u32[]{:S(2)}, u32[]{:S(2)}) collective-permute-start(bf16[128,2048]{1,0:T(8,128)(2,1)} %dynamic_slice.3), channel_id=1, source_target_pairs={{0,3},{1,0},{2,1},{3,2},{4,7},{5,4},{6,5},{7,6},{8,11},{9,8},{10,9... | collective-permute-start | bytes 1572872 | tf_op jit(solution)/shard_map/ppermute | solution.py:348
  7.8 22.7 %copy-start.21 = (s32[3]{0:T(128)}, s32[3]{0:T(128)S(1)}, u32[]{:S(2)}) copy-start(s32[3]{0:T(128)S(1)} %pad_add_fusion.2.refs_1_.refs_0_) | copy-start | bytes 40
  8.9 30.5 %copy-start = (bf16[256,4096]{1,0:T(8,128)(2,1)S(1)}, bf16[256,4096]{1,0:T(8,128)(2,1)}, u32[]{:S(2)}) copy-start(bf16[256,4096]{1,0:T(8,128)(2,1)} %refs_6_.1) | copy-start | bytes 6291460
  11.5 1.1 %copy-start.10 = (bf16[4,384,384]{2,1,0:T(8,128)(2,1)}, bf16[4,384,384]{2,1,0:T(8,128)(2,1)S(1)}, u32[]{:S(2)}) copy-start(bf16[4,384,384]{2,1,0:T(8,128)(2,1)S(1)} %get-tuple-element.58.refs_5_) | copy-start | bytes 3538948
  13.9 1.8 %collective-permute-start.2 = (f32[384,128]{1,0:T(8,128)}, f32[384,128]{1,0:T(8,128)}, u32[]{:S(2)}, u32[]{:S(2)}) collective-permute-start(f32[384,128]{1,0:T(8,128)} %get-tuple-element.39), channel_id=1, source_target_pairs={{0,4},{1,5},{2,6},{3,7},{4,0},{5,1},{6,2},{7,3},{8,12},{9,13},{10,... | collective-permute-start | bytes 589832 | tf_op jit(solution)/shard_map/ppermute | solution.py:348
  14.1 1.6 %collective-permute-start.1 = (bf16[384,128]{1,0:T(8,128)(2,1)}, bf16[384,128]{1,0:T(8,128)(2,1)S(1)}, u32[]{:S(2)}, u32[]{:S(2)}) collective-permute-start(bf16[384,128]{1,0:T(8,128)(2,1)} %get-tuple-element.38), channel_id=1, source_target_pairs={{0,4},{1,5},{2,6},{3,7},{4,0},{5,1},{6,2},{7,3},{8,12},{9,13},{10,... | collective-permute-start | bytes 294920 | tf_op jit(solution)/shard_map/ppermute | solution.py:348
  14.4 1.9 %collective-permute-start.3 = (f32[128,128]{1,0:T(8,128)}, f32[128,128]{1,0:T(8,128)}, u32[]{:S(2)}, u32[]{:S(2)}) collective-permute-start(f32[128,128]{1,0:T(8,128)} %get-tuple-element.40), channel_id=1, source_target_pairs={{0,4},{1,5},{2,6},{3,7},{4,0},{5,1},{6,2},{7,3},{8,12},{9,13},{10,... | collective-permute-start | bytes 196616 | tf_op jit(solution)/shard_map/ppermute | solution.py:348
  17.2 4.4 %collective-permute-start.4 = (f32[128,128]{1,0:T(8,128)S(1)}, f32[128,128]{1,0:T(8,128)S(1)}, u32[]{:S(2)}, u32[]{:S(2)}) collective-permute-start(f32[128,128]{1,0:T(8,128)S(1)} %add.12), channel_id=1, source_target_pairs={{0,8},{1,9},{2,10},{3,11},{4,12},{5,13},{6,14},{7,15},{8,0},{9,1},... | collective-permute-start | bytes 196616 | tf_op jit(solution)/shard_map/ppermute | solution.py:348
  18.9 4.3 %collective-permute-start.5 = (f32[128,128]{1,0:T(8,128)S(1)}, f32[128,128]{1,0:T(8,128)S(1)}, u32[]{:S(2)}, u32[]{:S(2)}) collective-permute-start(f32[128,128]{1,0:T(8,128)S(1)} %add.12), channel_id=1, source_target_pairs={{0,16},{1,17},{2,18},{3,19},{4,20},{5,21},{6,22},{7,23},{8,24},{9,... | collective-permute-start | bytes 196616 | tf_op jit(solution)/shard_map/ppermute | solution.py:348
  20.5 5.2 %collective-permute-start.6 = (f32[128,128]{1,0:T(8,128)S(1)}, f32[128,128]{1,0:T(8,128)S(1)}, u32[]{:S(2)}, u32[]{:S(2)}) collective-permute-start(f32[128,128]{1,0:T(8,128)S(1)} %add.12), channel_id=1, source_target_pairs={{0,24},{1,25},{2,26},{3,27},{4,28},{5,29},{6,30},{7,31},{8,16},{9,... | collective-permute-start | bytes 196616 | tf_op jit(solution)/shard_map/ppermute | solution.py:348
  25.6 0.9 %copy-start.6 = (bf16[384,256]{1,0:T(8,128)(2,1)S(1)}, bf16[384,256]{1,0:T(8,128)(2,1)}, u32[]{:S(2)}) copy-start(bf16[384,256]{1,0:T(8,128)(2,1)} %refs_1_.12) | copy-start | bytes 589828
  33.2 16.2 %collective-permute-start.9 = (bf16[128,2048]{1,0:T(8,128)(2,1)}, bf16[128,2048]{1,0:T(8,128)(2,1)S(1)}, u32[]{:S(2)}, u32[]{:S(2)}) collective-permute-start(bf16[128,2048]{1,0:T(8,128)(2,1)} %get-tuple-element.44.refs_4_.refs_3_), channel_id=1, source_target_pairs={{0,1},{1,2},{2,3},{3,0},{4,5},{5,6},{6,7},{7,4},{8,9},{9,10},{10,1... | collective-permute-start | bytes 1572872 | tf_op jit(solution)/shard_map/ppermute | solution.py:348
  33.2 16.2 %collective-permute-start.10 = (bf16[128,2048]{1,0:T(8,128)(2,1)}, bf16[128,2048]{1,0:T(8,128)(2,1)}, u32[]{:S(2)}, u32[]{:S(2)}) collective-permute-start(bf16[128,2048]{1,0:T(8,128)(2,1)} %get-tuple-element.44.refs_4_.refs_3_), channel_id=1, source_target_pairs={{0,8},{1,9},{2,10},{3,11},{4,12},{5,13},{6,14},{7,15},{8,0},{9,1},... | collective-permute-start | bytes 1572872 | tf_op jit(solution)/shard_map/ppermute | solution.py:348
  33.8 15.5 %collective-permute-start.11 = (bf16[128,2048]{1,0:T(8,128)(2,1)}, bf16[128,2048]{1,0:T(8,128)(2,1)}, u32[]{:S(2)}, u32[]{:S(2)}) collective-permute-start(bf16[128,2048]{1,0:T(8,128)(2,1)} %get-tuple-element.45.refs_5_), channel_id=1, source_target_pairs={{0,16},{1,17},{2,18},{3,19},{4,20},{5,21},{6,22},{7,23},{8,24},{9,... | collective-permute-start | bytes 1572872 | tf_op jit(solution)/shard_map/ppermute | solution.py:348
  35.4 13.9 %copy-start.23 = (s32[4]{0:T(128)}, s32[4]{0:T(128)S(1)}, u32[]{:S(2)}) copy-start(s32[4]{0:T(128)S(1)} %pad_add_fusion.1.refs_0_) | copy-start | bytes 52
  35.4 21.0 %all-to-all-start = ((bf16[4,192,128]{2,1,0:T(8,128)(2,1)}), bf16[4,192,128]{2,1,0:T(8,128)(2,1)}, u32[]{:S(2)}, u32[]{:S(2)}) async-start(bf16[4,192,128]{2,1,0:T(8,128)(2,1)} %copy-done.20), calls=%async_computation | async-start | bytes 393216 | tf_op jit(solution)/shard_map/all_to_all | solution.py:415
  39.5 1.1 %copy-start.1 = (bf16[96,4096]{1,0:T(8,128)(2,1)S(1)}, bf16[96,4096]{1,0:T(8,128)(2,1)}, u32[]{:S(2)}) copy-start(bf16[96,4096]{1,0:T(8,128)(2,1)} %refs_1_.10) | copy-start | bytes 2359300
  40.6 1.0 %copy-start.4 = (bf16[128,2048]{1,0:T(8,128)(2,1)S(1)}, bf16[128,2048]{1,0:T(8,128)(2,1)}, u32[]{:S(2)}) copy-start(bf16[128,2048]{1,0:T(8,128)(2,1)} %get-tuple-element.44.refs_4_.refs_3_) | copy-start | bytes 1572868
  52.5 8.7 %collective-permute-start.12 = (bf16[128,1024]{1,0:T(8,128)(2,1)}, bf16[128,1024]{1,0:T(8,128)(2,1)}, u32[]{:S(2)}, u32[]{:S(2)}) collective-permute-start(bf16[128,1024]{1,0:T(8,128)(2,1)} %get-tuple-element.47), channel_id=1, source_target_pairs={{0,8},{1,9},{2,10},{3,11},{4,12},{5,13},{6,14},{7,15},{8,0},{9,1},... | collective-permute-start | bytes 786440 | tf_op jit(solution)/shard_map/ppermute | solution.py:348
  53.1 8.1 %collective-permute-start.13 = (bf16[128,1024]{1,0:T(8,128)(2,1)}, bf16[128,1024]{1,0:T(8,128)(2,1)}, u32[]{:S(2)}, u32[]{:S(2)}) collective-permute-start(bf16[128,1024]{1,0:T(8,128)(2,1)} %get-tuple-element.48), channel_id=1, source_target_pairs={{0,16},{1,17},{2,18},{3,19},{4,20},{5,21},{6,22},{7,23},{8,24},{9,... | collective-permute-start | bytes 786440 | tf_op jit(solution)/shard_map/ppermute | solution.py:348
  54.4 4.8 %collective-permute-start.14 = (bf16[192,128]{1,0:T(8,128)(2,1)}, bf16[192,128]{1,0:T(8,128)(2,1)S(1)}, u32[]{:S(2)}, u32[]{:S(2)}) collective-permute-start(bf16[192,128]{1,0:T(8,128)(2,1)} %get-tuple-element.49), channel_id=1, source_target_pairs={{0,3},{1,0},{2,1},{3,2},{4,7},{5,4},{6,5},{7,6},{8,11},{9,8},{10,9... | collective-permute-start | bytes 147464 | tf_op jit(solution)/shard_map/ppermute | solution.py:348
  55.1 6.1 %collective-permute-start.15 = (bf16[192,128]{1,0:T(8,128)(2,1)}, bf16[192,128]{1,0:T(8,128)(2,1)S(1)}, u32[]{:S(2)}, u32[]{:S(2)}) collective-permute-start(bf16[192,128]{1,0:T(8,128)(2,1)} %get-tuple-element.50), channel_id=1, source_target_pairs={{0,1},{1,2},{2,3},{3,0},{4,5},{5,6},{6,7},{7,4},{8,9},{9,10},{10,1... | collective-permute-start | bytes 147464 | tf_op jit(solution)/shard_map/ppermute | solution.py:348
  56.5 7.0 %collective-permute-start.17 = (bf16[192,128]{1,0:T(8,128)(2,1)}, bf16[192,128]{1,0:T(8,128)(2,1)S(1)}, u32[]{:S(2)}, u32[]{:S(2)}) collective-permute-start(bf16[192,128]{1,0:T(8,128)(2,1)} %get-tuple-element.51.refs_2_), channel_id=1, source_target_pairs={{0,4},{1,5},{2,6},{3,7},{4,0},{5,1},{6,2},{7,3},{8,12},{9,13},{10,... | collective-permute-start | bytes 147464 | tf_op jit(solution)/shard_map/ppermute | solution.py:348
  56.5 1.1 %copy-start.2 = (bf16[96,4096]{1,0:T(8,128)(2,1)S(1)}, bf16[96,4096]{1,0:T(8,128)(2,1)}, u32[]{:S(2)}) copy-start(bf16[96,4096]{1,0:T(8,128)(2,1)} %refs_1_.10) | copy-start | bytes 2359300
  58.2 3.0 %copy-start.25 = (s32[4]{0:T(128)S(1)}, s32[4]{0:T(128)}, u32[]{:S(2)}) copy-start(s32[4]{0:T(128)} %copy-done.23) | copy-start | bytes 52
  58.2 10.3 %copy-start.5 = (bf16[128,2048]{1,0:T(8,128)(2,1)S(1)}, bf16[128,2048]{1,0:T(8,128)(2,1)}, u32[]{:S(2)}) copy-start(bf16[128,2048]{1,0:T(8,128)(2,1)} %get-tuple-element.44.refs_4_.refs_3_) | copy-start | bytes 1572868
  59.3 4.2 %collective-permute-start.18 = (bf16[192,128]{1,0:T(8,128)(2,1)S(1)}, bf16[192,128]{1,0:T(8,128)(2,1)S(1)}, u32[]{:S(2)}, u32[]{:S(2)}) collective-permute-start(bf16[192,128]{1,0:T(8,128)(2,1)S(1)} %collective-permute-done.14.refs_6_.refs_3_), channel_id=1, source_target_pairs={{0,4},{1,5},{2,6},{3,7},{4,0},{5,1},{6,2},{7,3},{8,12},{9,13},{10,... | collective-permute-start | bytes 147464 | tf_op jit(solution)/shard_map/ppermute | solution.py:348
  61.2 2.3 %collective-permute-start.19 = (bf16[192,128]{1,0:T(8,128)(2,1)S(1)}, bf16[192,128]{1,0:T(8,128)(2,1)S(1)}, u32[]{:S(2)}, u32[]{:S(2)}) collective-permute-start(bf16[192,128]{1,0:T(8,128)(2,1)S(1)} %collective-permute-done.15.refs_7_.refs_5_), channel_id=1, source_target_pairs={{0,4},{1,5},{2,6},{3,7},{4,0},{5,1},{6,2},{7,3},{8,12},{9,13},{10,... | collective-permute-start | bytes 147464 | tf_op jit(solution)/shard_map/ppermute | solution.py:348
  63.3 11.8 %copy-start.7 = (bf16[384,256]{1,0:T(8,128)(2,1)S(1)}, bf16[384,256]{1,0:T(8,128)(2,1)}, u32[]{:S(2)}) copy-start(bf16[384,256]{1,0:T(8,128)(2,1)} %refs_1_.12) | copy-start | bytes 589828
  63.3 11.8 %copy-start.22 = (s32[3]{0:T(128)S(1)}, s32[3]{0:T(128)}, u32[]{:S(2)}) copy-start(s32[3]{0:T(128)} %copy-done.21) | copy-start | bytes 40
  63.3 13.0 %copy-start.28 = (f32[128,128]{1,0:T(8,128)S(1)}, f32[128,128]{1,0:T(8,128)}, u32[]{:S(2)}) copy-start(f32[128,128]{1,0:T(8,128)} %copy-done.27) | copy-start | bytes 196612
  63.3 17.8 %copy-start.8 = (bf16[384,256]{1,0:T(8,128)(2,1)S(1)}, bf16[384,256]{1,0:T(8,128)(2,1)}, u32[]{:S(2)}) copy-start(bf16[384,256]{1,0:T(8,128)(2,1)} %refs_2_.5) | copy-start | bytes 589828
  63.3 17.8 %copy-start.9 = (bf16[384,256]{1,0:T(8,128)(2,1)S(1)}, bf16[384,256]{1,0:T(8,128)(2,1)}, u32[]{:S(2)}) copy-start(bf16[384,256]{1,0:T(8,128)(2,1)} %refs_1_.13) | copy-start | bytes 589828
  63.3 17.8 %copy-start.11 = (bf16[4,384,384]{2,1,0:T(8,128)(2,1)S(1)}, bf16[4,384,384]{2,1,0:T(8,128)(2,1)}, u32[]{:S(2)}) copy-start(bf16[4,384,384]{2,1,0:T(8,128)(2,1)} %copy-done.10) | copy-start | bytes 3538948
  63.3 17.8 %copy-start.17 = (f32[128,128]{1,0:T(8,128)S(1)}, f32[128,128]{1,0:T(8,128)}, u32[]{:S(2)}) copy-start(f32[128,128]{1,0:T(8,128)} %copy-done.16) | copy-start | bytes 196612
  63.3 5.2 %collective-permute-start.16 = (bf16[192,128]{1,0:T(8,128)(2,1)S(1)}, bf16[192,128]{1,0:T(8,128)(2,1)S(1)}, u32[]{:S(2)}, u32[]{:S(2)}) collective-permute-start(bf16[192,128]{1,0:T(8,128)(2,1)S(1)} %shard_map.100), channel_id=1, source_target_pairs={{0,2},{1,3},{2,0},{3,1},{4,6},{5,7},{6,4},{7,5},{8,10},{9,11},{10,... | collective-permute-start | bytes 147464 | tf_op jit(solution)/shard_map/ppermute | solution.py:348
  71.5 14.1 %collective-permute-start.20 = (f32[96,2048]{1,0:T(8,128)S(1)}, f32[96,2048]{1,0:T(8,128)S(1)}, u32[]{:S(2)}, u32[]{:S(2)}) collective-permute-start(f32[96,2048]{1,0:T(8,128)S(1)} %get-tuple-element.53), channel_id=1, source_target_pairs={{0,4},{1,5},{2,6},{3,7},{4,0},{5,1},{6,2},{7,3},{8,12},{9,13},{10,... | collective-permute-start | bytes 2359304 | tf_op jit(solution)/shard_map/ppermute | solution.py:348
  71.6 14.0 %collective-permute-start.21 = (f32[96,2048]{1,0:T(8,128)S(1)}, f32[96,2048]{1,0:T(8,128)S(1)}, u32[]{:S(2)}, u32[]{:S(2)}) collective-permute-start(f32[96,2048]{1,0:T(8,128)S(1)} %get-tuple-element.55), channel_id=1, source_target_pairs={{0,4},{1,5},{2,6},{3,7},{4,0},{5,1},{6,2},{7,3},{8,12},{9,13},{10,... | collective-permute-start | bytes 2359304 | tf_op jit(solution)/shard_map/ppermute | solution.py:348
  72.1 3.0 %collective-permute-start.22 = (bf16[192,128]{1,0:T(8,128)(2,1)S(1)}, bf16[192,128]{1,0:T(8,128)(2,1)S(1)}, u32[]{:S(2)}, u32[]{:S(2)}) collective-permute-start(bf16[192,128]{1,0:T(8,128)(2,1)S(1)} %collective-permute-done.16.refs_11_.refs_4_), channel_id=1, source_target_pairs={{0,4},{1,5},{2,6},{3,7},{4,0},{5,1},{6,2},{7,3},{8,12},{9,13},{10,... | collective-permute-start | bytes 147464 | tf_op jit(solution)/shard_map/ppermute | solution.py:348
  76.1 1.3 %collective-permute-start.24 = (f32[128,128]{1,0:T(8,128)S(1)}, f32[128,128]{1,0:T(8,128)S(1)}, u32[]{:S(2)}, u32[]{:S(2)}) collective-permute-start(f32[128,128]{1,0:T(8,128)S(1)} %get-tuple-element.61), channel_id=1, source_target_pairs={{0,4},{1,5},{2,6},{3,7},{4,0},{5,1},{6,2},{7,3},{8,12},{9,13},{10,... | collective-permute-start | bytes 196616 | tf_op jit(solution)/shard_map/ppermute | solution.py:348
  76.3 3.4 %collective-permute-start.23 = (f32[128,128]{1,0:T(8,128)S(1)}, f32[128,128]{1,0:T(8,128)S(1)}, u32[]{:S(2)}, u32[]{:S(2)}) collective-permute-start(f32[128,128]{1,0:T(8,128)S(1)} %copy-done.28), channel_id=1, source_target_pairs={{0,4},{1,5},{2,6},{3,7},{4,0},{5,1},{6,2},{7,3},{8,12},{9,13},{10,... | collective-permute-start | bytes 196616 | tf_op jit(solution)/shard_map/ppermute | solution.py:348
  77.5 6.7 %collective-permute-start.25 = (f32[128,128]{1,0:T(8,128)S(1)}, f32[128,128]{1,0:T(8,128)S(1)}, u32[]{:S(2)}, u32[]{:S(2)}) collective-permute-start(f32[128,128]{1,0:T(8,128)S(1)} %add.15.refs_8_), channel_id=1, source_target_pairs={{0,8},{1,9},{2,10},{3,11},{4,12},{5,13},{6,14},{7,15},{8,0},{9,1},... | collective-permute-start | bytes 196616 | tf_op jit(solution)/shard_map/ppermute | solution.py:348
  78.7 5.4 %collective-permute-start.26 = (f32[128,128]{1,0:T(8,128)S(1)}, f32[128,128]{1,0:T(8,128)S(1)}, u32[]{:S(2)}, u32[]{:S(2)}) collective-permute-start(f32[128,128]{1,0:T(8,128)S(1)} %add.15.refs_8_), channel_id=1, source_target_pairs={{0,16},{1,17},{2,18},{3,19},{4,20},{5,21},{6,22},{7,23},{8,24},{9,... | collective-permute-start | bytes 196616 | tf_op jit(solution)/shard_map/ppermute | solution.py:348
  79.7 5.2 %collective-permute-start.27 = (f32[128,128]{1,0:T(8,128)S(1)}, f32[128,128]{1,0:T(8,128)S(1)}, u32[]{:S(2)}, u32[]{:S(2)}) collective-permute-start(f32[128,128]{1,0:T(8,128)S(1)} %add.15.refs_8_), channel_id=1, source_target_pairs={{0,24},{1,25},{2,26},{3,27},{4,28},{5,29},{6,30},{7,31},{8,16},{9,... | collective-permute-start | bytes 196616 | tf_op jit(solution)/shard_map/ppermute | solution.py:348
  85.5 1.7 %collective-permute-start.28 = (f32[128,128]{1,0:T(8,128)S(1)}, f32[128,128]{1,0:T(8,128)S(1)}, u32[]{:S(2)}, u32[]{:S(2)}) collective-permute-start(f32[128,128]{1,0:T(8,128)S(1)} %get-tuple-element.66), channel_id=1, source_target_pairs={{0,4},{1,5},{2,6},{3,7},{4,0},{5,1},{6,2},{7,3},{8,12},{9,13},{10,... | collective-permute-start | bytes 196616 | tf_op jit(solution)/shard_map/ppermute | solution.py:348
  (11 other events, 7.9 us)

commit v18 on v17

--- a/solution.py
+++ b/solution.py
@@ -415,20 +415,22 @@
     attn = lax.all_to_all(attn, "head", 0, 0, tiled=True)
 
     work = near_and_far if board else by_gathers
-    both, across, joins, starts = work(
+    both, across, mix = work(
         attn, arrived, cotangent, mate_cotangent, out_weight, core, chip, colour, product
     )
-    mixed, done = call(
-        join_kernel, [((own, model), BF16), ((8, DH), F32)], joins, [jnp.stack(starts)]
-    )
-
     g, mine, other = call(
         functools.partial(collect_kernel, scale, count),
         [(flat, BF16), *pair],
         [query, *both, *across],
         [where],
+        linear[1:],
     )
     flags, parts, total = exchange(mine, other, core, chip, chips, True)
+    joins, starts = mix([total])
+    mixed, done = call(
+        join_kernel, [((own, model), BF16), ((8, DH), F32)], joins, [jnp.stack(starts)]
+    )
+
     grad_query, dk, dv = call(
         functools.partial(backward_kernel, scale),
         [(flat, BF16)] + [(flat, F32)] * 2,
@@ -524,37 +526,40 @@
         flops=product // 2,
     )
     both[2] = send(two, 0, -2)
+    across[2] = send(both[2], 1, 0)
 
     def quarter(n):
         return lambda ref, *_: ref.at[2 * DH : 3 * DH, n * wide // 2 : (n + 1) * wide // 2]
 
-    parts = call(
-        halves_kernel,
-        parts * 2,
-        [
-            fetch(attn.shape, (attn, all_of, all_of)),
-            fetch(
-                (4 * DH, wide),
-                (weight, own_columns(0), rows_at(0, DH)),
-                *((arrived[s], all_of, rows_at(s * DH, DH)) for s in (1, 2, 3)),
-            ),
-            fetch(
-                (4 * DH, wide),
-                (weight, own_columns(1), rows_at(0, DH)),
-                (second[1], all_of, rows_at(DH, DH)),
-                (second[3], all_of, rows_at(3 * DH, DH)),
-                *((a, all_of, quarter(n)) for n, a in enumerate(second[2])),
-            ),
-        ],
-        [spots],
-        [both[2], across[0], across[1], across[3]],
-        room=8,
-        flops=4 * product,
-        lazy=True,
-    )
-    joins = [parts[0], send(parts[1], 1, 0), parts[2], send(parts[3], 1, 0)]
-    across[2] = send(both[2], 1, 0)
-    return [both[s] for s in range(4)], [across[s] for s in range(4)], joins, [spots[0], spots[1]]
+    def mix(after):
+        outs = call(
+            halves_kernel,
+            parts * 2,
+            [
+                fetch(attn.shape, (attn, all_of, all_of)),
+                fetch(
+                    (4 * DH, wide),
+                    (weight, own_columns(0), rows_at(0, DH)),
+                    *((arrived[s], all_of, rows_at(s * DH, DH)) for s in (1, 2, 3)),
+                ),
+                fetch(
+                    (4 * DH, wide),
+                    (weight, own_columns(1), rows_at(0, DH)),
+                    (second[1], all_of, rows_at(DH, DH)),
+                    (second[3], all_of, rows_at(3 * DH, DH)),
+                    *((a, all_of, quarter(n)) for n, a in enumerate(second[2])),
+                ),
+            ],
+            [spots],
+            after,
+            room=8,
+            flops=4 * product,
+            lazy=True,
+        )
+        joins = [outs[0], send(outs[1], 1, 0), outs[2], send(outs[3], 1, 0)]
+        return joins, [spots[0], spots[1]]
+
+    return [both[s] for s in range(4)], [across[s] for s in range(4)], mix
 
 
 def by_gathers(attn, arrived, cotangent, mate_cotangent, out_weight, core, chip, colour, product):
@@ -579,15 +584,19 @@
             flops=product,
         )
         both.append(send(block, 0, -s) if s else block)
-    part, mate_part = call(
-        mixed_kernel,
-        [((own, model), F32)] * 2,
-        [attn, *chunks],
-        [lax.axis_index("head").reshape(1)],
-        room=6,
-        flops=count * product,
-    )
-    return both, [send(b, 1, 0) for b in both], [part, send(mate_part, 1, 0)], [jnp.int32(0)]
+    def mix(after):
+        part, mate_part = call(
+            mixed_kernel,
+            [((own, model), F32)] * 2,
+            [attn, *chunks],
+            [lax.axis_index("head").reshape(1)],
+            after,
+            room=16,
+            flops=count * product,
+        )
+        return [part, send(mate_part, 1, 0)], [jnp.int32(0)]
+
+    return both, [send(b, 1, 0) for b in both], mix
 
 
 def solution(mesh):

time: 89.6 us -> 91.2 us (1.018)
  starting transfers between devices: 25 us -> 27.3 us
    ppermute x29, starting transfers between devices: 21 us -> 23.3 us  [send(): return lax.ppermute(x, ('ctx', 'head'), pairs)]
  transfers between devices with their start and end apart: 30 -> 30, of which waited for: 10 -> 13; matrix products, arithmetic and copies ran while one was open for 5% -> 5% of each run, Pallas kernels for 21% -> 17%
where the time goes in v18:
time: 91.2 us; the launch traced here: 90.4 us
  starting transfers between devices  27.3 us (30%)
  Pallas kernels  23 us (25%)
  waiting for transfers between devices  22.2 us (24%)
  local copies, waits for them, and re-layouts  14.5 us (16%)
  other arithmetic  2.46 us (3%)
  between operations  0.95 us (1%)
    ppermute x29, starting transfers between devices, send(): return lax.ppermute(x, ('ctx', 'head'), pairs)  23.3 us
    pallas_call x12, Pallas kernels, call(): pl.pallas_call(kernel, out_shape=[jax.ShapeDtypeStruct(s, t) for s, t in...  23 us
    ppermute x29, waiting for transfers between devices, send(): return lax.ppermute(x, ('ctx', 'head'), pairs)  22.2 us
    unnamed x58, local copies, waits for them, and re-layouts  12.7 us
    all_to_all x1, starting transfers between devices, on_device(): attn = lax.all_to_all(attn, 'head', 0, 0, tiled=True)  3.99 us
    dynamic_slice x1, local copies, waits for them, and re-layouts, on_device(): lax.dynamic_slice(out_weight, (core * DH, colour * wide), (DH, wide))  1.88 us
  transfers between devices with their start and end apart: 30, of which 13 were waited for; matrix products, arithmetic and copies ran while one was open for 5% of the time, Pallas kernels for 17%

profile of v18, /device:TPU:0, one launch (start us, length us, event | category | flops | bytes accessed | tf_op | source)
XLA Modules:
  0.0 90.4 jit_solution(15604091546519575412)
XLA Ops:
  1.2 1.9 %dynamic_slice.3 = bf16[128,2048]{1,0:T(8,128)(2,1)} dynamic-slice(bf16[256,4096]{1,0:T(8,128)(2,1)} %refs_6_.1, s32[]{:T(128)S(6)} %select_n.6, s32[]{:T(128)S(6)} %select_n.7), dynamic_slice_sizes={128,2048} | dynamic-slice | bytes 1048580 | tf_op jit(solution)/shard_map/dynamic_slice | solution.py:388
  3.0 4.6 %collective-permute-start.8 = (bf16[128,2048]{1,0:T(8,128)(2,1)}, bf16[128,2048]{1,0:T(8,128)(2,1)S(1)}, u32[]{:S(2)}, u32[]{:S(2)}) collective-permute-start(bf16[128,2048]{1,0:T(8,128)(2,1)} %dynamic_slice.3), channel_id=1, source_target_pairs={{0,3},{1,0},{2,1},{3,2},{4,7},{5,4},{6,5},{7,6},{8,11},{9,8},{10,9... | collective-permute-start | bytes 1572872 | tf_op jit(solution)/shard_map/ppermute | solution.py:348
  7.8 1.2 %pad_maximum_fusion.refs_2_ = bf16[3,384,256]{2,1,0:T(8,128)(2,1)S(1)} fusion(bf16[1,384,256]{2,1,0:T(8,128)(2,1)} %bitcast.18, bf16[1,384,256]{2,1,0:T(8,128)(2,1)} %bitcast.19, bf16[1,384,256]{2,1,0:T(8,128)(2,1)} %bitcast.17), kind=kLoop, calls=%fused_computation | loop fusion | flops 589824 | bytes 1179648 | tf_op jit(solution)/shard_map/stack | solution.py:398
  9.0 2.6 %shard_map.93 = (bf16[4,384,384]{2,1,0:T(8,128)(2,1)S(1)}, f32[384,128]{1,0:T(8,128)S(1)}, f32[384,128]{1,0:T(8,128)}, bf16[384,128]{1,0:T(8,128)(2,1)}, f32[128,128]{1,0:T(8,128)S(1)}, /*index=5*/f32[128,128]{1,0:T(8,128)}) custom-call(s32[3,3]{1,0:T(4,128)S(1)} %copy-done.26, s32[3]{0:T(128)S(1)} %pad_add_fusion.2.refs_1_.refs_0_, ...), custom_call_target="tpu_custom_call" | custom-call | flops 264241152 | bytes 2392064 | tf_op jit(solution)/shard_map/pallas_call | solution.py:103
  11.5 1.1 %copy-done.10 = bf16[4,384,384]{2,1,0:T(8,128)(2,1)} copy-done((bf16[4,384,384]{2,1,0:T(8,128)(2,1)}, bf16[4,384,384]{2,1,0:T(8,128)(2,1)S(1)}, u32[]{:S(2)}) %copy-start.10) | copy-done | bytes 1179672
  13.2 0.7 copy-done.18
  14.6 1.1 %collective-permute-done.1.refs_1_.refs_8_ = bf16[384,128]{1,0:T(8,128)(2,1)S(1)} collective-permute-done((bf16[384,128]{1,0:T(8,128)(2,1)}, bf16[384,128]{1,0:T(8,128)(2,1)S(1)}, u32[]{:S(2)}, u32[]{:S(2)}) %collective-permute-start.1) | collective-permute-done | bytes 98336 | tf_op jit(solution)/shard_map/ppermute | solution.py:348
  15.7 0.6 copy-done.14
  16.3 0.9 add.12
  17.2 2.5 %collective-permute-start.6 = (f32[128,128]{1,0:T(8,128)S(1)}, f32[128,128]{1,0:T(8,128)S(1)}, u32[]{:S(2)}, u32[]{:S(2)}) collective-permute-start(f32[128,128]{1,0:T(8,128)S(1)} %add.12), channel_id=1, source_target_pairs={{0,24},{1,25},{2,26},{3,27},{4,28},{5,29},{6,30},{7,31},{8,16},{9,... | collective-permute-start | bytes 196616 | tf_op jit(solution)/shard_map/ppermute | solution.py:348
  20.8 1.6 %collective-permute-done.6.refs_6_ = f32[128,128]{1,0:T(8,128)S(1)} collective-permute-done((f32[128,128]{1,0:T(8,128)S(1)}, f32[128,128]{1,0:T(8,128)S(1)}, u32[]{:S(2)}, u32[]{:S(2)}) %collective-permute-start.6) | collective-permute-done | bytes 65568 | tf_op jit(solution)/shard_map/ppermute | solution.py:348
  22.5 1.5 %collective-permute-done.5.refs_5_ = f32[128,128]{1,0:T(8,128)S(1)} collective-permute-done((f32[128,128]{1,0:T(8,128)S(1)}, f32[128,128]{1,0:T(8,128)S(1)}, u32[]{:S(2)}, u32[]{:S(2)}) %collective-permute-start.5) | collective-permute-done | bytes 65568 | tf_op jit(solution)/shard_map/ppermute | solution.py:348
  24.5 0.9 %copy-done.6 = bf16[384,256]{1,0:T(8,128)(2,1)S(1)} copy-done((bf16[384,256]{1,0:T(8,128)(2,1)S(1)}, bf16[384,256]{1,0:T(8,128)(2,1)}, u32[]{:S(2)}) %copy-start.6) | copy-done | bytes 196632
  25.4 0.8 copy-done.13
  26.3 0.9 copy-done.15
  27.2 0.9 %copy-done.19 = f32[384,128]{1,0:T(8,128)S(1)} copy-done((f32[384,128]{1,0:T(8,128)S(1)}, f32[384,128]{1,0:T(8,128)}, u32[]{:S(2)}) %copy-start.19) | copy-done | bytes 196632
  28.1 1.2 %shard_map.95 = (bf16[4,192,128]{2,1,0:T(8,128)(2,1)S(1)}, f32[128,128]{1,0:T(8,128)S(1)}, f32[128,128]{1,0:T(8,128)S(1)}) custom-call(s32[4]{0:T(128)S(1)} %add_convert_fusion.refs_0_, s32[3]{0:T(128)S(1)} %pad_add_fusion.2.refs_1_.refs_0_, f32[128,128]{1,0:T(8,128)S(1)} %copy-done.13, f32[128,128]{1,0:T(8,128)} %collective-permute-done.3.refs_3_, ...), custom_call_target="tpu_custom_call" | custom-call | flops 1 | bytes 1343488 | tf_op jit(solution)/shard_map/pallas_call | solution.py:103
  30.0 0.6 copy-done.27
  30.6 0.7 copy-done.20
  31.3 0.7 collective-permute-done.7.refs_0_
  32.1 1.5 %collective-permute-start.11 = (bf16[128,2048]{1,0:T(8,128)(2,1)}, bf16[128,2048]{1,0:T(8,128)(2,1)}, u32[]{:S(2)}, u32[]{:S(2)}) collective-permute-start(bf16[128,2048]{1,0:T(8,128)(2,1)} %get-tuple-element.45.refs_5_), channel_id=1, source_target_pairs={{0,16},{1,17},{2,18},{3,19},{4,20},{5,21},{6,22},{7,23},{8,24},{9,... | collective-permute-start | bytes 1572872 | tf_op jit(solution)/shard_map/ppermute | solution.py:348
  33.6 1.4 %collective-permute-start.10 = (bf16[128,2048]{1,0:T(8,128)(2,1)}, bf16[128,2048]{1,0:T(8,128)(2,1)}, u32[]{:S(2)}, u32[]{:S(2)}) collective-permute-start(bf16[128,2048]{1,0:T(8,128)(2,1)} %get-tuple-element.44.refs_4_.refs_3_), channel_id=1, source_target_pairs={{0,8},{1,9},{2,10},{3,11},{4,12},{5,13},{6,14},{7,15},{8,0},{9,1},... | collective-permute-start | bytes 1572872 | tf_op jit(solution)/shard_map/ppermute | solution.py:348
  35.0 1.6 %collective-permute-start.9 = (bf16[128,2048]{1,0:T(8,128)(2,1)}, bf16[128,2048]{1,0:T(8,128)(2,1)S(1)}, u32[]{:S(2)}, u32[]{:S(2)}) collective-permute-start(bf16[128,2048]{1,0:T(8,128)(2,1)} %get-tuple-element.44.refs_4_.refs_3_), channel_id=1, source_target_pairs={{0,1},{1,2},{2,3},{3,0},{4,5},{5,6},{6,7},{7,4},{8,9},{9,10},{10,1... | collective-permute-start | bytes 1572872 | tf_op jit(solution)/shard_map/ppermute | solution.py:348
  36.7 4.0 %all-to-all-start = ((bf16[4,192,128]{2,1,0:T(8,128)(2,1)}), bf16[4,192,128]{2,1,0:T(8,128)(2,1)}, u32[]{:S(2)}, u32[]{:S(2)}) async-start(bf16[4,192,128]{2,1,0:T(8,128)(2,1)} %copy-done.20), calls=%async_computation | async-start | bytes 393216 | tf_op jit(solution)/shard_map/all_to_all | solution.py:415
  40.7 1.1 %copy-done.1 = bf16[96,4096]{1,0:T(8,128)(2,1)S(1)} copy-done((bf16[96,4096]{1,0:T(8,128)(2,1)S(1)}, bf16[96,4096]{1,0:T(8,128)(2,1)}, u32[]{:S(2)}) %copy-start.1) | copy-done | bytes 786456
  41.8 1.0 %copy-done.4 = bf16[128,2048]{1,0:T(8,128)(2,1)S(1)} copy-done((bf16[128,2048]{1,0:T(8,128)(2,1)S(1)}, bf16[128,2048]{1,0:T(8,128)(2,1)}, u32[]{:S(2)}) %copy-start.4) | copy-done | bytes 524312
  42.9 2.5 %shard_map.97 = (bf16[192,128]{1,0:T(8,128)(2,1)S(1)}, f32[192,256]{1,0:T(8,128)S(1)}) custom-call(s32[4]{0:T(128)S(1)} %pad_add_fusion.1.refs_0_, bf16[96,4096]{1,0:T(8,128)(2,1)S(1)} %copy-done.1, bf16[96,4096]{1,0:T(8,128)(2,1)S(1)} %collective-permute-done.refs_3_.refs_2_, bf16[256,4096]{1,0:T(8,128)(2,1)S(1)} %copy-done, ...), custom_call_target="tpu_custom_call" | custom-call | flops 402653184 | bytes 4964352 | tf_op jit(solution)/shard_map/pallas_call | solution.py:103
  45.8 1.2 %collective-permute-done.10.refs_3_.refs_7_ = bf16[128,2048]{1,0:T(8,128)(2,1)} collective-permute-done((bf16[128,2048]{1,0:T(8,128)(2,1)}, bf16[128,2048]{1,0:T(8,128)(2,1)}, u32[]{:S(2)}, u32[]{:S(2)}) %collective-permute-start.10) | collective-permute-done | bytes 524320 | tf_op jit(solution)/shard_map/ppermute | solution.py:348
  47.0 4.6 %collective-permute-done.9.refs_6_.refs_3_.refs_4_ = bf16[128,2048]{1,0:T(8,128)(2,1)S(1)} collective-permute-done((bf16[128,2048]{1,0:T(8,128)(2,1)}, bf16[128,2048]{1,0:T(8,128)(2,1)S(1)}, u32[]{:S(2)}, u32[]{:S(2)}) %collective-permute-start.9) | collective-permute-done | bytes 524320 | tf_op jit(solution)/shard_map/ppermute | solution.py:348
  51.6 3.1 %shard_map.98 = (bf16[192,128]{1,0:T(8,128)(2,1)}, bf16[192,128]{1,0:T(8,128)(2,1)}, bf16[128,1024]{1,0:T(8,128)(2,1)}, bf16[128,1024]{1,0:T(8,128)(2,1)}) custom-call(s32[4]{0:T(128)S(1)} %pad_add_fusion.1.refs_0_, bf16[96,4096]{1,0:T(8,128)(2,1)S(1)} %copy-done.1, bf16[96,4096]{1,0:T(8,128)(2,1)S(1)} %collective-permute-done.refs_3_.refs_2_, ...), custom_call_target="tpu_custom_call" | custom-call | flops 201326592 | bytes 3964928 | tf_op jit(solution)/shard_map/pallas_call | solution.py:103
  54.7 0.9 collective-permute-start.12
  55.9 2.7 %collective-permute-start.14 = (bf16[192,128]{1,0:T(8,128)(2,1)}, bf16[192,128]{1,0:T(8,128)(2,1)S(1)}, u32[]{:S(2)}, u32[]{:S(2)}) collective-permute-start(bf16[192,128]{1,0:T(8,128)(2,1)} %get-tuple-element.50), channel_id=1, source_target_pairs={{0,3},{1,0},{2,1},{3,2},{4,7},{5,4},{6,5},{7,6},{8,11},{9,8},{10,9... | collective-permute-start | bytes 147464 | tf_op jit(solution)/shard_map/ppermute | solution.py:348
  58.6 1.1 %copy-done.2 = bf16[96,4096]{1,0:T(8,128)(2,1)S(1)} copy-done((bf16[96,4096]{1,0:T(8,128)(2,1)S(1)}, bf16[96,4096]{1,0:T(8,128)(2,1)}, u32[]{:S(2)}) %copy-start.2) | copy-done | bytes 786456
  59.7 0.7 copy-done.24
  60.4 1.0 %shard_map.99.refs_5_ = f32[192,128]{1,0:T(8,128)S(1)} custom-call(s32[4]{0:T(128)S(1)} %copy-done.24, bf16[96,4096]{1,0:T(8,128)(2,1)S(1)} %copy-done.2, bf16[96,4096]{1,0:T(8,128)(2,1)S(1)} %collective-permute-done.refs_3_.refs_2_, bf16[128,2048]{1,0:T(8,128)(2,1)S(1)} %collective-permute-done.9.refs_6_.refs_3_.refs_4_, ...), custom_call_target="tpu_custom_call" | custom-call | flops 100663296 | bytes 2195456 | tf_op jit(solution)/shard_map/pallas_call | solution.py:103
  61.5 3.5 %collective-permute-done.15.refs_7_.refs_5_ = bf16[192,128]{1,0:T(8,128)(2,1)S(1)} collective-permute-done((bf16[192,128]{1,0:T(8,128)(2,1)}, bf16[192,128]{1,0:T(8,128)(2,1)S(1)}, u32[]{:S(2)}, u32[]{:S(2)}) %collective-permute-start.15) | collective-permute-done | bytes 49184 | tf_op jit(solution)/shard_map/ppermute | solution.py:348
  65.0 2.0 %shard_map.100 = bf16[192,128]{1,0:T(8,128)(2,1)S(1)} custom-call(s32[4]{0:T(128)S(1)} %copy-done.25, bf16[96,4096]{1,0:T(8,128)(2,1)S(1)} %copy-done.2, bf16[96,4096]{1,0:T(8,128)(2,1)S(1)} %collective-permute-done.refs_3_.refs_2_, bf16[128,1024]{1,0:T(8,128)(2,1)} %collective-permute-done.12.refs_3_.refs_9_, ...), custom_call_target="tpu_custom_call" | custom-call | flops 100663296 | bytes 2244608 | tf_op jit(solution)/shard_map/pallas_call | solution.py:103
  68.2 3.9 %collective-permute-done.16.refs_4_ = bf16[192,128]{1,0:T(8,128)(2,1)S(1)} collective-permute-done((bf16[192,128]{1,0:T(8,128)(2,1)S(1)}, bf16[192,128]{1,0:T(8,128)(2,1)S(1)}, u32[]{:S(2)}, u32[]{:S(2)}) %collective-permute-start.16) | collective-permute-done | bytes 49184 | tf_op jit(solution)/shard_map/ppermute | solution.py:348
  72.1 1.2 %collective-permute-done.19.refs_8_ = bf16[192,128]{1,0:T(8,128)(2,1)S(1)} collective-permute-done((bf16[192,128]{1,0:T(8,128)(2,1)S(1)}, bf16[192,128]{1,0:T(8,128)(2,1)S(1)}, u32[]{:S(2)}, u32[]{:S(2)}) %collective-permute-start.19) | collective-permute-done | bytes 49184 | tf_op jit(solution)/shard_map/ppermute | solution.py:348
  73.4 0.8 shard_map.101
  74.4 1.1 %collective-permute-done.22.refs_2_ = f32[128,128]{1,0:T(8,128)S(1)} collective-permute-done((f32[128,128]{1,0:T(8,128)S(1)}, f32[128,128]{1,0:T(8,128)S(1)}, u32[]{:S(2)}, u32[]{:S(2)}) %collective-permute-start.22) | collective-permute-done | bytes 65568 | tf_op jit(solution)/shard_map/ppermute | solution.py:348
  75.5 3.0 %shard_map.102 = (f32[96,2048]{1,0:T(8,128)S(1)}, f32[96,2048]{1,0:T(8,128)S(1)}, f32[96,2048]{1,0:T(8,128)S(1)}, f32[96,2048]{1,0:T(8,128)S(1)}) custom-call(s32[4]{0:T(128)S(1)} %copy-done.25, bf16[4,192,128]{2,1,0:T(8,128)(2,1)} %all-to-all-done.refs_4_.refs_1_, bf16[256,4096]{1,0:T(8,128)(2,1)S(1)} %copy-done, ...), custom_call_target="tpu_custom_call" | custom-call | flops 805306368 | bytes 10682368 | tf_op jit(solution)/shard_map/pallas_call | solution.py:103
  79.1 1.4 %collective-permute-start.27 = (f32[128,128]{1,0:T(8,128)S(1)}, f32[128,128]{1,0:T(8,128)S(1)}, u32[]{:S(2)}, u32[]{:S(2)}) collective-permute-start(f32[128,128]{1,0:T(8,128)S(1)} %add.15.refs_11_.refs_8_), channel_id=1, source_target_pairs={{0,24},{1,25},{2,26},{3,27},{4,28},{5,29},{6,30},{7,31},{8,16},{9,... | collective-permute-start | bytes 196616 | tf_op jit(solution)/shard_map/ppermute | solution.py:348
  80.5 1.7 %collective-permute-start.26 = (f32[128,128]{1,0:T(8,128)S(1)}, f32[128,128]{1,0:T(8,128)S(1)}, u32[]{:S(2)}, u32[]{:S(2)}) collective-permute-start(f32[128,128]{1,0:T(8,128)S(1)} %add.15.refs_11_.refs_8_), channel_id=1, source_target_pairs={{0,16},{1,17},{2,18},{3,19},{4,20},{5,21},{6,22},{7,23},{8,24},{9,... | collective-permute-start | bytes 196616 | tf_op jit(solution)/shard_map/ppermute | solution.py:348
  82.7 3.0 %shard_map.104 = (bf16[384,256]{1,0:T(8,128)(2,1)}, f32[384,256]{1,0:T(8,128)S(1)}, f32[384,256]{1,0:T(8,128)S(1)}) custom-call(s32[3]{0:T(128)S(1)} %copy-done.22, bf16[384,256]{1,0:T(8,128)(2,1)S(1)} %copy-done.7, bf16[384,256]{1,0:T(8,128)(2,1)S(1)} %copy-done.9, bf16[384,256]{1,0:T(8,128)(2,1)S(1)} %copy-done.8, ...), custom_call_target="tpu_custom_call" | custom-call | flops 528482304 | bytes 3080192 | tf_op jit(solution)/shard_map/pallas_call | solution.py:103
  85.7 0.8 collective-permute-done.25.refs_3_
  87.2 1.6 %shard_map.103 = (bf16[96,4096]{1,0:T(8,128)(2,1)}, f32[8,128]{1,0:T(8,128)S(1)}) custom-call(s32[2]{0:T(128)S(1)} %pad_add_fusion.refs_0_, f32[96,2048]{1,0:T(8,128)S(1)} %get-tuple-element.55.refs_1_, f32[96,2048]{1,0:T(8,128)S(1)} %collective-permute-done.23.refs_2_, f32[96,2048]{1,0:T(8,128)S(1)} %get-tuple-element.57.refs_3_, ...), custom_call_target="tpu_custom_call" | custom-call | flops 1 | bytes 3936256 | tf_op jit(solution)/shard_map/pallas_call | solution.py:103
  88.8 1.6 %shard_map.106 = (bf16[384,256]{1,0:T(8,128)(2,1)}, bf16[384,256]{1,0:T(8,128)(2,1)}) custom-call(s32[3]{0:T(128)S(1)} %copy-done.22, bf16[384,256]{1,0:T(8,128)(2,1)S(1)} %copy-done.9, bf16[384,256]{1,0:T(8,128)(2,1)S(1)} %copy-done.8, f32[384,256]{1,0:T(8,128)S(1)} %get-tuple-element.63.refs_6_.refs_3_, f32[384,256]{1,0:T(8,128)S(1)} %get-tuple-element.64.refs_4_, ...), custom_call_target="tpu_custom_call" | custom-call | flops 1 | bytes 1703936 | tf_op jit(solution)/shard_map/pallas_call | solution.py:103
  (93 shorter events, 8.3 us)
Async XLA Ops:
  0.6 8.3 %copy-start.26 = (s32[3,3]{1,0:T(4,128)S(1)}, s32[3,3]{1,0:T(4,128)}, u32[]{:S(2)}) copy-start(s32[3,3]{1,0:T(4,128)} %refs_0_.1) | copy-start | bytes 112
  0.6 8.3 %collective-permute-start = (bf16[96,4096]{1,0:T(8,128)(2,1)}, bf16[96,4096]{1,0:T(8,128)(2,1)S(1)}, u32[]{:S(2)}, u32[]{:S(2)}) collective-permute-start(bf16[96,4096]{1,0:T(8,128)(2,1)} %refs_1_.10), channel_id=1, source_target_pairs={{0,4},{1,5},{2,6},{3,7},{4,0},{5,1},{6,2},{7,3},{8,12},{9,13},{10,... | collective-permute-start | bytes 2359304 | tf_op jit(solution)/shard_map/ppermute | solution.py:348
  3.0 27.6 %collective-permute-start.8 = (bf16[128,2048]{1,0:T(8,128)(2,1)}, bf16[128,2048]{1,0:T(8,128)(2,1)S(1)}, u32[]{:S(2)}, u32[]{:S(2)}) collective-permute-start(bf16[128,2048]{1,0:T(8,128)(2,1)} %dynamic_slice.3), channel_id=1, source_target_pairs={{0,3},{1,0},{2,1},{3,2},{4,7},{5,4},{6,5},{7,6},{8,11},{9,8},{10,9... | collective-permute-start | bytes 1572872 | tf_op jit(solution)/shard_map/ppermute | solution.py:348
  7.7 24.3 %collective-permute-start.7 = (bf16[128,2048]{1,0:T(8,128)(2,1)}, bf16[128,2048]{1,0:T(8,128)(2,1)}, u32[]{:S(2)}, u32[]{:S(2)}) collective-permute-start(bf16[128,2048]{1,0:T(8,128)(2,1)} %dynamic_slice.3), channel_id=1, source_target_pairs={{0,1},{1,2},{2,3},{3,0},{4,5},{5,6},{6,7},{7,4},{8,9},{9,10},{10,1... | collective-permute-start | bytes 1572872 | tf_op jit(solution)/shard_map/ppermute | solution.py:348
  7.8 21.6 %copy-start.21 = (s32[3]{0:T(128)}, s32[3]{0:T(128)S(1)}, u32[]{:S(2)}) copy-start(s32[3]{0:T(128)S(1)} %pad_add_fusion.2.refs_1_.refs_0_) | copy-start | bytes 40
  8.9 31.7 %copy-start = (bf16[256,4096]{1,0:T(8,128)(2,1)S(1)}, bf16[256,4096]{1,0:T(8,128)(2,1)}, u32[]{:S(2)}) copy-start(bf16[256,4096]{1,0:T(8,128)(2,1)} %refs_6_.1) | copy-start | bytes 6291460
  11.5 1.1 %copy-start.10 = (bf16[4,384,384]{2,1,0:T(8,128)(2,1)}, bf16[4,384,384]{2,1,0:T(8,128)(2,1)S(1)}, u32[]{:S(2)}) copy-start(bf16[4,384,384]{2,1,0:T(8,128)(2,1)S(1)} %get-tuple-element.61.refs_5_) | copy-start | bytes 3538948
  13.9 1.8 %collective-permute-start.2 = (f32[384,128]{1,0:T(8,128)}, f32[384,128]{1,0:T(8,128)}, u32[]{:S(2)}, u32[]{:S(2)}) collective-permute-start(f32[384,128]{1,0:T(8,128)} %get-tuple-element.39), channel_id=1, source_target_pairs={{0,4},{1,5},{2,6},{3,7},{4,0},{5,1},{6,2},{7,3},{8,12},{9,13},{10,... | collective-permute-start | bytes 589832 | tf_op jit(solution)/shard_map/ppermute | solution.py:348
  14.1 1.6 %collective-permute-start.1 = (bf16[384,128]{1,0:T(8,128)(2,1)}, bf16[384,128]{1,0:T(8,128)(2,1)S(1)}, u32[]{:S(2)}, u32[]{:S(2)}) collective-permute-start(bf16[384,128]{1,0:T(8,128)(2,1)} %get-tuple-element.38), channel_id=1, source_target_pairs={{0,4},{1,5},{2,6},{3,7},{4,0},{5,1},{6,2},{7,3},{8,12},{9,13},{10,... | collective-permute-start | bytes 294920 | tf_op jit(solution)/shard_map/ppermute | solution.py:348
  14.4 1.9 %collective-permute-start.3 = (f32[128,128]{1,0:T(8,128)}, f32[128,128]{1,0:T(8,128)}, u32[]{:S(2)}, u32[]{:S(2)}) collective-permute-start(f32[128,128]{1,0:T(8,128)} %get-tuple-element.40), channel_id=1, source_target_pairs={{0,4},{1,5},{2,6},{3,7},{4,0},{5,1},{6,2},{7,3},{8,12},{9,13},{10,... | collective-permute-start | bytes 196616 | tf_op jit(solution)/shard_map/ppermute | solution.py:348
  17.2 5.2 %collective-permute-start.6 = (f32[128,128]{1,0:T(8,128)S(1)}, f32[128,128]{1,0:T(8,128)S(1)}, u32[]{:S(2)}, u32[]{:S(2)}) collective-permute-start(f32[128,128]{1,0:T(8,128)S(1)} %add.12), channel_id=1, source_target_pairs={{0,24},{1,25},{2,26},{3,27},{4,28},{5,29},{6,30},{7,31},{8,16},{9,... | collective-permute-start | bytes 196616 | tf_op jit(solution)/shard_map/ppermute | solution.py:348
  19.7 4.3 %collective-permute-start.5 = (f32[128,128]{1,0:T(8,128)S(1)}, f32[128,128]{1,0:T(8,128)S(1)}, u32[]{:S(2)}, u32[]{:S(2)}) collective-permute-start(f32[128,128]{1,0:T(8,128)S(1)} %add.12), channel_id=1, source_target_pairs={{0,16},{1,17},{2,18},{3,19},{4,20},{5,21},{6,22},{7,23},{8,24},{9,... | collective-permute-start | bytes 196616 | tf_op jit(solution)/shard_map/ppermute | solution.py:348
  20.2 4.3 %collective-permute-start.4 = (f32[128,128]{1,0:T(8,128)S(1)}, f32[128,128]{1,0:T(8,128)S(1)}, u32[]{:S(2)}, u32[]{:S(2)}) collective-permute-start(f32[128,128]{1,0:T(8,128)S(1)} %add.12), channel_id=1, source_target_pairs={{0,8},{1,9},{2,10},{3,11},{4,12},{5,13},{6,14},{7,15},{8,0},{9,1},... | collective-permute-start | bytes 196616 | tf_op jit(solution)/shard_map/ppermute | solution.py:348
  24.5 0.9 %copy-start.6 = (bf16[384,256]{1,0:T(8,128)(2,1)S(1)}, bf16[384,256]{1,0:T(8,128)(2,1)}, u32[]{:S(2)}) copy-start(bf16[384,256]{1,0:T(8,128)(2,1)} %refs_1_.12) | copy-start | bytes 589828
  32.1 13.7 %collective-permute-start.11 = (bf16[128,2048]{1,0:T(8,128)(2,1)}, bf16[128,2048]{1,0:T(8,128)(2,1)}, u32[]{:S(2)}, u32[]{:S(2)}) collective-permute-start(bf16[128,2048]{1,0:T(8,128)(2,1)} %get-tuple-element.45.refs_5_), channel_id=1, source_target_pairs={{0,16},{1,17},{2,18},{3,19},{4,20},{5,21},{6,22},{7,23},{8,24},{9,... | collective-permute-start | bytes 1572872 | tf_op jit(solution)/shard_map/ppermute | solution.py:348
  33.6 13.4 %collective-permute-start.10 = (bf16[128,2048]{1,0:T(8,128)(2,1)}, bf16[128,2048]{1,0:T(8,128)(2,1)}, u32[]{:S(2)}, u32[]{:S(2)}) collective-permute-start(bf16[128,2048]{1,0:T(8,128)(2,1)} %get-tuple-element.44.refs_4_.refs_3_), channel_id=1, source_target_pairs={{0,8},{1,9},{2,10},{3,11},{4,12},{5,13},{6,14},{7,15},{8,0},{9,1},... | collective-permute-start | bytes 1572872 | tf_op jit(solution)/shard_map/ppermute | solution.py:348
  35.0 16.6 %collective-permute-start.9 = (bf16[128,2048]{1,0:T(8,128)(2,1)}, bf16[128,2048]{1,0:T(8,128)(2,1)S(1)}, u32[]{:S(2)}, u32[]{:S(2)}) collective-permute-start(bf16[128,2048]{1,0:T(8,128)(2,1)} %get-tuple-element.44.refs_4_.refs_3_), channel_id=1, source_target_pairs={{0,1},{1,2},{2,3},{3,0},{4,5},{5,6},{6,7},{7,4},{8,9},{9,10},{10,1... | collective-permute-start | bytes 1572872 | tf_op jit(solution)/shard_map/ppermute | solution.py:348
  36.7 14.9 %copy-start.23 = (s32[4]{0:T(128)}, s32[4]{0:T(128)S(1)}, u32[]{:S(2)}) copy-start(s32[4]{0:T(128)S(1)} %pad_add_fusion.1.refs_0_) | copy-start | bytes 52
  36.7 21.9 %all-to-all-start = ((bf16[4,192,128]{2,1,0:T(8,128)(2,1)}), bf16[4,192,128]{2,1,0:T(8,128)(2,1)}, u32[]{:S(2)}, u32[]{:S(2)}) async-start(bf16[4,192,128]{2,1,0:T(8,128)(2,1)} %copy-done.20), calls=%async_computation | async-start | bytes 393216 | tf_op jit(solution)/shard_map/all_to_all | solution.py:415
  40.7 1.1 %copy-start.1 = (bf16[96,4096]{1,0:T(8,128)(2,1)S(1)}, bf16[96,4096]{1,0:T(8,128)(2,1)}, u32[]{:S(2)}) copy-start(bf16[96,4096]{1,0:T(8,128)(2,1)} %refs_1_.10) | copy-start | bytes 2359300
  41.8 1.0 %copy-start.4 = (bf16[128,2048]{1,0:T(8,128)(2,1)S(1)}, bf16[128,2048]{1,0:T(8,128)(2,1)}, u32[]{:S(2)}) copy-start(bf16[128,2048]{1,0:T(8,128)(2,1)} %get-tuple-element.45.refs_5_) | copy-start | bytes 1572868
  54.7 10.3 %collective-permute-start.12 = (bf16[128,1024]{1,0:T(8,128)(2,1)}, bf16[128,1024]{1,0:T(8,128)(2,1)}, u32[]{:S(2)}, u32[]{:S(2)}) collective-permute-start(bf16[128,1024]{1,0:T(8,128)(2,1)} %get-tuple-element.47), channel_id=1, source_target_pairs={{0,8},{1,9},{2,10},{3,11},{4,12},{5,13},{6,14},{7,15},{8,0},{9,1},... | collective-permute-start | bytes 786440 | tf_op jit(solution)/shard_map/ppermute | solution.py:348
  55.6 9.4 %collective-permute-start.13 = (bf16[128,1024]{1,0:T(8,128)(2,1)}, bf16[128,1024]{1,0:T(8,128)(2,1)}, u32[]{:S(2)}, u32[]{:S(2)}) collective-permute-start(bf16[128,1024]{1,0:T(8,128)(2,1)} %get-tuple-element.48), channel_id=1, source_target_pairs={{0,16},{1,17},{2,18},{3,19},{4,20},{5,21},{6,22},{7,23},{8,24},{9,... | collective-permute-start | bytes 786440 | tf_op jit(solution)/shard_map/ppermute | solution.py:348
  55.9 5.6 %collective-permute-start.14 = (bf16[192,128]{1,0:T(8,128)(2,1)}, bf16[192,128]{1,0:T(8,128)(2,1)S(1)}, u32[]{:S(2)}, u32[]{:S(2)}) collective-permute-start(bf16[192,128]{1,0:T(8,128)(2,1)} %get-tuple-element.50), channel_id=1, source_target_pairs={{0,3},{1,0},{2,1},{3,2},{4,7},{5,4},{6,5},{7,6},{8,11},{9,8},{10,9... | collective-permute-start | bytes 147464 | tf_op jit(solution)/shard_map/ppermute | solution.py:348
  58.6 6.4 %collective-permute-start.15 = (bf16[192,128]{1,0:T(8,128)(2,1)}, bf16[192,128]{1,0:T(8,128)(2,1)S(1)}, u32[]{:S(2)}, u32[]{:S(2)}) collective-permute-start(bf16[192,128]{1,0:T(8,128)(2,1)} %get-tuple-element.51), channel_id=1, source_target_pairs={{0,1},{1,2},{2,3},{3,0},{4,5},{5,6},{6,7},{7,4},{8,9},{9,10},{10,1... | collective-permute-start | bytes 147464 | tf_op jit(solution)/shard_map/ppermute | solution.py:348
  58.6 1.1 %copy-start.2 = (bf16[96,4096]{1,0:T(8,128)(2,1)S(1)}, bf16[96,4096]{1,0:T(8,128)(2,1)}, u32[]{:S(2)}) copy-start(bf16[96,4096]{1,0:T(8,128)(2,1)} %refs_1_.10) | copy-start | bytes 2359300
  60.4 4.6 %copy-start.25 = (s32[4]{0:T(128)S(1)}, s32[4]{0:T(128)}, u32[]{:S(2)}) copy-start(s32[4]{0:T(128)} %copy-done.23) | copy-start | bytes 52
  60.4 6.8 %copy-start.28 = (f32[128,128]{1,0:T(8,128)S(1)}, f32[128,128]{1,0:T(8,128)}, u32[]{:S(2)}) copy-start(f32[128,128]{1,0:T(8,128)} %copy-done.27) | copy-start | bytes 196612
  60.4 13.0 %copy-start.7 = (bf16[384,256]{1,0:T(8,128)(2,1)S(1)}, bf16[384,256]{1,0:T(8,128)(2,1)}, u32[]{:S(2)}) copy-start(bf16[384,256]{1,0:T(8,128)(2,1)} %refs_1_.12) | copy-start | bytes 589828
  60.4 13.0 %copy-start.22 = (s32[3]{0:T(128)S(1)}, s32[3]{0:T(128)}, u32[]{:S(2)}) copy-start(s32[3]{0:T(128)} %copy-done.21) | copy-start | bytes 40
  61.4 14.0 %copy-start.5 = (bf16[128,2048]{1,0:T(8,128)(2,1)S(1)}, bf16[128,2048]{1,0:T(8,128)(2,1)}, u32[]{:S(2)}) copy-start(bf16[128,2048]{1,0:T(8,128)(2,1)} %get-tuple-element.45.refs_5_) | copy-start | bytes 1572868
  67.1 5.1 %collective-permute-start.16 = (bf16[192,128]{1,0:T(8,128)(2,1)S(1)}, bf16[192,128]{1,0:T(8,128)(2,1)S(1)}, u32[]{:S(2)}, u32[]{:S(2)}) collective-permute-start(bf16[192,128]{1,0:T(8,128)(2,1)S(1)} %shard_map.100), channel_id=1, source_target_pairs={{0,2},{1,3},{2,0},{3,1},{4,6},{5,7},{6,4},{7,5},{8,10},{9,11},{10,... | collective-permute-start | bytes 147464 | tf_op jit(solution)/shard_map/ppermute | solution.py:348
  67.1 5.0 %collective-permute-start.21 = (f32[128,128]{1,0:T(8,128)S(1)}, f32[128,128]{1,0:T(8,128)S(1)}, u32[]{:S(2)}, u32[]{:S(2)}) collective-permute-start(f32[128,128]{1,0:T(8,128)S(1)} %copy-done.28), channel_id=1, source_target_pairs={{0,4},{1,5},{2,6},{3,7},{4,0},{5,1},{6,2},{7,3},{8,12},{9,13},{10,... | collective-permute-start | bytes 196616 | tf_op jit(solution)/shard_map/ppermute | solution.py:348
  67.2 4.9 %collective-permute-start.17 = (bf16[192,128]{1,0:T(8,128)(2,1)S(1)}, bf16[192,128]{1,0:T(8,128)(2,1)S(1)}, u32[]{:S(2)}, u32[]{:S(2)}) collective-permute-start(bf16[192,128]{1,0:T(8,128)(2,1)S(1)} %get-tuple-element.49.refs_2_), channel_id=1, source_target_pairs={{0,4},{1,5},{2,6},{3,7},{4,0},{5,1},{6,2},{7,3},{8,12},{9,13},{10,... | collective-permute-start | bytes 147464 | tf_op jit(solution)/shard_map/ppermute | solution.py:348
  67.7 4.4 %collective-permute-start.18 = (bf16[192,128]{1,0:T(8,128)(2,1)S(1)}, bf16[192,128]{1,0:T(8,128)(2,1)S(1)}, u32[]{:S(2)}, u32[]{:S(2)}) collective-permute-start(bf16[192,128]{1,0:T(8,128)(2,1)S(1)} %collective-permute-done.14.refs_6_.refs_3_), channel_id=1, source_target_pairs={{0,4},{1,5},{2,6},{3,7},{4,0},{5,1},{6,2},{7,3},{8,12},{9,13},{10,... | collective-permute-start | bytes 147464 | tf_op jit(solution)/shard_map/ppermute | solution.py:348
  67.8 4.3 %collective-permute-start.20 = (bf16[192,128]{1,0:T(8,128)(2,1)S(1)}, bf16[192,128]{1,0:T(8,128)(2,1)S(1)}, u32[]{:S(2)}, u32[]{:S(2)}) collective-permute-start(bf16[192,128]{1,0:T(8,128)(2,1)S(1)} %collective-permute-done.15.refs_7_.refs_5_), channel_id=1, source_target_pairs={{0,4},{1,5},{2,6},{3,7},{4,0},{5,1},{6,2},{7,3},{8,12},{9,13},{10,... | collective-permute-start | bytes 147464 | tf_op jit(solution)/shard_map/ppermute | solution.py:348
  72.1 1.2 %collective-permute-start.19 = (bf16[192,128]{1,0:T(8,128)(2,1)S(1)}, bf16[192,128]{1,0:T(8,128)(2,1)S(1)}, u32[]{:S(2)}, u32[]{:S(2)}) collective-permute-start(bf16[192,128]{1,0:T(8,128)(2,1)S(1)} %collective-permute-done.16.refs_4_), channel_id=1, source_target_pairs={{0,4},{1,5},{2,6},{3,7},{4,0},{5,1},{6,2},{7,3},{8,12},{9,13},{10,... | collective-permute-start | bytes 147464 | tf_op jit(solution)/shard_map/ppermute | solution.py:348
  74.2 1.3 %collective-permute-start.22 = (f32[128,128]{1,0:T(8,128)S(1)}, f32[128,128]{1,0:T(8,128)S(1)}, u32[]{:S(2)}, u32[]{:S(2)}) collective-permute-start(f32[128,128]{1,0:T(8,128)S(1)} %get-tuple-element.54), channel_id=1, source_target_pairs={{0,4},{1,5},{2,6},{3,7},{4,0},{5,1},{6,2},{7,3},{8,12},{9,13},{10,... | collective-permute-start | bytes 196616 | tf_op jit(solution)/shard_map/ppermute | solution.py:348
  75.5 7.2 %copy-start.8 = (bf16[384,256]{1,0:T(8,128)(2,1)S(1)}, bf16[384,256]{1,0:T(8,128)(2,1)}, u32[]{:S(2)}) copy-start(bf16[384,256]{1,0:T(8,128)(2,1)} %refs_2_.5) | copy-start | bytes 589828
  75.5 7.2 %copy-start.9 = (bf16[384,256]{1,0:T(8,128)(2,1)S(1)}, bf16[384,256]{1,0:T(8,128)(2,1)}, u32[]{:S(2)}) copy-start(bf16[384,256]{1,0:T(8,128)(2,1)} %refs_1_.13) | copy-start | bytes 589828
  75.5 7.1 %copy-start.11 = (bf16[4,384,384]{2,1,0:T(8,128)(2,1)S(1)}, bf16[4,384,384]{2,1,0:T(8,128)(2,1)}, u32[]{:S(2)}) copy-start(bf16[4,384,384]{2,1,0:T(8,128)(2,1)} %copy-done.10) | copy-start | bytes 3538948
  75.5 7.1 %copy-start.17 = (f32[128,128]{1,0:T(8,128)S(1)}, f32[128,128]{1,0:T(8,128)}, u32[]{:S(2)}) copy-start(f32[128,128]{1,0:T(8,128)} %copy-done.16) | copy-start | bytes 196612
  78.5 8.7 %collective-permute-start.23 = (f32[96,2048]{1,0:T(8,128)S(1)}, f32[96,2048]{1,0:T(8,128)S(1)}, u32[]{:S(2)}, u32[]{:S(2)}) collective-permute-start(f32[96,2048]{1,0:T(8,128)S(1)} %get-tuple-element.56), channel_id=1, source_target_pairs={{0,4},{1,5},{2,6},{3,7},{4,0},{5,1},{6,2},{7,3},{8,12},{9,13},{10,... | collective-permute-start | bytes 2359304 | tf_op jit(solution)/shard_map/ppermute | solution.py:348
  78.7 8.5 %collective-permute-start.24 = (f32[96,2048]{1,0:T(8,128)S(1)}, f32[96,2048]{1,0:T(8,128)S(1)}, u32[]{:S(2)}, u32[]{:S(2)}) collective-permute-start(f32[96,2048]{1,0:T(8,128)S(1)} %get-tuple-element.58), channel_id=1, source_target_pairs={{0,4},{1,5},{2,6},{3,7},{4,0},{5,1},{6,2},{7,3},{8,12},{9,13},{10,... | collective-permute-start | bytes 2359304 | tf_op jit(solution)/shard_map/ppermute | solution.py:348
  79.1 6.6 %collective-permute-start.27 = (f32[128,128]{1,0:T(8,128)S(1)}, f32[128,128]{1,0:T(8,128)S(1)}, u32[]{:S(2)}, u32[]{:S(2)}) collective-permute-start(f32[128,128]{1,0:T(8,128)S(1)} %add.15.refs_11_.refs_8_), channel_id=1, source_target_pairs={{0,24},{1,25},{2,26},{3,27},{4,28},{5,29},{6,30},{7,31},{8,16},{9,... | collective-permute-start | bytes 196616 | tf_op jit(solution)/shard_map/ppermute | solution.py:348
  80.5 5.2 %collective-permute-start.26 = (f32[128,128]{1,0:T(8,128)S(1)}, f32[128,128]{1,0:T(8,128)S(1)}, u32[]{:S(2)}, u32[]{:S(2)}) collective-permute-start(f32[128,128]{1,0:T(8,128)S(1)} %add.15.refs_11_.refs_8_), channel_id=1, source_target_pairs={{0,16},{1,17},{2,18},{3,19},{4,20},{5,21},{6,22},{7,23},{8,24},{9,... | collective-permute-start | bytes 196616 | tf_op jit(solution)/shard_map/ppermute | solution.py:348
  82.2 4.3 %collective-permute-start.25 = (f32[128,128]{1,0:T(8,128)S(1)}, f32[128,128]{1,0:T(8,128)S(1)}, u32[]{:S(2)}, u32[]{:S(2)}) collective-permute-start(f32[128,128]{1,0:T(8,128)S(1)} %add.15.refs_11_.refs_8_), channel_id=1, source_target_pairs={{0,8},{1,9},{2,10},{3,11},{4,12},{5,13},{6,14},{7,15},{8,0},{9,1},... | collective-permute-start | bytes 196616 | tf_op jit(solution)/shard_map/ppermute | solution.py:348
  87.1 1.7 %collective-permute-start.28 = (f32[128,128]{1,0:T(8,128)S(1)}, f32[128,128]{1,0:T(8,128)S(1)}, u32[]{:S(2)}, u32[]{:S(2)}) collective-permute-start(f32[128,128]{1,0:T(8,128)S(1)} %get-tuple-element.66), channel_id=1, source_target_pairs={{0,4},{1,5},{2,6},{3,7},{4,0},{5,1},{6,2},{7,3},{8,12},{9,13},{10,... | collective-permute-start | bytes 196616 | tf_op jit(solution)/shard_map/ppermute | solution.py:348
  (11 other events, 8.0 us)

commit v19 on v18

--- a/solution.py
+++ b/solution.py
@@ -490,6 +490,7 @@
         room=6,
         flops=2 * product,
     )
+    (half,) = hold([half], [arrived[2]])
     one, three, *cuts = call(
         second_kernel,
         [tokens] * 2 + [((DH, wide // 2), BF16)] * 2,

time: 91.2 us -> 93.5 us (1.025)
  local copies, waits for them, and re-layouts: 14.5 us -> 19 us
  waiting for transfers between devices: 22.2 us -> 18.7 us
  starting transfers between devices: 27.3 us -> 28.4 us
    unnamed x58 -> x70, local copies, waits for them, and re-layouts: 12.7 us -> 17.2 us
    ppermute x29, waiting for transfers between devices: 22.2 us -> 18.7 us  [send(): return lax.ppermute(x, ('ctx', 'head'), pairs)]
    ppermute x29, starting transfers between devices: 23.3 us -> 24.4 us  [send(): return lax.ppermute(x, ('ctx', 'head'), pairs)]
  transfers between devices with their start and end apart: 30 -> 30, of which waited for: 13 -> 11; matrix products, arithmetic and copies ran while one was open for 5% -> 5% of each run, Pallas kernels for 17% -> 17%
where the time goes in v19:
time: 93.5 us; the launch traced here: 92.6 us
  starting transfers between devices  28.4 us (30%)
  Pallas kernels  23.1 us (25%)
  local copies, waits for them, and re-layouts  19 us (20%)
  waiting for transfers between devices  18.7 us (20%)
  other arithmetic  2.46 us (3%)
  between operations  0.98 us (1%)
    ppermute x29, starting transfers between devices, send(): return lax.ppermute(x, ('ctx', 'head'), pairs)  24.4 us
    pallas_call x12, Pallas kernels, call(): pl.pallas_call(kernel, out_shape=[jax.ShapeDtypeStruct(s, t) for s, t in...  23.1 us
    ppermute x29, waiting for transfers between devices, send(): return lax.ppermute(x, ('ctx', 'head'), pairs)  18.7 us
    unnamed x70, local copies, waits for them, and re-layouts  17.2 us
    all_to_all x1, starting transfers between devices, on_device(): attn = lax.all_to_all(attn, 'head', 0, 0, tiled=True)  4 us
    dynamic_slice x1, local copies, waits for them, and re-layouts, on_device(): lax.dynamic_slice(out_weight, (core * DH, colour * wide), (DH, wide))  1.88 us
  transfers between devices with their start and end apart: 30, of which 11 were waited for; matrix products, arithmetic and copies ran while one was open for 5% of the time, Pallas kernels for 17%

profile of v19, /device:TPU:0, one launch (start us, length us, event | category | flops | bytes accessed | tf_op | source)
XLA Modules:
  0.0 92.6 jit_solution(8628731600913590488)
XLA Ops:
  1.2 1.9 %dynamic_slice.3 = bf16[128,2048]{1,0:T(8,128)(2,1)} dynamic-slice(bf16[256,4096]{1,0:T(8,128)(2,1)} %refs_6_.1, s32[]{:T(128)S(6)} %select_n.6, s32[]{:T(128)S(6)} %select_n.7), dynamic_slice_sizes={128,2048} | dynamic-slice | bytes 1048580 | tf_op jit(solution)/shard_map/dynamic_slice | solution.py:388
  3.0 4.6 %collective-permute-start.8 = (bf16[128,2048]{1,0:T(8,128)(2,1)}, bf16[128,2048]{1,0:T(8,128)(2,1)S(1)}, u32[]{:S(2)}, u32[]{:S(2)}) collective-permute-start(bf16[128,2048]{1,0:T(8,128)(2,1)} %dynamic_slice.3), channel_id=1, source_target_pairs={{0,3},{1,0},{2,1},{3,2},{4,7},{5,4},{6,5},{7,6},{8,11},{9,8},{10,9... | collective-permute-start | bytes 1572872 | tf_op jit(solution)/shard_map/ppermute | solution.py:348
  7.8 1.2 %pad_maximum_fusion.refs_2_ = bf16[3,384,256]{2,1,0:T(8,128)(2,1)S(1)} fusion(bf16[1,384,256]{2,1,0:T(8,128)(2,1)} %bitcast.18, bf16[1,384,256]{2,1,0:T(8,128)(2,1)} %bitcast.19, bf16[1,384,256]{2,1,0:T(8,128)(2,1)} %bitcast.17), kind=kLoop, calls=%fused_computation | loop fusion | flops 589824 | bytes 1179648 | tf_op jit(solution)/shard_map/stack | solution.py:398
  9.0 2.6 %shard_map.93 = (bf16[4,384,384]{2,1,0:T(8,128)(2,1)S(1)}, f32[384,128]{1,0:T(8,128)S(1)}, f32[384,128]{1,0:T(8,128)}, bf16[384,128]{1,0:T(8,128)(2,1)}, f32[128,128]{1,0:T(8,128)S(1)}, /*index=5*/f32[128,128]{1,0:T(8,128)}) custom-call(s32[3,3]{1,0:T(4,128)S(1)} %copy-done.32, s32[3]{0:T(128)S(1)} %pad_add_fusion.2.refs_1_.refs_0_, ...), custom_call_target="tpu_custom_call" | custom-call | flops 264241152 | bytes 2392064 | tf_op jit(solution)/shard_map/pallas_call | solution.py:103
  11.5 1.0 %copy-done.14 = bf16[4,384,384]{2,1,0:T(8,128)(2,1)} copy-done((bf16[4,384,384]{2,1,0:T(8,128)(2,1)}, bf16[4,384,384]{2,1,0:T(8,128)(2,1)S(1)}, u32[]{:S(2)}) %copy-start.14) | copy-done | bytes 1179672
  13.2 0.7 copy-done.24
  14.6 1.1 %collective-permute-done.1.refs_1_.refs_8_ = bf16[384,128]{1,0:T(8,128)(2,1)S(1)} collective-permute-done((bf16[384,128]{1,0:T(8,128)(2,1)}, bf16[384,128]{1,0:T(8,128)(2,1)S(1)}, u32[]{:S(2)}, u32[]{:S(2)}) %collective-permute-start.1) | collective-permute-done | bytes 98336 | tf_op jit(solution)/shard_map/ppermute | solution.py:348
  16.3 0.9 add.12
  17.2 2.5 %collective-permute-start.6 = (f32[128,128]{1,0:T(8,128)S(1)}, f32[128,128]{1,0:T(8,128)S(1)}, u32[]{:S(2)}, u32[]{:S(2)}) collective-permute-start(f32[128,128]{1,0:T(8,128)S(1)} %add.12), channel_id=1, source_target_pairs={{0,24},{1,25},{2,26},{3,27},{4,28},{5,29},{6,30},{7,31},{8,16},{9,... | collective-permute-start | bytes 196616 | tf_op jit(solution)/shard_map/ppermute | solution.py:348
  20.8 1.6 %collective-permute-done.6.refs_6_ = f32[128,128]{1,0:T(8,128)S(1)} collective-permute-done((f32[128,128]{1,0:T(8,128)S(1)}, f32[128,128]{1,0:T(8,128)S(1)}, u32[]{:S(2)}, u32[]{:S(2)}) %collective-permute-start.6) | collective-permute-done | bytes 65568 | tf_op jit(solution)/shard_map/ppermute | solution.py:348
  22.4 1.5 %collective-permute-done.5.refs_5_ = f32[128,128]{1,0:T(8,128)S(1)} collective-permute-done((f32[128,128]{1,0:T(8,128)S(1)}, f32[128,128]{1,0:T(8,128)S(1)}, u32[]{:S(2)}, u32[]{:S(2)}) %collective-permute-start.5) | collective-permute-done | bytes 65568 | tf_op jit(solution)/shard_map/ppermute | solution.py:348
  24.5 0.9 copy-done.10
  25.4 0.8 copy-done.19
  26.2 0.9 copy-done.21
  27.1 0.9 copy-done.25
  28.1 1.2 %shard_map.95 = (bf16[4,192,128]{2,1,0:T(8,128)(2,1)S(1)}, f32[128,128]{1,0:T(8,128)S(1)}, f32[128,128]{1,0:T(8,128)S(1)}) custom-call(s32[4]{0:T(128)S(1)} %add_convert_fusion.refs_0_, s32[3]{0:T(128)S(1)} %pad_add_fusion.2.refs_1_.refs_0_, f32[128,128]{1,0:T(8,128)S(1)} %copy-done.19, f32[128,128]{1,0:T(8,128)} %collective-permute-done.3.refs_3_, ...), custom_call_target="tpu_custom_call" | custom-call | flops 1 | bytes 1343488 | tf_op jit(solution)/shard_map/pallas_call | solution.py:103
  31.3 0.7 collective-permute-done.7.refs_0_
  32.1 1.5 %collective-permute-start.9 = (bf16[128,2048]{1,0:T(8,128)(2,1)}, bf16[128,2048]{1,0:T(8,128)(2,1)S(1)}, u32[]{:S(2)}, u32[]{:S(2)}) collective-permute-start(bf16[128,2048]{1,0:T(8,128)(2,1)} %get-tuple-element.44.refs_4_.refs_3_), channel_id=1, source_target_pairs={{0,1},{1,2},{2,3},{3,0},{4,5},{5,6},{6,7},{7,4},{8,9},{9,10},{10,1... | collective-permute-start | bytes 1572872 | tf_op jit(solution)/shard_map/ppermute | solution.py:348
  33.6 1.5 %collective-permute-start.11 = (bf16[128,2048]{1,0:T(8,128)(2,1)}, bf16[128,2048]{1,0:T(8,128)(2,1)}, u32[]{:S(2)}, u32[]{:S(2)}) collective-permute-start(bf16[128,2048]{1,0:T(8,128)(2,1)} %get-tuple-element.45.refs_5_), channel_id=1, source_target_pairs={{0,16},{1,17},{2,18},{3,19},{4,20},{5,21},{6,22},{7,23},{8,24},{9,... | collective-permute-start | bytes 1572872 | tf_op jit(solution)/shard_map/ppermute | solution.py:348
  35.1 1.5 %collective-permute-start.10 = (bf16[128,2048]{1,0:T(8,128)(2,1)}, bf16[128,2048]{1,0:T(8,128)(2,1)}, u32[]{:S(2)}, u32[]{:S(2)}) collective-permute-start(bf16[128,2048]{1,0:T(8,128)(2,1)} %get-tuple-element.44.refs_4_.refs_3_), channel_id=1, source_target_pairs={{0,8},{1,9},{2,10},{3,11},{4,12},{5,13},{6,14},{7,15},{8,0},{9,1},... | collective-permute-start | bytes 1572872 | tf_op jit(solution)/shard_map/ppermute | solution.py:348
  36.7 4.0 %all-to-all-start = ((bf16[4,192,128]{2,1,0:T(8,128)(2,1)}), bf16[4,192,128]{2,1,0:T(8,128)(2,1)}, u32[]{:S(2)}, u32[]{:S(2)}) async-start(bf16[4,192,128]{2,1,0:T(8,128)(2,1)} %copy-done.26), calls=%async_computation | async-start | bytes 393216 | tf_op jit(solution)/shard_map/all_to_all | solution.py:415
  40.7 1.1 %copy-done.1 = bf16[96,4096]{1,0:T(8,128)(2,1)S(1)} copy-done((bf16[96,4096]{1,0:T(8,128)(2,1)S(1)}, bf16[96,4096]{1,0:T(8,128)(2,1)}, u32[]{:S(2)}) %copy-start.1) | copy-done | bytes 786456
  41.8 1.0 %copy-done.8 = bf16[128,2048]{1,0:T(8,128)(2,1)S(1)} copy-done((bf16[128,2048]{1,0:T(8,128)(2,1)S(1)}, bf16[128,2048]{1,0:T(8,128)(2,1)}, u32[]{:S(2)}) %copy-start.8) | copy-done | bytes 524312
  42.9 2.5 %shard_map.97 = (bf16[192,128]{1,0:T(8,128)(2,1)S(1)}, f32[192,256]{1,0:T(8,128)S(1)}) custom-call(s32[4]{0:T(128)S(1)} %pad_add_fusion.1.refs_0_, bf16[96,4096]{1,0:T(8,128)(2,1)S(1)} %copy-done.1, bf16[96,4096]{1,0:T(8,128)(2,1)S(1)} %collective-permute-done.refs_3_.refs_2_, bf16[256,4096]{1,0:T(8,128)(2,1)S(1)} %copy-done, ...), custom_call_target="tpu_custom_call" | custom-call | flops 402653184 | bytes 4964352 | tf_op jit(solution)/shard_map/pallas_call | solution.py:103
  46.1 2.9 %collective-permute-done.9.refs_1_.refs_6_.refs_3_.refs_4_ = bf16[128,2048]{1,0:T(8,128)(2,1)S(1)} collective-permute-done((bf16[128,2048]{1,0:T(8,128)(2,1)}, bf16[128,2048]{1,0:T(8,128)(2,1)S(1)}, u32[]{:S(2)}, u32[]{:S(2)}) %collective-permute-start.9) | collective-permute-done | bytes 524320 | tf_op jit(solution)/shard_map/ppermute | solution.py:348
  49.0 0.8 copy-done.4
  49.8 1.1 %copy-done.2 = bf16[96,4096]{1,0:T(8,128)(2,1)S(1)} copy-done((bf16[96,4096]{1,0:T(8,128)(2,1)S(1)}, bf16[96,4096]{1,0:T(8,128)(2,1)}, u32[]{:S(2)}) %copy-start.2) | copy-done | bytes 786456
  51.0 1.0 %copy-done.5 = bf16[128,2048]{1,0:T(8,128)(2,1)S(1)} copy-done((bf16[128,2048]{1,0:T(8,128)(2,1)S(1)}, bf16[128,2048]{1,0:T(8,128)(2,1)}, u32[]{:S(2)}) %copy-start.5) | copy-done | bytes 524312
  52.0 0.9 copy-done.17
  52.9 3.1 %shard_map.99 = (bf16[192,128]{1,0:T(8,128)(2,1)}, bf16[192,128]{1,0:T(8,128)(2,1)}, bf16[128,1024]{1,0:T(8,128)(2,1)}, bf16[128,1024]{1,0:T(8,128)(2,1)}) custom-call(s32[4]{0:T(128)S(1)} %pad_add_fusion.1.refs_0_, bf16[96,4096]{1,0:T(8,128)(2,1)S(1)} %copy-done.2, bf16[96,4096]{1,0:T(8,128)(2,1)S(1)} %collective-permute-done.refs_3_.refs_2_, ...), custom_call_target="tpu_custom_call" | custom-call | flops 201326592 | bytes 3964928 | tf_op jit(solution)/shard_map/pallas_call | solution.py:103
  56.1 1.4 %collective-permute-start.12 = (bf16[128,1024]{1,0:T(8,128)(2,1)}, bf16[128,1024]{1,0:T(8,128)(2,1)}, u32[]{:S(2)}, u32[]{:S(2)}) collective-permute-start(bf16[128,1024]{1,0:T(8,128)(2,1)} %get-tuple-element.47), channel_id=1, source_target_pairs={{0,8},{1,9},{2,10},{3,11},{4,12},{5,13},{6,14},{7,15},{8,0},{9,1},... | collective-permute-start | bytes 786440 | tf_op jit(solution)/shard_map/ppermute | solution.py:348
  57.4 1.6 %collective-permute-start.13 = (bf16[128,1024]{1,0:T(8,128)(2,1)}, bf16[128,1024]{1,0:T(8,128)(2,1)}, u32[]{:S(2)}, u32[]{:S(2)}) collective-permute-start(bf16[128,1024]{1,0:T(8,128)(2,1)} %get-tuple-element.48), channel_id=1, source_target_pairs={{0,16},{1,17},{2,18},{3,19},{4,20},{5,21},{6,22},{7,23},{8,24},{9,... | collective-permute-start | bytes 786440 | tf_op jit(solution)/shard_map/ppermute | solution.py:348
  59.0 1.8 %collective-permute-start.14 = (bf16[192,128]{1,0:T(8,128)(2,1)}, bf16[192,128]{1,0:T(8,128)(2,1)S(1)}, u32[]{:S(2)}, u32[]{:S(2)}) collective-permute-start(bf16[192,128]{1,0:T(8,128)(2,1)} %get-tuple-element.50), channel_id=1, source_target_pairs={{0,3},{1,0},{2,1},{3,2},{4,7},{5,4},{6,5},{7,6},{8,11},{9,8},{10,9... | collective-permute-start | bytes 147464 | tf_op jit(solution)/shard_map/ppermute | solution.py:348
  61.1 1.1 %copy-done.3 = bf16[96,4096]{1,0:T(8,128)(2,1)S(1)} copy-done((bf16[96,4096]{1,0:T(8,128)(2,1)S(1)}, bf16[96,4096]{1,0:T(8,128)(2,1)}, u32[]{:S(2)}) %copy-start.3) | copy-done | bytes 786456
  62.8 1.0 %shard_map.100.refs_5_ = f32[192,128]{1,0:T(8,128)S(1)} custom-call(s32[4]{0:T(128)S(1)} %copy-done.30, bf16[96,4096]{1,0:T(8,128)(2,1)S(1)} %copy-done.3, bf16[96,4096]{1,0:T(8,128)(2,1)S(1)} %collective-permute-done.refs_3_.refs_2_, bf16[128,2048]{1,0:T(8,128)(2,1)S(1)} %copy-done.6, bf16[4,192,128]{2,1,0:T(8,128)(2,1)} %all-to-all-done.refs_4_.refs_1_), custom_call_target="tpu_custom_call" | custom-call | flops 100663296 | bytes 2195456 | tf_op jit(solution)/shard_map/pallas_call | solution.py:103
  63.9 3.0 %collective-permute-done.15.refs_7_.refs_5_ = bf16[192,128]{1,0:T(8,128)(2,1)S(1)} collective-permute-done((bf16[192,128]{1,0:T(8,128)(2,1)}, bf16[192,128]{1,0:T(8,128)(2,1)S(1)}, u32[]{:S(2)}, u32[]{:S(2)}) %collective-permute-start.15) | collective-permute-done | bytes 49184 | tf_op jit(solution)/shard_map/ppermute | solution.py:348
  66.9 2.0 %shard_map.101 = bf16[192,128]{1,0:T(8,128)(2,1)S(1)} custom-call(s32[4]{0:T(128)S(1)} %copy-done.31, bf16[96,4096]{1,0:T(8,128)(2,1)S(1)} %copy-done.3, bf16[96,4096]{1,0:T(8,128)(2,1)S(1)} %collective-permute-done.refs_3_.refs_2_, bf16[128,1024]{1,0:T(8,128)(2,1)} %collective-permute-done.12.refs_3_.refs_9_, ...), custom_call_target="tpu_custom_call" | custom-call | flops 100663296 | bytes 2244608 | tf_op jit(solution)/shard_map/pallas_call | solution.py:103
  70.1 3.9 %collective-permute-done.16.refs_4_ = bf16[192,128]{1,0:T(8,128)(2,1)S(1)} collective-permute-done((bf16[192,128]{1,0:T(8,128)(2,1)S(1)}, bf16[192,128]{1,0:T(8,128)(2,1)S(1)}, u32[]{:S(2)}, u32[]{:S(2)}) %collective-permute-start.16) | collective-permute-done | bytes 49184 | tf_op jit(solution)/shard_map/ppermute | solution.py:348
  74.1 1.2 %collective-permute-done.19.refs_8_ = bf16[192,128]{1,0:T(8,128)(2,1)S(1)} collective-permute-done((bf16[192,128]{1,0:T(8,128)(2,1)S(1)}, bf16[192,128]{1,0:T(8,128)(2,1)S(1)}, u32[]{:S(2)}, u32[]{:S(2)}) %collective-permute-start.19) | collective-permute-done | bytes 49184 | tf_op jit(solution)/shard_map/ppermute | solution.py:348
  75.3 0.8 shard_map.102
  76.3 1.1 %collective-permute-done.22.refs_2_ = f32[128,128]{1,0:T(8,128)S(1)} collective-permute-done((f32[128,128]{1,0:T(8,128)S(1)}, f32[128,128]{1,0:T(8,128)S(1)}, u32[]{:S(2)}, u32[]{:S(2)}) %collective-permute-start.22) | collective-permute-done | bytes 65568 | tf_op jit(solution)/shard_map/ppermute | solution.py:348
  77.5 3.0 %shard_map.103 = (f32[96,2048]{1,0:T(8,128)S(1)}, f32[96,2048]{1,0:T(8,128)S(1)}, f32[96,2048]{1,0:T(8,128)S(1)}, f32[96,2048]{1,0:T(8,128)S(1)}) custom-call(s32[4]{0:T(128)S(1)} %copy-done.31, bf16[4,192,128]{2,1,0:T(8,128)(2,1)} %all-to-all-done.refs_4_.refs_1_, bf16[256,4096]{1,0:T(8,128)(2,1)S(1)} %copy-done, ...), custom_call_target="tpu_custom_call" | custom-call | flops 805306368 | bytes 10682368 | tf_op jit(solution)/shard_map/pallas_call | solution.py:103
  81.0 1.4 %collective-permute-start.27 = (f32[128,128]{1,0:T(8,128)S(1)}, f32[128,128]{1,0:T(8,128)S(1)}, u32[]{:S(2)}, u32[]{:S(2)}) collective-permute-start(f32[128,128]{1,0:T(8,128)S(1)} %add.15.refs_11_.refs_8_), channel_id=1, source_target_pairs={{0,24},{1,25},{2,26},{3,27},{4,28},{5,29},{6,30},{7,31},{8,16},{9,... | collective-permute-start | bytes 196616 | tf_op jit(solution)/shard_map/ppermute | solution.py:348
  82.4 2.0 %collective-permute-start.26 = (f32[128,128]{1,0:T(8,128)S(1)}, f32[128,128]{1,0:T(8,128)S(1)}, u32[]{:S(2)}, u32[]{:S(2)}) collective-permute-start(f32[128,128]{1,0:T(8,128)S(1)} %add.15.refs_11_.refs_8_), channel_id=1, source_target_pairs={{0,16},{1,17},{2,18},{3,19},{4,20},{5,21},{6,22},{7,23},{8,24},{9,... | collective-permute-start | bytes 196616 | tf_op jit(solution)/shard_map/ppermute | solution.py:348
  84.6 3.0 %shard_map.105 = (bf16[384,256]{1,0:T(8,128)(2,1)}, f32[384,256]{1,0:T(8,128)S(1)}, f32[384,256]{1,0:T(8,128)S(1)}) custom-call(s32[3]{0:T(128)S(1)} %copy-done.28, bf16[384,256]{1,0:T(8,128)(2,1)S(1)} %copy-done.11, bf16[384,256]{1,0:T(8,128)(2,1)S(1)} %copy-done.13, bf16[384,256]{1,0:T(8,128)(2,1)S(1)} %copy-done.12, ...), custom_call_target="tpu_custom_call" | custom-call | flops 528482304 | bytes 3080192 | tf_op jit(solution)/shard_map/pallas_call | solution.py:103
  87.6 1.1 %collective-permute-done.25.refs_3_ = f32[128,128]{1,0:T(8,128)S(1)} collective-permute-done((f32[128,128]{1,0:T(8,128)S(1)}, f32[128,128]{1,0:T(8,128)S(1)}, u32[]{:S(2)}, u32[]{:S(2)}) %collective-permute-start.25) | collective-permute-done | bytes 65568 | tf_op jit(solution)/shard_map/ppermute | solution.py:348
  89.4 1.6 %shard_map.104 = (bf16[96,4096]{1,0:T(8,128)(2,1)}, f32[8,128]{1,0:T(8,128)S(1)}) custom-call(s32[2]{0:T(128)S(1)} %pad_add_fusion.refs_0_, f32[96,2048]{1,0:T(8,128)S(1)} %get-tuple-element.55.refs_1_, f32[96,2048]{1,0:T(8,128)S(1)} %collective-permute-done.23.refs_2_, f32[96,2048]{1,0:T(8,128)S(1)} %get-tuple-element.57.refs_3_, ...), custom_call_target="tpu_custom_call" | custom-call | flops 1 | bytes 3936256 | tf_op jit(solution)/shard_map/pallas_call | solution.py:103
  91.0 1.6 %shard_map.107 = (bf16[384,256]{1,0:T(8,128)(2,1)}, bf16[384,256]{1,0:T(8,128)(2,1)}) custom-call(s32[3]{0:T(128)S(1)} %copy-done.28, bf16[384,256]{1,0:T(8,128)(2,1)S(1)} %copy-done.13, bf16[384,256]{1,0:T(8,128)(2,1)S(1)} %copy-done.12, f32[384,256]{1,0:T(8,128)S(1)} %get-tuple-element.63.refs_6_.refs_3_, f32[384,256]{1,0:T(8,128)S(1)} %get-tuple-element.64.refs_4_, ...), custom_call_target="tpu_custom_call" | custom-call | flops 1 | bytes 1703936 | tf_op jit(solution)/shard_map/pallas_call | solution.py:103
  (106 shorter events, 10.8 us)
Async XLA Ops:
  0.6 8.3 %copy-start.32 = (s32[3,3]{1,0:T(4,128)S(1)}, s32[3,3]{1,0:T(4,128)}, u32[]{:S(2)}) copy-start(s32[3,3]{1,0:T(4,128)} %refs_0_.1) | copy-start | bytes 112
  0.6 8.3 %collective-permute-start = (bf16[96,4096]{1,0:T(8,128)(2,1)}, bf16[96,4096]{1,0:T(8,128)(2,1)S(1)}, u32[]{:S(2)}, u32[]{:S(2)}) collective-permute-start(bf16[96,4096]{1,0:T(8,128)(2,1)} %refs_1_.10), channel_id=1, source_target_pairs={{0,4},{1,5},{2,6},{3,7},{4,0},{5,1},{6,2},{7,3},{8,12},{9,13},{10,... | collective-permute-start | bytes 2359304 | tf_op jit(solution)/shard_map/ppermute | solution.py:348
  3.0 27.6 %collective-permute-start.8 = (bf16[128,2048]{1,0:T(8,128)(2,1)}, bf16[128,2048]{1,0:T(8,128)(2,1)S(1)}, u32[]{:S(2)}, u32[]{:S(2)}) collective-permute-start(bf16[128,2048]{1,0:T(8,128)(2,1)} %dynamic_slice.3), channel_id=1, source_target_pairs={{0,3},{1,0},{2,1},{3,2},{4,7},{5,4},{6,5},{7,6},{8,11},{9,8},{10,9... | collective-permute-start | bytes 1572872 | tf_op jit(solution)/shard_map/ppermute | solution.py:348
  7.7 24.3 %collective-permute-start.7 = (bf16[128,2048]{1,0:T(8,128)(2,1)}, bf16[128,2048]{1,0:T(8,128)(2,1)}, u32[]{:S(2)}, u32[]{:S(2)}) collective-permute-start(bf16[128,2048]{1,0:T(8,128)(2,1)} %dynamic_slice.3), channel_id=1, source_target_pairs={{0,1},{1,2},{2,3},{3,0},{4,5},{5,6},{6,7},{7,4},{8,9},{9,10},{10,1... | collective-permute-start | bytes 1572872 | tf_op jit(solution)/shard_map/ppermute | solution.py:348
  7.8 21.6 %copy-start.27 = (s32[3]{0:T(128)}, s32[3]{0:T(128)S(1)}, u32[]{:S(2)}) copy-start(s32[3]{0:T(128)S(1)} %pad_add_fusion.2.refs_1_.refs_0_) | copy-start | bytes 40
  8.9 31.7 %copy-start = (bf16[256,4096]{1,0:T(8,128)(2,1)S(1)}, bf16[256,4096]{1,0:T(8,128)(2,1)}, u32[]{:S(2)}) copy-start(bf16[256,4096]{1,0:T(8,128)(2,1)} %refs_6_.1) | copy-start | bytes 6291460
  13.9 1.8 %collective-permute-start.2 = (f32[384,128]{1,0:T(8,128)}, f32[384,128]{1,0:T(8,128)}, u32[]{:S(2)}, u32[]{:S(2)}) collective-permute-start(f32[384,128]{1,0:T(8,128)} %get-tuple-element.39), channel_id=1, source_target_pairs={{0,4},{1,5},{2,6},{3,7},{4,0},{5,1},{6,2},{7,3},{8,12},{9,13},{10,... | collective-permute-start | bytes 589832 | tf_op jit(solution)/shard_map/ppermute | solution.py:348
  14.1 1.6 %collective-permute-start.1 = (bf16[384,128]{1,0:T(8,128)(2,1)}, bf16[384,128]{1,0:T(8,128)(2,1)S(1)}, u32[]{:S(2)}, u32[]{:S(2)}) collective-permute-start(bf16[384,128]{1,0:T(8,128)(2,1)} %get-tuple-element.38), channel_id=1, source_target_pairs={{0,4},{1,5},{2,6},{3,7},{4,0},{5,1},{6,2},{7,3},{8,12},{9,13},{10,... | collective-permute-start | bytes 294920 | tf_op jit(solution)/shard_map/ppermute | solution.py:348
  14.4 1.9 %collective-permute-start.3 = (f32[128,128]{1,0:T(8,128)}, f32[128,128]{1,0:T(8,128)}, u32[]{:S(2)}, u32[]{:S(2)}) collective-permute-start(f32[128,128]{1,0:T(8,128)} %get-tuple-element.40), channel_id=1, source_target_pairs={{0,4},{1,5},{2,6},{3,7},{4,0},{5,1},{6,2},{7,3},{8,12},{9,13},{10,... | collective-permute-start | bytes 196616 | tf_op jit(solution)/shard_map/ppermute | solution.py:348
  17.2 5.2 %collective-permute-start.6 = (f32[128,128]{1,0:T(8,128)S(1)}, f32[128,128]{1,0:T(8,128)S(1)}, u32[]{:S(2)}, u32[]{:S(2)}) collective-permute-start(f32[128,128]{1,0:T(8,128)S(1)} %add.12), channel_id=1, source_target_pairs={{0,24},{1,25},{2,26},{3,27},{4,28},{5,29},{6,30},{7,31},{8,16},{9,... | collective-permute-start | bytes 196616 | tf_op jit(solution)/shard_map/ppermute | solution.py:348
  19.7 4.3 %collective-permute-start.5 = (f32[128,128]{1,0:T(8,128)S(1)}, f32[128,128]{1,0:T(8,128)S(1)}, u32[]{:S(2)}, u32[]{:S(2)}) collective-permute-start(f32[128,128]{1,0:T(8,128)S(1)} %add.12), channel_id=1, source_target_pairs={{0,16},{1,17},{2,18},{3,19},{4,20},{5,21},{6,22},{7,23},{8,24},{9,... | collective-permute-start | bytes 196616 | tf_op jit(solution)/shard_map/ppermute | solution.py:348
  20.2 4.3 %collective-permute-start.4 = (f32[128,128]{1,0:T(8,128)S(1)}, f32[128,128]{1,0:T(8,128)S(1)}, u32[]{:S(2)}, u32[]{:S(2)}) collective-permute-start(f32[128,128]{1,0:T(8,128)S(1)} %add.12), channel_id=1, source_target_pairs={{0,8},{1,9},{2,10},{3,11},{4,12},{5,13},{6,14},{7,15},{8,0},{9,1},... | collective-permute-start | bytes 196616 | tf_op jit(solution)/shard_map/ppermute | solution.py:348
  32.1 17.0 %collective-permute-start.9 = (bf16[128,2048]{1,0:T(8,128)(2,1)}, bf16[128,2048]{1,0:T(8,128)(2,1)S(1)}, u32[]{:S(2)}, u32[]{:S(2)}) collective-permute-start(bf16[128,2048]{1,0:T(8,128)(2,1)} %get-tuple-element.44.refs_4_.refs_3_), channel_id=1, source_target_pairs={{0,1},{1,2},{2,3},{3,0},{4,5},{5,6},{6,7},{7,4},{8,9},{9,10},{10,1... | collective-permute-start | bytes 1572872 | tf_op jit(solution)/shard_map/ppermute | solution.py:348
  33.6 16.2 %collective-permute-start.11 = (bf16[128,2048]{1,0:T(8,128)(2,1)}, bf16[128,2048]{1,0:T(8,128)(2,1)}, u32[]{:S(2)}, u32[]{:S(2)}) collective-permute-start(bf16[128,2048]{1,0:T(8,128)(2,1)} %get-tuple-element.45.refs_5_), channel_id=1, source_target_pairs={{0,16},{1,17},{2,18},{3,19},{4,20},{5,21},{6,22},{7,23},{8,24},{9,... | collective-permute-start | bytes 1572872 | tf_op jit(solution)/shard_map/ppermute | solution.py:348
  35.1 14.7 %collective-permute-start.10 = (bf16[128,2048]{1,0:T(8,128)(2,1)}, bf16[128,2048]{1,0:T(8,128)(2,1)}, u32[]{:S(2)}, u32[]{:S(2)}) collective-permute-start(bf16[128,2048]{1,0:T(8,128)(2,1)} %get-tuple-element.44.refs_4_.refs_3_), channel_id=1, source_target_pairs={{0,8},{1,9},{2,10},{3,11},{4,12},{5,13},{6,14},{7,15},{8,0},{9,1},... | collective-permute-start | bytes 1572872 | tf_op jit(solution)/shard_map/ppermute | solution.py:348
  36.7 13.2 %copy-start.29 = (s32[4]{0:T(128)}, s32[4]{0:T(128)S(1)}, u32[]{:S(2)}) copy-start(s32[4]{0:T(128)S(1)} %pad_add_fusion.1.refs_0_) | copy-start | bytes 52
  36.7 24.4 %all-to-all-start = ((bf16[4,192,128]{2,1,0:T(8,128)(2,1)}), bf16[4,192,128]{2,1,0:T(8,128)(2,1)}, u32[]{:S(2)}, u32[]{:S(2)}) async-start(bf16[4,192,128]{2,1,0:T(8,128)(2,1)} %copy-done.26), calls=%async_computation | async-start | bytes 393216 | tf_op jit(solution)/shard_map/all_to_all | solution.py:415
  40.7 1.1 %copy-start.1 = (bf16[96,4096]{1,0:T(8,128)(2,1)S(1)}, bf16[96,4096]{1,0:T(8,128)(2,1)}, u32[]{:S(2)}) copy-start(bf16[96,4096]{1,0:T(8,128)(2,1)} %refs_1_.10) | copy-start | bytes 2359300
  41.8 1.0 %copy-start.8 = (bf16[128,2048]{1,0:T(8,128)(2,1)S(1)}, bf16[128,2048]{1,0:T(8,128)(2,1)}, u32[]{:S(2)}) copy-start(bf16[128,2048]{1,0:T(8,128)(2,1)} %get-tuple-element.45.refs_5_) | copy-start | bytes 1572868
  49.8 1.1 %copy-start.2 = (bf16[96,4096]{1,0:T(8,128)(2,1)S(1)}, bf16[96,4096]{1,0:T(8,128)(2,1)}, u32[]{:S(2)}) copy-start(bf16[96,4096]{1,0:T(8,128)(2,1)} %refs_1_.10) | copy-start | bytes 2359300
  52.9 8.1 %copy-start.6 = (bf16[128,2048]{1,0:T(8,128)(2,1)S(1)}, bf16[128,2048]{1,0:T(8,128)(2,1)}, u32[]{:S(2)}) copy-start(bf16[128,2048]{1,0:T(8,128)(2,1)} %copy-done.4) | copy-start | bytes 1572868
  56.1 10.8 %collective-permute-start.12 = (bf16[128,1024]{1,0:T(8,128)(2,1)}, bf16[128,1024]{1,0:T(8,128)(2,1)}, u32[]{:S(2)}, u32[]{:S(2)}) collective-permute-start(bf16[128,1024]{1,0:T(8,128)(2,1)} %get-tuple-element.47), channel_id=1, source_target_pairs={{0,8},{1,9},{2,10},{3,11},{4,12},{5,13},{6,14},{7,15},{8,0},{9,1},... | collective-permute-start | bytes 786440 | tf_op jit(solution)/shard_map/ppermute | solution.py:348
  57.4 9.5 %collective-permute-start.13 = (bf16[128,1024]{1,0:T(8,128)(2,1)}, bf16[128,1024]{1,0:T(8,128)(2,1)}, u32[]{:S(2)}, u32[]{:S(2)}) collective-permute-start(bf16[128,1024]{1,0:T(8,128)(2,1)} %get-tuple-element.48), channel_id=1, source_target_pairs={{0,16},{1,17},{2,18},{3,19},{4,20},{5,21},{6,22},{7,23},{8,24},{9,... | collective-permute-start | bytes 786440 | tf_op jit(solution)/shard_map/ppermute | solution.py:348
  59.0 4.9 %collective-permute-start.14 = (bf16[192,128]{1,0:T(8,128)(2,1)}, bf16[192,128]{1,0:T(8,128)(2,1)S(1)}, u32[]{:S(2)}, u32[]{:S(2)}) collective-permute-start(bf16[192,128]{1,0:T(8,128)(2,1)} %get-tuple-element.50), channel_id=1, source_target_pairs={{0,3},{1,0},{2,1},{3,2},{4,7},{5,4},{6,5},{7,6},{8,11},{9,8},{10,9... | collective-permute-start | bytes 147464 | tf_op jit(solution)/shard_map/ppermute | solution.py:348
  60.8 6.1 %collective-permute-start.15 = (bf16[192,128]{1,0:T(8,128)(2,1)}, bf16[192,128]{1,0:T(8,128)(2,1)S(1)}, u32[]{:S(2)}, u32[]{:S(2)}) collective-permute-start(bf16[192,128]{1,0:T(8,128)(2,1)} %get-tuple-element.51), channel_id=1, source_target_pairs={{0,1},{1,2},{2,3},{3,0},{4,5},{5,6},{6,7},{7,4},{8,9},{9,10},{10,1... | collective-permute-start | bytes 147464 | tf_op jit(solution)/shard_map/ppermute | solution.py:348
  61.1 1.1 %copy-start.3 = (bf16[96,4096]{1,0:T(8,128)(2,1)S(1)}, bf16[96,4096]{1,0:T(8,128)(2,1)}, u32[]{:S(2)}) copy-start(bf16[96,4096]{1,0:T(8,128)(2,1)} %refs_1_.10) | copy-start | bytes 2359300
  62.8 4.1 %copy-start.31 = (s32[4]{0:T(128)S(1)}, s32[4]{0:T(128)}, u32[]{:S(2)}) copy-start(s32[4]{0:T(128)} %copy-done.29) | copy-start | bytes 52
  62.8 6.2 %copy-start.34 = (f32[128,128]{1,0:T(8,128)S(1)}, f32[128,128]{1,0:T(8,128)}, u32[]{:S(2)}) copy-start(f32[128,128]{1,0:T(8,128)} %copy-done.33) | copy-start | bytes 196612
  62.8 12.4 %copy-start.11 = (bf16[384,256]{1,0:T(8,128)(2,1)S(1)}, bf16[384,256]{1,0:T(8,128)(2,1)}, u32[]{:S(2)}) copy-start(bf16[384,256]{1,0:T(8,128)(2,1)} %refs_1_.12) | copy-start | bytes 589828
  62.8 12.4 %copy-start.28 = (s32[3]{0:T(128)S(1)}, s32[3]{0:T(128)}, u32[]{:S(2)}) copy-start(s32[3]{0:T(128)} %copy-done.27) | copy-start | bytes 40
  63.9 13.5 %copy-start.9 = (bf16[128,2048]{1,0:T(8,128)(2,1)S(1)}, bf16[128,2048]{1,0:T(8,128)(2,1)}, u32[]{:S(2)}) copy-start(bf16[128,2048]{1,0:T(8,128)(2,1)} %get-tuple-element.45.refs_5_) | copy-start | bytes 1572868
  69.0 5.1 %collective-permute-start.16 = (bf16[192,128]{1,0:T(8,128)(2,1)S(1)}, bf16[192,128]{1,0:T(8,128)(2,1)S(1)}, u32[]{:S(2)}, u32[]{:S(2)}) collective-permute-start(bf16[192,128]{1,0:T(8,128)(2,1)S(1)} %shard_map.101), channel_id=1, source_target_pairs={{0,2},{1,3},{2,0},{3,1},{4,6},{5,7},{6,4},{7,5},{8,10},{9,11},{10,... | collective-permute-start | bytes 147464 | tf_op jit(solution)/shard_map/ppermute | solution.py:348
  69.1 5.0 %collective-permute-start.21 = (f32[128,128]{1,0:T(8,128)S(1)}, f32[128,128]{1,0:T(8,128)S(1)}, u32[]{:S(2)}, u32[]{:S(2)}) collective-permute-start(f32[128,128]{1,0:T(8,128)S(1)} %copy-done.34), channel_id=1, source_target_pairs={{0,4},{1,5},{2,6},{3,7},{4,0},{5,1},{6,2},{7,3},{8,12},{9,13},{10,... | collective-permute-start | bytes 196616 | tf_op jit(solution)/shard_map/ppermute | solution.py:348
  69.1 4.9 %collective-permute-start.17 = (bf16[192,128]{1,0:T(8,128)(2,1)S(1)}, bf16[192,128]{1,0:T(8,128)(2,1)S(1)}, u32[]{:S(2)}, u32[]{:S(2)}) collective-permute-start(bf16[192,128]{1,0:T(8,128)(2,1)S(1)} %get-tuple-element.49.refs_2_), channel_id=1, source_target_pairs={{0,4},{1,5},{2,6},{3,7},{4,0},{5,1},{6,2},{7,3},{8,12},{9,13},{10,... | collective-permute-start | bytes 147464 | tf_op jit(solution)/shard_map/ppermute | solution.py:348
  69.6 4.4 %collective-permute-start.18 = (bf16[192,128]{1,0:T(8,128)(2,1)S(1)}, bf16[192,128]{1,0:T(8,128)(2,1)S(1)}, u32[]{:S(2)}, u32[]{:S(2)}) collective-permute-start(bf16[192,128]{1,0:T(8,128)(2,1)S(1)} %collective-permute-done.14.refs_6_.refs_3_), channel_id=1, source_target_pairs={{0,4},{1,5},{2,6},{3,7},{4,0},{5,1},{6,2},{7,3},{8,12},{9,13},{10,... | collective-permute-start | bytes 147464 | tf_op jit(solution)/shard_map/ppermute | solution.py:348
  69.7 4.3 %collective-permute-start.20 = (bf16[192,128]{1,0:T(8,128)(2,1)S(1)}, bf16[192,128]{1,0:T(8,128)(2,1)S(1)}, u32[]{:S(2)}, u32[]{:S(2)}) collective-permute-start(bf16[192,128]{1,0:T(8,128)(2,1)S(1)} %collective-permute-done.15.refs_7_.refs_5_), channel_id=1, source_target_pairs={{0,4},{1,5},{2,6},{3,7},{4,0},{5,1},{6,2},{7,3},{8,12},{9,13},{10,... | collective-permute-start | bytes 147464 | tf_op jit(solution)/shard_map/ppermute | solution.py:348
  74.0 1.2 %collective-permute-start.19 = (bf16[192,128]{1,0:T(8,128)(2,1)S(1)}, bf16[192,128]{1,0:T(8,128)(2,1)S(1)}, u32[]{:S(2)}, u32[]{:S(2)}) collective-permute-start(bf16[192,128]{1,0:T(8,128)(2,1)S(1)} %collective-permute-done.16.refs_4_), channel_id=1, source_target_pairs={{0,4},{1,5},{2,6},{3,7},{4,0},{5,1},{6,2},{7,3},{8,12},{9,13},{10,... | collective-permute-start | bytes 147464 | tf_op jit(solution)/shard_map/ppermute | solution.py:348
  76.1 1.3 %collective-permute-start.22 = (f32[128,128]{1,0:T(8,128)S(1)}, f32[128,128]{1,0:T(8,128)S(1)}, u32[]{:S(2)}, u32[]{:S(2)}) collective-permute-start(f32[128,128]{1,0:T(8,128)S(1)} %get-tuple-element.54), channel_id=1, source_target_pairs={{0,4},{1,5},{2,6},{3,7},{4,0},{5,1},{6,2},{7,3},{8,12},{9,13},{10,... | collective-permute-start | bytes 196616 | tf_op jit(solution)/shard_map/ppermute | solution.py:348
  77.4 7.2 %copy-start.12 = (bf16[384,256]{1,0:T(8,128)(2,1)S(1)}, bf16[384,256]{1,0:T(8,128)(2,1)}, u32[]{:S(2)}) copy-start(bf16[384,256]{1,0:T(8,128)(2,1)} %refs_2_.5) | copy-start | bytes 589828
  77.4 7.2 %copy-start.13 = (bf16[384,256]{1,0:T(8,128)(2,1)S(1)}, bf16[384,256]{1,0:T(8,128)(2,1)}, u32[]{:S(2)}) copy-start(bf16[384,256]{1,0:T(8,128)(2,1)} %refs_1_.13) | copy-start | bytes 589828
  77.4 7.1 %copy-start.15 = (bf16[4,384,384]{2,1,0:T(8,128)(2,1)S(1)}, bf16[4,384,384]{2,1,0:T(8,128)(2,1)}, u32[]{:S(2)}) copy-start(bf16[4,384,384]{2,1,0:T(8,128)(2,1)} %copy-done.14) | copy-start | bytes 3538948
  77.4 7.1 %copy-start.23 = (f32[128,128]{1,0:T(8,128)S(1)}, f32[128,128]{1,0:T(8,128)}, u32[]{:S(2)}) copy-start(f32[128,128]{1,0:T(8,128)} %copy-done.22) | copy-start | bytes 196612
  80.4 9.0 %collective-permute-start.23 = (f32[96,2048]{1,0:T(8,128)S(1)}, f32[96,2048]{1,0:T(8,128)S(1)}, u32[]{:S(2)}, u32[]{:S(2)}) collective-permute-start(f32[96,2048]{1,0:T(8,128)S(1)} %get-tuple-element.56), channel_id=1, source_target_pairs={{0,4},{1,5},{2,6},{3,7},{4,0},{5,1},{6,2},{7,3},{8,12},{9,13},{10,... | collective-permute-start | bytes 2359304 | tf_op jit(solution)/shard_map/ppermute | solution.py:348
  80.7 8.8 %collective-permute-start.24 = (f32[96,2048]{1,0:T(8,128)S(1)}, f32[96,2048]{1,0:T(8,128)S(1)}, u32[]{:S(2)}, u32[]{:S(2)}) collective-permute-start(f32[96,2048]{1,0:T(8,128)S(1)} %get-tuple-element.58), channel_id=1, source_target_pairs={{0,4},{1,5},{2,6},{3,7},{4,0},{5,1},{6,2},{7,3},{8,12},{9,13},{10,... | collective-permute-start | bytes 2359304 | tf_op jit(solution)/shard_map/ppermute | solution.py:348
  81.0 6.6 %collective-permute-start.27 = (f32[128,128]{1,0:T(8,128)S(1)}, f32[128,128]{1,0:T(8,128)S(1)}, u32[]{:S(2)}, u32[]{:S(2)}) collective-permute-start(f32[128,128]{1,0:T(8,128)S(1)} %add.15.refs_11_.refs_8_), channel_id=1, source_target_pairs={{0,24},{1,25},{2,26},{3,27},{4,28},{5,29},{6,30},{7,31},{8,16},{9,... | collective-permute-start | bytes 196616 | tf_op jit(solution)/shard_map/ppermute | solution.py:348
  82.4 5.2 %collective-permute-start.26 = (f32[128,128]{1,0:T(8,128)S(1)}, f32[128,128]{1,0:T(8,128)S(1)}, u32[]{:S(2)}, u32[]{:S(2)}) collective-permute-start(f32[128,128]{1,0:T(8,128)S(1)} %add.15.refs_11_.refs_8_), channel_id=1, source_target_pairs={{0,16},{1,17},{2,18},{3,19},{4,20},{5,21},{6,22},{7,23},{8,24},{9,... | collective-permute-start | bytes 196616 | tf_op jit(solution)/shard_map/ppermute | solution.py:348
  84.4 4.3 %collective-permute-start.25 = (f32[128,128]{1,0:T(8,128)S(1)}, f32[128,128]{1,0:T(8,128)S(1)}, u32[]{:S(2)}, u32[]{:S(2)}) collective-permute-start(f32[128,128]{1,0:T(8,128)S(1)} %add.15.refs_11_.refs_8_), channel_id=1, source_target_pairs={{0,8},{1,9},{2,10},{3,11},{4,12},{5,13},{6,14},{7,15},{8,0},{9,1},... | collective-permute-start | bytes 196616 | tf_op jit(solution)/shard_map/ppermute | solution.py:348
  89.3 1.7 %collective-permute-start.28 = (f32[128,128]{1,0:T(8,128)S(1)}, f32[128,128]{1,0:T(8,128)S(1)}, u32[]{:S(2)}, u32[]{:S(2)}) collective-permute-start(f32[128,128]{1,0:T(8,128)S(1)} %get-tuple-element.66), channel_id=1, source_target_pairs={{0,4},{1,5},{2,6},{3,7},{4,0},{5,1},{6,2},{7,3},{8,12},{9,13},{10,... | collective-permute-start | bytes 196616 | tf_op jit(solution)/shard_map/ppermute | solution.py:348
  (17 other events, 13.4 us)

commit v20 on v18

--- a/solution.py
+++ b/solution.py
@@ -539,15 +539,15 @@
                 fetch(attn.shape, (attn, all_of, all_of)),
                 fetch(
                     (4 * DH, wide),
-                    (weight, own_columns(0), rows_at(0, DH)),
-                    *((arrived[s], all_of, rows_at(s * DH, DH)) for s in (1, 2, 3)),
-                ),
-                fetch(
-                    (4 * DH, wide),
                     (weight, own_columns(1), rows_at(0, DH)),
                     (second[1], all_of, rows_at(DH, DH)),
                     (second[3], all_of, rows_at(3 * DH, DH)),
                     *((a, all_of, quarter(n)) for n, a in enumerate(second[2])),
+                ),
+                fetch(
+                    (4 * DH, wide),
+                    (weight, own_columns(0), rows_at(0, DH)),
+                    *((arrived[s], all_of, rows_at(s * DH, DH)) for s in (1, 2, 3)),
                 ),
             ],
             [spots],
@@ -557,7 +557,7 @@
             lazy=True,
         )
         joins = [outs[0], send(outs[1], 1, 0), outs[2], send(outs[3], 1, 0)]
-        return joins, [spots[0], spots[1]]
+        return joins, [spots[1], spots[0]]
 
     return [both[s] for s in range(4)], [across[s] for s in range(4)], mix
 

time: 91.2 us -> 90.6 us (level)
  waiting for transfers between devices: 22.2 us -> 20.3 us
  starting transfers between devices: 27.3 us -> 28.3 us
    ppermute x29, waiting for transfers between devices: 22.2 us -> 20.3 us  [send(): return lax.ppermute(x, ('ctx', 'head'), pairs)]
    ppermute x29, starting transfers between devices: 23.3 us -> 24.3 us  [send(): return lax.ppermute(x, ('ctx', 'head'), pairs)]
  transfers between devices with their start and end apart: 30 -> 30, of which waited for: 13 -> 11; matrix products, arithmetic and copies ran while one was open for 5% -> 5% of each run, Pallas kernels for 17% -> 17%
where the time goes in v20:
time: 90.6 us; the launch traced here: 89.9 us
  starting transfers between devices  28.3 us (31%)
  Pallas kernels  23.3 us (26%)
  waiting for transfers between devices  20.3 us (22%)
  local copies, waits for them, and re-layouts  14.5 us (16%)
  other arithmetic  2.46 us (3%)
  between operations  0.96 us (1%)
    ppermute x29, starting transfers between devices, send(): return lax.ppermute(x, ('ctx', 'head'), pairs)  24.3 us
    pallas_call x12, Pallas kernels, call(): pl.pallas_call(kernel, out_shape=[jax.ShapeDtypeStruct(s, t) for s, t in...  23.3 us
    ppermute x29, waiting for transfers between devices, send(): return lax.ppermute(x, ('ctx', 'head'), pairs)  20.3 us
    unnamed x58, local copies, waits for them, and re-layouts  12.7 us
    all_to_all x1, starting transfers between devices, on_device(): attn = lax.all_to_all(attn, 'head', 0, 0, tiled=True)  3.99 us
    dynamic_slice x1, local copies, waits for them, and re-layouts, on_device(): lax.dynamic_slice(out_weight, (core * DH, colour * wide), (DH, wide))  1.88 us
  transfers between devices with their start and end apart: 30, of which 11 were waited for; matrix products, arithmetic and copies ran while one was open for 5% of the time, Pallas kernels for 17%

profile of v20, /device:TPU:0, one launch (start us, length us, event | category | flops | bytes accessed | tf_op | source)
XLA Modules:
  0.0 89.9 jit_solution(17424537318873670191)
XLA Ops:
  1.2 1.9 %dynamic_slice.3 = bf16[128,2048]{1,0:T(8,128)(2,1)} dynamic-slice(bf16[256,4096]{1,0:T(8,128)(2,1)} %refs_7_.3, s32[]{:T(128)S(6)} %select_n.6, s32[]{:T(128)S(6)} %select_n.7), dynamic_slice_sizes={128,2048} | dynamic-slice | bytes 1048580 | tf_op jit(solution)/shard_map/dynamic_slice | solution.py:388
  3.0 4.6 %collective-permute-start.8 = (bf16[128,2048]{1,0:T(8,128)(2,1)}, bf16[128,2048]{1,0:T(8,128)(2,1)S(1)}, u32[]{:S(2)}, u32[]{:S(2)}) collective-permute-start(bf16[128,2048]{1,0:T(8,128)(2,1)} %dynamic_slice.3), channel_id=1, source_target_pairs={{0,3},{1,0},{2,1},{3,2},{4,7},{5,4},{6,5},{7,6},{8,11},{9,8},{10,9... | collective-permute-start | bytes 1572872 | tf_op jit(solution)/shard_map/ppermute | solution.py:348
  7.8 1.2 %pad_maximum_fusion.refs_2_ = bf16[3,384,256]{2,1,0:T(8,128)(2,1)S(1)} fusion(bf16[1,384,256]{2,1,0:T(8,128)(2,1)} %bitcast.18, bf16[1,384,256]{2,1,0:T(8,128)(2,1)} %bitcast.19, bf16[1,384,256]{2,1,0:T(8,128)(2,1)} %bitcast.17), kind=kLoop, calls=%fused_computation | loop fusion | flops 589824 | bytes 1179648 | tf_op jit(solution)/shard_map/stack | solution.py:398
  9.0 2.6 %shard_map.93 = (bf16[4,384,384]{2,1,0:T(8,128)(2,1)S(1)}, f32[384,128]{1,0:T(8,128)S(1)}, f32[384,128]{1,0:T(8,128)}, bf16[384,128]{1,0:T(8,128)(2,1)}, f32[128,128]{1,0:T(8,128)S(1)}, /*index=5*/f32[128,128]{1,0:T(8,128)}) custom-call(s32[3,3]{1,0:T(4,128)S(1)} %copy-done.26, s32[3]{0:T(128)S(1)} %pad_add_fusion.2.refs_1_.refs_0_, ...), custom_call_target="tpu_custom_call" | custom-call | flops 264241152 | bytes 2392064 | tf_op jit(solution)/shard_map/pallas_call | solution.py:103
  11.5 1.1 %copy-done.10 = bf16[4,384,384]{2,1,0:T(8,128)(2,1)} copy-done((bf16[4,384,384]{2,1,0:T(8,128)(2,1)}, bf16[4,384,384]{2,1,0:T(8,128)(2,1)S(1)}, u32[]{:S(2)}) %copy-start.10) | copy-done | bytes 1179672
  12.6 0.6 copy-done.12
  13.2 0.7 copy-done.18
  14.6 1.1 %collective-permute-done.1.refs_1_.refs_8_ = bf16[384,128]{1,0:T(8,128)(2,1)S(1)} collective-permute-done((bf16[384,128]{1,0:T(8,128)(2,1)}, bf16[384,128]{1,0:T(8,128)(2,1)S(1)}, u32[]{:S(2)}, u32[]{:S(2)}) %collective-permute-start.1) | collective-permute-done | bytes 98336 | tf_op jit(solution)/shard_map/ppermute | solution.py:348
  15.7 0.6 copy-done.14
  16.3 0.9 add.12
  17.2 2.5 %collective-permute-start.6 = (f32[128,128]{1,0:T(8,128)S(1)}, f32[128,128]{1,0:T(8,128)S(1)}, u32[]{:S(2)}, u32[]{:S(2)}) collective-permute-start(f32[128,128]{1,0:T(8,128)S(1)} %add.12), channel_id=1, source_target_pairs={{0,24},{1,25},{2,26},{3,27},{4,28},{5,29},{6,30},{7,31},{8,16},{9,... | collective-permute-start | bytes 196616 | tf_op jit(solution)/shard_map/ppermute | solution.py:348
  20.8 1.6 %collective-permute-done.6.refs_6_ = f32[128,128]{1,0:T(8,128)S(1)} collective-permute-done((f32[128,128]{1,0:T(8,128)S(1)}, f32[128,128]{1,0:T(8,128)S(1)}, u32[]{:S(2)}, u32[]{:S(2)}) %collective-permute-start.6) | collective-permute-done | bytes 65568 | tf_op jit(solution)/shard_map/ppermute | solution.py:348
  22.5 1.5 %collective-permute-done.5.refs_5_ = f32[128,128]{1,0:T(8,128)S(1)} collective-permute-done((f32[128,128]{1,0:T(8,128)S(1)}, f32[128,128]{1,0:T(8,128)S(1)}, u32[]{:S(2)}, u32[]{:S(2)}) %collective-permute-start.5) | collective-permute-done | bytes 65568 | tf_op jit(solution)/shard_map/ppermute | solution.py:348
  24.5 0.9 %copy-done.6 = bf16[384,256]{1,0:T(8,128)(2,1)S(1)} copy-done((bf16[384,256]{1,0:T(8,128)(2,1)S(1)}, bf16[384,256]{1,0:T(8,128)(2,1)}, u32[]{:S(2)}) %copy-start.6) | copy-done | bytes 196632
  25.4 0.8 copy-done.13
  26.3 0.9 copy-done.15
  27.2 0.9 %copy-done.19 = f32[384,128]{1,0:T(8,128)S(1)} copy-done((f32[384,128]{1,0:T(8,128)S(1)}, f32[384,128]{1,0:T(8,128)}, u32[]{:S(2)}) %copy-start.19) | copy-done | bytes 196632
  28.1 1.2 %shard_map.95 = (bf16[4,192,128]{2,1,0:T(8,128)(2,1)S(1)}, f32[128,128]{1,0:T(8,128)S(1)}, f32[128,128]{1,0:T(8,128)S(1)}) custom-call(s32[4]{0:T(128)S(1)} %add_convert_fusion.refs_0_, s32[3]{0:T(128)S(1)} %pad_add_fusion.2.refs_1_.refs_0_, f32[128,128]{1,0:T(8,128)S(1)} %copy-done.13, f32[128,128]{1,0:T(8,128)} %collective-permute-done.3.refs_3_, ...), custom_call_target="tpu_custom_call" | custom-call | flops 1 | bytes 1343488 | tf_op jit(solution)/shard_map/pallas_call | solution.py:103
  29.4 0.6 copy-done.16
  30.0 0.6 copy-done.27
  30.6 0.7 copy-done.20
  31.3 0.7 collective-permute-done.7.refs_0_
  32.1 1.5 %collective-permute-start.10 = (bf16[128,2048]{1,0:T(8,128)(2,1)}, bf16[128,2048]{1,0:T(8,128)(2,1)}, u32[]{:S(2)}, u32[]{:S(2)}) collective-permute-start(bf16[128,2048]{1,0:T(8,128)(2,1)} %get-tuple-element.45.refs_5_.refs_10_), channel_id=1, source_target_pairs={{0,16},{1,17},{2,18},{3,19},{4,20},{5,21},{6,22},{7,23},{8,24},{9,... | collective-permute-start | bytes 1572872 | tf_op jit(solution)/shard_map/ppermute | solution.py:348
  33.6 1.5 %collective-permute-start.11 = (bf16[128,2048]{1,0:T(8,128)(2,1)}, bf16[128,2048]{1,0:T(8,128)(2,1)S(1)}, u32[]{:S(2)}, u32[]{:S(2)}) collective-permute-start(bf16[128,2048]{1,0:T(8,128)(2,1)} %get-tuple-element.44.refs_4_.refs_8_), channel_id=1, source_target_pairs={{0,1},{1,2},{2,3},{3,0},{4,5},{5,6},{6,7},{7,4},{8,9},{9,10},{10,1... | collective-permute-start | bytes 1572872 | tf_op jit(solution)/shard_map/ppermute | solution.py:348
  35.1 1.5 %collective-permute-start.9 = (bf16[128,2048]{1,0:T(8,128)(2,1)}, bf16[128,2048]{1,0:T(8,128)(2,1)}, u32[]{:S(2)}, u32[]{:S(2)}) collective-permute-start(bf16[128,2048]{1,0:T(8,128)(2,1)} %get-tuple-element.44.refs_4_.refs_8_), channel_id=1, source_target_pairs={{0,8},{1,9},{2,10},{3,11},{4,12},{5,13},{6,14},{7,15},{8,0},{9,1},... | collective-permute-start | bytes 1572872 | tf_op jit(solution)/shard_map/ppermute | solution.py:348
  36.7 4.0 %all-to-all-start = ((bf16[4,192,128]{2,1,0:T(8,128)(2,1)}), bf16[4,192,128]{2,1,0:T(8,128)(2,1)}, u32[]{:S(2)}, u32[]{:S(2)}) async-start(bf16[4,192,128]{2,1,0:T(8,128)(2,1)} %copy-done.20), calls=%async_computation | async-start | bytes 393216 | tf_op jit(solution)/shard_map/all_to_all | solution.py:415
  40.7 1.1 %copy-done.1 = bf16[96,4096]{1,0:T(8,128)(2,1)S(1)} copy-done((bf16[96,4096]{1,0:T(8,128)(2,1)S(1)}, bf16[96,4096]{1,0:T(8,128)(2,1)}, u32[]{:S(2)}) %copy-start.1) | copy-done | bytes 786456
  41.8 1.0 %copy-done.4 = bf16[128,2048]{1,0:T(8,128)(2,1)S(1)} copy-done((bf16[128,2048]{1,0:T(8,128)(2,1)S(1)}, bf16[128,2048]{1,0:T(8,128)(2,1)}, u32[]{:S(2)}) %copy-start.4) | copy-done | bytes 524312
  42.9 2.5 %shard_map.97 = (bf16[192,128]{1,0:T(8,128)(2,1)S(1)}, f32[192,256]{1,0:T(8,128)S(1)}) custom-call(s32[4]{0:T(128)S(1)} %pad_add_fusion.1.refs_0_, bf16[96,4096]{1,0:T(8,128)(2,1)S(1)} %copy-done.1, bf16[96,4096]{1,0:T(8,128)(2,1)S(1)} %collective-permute-done.refs_3_.refs_2_, bf16[256,4096]{1,0:T(8,128)(2,1)S(1)} %copy-done, ...), custom_call_target="tpu_custom_call" | custom-call | flops 402653184 | bytes 4964352 | tf_op jit(solution)/shard_map/pallas_call | solution.py:103
  45.8 4.8 %collective-permute-done.11.refs_6_.refs_3_.refs_9_ = bf16[128,2048]{1,0:T(8,128)(2,1)S(1)} collective-permute-done((bf16[128,2048]{1,0:T(8,128)(2,1)}, bf16[128,2048]{1,0:T(8,128)(2,1)S(1)}, u32[]{:S(2)}, u32[]{:S(2)}) %collective-permute-start.11) | collective-permute-done | bytes 524320 | tf_op jit(solution)/shard_map/ppermute | solution.py:348
  50.5 3.1 %shard_map.98 = (bf16[192,128]{1,0:T(8,128)(2,1)}, bf16[192,128]{1,0:T(8,128)(2,1)}, bf16[128,1024]{1,0:T(8,128)(2,1)}, bf16[128,1024]{1,0:T(8,128)(2,1)}) custom-call(s32[4]{0:T(128)S(1)} %pad_add_fusion.1.refs_0_, bf16[96,4096]{1,0:T(8,128)(2,1)S(1)} %copy-done.1, bf16[96,4096]{1,0:T(8,128)(2,1)S(1)} %collective-permute-done.refs_3_.refs_2_, ...), custom_call_target="tpu_custom_call" | custom-call | flops 201326592 | bytes 3964928 | tf_op jit(solution)/shard_map/pallas_call | solution.py:103
  53.7 1.4 %collective-permute-start.12 = (bf16[128,1024]{1,0:T(8,128)(2,1)}, bf16[128,1024]{1,0:T(8,128)(2,1)}, u32[]{:S(2)}, u32[]{:S(2)}) collective-permute-start(bf16[128,1024]{1,0:T(8,128)(2,1)} %get-tuple-element.47), channel_id=1, source_target_pairs={{0,8},{1,9},{2,10},{3,11},{4,12},{5,13},{6,14},{7,15},{8,0},{9,1},... | collective-permute-start | bytes 786440 | tf_op jit(solution)/shard_map/ppermute | solution.py:348
  55.6 2.9 %collective-permute-start.14 = (bf16[192,128]{1,0:T(8,128)(2,1)}, bf16[192,128]{1,0:T(8,128)(2,1)S(1)}, u32[]{:S(2)}, u32[]{:S(2)}) collective-permute-start(bf16[192,128]{1,0:T(8,128)(2,1)} %get-tuple-element.50), channel_id=1, source_target_pairs={{0,3},{1,0},{2,1},{3,2},{4,7},{5,4},{6,5},{7,6},{8,11},{9,8},{10,9... | collective-permute-start | bytes 147464 | tf_op jit(solution)/shard_map/ppermute | solution.py:348
  58.5 1.1 %copy-done.2 = bf16[96,4096]{1,0:T(8,128)(2,1)S(1)} copy-done((bf16[96,4096]{1,0:T(8,128)(2,1)S(1)}, bf16[96,4096]{1,0:T(8,128)(2,1)}, u32[]{:S(2)}) %copy-start.2) | copy-done | bytes 786456
  59.7 0.7 copy-done.24
  60.4 1.0 %shard_map.99.refs_5_ = f32[192,128]{1,0:T(8,128)S(1)} custom-call(s32[4]{0:T(128)S(1)} %copy-done.24, bf16[96,4096]{1,0:T(8,128)(2,1)S(1)} %copy-done.2, bf16[96,4096]{1,0:T(8,128)(2,1)S(1)} %collective-permute-done.refs_3_.refs_2_, bf16[128,2048]{1,0:T(8,128)(2,1)S(1)} %collective-permute-done.11.refs_6_.refs_3_.refs_9_, ...), custom_call_target="tpu_custom_call" | custom-call | flops 100663296 | bytes 2195456 | tf_op jit(solution)/shard_map/pallas_call | solution.py:103
  61.4 3.5 %collective-permute-done.15.refs_7_.refs_5_ = bf16[192,128]{1,0:T(8,128)(2,1)S(1)} collective-permute-done((bf16[192,128]{1,0:T(8,128)(2,1)}, bf16[192,128]{1,0:T(8,128)(2,1)S(1)}, u32[]{:S(2)}, u32[]{:S(2)}) %collective-permute-start.15) | collective-permute-done | bytes 49184 | tf_op jit(solution)/shard_map/ppermute | solution.py:348
  64.9 2.0 %shard_map.100 = bf16[192,128]{1,0:T(8,128)(2,1)S(1)} custom-call(s32[4]{0:T(128)S(1)} %copy-done.25, bf16[96,4096]{1,0:T(8,128)(2,1)S(1)} %copy-done.2, bf16[96,4096]{1,0:T(8,128)(2,1)S(1)} %collective-permute-done.refs_3_.refs_2_, bf16[128,1024]{1,0:T(8,128)(2,1)} %collective-permute-done.12.refs_3_.refs_5_, ...), custom_call_target="tpu_custom_call" | custom-call | flops 100663296 | bytes 2244608 | tf_op jit(solution)/shard_map/pallas_call | solution.py:103
  68.2 3.9 %collective-permute-done.16.refs_4_ = bf16[192,128]{1,0:T(8,128)(2,1)S(1)} collective-permute-done((bf16[192,128]{1,0:T(8,128)(2,1)S(1)}, bf16[192,128]{1,0:T(8,128)(2,1)S(1)}, u32[]{:S(2)}, u32[]{:S(2)}) %collective-permute-start.16) | collective-permute-done | bytes 49184 | tf_op jit(solution)/shard_map/ppermute | solution.py:348
  72.1 1.2 %collective-permute-done.19.refs_8_ = bf16[192,128]{1,0:T(8,128)(2,1)S(1)} collective-permute-done((bf16[192,128]{1,0:T(8,128)(2,1)S(1)}, bf16[192,128]{1,0:T(8,128)(2,1)S(1)}, u32[]{:S(2)}, u32[]{:S(2)}) %collective-permute-start.19) | collective-permute-done | bytes 49184 | tf_op jit(solution)/shard_map/ppermute | solution.py:348
  73.3 0.8 shard_map.101
  74.3 1.1 %collective-permute-done.22.refs_2_ = f32[128,128]{1,0:T(8,128)S(1)} collective-permute-done((f32[128,128]{1,0:T(8,128)S(1)}, f32[128,128]{1,0:T(8,128)S(1)}, u32[]{:S(2)}, u32[]{:S(2)}) %collective-permute-start.22) | collective-permute-done | bytes 65568 | tf_op jit(solution)/shard_map/ppermute | solution.py:348
  75.5 3.3 %shard_map.102 = (f32[96,2048]{1,0:T(8,128)S(1)}, f32[96,2048]{1,0:T(8,128)S(1)}, f32[96,2048]{1,0:T(8,128)S(1)}, f32[96,2048]{1,0:T(8,128)S(1)}) custom-call(s32[4]{0:T(128)S(1)} %copy-done.25, bf16[4,192,128]{2,1,0:T(8,128)(2,1)} %all-to-all-done.refs_4_.refs_1_, bf16[256,4096]{1,0:T(8,128)(2,1)S(1)} %copy-done, ...), custom_call_target="tpu_custom_call" | custom-call | flops 805306368 | bytes 10682368 | tf_op jit(solution)/shard_map/pallas_call | solution.py:103
  79.3 1.2 %collective-permute-start.27 = (f32[128,128]{1,0:T(8,128)S(1)}, f32[128,128]{1,0:T(8,128)S(1)}, u32[]{:S(2)}, u32[]{:S(2)}) collective-permute-start(f32[128,128]{1,0:T(8,128)S(1)} %add.15.refs_11_.refs_8_), channel_id=1, source_target_pairs={{0,24},{1,25},{2,26},{3,27},{4,28},{5,29},{6,30},{7,31},{8,16},{9,... | collective-permute-start | bytes 196616 | tf_op jit(solution)/shard_map/ppermute | solution.py:348
  81.0 1.8 %collective-permute-start.25 = (f32[128,128]{1,0:T(8,128)S(1)}, f32[128,128]{1,0:T(8,128)S(1)}, u32[]{:S(2)}, u32[]{:S(2)}) collective-permute-start(f32[128,128]{1,0:T(8,128)S(1)} %add.15.refs_11_.refs_8_), channel_id=1, source_target_pairs={{0,8},{1,9},{2,10},{3,11},{4,12},{5,13},{6,14},{7,15},{8,0},{9,1},... | collective-permute-start | bytes 196616 | tf_op jit(solution)/shard_map/ppermute | solution.py:348
  82.9 3.0 %shard_map.104 = (bf16[384,256]{1,0:T(8,128)(2,1)}, f32[384,256]{1,0:T(8,128)S(1)}, f32[384,256]{1,0:T(8,128)S(1)}) custom-call(s32[3]{0:T(128)S(1)} %copy-done.22, bf16[384,256]{1,0:T(8,128)(2,1)S(1)} %copy-done.7, bf16[384,256]{1,0:T(8,128)(2,1)S(1)} %copy-done.9, bf16[384,256]{1,0:T(8,128)(2,1)S(1)} %copy-done.8, ...), custom_call_target="tpu_custom_call" | custom-call | flops 528482304 | bytes 3080192 | tf_op jit(solution)/shard_map/pallas_call | solution.py:103
  86.7 1.6 %shard_map.103 = (bf16[96,4096]{1,0:T(8,128)(2,1)}, f32[8,128]{1,0:T(8,128)S(1)}) custom-call(s32[2]{0:T(128)S(1)} %pad_add_fusion.refs_0_, f32[96,2048]{1,0:T(8,128)S(1)} %get-tuple-element.55.refs_1_, f32[96,2048]{1,0:T(8,128)S(1)} %collective-permute-done.23.refs_2_, f32[96,2048]{1,0:T(8,128)S(1)} %get-tuple-element.57.refs_3_, ...), custom_call_target="tpu_custom_call" | custom-call | flops 1 | bytes 3936256 | tf_op jit(solution)/shard_map/pallas_call | solution.py:103
  88.2 1.6 %shard_map.106 = (bf16[384,256]{1,0:T(8,128)(2,1)}, bf16[384,256]{1,0:T(8,128)(2,1)}) custom-call(s32[3]{0:T(128)S(1)} %copy-done.22, bf16[384,256]{1,0:T(8,128)(2,1)S(1)} %copy-done.9, bf16[384,256]{1,0:T(8,128)(2,1)S(1)} %copy-done.8, f32[384,256]{1,0:T(8,128)S(1)} %get-tuple-element.63.refs_6_.refs_3_, f32[384,256]{1,0:T(8,128)S(1)} %get-tuple-element.64.refs_4_, ...), custom_call_target="tpu_custom_call" | custom-call | flops 1 | bytes 1703936 | tf_op jit(solution)/shard_map/pallas_call | solution.py:103
  (93 shorter events, 7.5 us)
Async XLA Ops:
  0.6 8.3 %copy-start.26 = (s32[3,3]{1,0:T(4,128)S(1)}, s32[3,3]{1,0:T(4,128)}, u32[]{:S(2)}) copy-start(s32[3,3]{1,0:T(4,128)} %refs_0_.1) | copy-start | bytes 112
  0.6 8.3 %collective-permute-start = (bf16[96,4096]{1,0:T(8,128)(2,1)}, bf16[96,4096]{1,0:T(8,128)(2,1)S(1)}, u32[]{:S(2)}, u32[]{:S(2)}) collective-permute-start(bf16[96,4096]{1,0:T(8,128)(2,1)} %refs_1_.10), channel_id=1, source_target_pairs={{0,4},{1,5},{2,6},{3,7},{4,0},{5,1},{6,2},{7,3},{8,12},{9,13},{10,... | collective-permute-start | bytes 2359304 | tf_op jit(solution)/shard_map/ppermute | solution.py:348
  3.0 27.6 %collective-permute-start.8 = (bf16[128,2048]{1,0:T(8,128)(2,1)}, bf16[128,2048]{1,0:T(8,128)(2,1)S(1)}, u32[]{:S(2)}, u32[]{:S(2)}) collective-permute-start(bf16[128,2048]{1,0:T(8,128)(2,1)} %dynamic_slice.3), channel_id=1, source_target_pairs={{0,3},{1,0},{2,1},{3,2},{4,7},{5,4},{6,5},{7,6},{8,11},{9,8},{10,9... | collective-permute-start | bytes 1572872 | tf_op jit(solution)/shard_map/ppermute | solution.py:348
  7.7 24.3 %collective-permute-start.7 = (bf16[128,2048]{1,0:T(8,128)(2,1)}, bf16[128,2048]{1,0:T(8,128)(2,1)}, u32[]{:S(2)}, u32[]{:S(2)}) collective-permute-start(bf16[128,2048]{1,0:T(8,128)(2,1)} %dynamic_slice.3), channel_id=1, source_target_pairs={{0,1},{1,2},{2,3},{3,0},{4,5},{5,6},{6,7},{7,4},{8,9},{9,10},{10,1... | collective-permute-start | bytes 1572872 | tf_op jit(solution)/shard_map/ppermute | solution.py:348
  7.8 21.6 %copy-start.21 = (s32[3]{0:T(128)}, s32[3]{0:T(128)S(1)}, u32[]{:S(2)}) copy-start(s32[3]{0:T(128)S(1)} %pad_add_fusion.2.refs_1_.refs_0_) | copy-start | bytes 40
  8.9 31.7 %copy-start = (bf16[256,4096]{1,0:T(8,128)(2,1)S(1)}, bf16[256,4096]{1,0:T(8,128)(2,1)}, u32[]{:S(2)}) copy-start(bf16[256,4096]{1,0:T(8,128)(2,1)} %refs_7_.3) | copy-start | bytes 6291460
  11.5 1.1 %copy-start.10 = (bf16[4,384,384]{2,1,0:T(8,128)(2,1)}, bf16[4,384,384]{2,1,0:T(8,128)(2,1)S(1)}, u32[]{:S(2)}) copy-start(bf16[4,384,384]{2,1,0:T(8,128)(2,1)S(1)} %get-tuple-element.61.refs_5_) | copy-start | bytes 3538948
  13.9 1.8 %collective-permute-start.2 = (f32[384,128]{1,0:T(8,128)}, f32[384,128]{1,0:T(8,128)}, u32[]{:S(2)}, u32[]{:S(2)}) collective-permute-start(f32[384,128]{1,0:T(8,128)} %get-tuple-element.39), channel_id=1, source_target_pairs={{0,4},{1,5},{2,6},{3,7},{4,0},{5,1},{6,2},{7,3},{8,12},{9,13},{10,... | collective-permute-start | bytes 589832 | tf_op jit(solution)/shard_map/ppermute | solution.py:348
  14.1 1.6 %collective-permute-start.1 = (bf16[384,128]{1,0:T(8,128)(2,1)}, bf16[384,128]{1,0:T(8,128)(2,1)S(1)}, u32[]{:S(2)}, u32[]{:S(2)}) collective-permute-start(bf16[384,128]{1,0:T(8,128)(2,1)} %get-tuple-element.38), channel_id=1, source_target_pairs={{0,4},{1,5},{2,6},{3,7},{4,0},{5,1},{6,2},{7,3},{8,12},{9,13},{10,... | collective-permute-start | bytes 294920 | tf_op jit(solution)/shard_map/ppermute | solution.py:348
  14.4 1.9 %collective-permute-start.3 = (f32[128,128]{1,0:T(8,128)}, f32[128,128]{1,0:T(8,128)}, u32[]{:S(2)}, u32[]{:S(2)}) collective-permute-start(f32[128,128]{1,0:T(8,128)} %get-tuple-element.40), channel_id=1, source_target_pairs={{0,4},{1,5},{2,6},{3,7},{4,0},{5,1},{6,2},{7,3},{8,12},{9,13},{10,... | collective-permute-start | bytes 196616 | tf_op jit(solution)/shard_map/ppermute | solution.py:348
  17.2 5.2 %collective-permute-start.6 = (f32[128,128]{1,0:T(8,128)S(1)}, f32[128,128]{1,0:T(8,128)S(1)}, u32[]{:S(2)}, u32[]{:S(2)}) collective-permute-start(f32[128,128]{1,0:T(8,128)S(1)} %add.12), channel_id=1, source_target_pairs={{0,24},{1,25},{2,26},{3,27},{4,28},{5,29},{6,30},{7,31},{8,16},{9,... | collective-permute-start | bytes 196616 | tf_op jit(solution)/shard_map/ppermute | solution.py:348
  19.7 4.3 %collective-permute-start.5 = (f32[128,128]{1,0:T(8,128)S(1)}, f32[128,128]{1,0:T(8,128)S(1)}, u32[]{:S(2)}, u32[]{:S(2)}) collective-permute-start(f32[128,128]{1,0:T(8,128)S(1)} %add.12), channel_id=1, source_target_pairs={{0,16},{1,17},{2,18},{3,19},{4,20},{5,21},{6,22},{7,23},{8,24},{9,... | collective-permute-start | bytes 196616 | tf_op jit(solution)/shard_map/ppermute | solution.py:348
  20.2 4.3 %collective-permute-start.4 = (f32[128,128]{1,0:T(8,128)S(1)}, f32[128,128]{1,0:T(8,128)S(1)}, u32[]{:S(2)}, u32[]{:S(2)}) collective-permute-start(f32[128,128]{1,0:T(8,128)S(1)} %add.12), channel_id=1, source_target_pairs={{0,8},{1,9},{2,10},{3,11},{4,12},{5,13},{6,14},{7,15},{8,0},{9,1},... | collective-permute-start | bytes 196616 | tf_op jit(solution)/shard_map/ppermute | solution.py:348
  24.5 0.9 %copy-start.6 = (bf16[384,256]{1,0:T(8,128)(2,1)S(1)}, bf16[384,256]{1,0:T(8,128)(2,1)}, u32[]{:S(2)}) copy-start(bf16[384,256]{1,0:T(8,128)(2,1)} %refs_1_.12) | copy-start | bytes 589828
  32.1 13.7 %collective-permute-start.10 = (bf16[128,2048]{1,0:T(8,128)(2,1)}, bf16[128,2048]{1,0:T(8,128)(2,1)}, u32[]{:S(2)}, u32[]{:S(2)}) collective-permute-start(bf16[128,2048]{1,0:T(8,128)(2,1)} %get-tuple-element.45.refs_5_.refs_10_), channel_id=1, source_target_pairs={{0,16},{1,17},{2,18},{3,19},{4,20},{5,21},{6,22},{7,23},{8,24},{9,... | collective-permute-start | bytes 1572872 | tf_op jit(solution)/shard_map/ppermute | solution.py:348
  33.6 17.0 %collective-permute-start.11 = (bf16[128,2048]{1,0:T(8,128)(2,1)}, bf16[128,2048]{1,0:T(8,128)(2,1)S(1)}, u32[]{:S(2)}, u32[]{:S(2)}) collective-permute-start(bf16[128,2048]{1,0:T(8,128)(2,1)} %get-tuple-element.44.refs_4_.refs_8_), channel_id=1, source_target_pairs={{0,1},{1,2},{2,3},{3,0},{4,5},{5,6},{6,7},{7,4},{8,9},{9,10},{10,1... | collective-permute-start | bytes 1572872 | tf_op jit(solution)/shard_map/ppermute | solution.py:348
  35.1 15.4 %collective-permute-start.9 = (bf16[128,2048]{1,0:T(8,128)(2,1)}, bf16[128,2048]{1,0:T(8,128)(2,1)}, u32[]{:S(2)}, u32[]{:S(2)}) collective-permute-start(bf16[128,2048]{1,0:T(8,128)(2,1)} %get-tuple-element.44.refs_4_.refs_8_), channel_id=1, source_target_pairs={{0,8},{1,9},{2,10},{3,11},{4,12},{5,13},{6,14},{7,15},{8,0},{9,1},... | collective-permute-start | bytes 1572872 | tf_op jit(solution)/shard_map/ppermute | solution.py:348
  36.7 13.9 %copy-start.23 = (s32[4]{0:T(128)}, s32[4]{0:T(128)S(1)}, u32[]{:S(2)}) copy-start(s32[4]{0:T(128)S(1)} %pad_add_fusion.1.refs_0_) | copy-start | bytes 52
  36.7 21.9 %all-to-all-start = ((bf16[4,192,128]{2,1,0:T(8,128)(2,1)}), bf16[4,192,128]{2,1,0:T(8,128)(2,1)}, u32[]{:S(2)}, u32[]{:S(2)}) async-start(bf16[4,192,128]{2,1,0:T(8,128)(2,1)} %copy-done.20), calls=%async_computation | async-start | bytes 393216 | tf_op jit(solution)/shard_map/all_to_all | solution.py:415
  40.7 1.1 %copy-start.1 = (bf16[96,4096]{1,0:T(8,128)(2,1)S(1)}, bf16[96,4096]{1,0:T(8,128)(2,1)}, u32[]{:S(2)}) copy-start(bf16[96,4096]{1,0:T(8,128)(2,1)} %refs_1_.10) | copy-start | bytes 2359300
  41.8 1.0 %copy-start.4 = (bf16[128,2048]{1,0:T(8,128)(2,1)S(1)}, bf16[128,2048]{1,0:T(8,128)(2,1)}, u32[]{:S(2)}) copy-start(bf16[128,2048]{1,0:T(8,128)(2,1)} %get-tuple-element.45.refs_5_.refs_10_) | copy-start | bytes 1572868
  53.7 11.3 %collective-permute-start.12 = (bf16[128,1024]{1,0:T(8,128)(2,1)}, bf16[128,1024]{1,0:T(8,128)(2,1)}, u32[]{:S(2)}, u32[]{:S(2)}) collective-permute-start(bf16[128,1024]{1,0:T(8,128)(2,1)} %get-tuple-element.47), channel_id=1, source_target_pairs={{0,8},{1,9},{2,10},{3,11},{4,12},{5,13},{6,14},{7,15},{8,0},{9,1},... | collective-permute-start | bytes 786440 | tf_op jit(solution)/shard_map/ppermute | solution.py:348
  55.1 9.9 %collective-permute-start.13 = (bf16[128,1024]{1,0:T(8,128)(2,1)}, bf16[128,1024]{1,0:T(8,128)(2,1)}, u32[]{:S(2)}, u32[]{:S(2)}) collective-permute-start(bf16[128,1024]{1,0:T(8,128)(2,1)} %get-tuple-element.48), channel_id=1, source_target_pairs={{0,16},{1,17},{2,18},{3,19},{4,20},{5,21},{6,22},{7,23},{8,24},{9,... | collective-permute-start | bytes 786440 | tf_op jit(solution)/shard_map/ppermute | solution.py:348
  55.6 5.8 %collective-permute-start.14 = (bf16[192,128]{1,0:T(8,128)(2,1)}, bf16[192,128]{1,0:T(8,128)(2,1)S(1)}, u32[]{:S(2)}, u32[]{:S(2)}) collective-permute-start(bf16[192,128]{1,0:T(8,128)(2,1)} %get-tuple-element.50), channel_id=1, source_target_pairs={{0,3},{1,0},{2,1},{3,2},{4,7},{5,4},{6,5},{7,6},{8,11},{9,8},{10,9... | collective-permute-start | bytes 147464 | tf_op jit(solution)/shard_map/ppermute | solution.py:348
  58.5 6.4 %collective-permute-start.15 = (bf16[192,128]{1,0:T(8,128)(2,1)}, bf16[192,128]{1,0:T(8,128)(2,1)S(1)}, u32[]{:S(2)}, u32[]{:S(2)}) collective-permute-start(bf16[192,128]{1,0:T(8,128)(2,1)} %get-tuple-element.51), channel_id=1, source_target_pairs={{0,1},{1,2},{2,3},{3,0},{4,5},{5,6},{6,7},{7,4},{8,9},{9,10},{10,1... | collective-permute-start | bytes 147464 | tf_op jit(solution)/shard_map/ppermute | solution.py:348
  58.5 1.1 %copy-start.2 = (bf16[96,4096]{1,0:T(8,128)(2,1)S(1)}, bf16[96,4096]{1,0:T(8,128)(2,1)}, u32[]{:S(2)}) copy-start(bf16[96,4096]{1,0:T(8,128)(2,1)} %refs_1_.10) | copy-start | bytes 2359300
  60.4 4.6 %copy-start.25 = (s32[4]{0:T(128)S(1)}, s32[4]{0:T(128)}, u32[]{:S(2)}) copy-start(s32[4]{0:T(128)} %copy-done.23) | copy-start | bytes 52
  60.4 6.7 %copy-start.28 = (f32[128,128]{1,0:T(8,128)S(1)}, f32[128,128]{1,0:T(8,128)}, u32[]{:S(2)}) copy-start(f32[128,128]{1,0:T(8,128)} %copy-done.27) | copy-start | bytes 196612
  60.4 12.9 %copy-start.7 = (bf16[384,256]{1,0:T(8,128)(2,1)S(1)}, bf16[384,256]{1,0:T(8,128)(2,1)}, u32[]{:S(2)}) copy-start(bf16[384,256]{1,0:T(8,128)(2,1)} %refs_1_.12) | copy-start | bytes 589828
  60.4 12.9 %copy-start.22 = (s32[3]{0:T(128)S(1)}, s32[3]{0:T(128)}, u32[]{:S(2)}) copy-start(s32[3]{0:T(128)} %copy-done.21) | copy-start | bytes 40
  61.4 14.0 %copy-start.5 = (bf16[128,2048]{1,0:T(8,128)(2,1)S(1)}, bf16[128,2048]{1,0:T(8,128)(2,1)}, u32[]{:S(2)}) copy-start(bf16[128,2048]{1,0:T(8,128)(2,1)} %get-tuple-element.45.refs_5_.refs_10_) | copy-start | bytes 1572868
  67.0 5.1 %collective-permute-start.16 = (bf16[192,128]{1,0:T(8,128)(2,1)S(1)}, bf16[192,128]{1,0:T(8,128)(2,1)S(1)}, u32[]{:S(2)}, u32[]{:S(2)}) collective-permute-start(bf16[192,128]{1,0:T(8,128)(2,1)S(1)} %shard_map.100), channel_id=1, source_target_pairs={{0,2},{1,3},{2,0},{3,1},{4,6},{5,7},{6,4},{7,5},{8,10},{9,11},{10,... | collective-permute-start | bytes 147464 | tf_op jit(solution)/shard_map/ppermute | solution.py:348
  67.1 5.0 %collective-permute-start.21 = (f32[128,128]{1,0:T(8,128)S(1)}, f32[128,128]{1,0:T(8,128)S(1)}, u32[]{:S(2)}, u32[]{:S(2)}) collective-permute-start(f32[128,128]{1,0:T(8,128)S(1)} %copy-done.28), channel_id=1, source_target_pairs={{0,4},{1,5},{2,6},{3,7},{4,0},{5,1},{6,2},{7,3},{8,12},{9,13},{10,... | collective-permute-start | bytes 196616 | tf_op jit(solution)/shard_map/ppermute | solution.py:348
  67.2 4.9 %collective-permute-start.17 = (bf16[192,128]{1,0:T(8,128)(2,1)S(1)}, bf16[192,128]{1,0:T(8,128)(2,1)S(1)}, u32[]{:S(2)}, u32[]{:S(2)}) collective-permute-start(bf16[192,128]{1,0:T(8,128)(2,1)S(1)} %get-tuple-element.49.refs_2_), channel_id=1, source_target_pairs={{0,4},{1,5},{2,6},{3,7},{4,0},{5,1},{6,2},{7,3},{8,12},{9,13},{10,... | collective-permute-start | bytes 147464 | tf_op jit(solution)/shard_map/ppermute | solution.py:348
  67.7 4.4 %collective-permute-start.18 = (bf16[192,128]{1,0:T(8,128)(2,1)S(1)}, bf16[192,128]{1,0:T(8,128)(2,1)S(1)}, u32[]{:S(2)}, u32[]{:S(2)}) collective-permute-start(bf16[192,128]{1,0:T(8,128)(2,1)S(1)} %collective-permute-done.14.refs_6_.refs_3_), channel_id=1, source_target_pairs={{0,4},{1,5},{2,6},{3,7},{4,0},{5,1},{6,2},{7,3},{8,12},{9,13},{10,... | collective-permute-start | bytes 147464 | tf_op jit(solution)/shard_map/ppermute | solution.py:348
  67.7 4.3 %collective-permute-start.20 = (bf16[192,128]{1,0:T(8,128)(2,1)S(1)}, bf16[192,128]{1,0:T(8,128)(2,1)S(1)}, u32[]{:S(2)}, u32[]{:S(2)}) collective-permute-start(bf16[192,128]{1,0:T(8,128)(2,1)S(1)} %collective-permute-done.15.refs_7_.refs_5_), channel_id=1, source_target_pairs={{0,4},{1,5},{2,6},{3,7},{4,0},{5,1},{6,2},{7,3},{8,12},{9,13},{10,... | collective-permute-start | bytes 147464 | tf_op jit(solution)/shard_map/ppermute | solution.py:348
  72.0 1.2 %collective-permute-start.19 = (bf16[192,128]{1,0:T(8,128)(2,1)S(1)}, bf16[192,128]{1,0:T(8,128)(2,1)S(1)}, u32[]{:S(2)}, u32[]{:S(2)}) collective-permute-start(bf16[192,128]{1,0:T(8,128)(2,1)S(1)} %collective-permute-done.16.refs_4_), channel_id=1, source_target_pairs={{0,4},{1,5},{2,6},{3,7},{4,0},{5,1},{6,2},{7,3},{8,12},{9,13},{10,... | collective-permute-start | bytes 147464 | tf_op jit(solution)/shard_map/ppermute | solution.py:348
  74.1 1.3 %collective-permute-start.22 = (f32[128,128]{1,0:T(8,128)S(1)}, f32[128,128]{1,0:T(8,128)S(1)}, u32[]{:S(2)}, u32[]{:S(2)}) collective-permute-start(f32[128,128]{1,0:T(8,128)S(1)} %get-tuple-element.54), channel_id=1, source_target_pairs={{0,4},{1,5},{2,6},{3,7},{4,0},{5,1},{6,2},{7,3},{8,12},{9,13},{10,... | collective-permute-start | bytes 196616 | tf_op jit(solution)/shard_map/ppermute | solution.py:348
  75.4 7.5 %copy-start.8 = (bf16[384,256]{1,0:T(8,128)(2,1)S(1)}, bf16[384,256]{1,0:T(8,128)(2,1)}, u32[]{:S(2)}) copy-start(bf16[384,256]{1,0:T(8,128)(2,1)} %refs_2_.5) | copy-start | bytes 589828
  75.4 7.5 %copy-start.9 = (bf16[384,256]{1,0:T(8,128)(2,1)S(1)}, bf16[384,256]{1,0:T(8,128)(2,1)}, u32[]{:S(2)}) copy-start(bf16[384,256]{1,0:T(8,128)(2,1)} %refs_1_.13) | copy-start | bytes 589828
  75.5 7.4 %copy-start.11 = (bf16[4,384,384]{2,1,0:T(8,128)(2,1)S(1)}, bf16[4,384,384]{2,1,0:T(8,128)(2,1)}, u32[]{:S(2)}) copy-start(bf16[4,384,384]{2,1,0:T(8,128)(2,1)} %copy-done.10) | copy-start | bytes 3538948
  75.5 7.4 %copy-start.17 = (f32[128,128]{1,0:T(8,128)S(1)}, f32[128,128]{1,0:T(8,128)}, u32[]{:S(2)}) copy-start(f32[128,128]{1,0:T(8,128)} %copy-done.16) | copy-start | bytes 196612
  78.7 7.9 %collective-permute-start.23 = (f32[96,2048]{1,0:T(8,128)S(1)}, f32[96,2048]{1,0:T(8,128)S(1)}, u32[]{:S(2)}, u32[]{:S(2)}) collective-permute-start(f32[96,2048]{1,0:T(8,128)S(1)} %get-tuple-element.56), channel_id=1, source_target_pairs={{0,4},{1,5},{2,6},{3,7},{4,0},{5,1},{6,2},{7,3},{8,12},{9,13},{10,... | collective-permute-start | bytes 2359304 | tf_op jit(solution)/shard_map/ppermute | solution.py:348
  79.0 7.7 %collective-permute-start.24 = (f32[96,2048]{1,0:T(8,128)S(1)}, f32[96,2048]{1,0:T(8,128)S(1)}, u32[]{:S(2)}, u32[]{:S(2)}) collective-permute-start(f32[96,2048]{1,0:T(8,128)S(1)} %get-tuple-element.58), channel_id=1, source_target_pairs={{0,4},{1,5},{2,6},{3,7},{4,0},{5,1},{6,2},{7,3},{8,12},{9,13},{10,... | collective-permute-start | bytes 2359304 | tf_op jit(solution)/shard_map/ppermute | solution.py:348
  79.3 6.6 %collective-permute-start.27 = (f32[128,128]{1,0:T(8,128)S(1)}, f32[128,128]{1,0:T(8,128)S(1)}, u32[]{:S(2)}, u32[]{:S(2)}) collective-permute-start(f32[128,128]{1,0:T(8,128)S(1)} %add.15.refs_11_.refs_8_), channel_id=1, source_target_pairs={{0,24},{1,25},{2,26},{3,27},{4,28},{5,29},{6,30},{7,31},{8,16},{9,... | collective-permute-start | bytes 196616 | tf_op jit(solution)/shard_map/ppermute | solution.py:348
  80.5 5.4 %collective-permute-start.26 = (f32[128,128]{1,0:T(8,128)S(1)}, f32[128,128]{1,0:T(8,128)S(1)}, u32[]{:S(2)}, u32[]{:S(2)}) collective-permute-start(f32[128,128]{1,0:T(8,128)S(1)} %add.15.refs_11_.refs_8_), channel_id=1, source_target_pairs={{0,16},{1,17},{2,18},{3,19},{4,20},{5,21},{6,22},{7,23},{8,24},{9,... | collective-permute-start | bytes 196616 | tf_op jit(solution)/shard_map/ppermute | solution.py:348
  81.0 4.9 %collective-permute-start.25 = (f32[128,128]{1,0:T(8,128)S(1)}, f32[128,128]{1,0:T(8,128)S(1)}, u32[]{:S(2)}, u32[]{:S(2)}) collective-permute-start(f32[128,128]{1,0:T(8,128)S(1)} %add.15.refs_11_.refs_8_), channel_id=1, source_target_pairs={{0,8},{1,9},{2,10},{3,11},{4,12},{5,13},{6,14},{7,15},{8,0},{9,1},... | collective-permute-start | bytes 196616 | tf_op jit(solution)/shard_map/ppermute | solution.py:348
  86.5 1.7 %collective-permute-start.28 = (f32[128,128]{1,0:T(8,128)S(1)}, f32[128,128]{1,0:T(8,128)S(1)}, u32[]{:S(2)}, u32[]{:S(2)}) collective-permute-start(f32[128,128]{1,0:T(8,128)S(1)} %get-tuple-element.66), channel_id=1, source_target_pairs={{0,4},{1,5},{2,6},{3,7},{4,0},{5,1},{6,2},{7,3},{8,12},{9,13},{10,... | collective-permute-start | bytes 196616 | tf_op jit(solution)/shard_map/ppermute | solution.py:348
  (11 other events, 8.0 us)

commit v21 on v20

--- a/solution.py
+++ b/solution.py
@@ -521,7 +521,7 @@
         [tokens],
         [left[1], fetch((DH, wide), *quarters), half],
         [spots],
-        [both[1], both[3]],
+        [both[1]],
         room=6,
         flops=product // 2,
     )

time: 90.6 us -> 87.8 us (0.969)
  waiting for transfers between devices: 20.3 us -> 17.5 us
    ppermute x29, waiting for transfers between devices: 20.3 us -> 17.5 us  [send(): return lax.ppermute(x, ('ctx', 'head'), pairs)]
  transfers between devices with their start and end apart: 30 -> 30, of which waited for: 11 -> 13; matrix products, arithmetic and copies ran while one was open for 5% -> 5% of each run, Pallas kernels for 17% -> 20%
where the time goes in v21:
time: 87.8 us; the launch traced here: 87 us
  starting transfers between devices  28.2 us (32%)
  Pallas kernels  23.3 us (27%)
  waiting for transfers between devices  17.5 us (20%)
  local copies, waits for them, and re-layouts  14.5 us (17%)
  other arithmetic  2.46 us (3%)
  between operations  0.94 us (1%)
    ppermute x29, starting transfers between devices, send(): return lax.ppermute(x, ('ctx', 'head'), pairs)  24.2 us
    pallas_call x12, Pallas kernels, call(): pl.pallas_call(kernel, out_shape=[jax.ShapeDtypeStruct(s, t) for s, t in...  23.3 us
    ppermute x29, waiting for transfers between devices, send(): return lax.ppermute(x, ('ctx', 'head'), pairs)  17.5 us
    unnamed x58, local copies, waits for them, and re-layouts  12.7 us
    all_to_all x1, starting transfers between devices, on_device(): attn = lax.all_to_all(attn, 'head', 0, 0, tiled=True)  3.99 us
    dynamic_slice x1, local copies, waits for them, and re-layouts, on_device(): lax.dynamic_slice(out_weight, (core * DH, colour * wide), (DH, wide))  1.88 us
  transfers between devices with their start and end apart: 30, of which 13 were waited for; matrix products, arithmetic and copies ran while one was open for 5% of the time, Pallas kernels for 20%

profile of v21, /device:TPU:0, one launch (start us, length us, event | category | flops | bytes accessed | tf_op | source)
XLA Modules:
  0.0 87.0 jit_solution(15235102440227882684)
XLA Ops:
  1.2 1.9 %dynamic_slice.3 = bf16[128,2048]{1,0:T(8,128)(2,1)} dynamic-slice(bf16[256,4096]{1,0:T(8,128)(2,1)} %refs_7_.3, s32[]{:T(128)S(6)} %select_n.6, s32[]{:T(128)S(6)} %select_n.7), dynamic_slice_sizes={128,2048} | dynamic-slice | bytes 1048580 | tf_op jit(solution)/shard_map/dynamic_slice | solution.py:388
  3.0 4.6 %collective-permute-start.8 = (bf16[128,2048]{1,0:T(8,128)(2,1)}, bf16[128,2048]{1,0:T(8,128)(2,1)S(1)}, u32[]{:S(2)}, u32[]{:S(2)}) collective-permute-start(bf16[128,2048]{1,0:T(8,128)(2,1)} %dynamic_slice.3), channel_id=1, source_target_pairs={{0,3},{1,0},{2,1},{3,2},{4,7},{5,4},{6,5},{7,6},{8,11},{9,8},{10,9... | collective-permute-start | bytes 1572872 | tf_op jit(solution)/shard_map/ppermute | solution.py:348
  7.8 1.2 %pad_maximum_fusion.refs_2_ = bf16[3,384,256]{2,1,0:T(8,128)(2,1)S(1)} fusion(bf16[1,384,256]{2,1,0:T(8,128)(2,1)} %bitcast.18, bf16[1,384,256]{2,1,0:T(8,128)(2,1)} %bitcast.19, bf16[1,384,256]{2,1,0:T(8,128)(2,1)} %bitcast.17), kind=kLoop, calls=%fused_computation | loop fusion | flops 589824 | bytes 1179648 | tf_op jit(solution)/shard_map/stack | solution.py:398
  9.0 2.6 %shard_map.93 = (bf16[4,384,384]{2,1,0:T(8,128)(2,1)S(1)}, f32[384,128]{1,0:T(8,128)S(1)}, f32[384,128]{1,0:T(8,128)}, bf16[384,128]{1,0:T(8,128)(2,1)}, f32[128,128]{1,0:T(8,128)S(1)}, /*index=5*/f32[128,128]{1,0:T(8,128)}) custom-call(s32[3,3]{1,0:T(4,128)S(1)} %copy-done.26, s32[3]{0:T(128)S(1)} %pad_add_fusion.2.refs_1_.refs_0_, ...), custom_call_target="tpu_custom_call" | custom-call | flops 264241152 | bytes 2392064 | tf_op jit(solution)/shard_map/pallas_call | solution.py:103
  11.5 1.1 %copy-done.10 = bf16[4,384,384]{2,1,0:T(8,128)(2,1)} copy-done((bf16[4,384,384]{2,1,0:T(8,128)(2,1)}, bf16[4,384,384]{2,1,0:T(8,128)(2,1)S(1)}, u32[]{:S(2)}) %copy-start.10) | copy-done | bytes 1179672
  12.6 0.6 copy-done.12
  13.2 0.7 copy-done.18
  14.6 1.1 %collective-permute-done.1.refs_1_.refs_8_ = bf16[384,128]{1,0:T(8,128)(2,1)S(1)} collective-permute-done((bf16[384,128]{1,0:T(8,128)(2,1)}, bf16[384,128]{1,0:T(8,128)(2,1)S(1)}, u32[]{:S(2)}, u32[]{:S(2)}) %collective-permute-start.1) | collective-permute-done | bytes 98336 | tf_op jit(solution)/shard_map/ppermute | solution.py:348
  15.7 0.6 copy-done.14
  16.3 0.9 %add.12 = f32[128,128]{1,0:T(8,128)S(1)} add(f32[128,128]{1,0:T(8,128)} %shard_map.94.refs_2_, f32[128,128]{1,0:T(8,128)} %collective-permute-done.3.refs_3_) | non-fusion elementwise | flops 16384 | bytes 196608 | tf_op jit(solution)/shard_map/add | solution.py:353
  17.2 2.5 %collective-permute-start.6 = (f32[128,128]{1,0:T(8,128)S(1)}, f32[128,128]{1,0:T(8,128)S(1)}, u32[]{:S(2)}, u32[]{:S(2)}) collective-permute-start(f32[128,128]{1,0:T(8,128)S(1)} %add.12), channel_id=1, source_target_pairs={{0,24},{1,25},{2,26},{3,27},{4,28},{5,29},{6,30},{7,31},{8,16},{9,... | collective-permute-start | bytes 196616 | tf_op jit(solution)/shard_map/ppermute | solution.py:348
  20.8 1.6 %collective-permute-done.6.refs_6_ = f32[128,128]{1,0:T(8,128)S(1)} collective-permute-done((f32[128,128]{1,0:T(8,128)S(1)}, f32[128,128]{1,0:T(8,128)S(1)}, u32[]{:S(2)}, u32[]{:S(2)}) %collective-permute-start.6) | collective-permute-done | bytes 65568 | tf_op jit(solution)/shard_map/ppermute | solution.py:348
  22.5 1.5 %collective-permute-done.5.refs_5_ = f32[128,128]{1,0:T(8,128)S(1)} collective-permute-done((f32[128,128]{1,0:T(8,128)S(1)}, f32[128,128]{1,0:T(8,128)S(1)}, u32[]{:S(2)}, u32[]{:S(2)}) %collective-permute-start.5) | collective-permute-done | bytes 65568 | tf_op jit(solution)/shard_map/ppermute | solution.py:348
  24.5 0.9 %copy-done.6 = bf16[384,256]{1,0:T(8,128)(2,1)S(1)} copy-done((bf16[384,256]{1,0:T(8,128)(2,1)S(1)}, bf16[384,256]{1,0:T(8,128)(2,1)}, u32[]{:S(2)}) %copy-start.6) | copy-done | bytes 196632
  25.4 0.8 copy-done.13
  26.3 0.9 %copy-done.15 = bf16[384,128]{1,0:T(8,128)(2,1)S(1)} copy-done((bf16[384,128]{1,0:T(8,128)(2,1)S(1)}, bf16[384,128]{1,0:T(8,128)(2,1)}, u32[]{:S(2)}) %copy-start.15) | copy-done | bytes 98328
  27.2 0.9 %copy-done.19 = f32[384,128]{1,0:T(8,128)S(1)} copy-done((f32[384,128]{1,0:T(8,128)S(1)}, f32[384,128]{1,0:T(8,128)}, u32[]{:S(2)}) %copy-start.19) | copy-done | bytes 196632
  28.1 1.2 %shard_map.95 = (bf16[4,192,128]{2,1,0:T(8,128)(2,1)S(1)}, f32[128,128]{1,0:T(8,128)S(1)}, f32[128,128]{1,0:T(8,128)S(1)}) custom-call(s32[4]{0:T(128)S(1)} %add_convert_fusion.refs_0_, s32[3]{0:T(128)S(1)} %pad_add_fusion.2.refs_1_.refs_0_, f32[128,128]{1,0:T(8,128)S(1)} %copy-done.13, f32[128,128]{1,0:T(8,128)} %collective-permute-done.3.refs_3_, ...), custom_call_target="tpu_custom_call" | custom-call | flops 1 | bytes 1343488 | tf_op jit(solution)/shard_map/pallas_call | solution.py:103
  29.4 0.6 copy-done.16
  30.0 0.6 copy-done.27
  30.6 0.7 copy-done.20
  31.3 0.7 collective-permute-done.7.refs_0_
  32.1 1.5 %collective-permute-start.10 = (bf16[128,2048]{1,0:T(8,128)(2,1)}, bf16[128,2048]{1,0:T(8,128)(2,1)}, u32[]{:S(2)}, u32[]{:S(2)}) collective-permute-start(bf16[128,2048]{1,0:T(8,128)(2,1)} %get-tuple-element.45.refs_5_.refs_10_), channel_id=1, source_target_pairs={{0,16},{1,17},{2,18},{3,19},{4,20},{5,21},{6,22},{7,23},{8,24},{9,... | collective-permute-start | bytes 1572872 | tf_op jit(solution)/shard_map/ppermute | solution.py:348
  33.6 1.5 %collective-permute-start.11 = (bf16[128,2048]{1,0:T(8,128)(2,1)}, bf16[128,2048]{1,0:T(8,128)(2,1)S(1)}, u32[]{:S(2)}, u32[]{:S(2)}) collective-permute-start(bf16[128,2048]{1,0:T(8,128)(2,1)} %get-tuple-element.44.refs_4_.refs_8_), channel_id=1, source_target_pairs={{0,1},{1,2},{2,3},{3,0},{4,5},{5,6},{6,7},{7,4},{8,9},{9,10},{10,1... | collective-permute-start | bytes 1572872 | tf_op jit(solution)/shard_map/ppermute | solution.py:348
  35.1 1.5 %collective-permute-start.9 = (bf16[128,2048]{1,0:T(8,128)(2,1)}, bf16[128,2048]{1,0:T(8,128)(2,1)}, u32[]{:S(2)}, u32[]{:S(2)}) collective-permute-start(bf16[128,2048]{1,0:T(8,128)(2,1)} %get-tuple-element.44.refs_4_.refs_8_), channel_id=1, source_target_pairs={{0,8},{1,9},{2,10},{3,11},{4,12},{5,13},{6,14},{7,15},{8,0},{9,1},... | collective-permute-start | bytes 1572872 | tf_op jit(solution)/shard_map/ppermute | solution.py:348
  36.7 4.0 %all-to-all-start = ((bf16[4,192,128]{2,1,0:T(8,128)(2,1)}), bf16[4,192,128]{2,1,0:T(8,128)(2,1)}, u32[]{:S(2)}, u32[]{:S(2)}) async-start(bf16[4,192,128]{2,1,0:T(8,128)(2,1)} %copy-done.20), calls=%async_computation | async-start | bytes 393216 | tf_op jit(solution)/shard_map/all_to_all | solution.py:415
  40.7 1.1 %copy-done.1 = bf16[96,4096]{1,0:T(8,128)(2,1)S(1)} copy-done((bf16[96,4096]{1,0:T(8,128)(2,1)S(1)}, bf16[96,4096]{1,0:T(8,128)(2,1)}, u32[]{:S(2)}) %copy-start.1) | copy-done | bytes 786456
  41.8 1.0 %copy-done.4 = bf16[128,2048]{1,0:T(8,128)(2,1)S(1)} copy-done((bf16[128,2048]{1,0:T(8,128)(2,1)S(1)}, bf16[128,2048]{1,0:T(8,128)(2,1)}, u32[]{:S(2)}) %copy-start.4) | copy-done | bytes 524312
  42.9 2.5 %shard_map.97 = (bf16[192,128]{1,0:T(8,128)(2,1)S(1)}, f32[192,256]{1,0:T(8,128)S(1)}) custom-call(s32[4]{0:T(128)S(1)} %pad_add_fusion.1.refs_0_, bf16[96,4096]{1,0:T(8,128)(2,1)S(1)} %copy-done.1, bf16[96,4096]{1,0:T(8,128)(2,1)S(1)} %collective-permute-done.refs_3_.refs_2_, bf16[256,4096]{1,0:T(8,128)(2,1)S(1)} %copy-done, ...), custom_call_target="tpu_custom_call" | custom-call | flops 402653184 | bytes 4964352 | tf_op jit(solution)/shard_map/pallas_call | solution.py:103
  45.8 4.8 %collective-permute-done.11.refs_6_.refs_3_.refs_9_ = bf16[128,2048]{1,0:T(8,128)(2,1)S(1)} collective-permute-done((bf16[128,2048]{1,0:T(8,128)(2,1)}, bf16[128,2048]{1,0:T(8,128)(2,1)S(1)}, u32[]{:S(2)}, u32[]{:S(2)}) %collective-permute-start.11) | collective-permute-done | bytes 524320 | tf_op jit(solution)/shard_map/ppermute | solution.py:348
  50.5 3.1 %shard_map.98 = (bf16[192,128]{1,0:T(8,128)(2,1)}, bf16[192,128]{1,0:T(8,128)(2,1)}, bf16[128,1024]{1,0:T(8,128)(2,1)}, bf16[128,1024]{1,0:T(8,128)(2,1)}) custom-call(s32[4]{0:T(128)S(1)} %pad_add_fusion.1.refs_0_, bf16[96,4096]{1,0:T(8,128)(2,1)S(1)} %copy-done.1, bf16[96,4096]{1,0:T(8,128)(2,1)S(1)} %collective-permute-done.refs_3_.refs_2_, ...), custom_call_target="tpu_custom_call" | custom-call | flops 201326592 | bytes 3964928 | tf_op jit(solution)/shard_map/pallas_call | solution.py:103
  53.7 1.4 %collective-permute-start.12 = (bf16[128,1024]{1,0:T(8,128)(2,1)}, bf16[128,1024]{1,0:T(8,128)(2,1)}, u32[]{:S(2)}, u32[]{:S(2)}) collective-permute-start(bf16[128,1024]{1,0:T(8,128)(2,1)} %get-tuple-element.47), channel_id=1, source_target_pairs={{0,8},{1,9},{2,10},{3,11},{4,12},{5,13},{6,14},{7,15},{8,0},{9,1},... | collective-permute-start | bytes 786440 | tf_op jit(solution)/shard_map/ppermute | solution.py:348
  55.6 2.9 %collective-permute-start.14 = (bf16[192,128]{1,0:T(8,128)(2,1)}, bf16[192,128]{1,0:T(8,128)(2,1)S(1)}, u32[]{:S(2)}, u32[]{:S(2)}) collective-permute-start(bf16[192,128]{1,0:T(8,128)(2,1)} %get-tuple-element.50), channel_id=1, source_target_pairs={{0,3},{1,0},{2,1},{3,2},{4,7},{5,4},{6,5},{7,6},{8,11},{9,8},{10,9... | collective-permute-start | bytes 147464 | tf_op jit(solution)/shard_map/ppermute | solution.py:348
  58.5 1.1 %copy-done.2 = bf16[96,4096]{1,0:T(8,128)(2,1)S(1)} copy-done((bf16[96,4096]{1,0:T(8,128)(2,1)S(1)}, bf16[96,4096]{1,0:T(8,128)(2,1)}, u32[]{:S(2)}) %copy-start.2) | copy-done | bytes 786456
  59.7 0.7 copy-done.24
  60.4 1.0 %shard_map.99.refs_5_ = f32[192,128]{1,0:T(8,128)S(1)} custom-call(s32[4]{0:T(128)S(1)} %copy-done.24, bf16[96,4096]{1,0:T(8,128)(2,1)S(1)} %copy-done.2, bf16[96,4096]{1,0:T(8,128)(2,1)S(1)} %collective-permute-done.refs_3_.refs_2_, bf16[128,2048]{1,0:T(8,128)(2,1)S(1)} %collective-permute-done.11.refs_6_.refs_3_.refs_9_, ...), custom_call_target="tpu_custom_call" | custom-call | flops 100663296 | bytes 2195456 | tf_op jit(solution)/shard_map/pallas_call | solution.py:103
  61.8 2.0 %shard_map.100 = bf16[192,128]{1,0:T(8,128)(2,1)S(1)} custom-call(s32[4]{0:T(128)S(1)} %copy-done.25, bf16[96,4096]{1,0:T(8,128)(2,1)S(1)} %copy-done.2, bf16[96,4096]{1,0:T(8,128)(2,1)S(1)} %collective-permute-done.refs_3_.refs_2_, bf16[128,1024]{1,0:T(8,128)(2,1)} %collective-permute-done.12.refs_3_.refs_5_, ...), custom_call_target="tpu_custom_call" | custom-call | flops 100663296 | bytes 2244608 | tf_op jit(solution)/shard_map/pallas_call | solution.py:103
  65.2 3.7 %collective-permute-done.15.refs_4_ = bf16[192,128]{1,0:T(8,128)(2,1)S(1)} collective-permute-done((bf16[192,128]{1,0:T(8,128)(2,1)S(1)}, bf16[192,128]{1,0:T(8,128)(2,1)S(1)}, u32[]{:S(2)}, u32[]{:S(2)}) %collective-permute-start.15) | collective-permute-done | bytes 49184 | tf_op jit(solution)/shard_map/ppermute | solution.py:348
  68.9 1.2 %collective-permute-done.19.refs_8_ = bf16[192,128]{1,0:T(8,128)(2,1)S(1)} collective-permute-done((bf16[192,128]{1,0:T(8,128)(2,1)S(1)}, bf16[192,128]{1,0:T(8,128)(2,1)S(1)}, u32[]{:S(2)}, u32[]{:S(2)}) %collective-permute-start.19) | collective-permute-done | bytes 49184 | tf_op jit(solution)/shard_map/ppermute | solution.py:348
  70.1 0.8 shard_map.101
  71.1 1.1 %collective-permute-done.22.refs_2_ = f32[128,128]{1,0:T(8,128)S(1)} collective-permute-done((f32[128,128]{1,0:T(8,128)S(1)}, f32[128,128]{1,0:T(8,128)S(1)}, u32[]{:S(2)}, u32[]{:S(2)}) %collective-permute-start.22) | collective-permute-done | bytes 65568 | tf_op jit(solution)/shard_map/ppermute | solution.py:348
  72.3 3.3 %shard_map.102 = (f32[96,2048]{1,0:T(8,128)S(1)}, f32[96,2048]{1,0:T(8,128)S(1)}, f32[96,2048]{1,0:T(8,128)S(1)}, f32[96,2048]{1,0:T(8,128)S(1)}) custom-call(s32[4]{0:T(128)S(1)} %copy-done.25, bf16[4,192,128]{2,1,0:T(8,128)(2,1)} %all-to-all-done.refs_4_.refs_1_, bf16[256,4096]{1,0:T(8,128)(2,1)S(1)} %copy-done, ...), custom_call_target="tpu_custom_call" | custom-call | flops 805306368 | bytes 10682368 | tf_op jit(solution)/shard_map/pallas_call | solution.py:103
  76.1 1.2 %collective-permute-start.27 = (f32[128,128]{1,0:T(8,128)S(1)}, f32[128,128]{1,0:T(8,128)S(1)}, u32[]{:S(2)}, u32[]{:S(2)}) collective-permute-start(f32[128,128]{1,0:T(8,128)S(1)} %add.15.refs_11_.refs_8_), channel_id=1, source_target_pairs={{0,24},{1,25},{2,26},{3,27},{4,28},{5,29},{6,30},{7,31},{8,16},{9,... | collective-permute-start | bytes 196616 | tf_op jit(solution)/shard_map/ppermute | solution.py:348
  77.3 1.5 %collective-permute-start.26 = (f32[128,128]{1,0:T(8,128)S(1)}, f32[128,128]{1,0:T(8,128)S(1)}, u32[]{:S(2)}, u32[]{:S(2)}) collective-permute-start(f32[128,128]{1,0:T(8,128)S(1)} %add.15.refs_11_.refs_8_), channel_id=1, source_target_pairs={{0,16},{1,17},{2,18},{3,19},{4,20},{5,21},{6,22},{7,23},{8,24},{9,... | collective-permute-start | bytes 196616 | tf_op jit(solution)/shard_map/ppermute | solution.py:348
  78.8 0.8 collective-permute-start.25
  79.7 3.0 %shard_map.104 = (bf16[384,256]{1,0:T(8,128)(2,1)}, f32[384,256]{1,0:T(8,128)S(1)}, f32[384,256]{1,0:T(8,128)S(1)}) custom-call(s32[3]{0:T(128)S(1)} %copy-done.22, bf16[384,256]{1,0:T(8,128)(2,1)S(1)} %copy-done.7, bf16[384,256]{1,0:T(8,128)(2,1)S(1)} %copy-done.9, bf16[384,256]{1,0:T(8,128)(2,1)S(1)} %copy-done.8, ...), custom_call_target="tpu_custom_call" | custom-call | flops 528482304 | bytes 3080192 | tf_op jit(solution)/shard_map/pallas_call | solution.py:103
  83.8 1.6 %shard_map.103 = (bf16[96,4096]{1,0:T(8,128)(2,1)}, f32[8,128]{1,0:T(8,128)S(1)}) custom-call(s32[2]{0:T(128)S(1)} %pad_add_fusion.refs_0_, f32[96,2048]{1,0:T(8,128)S(1)} %get-tuple-element.55.refs_1_, f32[96,2048]{1,0:T(8,128)S(1)} %collective-permute-done.23.refs_2_, f32[96,2048]{1,0:T(8,128)S(1)} %get-tuple-element.57.refs_3_, ...), custom_call_target="tpu_custom_call" | custom-call | flops 1 | bytes 3936256 | tf_op jit(solution)/shard_map/pallas_call | solution.py:103
  85.4 1.6 %shard_map.106 = (bf16[384,256]{1,0:T(8,128)(2,1)}, bf16[384,256]{1,0:T(8,128)(2,1)}) custom-call(s32[3]{0:T(128)S(1)} %copy-done.22, bf16[384,256]{1,0:T(8,128)(2,1)S(1)} %copy-done.9, bf16[384,256]{1,0:T(8,128)(2,1)S(1)} %copy-done.8, f32[384,256]{1,0:T(8,128)S(1)} %get-tuple-element.63.refs_6_.refs_3_, f32[384,256]{1,0:T(8,128)S(1)} %get-tuple-element.64.refs_4_, ...), custom_call_target="tpu_custom_call" | custom-call | flops 1 | bytes 1703936 | tf_op jit(solution)/shard_map/pallas_call | solution.py:103
  (93 shorter events, 7.8 us)
Async XLA Ops:
  0.6 8.3 %copy-start.26 = (s32[3,3]{1,0:T(4,128)S(1)}, s32[3,3]{1,0:T(4,128)}, u32[]{:S(2)}) copy-start(s32[3,3]{1,0:T(4,128)} %refs_0_.1) | copy-start | bytes 112
  0.6 8.3 %collective-permute-start = (bf16[96,4096]{1,0:T(8,128)(2,1)}, bf16[96,4096]{1,0:T(8,128)(2,1)S(1)}, u32[]{:S(2)}, u32[]{:S(2)}) collective-permute-start(bf16[96,4096]{1,0:T(8,128)(2,1)} %refs_1_.10), channel_id=1, source_target_pairs={{0,4},{1,5},{2,6},{3,7},{4,0},{5,1},{6,2},{7,3},{8,12},{9,13},{10,... | collective-permute-start | bytes 2359304 | tf_op jit(solution)/shard_map/ppermute | solution.py:348
  3.0 27.6 %collective-permute-start.8 = (bf16[128,2048]{1,0:T(8,128)(2,1)}, bf16[128,2048]{1,0:T(8,128)(2,1)S(1)}, u32[]{:S(2)}, u32[]{:S(2)}) collective-permute-start(bf16[128,2048]{1,0:T(8,128)(2,1)} %dynamic_slice.3), channel_id=1, source_target_pairs={{0,3},{1,0},{2,1},{3,2},{4,7},{5,4},{6,5},{7,6},{8,11},{9,8},{10,9... | collective-permute-start | bytes 1572872 | tf_op jit(solution)/shard_map/ppermute | solution.py:348
  7.7 24.3 %collective-permute-start.7 = (bf16[128,2048]{1,0:T(8,128)(2,1)}, bf16[128,2048]{1,0:T(8,128)(2,1)}, u32[]{:S(2)}, u32[]{:S(2)}) collective-permute-start(bf16[128,2048]{1,0:T(8,128)(2,1)} %dynamic_slice.3), channel_id=1, source_target_pairs={{0,1},{1,2},{2,3},{3,0},{4,5},{5,6},{6,7},{7,4},{8,9},{9,10},{10,1... | collective-permute-start | bytes 1572872 | tf_op jit(solution)/shard_map/ppermute | solution.py:348
  7.8 21.6 %copy-start.21 = (s32[3]{0:T(128)}, s32[3]{0:T(128)S(1)}, u32[]{:S(2)}) copy-start(s32[3]{0:T(128)S(1)} %pad_add_fusion.2.refs_1_.refs_0_) | copy-start | bytes 40
  8.9 31.7 %copy-start = (bf16[256,4096]{1,0:T(8,128)(2,1)S(1)}, bf16[256,4096]{1,0:T(8,128)(2,1)}, u32[]{:S(2)}) copy-start(bf16[256,4096]{1,0:T(8,128)(2,1)} %refs_7_.3) | copy-start | bytes 6291460
  11.5 1.1 %copy-start.10 = (bf16[4,384,384]{2,1,0:T(8,128)(2,1)}, bf16[4,384,384]{2,1,0:T(8,128)(2,1)S(1)}, u32[]{:S(2)}) copy-start(bf16[4,384,384]{2,1,0:T(8,128)(2,1)S(1)} %get-tuple-element.61.refs_5_) | copy-start | bytes 3538948
  13.9 1.8 %collective-permute-start.2 = (f32[384,128]{1,0:T(8,128)}, f32[384,128]{1,0:T(8,128)}, u32[]{:S(2)}, u32[]{:S(2)}) collective-permute-start(f32[384,128]{1,0:T(8,128)} %get-tuple-element.39), channel_id=1, source_target_pairs={{0,4},{1,5},{2,6},{3,7},{4,0},{5,1},{6,2},{7,3},{8,12},{9,13},{10,... | collective-permute-start | bytes 589832 | tf_op jit(solution)/shard_map/ppermute | solution.py:348
  14.1 1.6 %collective-permute-start.1 = (bf16[384,128]{1,0:T(8,128)(2,1)}, bf16[384,128]{1,0:T(8,128)(2,1)S(1)}, u32[]{:S(2)}, u32[]{:S(2)}) collective-permute-start(bf16[384,128]{1,0:T(8,128)(2,1)} %get-tuple-element.38), channel_id=1, source_target_pairs={{0,4},{1,5},{2,6},{3,7},{4,0},{5,1},{6,2},{7,3},{8,12},{9,13},{10,... | collective-permute-start | bytes 294920 | tf_op jit(solution)/shard_map/ppermute | solution.py:348
  14.4 1.9 %collective-permute-start.3 = (f32[128,128]{1,0:T(8,128)}, f32[128,128]{1,0:T(8,128)}, u32[]{:S(2)}, u32[]{:S(2)}) collective-permute-start(f32[128,128]{1,0:T(8,128)} %get-tuple-element.40), channel_id=1, source_target_pairs={{0,4},{1,5},{2,6},{3,7},{4,0},{5,1},{6,2},{7,3},{8,12},{9,13},{10,... | collective-permute-start | bytes 196616 | tf_op jit(solution)/shard_map/ppermute | solution.py:348
  17.2 5.2 %collective-permute-start.6 = (f32[128,128]{1,0:T(8,128)S(1)}, f32[128,128]{1,0:T(8,128)S(1)}, u32[]{:S(2)}, u32[]{:S(2)}) collective-permute-start(f32[128,128]{1,0:T(8,128)S(1)} %add.12), channel_id=1, source_target_pairs={{0,24},{1,25},{2,26},{3,27},{4,28},{5,29},{6,30},{7,31},{8,16},{9,... | collective-permute-start | bytes 196616 | tf_op jit(solution)/shard_map/ppermute | solution.py:348
  19.7 4.3 %collective-permute-start.5 = (f32[128,128]{1,0:T(8,128)S(1)}, f32[128,128]{1,0:T(8,128)S(1)}, u32[]{:S(2)}, u32[]{:S(2)}) collective-permute-start(f32[128,128]{1,0:T(8,128)S(1)} %add.12), channel_id=1, source_target_pairs={{0,16},{1,17},{2,18},{3,19},{4,20},{5,21},{6,22},{7,23},{8,24},{9,... | collective-permute-start | bytes 196616 | tf_op jit(solution)/shard_map/ppermute | solution.py:348
  20.2 4.3 %collective-permute-start.4 = (f32[128,128]{1,0:T(8,128)S(1)}, f32[128,128]{1,0:T(8,128)S(1)}, u32[]{:S(2)}, u32[]{:S(2)}) collective-permute-start(f32[128,128]{1,0:T(8,128)S(1)} %add.12), channel_id=1, source_target_pairs={{0,8},{1,9},{2,10},{3,11},{4,12},{5,13},{6,14},{7,15},{8,0},{9,1},... | collective-permute-start | bytes 196616 | tf_op jit(solution)/shard_map/ppermute | solution.py:348
  24.5 0.9 %copy-start.6 = (bf16[384,256]{1,0:T(8,128)(2,1)S(1)}, bf16[384,256]{1,0:T(8,128)(2,1)}, u32[]{:S(2)}) copy-start(bf16[384,256]{1,0:T(8,128)(2,1)} %refs_1_.12) | copy-start | bytes 589828
  32.1 13.7 %collective-permute-start.10 = (bf16[128,2048]{1,0:T(8,128)(2,1)}, bf16[128,2048]{1,0:T(8,128)(2,1)}, u32[]{:S(2)}, u32[]{:S(2)}) collective-permute-start(bf16[128,2048]{1,0:T(8,128)(2,1)} %get-tuple-element.45.refs_5_.refs_10_), channel_id=1, source_target_pairs={{0,16},{1,17},{2,18},{3,19},{4,20},{5,21},{6,22},{7,23},{8,24},{9,... | collective-permute-start | bytes 1572872 | tf_op jit(solution)/shard_map/ppermute | solution.py:348
  33.6 17.0 %collective-permute-start.11 = (bf16[128,2048]{1,0:T(8,128)(2,1)}, bf16[128,2048]{1,0:T(8,128)(2,1)S(1)}, u32[]{:S(2)}, u32[]{:S(2)}) collective-permute-start(bf16[128,2048]{1,0:T(8,128)(2,1)} %get-tuple-element.44.refs_4_.refs_8_), channel_id=1, source_target_pairs={{0,1},{1,2},{2,3},{3,0},{4,5},{5,6},{6,7},{7,4},{8,9},{9,10},{10,1... | collective-permute-start | bytes 1572872 | tf_op jit(solution)/shard_map/ppermute | solution.py:348
  35.1 15.4 %collective-permute-start.9 = (bf16[128,2048]{1,0:T(8,128)(2,1)}, bf16[128,2048]{1,0:T(8,128)(2,1)}, u32[]{:S(2)}, u32[]{:S(2)}) collective-permute-start(bf16[128,2048]{1,0:T(8,128)(2,1)} %get-tuple-element.44.refs_4_.refs_8_), channel_id=1, source_target_pairs={{0,8},{1,9},{2,10},{3,11},{4,12},{5,13},{6,14},{7,15},{8,0},{9,1},... | collective-permute-start | bytes 1572872 | tf_op jit(solution)/shard_map/ppermute | solution.py:348
  36.7 13.9 %copy-start.23 = (s32[4]{0:T(128)}, s32[4]{0:T(128)S(1)}, u32[]{:S(2)}) copy-start(s32[4]{0:T(128)S(1)} %pad_add_fusion.1.refs_0_) | copy-start | bytes 52
  36.7 21.9 %all-to-all-start = ((bf16[4,192,128]{2,1,0:T(8,128)(2,1)}), bf16[4,192,128]{2,1,0:T(8,128)(2,1)}, u32[]{:S(2)}, u32[]{:S(2)}) async-start(bf16[4,192,128]{2,1,0:T(8,128)(2,1)} %copy-done.20), calls=%async_computation | async-start | bytes 393216 | tf_op jit(solution)/shard_map/all_to_all | solution.py:415
  40.7 1.1 %copy-start.1 = (bf16[96,4096]{1,0:T(8,128)(2,1)S(1)}, bf16[96,4096]{1,0:T(8,128)(2,1)}, u32[]{:S(2)}) copy-start(bf16[96,4096]{1,0:T(8,128)(2,1)} %refs_1_.10) | copy-start | bytes 2359300
  41.8 1.0 %copy-start.4 = (bf16[128,2048]{1,0:T(8,128)(2,1)S(1)}, bf16[128,2048]{1,0:T(8,128)(2,1)}, u32[]{:S(2)}) copy-start(bf16[128,2048]{1,0:T(8,128)(2,1)} %get-tuple-element.45.refs_5_.refs_10_) | copy-start | bytes 1572868
  53.7 7.8 %collective-permute-start.12 = (bf16[128,1024]{1,0:T(8,128)(2,1)}, bf16[128,1024]{1,0:T(8,128)(2,1)}, u32[]{:S(2)}, u32[]{:S(2)}) collective-permute-start(bf16[128,1024]{1,0:T(8,128)(2,1)} %get-tuple-element.47), channel_id=1, source_target_pairs={{0,8},{1,9},{2,10},{3,11},{4,12},{5,13},{6,14},{7,15},{8,0},{9,1},... | collective-permute-start | bytes 786440 | tf_op jit(solution)/shard_map/ppermute | solution.py:348
  55.1 6.7 %collective-permute-start.13 = (bf16[128,1024]{1,0:T(8,128)(2,1)}, bf16[128,1024]{1,0:T(8,128)(2,1)}, u32[]{:S(2)}, u32[]{:S(2)}) collective-permute-start(bf16[128,1024]{1,0:T(8,128)(2,1)} %get-tuple-element.48), channel_id=1, source_target_pairs={{0,16},{1,17},{2,18},{3,19},{4,20},{5,21},{6,22},{7,23},{8,24},{9,... | collective-permute-start | bytes 786440 | tf_op jit(solution)/shard_map/ppermute | solution.py:348
  55.6 5.8 %collective-permute-start.14 = (bf16[192,128]{1,0:T(8,128)(2,1)}, bf16[192,128]{1,0:T(8,128)(2,1)S(1)}, u32[]{:S(2)}, u32[]{:S(2)}) collective-permute-start(bf16[192,128]{1,0:T(8,128)(2,1)} %get-tuple-element.50), channel_id=1, source_target_pairs={{0,3},{1,0},{2,1},{3,2},{4,7},{5,4},{6,5},{7,6},{8,11},{9,8},{10,9... | collective-permute-start | bytes 147464 | tf_op jit(solution)/shard_map/ppermute | solution.py:348
  58.5 6.4 %collective-permute-start.16 = (bf16[192,128]{1,0:T(8,128)(2,1)}, bf16[192,128]{1,0:T(8,128)(2,1)S(1)}, u32[]{:S(2)}, u32[]{:S(2)}) collective-permute-start(bf16[192,128]{1,0:T(8,128)(2,1)} %get-tuple-element.51), channel_id=1, source_target_pairs={{0,1},{1,2},{2,3},{3,0},{4,5},{5,6},{6,7},{7,4},{8,9},{9,10},{10,1... | collective-permute-start | bytes 147464 | tf_op jit(solution)/shard_map/ppermute | solution.py:348
  58.5 1.1 %copy-start.2 = (bf16[96,4096]{1,0:T(8,128)(2,1)S(1)}, bf16[96,4096]{1,0:T(8,128)(2,1)}, u32[]{:S(2)}) copy-start(bf16[96,4096]{1,0:T(8,128)(2,1)} %refs_1_.10) | copy-start | bytes 2359300
  60.4 1.4 %copy-start.25 = (s32[4]{0:T(128)S(1)}, s32[4]{0:T(128)}, u32[]{:S(2)}) copy-start(s32[4]{0:T(128)} %copy-done.23) | copy-start | bytes 52
  60.4 3.8 %copy-start.28 = (f32[128,128]{1,0:T(8,128)S(1)}, f32[128,128]{1,0:T(8,128)}, u32[]{:S(2)}) copy-start(f32[128,128]{1,0:T(8,128)} %copy-done.27) | copy-start | bytes 196612
  60.4 9.7 %copy-start.7 = (bf16[384,256]{1,0:T(8,128)(2,1)S(1)}, bf16[384,256]{1,0:T(8,128)(2,1)}, u32[]{:S(2)}) copy-start(bf16[384,256]{1,0:T(8,128)(2,1)} %refs_1_.12) | copy-start | bytes 589828
  60.4 9.7 %copy-start.22 = (s32[3]{0:T(128)S(1)}, s32[3]{0:T(128)}, u32[]{:S(2)}) copy-start(s32[3]{0:T(128)} %copy-done.21) | copy-start | bytes 40
  61.4 10.8 %copy-start.5 = (bf16[128,2048]{1,0:T(8,128)(2,1)S(1)}, bf16[128,2048]{1,0:T(8,128)(2,1)}, u32[]{:S(2)}) copy-start(bf16[128,2048]{1,0:T(8,128)(2,1)} %get-tuple-element.45.refs_5_.refs_10_) | copy-start | bytes 1572868
  63.8 5.1 %collective-permute-start.15 = (bf16[192,128]{1,0:T(8,128)(2,1)S(1)}, bf16[192,128]{1,0:T(8,128)(2,1)S(1)}, u32[]{:S(2)}, u32[]{:S(2)}) collective-permute-start(bf16[192,128]{1,0:T(8,128)(2,1)S(1)} %shard_map.100), channel_id=1, source_target_pairs={{0,2},{1,3},{2,0},{3,1},{4,6},{5,7},{6,4},{7,5},{8,10},{9,11},{10,... | collective-permute-start | bytes 147464 | tf_op jit(solution)/shard_map/ppermute | solution.py:348
  64.1 4.7 %collective-permute-start.21 = (f32[128,128]{1,0:T(8,128)S(1)}, f32[128,128]{1,0:T(8,128)S(1)}, u32[]{:S(2)}, u32[]{:S(2)}) collective-permute-start(f32[128,128]{1,0:T(8,128)S(1)} %copy-done.28), channel_id=1, source_target_pairs={{0,4},{1,5},{2,6},{3,7},{4,0},{5,1},{6,2},{7,3},{8,12},{9,13},{10,... | collective-permute-start | bytes 196616 | tf_op jit(solution)/shard_map/ppermute | solution.py:348
  64.1 4.7 %collective-permute-start.17 = (bf16[192,128]{1,0:T(8,128)(2,1)S(1)}, bf16[192,128]{1,0:T(8,128)(2,1)S(1)}, u32[]{:S(2)}, u32[]{:S(2)}) collective-permute-start(bf16[192,128]{1,0:T(8,128)(2,1)S(1)} %get-tuple-element.49.refs_2_), channel_id=1, source_target_pairs={{0,4},{1,5},{2,6},{3,7},{4,0},{5,1},{6,2},{7,3},{8,12},{9,13},{10,... | collective-permute-start | bytes 147464 | tf_op jit(solution)/shard_map/ppermute | solution.py:348
  64.6 4.2 %collective-permute-start.18 = (bf16[192,128]{1,0:T(8,128)(2,1)S(1)}, bf16[192,128]{1,0:T(8,128)(2,1)S(1)}, u32[]{:S(2)}, u32[]{:S(2)}) collective-permute-start(bf16[192,128]{1,0:T(8,128)(2,1)S(1)} %collective-permute-done.14.refs_6_.refs_3_), channel_id=1, source_target_pairs={{0,4},{1,5},{2,6},{3,7},{4,0},{5,1},{6,2},{7,3},{8,12},{9,13},{10,... | collective-permute-start | bytes 147464 | tf_op jit(solution)/shard_map/ppermute | solution.py:348
  64.9 3.9 %collective-permute-start.20 = (bf16[192,128]{1,0:T(8,128)(2,1)S(1)}, bf16[192,128]{1,0:T(8,128)(2,1)S(1)}, u32[]{:S(2)}, u32[]{:S(2)}) collective-permute-start(bf16[192,128]{1,0:T(8,128)(2,1)S(1)} %collective-permute-done.16.refs_5_), channel_id=1, source_target_pairs={{0,4},{1,5},{2,6},{3,7},{4,0},{5,1},{6,2},{7,3},{8,12},{9,13},{10,... | collective-permute-start | bytes 147464 | tf_op jit(solution)/shard_map/ppermute | solution.py:348
  68.9 1.2 %collective-permute-start.19 = (bf16[192,128]{1,0:T(8,128)(2,1)S(1)}, bf16[192,128]{1,0:T(8,128)(2,1)S(1)}, u32[]{:S(2)}, u32[]{:S(2)}) collective-permute-start(bf16[192,128]{1,0:T(8,128)(2,1)S(1)} %collective-permute-done.15.refs_4_), channel_id=1, source_target_pairs={{0,4},{1,5},{2,6},{3,7},{4,0},{5,1},{6,2},{7,3},{8,12},{9,13},{10,... | collective-permute-start | bytes 147464 | tf_op jit(solution)/shard_map/ppermute | solution.py:348
  70.9 1.3 %collective-permute-start.22 = (f32[128,128]{1,0:T(8,128)S(1)}, f32[128,128]{1,0:T(8,128)S(1)}, u32[]{:S(2)}, u32[]{:S(2)}) collective-permute-start(f32[128,128]{1,0:T(8,128)S(1)} %get-tuple-element.54), channel_id=1, source_target_pairs={{0,4},{1,5},{2,6},{3,7},{4,0},{5,1},{6,2},{7,3},{8,12},{9,13},{10,... | collective-permute-start | bytes 196616 | tf_op jit(solution)/shard_map/ppermute | solution.py:348
  72.2 7.5 %copy-start.8 = (bf16[384,256]{1,0:T(8,128)(2,1)S(1)}, bf16[384,256]{1,0:T(8,128)(2,1)}, u32[]{:S(2)}) copy-start(bf16[384,256]{1,0:T(8,128)(2,1)} %refs_2_.5) | copy-start | bytes 589828
  72.3 7.5 %copy-start.9 = (bf16[384,256]{1,0:T(8,128)(2,1)S(1)}, bf16[384,256]{1,0:T(8,128)(2,1)}, u32[]{:S(2)}) copy-start(bf16[384,256]{1,0:T(8,128)(2,1)} %refs_1_.13) | copy-start | bytes 589828
  72.3 7.4 %copy-start.11 = (bf16[4,384,384]{2,1,0:T(8,128)(2,1)S(1)}, bf16[4,384,384]{2,1,0:T(8,128)(2,1)}, u32[]{:S(2)}) copy-start(bf16[4,384,384]{2,1,0:T(8,128)(2,1)} %copy-done.10) | copy-start | bytes 3538948
  72.3 7.4 %copy-start.17 = (f32[128,128]{1,0:T(8,128)S(1)}, f32[128,128]{1,0:T(8,128)}, u32[]{:S(2)}) copy-start(f32[128,128]{1,0:T(8,128)} %copy-done.16) | copy-start | bytes 196612
  75.6 8.2 %collective-permute-start.23 = (f32[96,2048]{1,0:T(8,128)S(1)}, f32[96,2048]{1,0:T(8,128)S(1)}, u32[]{:S(2)}, u32[]{:S(2)}) collective-permute-start(f32[96,2048]{1,0:T(8,128)S(1)} %get-tuple-element.56), channel_id=1, source_target_pairs={{0,4},{1,5},{2,6},{3,7},{4,0},{5,1},{6,2},{7,3},{8,12},{9,13},{10,... | collective-permute-start | bytes 2359304 | tf_op jit(solution)/shard_map/ppermute | solution.py:348
  75.8 8.0 %collective-permute-start.24 = (f32[96,2048]{1,0:T(8,128)S(1)}, f32[96,2048]{1,0:T(8,128)S(1)}, u32[]{:S(2)}, u32[]{:S(2)}) collective-permute-start(f32[96,2048]{1,0:T(8,128)S(1)} %get-tuple-element.58), channel_id=1, source_target_pairs={{0,4},{1,5},{2,6},{3,7},{4,0},{5,1},{6,2},{7,3},{8,12},{9,13},{10,... | collective-permute-start | bytes 2359304 | tf_op jit(solution)/shard_map/ppermute | solution.py:348
  76.1 6.6 %collective-permute-start.27 = (f32[128,128]{1,0:T(8,128)S(1)}, f32[128,128]{1,0:T(8,128)S(1)}, u32[]{:S(2)}, u32[]{:S(2)}) collective-permute-start(f32[128,128]{1,0:T(8,128)S(1)} %add.15.refs_11_.refs_8_), channel_id=1, source_target_pairs={{0,24},{1,25},{2,26},{3,27},{4,28},{5,29},{6,30},{7,31},{8,16},{9,... | collective-permute-start | bytes 196616 | tf_op jit(solution)/shard_map/ppermute | solution.py:348
  77.3 5.4 %collective-permute-start.26 = (f32[128,128]{1,0:T(8,128)S(1)}, f32[128,128]{1,0:T(8,128)S(1)}, u32[]{:S(2)}, u32[]{:S(2)}) collective-permute-start(f32[128,128]{1,0:T(8,128)S(1)} %add.15.refs_11_.refs_8_), channel_id=1, source_target_pairs={{0,16},{1,17},{2,18},{3,19},{4,20},{5,21},{6,22},{7,23},{8,24},{9,... | collective-permute-start | bytes 196616 | tf_op jit(solution)/shard_map/ppermute | solution.py:348
  78.8 4.3 %collective-permute-start.25 = (f32[128,128]{1,0:T(8,128)S(1)}, f32[128,128]{1,0:T(8,128)S(1)}, u32[]{:S(2)}, u32[]{:S(2)}) collective-permute-start(f32[128,128]{1,0:T(8,128)S(1)} %add.15.refs_11_.refs_8_), channel_id=1, source_target_pairs={{0,8},{1,9},{2,10},{3,11},{4,12},{5,13},{6,14},{7,15},{8,0},{9,1},... | collective-permute-start | bytes 196616 | tf_op jit(solution)/shard_map/ppermute | solution.py:348
  83.7 1.7 %collective-permute-start.28 = (f32[128,128]{1,0:T(8,128)S(1)}, f32[128,128]{1,0:T(8,128)S(1)}, u32[]{:S(2)}, u32[]{:S(2)}) collective-permute-start(f32[128,128]{1,0:T(8,128)S(1)} %get-tuple-element.66), channel_id=1, source_target_pairs={{0,4},{1,5},{2,6},{3,7},{4,0},{5,1},{6,2},{7,3},{8,12},{9,13},{10,... | collective-permute-start | bytes 196616 | tf_op jit(solution)/shard_map/ppermute | solution.py:348
  (11 other events, 8.0 us)
